TPU v7x, 32 devices: a whole 2x2x4 slice. The times are simulated.
32 devices in a mesh: parts: 2 (over y), gx: 16 (over z, x, core).
Axes of the slice: x: 2, y: 2, z: 4, core: 2. Of those that a mesh axis runs over, the one named last changes fastest.
Arguments:
- embeddings: bfloat16 [8192, 1024], P(('parts', 'gx')), parts along dimension 0, may hold values from -6 to 6
- cluster_ids: int32 [8192], P(('parts', 'gx')), parts along dimension 0, may hold values from 0 to 15, as said below
Outputs:
- density: float32 [8192], P(('parts', 'gx')), parts along dimension 0
There are 2 independent parts, one for each index of `parts`. A program takes and returns all parts, laid end to end along the dimension named above; each array names one. Nothing has to cross between parts.
Inputs may be any that keep to these rules, and one draw needn't show every extreme that they name: `cluster_ids`: the owner of cluster c is c. Among the 256 rows of one device, at most 48 belong to clusters of one owner, and in every device's rows some owner has exactly 48.
All inputs are finite; a program needn't handle non-finite values.
Results may differ from a plain program's by a relative error of at most 0.0003.
Values may be sent and summed in bfloat16 or wider, within the bound.
No kernel may reach another device: no remote copies, remote signals or barrier semaphores. Data moves between devices by JAX's collectives and lax.ppermute only.
A program may use at most 64 MiB of HBM per device.

v0:
```python
import jax
import jax.numpy as jnp
from jax import lax
from jax.sharding import PartitionSpec as P

CLU_DEV = 1


inverse_temp = 20.0


def tile_mass(query_rows, key_rows, query_ids, key_ids, query_start):
    similar = lax.dot_general(
        query_rows, key_rows, (((1,), (1,)), ((), ())), preferred_element_type=jnp.float32
    )
    query_pos = jnp.arange(query_rows.shape[0], dtype=jnp.int32) + query_start
    key_pos = jnp.arange(key_rows.shape[0], dtype=jnp.int32)
    mate_mask = (query_ids[:, None] == key_ids[None, :]) & (query_ids[:, None] >= 0)
    mate_mask = mate_mask & (query_pos[:, None] != key_pos[None, :])
    return jnp.where(mate_mask, jnp.exp(similar * inverse_temp), 0.0)


def density_scores(key_rows, key_ids):
    total_rows = key_rows.shape[0]
    block_rows = total_rows // 3
    pieces = [key_rows[i * block_rows : (i + 1) * block_rows] for i in range(3)]
    piece_ids = [key_ids[i * block_rows : (i + 1) * block_rows] for i in range(3)]
    sums = []
    for first in range(3):
        masses = tile_mass(pieces[first], key_rows, piece_ids[first], key_ids, first * block_rows)
        sums.append(jnp.sum(masses, axis=1))
    mass_sum = jnp.concatenate(sums, axis=0)
    return jnp.log1p(mass_sum)


def on_device(embeddings, cluster_ids):
    peer_count = lax.axis_size("gx")
    row_count = embeddings.shape[0]
    features = embeddings.shape[1]
    capacity = 3 * row_count // peer_count
    slot_total = peer_count * capacity
    squares = jnp.sum(jnp.square(embeddings.astype(jnp.float32)), axis=1)
    unit_rows = (embeddings.astype(jnp.float32) * lax.rsqrt(squares + 1e-06)[:, None]).astype(
        jnp.bfloat16
    )
    owner_of = cluster_ids // CLU_DEV
    onehot = (owner_of[:, None] == jnp.arange(peer_count, dtype=jnp.int32)[None, :]).astype(
        jnp.bfloat16
    )
    row_range = jnp.arange(row_count, dtype=jnp.int32)
    lower_tri = (row_range[:, None] >= row_range[None, :]).astype(jnp.bfloat16)
    running = jnp.dot(lower_tri, onehot, preferred_element_type=jnp.float32)
    slot_index = (jnp.sum(running * onehot.astype(jnp.float32), axis=1) - 1.0).astype(jnp.int32)
    target_slot = owner_of * capacity + slot_index
    slot_range = jnp.arange(slot_total, dtype=jnp.int32)
    select_mask = slot_range[:, None] == target_slot[None, :]
    outgoing = jnp.dot(
        select_mask.astype(jnp.bfloat16), unit_rows, preferred_element_type=jnp.float32
    )
    outgoing = outgoing.astype(jnp.bfloat16).reshape(peer_count, capacity, features)
    outgoing_ids = jnp.sum(jnp.where(select_mask, cluster_ids[None, :] + 1, 0), axis=1) - 1
    outgoing_ids = outgoing_ids.reshape(peer_count, capacity)
    arrived, arrived_ids = (
        lax.all_to_all(outgoing, "gx", split_axis=0, concat_axis=0, tiled=True),
        lax.all_to_all(outgoing_ids, "gx", split_axis=0, concat_axis=0, tiled=True),
    )
    key_rows = arrived.reshape(slot_total, features)
    key_ids = arrived_ids.reshape(slot_total)
    scores = density_scores(key_rows, key_ids)
    returned = lax.all_to_all(
        scores.reshape(peer_count, capacity), "gx", split_axis=0, concat_axis=0, tiled=True
    )
    flat_scores = returned.reshape(slot_total)
    pick_mask = target_slot[:, None] == slot_range[None, :]
    return jnp.sum(jnp.where(pick_mask, flat_scores[None, :], 0.0), axis=1)


def solution(mesh):
    in_specs = (P(("parts", "gx"), None), P(("parts", "gx")))
    out_specs = P(("parts", "gx"))
    return jax.shard_map(
        on_device, mesh=mesh, in_specs=in_specs, out_specs=out_specs, check_vma=False
    )
```

profile of v0, /device:TPU:0, one launch (start us, length us, event | category | flops | bytes accessed | tf_op | source)
XLA Modules:
  0.0 71.8 jit_solution(5077442155085874950)
XLA Ops:
  0.0 1.0 %fusion.9 = f32[256]{0:T(256)S(1)} fusion(s32[256]{0:T(256)} %param.3), kind=kOutput, calls=%fused_computation.16 | convolution fusion | flops 2187008 | bytes 2048 | tf_op jit(solution)/shard_map/dot_general | solution.py:52
  1.0 0.7 broadcast_add_fusion.1
  1.6 0.2 select_reduce_fusion.1
  1.8 0.7 sub.16
  2.5 7.4 %all-to-all-start = ((s32[16,1,48]{2,1,0:T(1,128)}), s32[16,1,48]{2,1,0:T(1,128)S(1)}, u32[]{:S(2)}, u32[]{:S(2)}) async-start(s32[16,1,48]{2,1,0:T(1,128)} %sub.16), calls=%async_computation | async-start | bytes 16384 | tf_op jit(solution)/shard_map/all_to_all | solution.py:65
  9.9 1.2 %fusion.10 = f32[256]{0:T(256)S(1)} fusion(bf16[256,1024]{1,0:T(8,128)(2,1)} %param.2), kind=kLoop, calls=%fused_computation.17 | loop fusion | flops 786176 | bytes 525312 | tf_op jit(solution)/shard_map/reduce_sum | solution.py:42
  11.1 2.9 %convolution_convert_fusion = bf16[768,1024]{1,0:T(8,128)(2,1)} fusion(bf16[256,1024]{1,0:T(8,128)(2,1)} %param.2, f32[256]{0:T(256)S(1)} %add_rsqrt_fusion, s32[256]{0:T(256)S(1)} %get-tuple-element.12), kind=kOutput, calls=%fused_computation | convolution fusion | flops 404422656 | bytes 2099200 | tf_op jit(solution)/shard_map/dot_general | solution.py:57
  14.0 2.3 %all-to-all-done = s32[16,1,48]{2,1,0:T(1,128)S(1)} async-done(((s32[16,1,48]{2,1,0:T(1,128)}), s32[16,1,48]{2,1,0:T(1,128)S(1)}, u32[]{:S(2)}, u32[]{:S(2)}) %all-to-all-start) | async-done | bytes 3104 | tf_op jit(solution)/shard_map/all_to_all | solution.py:65
  16.3 3.7 %all-to-all-start.1 = ((bf16[16,48,1024]{2,1,0:T(8,128)(2,1)}), bf16[16,48,1024]{2,1,0:T(8,128)(2,1)S(1)}, u32[]{:S(2)}, u32[]{:S(2)}) async-start(bf16[16,48,1024]{2,1,0:T(8,128)(2,1)} %bitcast), calls=%async_computation.1 | async-start | bytes 3145728 | tf_op jit(solution)/shard_map/all_to_all | solution.py:64
  20.0 0.5 broadcast.66
  20.5 0.7 reduce.6
  21.2 0.1 reshape.71
  21.3 30.7 %all-to-all-done.1 = bf16[16,48,1024]{2,1,0:T(8,128)(2,1)S(1)} async-done(((bf16[16,48,1024]{2,1,0:T(8,128)(2,1)}), bf16[16,48,1024]{2,1,0:T(8,128)(2,1)S(1)}, u32[]{:S(2)}, u32[]{:S(2)}) %all-to-all-start.1) | async-done | bytes 1572896 | tf_op jit(solution)/shard_map/all_to_all | solution.py:64
  52.0 0.7 %fusion.6 = f32[256]{0:T(256)S(1)} fusion(bf16[768,1024]{1,0:T(8,128)(2,1)S(1)} %bitcast.5, s32[768]{0:T(1024)S(1)} %reshape.71, s32[256]{0:T(256)S(1)} %get-tuple-element.8, pred[256]{0:T(512)(128)(4,1)S(1)} %get-tuple-element.5), kind=kOutput, calls=%fused_computation.12 | convolution fusion | flops 404029184 | bytes 2103808 | tf_op jit(solution)/shard_map/dot_general | solution.py:13
  52.7 0.8 %fusion.8 = f32[256]{0:T(256)S(1)} fusion(bf16[768,1024]{1,0:T(8,128)(2,1)S(1)} %bitcast.6, s32[256]{0:T(256)S(1)} %iota_add_fusion, s32[768]{0:T(1024)S(1)} %reshape.71, s32[256]{0:T(256)S(1)} %get-tuple-element.9, pred[256]{0:T(512)(128)(4,1)S(1)} %get-tuple-element.7), kind=kOutput, calls=%fused_computation.14 | convolution fusion | flops 404029184 | bytes 2104832 | tf_op jit(solution)/shard_map/dot_general | solution.py:13
  53.5 0.8 %fusion.7 = f32[256]{0:T(256)S(1)} fusion(bf16[768,1024]{1,0:T(8,128)(2,1)S(1)} %bitcast.7, s32[256]{0:T(256)S(1)} %iota_add_fusion.1, s32[768]{0:T(1024)S(1)} %reshape.71, s32[256]{0:T(256)S(1)} %get-tuple-element.10, pred[256]{0:T(512)(128)(4,1)S(1)} %get-tuple-element.6), kind=kOutput, calls=%fused_computation.13 | convolution fusion | flops 404029184 | bytes 2104832 | tf_op jit(solution)/shard_map/dot_general | solution.py:13
  54.3 0.1 log1p.15
  54.4 15.3 %all_to_all.17 = f32[16,1,48]{2,1,0:T(1,128)S(1)} all-to-all(f32[16,1,48]{2,1,0:T(1,128)S(1)} %log1p.15), channel_id=1, replica_groups=mesh['parts'=2,'gx'=16] {'gx'}, dimensions={0} | all-to-all | bytes 6144 | tf_op jit(solution)/shard_map/all_to_all | solution.py:70
  69.7 0.5 broadcast.67
  70.2 0.7 reduce.7
  70.9 0.1 broadcast_in_dim.29
  71.0 0.8 %select_reduce_fusion = f32[256]{0:T(256)} fusion(f32[768]{0:T(1024)S(1)} %broadcast_in_dim.29, s32[256]{0:T(256)S(1)} %get-tuple-element.12), kind=kLoop, calls=%fused_computation.19 | loop fusion | flops 589568 | bytes 5120 | tf_op jit(solution)/shard_map/reduce_sum | solution.py:75
  (7 shorter events, 0.0 us)
Async XLA Ops:
  2.5 13.8 %all-to-all-start = ((s32[16,1,48]{2,1,0:T(1,128)}), s32[16,1,48]{2,1,0:T(1,128)S(1)}, u32[]{:S(2)}, u32[]{:S(2)}) async-start(s32[16,1,48]{2,1,0:T(1,128)} %sub.16), calls=%async_computation | async-start | bytes 16384 | tf_op jit(solution)/shard_map/all_to_all | solution.py:65
  16.3 35.7 %all-to-all-start.1 = ((bf16[16,48,1024]{2,1,0:T(8,128)(2,1)}), bf16[16,48,1024]{2,1,0:T(8,128)(2,1)S(1)}, u32[]{:S(2)}, u32[]{:S(2)}) async-start(bf16[16,48,1024]{2,1,0:T(8,128)(2,1)} %bitcast), calls=%async_computation.1 | async-start | bytes 3145728 | tf_op jit(solution)/shard_map/all_to_all | solution.py:64
where the time goes:
time: 72.2 us; the launch traced here: 71.8 us
  waiting for transfers between devices  33 us (46%)
  blocking collectives  15.3 us (21%)
  starting transfers between devices  11.1 us (15%)
  matrix products  6.13 us (8%)
  other arithmetic  4.27 us (6%)
  local copies, waits for them, and re-layouts  1.94 us (3%)
    all_to_all x1, waiting for transfers between devices, on_device(): lax.all_to_all(outgoing, 'gx', split_axis=0, concat_axis=0, tiled=True)  30.7 us
    all_to_all x1, blocking collectives, on_device(): lax.all_to_all(scores.reshape(peer_count, capacity), 'gx', split_axis=0,...  15.3 us
    all_to_all x1, starting transfers between devices, on_device(): lax.all_to_all(outgoing_ids, 'gx', split_axis=0, concat_axis=0, tiled=True)  7.36 us
    all_to_all x1, starting transfers between devices, on_device(): lax.all_to_all(outgoing, 'gx', split_axis=0, concat_axis=0, tiled=True)  3.72 us
    dot_general x1, matrix products, on_device(): jnp.dot(select_mask.astype(jnp.bfloat16), unit_rows, preferred_element_ty...  2.86 us
    dot_general x3, matrix products, tile_mass(): lax.dot_general(query_rows, key_rows, (((1,), (1,)), ((), ())), preferred...  2.32 us
    all_to_all x1, waiting for transfers between devices, on_device(): lax.all_to_all(outgoing_ids, 'gx', split_axis=0, concat_axis=0, tiled=True)  2.3 us
  transfers between devices with their start and end apart: 2, of which 2 were waited for; matrix products, arithmetic and copies ran while one was open for 7% of the time, Pallas kernels for 0%

commit v1 on v0

--- a/solution.py
+++ b/solution.py
@@ -1,11 +1,14 @@
+import functools
+
 import jax
 import jax.numpy as jnp
 from jax import lax
+from jax.experimental import pallas as pl
+from jax.experimental.pallas import tpu as pltpu
 from jax.sharding import PartitionSpec as P
 
 CLU_DEV = 1
-
-
+PAD_MARK = 64.0
 inverse_temp = 20.0
 
 
@@ -33,7 +36,7 @@
     return jnp.log1p(mass_sum)
 
 
-def on_device(embeddings, cluster_ids):
+def plain_plan(embeddings, cluster_ids):
     peer_count = lax.axis_size("gx")
     row_count = embeddings.shape[0]
     features = embeddings.shape[1]
@@ -75,6 +78,130 @@
     return jnp.sum(jnp.where(pick_mask, flat_scores[None, :], 0.0), axis=1)
 
 
+LANES = 128
+PLANE = 4
+ID_ROWS = 16
+
+
+def unit_kernel(rows_ref, ids_ref, block_ref):
+    row_count, width = rows_ref.shape
+    features = rows_ref[...].astype(jnp.float32)
+    squares = jnp.sum(features * features, axis=1, keepdims=True)
+    block_ref[:row_count, :] = (features * lax.rsqrt(squares + 1e-06)).astype(jnp.bfloat16)
+    block_ref[row_count:, :] = jnp.zeros((ID_ROWS, width), jnp.bfloat16)
+    block_ref[row_count:, :row_count] = jnp.broadcast_to(
+        ids_ref[...].astype(jnp.float32), (ID_ROWS, row_count)
+    ).astype(jnp.bfloat16)
+
+
+def ids_along_lanes(block_ref):
+    row_count = block_ref.shape[0] - ID_ROWS
+    return block_ref[row_count:, :row_count].astype(jnp.float32)[:1]
+
+
+def ids_along_rows(block_ref):
+    ids = ids_along_lanes(block_ref)
+    return jnp.broadcast_to(ids, (LANES, ids.shape[1])).T
+
+
+def mate_mass(query_rows, query_ids, key_rows, key_ids, same_block):
+    similar = lax.dot_general(
+        query_rows, key_rows, (((1,), (1,)), ((), ())), preferred_element_type=jnp.float32
+    )
+    repeats = similar.shape[1] // LANES
+    mates = jnp.concatenate([query_ids] * repeats, axis=1) == key_ids
+    if same_block:
+        query_pos = lax.broadcasted_iota(jnp.int32, similar.shape, 0)
+        key_pos = lax.broadcasted_iota(jnp.int32, similar.shape, 1)
+        mates = mates & (query_pos != key_pos)
+    return jnp.where(mates, jnp.exp(similar * inverse_temp), 0.0)
+
+
+def score_kernel(planes, *refs):
+    plane_refs, line_refs = refs[:PLANE], refs[PLANE : PLANE + 2]
+    row_refs, column_refs = refs[PLANE + 2 : 2 * PLANE + 2], refs[2 * PLANE + 2 : -2]
+    row_ids, lane_sums = refs[-2:]
+    rows = row_refs[0].shape[1]
+    plane = lax.axis_index("gx") // PLANE
+    own_ref = plane_refs[0]
+    own_ids = ids_along_lanes(own_ref)
+    own_mass = jnp.zeros((1, rows), jnp.float32)
+    for m in range(PLANE):
+        part = pl.ds(m * rows, rows)
+        query_ids = ids_along_rows(plane_refs[m])
+        row_ids[part, :] = query_ids
+        masses = mate_mass(
+            plane_refs[m][:rows, :], query_ids, own_ref[:rows, :], own_ids, m == 0
+        )
+        own_mass = own_mass + jnp.sum(masses, axis=0, keepdims=True)
+    lane_sums[...] = jnp.zeros_like(lane_sums)
+    for n in range(2):
+        line_ref, column_ref = line_refs[n], column_refs[n]
+        column_ref[...] = jnp.zeros_like(column_ref)
+        arrived = plane != (planes - 1 if n == 0 else 0)
+
+        @pl.when(arrived)
+        def _():
+            key_ids = ids_along_lanes(line_ref)
+            for m in range(PLANE):
+                part = pl.ds(m * rows, rows)
+                masses = mate_mass(
+                    plane_refs[m][:rows, :], row_ids[part, :], line_ref[:rows, :], key_ids, False
+                )
+                column_ref[...] += jnp.sum(masses, axis=0, keepdims=True)
+                folded = masses[:, :LANES]
+                for first in range(LANES, rows, LANES):
+                    folded = folded + masses[:, first : first + LANES]
+                lane_sums[part, :] += folded
+
+    for m in range(PLANE):
+        part = pl.ds(m * rows, rows)
+        row_sum = jnp.sum(lane_sums[part, :].T, axis=0, keepdims=True)
+        row_refs[m][...] = own_mass + row_sum if m == 0 else row_sum
+
+
+def grid_plan(embeddings, cluster_ids):
+    peers = lax.axis_size("gx")
+    row_count, features = embeddings.shape
+    planes = peers // PLANE
+
+    def in_plane(value, step):
+        return lax.ppermute(value, "gx", [(i, i ^ step) for i in range(peers)])
+
+    def on_line(value, moves):
+        pairs = [(a * PLANE + n, b * PLANE + n) for a, b in moves for n in range(PLANE)]
+        return lax.ppermute(value, "gx", pairs)
+
+    first_moves = [(0, 1), (3, 2), (2, 0)]
+    second_moves = [(1, 2), (0, 3), (3, 1)]
+    first_back = [(b, a) for a, b in first_moves]
+    second_back = [(b, a) for a, b in second_moves]
+
+    block = pl.pallas_call(
+        unit_kernel,
+        out_shape=jax.ShapeDtypeStruct((row_count + ID_ROWS, features), jnp.bfloat16),
+    )(embeddings, cluster_ids.reshape(1, row_count))
+    plane_blocks = [block] + [in_plane(block, step) for step in range(1, PLANE)]
+    line_blocks = [on_line(block, first_moves), on_line(block, second_moves)]
+    vector = jax.ShapeDtypeStruct((1, row_count), jnp.float32)
+    sums = pl.pallas_call(
+        functools.partial(score_kernel, planes),
+        out_shape=[vector] * (PLANE + 2),
+        scratch_shapes=[pltpu.VMEM((PLANE * row_count, LANES), jnp.float32)] * 2,
+    )(*plane_blocks, *line_blocks)
+    mass = sums[0]
+    for step in range(1, PLANE):
+        mass = mass + in_plane(sums[step], step)
+    mass = mass + on_line(sums[PLANE], first_back) + on_line(sums[PLANE + 1], second_back)
+    return jnp.log1p(mass).reshape(row_count)
+
+
+def on_device(embeddings, cluster_ids):
+    if lax.axis_size("gx") == 4 * PLANE and embeddings.shape[0] % LANES == 0:
+        return grid_plan(embeddings, cluster_ids)
+    return plain_plan(embeddings, cluster_ids)
+
+
 def solution(mesh):
     in_specs = (P(("parts", "gx"), None), P(("parts", "gx")))
     out_specs = P(("parts", "gx"))

time: 72.2 us -> 61 us (0.84)
  blocking collectives: 15.3 us -> 0 us
  starting transfers between devices: 11.1 us -> 19.2 us
  Pallas kernels: 0 us -> 6.55 us
  matrix products: 6.13 us -> 0 us
  other arithmetic: 4.27 us -> 0.58 us
  waiting for transfers between devices: 33 us -> 31.1 us
  local copies, waits for them, and re-layouts: 1.94 us -> 3.11 us
    all_to_all x2 -> x0, waiting for transfers between devices: 33 us -> none  [the longest x1 30.7 us: on_device(): lax.all_to_all(outgoing, 'gx', split_axis=0, concat_axis=0, tiled=True)]
    ppermute x0 -> x10, waiting for transfers between devices: none -> 31.1 us  [the longest x4 26.8 us: on_line(): return lax.ppermute(value, 'gx', pairs)]
    ppermute x0 -> x10, starting transfers between devices: none -> 19.2 us  [the longest x4 15.8 us: on_line(): return lax.ppermute(value, 'gx', pairs)]
    all_to_all x1 -> x0, blocking collectives: 15.3 us -> none  [on_device(): lax.all_to_all(scores.reshape(peer_count, capacity), 'gx', split_axis=0,...]
    all_to_all x2 -> x0, starting transfers between devices: 11.1 us -> none  [the longest x1 7.36 us: on_device(): lax.all_to_all(outgoing_ids, 'gx', split_axis=0, concat_axis=0, tiled=True)]
    pallas_call x0 -> x2, Pallas kernels: none -> 6.55 us  [the longest x1 4.5 us: grid_plan(): pl.pallas_call(functools.partial(score_kernel, planes), out_shape=[vector...]
    dot_general x5 -> x0, matrix products: 6.13 us -> none  [the longest x1 2.86 us: on_device(): jnp.dot(select_mask.astype(jnp.bfloat16), unit_rows, preferred_element_ty...]
    unnamed x0 -> x22, local copies, waits for them, and re-layouts: none -> 3.11 us
  transfers between devices with their start and end apart: 2 -> 10, of which waited for: 2 -> 4; matrix products, arithmetic and copies ran while one was open for 7% -> 0% of each run, Pallas kernels for 0% -> 0%
where the time goes in v1:
time: 61 us; the launch traced here: 60.7 us
  waiting for transfers between devices  31.1 us (51%)
  starting transfers between devices  19.2 us (31%)
  Pallas kernels  6.55 us (11%)
  local copies, waits for them, and re-layouts  3.11 us (5%)
    ppermute x4, waiting for transfers between devices, on_line(): return lax.ppermute(value, 'gx', pairs)  26.8 us
    ppermute x4, starting transfers between devices, on_line(): return lax.ppermute(value, 'gx', pairs)  15.8 us
    pallas_call x1, Pallas kernels, grid_plan(): pl.pallas_call(functools.partial(score_kernel, planes), out_shape=[vector...  4.5 us
    ppermute x6, waiting for transfers between devices, in_plane(): return lax.ppermute(value, 'gx', [(i, i ^ step) for i in range(peers)])  4.3 us
    ppermute x6, starting transfers between devices, in_plane(): return lax.ppermute(value, 'gx', [(i, i ^ step) for i in range(peers)])  3.4 us
    unnamed x22, local copies, waits for them, and re-layouts  3.11 us
    pallas_call x1, Pallas kernels, grid_plan(): pl.pallas_call(unit_kernel, out_shape=jax.ShapeDtypeStruct((row_count + I...  2.04 us
  transfers between devices with their start and end apart: 10, of which 4 were waited for; matrix products, arithmetic and copies ran while one was open for 0% of the time, Pallas kernels for 0%

profile of v1, /device:TPU:0, one launch (start us, length us, event | category | flops | bytes accessed | tf_op | source)
XLA Modules:
  0.0 60.7 jit_solution(13603795167820436842)
XLA Ops:
  0.0 2.0 %shard_map.28.refs_0_ = bf16[272,1024]{1,0:T(8,128)(2,1)} custom-call(bf16[256,1024]{1,0:T(8,128)(2,1)} %rows_ref.1, s32[1,256]{1,0:T(1,128)} %bitcast.2), custom_call_target="tpu_custom_call" | custom-call | tf_op jit(solution)/shard_map/pallas_call | solution.py:180
  2.0 7.0 %collective-permute-start.4 = (bf16[272,1024]{1,0:T(8,128)(2,1)}, bf16[272,1024]{1,0:T(8,128)(2,1)S(1)}, u32[]{:S(2)}, u32[]{:S(2)}) collective-permute-start(bf16[272,1024]{1,0:T(8,128)(2,1)} %shard_map.28.refs_0_), channel_id=1, source_target_pairs={{4,8},{5,9},{6,10},{7,11},{0,12},{1,13},{2,14},{3,15},{12,4},{13,5... | collective-permute-start | bytes 1671176 | tf_op jit(solution)/shard_map/ppermute | solution.py:173
  9.0 1.9 %collective-permute-start.3 = (bf16[272,1024]{1,0:T(8,128)(2,1)}, bf16[272,1024]{1,0:T(8,128)(2,1)S(1)}, u32[]{:S(2)}, u32[]{:S(2)}) collective-permute-start(bf16[272,1024]{1,0:T(8,128)(2,1)} %shard_map.28.refs_0_), channel_id=1, source_target_pairs={{0,4},{1,5},{2,6},{3,7},{12,8},{13,9},{14,10},{15,11},{8,0},{9,1},... | collective-permute-start | bytes 1671176 | tf_op jit(solution)/shard_map/ppermute | solution.py:173
  11.0 0.7 %collective-permute-start.2 = (bf16[272,1024]{1,0:T(8,128)(2,1)}, bf16[272,1024]{1,0:T(8,128)(2,1)S(1)}, u32[]{:S(2)}, u32[]{:S(2)}) collective-permute-start(bf16[272,1024]{1,0:T(8,128)(2,1)} %shard_map.28.refs_0_), channel_id=1, source_target_pairs={{0,3},{1,2},{2,1},{3,0},{4,7},{5,6},{6,5},{7,4},{8,11},{9,10},{10,... | collective-permute-start | bytes 1671176 | tf_op jit(solution)/shard_map/ppermute | solution.py:169
  11.7 0.9 %collective-permute-start.1 = (bf16[272,1024]{1,0:T(8,128)(2,1)}, bf16[272,1024]{1,0:T(8,128)(2,1)S(1)}, u32[]{:S(2)}, u32[]{:S(2)}) collective-permute-start(bf16[272,1024]{1,0:T(8,128)(2,1)} %shard_map.28.refs_0_), channel_id=1, source_target_pairs={{0,2},{1,3},{2,0},{3,1},{4,6},{5,7},{6,4},{7,5},{8,10},{9,11},{10,... | collective-permute-start | bytes 1671176 | tf_op jit(solution)/shard_map/ppermute | solution.py:169
  12.6 0.3 collective-permute-start
  12.9 9.4 %collective-permute-done.4.refs_5_ = bf16[272,1024]{1,0:T(8,128)(2,1)S(1)} collective-permute-done((bf16[272,1024]{1,0:T(8,128)(2,1)}, bf16[272,1024]{1,0:T(8,128)(2,1)S(1)}, u32[]{:S(2)}, u32[]{:S(2)}) %collective-permute-start.4) | collective-permute-done | bytes 557088 | tf_op jit(solution)/shard_map/ppermute | solution.py:173
  22.3 0.0 copy-start
  22.3 11.5 %collective-permute-done.3.refs_4_ = bf16[272,1024]{1,0:T(8,128)(2,1)S(1)} collective-permute-done((bf16[272,1024]{1,0:T(8,128)(2,1)}, bf16[272,1024]{1,0:T(8,128)(2,1)S(1)}, u32[]{:S(2)}, u32[]{:S(2)}) %collective-permute-start.3) | collective-permute-done | bytes 557088 | tf_op jit(solution)/shard_map/ppermute | solution.py:173
  33.8 0.0 copy-start.1
  33.8 0.0 collective-permute-done.2.refs_3_
  33.8 0.0 copy-start.2
  33.8 4.3 %collective-permute-done.1.refs_2_ = bf16[272,1024]{1,0:T(8,128)(2,1)S(1)} collective-permute-done((bf16[272,1024]{1,0:T(8,128)(2,1)}, bf16[272,1024]{1,0:T(8,128)(2,1)S(1)}, u32[]{:S(2)}, u32[]{:S(2)}) %collective-permute-start.1) | collective-permute-done | bytes 557088 | tf_op jit(solution)/shard_map/ppermute | solution.py:169
  38.1 0.0 copy-start.3
  38.1 0.0 collective-permute-done.refs_1_
  38.1 0.0 copy-done
  38.1 0.0 copy-done.1
  38.1 0.0 copy-done.2
  38.1 0.8 %copy-done.3 = bf16[272,1024]{1,0:T(8,128)(2,1)} copy-done((bf16[272,1024]{1,0:T(8,128)(2,1)}, bf16[272,1024]{1,0:T(8,128)(2,1)S(1)}, u32[]{:S(2)}) %copy-start.3) | copy-done | bytes 557080
  38.9 0.0 copy-start.4
  38.9 0.8 %copy-done.4 = bf16[272,1024]{1,0:T(8,128)(2,1)} copy-done((bf16[272,1024]{1,0:T(8,128)(2,1)}, bf16[272,1024]{1,0:T(8,128)(2,1)S(1)}, u32[]{:S(2)}) %copy-start.4) | copy-done | bytes 557080
  39.7 4.5 %shard_map.29 = (f32[1,256]{1,0:T(1,128)}, f32[1,256]{1,0:T(1,128)}, f32[1,256]{1,0:T(1,128)}, f32[1,256]{1,0:T(1,128)}, f32[1,256]{1,0:T(1,128)}, /*index=5*/f32[1,256]{1,0:T(1,128)}) custom-call(bf16[272,1024]{1,0:T(8,128)(2,1)} %shard_map.28.refs_0_, bf16[272,1024]{1,0:T(8,128)(2,1)} %copy-done.4, bf16[272,1024]{1,0:T(8,128)(2,1)} %copy-done.3, ...), custom_call_target="tpu_custom_call" | custom-call | tf_op jit(solution)/shard_map/pallas_call | solution.py:187
  44.2 0.0 copy-start.10
  44.2 0.7 %copy-done.10 = f32[1,256]{1,0:T(1,128)S(1)} copy-done((f32[1,256]{1,0:T(1,128)S(1)}, f32[1,256]{1,0:T(1,128)}, u32[]{:S(2)}) %copy-start.10) | copy-done | bytes 1048
  44.9 0.0 copy-start.9
  44.9 0.1 collective-permute-start.5
  45.0 0.6 copy-done.9
  45.6 0.0 copy-start.8
  45.6 1.0 %collective-permute-start.6 = (f32[1,256]{1,0:T(1,128)S(1)}, f32[1,256]{1,0:T(1,128)S(1)}, u32[]{:S(2)}, u32[]{:S(2)}) collective-permute-start(f32[1,256]{1,0:T(1,128)S(1)} %copy-done.9), channel_id=1, source_target_pairs={{0,2},{1,3},{2,0},{3,1},{4,6},{5,7},{6,4},{7,5},{8,10},{9,11},{10,... | collective-permute-start | bytes 3080 | tf_op jit(solution)/shard_map/ppermute | solution.py:169
  46.5 0.0 copy-done.8
  46.5 0.0 copy-start.7
  46.5 0.5 collective-permute-start.7
  47.0 0.2 copy-done.7
  47.2 0.0 copy-start.6
  47.2 5.6 %collective-permute-start.8 = (f32[1,256]{1,0:T(1,128)S(1)}, f32[1,256]{1,0:T(1,128)S(1)}, u32[]{:S(2)}, u32[]{:S(2)}) collective-permute-start(f32[1,256]{1,0:T(1,128)S(1)} %copy-done.7), channel_id=1, source_target_pairs={{4,0},{5,1},{6,2},{7,3},{8,12},{9,13},{10,14},{11,15},{0,8},{1,9},... | collective-permute-start | bytes 3080 | tf_op jit(solution)/shard_map/ppermute | solution.py:173
  52.9 0.0 copy-done.6
  52.9 0.0 copy-start.5
  52.9 1.3 %collective-permute-start.9 = (f32[1,256]{1,0:T(1,128)S(1)}, f32[1,256]{1,0:T(1,128)S(1)}, u32[]{:S(2)}, u32[]{:S(2)}) collective-permute-start(f32[1,256]{1,0:T(1,128)S(1)} %copy-done.6), channel_id=1, source_target_pairs={{8,4},{9,5},{10,6},{11,7},{12,0},{13,1},{14,2},{15,3},{4,12},{5,13... | collective-permute-start | bytes 3080 | tf_op jit(solution)/shard_map/ppermute | solution.py:173
  54.2 0.0 collective-permute-done.5
  54.2 0.0 collective-permute-done.6
  54.2 0.0 collective-permute-done.7
  54.2 0.0 collective-permute-done.8
  54.2 5.9 %collective-permute-done.9 = f32[1,256]{1,0:T(1,128)S(1)} collective-permute-done((f32[1,256]{1,0:T(1,128)S(1)}, f32[1,256]{1,0:T(1,128)S(1)}, u32[]{:S(2)}, u32[]{:S(2)}) %collective-permute-start.9) | collective-permute-done | bytes 1056 | tf_op jit(solution)/shard_map/ppermute | solution.py:173
  60.1 0.0 copy-done.5
  60.1 0.6 add_log-plus-one_fusion
Async XLA Ops:
  2.0 20.3 %collective-permute-start.4 = (bf16[272,1024]{1,0:T(8,128)(2,1)}, bf16[272,1024]{1,0:T(8,128)(2,1)S(1)}, u32[]{:S(2)}, u32[]{:S(2)}) collective-permute-start(bf16[272,1024]{1,0:T(8,128)(2,1)} %shard_map.28.refs_0_), channel_id=1, source_target_pairs={{4,8},{5,9},{6,10},{7,11},{0,12},{1,13},{2,14},{3,15},{12,4},{13,5... | collective-permute-start | bytes 1671176 | tf_op jit(solution)/shard_map/ppermute | solution.py:173
  9.0 24.8 %collective-permute-start.3 = (bf16[272,1024]{1,0:T(8,128)(2,1)}, bf16[272,1024]{1,0:T(8,128)(2,1)S(1)}, u32[]{:S(2)}, u32[]{:S(2)}) collective-permute-start(bf16[272,1024]{1,0:T(8,128)(2,1)} %shard_map.28.refs_0_), channel_id=1, source_target_pairs={{0,4},{1,5},{2,6},{3,7},{12,8},{13,9},{14,10},{15,11},{8,0},{9,1},... | collective-permute-start | bytes 1671176 | tf_op jit(solution)/shard_map/ppermute | solution.py:173
  11.0 22.8 %collective-permute-start.2 = (bf16[272,1024]{1,0:T(8,128)(2,1)}, bf16[272,1024]{1,0:T(8,128)(2,1)S(1)}, u32[]{:S(2)}, u32[]{:S(2)}) collective-permute-start(bf16[272,1024]{1,0:T(8,128)(2,1)} %shard_map.28.refs_0_), channel_id=1, source_target_pairs={{0,3},{1,2},{2,1},{3,0},{4,7},{5,6},{6,5},{7,4},{8,11},{9,10},{10,... | collective-permute-start | bytes 1671176 | tf_op jit(solution)/shard_map/ppermute | solution.py:169
  11.7 26.4 %collective-permute-start.1 = (bf16[272,1024]{1,0:T(8,128)(2,1)}, bf16[272,1024]{1,0:T(8,128)(2,1)S(1)}, u32[]{:S(2)}, u32[]{:S(2)}) collective-permute-start(bf16[272,1024]{1,0:T(8,128)(2,1)} %shard_map.28.refs_0_), channel_id=1, source_target_pairs={{0,2},{1,3},{2,0},{3,1},{4,6},{5,7},{6,4},{7,5},{8,10},{9,11},{10,... | collective-permute-start | bytes 1671176 | tf_op jit(solution)/shard_map/ppermute | solution.py:169
  12.6 25.5 %collective-permute-start = (bf16[272,1024]{1,0:T(8,128)(2,1)}, bf16[272,1024]{1,0:T(8,128)(2,1)S(1)}, u32[]{:S(2)}, u32[]{:S(2)}) collective-permute-start(bf16[272,1024]{1,0:T(8,128)(2,1)} %shard_map.28.refs_0_), channel_id=1, source_target_pairs={{0,1},{1,0},{2,3},{3,2},{4,5},{5,4},{6,7},{7,6},{8,9},{9,8},{10,11... | collective-permute-start | bytes 1671176 | tf_op jit(solution)/shard_map/ppermute | solution.py:169
  22.3 15.8 %copy-start = (bf16[272,1024]{1,0:T(8,128)(2,1)}, bf16[272,1024]{1,0:T(8,128)(2,1)S(1)}, u32[]{:S(2)}) copy-start(bf16[272,1024]{1,0:T(8,128)(2,1)S(1)} %collective-permute-done.4.refs_5_) | copy-start | bytes 1671172
  33.8 4.3 %copy-start.1 = (bf16[272,1024]{1,0:T(8,128)(2,1)}, bf16[272,1024]{1,0:T(8,128)(2,1)S(1)}, u32[]{:S(2)}) copy-start(bf16[272,1024]{1,0:T(8,128)(2,1)S(1)} %collective-permute-done.3.refs_4_) | copy-start | bytes 1671172
  33.8 4.3 %copy-start.2 = (bf16[272,1024]{1,0:T(8,128)(2,1)}, bf16[272,1024]{1,0:T(8,128)(2,1)S(1)}, u32[]{:S(2)}) copy-start(bf16[272,1024]{1,0:T(8,128)(2,1)S(1)} %collective-permute-done.2.refs_3_) | copy-start | bytes 1671172
  38.1 0.8 %copy-start.3 = (bf16[272,1024]{1,0:T(8,128)(2,1)}, bf16[272,1024]{1,0:T(8,128)(2,1)S(1)}, u32[]{:S(2)}) copy-start(bf16[272,1024]{1,0:T(8,128)(2,1)S(1)} %collective-permute-done.1.refs_2_) | copy-start | bytes 1671172
  38.9 0.8 %copy-start.4 = (bf16[272,1024]{1,0:T(8,128)(2,1)}, bf16[272,1024]{1,0:T(8,128)(2,1)S(1)}, u32[]{:S(2)}) copy-start(bf16[272,1024]{1,0:T(8,128)(2,1)S(1)} %collective-permute-done.refs_1_) | copy-start | bytes 1671172
  44.2 0.7 %copy-start.10 = (f32[1,256]{1,0:T(1,128)S(1)}, f32[1,256]{1,0:T(1,128)}, u32[]{:S(2)}) copy-start(f32[1,256]{1,0:T(1,128)} %get-tuple-element.12) | copy-start | bytes 3076
  44.9 0.7 %copy-start.9 = (f32[1,256]{1,0:T(1,128)S(1)}, f32[1,256]{1,0:T(1,128)}, u32[]{:S(2)}) copy-start(f32[1,256]{1,0:T(1,128)} %get-tuple-element.13) | copy-start | bytes 3076
  44.9 9.3 %collective-permute-start.5 = (f32[1,256]{1,0:T(1,128)S(1)}, f32[1,256]{1,0:T(1,128)S(1)}, u32[]{:S(2)}, u32[]{:S(2)}) collective-permute-start(f32[1,256]{1,0:T(1,128)S(1)} %copy-done.10), channel_id=1, source_target_pairs={{0,1},{1,0},{2,3},{3,2},{4,5},{5,4},{6,7},{7,6},{8,9},{9,8},{10,11... | collective-permute-start | bytes 3080 | tf_op jit(solution)/shard_map/ppermute | solution.py:169
  45.6 1.0 %copy-start.8 = (f32[1,256]{1,0:T(1,128)S(1)}, f32[1,256]{1,0:T(1,128)}, u32[]{:S(2)}) copy-start(f32[1,256]{1,0:T(1,128)} %get-tuple-element.14) | copy-start | bytes 3076
  45.6 8.6 %collective-permute-start.6 = (f32[1,256]{1,0:T(1,128)S(1)}, f32[1,256]{1,0:T(1,128)S(1)}, u32[]{:S(2)}, u32[]{:S(2)}) collective-permute-start(f32[1,256]{1,0:T(1,128)S(1)} %copy-done.9), channel_id=1, source_target_pairs={{0,2},{1,3},{2,0},{3,1},{4,6},{5,7},{6,4},{7,5},{8,10},{9,11},{10,... | collective-permute-start | bytes 3080 | tf_op jit(solution)/shard_map/ppermute | solution.py:169
  46.5 0.7 %copy-start.7 = (f32[1,256]{1,0:T(1,128)S(1)}, f32[1,256]{1,0:T(1,128)}, u32[]{:S(2)}) copy-start(f32[1,256]{1,0:T(1,128)} %get-tuple-element.15) | copy-start | bytes 3076
  46.5 7.7 %collective-permute-start.7 = (f32[1,256]{1,0:T(1,128)S(1)}, f32[1,256]{1,0:T(1,128)S(1)}, u32[]{:S(2)}, u32[]{:S(2)}) collective-permute-start(f32[1,256]{1,0:T(1,128)S(1)} %copy-done.8), channel_id=1, source_target_pairs={{0,3},{1,2},{2,1},{3,0},{4,7},{5,6},{6,5},{7,4},{8,11},{9,10},{10,... | collective-permute-start | bytes 3080 | tf_op jit(solution)/shard_map/ppermute | solution.py:169
  47.2 5.6 %copy-start.6 = (f32[1,256]{1,0:T(1,128)S(1)}, f32[1,256]{1,0:T(1,128)}, u32[]{:S(2)}) copy-start(f32[1,256]{1,0:T(1,128)} %get-tuple-element.16) | copy-start | bytes 3076
  47.2 7.0 %collective-permute-start.8 = (f32[1,256]{1,0:T(1,128)S(1)}, f32[1,256]{1,0:T(1,128)S(1)}, u32[]{:S(2)}, u32[]{:S(2)}) collective-permute-start(f32[1,256]{1,0:T(1,128)S(1)} %copy-done.7), channel_id=1, source_target_pairs={{4,0},{5,1},{6,2},{7,3},{8,12},{9,13},{10,14},{11,15},{0,8},{1,9},... | collective-permute-start | bytes 3080 | tf_op jit(solution)/shard_map/ppermute | solution.py:173
  52.9 7.3 %copy-start.5 = (f32[1,256]{1,0:T(1,128)S(1)}, f32[1,256]{1,0:T(1,128)}, u32[]{:S(2)}) copy-start(f32[1,256]{1,0:T(1,128)} %get-tuple-element.11) | copy-start | bytes 3076
  52.9 7.3 %collective-permute-start.9 = (f32[1,256]{1,0:T(1,128)S(1)}, f32[1,256]{1,0:T(1,128)S(1)}, u32[]{:S(2)}, u32[]{:S(2)}) collective-permute-start(f32[1,256]{1,0:T(1,128)S(1)} %copy-done.6), channel_id=1, source_target_pairs={{8,4},{9,5},{10,6},{11,7},{12,0},{13,1},{14,2},{15,3},{4,12},{5,13... | collective-permute-start | bytes 3080 | tf_op jit(solution)/shard_map/ppermute | solution.py:173

commit v2 on v0

--- a/solution.py
+++ b/solution.py
@@ -1,11 +1,14 @@
+import functools
+
 import jax
 import jax.numpy as jnp
 from jax import lax
+from jax.experimental import pallas as pl
+from jax.experimental.pallas import tpu as pltpu
 from jax.sharding import PartitionSpec as P
 
 CLU_DEV = 1
-
-
+PAD_MARK = 64.0
 inverse_temp = 20.0
 
 
@@ -33,7 +36,7 @@
     return jnp.log1p(mass_sum)
 
 
-def on_device(embeddings, cluster_ids):
+def plain_plan(embeddings, cluster_ids):
     peer_count = lax.axis_size("gx")
     row_count = embeddings.shape[0]
     features = embeddings.shape[1]
@@ -75,6 +78,159 @@
     return jnp.sum(jnp.where(pick_mask, flat_scores[None, :], 0.0), axis=1)
 
 
+LANES = 128
+PLANE = 4
+VMEM_BYTES = 16 * 1024 * 1024
+
+
+def along_rows(values):
+    return jnp.broadcast_to(values, (LANES, values.shape[1])).T
+
+
+def unit_rows(raw, scale):
+    features = raw.astype(jnp.float32)
+    wide = jnp.concatenate([scale] * (features.shape[1] // LANES), axis=1)
+    return (features * wide).astype(jnp.bfloat16)
+
+
+def mate_mass(query_rows, query_ids, key_rows, key_ids, same_block):
+    similar = lax.dot_general(
+        query_rows, key_rows, (((1,), (1,)), ((), ())), preferred_element_type=jnp.float32
+    )
+    repeats = similar.shape[1] // LANES
+    mates = jnp.concatenate([query_ids] * repeats, axis=1) == key_ids
+    if same_block:
+        query_pos = lax.broadcasted_iota(jnp.int32, similar.shape, 0)
+        key_pos = lax.broadcasted_iota(jnp.int32, similar.shape, 1)
+        mates = mates & (query_pos != key_pos)
+    return jnp.where(mates, jnp.exp(similar * inverse_temp), 0.0)
+
+
+def info_kernel(rows_ref, ids_ref, info_ref):
+    peers, _, width = info_ref.shape
+    rows = width // 2
+    features = rows_ref[...].astype(jnp.float32)
+    squares = jnp.sum(features * features, axis=1, keepdims=True)
+    scale = jnp.broadcast_to(lax.rsqrt(squares + 1e-06), (rows, LANES)).T[:1]
+    info = jnp.concatenate([ids_ref[...].astype(jnp.float32), scale], axis=1)
+    for peer in range(peers):
+        info_ref[peer] = info
+
+
+def plane_kernel(info_ref, *refs):
+    block_refs, (units_ref, ids_ref, mass_ref) = refs[:-3], refs[-3:]
+    rows = mass_ref.shape[1]
+    here = lax.axis_index("gx")
+    own_ids = info_ref[here][:, :rows]
+    first = 0
+    for ref in block_refs:
+        block = first // rows
+        info = info_ref[here ^ block]
+        size = ref.shape[0]
+        inside = first % rows
+        scale = along_rows(info[:, rows:])[inside : inside + size]
+        units_ref[first : first + size, :] = unit_rows(ref[...], scale)
+        first += size
+    mass = jnp.zeros((1, rows), jnp.float32)
+    for m in range(PLANE):
+        part = pl.ds(m * rows, rows)
+        query_ids = along_rows(info_ref[here ^ m][:, :rows])
+        ids_ref[part, :] = query_ids
+        masses = mate_mass(units_ref[part, :], query_ids, units_ref[:rows, :], own_ids, m == 0)
+        mass = mass + jnp.sum(masses, axis=0, keepdims=True)
+    mass_ref[...] = mass
+
+
+def line_kernel(moves, info_ref, units_ref, ids_ref, mass_ref, *refs):
+    line_refs, sums_ref, lane_sums = refs[:-2], refs[-2], refs[-1]
+    rows = mass_ref.shape[1]
+    here = lax.axis_index("gx")
+    plane, line = here // PLANE, here % PLANE
+    sums_ref[...] = jnp.zeros_like(sums_ref)
+    lane_sums[...] = jnp.zeros_like(lane_sums)
+    for line_ref, pairs in zip(line_refs, moves):
+        source = jnp.int32(-1)
+        for sender, receiver in pairs:
+            source = jnp.where(plane == receiver, sender, source)
+
+        @pl.when(source >= 0)
+        def _():
+            sender = source * PLANE + line
+            info = info_ref[sender]
+            key_ids = info[:, :rows]
+            key_rows = unit_rows(line_ref[...], along_rows(info[:, rows:]))
+            column = jnp.zeros((1, rows), jnp.float32)
+            for m in range(PLANE):
+                part = pl.ds(m * rows, rows)
+                masses = mate_mass(units_ref[part, :], ids_ref[part, :], key_rows, key_ids, False)
+                column = column + jnp.sum(masses, axis=0, keepdims=True)
+                folded = masses[:, :LANES]
+                for first in range(LANES, rows, LANES):
+                    folded = folded + masses[:, first : first + LANES]
+                lane_sums[part, :] += folded
+            sums_ref[sender] = column
+
+    for m in range(PLANE):
+        part = pl.ds(m * rows, rows)
+        row_sum = jnp.sum(lane_sums[part, :].T, axis=0, keepdims=True)
+        sums_ref[here ^ m] = mass_ref[...] + row_sum if m == 0 else row_sum
+
+
+def grid_plan(embeddings, cluster_ids):
+    peers = lax.axis_size("gx")
+    row_count, features = embeddings.shape
+    params = pltpu.CompilerParams(vmem_limit_bytes=VMEM_BYTES)
+
+    def in_plane(value, step):
+        return lax.ppermute(value, "gx", [(i, i ^ step) for i in range(peers)])
+
+    def on_line(value, moves):
+        pairs = [(a * PLANE + n, b * PLANE + n) for a, b in moves for n in range(PLANE)]
+        return lax.ppermute(value, "gx", pairs)
+
+    def to_all(value):
+        return lax.all_to_all(value, "gx", split_axis=0, concat_axis=0, tiled=True)
+
+    moves = [[(0, 1), (3, 2), (2, 0)], [(1, 2), (0, 3), (3, 1)]]
+    lines = [on_line(embeddings, pairs) for pairs in moves]
+    across = in_plane(embeddings, 2)
+    sibling = in_plane(embeddings, 1)
+    info = to_all(
+        pl.pallas_call(
+            info_kernel,
+            out_shape=jax.ShapeDtypeStruct((peers, 1, 2 * row_count), jnp.float32),
+            compiler_params=params,
+        )(embeddings, cluster_ids.reshape(1, row_count))
+    )
+    across, info = lax.optimization_barrier((across, info))
+    cut = row_count // 2
+    corner = [in_plane(part, 1) for part in (across[:cut], across[cut:])]
+    plane_rows = PLANE * row_count
+    units, ids, mass = pl.pallas_call(
+        plane_kernel,
+        out_shape=(
+            jax.ShapeDtypeStruct((plane_rows, features), jnp.bfloat16),
+            jax.ShapeDtypeStruct((plane_rows, LANES), jnp.float32),
+            jax.ShapeDtypeStruct((1, row_count), jnp.float32),
+        ),
+        cost_estimate=pl.CostEstimate(flops=1, bytes_accessed=1, transcendentals=0),
+        compiler_params=params,
+    )(info, embeddings, sibling, across, *corner)
+    sums = pl.pallas_call(
+        functools.partial(line_kernel, moves),
+        out_shape=jax.ShapeDtypeStruct((peers, 1, row_count), jnp.float32),
+        scratch_shapes=[pltpu.VMEM((plane_rows, LANES), jnp.float32)],
+        compiler_params=params,
+    )(info, units, ids, mass, *lines)
+    return jnp.log1p(jnp.sum(to_all(sums), axis=0)).reshape(row_count)
+
+
+def on_device(embeddings, cluster_ids):
+    if lax.axis_size("gx") == 4 * PLANE and embeddings.shape[0] % (2 * LANES) == 0:
+        return grid_plan(embeddings, cluster_ids)
+    return plain_plan(embeddings, cluster_ids)
+
+
 def solution(mesh):
     in_specs = (P(("parts", "gx"), None), P(("parts", "gx")))
     out_specs = P(("parts", "gx"))

time: 72.2 us -> 55 us (0.76)
  waiting for transfers between devices: 33 us -> 16.2 us
  matrix products: 6.13 us -> 0 us
  starting transfers between devices: 11.1 us -> 16.8 us
  other arithmetic: 4.27 us -> 0.04 us
  Pallas kernels: 0 us -> 3.08 us
  local copies, waits for them, and re-layouts: 1.94 us -> 3.41 us
    all_to_all x2 -> x1, waiting for transfers between devices: 33 us -> 0.01 us  [to_all(): return lax.all_to_all(value, 'gx', split_axis=0, concat_axis=0, tiled=True)]
    ppermute x0 -> x6, waiting for transfers between devices: none -> 16.2 us  [the longest x2 14.8 us: on_line(): return lax.ppermute(value, 'gx', pairs)]
    ppermute x0 -> x6, starting transfers between devices: none -> 11.8 us  [the longest x2 7.91 us: on_line(): return lax.ppermute(value, 'gx', pairs)]
    dot_general x5 -> x0, matrix products: 6.13 us -> none  [the longest x1 2.86 us: on_device(): jnp.dot(select_mask.astype(jnp.bfloat16), unit_rows, preferred_element_ty...]
    all_to_all x2 -> x1, starting transfers between devices: 11.1 us -> 4.98 us  [to_all(): return lax.all_to_all(value, 'gx', split_axis=0, concat_axis=0, tiled=True)]
    pallas_call x0 -> x3, Pallas kernels: none -> 3.08 us  [the longest x1 1.22 us: grid_plan(): pl.pallas_call(functools.partial(line_kernel, moves), out_shape=jax.Shape...]
    unnamed x0 -> x6, local copies, waits for them, and re-layouts: none -> 2.79 us
    reduce_sum x3 -> x1, other arithmetic: 2.19 us -> 0.04 us  [grid_plan(): return jnp.log1p(jnp.sum(to_all(sums), axis=0)).reshape(row_count)]
  transfers between devices with their start and end apart: 2 -> 7, of which waited for: 2 -> 4; matrix products, arithmetic and copies ran while one was open for 7% -> 0% of each run, Pallas kernels for 0% -> 3%
where the time goes in v2:
time: 55 us; the launch traced here: 54.6 us
  starting transfers between devices  16.8 us (31%)
  waiting for transfers between devices  16.2 us (29%)
  blocking collectives  15 us (27%)
  local copies, waits for them, and re-layouts  3.41 us (6%)
  Pallas kernels  3.08 us (6%)
    all_to_all x1, blocking collectives, to_all(): return lax.all_to_all(value, 'gx', split_axis=0, concat_axis=0, tiled=True)  15 us
    ppermute x2, waiting for transfers between devices, on_line(): return lax.ppermute(value, 'gx', pairs)  14.8 us
    ppermute x2, starting transfers between devices, on_line(): return lax.ppermute(value, 'gx', pairs)  7.91 us
    all_to_all x1, starting transfers between devices, to_all(): return lax.all_to_all(value, 'gx', split_axis=0, concat_axis=0, tiled=True)  4.98 us
    ppermute x4, starting transfers between devices, in_plane(): return lax.ppermute(value, 'gx', [(i, i ^ step) for i in range(peers)])  3.92 us
    unnamed x6, local copies, waits for them, and re-layouts  2.79 us
    ppermute x4, waiting for transfers between devices, in_plane(): return lax.ppermute(value, 'gx', [(i, i ^ step) for i in range(peers)])  1.4 us
    pallas_call x1, Pallas kernels, grid_plan(): pl.pallas_call(functools.partial(line_kernel, moves), out_shape=jax.Shape...  1.22 us
  transfers between devices with their start and end apart: 7, of which 4 were waited for; matrix products, arithmetic and copies ran while one was open for 0% of the time, Pallas kernels for 3%

profile of v2, /device:TPU:0, one launch (start us, length us, event | category | flops | bytes accessed | tf_op | source)
XLA Modules:
  0.0 54.6 jit_solution(9194228718317235316)
XLA Ops:
  0.0 2.9 %collective-permute-start = (bf16[256,1024]{1,0:T(8,128)(2,1)}, bf16[256,1024]{1,0:T(8,128)(2,1)S(1)}, u32[]{:S(2)}, u32[]{:S(2)}) collective-permute-start(bf16[256,1024]{1,0:T(8,128)(2,1)} %refs_0_.1), channel_id=1, source_target_pairs={{0,2},{1,3},{2,0},{3,1},{4,6},{5,7},{6,4},{7,5},{8,10},{9,11},{10,... | collective-permute-start | bytes 1572872 | tf_op jit(solution)/shard_map/ppermute | solution.py:185
  2.9 0.0 copy-start
  2.9 1.1 %copy-done = bf16[256,1024]{1,0:T(8,128)(2,1)S(1)} copy-done((bf16[256,1024]{1,0:T(8,128)(2,1)S(1)}, bf16[256,1024]{1,0:T(8,128)(2,1)}, u32[]{:S(2)}) %copy-start) | copy-done | bytes 524312
  4.0 0.0 copy-start.2
  4.0 0.7 %copy-done.2 = s32[256]{0:T(256)S(1)} copy-done((s32[256]{0:T(256)S(1)}, s32[256]{0:T(256)}, u32[]{:S(2)}) %copy-start.2) | copy-done | bytes 1048
  4.7 0.8 %shard_map.28 = f32[16,1,512]{2,1,0:T(1,128)} custom-call(bf16[256,1024]{1,0:T(8,128)(2,1)S(1)} %copy-done, s32[1,256]{1,0:T(1,128)S(1)} %bitcast.1), custom_call_target="tpu_custom_call" | custom-call | tf_op jit(solution)/shard_map/pallas_call | solution.py:199
  5.5 5.0 %all-to-all-start = ((f32[16,1,512]{2,1,0:T(1,128)}), f32[16,1,512]{2,1,0:T(1,128)S(1)}, u32[]{:S(2)}, u32[]{:S(2)}) async-start(f32[16,1,512]{2,1,0:T(1,128)} %shard_map.28), calls=%async_computation | async-start | bytes 65536 | tf_op jit(solution)/shard_map/all_to_all | solution.py:192
  10.5 0.4 collective-permute-start.1
  10.9 3.6 %collective-permute-start.4 = (bf16[256,1024]{1,0:T(8,128)(2,1)}, bf16[256,1024]{1,0:T(8,128)(2,1)S(1)}, u32[]{:S(2)}, u32[]{:S(2)}) collective-permute-start(bf16[256,1024]{1,0:T(8,128)(2,1)} %refs_0_.1), channel_id=1, source_target_pairs={{0,4},{1,5},{2,6},{3,7},{12,8},{13,9},{14,10},{15,11},{8,0},{9,1},... | collective-permute-start | bytes 1572872 | tf_op jit(solution)/shard_map/ppermute | solution.py:189
  14.5 4.3 %collective-permute-start.5 = (bf16[256,1024]{1,0:T(8,128)(2,1)}, bf16[256,1024]{1,0:T(8,128)(2,1)S(1)}, u32[]{:S(2)}, u32[]{:S(2)}) collective-permute-start(bf16[256,1024]{1,0:T(8,128)(2,1)} %refs_0_.1), channel_id=1, source_target_pairs={{4,8},{5,9},{6,10},{7,11},{0,12},{1,13},{2,14},{3,15},{12,4},{13,5... | collective-permute-start | bytes 1572872 | tf_op jit(solution)/shard_map/ppermute | solution.py:189
  18.9 0.0 all-to-all-done.info_ref
  18.9 0.0 collective-permute-done.refs_2_
  18.9 0.1 collective-permute-start.2
  19.0 0.5 collective-permute-start.3
  19.5 0.0 collective-permute-done.1.refs_1_
  19.5 1.0 %collective-permute-done.2.refs_3_ = bf16[128,1024]{1,0:T(8,128)(2,1)S(1)} collective-permute-done((bf16[128,1024]{1,0:T(8,128)(2,1)S(1)}, bf16[128,1024]{1,0:T(8,128)(2,1)S(1)}, u32[]{:S(2)}, u32[]{:S(2)}) %collective-permute-start.2) | collective-permute-done | bytes 262176 | tf_op jit(solution)/shard_map/ppermute | solution.py:185
  20.5 0.4 collective-permute-done.3.refs_4_
  20.9 0.0 copy-start.1
  20.9 1.0 %copy-done.1 = bf16[256,1024]{1,0:T(8,128)(2,1)S(1)} copy-done((bf16[256,1024]{1,0:T(8,128)(2,1)S(1)}, bf16[256,1024]{1,0:T(8,128)(2,1)}, u32[]{:S(2)}) %copy-start.1) | copy-done | bytes 524312
  21.9 1.0 %shard_map.29 = (bf16[1024,1024]{1,0:T(8,128)(2,1)S(1)}, f32[1024,128]{1,0:T(8,128)S(1)}, f32[1,256]{1,0:T(1,128)S(1)}) custom-call(f32[16,1,512]{2,1,0:T(1,128)S(1)} %all-to-all-done.info_ref, bf16[256,1024]{1,0:T(8,128)(2,1)S(1)} %copy-done.1, bf16[256,1024]{1,0:T(8,128)(2,1)S(1)} %collective-permute-done.1.refs_1_, ...), custom_call_target="tpu_custom_call" | custom-call | flops 1 | bytes 1 | tf_op jit(solution)/shard_map/pallas_call | solution.py:209
  23.0 5.1 %collective-permute-done.4.refs_0_ = bf16[256,1024]{1,0:T(8,128)(2,1)S(1)} collective-permute-done((bf16[256,1024]{1,0:T(8,128)(2,1)}, bf16[256,1024]{1,0:T(8,128)(2,1)S(1)}, u32[]{:S(2)}, u32[]{:S(2)}) %collective-permute-start.4) | collective-permute-done | bytes 524320 | tf_op jit(solution)/shard_map/ppermute | solution.py:189
  28.1 9.7 %collective-permute-done.5.refs_1_ = bf16[256,1024]{1,0:T(8,128)(2,1)S(1)} collective-permute-done((bf16[256,1024]{1,0:T(8,128)(2,1)}, bf16[256,1024]{1,0:T(8,128)(2,1)S(1)}, u32[]{:S(2)}, u32[]{:S(2)}) %collective-permute-start.5) | collective-permute-done | bytes 524320 | tf_op jit(solution)/shard_map/ppermute | solution.py:189
  37.8 1.2 %shard_map.30 = f32[16,1,256]{2,1,0:T(1,128)S(1)} custom-call(f32[16,1,512]{2,1,0:T(1,128)S(1)} %all-to-all-done.info_ref, bf16[1024,1024]{1,0:T(8,128)(2,1)S(1)} %get-tuple-element.12.units_ref, f32[1024,128]{1,0:T(8,128)S(1)} %get-tuple-element.13.ids_ref, f32[1,256]{1,0:T(1,128)S(1)} %get-tuple-element.14.mass_ref, ...), custom_call_target="tpu_custom_call" | custom-call | tf_op jit(solution)/shard_map/pallas_call | solution.py:219
  39.0 15.0 %all_to_all.10 = f32[16,1,256]{2,1,0:T(1,128)S(1)} all-to-all(f32[16,1,256]{2,1,0:T(1,128)S(1)} %shard_map.30), channel_id=1, replica_groups=mesh['parts'=2,'gx'=16] {'gx'}, dimensions={0} | all-to-all | bytes 32768 | tf_op jit(solution)/shard_map/all_to_all | solution.py:192
  54.0 0.6 %log1p.6 = f32[256]{0:T(256)} log-plus-one(f32[256]{0:T(256)S(1)} %reduce_sum.9) | non-fusion elementwise | bytes 2048 | tf_op jit(solution)/shard_map/log1p | solution.py:225
  (2 shorter events, 0.1 us)
Async XLA Ops:
  0.0 18.9 %collective-permute-start = (bf16[256,1024]{1,0:T(8,128)(2,1)}, bf16[256,1024]{1,0:T(8,128)(2,1)S(1)}, u32[]{:S(2)}, u32[]{:S(2)}) collective-permute-start(bf16[256,1024]{1,0:T(8,128)(2,1)} %refs_0_.1), channel_id=1, source_target_pairs={{0,2},{1,3},{2,0},{3,1},{4,6},{5,7},{6,4},{7,5},{8,10},{9,11},{10,... | collective-permute-start | bytes 1572872 | tf_op jit(solution)/shard_map/ppermute | solution.py:185
  2.9 1.1 %copy-start = (bf16[256,1024]{1,0:T(8,128)(2,1)S(1)}, bf16[256,1024]{1,0:T(8,128)(2,1)}, u32[]{:S(2)}) copy-start(bf16[256,1024]{1,0:T(8,128)(2,1)} %refs_0_.1) | copy-start | bytes 1572868
  4.0 0.7 %copy-start.2 = (s32[256]{0:T(256)S(1)}, s32[256]{0:T(256)}, u32[]{:S(2)}) copy-start(s32[256]{0:T(256)} %param.3) | copy-start | bytes 3076
  5.5 13.3 %all-to-all-start = ((f32[16,1,512]{2,1,0:T(1,128)}), f32[16,1,512]{2,1,0:T(1,128)S(1)}, u32[]{:S(2)}, u32[]{:S(2)}) async-start(f32[16,1,512]{2,1,0:T(1,128)} %shard_map.28), calls=%async_computation | async-start | bytes 65536 | tf_op jit(solution)/shard_map/all_to_all | solution.py:192
  10.5 9.0 %collective-permute-start.1 = (bf16[256,1024]{1,0:T(8,128)(2,1)}, bf16[256,1024]{1,0:T(8,128)(2,1)S(1)}, u32[]{:S(2)}, u32[]{:S(2)}) collective-permute-start(bf16[256,1024]{1,0:T(8,128)(2,1)} %refs_0_.1), channel_id=1, source_target_pairs={{0,1},{1,0},{2,3},{3,2},{4,5},{5,4},{6,7},{7,6},{8,9},{9,8},{10,11... | collective-permute-start | bytes 1572872 | tf_op jit(solution)/shard_map/ppermute | solution.py:185
  10.9 17.1 %collective-permute-start.4 = (bf16[256,1024]{1,0:T(8,128)(2,1)}, bf16[256,1024]{1,0:T(8,128)(2,1)S(1)}, u32[]{:S(2)}, u32[]{:S(2)}) collective-permute-start(bf16[256,1024]{1,0:T(8,128)(2,1)} %refs_0_.1), channel_id=1, source_target_pairs={{0,4},{1,5},{2,6},{3,7},{12,8},{13,9},{14,10},{15,11},{8,0},{9,1},... | collective-permute-start | bytes 1572872 | tf_op jit(solution)/shard_map/ppermute | solution.py:189
  14.5 23.3 %collective-permute-start.5 = (bf16[256,1024]{1,0:T(8,128)(2,1)}, bf16[256,1024]{1,0:T(8,128)(2,1)S(1)}, u32[]{:S(2)}, u32[]{:S(2)}) collective-permute-start(bf16[256,1024]{1,0:T(8,128)(2,1)} %refs_0_.1), channel_id=1, source_target_pairs={{4,8},{5,9},{6,10},{7,11},{0,12},{1,13},{2,14},{3,15},{12,4},{13,5... | collective-permute-start | bytes 1572872 | tf_op jit(solution)/shard_map/ppermute | solution.py:189
  18.9 1.6 %collective-permute-start.2 = (bf16[128,1024]{1,0:T(8,128)(2,1)S(1)}, bf16[128,1024]{1,0:T(8,128)(2,1)S(1)}, u32[]{:S(2)}, u32[]{:S(2)}) collective-permute-start(bf16[128,1024]{1,0:T(8,128)(2,1)S(1)} %get-tuple-element.16), channel_id=1, source_target_pairs={{0,1},{1,0},{2,3},{3,2},{4,5},{5,4},{6,7},{7,6},{8,9},{9,8},{10,11... | collective-permute-start | bytes 786440 | tf_op jit(solution)/shard_map/ppermute | solution.py:185
  19.0 1.9 %collective-permute-start.3 = (bf16[128,1024]{1,0:T(8,128)(2,1)S(1)}, bf16[128,1024]{1,0:T(8,128)(2,1)S(1)}, u32[]{:S(2)}, u32[]{:S(2)}) collective-permute-start(bf16[128,1024]{1,0:T(8,128)(2,1)S(1)} %get-tuple-element.15), channel_id=1, source_target_pairs={{0,1},{1,0},{2,3},{3,2},{4,5},{5,4},{6,7},{7,6},{8,9},{9,8},{10,11... | collective-permute-start | bytes 786440 | tf_op jit(solution)/shard_map/ppermute | solution.py:185
  20.9 1.0 %copy-start.1 = (bf16[256,1024]{1,0:T(8,128)(2,1)S(1)}, bf16[256,1024]{1,0:T(8,128)(2,1)}, u32[]{:S(2)}) copy-start(bf16[256,1024]{1,0:T(8,128)(2,1)} %refs_0_.1) | copy-start | bytes 1572868

commit v3 on v2

--- a/solution.py
+++ b/solution.py
@@ -195,16 +195,15 @@
     lines = [on_line(embeddings, pairs) for pairs in moves]
     across = in_plane(embeddings, 2)
     sibling = in_plane(embeddings, 1)
+    across, rows, row_ids = lax.optimization_barrier((across, embeddings, cluster_ids))
     info = to_all(
         pl.pallas_call(
             info_kernel,
             out_shape=jax.ShapeDtypeStruct((peers, 1, 2 * row_count), jnp.float32),
             compiler_params=params,
-        )(embeddings, cluster_ids.reshape(1, row_count))
-    )
-    across, info = lax.optimization_barrier((across, info))
-    cut = row_count // 2
-    corner = [in_plane(part, 1) for part in (across[:cut], across[cut:])]
+        )(rows, row_ids.reshape(1, row_count))
+    )
+    corner = [in_plane(part, 1) for part in jnp.split(across, 2)]
     plane_rows = PLANE * row_count
     units, ids, mass = pl.pallas_call(
         plane_kernel,

time: 55 us -> 49.6 us (0.902)
  waiting for transfers between devices: 16.2 us -> 13 us
  blocking collectives: 15 us -> 12.1 us
  starting transfers between devices: 16.8 us -> 17.6 us
    ppermute x2, waiting for transfers between devices: 14.8 us -> 0.01 us  [on_line(): return lax.ppermute(value, 'gx', pairs)]
    all_to_all x1, waiting for transfers between devices: 0.01 us -> 8.74 us  [to_all(): return lax.all_to_all(value, 'gx', split_axis=0, concat_axis=0, tiled=True)]
    all_to_all x1, blocking collectives: 15 us -> 12.1 us  [to_all(): return lax.all_to_all(value, 'gx', split_axis=0, concat_axis=0, tiled=True)]
    ppermute x4, waiting for transfers between devices: 1.4 us -> 4.2 us  [in_plane(): return lax.ppermute(value, 'gx', [(i, i ^ step) for i in range(peers)])]
    all_to_all x1, starting transfers between devices: 4.98 us -> 6.16 us  [to_all(): return lax.all_to_all(value, 'gx', split_axis=0, concat_axis=0, tiled=True)]
  transfers between devices with their start and end apart: 7 -> 7, of which waited for: 4 -> 2; matrix products, arithmetic and copies ran while one was open for 0% -> 0% of each run, Pallas kernels for 3% -> 4%
where the time goes in v3:
time: 49.6 us; the launch traced here: 49.2 us
  starting transfers between devices  17.6 us (35%)
  waiting for transfers between devices  13 us (26%)
  blocking collectives  12.1 us (24%)
  local copies, waits for them, and re-layouts  3.37 us (7%)
  Pallas kernels  3.1 us (6%)
    all_to_all x1, blocking collectives, to_all(): return lax.all_to_all(value, 'gx', split_axis=0, concat_axis=0, tiled=True)  12.1 us
    all_to_all x1, waiting for transfers between devices, to_all(): return lax.all_to_all(value, 'gx', split_axis=0, concat_axis=0, tiled=True)  8.74 us
    ppermute x2, starting transfers between devices, on_line(): return lax.ppermute(value, 'gx', pairs)  7.92 us
    all_to_all x1, starting transfers between devices, to_all(): return lax.all_to_all(value, 'gx', split_axis=0, concat_axis=0, tiled=True)  6.16 us
    ppermute x4, waiting for transfers between devices, in_plane(): return lax.ppermute(value, 'gx', [(i, i ^ step) for i in range(peers)])  4.2 us
    ppermute x4, starting transfers between devices, in_plane(): return lax.ppermute(value, 'gx', [(i, i ^ step) for i in range(peers)])  3.51 us
    unnamed x6, local copies, waits for them, and re-layouts  2.76 us
    pallas_call x1, Pallas kernels, grid_plan(): pl.pallas_call(functools.partial(line_kernel, moves), out_shape=jax.Shape...  1.22 us
  transfers between devices with their start and end apart: 7, of which 2 were waited for; matrix products, arithmetic and copies ran while one was open for 0% of the time, Pallas kernels for 4%

profile of v3, /device:TPU:0, one launch (start us, length us, event | category | flops | bytes accessed | tf_op | source)
XLA Modules:
  0.0 49.2 jit_solution(4820624604649551801)
XLA Ops:
  0.0 2.9 %collective-permute-start = (bf16[256,1024]{1,0:T(8,128)(2,1)}, bf16[256,1024]{1,0:T(8,128)(2,1)S(1)}, u32[]{:S(2)}, u32[]{:S(2)}) collective-permute-start(bf16[256,1024]{1,0:T(8,128)(2,1)} %refs_0_.1), channel_id=1, source_target_pairs={{0,2},{1,3},{2,0},{3,1},{4,6},{5,7},{6,4},{7,5},{8,10},{9,11},{10,... | collective-permute-start | bytes 1572872 | tf_op jit(solution)/shard_map/ppermute | solution.py:185
  2.9 0.0 collective-permute-start.1
  2.9 3.5 %collective-permute-start.4 = (bf16[256,1024]{1,0:T(8,128)(2,1)}, bf16[256,1024]{1,0:T(8,128)(2,1)S(1)}, u32[]{:S(2)}, u32[]{:S(2)}) collective-permute-start(bf16[256,1024]{1,0:T(8,128)(2,1)} %refs_0_.1), channel_id=1, source_target_pairs={{0,4},{1,5},{2,6},{3,7},{12,8},{13,9},{14,10},{15,11},{8,0},{9,1},... | collective-permute-start | bytes 1572872 | tf_op jit(solution)/shard_map/ppermute | solution.py:189
  6.4 4.4 %collective-permute-start.5 = (bf16[256,1024]{1,0:T(8,128)(2,1)}, bf16[256,1024]{1,0:T(8,128)(2,1)S(1)}, u32[]{:S(2)}, u32[]{:S(2)}) collective-permute-start(bf16[256,1024]{1,0:T(8,128)(2,1)} %refs_0_.1), channel_id=1, source_target_pairs={{4,8},{5,9},{6,10},{7,11},{0,12},{1,13},{2,14},{3,15},{12,4},{13,5... | collective-permute-start | bytes 1572872 | tf_op jit(solution)/shard_map/ppermute | solution.py:189
  10.9 4.2 %collective-permute-done.refs_2_ = bf16[256,1024]{1,0:T(8,128)(2,1)S(1)} collective-permute-done((bf16[256,1024]{1,0:T(8,128)(2,1)}, bf16[256,1024]{1,0:T(8,128)(2,1)S(1)}, u32[]{:S(2)}, u32[]{:S(2)}) %collective-permute-start) | collective-permute-done | bytes 524320 | tf_op jit(solution)/shard_map/ppermute | solution.py:185
  15.1 0.1 collective-permute-start.2
  15.2 0.5 %collective-permute-start.3 = (bf16[128,1024]{1,0:T(8,128)(2,1)S(1)}, bf16[128,1024]{1,0:T(8,128)(2,1)S(1)}, u32[]{:S(2)}, u32[]{:S(2)}) collective-permute-start(bf16[128,1024]{1,0:T(8,128)(2,1)S(1)} %get-tuple-element.17), channel_id=1, source_target_pairs={{0,1},{1,0},{2,3},{3,2},{4,5},{5,4},{6,7},{7,6},{8,9},{9,8},{10,11... | collective-permute-start | bytes 786440 | tf_op jit(solution)/shard_map/ppermute | solution.py:185
  15.7 0.0 copy-start
  15.7 1.0 %copy-done = bf16[256,1024]{1,0:T(8,128)(2,1)S(1)} copy-done((bf16[256,1024]{1,0:T(8,128)(2,1)S(1)}, bf16[256,1024]{1,0:T(8,128)(2,1)}, u32[]{:S(2)}) %copy-start) | copy-done | bytes 524312
  16.7 0.0 copy-start.2
  16.7 0.7 %copy-done.2 = s32[256]{0:T(256)S(1)} copy-done((s32[256]{0:T(256)S(1)}, s32[256]{0:T(256)}, u32[]{:S(2)}) %copy-start.2) | copy-done | bytes 1048
  17.4 0.8 %shard_map.28 = f32[16,1,512]{2,1,0:T(1,128)} custom-call(bf16[256,1024]{1,0:T(8,128)(2,1)S(1)} %copy-done, s32[1,256]{1,0:T(1,128)S(1)} %bitcast.1), custom_call_target="tpu_custom_call" | custom-call | tf_op jit(solution)/shard_map/pallas_call | solution.py:200
  18.3 6.2 %all-to-all-start = ((f32[16,1,512]{2,1,0:T(1,128)}), f32[16,1,512]{2,1,0:T(1,128)S(1)}, u32[]{:S(2)}, u32[]{:S(2)}) async-start(f32[16,1,512]{2,1,0:T(1,128)} %shard_map.28), calls=%async_computation | async-start | bytes 65536 | tf_op jit(solution)/shard_map/all_to_all | solution.py:192
  24.4 0.0 collective-permute-done.1.refs_1_
  24.4 8.7 %all-to-all-done.info_ref = f32[16,1,512]{2,1,0:T(1,128)S(1)} async-done(((f32[16,1,512]{2,1,0:T(1,128)}), f32[16,1,512]{2,1,0:T(1,128)S(1)}, u32[]{:S(2)}, u32[]{:S(2)}) %all-to-all-start) | async-done | bytes 32800 | tf_op jit(solution)/shard_map/all_to_all | solution.py:192
  33.2 0.0 collective-permute-done.2.refs_3_
  33.2 0.0 collective-permute-done.3.refs_4_
  33.2 0.0 copy-start.1
  33.2 1.0 %copy-done.1 = bf16[256,1024]{1,0:T(8,128)(2,1)S(1)} copy-done((bf16[256,1024]{1,0:T(8,128)(2,1)S(1)}, bf16[256,1024]{1,0:T(8,128)(2,1)}, u32[]{:S(2)}) %copy-start.1) | copy-done | bytes 524312
  34.2 1.0 %shard_map.29 = (bf16[1024,1024]{1,0:T(8,128)(2,1)S(1)}, f32[1024,128]{1,0:T(8,128)S(1)}, f32[1,256]{1,0:T(1,128)S(1)}) custom-call(f32[16,1,512]{2,1,0:T(1,128)S(1)} %all-to-all-done.info_ref, bf16[256,1024]{1,0:T(8,128)(2,1)S(1)} %copy-done.1, bf16[256,1024]{1,0:T(8,128)(2,1)S(1)} %collective-permute-done.1.refs_1_, ...), custom_call_target="tpu_custom_call" | custom-call | flops 1 | bytes 1 | tf_op jit(solution)/shard_map/pallas_call | solution.py:208
  35.3 0.0 collective-permute-done.4.refs_0_
  35.3 0.0 collective-permute-done.5.refs_1_
  35.3 1.2 %shard_map.30 = f32[16,1,256]{2,1,0:T(1,128)S(1)} custom-call(f32[16,1,512]{2,1,0:T(1,128)S(1)} %all-to-all-done.info_ref, bf16[1024,1024]{1,0:T(8,128)(2,1)S(1)} %get-tuple-element.14.units_ref, f32[1024,128]{1,0:T(8,128)S(1)} %get-tuple-element.15.ids_ref, f32[1,256]{1,0:T(1,128)S(1)} %get-tuple-element.16.mass_ref, ...), custom_call_target="tpu_custom_call" | custom-call | tf_op jit(solution)/shard_map/pallas_call | solution.py:218
  36.5 12.1 %all_to_all.10 = f32[16,1,256]{2,1,0:T(1,128)S(1)} all-to-all(f32[16,1,256]{2,1,0:T(1,128)S(1)} %shard_map.30), channel_id=1, replica_groups=mesh['parts'=2,'gx'=16] {'gx'}, dimensions={0} | all-to-all | bytes 32768 | tf_op jit(solution)/shard_map/all_to_all | solution.py:192
  48.7 0.6 %log1p.6 = f32[256]{0:T(256)} log-plus-one(f32[256]{0:T(256)S(1)} %reduce_sum.9) | non-fusion elementwise | bytes 2048 | tf_op jit(solution)/shard_map/log1p | solution.py:224
  (2 shorter events, 0.1 us)
Async XLA Ops:
  0.0 15.1 %collective-permute-start = (bf16[256,1024]{1,0:T(8,128)(2,1)}, bf16[256,1024]{1,0:T(8,128)(2,1)S(1)}, u32[]{:S(2)}, u32[]{:S(2)}) collective-permute-start(bf16[256,1024]{1,0:T(8,128)(2,1)} %refs_0_.1), channel_id=1, source_target_pairs={{0,2},{1,3},{2,0},{3,1},{4,6},{5,7},{6,4},{7,5},{8,10},{9,11},{10,... | collective-permute-start | bytes 1572872 | tf_op jit(solution)/shard_map/ppermute | solution.py:185
  2.9 21.5 %collective-permute-start.1 = (bf16[256,1024]{1,0:T(8,128)(2,1)}, bf16[256,1024]{1,0:T(8,128)(2,1)S(1)}, u32[]{:S(2)}, u32[]{:S(2)}) collective-permute-start(bf16[256,1024]{1,0:T(8,128)(2,1)} %refs_0_.1), channel_id=1, source_target_pairs={{0,1},{1,0},{2,3},{3,2},{4,5},{5,4},{6,7},{7,6},{8,9},{9,8},{10,11... | collective-permute-start | bytes 1572872 | tf_op jit(solution)/shard_map/ppermute | solution.py:185
  2.9 32.3 %collective-permute-start.4 = (bf16[256,1024]{1,0:T(8,128)(2,1)}, bf16[256,1024]{1,0:T(8,128)(2,1)S(1)}, u32[]{:S(2)}, u32[]{:S(2)}) collective-permute-start(bf16[256,1024]{1,0:T(8,128)(2,1)} %refs_0_.1), channel_id=1, source_target_pairs={{0,4},{1,5},{2,6},{3,7},{12,8},{13,9},{14,10},{15,11},{8,0},{9,1},... | collective-permute-start | bytes 1572872 | tf_op jit(solution)/shard_map/ppermute | solution.py:189
  6.4 28.9 %collective-permute-start.5 = (bf16[256,1024]{1,0:T(8,128)(2,1)}, bf16[256,1024]{1,0:T(8,128)(2,1)S(1)}, u32[]{:S(2)}, u32[]{:S(2)}) collective-permute-start(bf16[256,1024]{1,0:T(8,128)(2,1)} %refs_0_.1), channel_id=1, source_target_pairs={{4,8},{5,9},{6,10},{7,11},{0,12},{1,13},{2,14},{3,15},{12,4},{13,5... | collective-permute-start | bytes 1572872 | tf_op jit(solution)/shard_map/ppermute | solution.py:189
  15.1 18.1 %collective-permute-start.2 = (bf16[128,1024]{1,0:T(8,128)(2,1)S(1)}, bf16[128,1024]{1,0:T(8,128)(2,1)S(1)}, u32[]{:S(2)}, u32[]{:S(2)}) collective-permute-start(bf16[128,1024]{1,0:T(8,128)(2,1)S(1)} %get-tuple-element.18), channel_id=1, source_target_pairs={{0,1},{1,0},{2,3},{3,2},{4,5},{5,4},{6,7},{7,6},{8,9},{9,8},{10,11... | collective-permute-start | bytes 786440 | tf_op jit(solution)/shard_map/ppermute | solution.py:185
  15.2 18.0 %collective-permute-start.3 = (bf16[128,1024]{1,0:T(8,128)(2,1)S(1)}, bf16[128,1024]{1,0:T(8,128)(2,1)S(1)}, u32[]{:S(2)}, u32[]{:S(2)}) collective-permute-start(bf16[128,1024]{1,0:T(8,128)(2,1)S(1)} %get-tuple-element.17), channel_id=1, source_target_pairs={{0,1},{1,0},{2,3},{3,2},{4,5},{5,4},{6,7},{7,6},{8,9},{9,8},{10,11... | collective-permute-start | bytes 786440 | tf_op jit(solution)/shard_map/ppermute | solution.py:185
  15.7 1.0 %copy-start = (bf16[256,1024]{1,0:T(8,128)(2,1)S(1)}, bf16[256,1024]{1,0:T(8,128)(2,1)}, u32[]{:S(2)}) copy-start(bf16[256,1024]{1,0:T(8,128)(2,1)} %refs_0_.1) | copy-start | bytes 1572868
  16.7 0.7 %copy-start.2 = (s32[256]{0:T(256)S(1)}, s32[256]{0:T(256)}, u32[]{:S(2)}) copy-start(s32[256]{0:T(256)} %param.3) | copy-start | bytes 3076
  18.3 14.9 %all-to-all-start = ((f32[16,1,512]{2,1,0:T(1,128)}), f32[16,1,512]{2,1,0:T(1,128)S(1)}, u32[]{:S(2)}, u32[]{:S(2)}) async-start(f32[16,1,512]{2,1,0:T(1,128)} %shard_map.28), calls=%async_computation | async-start | bytes 65536 | tf_op jit(solution)/shard_map/all_to_all | solution.py:192
  33.2 1.0 %copy-start.1 = (bf16[256,1024]{1,0:T(8,128)(2,1)S(1)}, bf16[256,1024]{1,0:T(8,128)(2,1)}, u32[]{:S(2)}) copy-start(bf16[256,1024]{1,0:T(8,128)(2,1)} %refs_0_.1) | copy-start | bytes 1572868

commit v4 on v0

--- a/solution.py
+++ b/solution.py
@@ -1,11 +1,14 @@
+import functools
+
 import jax
 import jax.numpy as jnp
 from jax import lax
+from jax.experimental import pallas as pl
+from jax.experimental.pallas import tpu as pltpu
 from jax.sharding import PartitionSpec as P
 
 CLU_DEV = 1
-
-
+PAD_MARK = 64.0
 inverse_temp = 20.0
 
 
@@ -33,7 +36,7 @@
     return jnp.log1p(mass_sum)
 
 
-def on_device(embeddings, cluster_ids):
+def plain_plan(embeddings, cluster_ids):
     peer_count = lax.axis_size("gx")
     row_count = embeddings.shape[0]
     features = embeddings.shape[1]
@@ -75,6 +78,166 @@
     return jnp.sum(jnp.where(pick_mask, flat_scores[None, :], 0.0), axis=1)
 
 
+LANES = 128
+PLANE = 4
+VMEM_BYTES = 16 * 1024 * 1024
+
+
+def along_rows(values):
+    return jnp.broadcast_to(values, (LANES, values.shape[1])).T
+
+
+def unit_rows(raw, scale):
+    features = raw.astype(jnp.float32)
+    wide = jnp.concatenate([scale] * (features.shape[1] // LANES), axis=1)
+    return (features * wide).astype(jnp.bfloat16)
+
+
+def mate_mass(query_rows, query_ids, key_rows, key_ids, same_block):
+    similar = lax.dot_general(
+        query_rows, key_rows, (((1,), (1,)), ((), ())), preferred_element_type=jnp.float32
+    )
+    repeats = similar.shape[1] // LANES
+    mates = jnp.concatenate([query_ids] * repeats, axis=1) == key_ids
+    if same_block:
+        query_pos = lax.broadcasted_iota(jnp.int32, similar.shape, 0)
+        key_pos = lax.broadcasted_iota(jnp.int32, similar.shape, 1)
+        mates = mates & (query_pos != key_pos)
+    return jnp.where(mates, jnp.exp(similar * inverse_temp), 0.0)
+
+
+def info_kernel(rows_ref, ids_ref, info_ref):
+    rows = rows_ref.shape[0]
+    features = rows_ref[...].astype(jnp.float32)
+    squares = jnp.sum(features * features, axis=1, keepdims=True)
+    scale = jnp.broadcast_to(lax.rsqrt(squares + 1e-06), (rows, LANES)).T[:1]
+    info_ref[:, :rows] = ids_ref[...].astype(jnp.float32)
+    info_ref[:, rows:] = scale
+
+
+def plane_kernel(*refs):
+    info_refs, block_refs = refs[:PLANE], refs[PLANE:-3]
+    units_ref, ids_ref, mass_ref = refs[-3:]
+    rows = mass_ref.shape[1]
+    first = 0
+    for ref in block_refs:
+        size, inside = ref.shape[0], first % rows
+        scale = along_rows(info_refs[first // rows][:, rows:])[inside : inside + size]
+        units_ref[first : first + size, :] = unit_rows(ref[...], scale)
+        first += size
+    own_ids = info_refs[0][:, :rows]
+    mass = jnp.zeros((1, rows), jnp.float32)
+    for m in range(PLANE):
+        part = pl.ds(m * rows, rows)
+        query_ids = along_rows(info_refs[m][:, :rows])
+        ids_ref[part, :] = query_ids
+        masses = mate_mass(units_ref[part, :], query_ids, units_ref[:rows, :], own_ids, m == 0)
+        mass = mass + jnp.sum(masses, axis=0, keepdims=True)
+    mass_ref[...] = mass
+
+
+def line_sums(moves, info_ref, line_ref, units_ref, ids_ref, column_ref, sums_ref):
+    rows = column_ref.shape[1]
+    plane = lax.axis_index("gx") // PLANE
+    arrived = functools.reduce(jnp.logical_or, [plane == receiver for _, receiver in moves])
+    column_ref[...] = jnp.zeros_like(column_ref)
+
+    @pl.when(arrived)
+    def _():
+        key_ids = info_ref[:, :rows]
+        key_rows = unit_rows(line_ref[...], along_rows(info_ref[:, rows:]))
+        column = jnp.zeros((1, rows), jnp.float32)
+        for m in range(PLANE):
+            part = pl.ds(m * rows, rows)
+            masses = mate_mass(units_ref[part, :], ids_ref[part, :], key_rows, key_ids, False)
+            column = column + jnp.sum(masses, axis=0, keepdims=True)
+            folded = masses[:, :LANES]
+            for first in range(LANES, rows, LANES):
+                folded = folded + masses[:, first : first + LANES]
+            sums_ref[part, :] += folded
+        column_ref[...] = column
+
+
+def first_line_kernel(moves, info_ref, line_ref, units_ref, ids_ref, column_ref, sums_ref):
+    sums_ref[...] = jnp.zeros_like(sums_ref)
+    line_sums(moves, info_ref, line_ref, units_ref, ids_ref, column_ref, sums_ref)
+
+
+def last_line_kernel(moves, info_ref, line_ref, units_ref, ids_ref, earlier_ref, *refs):
+    mass_refs, column_ref, row_refs, sums_ref = refs[:2], refs[2], refs[3:-1], refs[-1]
+    rows = column_ref.shape[1]
+    sums_ref[...] = earlier_ref[...]
+    line_sums(moves, info_ref, line_ref, units_ref, ids_ref, column_ref, sums_ref)
+    for m in range(PLANE):
+        row_sum = jnp.sum(sums_ref[pl.ds(m * rows, rows), :].T, axis=0, keepdims=True)
+        if m == 0:
+            row_sum = row_sum + mass_refs[0][...] + mass_refs[1][...]
+        row_refs[m][...] = row_sum
+
+
+def grid_plan(embeddings, cluster_ids):
+    peers = lax.axis_size("gx")
+    row_count, features = embeddings.shape
+    plane_rows = PLANE * row_count
+    params = pltpu.CompilerParams(vmem_limit_bytes=VMEM_BYTES)
+    vector = jax.ShapeDtypeStruct((1, row_count), jnp.float32)
+    lanes = jax.ShapeDtypeStruct((plane_rows, LANES), jnp.float32)
+
+    def in_plane(value, step):
+        return lax.ppermute(value, "gx", [(i, i ^ step) for i in range(peers)])
+
+    def on_line(value, moves):
+        pairs = [(a * PLANE + n, b * PLANE + n) for a, b in moves for n in range(PLANE)]
+        return lax.ppermute(value, "gx", pairs)
+
+    first_moves = [(0, 1), (3, 2), (2, 0)]
+    last_moves = [(1, 2), (0, 3), (3, 1)]
+    first_back = [(b, a) for a, b in first_moves]
+    last_back = [(b, a) for a, b in last_moves]
+
+    first_line = on_line(embeddings, first_moves)
+    last_line = on_line(embeddings, last_moves)
+    across = in_plane(embeddings, 2)
+    sibling = in_plane(embeddings, 1)
+    across, rows, row_ids = lax.optimization_barrier((across, embeddings, cluster_ids))
+    info = pl.pallas_call(
+        info_kernel,
+        out_shape=jax.ShapeDtypeStruct((1, 2 * row_count), jnp.float32),
+        compiler_params=params,
+    )(rows, row_ids.reshape(1, row_count))
+    plane_info = [info] + [in_plane(info, step) for step in range(1, PLANE)]
+    first_info = on_line(info, first_moves)
+    last_info = on_line(info, last_moves)
+    corner = [in_plane(part, 1) for part in jnp.split(across, 2)]
+    units, ids, mass = pl.pallas_call(
+        plane_kernel,
+        out_shape=(jax.ShapeDtypeStruct((plane_rows, features), jnp.bfloat16), lanes, vector),
+        cost_estimate=pl.CostEstimate(flops=1, bytes_accessed=1, transcendentals=0),
+        compiler_params=params,
+    )(*plane_info, embeddings, sibling, across, *corner)
+    first_column, first_sums = pl.pallas_call(
+        functools.partial(first_line_kernel, first_moves),
+        out_shape=(vector, lanes),
+        cost_estimate=pl.CostEstimate(flops=1, bytes_accessed=1, transcendentals=0),
+        compiler_params=params,
+    )(first_info, first_line, units, ids)
+    last_column, *row_sums = pl.pallas_call(
+        functools.partial(last_line_kernel, last_moves),
+        out_shape=[vector] * (1 + PLANE),
+        scratch_shapes=[pltpu.VMEM(lanes.shape, lanes.dtype)],
+        compiler_params=params,
+    )(last_info, last_line, units, ids, first_sums, mass, on_line(first_column, first_back))
+    returned = [in_plane(row_sums[step], step) for step in range(1, PLANE)]
+    returned.append(on_line(last_column, last_back))
+    return jnp.log1p(sum(returned, row_sums[0])).reshape(row_count)
+
+
+def on_device(embeddings, cluster_ids):
+    if lax.axis_size("gx") == 4 * PLANE and embeddings.shape[0] % (2 * LANES) == 0:
+        return grid_plan(embeddings, cluster_ids)
+    return plain_plan(embeddings, cluster_ids)
+
+
 def solution(mesh):
     in_specs = (P(("parts", "gx"), None), P(("parts", "gx")))
     out_specs = P(("parts", "gx"))

time: 72.2 us -> 51.4 us (0.71)
  starting transfers between devices: 11.1 us -> 26.9 us
  blocking collectives: 15.3 us -> 0 us
  waiting for transfers between devices: 33 us -> 19.2 us
  matrix products: 6.13 us -> 0 us
  other arithmetic: 4.27 us -> 0.58 us
  Pallas kernels: 0 us -> 2.48 us
    all_to_all x2 -> x0, waiting for transfers between devices: 33 us -> none  [the longest x1 30.7 us: on_device(): lax.all_to_all(outgoing, 'gx', split_axis=0, concat_axis=0, tiled=True)]
    ppermute x0 -> x16, starting transfers between devices: none -> 26.9 us  [the longest x6 19.2 us: on_line(): return lax.ppermute(value, 'gx', pairs)]
    ppermute x0 -> x16, waiting for transfers between devices: none -> 19.2 us  [the longest x10 11.2 us: in_plane(): return lax.ppermute(value, 'gx', [(i, i ^ step) for i in range(peers)])]
    all_to_all x1 -> x0, blocking collectives: 15.3 us -> none  [on_device(): lax.all_to_all(scores.reshape(peer_count, capacity), 'gx', split_axis=0,...]
    all_to_all x2 -> x0, starting transfers between devices: 11.1 us -> none  [the longest x1 7.36 us: on_device(): lax.all_to_all(outgoing_ids, 'gx', split_axis=0, concat_axis=0, tiled=True)]
    dot_general x5 -> x0, matrix products: 6.13 us -> none  [the longest x1 2.86 us: on_device(): jnp.dot(select_mask.astype(jnp.bfloat16), unit_rows, preferred_element_ty...]
    pallas_call x0 -> x4, Pallas kernels: none -> 2.48 us  [the longest x1 1.03 us: grid_plan(): pl.pallas_call(plane_kernel, out_shape=(jax.ShapeDtypeStruct((plane_rows,...]
    reduce_sum x3 -> x0, other arithmetic: 2.19 us -> none  [the longest x1 1.22 us: on_device(): squares = jnp.sum(jnp.square(embeddings.astype(jnp.float32)), axis=1)]
  transfers between devices with their start and end apart: 2 -> 16, of which waited for: 2 -> 8; matrix products, arithmetic and copies ran while one was open for 7% -> 0% of each run, Pallas kernels for 0% -> 4%
where the time goes in v4:
time: 51.4 us; the launch traced here: 51.1 us
  starting transfers between devices  26.9 us (52%)
  waiting for transfers between devices  19.2 us (37%)
  Pallas kernels  2.48 us (5%)
  local copies, waits for them, and re-layouts  1.75 us (3%)
  other arithmetic  0.58 us (1%)
    ppermute x6, starting transfers between devices, on_line(): return lax.ppermute(value, 'gx', pairs)  19.2 us
    ppermute x10, waiting for transfers between devices, in_plane(): return lax.ppermute(value, 'gx', [(i, i ^ step) for i in range(peers)])  11.2 us
    ppermute x6, waiting for transfers between devices, on_line(): return lax.ppermute(value, 'gx', pairs)  8.08 us
    ppermute x10, starting transfers between devices, in_plane(): return lax.ppermute(value, 'gx', [(i, i ^ step) for i in range(peers)])  7.68 us
    unnamed x4, local copies, waits for them, and re-layouts  1.72 us
  transfers between devices with their start and end apart: 16, of which 8 were waited for; matrix products, arithmetic and copies ran while one was open for 0% of the time, Pallas kernels for 4%

profile of v4, /device:TPU:0, one launch (start us, length us, event | category | flops | bytes accessed | tf_op | source)
XLA Modules:
  0.0 51.1 jit_solution(11434180930882028909)
XLA Ops:
  0.0 2.9 %collective-permute-start = (bf16[256,1024]{1,0:T(8,128)(2,1)}, bf16[256,1024]{1,0:T(8,128)(2,1)S(1)}, u32[]{:S(2)}, u32[]{:S(2)}) collective-permute-start(bf16[256,1024]{1,0:T(8,128)(2,1)} %refs_4_.1), channel_id=1, source_target_pairs={{0,2},{1,3},{2,0},{3,1},{4,6},{5,7},{6,4},{7,5},{8,10},{9,11},{10,... | collective-permute-start | bytes 1572872 | tf_op jit(solution)/shard_map/ppermute | solution.py:187
  2.9 0.0 collective-permute-start.6
  2.9 3.5 %collective-permute-start.10 = (bf16[256,1024]{1,0:T(8,128)(2,1)}, bf16[256,1024]{1,0:T(8,128)(2,1)S(1)}, u32[]{:S(2)}, u32[]{:S(2)}) collective-permute-start(bf16[256,1024]{1,0:T(8,128)(2,1)} %refs_4_.1), channel_id=1, source_target_pairs={{0,4},{1,5},{2,6},{3,7},{12,8},{13,9},{14,10},{15,11},{8,0},{9,1},... | collective-permute-start | bytes 1572872 | tf_op jit(solution)/shard_map/ppermute | solution.py:191
  6.4 4.4 %collective-permute-start.2 = (bf16[256,1024]{1,0:T(8,128)(2,1)}, bf16[256,1024]{1,0:T(8,128)(2,1)S(1)}, u32[]{:S(2)}, u32[]{:S(2)}) collective-permute-start(bf16[256,1024]{1,0:T(8,128)(2,1)} %refs_4_.1), channel_id=1, source_target_pairs={{4,8},{5,9},{6,10},{7,11},{0,12},{1,13},{2,14},{3,15},{12,4},{13,5... | collective-permute-start | bytes 1572872 | tf_op jit(solution)/shard_map/ppermute | solution.py:191
  10.9 4.2 %collective-permute-done.refs_6_ = bf16[256,1024]{1,0:T(8,128)(2,1)S(1)} collective-permute-done((bf16[256,1024]{1,0:T(8,128)(2,1)}, bf16[256,1024]{1,0:T(8,128)(2,1)S(1)}, u32[]{:S(2)}, u32[]{:S(2)}) %collective-permute-start) | collective-permute-done | bytes 524320 | tf_op jit(solution)/shard_map/ppermute | solution.py:187
  15.1 0.1 collective-permute-start.7
  15.2 0.5 collective-permute-start.8
  15.7 0.0 copy-start
  15.7 1.0 %copy-done = bf16[256,1024]{1,0:T(8,128)(2,1)S(1)} copy-done((bf16[256,1024]{1,0:T(8,128)(2,1)S(1)}, bf16[256,1024]{1,0:T(8,128)(2,1)}, u32[]{:S(2)}) %copy-start) | copy-done | bytes 524312
  16.7 0.0 copy-start.1
  16.7 0.7 %copy-done.1 = s32[256]{0:T(256)S(1)} copy-done((s32[256]{0:T(256)S(1)}, s32[256]{0:T(256)}, u32[]{:S(2)}) %copy-start.1) | copy-done | bytes 1048
  17.4 0.2 shard_map.28.refs_0_
  17.6 0.0 collective-permute-done.6.refs_5_
  17.6 0.1 collective-permute-start.3
  17.7 1.1 %collective-permute-done.3.refs_1_ = f32[1,512]{1,0:T(1,128)S(1)} collective-permute-done((f32[1,512]{1,0:T(1,128)S(1)}, f32[1,512]{1,0:T(1,128)S(1)}, u32[]{:S(2)}, u32[]{:S(2)}) %collective-permute-start.3) | collective-permute-done | bytes 2080 | tf_op jit(solution)/shard_map/ppermute | solution.py:187
  18.8 1.7 %collective-permute-start.4 = (f32[1,512]{1,0:T(1,128)S(1)}, f32[1,512]{1,0:T(1,128)S(1)}, u32[]{:S(2)}, u32[]{:S(2)}) collective-permute-start(f32[1,512]{1,0:T(1,128)S(1)} %shard_map.28.refs_0_), channel_id=1, source_target_pairs={{0,2},{1,3},{2,0},{3,1},{4,6},{5,7},{6,4},{7,5},{8,10},{9,11},{10,... | collective-permute-start | bytes 6152 | tf_op jit(solution)/shard_map/ppermute | solution.py:187
  20.6 1.8 %collective-permute-done.4.refs_2_ = f32[1,512]{1,0:T(1,128)S(1)} collective-permute-done((f32[1,512]{1,0:T(1,128)S(1)}, f32[1,512]{1,0:T(1,128)S(1)}, u32[]{:S(2)}, u32[]{:S(2)}) %collective-permute-start.4) | collective-permute-done | bytes 2080 | tf_op jit(solution)/shard_map/ppermute | solution.py:187
  22.4 0.4 collective-permute-start.5
  22.8 2.6 %collective-permute-done.5.refs_3_ = f32[1,512]{1,0:T(1,128)S(1)} collective-permute-done((f32[1,512]{1,0:T(1,128)S(1)}, f32[1,512]{1,0:T(1,128)S(1)}, u32[]{:S(2)}, u32[]{:S(2)}) %collective-permute-start.5) | collective-permute-done | bytes 2080 | tf_op jit(solution)/shard_map/ppermute | solution.py:187
  25.4 3.7 %collective-permute-start.9 = (f32[1,512]{1,0:T(1,128)S(1)}, f32[1,512]{1,0:T(1,128)S(1)}, u32[]{:S(2)}, u32[]{:S(2)}) collective-permute-start(f32[1,512]{1,0:T(1,128)S(1)} %shard_map.28.refs_0_), channel_id=1, source_target_pairs={{0,4},{1,5},{2,6},{3,7},{12,8},{13,9},{14,10},{15,11},{8,0},{9,1},... | collective-permute-start | bytes 6152 | tf_op jit(solution)/shard_map/ppermute | solution.py:191
  29.2 0.0 collective-permute-done.7.refs_7_
  29.2 4.4 %collective-permute-start.1 = (f32[1,512]{1,0:T(1,128)S(1)}, f32[1,512]{1,0:T(1,128)S(1)}, u32[]{:S(2)}, u32[]{:S(2)}) collective-permute-start(f32[1,512]{1,0:T(1,128)S(1)} %shard_map.28.refs_0_), channel_id=1, source_target_pairs={{4,8},{5,9},{6,10},{7,11},{0,12},{1,13},{2,14},{3,15},{12,4},{13,5... | collective-permute-start | bytes 6152 | tf_op jit(solution)/shard_map/ppermute | solution.py:191
  33.5 0.0 collective-permute-done.8.refs_8_
  33.6 1.0 %shard_map.29 = (bf16[1024,1024]{1,0:T(8,128)(2,1)S(1)}, f32[1024,128]{1,0:T(8,128)S(1)}, f32[1,256]{1,0:T(1,128)S(1)}) custom-call(f32[1,512]{1,0:T(1,128)S(1)} %shard_map.28.refs_0_, f32[1,512]{1,0:T(1,128)S(1)} %collective-permute-done.3.refs_1_, f32[1,512]{1,0:T(1,128)S(1)} %collective-permute-done.4.refs_2_, ...), custom_call_target="tpu_custom_call" | custom-call | flops 1 | bytes 1 | tf_op jit(solution)/shard_map/pallas_call | solution.py:212
  34.6 0.0 collective-permute-done.10.line_ref
  34.6 0.0 collective-permute-done.9.info_ref
  34.6 1.0 %shard_map.30 = (f32[1,256]{1,0:T(1,128)S(1)}, f32[1024,128]{1,0:T(8,128)S(1)}) custom-call(f32[1,512]{1,0:T(1,128)S(1)} %collective-permute-done.9.info_ref, bf16[256,1024]{1,0:T(8,128)(2,1)S(1)} %collective-permute-done.10.line_ref, bf16[1024,1024]{1,0:T(8,128)(2,1)S(1)} %get-tuple-element.21.units_ref, f32[1024,128]{1,0:T(8,128)S(1)} %get-tuple-element.22.ids_ref), custom_call_target="tpu_custom_call" | custom-call | flops 1 | bytes 1 | tf_op jit(solution)/shard_map/pallas_call | solution.py:218
  35.6 1.9 %collective-permute-start.11 = (f32[1,256]{1,0:T(1,128)S(1)}, f32[1,256]{1,0:T(1,128)S(1)}, u32[]{:S(2)}, u32[]{:S(2)}) collective-permute-start(f32[1,256]{1,0:T(1,128)S(1)} %get-tuple-element.25), channel_id=1, source_target_pairs={{4,0},{5,1},{6,2},{7,3},{8,12},{9,13},{10,14},{11,15},{0,8},{1,9},... | collective-permute-start | bytes 3080 | tf_op jit(solution)/shard_map/ppermute | solution.py:191
  37.5 0.0 collective-permute-done.2.line_ref
  37.6 0.0 collective-permute-done.1.info_ref
  37.6 3.5 %collective-permute-done.11.refs_1_ = f32[1,256]{1,0:T(1,128)S(1)} collective-permute-done((f32[1,256]{1,0:T(1,128)S(1)}, f32[1,256]{1,0:T(1,128)S(1)}, u32[]{:S(2)}, u32[]{:S(2)}) %collective-permute-start.11) | collective-permute-done | bytes 1056 | tf_op jit(solution)/shard_map/ppermute | solution.py:191
  41.1 0.2 shard_map.31
  41.3 0.1 collective-permute-start.12
  41.4 1.6 %collective-permute-start.13 = (f32[1,256]{1,0:T(1,128)S(1)}, f32[1,256]{1,0:T(1,128)S(1)}, u32[]{:S(2)}, u32[]{:S(2)}) collective-permute-start(f32[1,256]{1,0:T(1,128)S(1)} %get-tuple-element.28), channel_id=1, source_target_pairs={{0,2},{1,3},{2,0},{3,1},{4,6},{5,7},{6,4},{7,5},{8,10},{9,11},{10,... | collective-permute-start | bytes 3080 | tf_op jit(solution)/shard_map/ppermute | solution.py:187
  43.0 0.3 collective-permute-start.14
  43.3 1.3 %collective-permute-start.15 = (f32[1,256]{1,0:T(1,128)S(1)}, f32[1,256]{1,0:T(1,128)S(1)}, u32[]{:S(2)}, u32[]{:S(2)}) collective-permute-start(f32[1,256]{1,0:T(1,128)S(1)} %get-tuple-element.30), channel_id=1, source_target_pairs={{8,4},{9,5},{10,6},{11,7},{12,0},{13,1},{14,2},{15,3},{4,12},{5,13... | collective-permute-start | bytes 3080 | tf_op jit(solution)/shard_map/ppermute | solution.py:191
  44.6 0.0 collective-permute-done.12
  44.6 0.5 collective-permute-done.13
  45.0 0.9 %collective-permute-done.14 = f32[1,256]{1,0:T(1,128)S(1)} collective-permute-done((f32[1,256]{1,0:T(1,128)S(1)}, f32[1,256]{1,0:T(1,128)S(1)}, u32[]{:S(2)}, u32[]{:S(2)}) %collective-permute-start.14) | collective-permute-done | bytes 1056 | tf_op jit(solution)/shard_map/ppermute | solution.py:187
  46.0 4.6 %collective-permute-done.15 = f32[1,256]{1,0:T(1,128)S(1)} collective-permute-done((f32[1,256]{1,0:T(1,128)S(1)}, f32[1,256]{1,0:T(1,128)S(1)}, u32[]{:S(2)}, u32[]{:S(2)}) %collective-permute-start.15) | collective-permute-done | bytes 1056 | tf_op jit(solution)/shard_map/ppermute | solution.py:191
  50.5 0.6 %add_log-plus-one_fusion = f32[1,256]{1,0:T(1,128)} fusion(f32[1,256]{1,0:T(1,128)S(1)} %collective-permute-done.15, f32[1,256]{1,0:T(1,128)S(1)} %collective-permute-done.14, f32[1,256]{1,0:T(1,128)S(1)} %collective-permute-done.13, f32[1,256]{1,0:T(1,128)S(1)} %get-tuple-element.26, f32[1,256]{1,0:T(1,128)S(1)} %collective-permute-done.12), kind=kLoop, calls=%fused_computation | loop fusion | flops 1024 | bytes 6144 | tf_op jit(solution)/shard_map/log1p | solution.py:232
  (1 shorter events, 0.0 us)
Async XLA Ops:
  0.0 15.1 %collective-permute-start = (bf16[256,1024]{1,0:T(8,128)(2,1)}, bf16[256,1024]{1,0:T(8,128)(2,1)S(1)}, u32[]{:S(2)}, u32[]{:S(2)}) collective-permute-start(bf16[256,1024]{1,0:T(8,128)(2,1)} %refs_4_.1), channel_id=1, source_target_pairs={{0,2},{1,3},{2,0},{3,1},{4,6},{5,7},{6,4},{7,5},{8,10},{9,11},{10,... | collective-permute-start | bytes 1572872 | tf_op jit(solution)/shard_map/ppermute | solution.py:187
  2.9 14.7 %collective-permute-start.6 = (bf16[256,1024]{1,0:T(8,128)(2,1)}, bf16[256,1024]{1,0:T(8,128)(2,1)S(1)}, u32[]{:S(2)}, u32[]{:S(2)}) collective-permute-start(bf16[256,1024]{1,0:T(8,128)(2,1)} %refs_4_.1), channel_id=1, source_target_pairs={{0,1},{1,0},{2,3},{3,2},{4,5},{5,4},{6,7},{7,6},{8,9},{9,8},{10,11... | collective-permute-start | bytes 1572872 | tf_op jit(solution)/shard_map/ppermute | solution.py:187
  2.9 31.7 %collective-permute-start.10 = (bf16[256,1024]{1,0:T(8,128)(2,1)}, bf16[256,1024]{1,0:T(8,128)(2,1)S(1)}, u32[]{:S(2)}, u32[]{:S(2)}) collective-permute-start(bf16[256,1024]{1,0:T(8,128)(2,1)} %refs_4_.1), channel_id=1, source_target_pairs={{0,4},{1,5},{2,6},{3,7},{12,8},{13,9},{14,10},{15,11},{8,0},{9,1},... | collective-permute-start | bytes 1572872 | tf_op jit(solution)/shard_map/ppermute | solution.py:191
  6.4 31.1 %collective-permute-start.2 = (bf16[256,1024]{1,0:T(8,128)(2,1)}, bf16[256,1024]{1,0:T(8,128)(2,1)S(1)}, u32[]{:S(2)}, u32[]{:S(2)}) collective-permute-start(bf16[256,1024]{1,0:T(8,128)(2,1)} %refs_4_.1), channel_id=1, source_target_pairs={{4,8},{5,9},{6,10},{7,11},{0,12},{1,13},{2,14},{3,15},{12,4},{13,5... | collective-permute-start | bytes 1572872 | tf_op jit(solution)/shard_map/ppermute | solution.py:191
  15.1 14.0 %collective-permute-start.7 = (bf16[128,1024]{1,0:T(8,128)(2,1)S(1)}, bf16[128,1024]{1,0:T(8,128)(2,1)S(1)}, u32[]{:S(2)}, u32[]{:S(2)}) collective-permute-start(bf16[128,1024]{1,0:T(8,128)(2,1)S(1)} %get-tuple-element.32), channel_id=1, source_target_pairs={{0,1},{1,0},{2,3},{3,2},{4,5},{5,4},{6,7},{7,6},{8,9},{9,8},{10,11... | collective-permute-start | bytes 786440 | tf_op jit(solution)/shard_map/ppermute | solution.py:187
  15.2 18.4 %collective-permute-start.8 = (bf16[128,1024]{1,0:T(8,128)(2,1)S(1)}, bf16[128,1024]{1,0:T(8,128)(2,1)S(1)}, u32[]{:S(2)}, u32[]{:S(2)}) collective-permute-start(bf16[128,1024]{1,0:T(8,128)(2,1)S(1)} %get-tuple-element.31), channel_id=1, source_target_pairs={{0,1},{1,0},{2,3},{3,2},{4,5},{5,4},{6,7},{7,6},{8,9},{9,8},{10,11... | collective-permute-start | bytes 786440 | tf_op jit(solution)/shard_map/ppermute | solution.py:187
  15.7 1.0 %copy-start = (bf16[256,1024]{1,0:T(8,128)(2,1)S(1)}, bf16[256,1024]{1,0:T(8,128)(2,1)}, u32[]{:S(2)}) copy-start(bf16[256,1024]{1,0:T(8,128)(2,1)} %refs_4_.1) | copy-start | bytes 1572868
  16.7 0.7 %copy-start.1 = (s32[256]{0:T(256)S(1)}, s32[256]{0:T(256)}, u32[]{:S(2)}) copy-start(s32[256]{0:T(256)} %param.3) | copy-start | bytes 3076
  17.6 1.2 %collective-permute-start.3 = (f32[1,512]{1,0:T(1,128)S(1)}, f32[1,512]{1,0:T(1,128)S(1)}, u32[]{:S(2)}, u32[]{:S(2)}) collective-permute-start(f32[1,512]{1,0:T(1,128)S(1)} %shard_map.28.refs_0_), channel_id=1, source_target_pairs={{0,1},{1,0},{2,3},{3,2},{4,5},{5,4},{6,7},{7,6},{8,9},{9,8},{10,11... | collective-permute-start | bytes 6152 | tf_op jit(solution)/shard_map/ppermute | solution.py:187
  18.8 3.6 %collective-permute-start.4 = (f32[1,512]{1,0:T(1,128)S(1)}, f32[1,512]{1,0:T(1,128)S(1)}, u32[]{:S(2)}, u32[]{:S(2)}) collective-permute-start(f32[1,512]{1,0:T(1,128)S(1)} %shard_map.28.refs_0_), channel_id=1, source_target_pairs={{0,2},{1,3},{2,0},{3,1},{4,6},{5,7},{6,4},{7,5},{8,10},{9,11},{10,... | collective-permute-start | bytes 6152 | tf_op jit(solution)/shard_map/ppermute | solution.py:187
  22.4 3.0 %collective-permute-start.5 = (f32[1,512]{1,0:T(1,128)S(1)}, f32[1,512]{1,0:T(1,128)S(1)}, u32[]{:S(2)}, u32[]{:S(2)}) collective-permute-start(f32[1,512]{1,0:T(1,128)S(1)} %shard_map.28.refs_0_), channel_id=1, source_target_pairs={{0,3},{1,2},{2,1},{3,0},{4,7},{5,6},{6,5},{7,4},{8,11},{9,10},{10,... | collective-permute-start | bytes 6152 | tf_op jit(solution)/shard_map/ppermute | solution.py:187
  25.4 9.2 %collective-permute-start.9 = (f32[1,512]{1,0:T(1,128)S(1)}, f32[1,512]{1,0:T(1,128)S(1)}, u32[]{:S(2)}, u32[]{:S(2)}) collective-permute-start(f32[1,512]{1,0:T(1,128)S(1)} %shard_map.28.refs_0_), channel_id=1, source_target_pairs={{0,4},{1,5},{2,6},{3,7},{12,8},{13,9},{14,10},{15,11},{8,0},{9,1},... | collective-permute-start | bytes 6152 | tf_op jit(solution)/shard_map/ppermute | solution.py:191
  29.2 8.4 %collective-permute-start.1 = (f32[1,512]{1,0:T(1,128)S(1)}, f32[1,512]{1,0:T(1,128)S(1)}, u32[]{:S(2)}, u32[]{:S(2)}) collective-permute-start(f32[1,512]{1,0:T(1,128)S(1)} %shard_map.28.refs_0_), channel_id=1, source_target_pairs={{4,8},{5,9},{6,10},{7,11},{0,12},{1,13},{2,14},{3,15},{12,4},{13,5... | collective-permute-start | bytes 6152 | tf_op jit(solution)/shard_map/ppermute | solution.py:191
  35.6 5.5 %collective-permute-start.11 = (f32[1,256]{1,0:T(1,128)S(1)}, f32[1,256]{1,0:T(1,128)S(1)}, u32[]{:S(2)}, u32[]{:S(2)}) collective-permute-start(f32[1,256]{1,0:T(1,128)S(1)} %get-tuple-element.25), channel_id=1, source_target_pairs={{4,0},{5,1},{6,2},{7,3},{8,12},{9,13},{10,14},{11,15},{0,8},{1,9},... | collective-permute-start | bytes 3080 | tf_op jit(solution)/shard_map/ppermute | solution.py:191
  41.3 3.2 %collective-permute-start.12 = (f32[1,256]{1,0:T(1,128)S(1)}, f32[1,256]{1,0:T(1,128)S(1)}, u32[]{:S(2)}, u32[]{:S(2)}) collective-permute-start(f32[1,256]{1,0:T(1,128)S(1)} %get-tuple-element.27), channel_id=1, source_target_pairs={{0,1},{1,0},{2,3},{3,2},{4,5},{5,4},{6,7},{7,6},{8,9},{9,8},{10,11... | collective-permute-start | bytes 3080 | tf_op jit(solution)/shard_map/ppermute | solution.py:187
  41.4 3.6 %collective-permute-start.13 = (f32[1,256]{1,0:T(1,128)S(1)}, f32[1,256]{1,0:T(1,128)S(1)}, u32[]{:S(2)}, u32[]{:S(2)}) collective-permute-start(f32[1,256]{1,0:T(1,128)S(1)} %get-tuple-element.28), channel_id=1, source_target_pairs={{0,2},{1,3},{2,0},{3,1},{4,6},{5,7},{6,4},{7,5},{8,10},{9,11},{10,... | collective-permute-start | bytes 3080 | tf_op jit(solution)/shard_map/ppermute | solution.py:187
  43.0 3.0 %collective-permute-start.14 = (f32[1,256]{1,0:T(1,128)S(1)}, f32[1,256]{1,0:T(1,128)S(1)}, u32[]{:S(2)}, u32[]{:S(2)}) collective-permute-start(f32[1,256]{1,0:T(1,128)S(1)} %get-tuple-element.29), channel_id=1, source_target_pairs={{0,3},{1,2},{2,1},{3,0},{4,7},{5,6},{6,5},{7,4},{8,11},{9,10},{10,... | collective-permute-start | bytes 3080 | tf_op jit(solution)/shard_map/ppermute | solution.py:187
  43.3 7.2 %collective-permute-start.15 = (f32[1,256]{1,0:T(1,128)S(1)}, f32[1,256]{1,0:T(1,128)S(1)}, u32[]{:S(2)}, u32[]{:S(2)}) collective-permute-start(f32[1,256]{1,0:T(1,128)S(1)} %get-tuple-element.30), channel_id=1, source_target_pairs={{8,4},{9,5},{10,6},{11,7},{12,0},{13,1},{14,2},{15,3},{4,12},{5,13... | collective-permute-start | bytes 3080 | tf_op jit(solution)/shard_map/ppermute | solution.py:191

commit v5 on v4

--- a/solution.py
+++ b/solution.py
@@ -116,20 +116,20 @@
 
 
 def plane_kernel(*refs):
-    info_refs, block_refs = refs[:PLANE], refs[PLANE:-3]
+    infos, block_refs = [ref[...] for ref in refs[:PLANE]], refs[PLANE:-3]
     units_ref, ids_ref, mass_ref = refs[-3:]
     rows = mass_ref.shape[1]
     first = 0
     for ref in block_refs:
         size, inside = ref.shape[0], first % rows
-        scale = along_rows(info_refs[first // rows][:, rows:])[inside : inside + size]
+        scale = along_rows(infos[first // rows][:, rows:])[inside : inside + size]
         units_ref[first : first + size, :] = unit_rows(ref[...], scale)
         first += size
-    own_ids = info_refs[0][:, :rows]
+    own_ids = infos[0][:, :rows]
     mass = jnp.zeros((1, rows), jnp.float32)
     for m in range(PLANE):
         part = pl.ds(m * rows, rows)
-        query_ids = along_rows(info_refs[m][:, :rows])
+        query_ids = along_rows(infos[m][:, :rows])
         ids_ref[part, :] = query_ids
         masses = mate_mass(units_ref[part, :], query_ids, units_ref[:rows, :], own_ids, m == 0)
         mass = mass + jnp.sum(masses, axis=0, keepdims=True)
@@ -190,8 +190,8 @@
         pairs = [(a * PLANE + n, b * PLANE + n) for a, b in moves for n in range(PLANE)]
         return lax.ppermute(value, "gx", pairs)
 
-    first_moves = [(0, 1), (3, 2), (2, 0)]
-    last_moves = [(1, 2), (0, 3), (3, 1)]
+    first_moves = [(0, 1), (1, 2), (2, 3), (3, 0)]
+    last_moves = [(0, 2), (3, 1)]
     first_back = [(b, a) for a, b in first_moves]
     last_back = [(b, a) for a, b in last_moves]
 
@@ -199,22 +199,23 @@
     last_line = on_line(embeddings, last_moves)
     across = in_plane(embeddings, 2)
     sibling = in_plane(embeddings, 1)
-    across, rows, row_ids = lax.optimization_barrier((across, embeddings, cluster_ids))
     info = pl.pallas_call(
         info_kernel,
         out_shape=jax.ShapeDtypeStruct((1, 2 * row_count), jnp.float32),
-        compiler_params=params,
-    )(rows, row_ids.reshape(1, row_count))
-    plane_info = [info] + [in_plane(info, step) for step in range(1, PLANE)]
+        cost_estimate=pl.CostEstimate(flops=1, bytes_accessed=1, transcendentals=0),
+        compiler_params=params,
+    )(embeddings, cluster_ids.reshape(1, row_count))
+    plane_info = [in_plane(info, step) for step in range(1, PLANE)]
     first_info = on_line(info, first_moves)
     last_info = on_line(info, last_moves)
+    across, *plane_info = lax.optimization_barrier((across, *plane_info))
     corner = [in_plane(part, 1) for part in jnp.split(across, 2)]
     units, ids, mass = pl.pallas_call(
         plane_kernel,
         out_shape=(jax.ShapeDtypeStruct((plane_rows, features), jnp.bfloat16), lanes, vector),
         cost_estimate=pl.CostEstimate(flops=1, bytes_accessed=1, transcendentals=0),
         compiler_params=params,
-    )(*plane_info, embeddings, sibling, across, *corner)
+    )(info, *plane_info, embeddings, sibling, across, *corner)
     first_column, first_sums = pl.pallas_call(
         functools.partial(first_line_kernel, first_moves),
         out_shape=(vector, lanes),
@@ -227,8 +228,8 @@
         scratch_shapes=[pltpu.VMEM(lanes.shape, lanes.dtype)],
         compiler_params=params,
     )(last_info, last_line, units, ids, first_sums, mass, on_line(first_column, first_back))
-    returned = [in_plane(row_sums[step], step) for step in range(1, PLANE)]
-    returned.append(on_line(last_column, last_back))
+    returned = [on_line(last_column, last_back)]
+    returned += [in_plane(row_sums[step], step) for step in (2, 3, 1)]
     return jnp.log1p(sum(returned, row_sums[0])).reshape(row_count)
 
 

time: 51.4 us -> 42.7 us (0.83)
  starting transfers between devices: 26.9 us -> 19.4 us
  waiting for transfers between devices: 19.2 us -> 18.2 us
    ppermute x6, starting transfers between devices: 19.2 us -> 13.1 us  [on_line(): return lax.ppermute(value, 'gx', pairs)]
    ppermute x10, waiting for transfers between devices: 11.2 us -> 7.22 us  [in_plane(): return lax.ppermute(value, 'gx', [(i, i ^ step) for i in range(peers)])]
    ppermute x6, waiting for transfers between devices: 8.08 us -> 10.9 us  [on_line(): return lax.ppermute(value, 'gx', pairs)]
    ppermute x10, starting transfers between devices: 7.68 us -> 6.29 us  [in_plane(): return lax.ppermute(value, 'gx', [(i, i ^ step) for i in range(peers)])]
  transfers between devices with their start and end apart: 16 -> 16, of which waited for: 8 -> 6; matrix products, arithmetic and copies ran while one was open for 0% -> 0% of each run, Pallas kernels for 4% -> 5%
where the time goes in v5:
time: 42.7 us; the launch traced here: 42.5 us
  starting transfers between devices  19.4 us (45%)
  waiting for transfers between devices  18.2 us (43%)
  Pallas kernels  2.48 us (6%)
  local copies, waits for them, and re-layouts  1.77 us (4%)
  other arithmetic  0.58 us (1%)
    ppermute x6, starting transfers between devices, on_line(): return lax.ppermute(value, 'gx', pairs)  13.1 us
    ppermute x6, waiting for transfers between devices, on_line(): return lax.ppermute(value, 'gx', pairs)  10.9 us
    ppermute x10, waiting for transfers between devices, in_plane(): return lax.ppermute(value, 'gx', [(i, i ^ step) for i in range(peers)])  7.22 us
    ppermute x10, starting transfers between devices, in_plane(): return lax.ppermute(value, 'gx', [(i, i ^ step) for i in range(peers)])  6.29 us
    unnamed x4, local copies, waits for them, and re-layouts  1.73 us
    pallas_call x1, Pallas kernels, grid_plan(): pl.pallas_call(plane_kernel, out_shape=(jax.ShapeDtypeStruct((plane_rows,...  1.03 us
    pallas_call x1, Pallas kernels, grid_plan(): pl.pallas_call(functools.partial(first_line_kernel, first_moves), out_sha...  0.99 us
  transfers between devices with their start and end apart: 16, of which 6 were waited for; matrix products, arithmetic and copies ran while one was open for 0% of the time, Pallas kernels for 5%

profile of v5, /device:TPU:0, one launch (start us, length us, event | category | flops | bytes accessed | tf_op | source)
XLA Modules:
  0.0 42.5 jit_solution(8691964384977784379)
XLA Ops:
  0.0 2.9 %collective-permute-start.2 = (bf16[256,1024]{1,0:T(8,128)(2,1)}, bf16[256,1024]{1,0:T(8,128)(2,1)S(1)}, u32[]{:S(2)}, u32[]{:S(2)}) collective-permute-start(bf16[256,1024]{1,0:T(8,128)(2,1)} %refs_4_.1), channel_id=1, source_target_pairs={{0,2},{1,3},{2,0},{3,1},{4,6},{5,7},{6,4},{7,5},{8,10},{9,11},{10,... | collective-permute-start | bytes 1572872 | tf_op jit(solution)/shard_map/ppermute | solution.py:187
  2.9 0.0 collective-permute-start.6
  2.9 1.6 %collective-permute-start.10 = (bf16[256,1024]{1,0:T(8,128)(2,1)}, bf16[256,1024]{1,0:T(8,128)(2,1)S(1)}, u32[]{:S(2)}, u32[]{:S(2)}) collective-permute-start(bf16[256,1024]{1,0:T(8,128)(2,1)} %refs_4_.1), channel_id=1, source_target_pairs={{0,4},{1,5},{2,6},{3,7},{4,8},{5,9},{6,10},{7,11},{8,12},{9,13},{1... | collective-permute-start | bytes 1572872 | tf_op jit(solution)/shard_map/ppermute | solution.py:191
  4.5 4.5 %collective-permute-start.1 = (bf16[256,1024]{1,0:T(8,128)(2,1)}, bf16[256,1024]{1,0:T(8,128)(2,1)S(1)}, u32[]{:S(2)}, u32[]{:S(2)}) collective-permute-start(bf16[256,1024]{1,0:T(8,128)(2,1)} %refs_4_.1), channel_id=1, source_target_pairs={{0,8},{1,9},{2,10},{3,11},{12,4},{13,5},{14,6},{15,7},{16,24},{17,... | collective-permute-start | bytes 1572872 | tf_op jit(solution)/shard_map/ppermute | solution.py:191
  9.0 0.0 copy-start
  9.1 1.1 %copy-done = bf16[256,1024]{1,0:T(8,128)(2,1)S(1)} copy-done((bf16[256,1024]{1,0:T(8,128)(2,1)S(1)}, bf16[256,1024]{1,0:T(8,128)(2,1)}, u32[]{:S(2)}) %copy-start) | copy-done | bytes 524312
  10.1 0.0 copy-start.1
  10.1 0.7 %copy-done.1 = s32[256]{0:T(256)S(1)} copy-done((s32[256]{0:T(256)S(1)}, s32[256]{0:T(256)}, u32[]{:S(2)}) %copy-start.1) | copy-done | bytes 1048
  10.8 0.2 shard_map.28.refs_0_
  11.0 0.0 collective-permute-start.3
  11.0 1.1 %collective-permute-done.3.refs_1_ = f32[1,512]{1,0:T(1,128)S(1)} collective-permute-done((f32[1,512]{1,0:T(1,128)S(1)}, f32[1,512]{1,0:T(1,128)S(1)}, u32[]{:S(2)}, u32[]{:S(2)}) %collective-permute-start.3) | collective-permute-done | bytes 2080 | tf_op jit(solution)/shard_map/ppermute | solution.py:187
  12.2 0.5 %collective-permute-start.4 = (f32[1,512]{1,0:T(1,128)S(1)}, f32[1,512]{1,0:T(1,128)S(1)}, u32[]{:S(2)}, u32[]{:S(2)}) collective-permute-start(f32[1,512]{1,0:T(1,128)S(1)} %shard_map.28.refs_0_), channel_id=1, source_target_pairs={{0,2},{1,3},{2,0},{3,1},{4,6},{5,7},{6,4},{7,5},{8,10},{9,11},{10,... | collective-permute-start | bytes 6152 | tf_op jit(solution)/shard_map/ppermute | solution.py:187
  12.7 3.0 %collective-permute-done.4.refs_2_ = f32[1,512]{1,0:T(1,128)S(1)} collective-permute-done((f32[1,512]{1,0:T(1,128)S(1)}, f32[1,512]{1,0:T(1,128)S(1)}, u32[]{:S(2)}, u32[]{:S(2)}) %collective-permute-start.4) | collective-permute-done | bytes 2080 | tf_op jit(solution)/shard_map/ppermute | solution.py:187
  15.8 0.0 collective-permute-start.5
  15.8 3.0 %collective-permute-done.5.refs_3_ = f32[1,512]{1,0:T(1,128)S(1)} collective-permute-done((f32[1,512]{1,0:T(1,128)S(1)}, f32[1,512]{1,0:T(1,128)S(1)}, u32[]{:S(2)}, u32[]{:S(2)}) %collective-permute-start.5) | collective-permute-done | bytes 2080 | tf_op jit(solution)/shard_map/ppermute | solution.py:187
  18.8 0.0 collective-permute-done.2.refs_6_
  18.8 0.1 collective-permute-start.7
  18.9 0.5 %collective-permute-start.8 = (bf16[128,1024]{1,0:T(8,128)(2,1)S(1)}, bf16[128,1024]{1,0:T(8,128)(2,1)S(1)}, u32[]{:S(2)}, u32[]{:S(2)}) collective-permute-start(bf16[128,1024]{1,0:T(8,128)(2,1)S(1)} %get-tuple-element.33), channel_id=1, source_target_pairs={{0,1},{1,0},{2,3},{3,2},{4,5},{5,4},{6,7},{7,6},{8,9},{9,8},{10,11... | collective-permute-start | bytes 786440 | tf_op jit(solution)/shard_map/ppermute | solution.py:187
  19.4 0.0 collective-permute-done.6.refs_5_
  19.4 1.2 %collective-permute-start.9 = (f32[1,512]{1,0:T(1,128)S(1)}, f32[1,512]{1,0:T(1,128)S(1)}, u32[]{:S(2)}, u32[]{:S(2)}) collective-permute-start(f32[1,512]{1,0:T(1,128)S(1)} %shard_map.28.refs_0_), channel_id=1, source_target_pairs={{0,4},{1,5},{2,6},{3,7},{4,8},{5,9},{6,10},{7,11},{8,12},{9,13},{1... | collective-permute-start | bytes 6152 | tf_op jit(solution)/shard_map/ppermute | solution.py:191
  20.6 0.0 collective-permute-done.7.refs_7_
  20.6 4.5 %collective-permute-start = (f32[1,512]{1,0:T(1,128)S(1)}, f32[1,512]{1,0:T(1,128)S(1)}, u32[]{:S(2)}, u32[]{:S(2)}) collective-permute-start(f32[1,512]{1,0:T(1,128)S(1)} %shard_map.28.refs_0_), channel_id=1, source_target_pairs={{0,8},{1,9},{2,10},{3,11},{12,4},{13,5},{14,6},{15,7},{16,24},{17,... | collective-permute-start | bytes 6152 | tf_op jit(solution)/shard_map/ppermute | solution.py:191
  25.1 0.0 collective-permute-done.8.refs_8_
  25.1 1.0 %shard_map.29 = (bf16[1024,1024]{1,0:T(8,128)(2,1)S(1)}, f32[1024,128]{1,0:T(8,128)S(1)}, f32[1,256]{1,0:T(1,128)S(1)}) custom-call(f32[1,512]{1,0:T(1,128)S(1)} %shard_map.28.refs_0_, f32[1,512]{1,0:T(1,128)S(1)} %collective-permute-done.3.refs_1_, f32[1,512]{1,0:T(1,128)S(1)} %collective-permute-done.4.refs_2_, ...), custom_call_target="tpu_custom_call" | custom-call | flops 1 | bytes 1 | tf_op jit(solution)/shard_map/pallas_call | solution.py:213
  26.1 4.5 %collective-permute-done.9.info_ref = f32[1,512]{1,0:T(1,128)S(1)} collective-permute-done((f32[1,512]{1,0:T(1,128)S(1)}, f32[1,512]{1,0:T(1,128)S(1)}, u32[]{:S(2)}, u32[]{:S(2)}) %collective-permute-start.9) | collective-permute-done | bytes 2080 | tf_op jit(solution)/shard_map/ppermute | solution.py:191
  30.6 0.0 collective-permute-done.10.line_ref
  30.7 1.0 %shard_map.30 = (f32[1,256]{1,0:T(1,128)S(1)}, f32[1024,128]{1,0:T(8,128)S(1)}) custom-call(f32[1,512]{1,0:T(1,128)S(1)} %collective-permute-done.9.info_ref, bf16[256,1024]{1,0:T(8,128)(2,1)S(1)} %collective-permute-done.10.line_ref, bf16[1024,1024]{1,0:T(8,128)(2,1)S(1)} %get-tuple-element.23.units_ref, f32[1024,128]{1,0:T(8,128)S(1)} %get-tuple-element.24.ids_ref), custom_call_target="tpu_custom_call" | custom-call | flops 1 | bytes 1 | tf_op jit(solution)/shard_map/pallas_call | solution.py:219
  31.7 0.1 collective-permute-start.11
  31.7 0.0 collective-permute-done.info_ref
  31.7 0.0 collective-permute-done.1.line_ref
  31.7 3.5 %collective-permute-done.11.refs_1_ = f32[1,256]{1,0:T(1,128)S(1)} collective-permute-done((f32[1,256]{1,0:T(1,128)S(1)}, f32[1,256]{1,0:T(1,128)S(1)}, u32[]{:S(2)}, u32[]{:S(2)}) %collective-permute-start.11) | collective-permute-done | bytes 1056 | tf_op jit(solution)/shard_map/ppermute | solution.py:191
  35.3 0.2 shard_map.31
  35.5 1.3 %collective-permute-start.12 = (f32[1,256]{1,0:T(1,128)S(1)}, f32[1,256]{1,0:T(1,128)S(1)}, u32[]{:S(2)}, u32[]{:S(2)}) collective-permute-start(f32[1,256]{1,0:T(1,128)S(1)} %get-tuple-element.29), channel_id=1, source_target_pairs={{8,0},{9,1},{10,2},{11,3},{4,12},{5,13},{6,14},{7,15},{24,16},{25,... | collective-permute-start | bytes 3080 | tf_op jit(solution)/shard_map/ppermute | solution.py:191
  36.8 0.6 %collective-permute-start.13 = (f32[1,256]{1,0:T(1,128)S(1)}, f32[1,256]{1,0:T(1,128)S(1)}, u32[]{:S(2)}, u32[]{:S(2)}) collective-permute-start(f32[1,256]{1,0:T(1,128)S(1)} %get-tuple-element.30), channel_id=1, source_target_pairs={{0,2},{1,3},{2,0},{3,1},{4,6},{5,7},{6,4},{7,5},{8,10},{9,11},{10,... | collective-permute-start | bytes 3080 | tf_op jit(solution)/shard_map/ppermute | solution.py:187
  37.4 0.0 collective-permute-start.14
  37.4 1.6 %collective-permute-start.15 = (f32[1,256]{1,0:T(1,128)S(1)}, f32[1,256]{1,0:T(1,128)S(1)}, u32[]{:S(2)}, u32[]{:S(2)}) collective-permute-start(f32[1,256]{1,0:T(1,128)S(1)} %get-tuple-element.32), channel_id=1, source_target_pairs={{0,1},{1,0},{2,3},{3,2},{4,5},{5,4},{6,7},{7,6},{8,9},{9,8},{10,11... | collective-permute-start | bytes 3080 | tf_op jit(solution)/shard_map/ppermute | solution.py:187
  39.0 2.9 %collective-permute-done.12 = f32[1,256]{1,0:T(1,128)S(1)} collective-permute-done((f32[1,256]{1,0:T(1,128)S(1)}, f32[1,256]{1,0:T(1,128)S(1)}, u32[]{:S(2)}, u32[]{:S(2)}) %collective-permute-start.12) | collective-permute-done | bytes 1056 | tf_op jit(solution)/shard_map/ppermute | solution.py:191
  41.9 0.0 collective-permute-done.13
  41.9 0.0 collective-permute-done.14
  41.9 0.0 collective-permute-done.15
  41.9 0.6 %add_log-plus-one_fusion = f32[1,256]{1,0:T(1,128)} fusion(f32[1,256]{1,0:T(1,128)S(1)} %collective-permute-done.15, f32[1,256]{1,0:T(1,128)S(1)} %collective-permute-done.14, f32[1,256]{1,0:T(1,128)S(1)} %collective-permute-done.13, f32[1,256]{1,0:T(1,128)S(1)} %get-tuple-element.28, f32[1,256]{1,0:T(1,128)S(1)} %collective-permute-done.12), kind=kLoop, calls=%fused_computation | loop fusion | flops 1024 | bytes 6144 | tf_op jit(solution)/shard_map/log1p | solution.py:233
  (1 shorter events, 0.0 us)
Async XLA Ops:
  0.0 18.8 %collective-permute-start.2 = (bf16[256,1024]{1,0:T(8,128)(2,1)}, bf16[256,1024]{1,0:T(8,128)(2,1)S(1)}, u32[]{:S(2)}, u32[]{:S(2)}) collective-permute-start(bf16[256,1024]{1,0:T(8,128)(2,1)} %refs_4_.1), channel_id=1, source_target_pairs={{0,2},{1,3},{2,0},{3,1},{4,6},{5,7},{6,4},{7,5},{8,10},{9,11},{10,... | collective-permute-start | bytes 1572872 | tf_op jit(solution)/shard_map/ppermute | solution.py:187
  2.9 16.5 %collective-permute-start.6 = (bf16[256,1024]{1,0:T(8,128)(2,1)}, bf16[256,1024]{1,0:T(8,128)(2,1)S(1)}, u32[]{:S(2)}, u32[]{:S(2)}) collective-permute-start(bf16[256,1024]{1,0:T(8,128)(2,1)} %refs_4_.1), channel_id=1, source_target_pairs={{0,1},{1,0},{2,3},{3,2},{4,5},{5,4},{6,7},{7,6},{8,9},{9,8},{10,11... | collective-permute-start | bytes 1572872 | tf_op jit(solution)/shard_map/ppermute | solution.py:187
  2.9 27.7 %collective-permute-start.10 = (bf16[256,1024]{1,0:T(8,128)(2,1)}, bf16[256,1024]{1,0:T(8,128)(2,1)S(1)}, u32[]{:S(2)}, u32[]{:S(2)}) collective-permute-start(bf16[256,1024]{1,0:T(8,128)(2,1)} %refs_4_.1), channel_id=1, source_target_pairs={{0,4},{1,5},{2,6},{3,7},{4,8},{5,9},{6,10},{7,11},{8,12},{9,13},{1... | collective-permute-start | bytes 1572872 | tf_op jit(solution)/shard_map/ppermute | solution.py:191
  4.5 27.2 %collective-permute-start.1 = (bf16[256,1024]{1,0:T(8,128)(2,1)}, bf16[256,1024]{1,0:T(8,128)(2,1)S(1)}, u32[]{:S(2)}, u32[]{:S(2)}) collective-permute-start(bf16[256,1024]{1,0:T(8,128)(2,1)} %refs_4_.1), channel_id=1, source_target_pairs={{0,8},{1,9},{2,10},{3,11},{12,4},{13,5},{14,6},{15,7},{16,24},{17,... | collective-permute-start | bytes 1572872 | tf_op jit(solution)/shard_map/ppermute | solution.py:191
  9.0 1.1 %copy-start = (bf16[256,1024]{1,0:T(8,128)(2,1)S(1)}, bf16[256,1024]{1,0:T(8,128)(2,1)}, u32[]{:S(2)}) copy-start(bf16[256,1024]{1,0:T(8,128)(2,1)} %refs_4_.1) | copy-start | bytes 1572868
  10.1 0.7 %copy-start.1 = (s32[256]{0:T(256)S(1)}, s32[256]{0:T(256)}, u32[]{:S(2)}) copy-start(s32[256]{0:T(256)} %param.3) | copy-start | bytes 3076
  11.0 1.2 %collective-permute-start.3 = (f32[1,512]{1,0:T(1,128)S(1)}, f32[1,512]{1,0:T(1,128)S(1)}, u32[]{:S(2)}, u32[]{:S(2)}) collective-permute-start(f32[1,512]{1,0:T(1,128)S(1)} %shard_map.28.refs_0_), channel_id=1, source_target_pairs={{0,1},{1,0},{2,3},{3,2},{4,5},{5,4},{6,7},{7,6},{8,9},{9,8},{10,11... | collective-permute-start | bytes 6152 | tf_op jit(solution)/shard_map/ppermute | solution.py:187
  12.2 3.6 %collective-permute-start.4 = (f32[1,512]{1,0:T(1,128)S(1)}, f32[1,512]{1,0:T(1,128)S(1)}, u32[]{:S(2)}, u32[]{:S(2)}) collective-permute-start(f32[1,512]{1,0:T(1,128)S(1)} %shard_map.28.refs_0_), channel_id=1, source_target_pairs={{0,2},{1,3},{2,0},{3,1},{4,6},{5,7},{6,4},{7,5},{8,10},{9,11},{10,... | collective-permute-start | bytes 6152 | tf_op jit(solution)/shard_map/ppermute | solution.py:187
  15.8 3.0 %collective-permute-start.5 = (f32[1,512]{1,0:T(1,128)S(1)}, f32[1,512]{1,0:T(1,128)S(1)}, u32[]{:S(2)}, u32[]{:S(2)}) collective-permute-start(f32[1,512]{1,0:T(1,128)S(1)} %shard_map.28.refs_0_), channel_id=1, source_target_pairs={{0,3},{1,2},{2,1},{3,0},{4,7},{5,6},{6,5},{7,4},{8,11},{9,10},{10,... | collective-permute-start | bytes 6152 | tf_op jit(solution)/shard_map/ppermute | solution.py:187
  18.8 1.7 %collective-permute-start.7 = (bf16[128,1024]{1,0:T(8,128)(2,1)S(1)}, bf16[128,1024]{1,0:T(8,128)(2,1)S(1)}, u32[]{:S(2)}, u32[]{:S(2)}) collective-permute-start(bf16[128,1024]{1,0:T(8,128)(2,1)S(1)} %get-tuple-element.34), channel_id=1, source_target_pairs={{0,1},{1,0},{2,3},{3,2},{4,5},{5,4},{6,7},{7,6},{8,9},{9,8},{10,11... | collective-permute-start | bytes 786440 | tf_op jit(solution)/shard_map/ppermute | solution.py:187
  18.9 6.2 %collective-permute-start.8 = (bf16[128,1024]{1,0:T(8,128)(2,1)S(1)}, bf16[128,1024]{1,0:T(8,128)(2,1)S(1)}, u32[]{:S(2)}, u32[]{:S(2)}) collective-permute-start(bf16[128,1024]{1,0:T(8,128)(2,1)S(1)} %get-tuple-element.33), channel_id=1, source_target_pairs={{0,1},{1,0},{2,3},{3,2},{4,5},{5,4},{6,7},{7,6},{8,9},{9,8},{10,11... | collective-permute-start | bytes 786440 | tf_op jit(solution)/shard_map/ppermute | solution.py:187
  19.4 11.2 %collective-permute-start.9 = (f32[1,512]{1,0:T(1,128)S(1)}, f32[1,512]{1,0:T(1,128)S(1)}, u32[]{:S(2)}, u32[]{:S(2)}) collective-permute-start(f32[1,512]{1,0:T(1,128)S(1)} %shard_map.28.refs_0_), channel_id=1, source_target_pairs={{0,4},{1,5},{2,6},{3,7},{4,8},{5,9},{6,10},{7,11},{8,12},{9,13},{1... | collective-permute-start | bytes 6152 | tf_op jit(solution)/shard_map/ppermute | solution.py:191
  20.6 11.1 %collective-permute-start = (f32[1,512]{1,0:T(1,128)S(1)}, f32[1,512]{1,0:T(1,128)S(1)}, u32[]{:S(2)}, u32[]{:S(2)}) collective-permute-start(f32[1,512]{1,0:T(1,128)S(1)} %shard_map.28.refs_0_), channel_id=1, source_target_pairs={{0,8},{1,9},{2,10},{3,11},{12,4},{13,5},{14,6},{15,7},{16,24},{17,... | collective-permute-start | bytes 6152 | tf_op jit(solution)/shard_map/ppermute | solution.py:191
  31.7 3.6 %collective-permute-start.11 = (f32[1,256]{1,0:T(1,128)S(1)}, f32[1,256]{1,0:T(1,128)S(1)}, u32[]{:S(2)}, u32[]{:S(2)}) collective-permute-start(f32[1,256]{1,0:T(1,128)S(1)} %get-tuple-element.27), channel_id=1, source_target_pairs={{4,0},{5,1},{6,2},{7,3},{8,4},{9,5},{10,6},{11,7},{12,8},{13,9},{1... | collective-permute-start | bytes 3080 | tf_op jit(solution)/shard_map/ppermute | solution.py:191
  35.5 6.4 %collective-permute-start.12 = (f32[1,256]{1,0:T(1,128)S(1)}, f32[1,256]{1,0:T(1,128)S(1)}, u32[]{:S(2)}, u32[]{:S(2)}) collective-permute-start(f32[1,256]{1,0:T(1,128)S(1)} %get-tuple-element.29), channel_id=1, source_target_pairs={{8,0},{9,1},{10,2},{11,3},{4,12},{5,13},{6,14},{7,15},{24,16},{25,... | collective-permute-start | bytes 3080 | tf_op jit(solution)/shard_map/ppermute | solution.py:191
  36.8 5.1 %collective-permute-start.13 = (f32[1,256]{1,0:T(1,128)S(1)}, f32[1,256]{1,0:T(1,128)S(1)}, u32[]{:S(2)}, u32[]{:S(2)}) collective-permute-start(f32[1,256]{1,0:T(1,128)S(1)} %get-tuple-element.30), channel_id=1, source_target_pairs={{0,2},{1,3},{2,0},{3,1},{4,6},{5,7},{6,4},{7,5},{8,10},{9,11},{10,... | collective-permute-start | bytes 3080 | tf_op jit(solution)/shard_map/ppermute | solution.py:187
  37.4 4.5 %collective-permute-start.14 = (f32[1,256]{1,0:T(1,128)S(1)}, f32[1,256]{1,0:T(1,128)S(1)}, u32[]{:S(2)}, u32[]{:S(2)}) collective-permute-start(f32[1,256]{1,0:T(1,128)S(1)} %get-tuple-element.31), channel_id=1, source_target_pairs={{0,3},{1,2},{2,1},{3,0},{4,7},{5,6},{6,5},{7,4},{8,11},{9,10},{10,... | collective-permute-start | bytes 3080 | tf_op jit(solution)/shard_map/ppermute | solution.py:187
  37.4 4.5 %collective-permute-start.15 = (f32[1,256]{1,0:T(1,128)S(1)}, f32[1,256]{1,0:T(1,128)S(1)}, u32[]{:S(2)}, u32[]{:S(2)}) collective-permute-start(f32[1,256]{1,0:T(1,128)S(1)} %get-tuple-element.32), channel_id=1, source_target_pairs={{0,1},{1,0},{2,3},{3,2},{4,5},{5,4},{6,7},{7,6},{8,9},{9,8},{10,11... | collective-permute-start | bytes 3080 | tf_op jit(solution)/shard_map/ppermute | solution.py:187

commit v6 on v5

v6 whole, which is shorter than its diff:
```python
import functools

import jax
import jax.numpy as jnp
from jax import lax
from jax.experimental import pallas as pl
from jax.experimental.pallas import tpu as pltpu
from jax.sharding import PartitionSpec as P

CLU_DEV = 1
PAD_MARK = 64.0
inverse_temp = 20.0


def tile_mass(query_rows, key_rows, query_ids, key_ids, query_start):
    similar = lax.dot_general(
        query_rows, key_rows, (((1,), (1,)), ((), ())), preferred_element_type=jnp.float32
    )
    query_pos = jnp.arange(query_rows.shape[0], dtype=jnp.int32) + query_start
    key_pos = jnp.arange(key_rows.shape[0], dtype=jnp.int32)
    mate_mask = (query_ids[:, None] == key_ids[None, :]) & (query_ids[:, None] >= 0)
    mate_mask = mate_mask & (query_pos[:, None] != key_pos[None, :])
    return jnp.where(mate_mask, jnp.exp(similar * inverse_temp), 0.0)


def density_scores(key_rows, key_ids):
    total_rows = key_rows.shape[0]
    block_rows = total_rows // 3
    pieces = [key_rows[i * block_rows : (i + 1) * block_rows] for i in range(3)]
    piece_ids = [key_ids[i * block_rows : (i + 1) * block_rows] for i in range(3)]
    sums = []
    for first in range(3):
        masses = tile_mass(pieces[first], key_rows, piece_ids[first], key_ids, first * block_rows)
        sums.append(jnp.sum(masses, axis=1))
    mass_sum = jnp.concatenate(sums, axis=0)
    return jnp.log1p(mass_sum)


def plain_plan(embeddings, cluster_ids):
    peer_count = lax.axis_size("gx")
    row_count = embeddings.shape[0]
    features = embeddings.shape[1]
    capacity = 3 * row_count // peer_count
    slot_total = peer_count * capacity
    squares = jnp.sum(jnp.square(embeddings.astype(jnp.float32)), axis=1)
    unit_rows = (embeddings.astype(jnp.float32) * lax.rsqrt(squares + 1e-06)[:, None]).astype(
        jnp.bfloat16
    )
    owner_of = cluster_ids // CLU_DEV
    onehot = (owner_of[:, None] == jnp.arange(peer_count, dtype=jnp.int32)[None, :]).astype(
        jnp.bfloat16
    )
    row_range = jnp.arange(row_count, dtype=jnp.int32)
    lower_tri = (row_range[:, None] >= row_range[None, :]).astype(jnp.bfloat16)
    running = jnp.dot(lower_tri, onehot, preferred_element_type=jnp.float32)
    slot_index = (jnp.sum(running * onehot.astype(jnp.float32), axis=1) - 1.0).astype(jnp.int32)
    target_slot = owner_of * capacity + slot_index
    slot_range = jnp.arange(slot_total, dtype=jnp.int32)
    select_mask = slot_range[:, None] == target_slot[None, :]
    outgoing = jnp.dot(
        select_mask.astype(jnp.bfloat16), unit_rows, preferred_element_type=jnp.float32
    )
    outgoing = outgoing.astype(jnp.bfloat16).reshape(peer_count, capacity, features)
    outgoing_ids = jnp.sum(jnp.where(select_mask, cluster_ids[None, :] + 1, 0), axis=1) - 1
    outgoing_ids = outgoing_ids.reshape(peer_count, capacity)
    arrived, arrived_ids = (
        lax.all_to_all(outgoing, "gx", split_axis=0, concat_axis=0, tiled=True),
        lax.all_to_all(outgoing_ids, "gx", split_axis=0, concat_axis=0, tiled=True),
    )
    key_rows = arrived.reshape(slot_total, features)
    key_ids = arrived_ids.reshape(slot_total)
    scores = density_scores(key_rows, key_ids)
    returned = lax.all_to_all(
        scores.reshape(peer_count, capacity), "gx", split_axis=0, concat_axis=0, tiled=True
    )
    flat_scores = returned.reshape(slot_total)
    pick_mask = target_slot[:, None] == slot_range[None, :]
    return jnp.sum(jnp.where(pick_mask, flat_scores[None, :], 0.0), axis=1)


LANES = 128
PLANE = 4
ID_ROWS = 16
VMEM_BYTES = 16 * 1024 * 1024


def along_rows(values):
    return jnp.broadcast_to(values, (LANES, values.shape[1])).T


def ids_block(ids, width):
    wide = jnp.concatenate([ids, jnp.zeros((1, width - ids.shape[1]), jnp.float32)], axis=1)
    return jnp.broadcast_to(wide, (ID_ROWS, width)).astype(jnp.bfloat16)


def ids_of(ref):
    first = ref.shape[0] - ID_ROWS
    return ref[first:, :].astype(jnp.float32)[:1]


def mate_mass(query_rows, query_ids, key_rows, key_ids, shift=None):
    similar = lax.dot_general(
        query_rows, key_rows, (((1,), (1,)), ((), ())), preferred_element_type=jnp.float32
    )
    repeats = similar.shape[1] // LANES
    mates = jnp.concatenate([query_ids] * repeats, axis=1) == key_ids
    if shift is not None:
        query_pos = lax.broadcasted_iota(jnp.int32, similar.shape, 0) + shift
        key_pos = lax.broadcasted_iota(jnp.int32, similar.shape, 1)
        mates = mates & (query_pos != key_pos)
    return jnp.where(mates, jnp.exp(similar * inverse_temp), 0.0)


def unit_kernel(rows_ref, ids_ref, block_ref, info_ref):
    rows, width = rows_ref.shape
    features = rows_ref[...].astype(jnp.float32)
    scale = lax.rsqrt(jnp.sum(features * features, axis=1, keepdims=True) + 1e-06)
    ids = ids_ref[...].astype(jnp.float32)
    block_ref[:rows, :] = (features * scale).astype(jnp.bfloat16)
    block_ref[rows:, :] = ids_block(ids, width)
    info_ref[:, :rows] = ids
    info_ref[:, rows:] = jnp.broadcast_to(scale, (rows, LANES)).T[:1]


def across_kernel(rows_ref, info_ref, *piece_refs):
    rows, width = rows_ref.shape
    wide = jnp.concatenate([along_rows(info_ref[:, rows:])] * (width // LANES), axis=1)
    units = (rows_ref[...].astype(jnp.float32) * wide).astype(jnp.bfloat16)
    first = 0
    for ref in piece_refs:
        size = min(ref.shape[0], rows - first)
        ref[:size, :] = units[first : first + size]
        first += size
    piece_refs[-1][size:, :] = ids_block(info_ref[:, :rows], width)


def line_sums(moves, query_parts, ids_ref, line_ref, column_ref, sums_ref):
    rows = column_ref.shape[1]
    plane = lax.axis_index("gx") // PLANE
    arrived = functools.reduce(jnp.logical_or, [plane == receiver for _, receiver in moves])
    column_ref[...] = jnp.zeros_like(column_ref)

    @pl.when(arrived)
    def _():
        key_ids = ids_of(line_ref)[:, :rows]
        column = jnp.zeros((1, rows), jnp.float32)
        first = 0
        for query_ref, size in query_parts:
            part = pl.ds(first, size)
            masses = mate_mass(query_ref[:size, :], ids_ref[part, :], line_ref[:rows, :], key_ids)
            column = column + jnp.sum(masses, axis=0, keepdims=True)
            folded = masses[:, :LANES]
            for lane in range(LANES, rows, LANES):
                folded = folded + masses[:, lane : lane + LANES]
            sums_ref[part, :] += folded
            first += size
        column_ref[...] = column


def query_parts_of(refs, rows):
    sizes = [min(ref.shape[0], rows) for ref in refs[:2]]
    sizes += [rows // 2] * (len(refs) - 2)
    return list(zip(refs, sizes))


def first_kernel(moves, line_ref, *refs):
    query_refs, (ids_ref, column_ref, sums_ref, mass_ref) = refs[:-4], refs[-4:]
    rows = mass_ref.shape[1]
    query_parts = query_parts_of(query_refs, rows)
    own_ref = query_refs[0]
    own_ids = ids_of(own_ref)[:, :rows]
    for m, ref in enumerate((query_refs[0], query_refs[1], query_refs[3], query_refs[5])):
        ids_ref[pl.ds(m * rows, rows), :] = along_rows(ids_of(ref)[:, :rows])
    mass = jnp.zeros((1, rows), jnp.float32)
    first = 0
    for ref, size in query_parts:
        shift = first if first < rows else None
        masses = mate_mass(
            ref[:size, :], ids_ref[pl.ds(first, size), :], own_ref[:rows, :], own_ids, shift
        )
        mass = mass + jnp.sum(masses, axis=0, keepdims=True)
        first += size
    mass_ref[...] = mass
    sums_ref[...] = jnp.zeros_like(sums_ref)
    line_sums(moves, query_parts, ids_ref, line_ref, column_ref, sums_ref)


def last_kernel(moves, line_ref, ids_ref, earlier_ref, mass_ref, back_ref, *refs):
    query_refs, refs = refs[: -PLANE - 2], refs[-PLANE - 2 :]
    column_ref, row_refs, sums_ref = refs[0], refs[1:-1], refs[-1]
    rows = column_ref.shape[1]
    sums_ref[...] = earlier_ref[...]
    line_sums(moves, query_parts_of(query_refs, rows), ids_ref, line_ref, column_ref, sums_ref)
    for m in range(PLANE):
        row_sum = jnp.sum(sums_ref[pl.ds(m * rows, rows), :].T, axis=0, keepdims=True)
        if m == 0:
            row_sum = row_sum + mass_ref[...] + back_ref[...]
        row_refs[m][...] = row_sum


def grid_plan(embeddings, cluster_ids):
    peers = lax.axis_size("gx")
    row_count, features = embeddings.shape
    plane_rows = PLANE * row_count
    params = pltpu.CompilerParams(vmem_limit_bytes=VMEM_BYTES)
    small = pl.CostEstimate(flops=1, bytes_accessed=1, transcendentals=0)
    vector = jax.ShapeDtypeStruct((1, row_count), jnp.float32)
    lanes = jax.ShapeDtypeStruct((plane_rows, LANES), jnp.float32)

    def rows_of(count):
        return jax.ShapeDtypeStruct((count, features), jnp.bfloat16)

    def in_plane(value, step):
        return lax.ppermute(value, "gx", [(i, i ^ step) for i in range(peers)])

    def on_line(value, moves):
        pairs = [(a * PLANE + n, b * PLANE + n) for a, b in moves for n in range(PLANE)]
        return lax.ppermute(value, "gx", pairs)

    first_moves = [(0, 1), (1, 2), (2, 3), (3, 0)]
    last_moves = [(0, 2), (3, 1)]
    first_back = [(b, a) for a, b in first_moves]
    last_back = [(b, a) for a, b in last_moves]

    across_raw = in_plane(embeddings, 2)
    block, info = pl.pallas_call(
        unit_kernel,
        out_shape=(
            rows_of(row_count + ID_ROWS),
            jax.ShapeDtypeStruct((1, 2 * row_count), jnp.float32),
        ),
        cost_estimate=small,
        compiler_params=params,
    )(embeddings, cluster_ids.reshape(1, row_count))
    first_line = on_line(block, first_moves)
    last_line = on_line(block, last_moves)
    sibling = in_plane(block, 1)
    across = pl.pallas_call(
        across_kernel,
        out_shape=(rows_of(row_count // 2), rows_of(row_count // 2 + ID_ROWS)),
        cost_estimate=small,
        compiler_params=params,
    )(across_raw, in_plane(info, 2))
    corner = [in_plane(piece, 1) for piece in across]
    queries = (block, sibling, *across, *corner)
    ids, first_column, first_sums, mass = pl.pallas_call(
        functools.partial(first_kernel, first_moves),
        out_shape=(lanes, vector, lanes, vector),
        cost_estimate=small,
        compiler_params=params,
    )(first_line, *queries)
    returned_first = on_line(first_column, first_back)
    last_column, *row_sums = pl.pallas_call(
        functools.partial(last_kernel, last_moves),
        out_shape=[vector] * (1 + PLANE),
        scratch_shapes=[pltpu.VMEM(lanes.shape, lanes.dtype)],
        compiler_params=params,
    )(last_line, ids, first_sums, mass, returned_first, *queries)
    returned = [on_line(last_column, last_back)]
    returned += [in_plane(row_sums[step], step) for step in (2, 3, 1)]
    return jnp.log1p(sum(returned, row_sums[0])).reshape(row_count)


def on_device(embeddings, cluster_ids):
    if lax.axis_size("gx") == 4 * PLANE and embeddings.shape[0] % (2 * LANES) == 0:
        return grid_plan(embeddings, cluster_ids)
    return plain_plan(embeddings, cluster_ids)


def solution(mesh):
    in_specs = (P(("parts", "gx"), None), P(("parts", "gx")))
    out_specs = P(("parts", "gx"))
    return jax.shard_map(
        on_device, mesh=mesh, in_specs=in_specs, out_specs=out_specs, check_vma=False
    )
```

time: 42.7 us -> 44.9 us (1.052)
  waiting for transfers between devices: 18.2 us -> 24.7 us
  starting transfers between devices: 19.4 us -> 15.3 us
  local copies, waits for them, and re-layouts: 1.77 us -> 1.08 us
  Pallas kernels: 2.48 us -> 2.95 us
    ppermute x6 -> x4, waiting for transfers between devices: 10.9 us -> 20.7 us  [on_line(): return lax.ppermute(value, 'gx', pairs)]
    ppermute x6 -> x4, starting transfers between devices: 13.1 us -> 8.85 us  [on_line(): return lax.ppermute(value, 'gx', pairs)]
    ppermute x10 -> x8, waiting for transfers between devices: 7.22 us -> 3.98 us  [in_plane(): return lax.ppermute(value, 'gx', [(i, i ^ step) for i in range(peers)])]
    unnamed x4, local copies, waits for them, and re-layouts: 1.73 us -> 1.08 us
    pallas_call x4, Pallas kernels: 2.48 us -> 2.95 us  [the longest x1 2.33 us: grid_plan(): pl.pallas_call(functools.partial(first_kernel, first_moves), out_shape=(l...]
    ppermute x10 -> x8, starting transfers between devices: 6.29 us -> 6.46 us  [in_plane(): return lax.ppermute(value, 'gx', [(i, i ^ step) for i in range(peers)])]
  transfers between devices with their start and end apart: 16 -> 12, of which waited for: 6 -> 4; matrix products, arithmetic and copies ran while one was open for 0% -> 0% of each run, Pallas kernels for 5% -> 6%
where the time goes in v6:
time: 44.9 us; the launch traced here: 44.7 us
  waiting for transfers between devices  24.7 us (55%)
  starting transfers between devices  15.3 us (34%)
  Pallas kernels  2.95 us (7%)
  local copies, waits for them, and re-layouts  1.08 us (2%)
  other arithmetic  0.58 us (1%)
    ppermute x4, waiting for transfers between devices, on_line(): return lax.ppermute(value, 'gx', pairs)  20.7 us
    ppermute x4, starting transfers between devices, on_line(): return lax.ppermute(value, 'gx', pairs)  8.85 us
    ppermute x8, starting transfers between devices, in_plane(): return lax.ppermute(value, 'gx', [(i, i ^ step) for i in range(peers)])  6.46 us
    ppermute x8, waiting for transfers between devices, in_plane(): return lax.ppermute(value, 'gx', [(i, i ^ step) for i in range(peers)])  3.98 us
    pallas_call x1, Pallas kernels, grid_plan(): pl.pallas_call(functools.partial(first_kernel, first_moves), out_shape=(l...  2.33 us
    unnamed x4, local copies, waits for them, and re-layouts  1.08 us
  transfers between devices with their start and end apart: 12, of which 4 were waited for; matrix products, arithmetic and copies ran while one was open for 0% of the time, Pallas kernels for 6%

profile of v6, /device:TPU:0, one launch (start us, length us, event | category | flops | bytes accessed | tf_op | source)
XLA Modules:
  0.0 44.7 jit_solution(8048510589047972260)
XLA Ops:
  0.0 0.0 copy-start.1
  0.0 2.9 %collective-permute-start.3 = (bf16[256,1024]{1,0:T(8,128)(2,1)}, bf16[256,1024]{1,0:T(8,128)(2,1)S(1)}, u32[]{:S(2)}, u32[]{:S(2)}) collective-permute-start(bf16[256,1024]{1,0:T(8,128)(2,1)} %rows_ref.1), channel_id=1, source_target_pairs={{0,2},{1,3},{2,0},{3,1},{4,6},{5,7},{6,4},{7,5},{8,10},{9,11},{10,... | collective-permute-start | bytes 1572872 | tf_op jit(solution)/shard_map/ppermute | solution.py:214
  2.9 0.0 copy-done.1
  2.9 0.0 copy-start
  2.9 1.1 %copy-done = bf16[256,1024]{1,0:T(8,128)(2,1)S(1)} copy-done((bf16[256,1024]{1,0:T(8,128)(2,1)S(1)}, bf16[256,1024]{1,0:T(8,128)(2,1)}, u32[]{:S(2)}) %copy-start) | copy-done | bytes 524312
  4.0 0.2 shard_map.28
  4.2 0.0 collective-permute-start.2
  4.3 1.6 %collective-permute-start.1 = (bf16[272,1024]{1,0:T(8,128)(2,1)S(1)}, bf16[272,1024]{1,0:T(8,128)(2,1)S(1)}, u32[]{:S(2)}, u32[]{:S(2)}) collective-permute-start(bf16[272,1024]{1,0:T(8,128)(2,1)S(1)} %get-tuple-element.18.refs_0_), channel_id=1, source_target_pairs={{0,4},{1,5},{2,6},{3,7},{4,8},{5,9},{6,10},{7,11},{8,12},{9,13},{1... | collective-permute-start | bytes 1671176 | tf_op jit(solution)/shard_map/ppermute | solution.py:218
  5.9 4.5 %collective-permute-start = (bf16[272,1024]{1,0:T(8,128)(2,1)S(1)}, bf16[272,1024]{1,0:T(8,128)(2,1)S(1)}, u32[]{:S(2)}, u32[]{:S(2)}) collective-permute-start(bf16[272,1024]{1,0:T(8,128)(2,1)S(1)} %get-tuple-element.18.refs_0_), channel_id=1, source_target_pairs={{0,8},{1,9},{2,10},{3,11},{12,4},{13,5},{14,6},{15,7},{16,24},{17,... | collective-permute-start | bytes 1671176 | tf_op jit(solution)/shard_map/ppermute | solution.py:218
  10.4 0.7 %collective-permute-start.4 = (f32[1,512]{1,0:T(1,128)S(1)}, f32[1,512]{1,0:T(1,128)S(1)}, u32[]{:S(2)}, u32[]{:S(2)}) collective-permute-start(f32[1,512]{1,0:T(1,128)S(1)} %get-tuple-element.19), channel_id=1, source_target_pairs={{0,2},{1,3},{2,0},{3,1},{4,6},{5,7},{6,4},{7,5},{8,10},{9,11},{10,... | collective-permute-start | bytes 6152 | tf_op jit(solution)/shard_map/ppermute | solution.py:214
  11.2 4.0 %collective-permute-done.4.info_ref = f32[1,512]{1,0:T(1,128)S(1)} collective-permute-done((f32[1,512]{1,0:T(1,128)S(1)}, f32[1,512]{1,0:T(1,128)S(1)}, u32[]{:S(2)}, u32[]{:S(2)}) %collective-permute-start.4) | collective-permute-done | bytes 2080 | tf_op jit(solution)/shard_map/ppermute | solution.py:214
  15.1 0.0 collective-permute-done.3.rows_ref
  15.1 0.2 shard_map.29
  15.3 0.1 collective-permute-start.6
  15.4 0.5 %collective-permute-start.5 = (bf16[128,1024]{1,0:T(8,128)(2,1)S(1)}, bf16[128,1024]{1,0:T(8,128)(2,1)S(1)}, u32[]{:S(2)}, u32[]{:S(2)}) collective-permute-start(bf16[128,1024]{1,0:T(8,128)(2,1)S(1)} %get-tuple-element.20.refs_2_), channel_id=1, source_target_pairs={{0,1},{1,0},{2,3},{3,2},{4,5},{5,4},{6,7},{7,6},{8,9},{9,8},{10,11... | collective-permute-start | bytes 786440 | tf_op jit(solution)/shard_map/ppermute | solution.py:214
  15.9 0.0 collective-permute-done.2.refs_1_
  15.9 5.7 %collective-permute-done.1.line_ref = bf16[272,1024]{1,0:T(8,128)(2,1)S(1)} collective-permute-done((bf16[272,1024]{1,0:T(8,128)(2,1)S(1)}, bf16[272,1024]{1,0:T(8,128)(2,1)S(1)}, u32[]{:S(2)}, u32[]{:S(2)}) %collective-permute-start.1) | collective-permute-done | bytes 557088 | tf_op jit(solution)/shard_map/ppermute | solution.py:218
  21.6 0.0 collective-permute-done.5.refs_4_
  21.6 0.0 collective-permute-done.6.refs_5_
  21.6 2.3 %shard_map.30 = (f32[1024,128]{1,0:T(8,128)S(1)}, f32[1,256]{1,0:T(1,128)S(1)}, f32[1024,128]{1,0:T(8,128)S(1)}, f32[1,256]{1,0:T(1,128)S(1)}) custom-call(bf16[272,1024]{1,0:T(8,128)(2,1)S(1)} %collective-permute-done.1.line_ref, bf16[272,1024]{1,0:T(8,128)(2,1)S(1)} %get-tuple-element.18.refs_0_, bf16[272,1024]{1,0:T(8,128)(2,1)S(1)} %collective-permute-done.2.refs_1_, ...), custom_call_target="tpu_custom_call" | custom-call | flops 1 | bytes 1 | tf_op jit(solution)/shard_map/pallas_call | solution.py:246
  23.9 1.4 %collective-permute-start.7 = (f32[1,256]{1,0:T(1,128)S(1)}, f32[1,256]{1,0:T(1,128)S(1)}, u32[]{:S(2)}, u32[]{:S(2)}) collective-permute-start(f32[1,256]{1,0:T(1,128)S(1)} %get-tuple-element.25), channel_id=1, source_target_pairs={{4,0},{5,1},{6,2},{7,3},{8,4},{9,5},{10,6},{11,7},{12,8},{13,9},{1... | collective-permute-start | bytes 3080 | tf_op jit(solution)/shard_map/ppermute | solution.py:218
  25.3 5.1 %collective-permute-done.line_ref = bf16[272,1024]{1,0:T(8,128)(2,1)S(1)} collective-permute-done((bf16[272,1024]{1,0:T(8,128)(2,1)S(1)}, bf16[272,1024]{1,0:T(8,128)(2,1)S(1)}, u32[]{:S(2)}, u32[]{:S(2)}) %collective-permute-start) | collective-permute-done | bytes 557088 | tf_op jit(solution)/shard_map/ppermute | solution.py:218
  30.4 0.0 collective-permute-done.7.back_ref
  30.4 0.2 shard_map.31
  30.7 1.3 %collective-permute-start.8 = (f32[1,256]{1,0:T(1,128)S(1)}, f32[1,256]{1,0:T(1,128)S(1)}, u32[]{:S(2)}, u32[]{:S(2)}) collective-permute-start(f32[1,256]{1,0:T(1,128)S(1)} %get-tuple-element.27), channel_id=1, source_target_pairs={{8,0},{9,1},{10,2},{11,3},{4,12},{5,13},{6,14},{7,15},{24,16},{25,... | collective-permute-start | bytes 3080 | tf_op jit(solution)/shard_map/ppermute | solution.py:218
  32.0 0.7 %collective-permute-start.9 = (f32[1,256]{1,0:T(1,128)S(1)}, f32[1,256]{1,0:T(1,128)S(1)}, u32[]{:S(2)}, u32[]{:S(2)}) collective-permute-start(f32[1,256]{1,0:T(1,128)S(1)} %get-tuple-element.28), channel_id=1, source_target_pairs={{0,2},{1,3},{2,0},{3,1},{4,6},{5,7},{6,4},{7,5},{8,10},{9,11},{10,... | collective-permute-start | bytes 3080 | tf_op jit(solution)/shard_map/ppermute | solution.py:214
  32.7 0.4 collective-permute-start.10
  33.0 1.1 %collective-permute-start.11 = (f32[1,256]{1,0:T(1,128)S(1)}, f32[1,256]{1,0:T(1,128)S(1)}, u32[]{:S(2)}, u32[]{:S(2)}) collective-permute-start(f32[1,256]{1,0:T(1,128)S(1)} %get-tuple-element.30), channel_id=1, source_target_pairs={{0,1},{1,0},{2,3},{3,2},{4,5},{5,4},{6,7},{7,6},{8,9},{9,8},{10,11... | collective-permute-start | bytes 3080 | tf_op jit(solution)/shard_map/ppermute | solution.py:214
  34.2 9.9 %collective-permute-done.8 = f32[1,256]{1,0:T(1,128)S(1)} collective-permute-done((f32[1,256]{1,0:T(1,128)S(1)}, f32[1,256]{1,0:T(1,128)S(1)}, u32[]{:S(2)}, u32[]{:S(2)}) %collective-permute-start.8) | collective-permute-done | bytes 1056 | tf_op jit(solution)/shard_map/ppermute | solution.py:218
  44.1 0.0 collective-permute-done.9
  44.1 0.0 collective-permute-done.10
  44.1 0.0 collective-permute-done.11
  44.1 0.6 %add_log-plus-one_fusion = f32[1,256]{1,0:T(1,128)} fusion(f32[1,256]{1,0:T(1,128)S(1)} %collective-permute-done.11, f32[1,256]{1,0:T(1,128)S(1)} %collective-permute-done.10, f32[1,256]{1,0:T(1,128)S(1)} %collective-permute-done.9, f32[1,256]{1,0:T(1,128)S(1)} %get-tuple-element.26, f32[1,256]{1,0:T(1,128)S(1)} %collective-permute-done.8), kind=kLoop, calls=%fused_computation | loop fusion | flops 1024 | bytes 6144 | tf_op jit(solution)/shard_map/log1p | solution.py:261
Async XLA Ops:
  0.0 2.9 %copy-start.1 = (s32[256]{0:T(256)S(1)}, s32[256]{0:T(256)}, u32[]{:S(2)}) copy-start(s32[256]{0:T(256)} %param.3) | copy-start | bytes 3076
  0.0 15.1 %collective-permute-start.3 = (bf16[256,1024]{1,0:T(8,128)(2,1)}, bf16[256,1024]{1,0:T(8,128)(2,1)S(1)}, u32[]{:S(2)}, u32[]{:S(2)}) collective-permute-start(bf16[256,1024]{1,0:T(8,128)(2,1)} %rows_ref.1), channel_id=1, source_target_pairs={{0,2},{1,3},{2,0},{3,1},{4,6},{5,7},{6,4},{7,5},{8,10},{9,11},{10,... | collective-permute-start | bytes 1572872 | tf_op jit(solution)/shard_map/ppermute | solution.py:214
  2.9 1.1 %copy-start = (bf16[256,1024]{1,0:T(8,128)(2,1)S(1)}, bf16[256,1024]{1,0:T(8,128)(2,1)}, u32[]{:S(2)}) copy-start(bf16[256,1024]{1,0:T(8,128)(2,1)} %rows_ref.1) | copy-start | bytes 1572868
  4.2 11.6 %collective-permute-start.2 = (bf16[272,1024]{1,0:T(8,128)(2,1)S(1)}, bf16[272,1024]{1,0:T(8,128)(2,1)S(1)}, u32[]{:S(2)}, u32[]{:S(2)}) collective-permute-start(bf16[272,1024]{1,0:T(8,128)(2,1)S(1)} %get-tuple-element.18.refs_0_), channel_id=1, source_target_pairs={{0,1},{1,0},{2,3},{3,2},{4,5},{5,4},{6,7},{7,6},{8,9},{9,8},{10,11... | collective-permute-start | bytes 1671176 | tf_op jit(solution)/shard_map/ppermute | solution.py:214
  4.3 17.3 %collective-permute-start.1 = (bf16[272,1024]{1,0:T(8,128)(2,1)S(1)}, bf16[272,1024]{1,0:T(8,128)(2,1)S(1)}, u32[]{:S(2)}, u32[]{:S(2)}) collective-permute-start(bf16[272,1024]{1,0:T(8,128)(2,1)S(1)} %get-tuple-element.18.refs_0_), channel_id=1, source_target_pairs={{0,4},{1,5},{2,6},{3,7},{4,8},{5,9},{6,10},{7,11},{8,12},{9,13},{1... | collective-permute-start | bytes 1671176 | tf_op jit(solution)/shard_map/ppermute | solution.py:218
  5.9 24.5 %collective-permute-start = (bf16[272,1024]{1,0:T(8,128)(2,1)S(1)}, bf16[272,1024]{1,0:T(8,128)(2,1)S(1)}, u32[]{:S(2)}, u32[]{:S(2)}) collective-permute-start(bf16[272,1024]{1,0:T(8,128)(2,1)S(1)} %get-tuple-element.18.refs_0_), channel_id=1, source_target_pairs={{0,8},{1,9},{2,10},{3,11},{12,4},{13,5},{14,6},{15,7},{16,24},{17,... | collective-permute-start | bytes 1671176 | tf_op jit(solution)/shard_map/ppermute | solution.py:218
  10.4 4.7 %collective-permute-start.4 = (f32[1,512]{1,0:T(1,128)S(1)}, f32[1,512]{1,0:T(1,128)S(1)}, u32[]{:S(2)}, u32[]{:S(2)}) collective-permute-start(f32[1,512]{1,0:T(1,128)S(1)} %get-tuple-element.19), channel_id=1, source_target_pairs={{0,2},{1,3},{2,0},{3,1},{4,6},{5,7},{6,4},{7,5},{8,10},{9,11},{10,... | collective-permute-start | bytes 6152 | tf_op jit(solution)/shard_map/ppermute | solution.py:214
  15.3 6.3 %collective-permute-start.6 = (bf16[144,1024]{1,0:T(8,128)(2,1)S(1)}, bf16[144,1024]{1,0:T(8,128)(2,1)S(1)}, u32[]{:S(2)}, u32[]{:S(2)}) collective-permute-start(bf16[144,1024]{1,0:T(8,128)(2,1)S(1)} %get-tuple-element.21.refs_3_), channel_id=1, source_target_pairs={{0,1},{1,0},{2,3},{3,2},{4,5},{5,4},{6,7},{7,6},{8,9},{9,8},{10,11... | collective-permute-start | bytes 884744 | tf_op jit(solution)/shard_map/ppermute | solution.py:214
  15.4 6.2 %collective-permute-start.5 = (bf16[128,1024]{1,0:T(8,128)(2,1)S(1)}, bf16[128,1024]{1,0:T(8,128)(2,1)S(1)}, u32[]{:S(2)}, u32[]{:S(2)}) collective-permute-start(bf16[128,1024]{1,0:T(8,128)(2,1)S(1)} %get-tuple-element.20.refs_2_), channel_id=1, source_target_pairs={{0,1},{1,0},{2,3},{3,2},{4,5},{5,4},{6,7},{7,6},{8,9},{9,8},{10,11... | collective-permute-start | bytes 786440 | tf_op jit(solution)/shard_map/ppermute | solution.py:214
  23.9 6.5 %collective-permute-start.7 = (f32[1,256]{1,0:T(1,128)S(1)}, f32[1,256]{1,0:T(1,128)S(1)}, u32[]{:S(2)}, u32[]{:S(2)}) collective-permute-start(f32[1,256]{1,0:T(1,128)S(1)} %get-tuple-element.25), channel_id=1, source_target_pairs={{4,0},{5,1},{6,2},{7,3},{8,4},{9,5},{10,6},{11,7},{12,8},{13,9},{1... | collective-permute-start | bytes 3080 | tf_op jit(solution)/shard_map/ppermute | solution.py:218
  30.7 13.4 %collective-permute-start.8 = (f32[1,256]{1,0:T(1,128)S(1)}, f32[1,256]{1,0:T(1,128)S(1)}, u32[]{:S(2)}, u32[]{:S(2)}) collective-permute-start(f32[1,256]{1,0:T(1,128)S(1)} %get-tuple-element.27), channel_id=1, source_target_pairs={{8,0},{9,1},{10,2},{11,3},{4,12},{5,13},{6,14},{7,15},{24,16},{25,... | collective-permute-start | bytes 3080 | tf_op jit(solution)/shard_map/ppermute | solution.py:218
  32.0 12.1 %collective-permute-start.9 = (f32[1,256]{1,0:T(1,128)S(1)}, f32[1,256]{1,0:T(1,128)S(1)}, u32[]{:S(2)}, u32[]{:S(2)}) collective-permute-start(f32[1,256]{1,0:T(1,128)S(1)} %get-tuple-element.28), channel_id=1, source_target_pairs={{0,2},{1,3},{2,0},{3,1},{4,6},{5,7},{6,4},{7,5},{8,10},{9,11},{10,... | collective-permute-start | bytes 3080 | tf_op jit(solution)/shard_map/ppermute | solution.py:214
  32.7 11.4 %collective-permute-start.10 = (f32[1,256]{1,0:T(1,128)S(1)}, f32[1,256]{1,0:T(1,128)S(1)}, u32[]{:S(2)}, u32[]{:S(2)}) collective-permute-start(f32[1,256]{1,0:T(1,128)S(1)} %get-tuple-element.29), channel_id=1, source_target_pairs={{0,3},{1,2},{2,1},{3,0},{4,7},{5,6},{6,5},{7,4},{8,11},{9,10},{10,... | collective-permute-start | bytes 3080 | tf_op jit(solution)/shard_map/ppermute | solution.py:214
  33.0 11.1 %collective-permute-start.11 = (f32[1,256]{1,0:T(1,128)S(1)}, f32[1,256]{1,0:T(1,128)S(1)}, u32[]{:S(2)}, u32[]{:S(2)}) collective-permute-start(f32[1,256]{1,0:T(1,128)S(1)} %get-tuple-element.30), channel_id=1, source_target_pairs={{0,1},{1,0},{2,3},{3,2},{4,5},{5,4},{6,7},{7,6},{8,9},{9,8},{10,11... | collective-permute-start | bytes 3080 | tf_op jit(solution)/shard_map/ppermute | solution.py:214

commit v7 on v6

--- a/solution.py
+++ b/solution.py
@@ -111,30 +111,31 @@
     return jnp.where(mates, jnp.exp(similar * inverse_temp), 0.0)
 
 
-def unit_kernel(rows_ref, ids_ref, block_ref, info_ref):
+def unit_kernel(rows_ref, ids_ref, units_ref, info_ref, *block_refs):
     rows, width = rows_ref.shape
     features = rows_ref[...].astype(jnp.float32)
     scale = lax.rsqrt(jnp.sum(features * features, axis=1, keepdims=True) + 1e-06)
     ids = ids_ref[...].astype(jnp.float32)
-    block_ref[:rows, :] = (features * scale).astype(jnp.bfloat16)
-    block_ref[rows:, :] = ids_block(ids, width)
+    units = (features * scale).astype(jnp.bfloat16)
+    units_ref[...] = units
     info_ref[:, :rows] = ids
     info_ref[:, rows:] = jnp.broadcast_to(scale, (rows, LANES)).T[:1]
-
-
-def across_kernel(rows_ref, info_ref, *piece_refs):
+    first = 0
+    for ref in block_refs:
+        size = min(ref.shape[0], rows - first)
+        ref[:size, :] = units[first : first + size]
+        if ref.shape[0] > size:
+            ref[size:, :] = ids_block(ids, width)
+        first = (first + size) % rows
+
+
+def scaled_rows(rows_ref, info_ref):
     rows, width = rows_ref.shape
     wide = jnp.concatenate([along_rows(info_ref[:, rows:])] * (width // LANES), axis=1)
-    units = (rows_ref[...].astype(jnp.float32) * wide).astype(jnp.bfloat16)
-    first = 0
-    for ref in piece_refs:
-        size = min(ref.shape[0], rows - first)
-        ref[:size, :] = units[first : first + size]
-        first += size
-    piece_refs[-1][size:, :] = ids_block(info_ref[:, :rows], width)
-
-
-def line_sums(moves, query_parts, ids_ref, line_ref, column_ref, sums_ref):
+    return (rows_ref[...].astype(jnp.float32) * wide).astype(jnp.bfloat16)
+
+
+def line_sums(moves, query_parts, ids_ref, info_ref, line_ref, is_raw, column_ref, sums_ref):
     rows = column_ref.shape[1]
     plane = lax.axis_index("gx") // PLANE
     arrived = functools.reduce(jnp.logical_or, [plane == receiver for _, receiver in moves])
@@ -142,12 +143,13 @@
 
     @pl.when(arrived)
     def _():
-        key_ids = ids_of(line_ref)[:, :rows]
+        key_ids = info_ref[:, :rows]
+        key_rows = scaled_rows(line_ref, info_ref) if is_raw else line_ref[...]
         column = jnp.zeros((1, rows), jnp.float32)
         first = 0
         for query_ref, size in query_parts:
             part = pl.ds(first, size)
-            masses = mate_mass(query_ref[:size, :], ids_ref[part, :], line_ref[:rows, :], key_ids)
+            masses = mate_mass(query_ref[:size, :], ids_ref[part, :], key_rows, key_ids)
             column = column + jnp.sum(masses, axis=0, keepdims=True)
             folded = masses[:, :LANES]
             for lane in range(LANES, rows, LANES):
@@ -158,18 +160,16 @@
 
 
 def query_parts_of(refs, rows):
-    sizes = [min(ref.shape[0], rows) for ref in refs[:2]]
-    sizes += [rows // 2] * (len(refs) - 2)
-    return list(zip(refs, sizes))
-
-
-def first_kernel(moves, line_ref, *refs):
+    return [(ref, rows) for ref in refs[:3]] + [(ref, rows // 2) for ref in refs[3:]]
+
+
+def first_kernel(moves, info_ref, line_ref, *refs):
     query_refs, (ids_ref, column_ref, sums_ref, mass_ref) = refs[:-4], refs[-4:]
     rows = mass_ref.shape[1]
     query_parts = query_parts_of(query_refs, rows)
     own_ref = query_refs[0]
     own_ids = ids_of(own_ref)[:, :rows]
-    for m, ref in enumerate((query_refs[0], query_refs[1], query_refs[3], query_refs[5])):
+    for m, ref in enumerate((*query_refs[:3], query_refs[4])):
         ids_ref[pl.ds(m * rows, rows), :] = along_rows(ids_of(ref)[:, :rows])
     mass = jnp.zeros((1, rows), jnp.float32)
     first = 0
@@ -182,15 +182,16 @@
         first += size
     mass_ref[...] = mass
     sums_ref[...] = jnp.zeros_like(sums_ref)
-    line_sums(moves, query_parts, ids_ref, line_ref, column_ref, sums_ref)
-
-
-def last_kernel(moves, line_ref, ids_ref, earlier_ref, mass_ref, back_ref, *refs):
+    line_sums(moves, query_parts, ids_ref, info_ref, line_ref, True, column_ref, sums_ref)
+
+
+def last_kernel(moves, info_ref, line_ref, ids_ref, earlier_ref, mass_ref, back_ref, *refs):
     query_refs, refs = refs[: -PLANE - 2], refs[-PLANE - 2 :]
     column_ref, row_refs, sums_ref = refs[0], refs[1:-1], refs[-1]
     rows = column_ref.shape[1]
     sums_ref[...] = earlier_ref[...]
-    line_sums(moves, query_parts_of(query_refs, rows), ids_ref, line_ref, column_ref, sums_ref)
+    query_parts = query_parts_of(query_refs, rows)
+    line_sums(moves, query_parts, ids_ref, info_ref, line_ref, False, column_ref, sums_ref)
     for m in range(PLANE):
         row_sum = jnp.sum(sums_ref[pl.ds(m * rows, rows), :].T, axis=0, keepdims=True)
         if m == 0:
@@ -222,40 +223,40 @@
     first_back = [(b, a) for a, b in first_moves]
     last_back = [(b, a) for a, b in last_moves]
 
-    across_raw = in_plane(embeddings, 2)
-    block, info = pl.pallas_call(
+    half = row_count // 2
+    first_line = on_line(embeddings, first_moves)
+    units, info, block = pl.pallas_call(
         unit_kernel,
         out_shape=(
+            rows_of(row_count),
+            jax.ShapeDtypeStruct((1, 2 * row_count), jnp.float32),
             rows_of(row_count + ID_ROWS),
-            jax.ShapeDtypeStruct((1, 2 * row_count), jnp.float32),
         ),
         cost_estimate=small,
         compiler_params=params,
     )(embeddings, cluster_ids.reshape(1, row_count))
-    first_line = on_line(block, first_moves)
-    last_line = on_line(block, last_moves)
+    across = in_plane(block, 2)
     sibling = in_plane(block, 1)
-    across = pl.pallas_call(
-        across_kernel,
-        out_shape=(rows_of(row_count // 2), rows_of(row_count // 2 + ID_ROWS)),
-        cost_estimate=small,
-        compiler_params=params,
-    )(across_raw, in_plane(info, 2))
-    corner = [in_plane(piece, 1) for piece in across]
-    queries = (block, sibling, *across, *corner)
+    first_info, last_info = on_line(info, first_moves), on_line(info, last_moves)
+    first_line, first_info, last_info, units = lax.optimization_barrier(
+        (first_line, first_info, last_info, units)
+    )
+    last_line = on_line(units, last_moves)
+    corner = [in_plane(piece, 1) for piece in (across[:half], across[half:])]
+    queries = (block, sibling, across, *corner)
     ids, first_column, first_sums, mass = pl.pallas_call(
         functools.partial(first_kernel, first_moves),
         out_shape=(lanes, vector, lanes, vector),
         cost_estimate=small,
         compiler_params=params,
-    )(first_line, *queries)
+    )(first_info, first_line, *queries)
     returned_first = on_line(first_column, first_back)
     last_column, *row_sums = pl.pallas_call(
         functools.partial(last_kernel, last_moves),
         out_shape=[vector] * (1 + PLANE),
         scratch_shapes=[pltpu.VMEM(lanes.shape, lanes.dtype)],
         compiler_params=params,
-    )(last_line, ids, first_sums, mass, returned_first, *queries)
+    )(last_info, last_line, ids, first_sums, mass, returned_first, *queries)
     returned = [on_line(last_column, last_back)]
     returned += [in_plane(row_sums[step], step) for step in (2, 3, 1)]
     return jnp.log1p(sum(returned, row_sums[0])).reshape(row_count)

time: 44.9 us -> 39.5 us (0.88)
  the two profiles are of different devices: /device:TPU:0 before, /device:TPU:8 now
where the time goes in v7:
time: 39.5 us; the launch traced here: 39.3 us
  waiting for transfers between devices  19.4 us (49%)
  starting transfers between devices  14.7 us (37%)
  Pallas kernels  3.48 us (9%)
  local copies, waits for them, and re-layouts  1.11 us (3%)
  other arithmetic  0.58 us (1%)
    ppermute x6, waiting for transfers between devices, on_line(): return lax.ppermute(value, 'gx', pairs)  14.8 us
    ppermute x6, starting transfers between devices, on_line(): return lax.ppermute(value, 'gx', pairs)  10.3 us
    ppermute x7, waiting for transfers between devices, in_plane(): return lax.ppermute(value, 'gx', [(i, i ^ step) for i in range(peers)])  4.62 us
    ppermute x7, starting transfers between devices, in_plane(): return lax.ppermute(value, 'gx', [(i, i ^ step) for i in range(peers)])  4.37 us
    pallas_call x1, Pallas kernels, grid_plan(): pl.pallas_call(functools.partial(first_kernel, first_moves), out_shape=(l...  2.03 us
    pallas_call x1, Pallas kernels, grid_plan(): pl.pallas_call(functools.partial(last_kernel, last_moves), out_shape=[vec...  1.23 us
    unnamed x4, local copies, waits for them, and re-layouts  1.08 us
  transfers between devices with their start and end apart: 13, of which 7 were waited for; matrix products, arithmetic and copies ran while one was open for 0% of the time, Pallas kernels for 6%

profile of v7, /device:TPU:8, one launch (start us, length us, event | category | flops | bytes accessed | tf_op | source)
XLA Modules:
  0.0 39.3 jit_solution(13846072541794519527)
XLA Ops:
  0.0 0.0 copy-start.1
  0.0 1.6 %collective-permute-start = (bf16[256,1024]{1,0:T(8,128)(2,1)}, bf16[256,1024]{1,0:T(8,128)(2,1)S(1)}, u32[]{:S(2)}, u32[]{:S(2)}) collective-permute-start(bf16[256,1024]{1,0:T(8,128)(2,1)} %rows_ref.1), channel_id=1, source_target_pairs={{0,4},{1,5},{2,6},{3,7},{4,8},{5,9},{6,10},{7,11},{8,12},{9,13},{1... | collective-permute-start | bytes 1572872 | tf_op jit(solution)/shard_map/ppermute | solution.py:219
  1.6 0.0 copy-done.1
  1.6 0.0 copy-start
  1.6 1.1 %copy-done = bf16[256,1024]{1,0:T(8,128)(2,1)S(1)} copy-done((bf16[256,1024]{1,0:T(8,128)(2,1)S(1)}, bf16[256,1024]{1,0:T(8,128)(2,1)}, u32[]{:S(2)}) %copy-start) | copy-done | bytes 524312
  2.7 0.2 shard_map.28
  2.9 1.5 %collective-permute-start.5 = (bf16[272,1024]{1,0:T(8,128)(2,1)S(1)}, bf16[272,1024]{1,0:T(8,128)(2,1)S(1)}, u32[]{:S(2)}, u32[]{:S(2)}) collective-permute-start(bf16[272,1024]{1,0:T(8,128)(2,1)S(1)} %get-tuple-element.27.refs_0_), channel_id=1, source_target_pairs={{0,2},{1,3},{2,0},{3,1},{4,6},{5,7},{6,4},{7,5},{8,10},{9,11},{10,... | collective-permute-start | bytes 1671176 | tf_op jit(solution)/shard_map/ppermute | solution.py:215
  4.4 0.0 collective-permute-start.4
  4.4 1.3 %collective-permute-start.2 = (f32[1,512]{1,0:T(1,128)S(1)}, f32[1,512]{1,0:T(1,128)S(1)}, u32[]{:S(2)}, u32[]{:S(2)}) collective-permute-start(f32[1,512]{1,0:T(1,128)S(1)} %get-tuple-element.21), channel_id=1, source_target_pairs={{0,8},{1,9},{2,10},{3,11},{12,4},{13,5},{14,6},{15,7},{16,24},{17,... | collective-permute-start | bytes 6152 | tf_op jit(solution)/shard_map/ppermute | solution.py:219
  5.7 1.6 %collective-permute-start.1 = (f32[1,512]{1,0:T(1,128)S(1)}, f32[1,512]{1,0:T(1,128)S(1)}, u32[]{:S(2)}, u32[]{:S(2)}) collective-permute-start(f32[1,512]{1,0:T(1,128)S(1)} %get-tuple-element.21), channel_id=1, source_target_pairs={{0,4},{1,5},{2,6},{3,7},{4,8},{5,9},{6,10},{7,11},{8,12},{9,13},{1... | collective-permute-start | bytes 6152 | tf_op jit(solution)/shard_map/ppermute | solution.py:219
  7.3 7.5 %collective-permute-done.2.info_ref = f32[1,512]{1,0:T(1,128)S(1)} collective-permute-done((f32[1,512]{1,0:T(1,128)S(1)}, f32[1,512]{1,0:T(1,128)S(1)}, u32[]{:S(2)}, u32[]{:S(2)}) %collective-permute-start.2) | collective-permute-done | bytes 2080 | tf_op jit(solution)/shard_map/ppermute | solution.py:219
  14.8 0.0 collective-permute-done.1.info_ref
  14.8 0.0 collective-permute-done.line_ref
  14.8 1.3 %collective-permute-start.3 = (bf16[256,1024]{1,0:T(8,128)(2,1)S(1)}, bf16[256,1024]{1,0:T(8,128)(2,1)S(1)}, u32[]{:S(2)}, u32[]{:S(2)}) collective-permute-start(bf16[256,1024]{1,0:T(8,128)(2,1)S(1)} %get-tuple-element.24), channel_id=1, source_target_pairs={{0,8},{1,9},{2,10},{3,11},{12,4},{13,5},{14,6},{15,7},{16,24},{17,... | collective-permute-start | bytes 1572872 | tf_op jit(solution)/shard_map/ppermute | solution.py:219
  16.1 0.9 %collective-permute-done.5.refs_2_ = bf16[272,1024]{1,0:T(8,128)(2,1)S(1)} collective-permute-done((bf16[272,1024]{1,0:T(8,128)(2,1)S(1)}, bf16[272,1024]{1,0:T(8,128)(2,1)S(1)}, u32[]{:S(2)}, u32[]{:S(2)}) %collective-permute-start.5) | collective-permute-done | bytes 557088 | tf_op jit(solution)/shard_map/ppermute | solution.py:215
  17.0 0.1 collective-permute-start.7
  17.1 0.6 %collective-permute-start.6 = (bf16[128,1024]{1,0:T(8,128)(2,1)S(1)}, bf16[128,1024]{1,0:T(8,128)(2,1)S(1)}, u32[]{:S(2)}, u32[]{:S(2)}) collective-permute-start(bf16[128,1024]{1,0:T(8,128)(2,1)S(1)} %slice.8), channel_id=1, source_target_pairs={{0,1},{1,0},{2,3},{3,2},{4,5},{5,4},{6,7},{7,6},{8,9},{9,8},{10,11... | collective-permute-start | bytes 786440 | tf_op jit(solution)/shard_map/ppermute | solution.py:215
  17.7 0.0 collective-permute-done.4.refs_1_
  17.7 1.4 %collective-permute-done.6.refs_3_ = bf16[128,1024]{1,0:T(8,128)(2,1)S(1)} collective-permute-done((bf16[128,1024]{1,0:T(8,128)(2,1)S(1)}, bf16[128,1024]{1,0:T(8,128)(2,1)S(1)}, u32[]{:S(2)}, u32[]{:S(2)}) %collective-permute-start.6) | collective-permute-done | bytes 262176 | tf_op jit(solution)/shard_map/ppermute | solution.py:215
  19.1 0.0 collective-permute-done.7.refs_4_
  19.1 2.0 %shard_map.29 = (f32[1024,128]{1,0:T(8,128)S(1)}, f32[1,256]{1,0:T(1,128)S(1)}, f32[1024,128]{1,0:T(8,128)S(1)}, f32[1,256]{1,0:T(1,128)S(1)}) custom-call(f32[1,512]{1,0:T(1,128)S(1)} %collective-permute-done.1.info_ref, bf16[256,1024]{1,0:T(8,128)(2,1)S(1)} %collective-permute-done.line_ref, bf16[272,1024]{1,0:T(8,128)(2,1)S(1)} %get-tuple-element.27.refs_0_, ...), custom_call_target="tpu_custom_call" | custom-call | flops 1 | bytes 1 | tf_op jit(solution)/shard_map/pallas_call | solution.py:247
  21.1 2.0 %collective-permute-start.8 = (f32[1,256]{1,0:T(1,128)S(1)}, f32[1,256]{1,0:T(1,128)S(1)}, u32[]{:S(2)}, u32[]{:S(2)}) collective-permute-start(f32[1,256]{1,0:T(1,128)S(1)} %get-tuple-element.31), channel_id=1, source_target_pairs={{4,0},{5,1},{6,2},{7,3},{8,4},{9,5},{10,6},{11,7},{12,8},{13,9},{1... | collective-permute-start | bytes 3080 | tf_op jit(solution)/shard_map/ppermute | solution.py:219
  23.1 1.7 %collective-permute-done.8.back_ref = f32[1,256]{1,0:T(1,128)S(1)} collective-permute-done((f32[1,256]{1,0:T(1,128)S(1)}, f32[1,256]{1,0:T(1,128)S(1)}, u32[]{:S(2)}, u32[]{:S(2)}) %collective-permute-start.8) | collective-permute-done | bytes 1056 | tf_op jit(solution)/shard_map/ppermute | solution.py:219
  24.8 5.6 %collective-permute-done.3.line_ref = bf16[256,1024]{1,0:T(8,128)(2,1)S(1)} collective-permute-done((bf16[256,1024]{1,0:T(8,128)(2,1)S(1)}, bf16[256,1024]{1,0:T(8,128)(2,1)S(1)}, u32[]{:S(2)}, u32[]{:S(2)}) %collective-permute-start.3) | collective-permute-done | bytes 524320 | tf_op jit(solution)/shard_map/ppermute | solution.py:219
  30.4 1.2 %shard_map.30 = (f32[1,256]{1,0:T(1,128)S(1)}, f32[1,256]{1,0:T(1,128)S(1)}, f32[1,256]{1,0:T(1,128)S(1)}, f32[1,256]{1,0:T(1,128)S(1)}, f32[1,256]{1,0:T(1,128)S(1)}) custom-call(f32[1,512]{1,0:T(1,128)S(1)} %collective-permute-done.2.info_ref, bf16[256,1024]{1,0:T(8,128)(2,1)S(1)} %collective-permute-done.3.line_ref, ...), custom_call_target="tpu_custom_call" | custom-call | tf_op jit(solution)/shard_map/pallas_call | solution.py:254
  31.6 2.5 %collective-permute-start.9 = (f32[1,256]{1,0:T(1,128)S(1)}, f32[1,256]{1,0:T(1,128)S(1)}, u32[]{:S(2)}, u32[]{:S(2)}) collective-permute-start(f32[1,256]{1,0:T(1,128)S(1)} %get-tuple-element.33), channel_id=1, source_target_pairs={{8,0},{9,1},{10,2},{11,3},{4,12},{5,13},{6,14},{7,15},{24,16},{25,... | collective-permute-start | bytes 3080 | tf_op jit(solution)/shard_map/ppermute | solution.py:219
  34.2 1.6 %collective-permute-start.10 = (f32[1,256]{1,0:T(1,128)S(1)}, f32[1,256]{1,0:T(1,128)S(1)}, u32[]{:S(2)}, u32[]{:S(2)}) collective-permute-start(f32[1,256]{1,0:T(1,128)S(1)} %get-tuple-element.34), channel_id=1, source_target_pairs={{0,2},{1,3},{2,0},{3,1},{4,6},{5,7},{6,4},{7,5},{8,10},{9,11},{10,... | collective-permute-start | bytes 3080 | tf_op jit(solution)/shard_map/ppermute | solution.py:215
  35.7 0.0 collective-permute-start.11
  35.7 0.6 %collective-permute-start.12 = (f32[1,256]{1,0:T(1,128)S(1)}, f32[1,256]{1,0:T(1,128)S(1)}, u32[]{:S(2)}, u32[]{:S(2)}) collective-permute-start(f32[1,256]{1,0:T(1,128)S(1)} %get-tuple-element.36), channel_id=1, source_target_pairs={{0,1},{1,0},{2,3},{3,2},{4,5},{5,4},{6,7},{7,6},{8,9},{9,8},{10,11... | collective-permute-start | bytes 3080 | tf_op jit(solution)/shard_map/ppermute | solution.py:215
  36.4 0.0 collective-permute-done.9
  36.4 1.4 %collective-permute-done.10 = f32[1,256]{1,0:T(1,128)S(1)} collective-permute-done((f32[1,256]{1,0:T(1,128)S(1)}, f32[1,256]{1,0:T(1,128)S(1)}, u32[]{:S(2)}, u32[]{:S(2)}) %collective-permute-start.10) | collective-permute-done | bytes 1056 | tf_op jit(solution)/shard_map/ppermute | solution.py:215
  37.8 0.9 %collective-permute-done.11 = f32[1,256]{1,0:T(1,128)S(1)} collective-permute-done((f32[1,256]{1,0:T(1,128)S(1)}, f32[1,256]{1,0:T(1,128)S(1)}, u32[]{:S(2)}, u32[]{:S(2)}) %collective-permute-start.11) | collective-permute-done | bytes 1056 | tf_op jit(solution)/shard_map/ppermute | solution.py:215
  38.7 0.0 collective-permute-done.12
  38.7 0.6 %add_log-plus-one_fusion = f32[1,256]{1,0:T(1,128)} fusion(f32[1,256]{1,0:T(1,128)S(1)} %collective-permute-done.12, f32[1,256]{1,0:T(1,128)S(1)} %collective-permute-done.11, f32[1,256]{1,0:T(1,128)S(1)} %collective-permute-done.10, f32[1,256]{1,0:T(1,128)S(1)} %get-tuple-element.32, f32[1,256]{1,0:T(1,128)S(1)} %collective-permute-done.9), kind=kLoop, calls=%fused_computation | loop fusion | flops 1024 | bytes 6144 | tf_op jit(solution)/shard_map/log1p | solution.py:262
  (2 shorter events, 0.0 us)
Async XLA Ops:
  0.0 1.6 %copy-start.1 = (s32[256]{0:T(256)S(1)}, s32[256]{0:T(256)}, u32[]{:S(2)}) copy-start(s32[256]{0:T(256)} %param.3) | copy-start | bytes 3076
  0.0 14.8 %collective-permute-start = (bf16[256,1024]{1,0:T(8,128)(2,1)}, bf16[256,1024]{1,0:T(8,128)(2,1)S(1)}, u32[]{:S(2)}, u32[]{:S(2)}) collective-permute-start(bf16[256,1024]{1,0:T(8,128)(2,1)} %rows_ref.1), channel_id=1, source_target_pairs={{0,4},{1,5},{2,6},{3,7},{4,8},{5,9},{6,10},{7,11},{8,12},{9,13},{1... | collective-permute-start | bytes 1572872 | tf_op jit(solution)/shard_map/ppermute | solution.py:219
  1.6 1.1 %copy-start = (bf16[256,1024]{1,0:T(8,128)(2,1)S(1)}, bf16[256,1024]{1,0:T(8,128)(2,1)}, u32[]{:S(2)}) copy-start(bf16[256,1024]{1,0:T(8,128)(2,1)} %rows_ref.1) | copy-start | bytes 1572868
  2.9 14.1 %collective-permute-start.5 = (bf16[272,1024]{1,0:T(8,128)(2,1)S(1)}, bf16[272,1024]{1,0:T(8,128)(2,1)S(1)}, u32[]{:S(2)}, u32[]{:S(2)}) collective-permute-start(bf16[272,1024]{1,0:T(8,128)(2,1)S(1)} %get-tuple-element.27.refs_0_), channel_id=1, source_target_pairs={{0,2},{1,3},{2,0},{3,1},{4,6},{5,7},{6,4},{7,5},{8,10},{9,11},{10,... | collective-permute-start | bytes 1671176 | tf_op jit(solution)/shard_map/ppermute | solution.py:215
  4.4 13.3 %collective-permute-start.4 = (bf16[272,1024]{1,0:T(8,128)(2,1)S(1)}, bf16[272,1024]{1,0:T(8,128)(2,1)S(1)}, u32[]{:S(2)}, u32[]{:S(2)}) collective-permute-start(bf16[272,1024]{1,0:T(8,128)(2,1)S(1)} %get-tuple-element.27.refs_0_), channel_id=1, source_target_pairs={{0,1},{1,0},{2,3},{3,2},{4,5},{5,4},{6,7},{7,6},{8,9},{9,8},{10,11... | collective-permute-start | bytes 1671176 | tf_op jit(solution)/shard_map/ppermute | solution.py:215
  4.4 10.4 %collective-permute-start.2 = (f32[1,512]{1,0:T(1,128)S(1)}, f32[1,512]{1,0:T(1,128)S(1)}, u32[]{:S(2)}, u32[]{:S(2)}) collective-permute-start(f32[1,512]{1,0:T(1,128)S(1)} %get-tuple-element.21), channel_id=1, source_target_pairs={{0,8},{1,9},{2,10},{3,11},{12,4},{13,5},{14,6},{15,7},{16,24},{17,... | collective-permute-start | bytes 6152 | tf_op jit(solution)/shard_map/ppermute | solution.py:219
  5.7 9.1 %collective-permute-start.1 = (f32[1,512]{1,0:T(1,128)S(1)}, f32[1,512]{1,0:T(1,128)S(1)}, u32[]{:S(2)}, u32[]{:S(2)}) collective-permute-start(f32[1,512]{1,0:T(1,128)S(1)} %get-tuple-element.21), channel_id=1, source_target_pairs={{0,4},{1,5},{2,6},{3,7},{4,8},{5,9},{6,10},{7,11},{8,12},{9,13},{1... | collective-permute-start | bytes 6152 | tf_op jit(solution)/shard_map/ppermute | solution.py:219
  14.8 15.6 %collective-permute-start.3 = (bf16[256,1024]{1,0:T(8,128)(2,1)S(1)}, bf16[256,1024]{1,0:T(8,128)(2,1)S(1)}, u32[]{:S(2)}, u32[]{:S(2)}) collective-permute-start(bf16[256,1024]{1,0:T(8,128)(2,1)S(1)} %get-tuple-element.24), channel_id=1, source_target_pairs={{0,8},{1,9},{2,10},{3,11},{12,4},{13,5},{14,6},{15,7},{16,24},{17,... | collective-permute-start | bytes 1572872 | tf_op jit(solution)/shard_map/ppermute | solution.py:219
  17.0 2.0 %collective-permute-start.7 = (bf16[144,1024]{1,0:T(8,128)(2,1)S(1)}, bf16[144,1024]{1,0:T(8,128)(2,1)S(1)}, u32[]{:S(2)}, u32[]{:S(2)}) collective-permute-start(bf16[144,1024]{1,0:T(8,128)(2,1)S(1)} %slice.9), channel_id=1, source_target_pairs={{0,1},{1,0},{2,3},{3,2},{4,5},{5,4},{6,7},{7,6},{8,9},{9,8},{10,11... | collective-permute-start | bytes 884744 | tf_op jit(solution)/shard_map/ppermute | solution.py:215
  17.1 1.9 %collective-permute-start.6 = (bf16[128,1024]{1,0:T(8,128)(2,1)S(1)}, bf16[128,1024]{1,0:T(8,128)(2,1)S(1)}, u32[]{:S(2)}, u32[]{:S(2)}) collective-permute-start(bf16[128,1024]{1,0:T(8,128)(2,1)S(1)} %slice.8), channel_id=1, source_target_pairs={{0,1},{1,0},{2,3},{3,2},{4,5},{5,4},{6,7},{7,6},{8,9},{9,8},{10,11... | collective-permute-start | bytes 786440 | tf_op jit(solution)/shard_map/ppermute | solution.py:215
  21.1 3.7 %collective-permute-start.8 = (f32[1,256]{1,0:T(1,128)S(1)}, f32[1,256]{1,0:T(1,128)S(1)}, u32[]{:S(2)}, u32[]{:S(2)}) collective-permute-start(f32[1,256]{1,0:T(1,128)S(1)} %get-tuple-element.31), channel_id=1, source_target_pairs={{4,0},{5,1},{6,2},{7,3},{8,4},{9,5},{10,6},{11,7},{12,8},{13,9},{1... | collective-permute-start | bytes 3080 | tf_op jit(solution)/shard_map/ppermute | solution.py:219
  31.6 4.8 %collective-permute-start.9 = (f32[1,256]{1,0:T(1,128)S(1)}, f32[1,256]{1,0:T(1,128)S(1)}, u32[]{:S(2)}, u32[]{:S(2)}) collective-permute-start(f32[1,256]{1,0:T(1,128)S(1)} %get-tuple-element.33), channel_id=1, source_target_pairs={{8,0},{9,1},{10,2},{11,3},{4,12},{5,13},{6,14},{7,15},{24,16},{25,... | collective-permute-start | bytes 3080 | tf_op jit(solution)/shard_map/ppermute | solution.py:219
  34.2 3.6 %collective-permute-start.10 = (f32[1,256]{1,0:T(1,128)S(1)}, f32[1,256]{1,0:T(1,128)S(1)}, u32[]{:S(2)}, u32[]{:S(2)}) collective-permute-start(f32[1,256]{1,0:T(1,128)S(1)} %get-tuple-element.34), channel_id=1, source_target_pairs={{0,2},{1,3},{2,0},{3,1},{4,6},{5,7},{6,4},{7,5},{8,10},{9,11},{10,... | collective-permute-start | bytes 3080 | tf_op jit(solution)/shard_map/ppermute | solution.py:215
  35.7 3.0 %collective-permute-start.11 = (f32[1,256]{1,0:T(1,128)S(1)}, f32[1,256]{1,0:T(1,128)S(1)}, u32[]{:S(2)}, u32[]{:S(2)}) collective-permute-start(f32[1,256]{1,0:T(1,128)S(1)} %get-tuple-element.35), channel_id=1, source_target_pairs={{0,3},{1,2},{2,1},{3,0},{4,7},{5,6},{6,5},{7,4},{8,11},{9,10},{10,... | collective-permute-start | bytes 3080 | tf_op jit(solution)/shard_map/ppermute | solution.py:215
  35.7 3.0 %collective-permute-start.12 = (f32[1,256]{1,0:T(1,128)S(1)}, f32[1,256]{1,0:T(1,128)S(1)}, u32[]{:S(2)}, u32[]{:S(2)}) collective-permute-start(f32[1,256]{1,0:T(1,128)S(1)} %get-tuple-element.36), channel_id=1, source_target_pairs={{0,1},{1,0},{2,3},{3,2},{4,5},{5,4},{6,7},{7,6},{8,9},{9,8},{10,11... | collective-permute-start | bytes 3080 | tf_op jit(solution)/shard_map/ppermute | solution.py:215

commit v8 on v6

--- a/solution.py
+++ b/solution.py
@@ -111,27 +111,19 @@
     return jnp.where(mates, jnp.exp(similar * inverse_temp), 0.0)
 
 
-def unit_kernel(rows_ref, ids_ref, block_ref, info_ref):
+def unit_kernel(rows_ref, ids_ref, *block_refs):
     rows, width = rows_ref.shape
     features = rows_ref[...].astype(jnp.float32)
     scale = lax.rsqrt(jnp.sum(features * features, axis=1, keepdims=True) + 1e-06)
-    ids = ids_ref[...].astype(jnp.float32)
-    block_ref[:rows, :] = (features * scale).astype(jnp.bfloat16)
-    block_ref[rows:, :] = ids_block(ids, width)
-    info_ref[:, :rows] = ids
-    info_ref[:, rows:] = jnp.broadcast_to(scale, (rows, LANES)).T[:1]
-
-
-def across_kernel(rows_ref, info_ref, *piece_refs):
-    rows, width = rows_ref.shape
-    wide = jnp.concatenate([along_rows(info_ref[:, rows:])] * (width // LANES), axis=1)
-    units = (rows_ref[...].astype(jnp.float32) * wide).astype(jnp.bfloat16)
+    units = (features * scale).astype(jnp.bfloat16)
+    ids = ids_block(ids_ref[...].astype(jnp.float32), width)
     first = 0
-    for ref in piece_refs:
+    for ref in block_refs:
         size = min(ref.shape[0], rows - first)
         ref[:size, :] = units[first : first + size]
-        first += size
-    piece_refs[-1][size:, :] = ids_block(info_ref[:, :rows], width)
+        if ref.shape[0] > size:
+            ref[size:, :] = ids
+        first = (first + size) % rows
 
 
 def line_sums(moves, query_parts, ids_ref, line_ref, column_ref, sums_ref):
@@ -158,8 +150,8 @@
 
 
 def query_parts_of(refs, rows):
-    sizes = [min(ref.shape[0], rows) for ref in refs[:2]]
-    sizes += [rows // 2] * (len(refs) - 2)
+    head = refs[2].shape[0]
+    sizes = [rows, rows] + [head, rows - head] * (PLANE - 2)
     return list(zip(refs, sizes))
 
 
@@ -169,7 +161,7 @@
     query_parts = query_parts_of(query_refs, rows)
     own_ref = query_refs[0]
     own_ids = ids_of(own_ref)[:, :rows]
-    for m, ref in enumerate((query_refs[0], query_refs[1], query_refs[3], query_refs[5])):
+    for m, ref in enumerate((*query_refs[:2], query_refs[3], query_refs[5])):
         ids_ref[pl.ds(m * rows, rows), :] = along_rows(ids_of(ref)[:, :rows])
     mass = jnp.zeros((1, rows), jnp.float32)
     first = 0
@@ -190,7 +182,8 @@
     column_ref, row_refs, sums_ref = refs[0], refs[1:-1], refs[-1]
     rows = column_ref.shape[1]
     sums_ref[...] = earlier_ref[...]
-    line_sums(moves, query_parts_of(query_refs, rows), ids_ref, line_ref, column_ref, sums_ref)
+    query_parts = query_parts_of(query_refs, rows)
+    line_sums(moves, query_parts, ids_ref, line_ref, column_ref, sums_ref)
     for m in range(PLANE):
         row_sum = jnp.sum(sums_ref[pl.ds(m * rows, rows), :].T, axis=0, keepdims=True)
         if m == 0:
@@ -218,29 +211,26 @@
         return lax.ppermute(value, "gx", pairs)
 
     first_moves = [(0, 1), (1, 2), (2, 3), (3, 0)]
-    last_moves = [(0, 2), (3, 1)]
+    last_moves = [(1, 3), (2, 0)]
     first_back = [(b, a) for a, b in first_moves]
     last_back = [(b, a) for a, b in last_moves]
 
-    across_raw = in_plane(embeddings, 2)
-    block, info = pl.pallas_call(
+    head = 3 * row_count // 8
+    block, *pieces = pl.pallas_call(
         unit_kernel,
         out_shape=(
             rows_of(row_count + ID_ROWS),
-            jax.ShapeDtypeStruct((1, 2 * row_count), jnp.float32),
+            rows_of(head),
+            rows_of(row_count - head + ID_ROWS),
         ),
         cost_estimate=small,
         compiler_params=params,
     )(embeddings, cluster_ids.reshape(1, row_count))
     first_line = on_line(block, first_moves)
     last_line = on_line(block, last_moves)
+    across = [in_plane(piece, 2) for piece in pieces]
     sibling = in_plane(block, 1)
-    across = pl.pallas_call(
-        across_kernel,
-        out_shape=(rows_of(row_count // 2), rows_of(row_count // 2 + ID_ROWS)),
-        cost_estimate=small,
-        compiler_params=params,
-    )(across_raw, in_plane(info, 2))
+    first_line, across[1] = lax.optimization_barrier((first_line, across[1]))
     corner = [in_plane(piece, 1) for piece in across]
     queries = (block, sibling, *across, *corner)
     ids, first_column, first_sums, mass = pl.pallas_call(

time: 44.9 us -> 47.3 us (1.053)
  starting transfers between devices: 15.3 us -> 24.3 us
  waiting for transfers between devices: 24.7 us -> 16.5 us
  Pallas kernels: 2.95 us -> 3.92 us
  local copies, waits for them, and re-layouts: 1.08 us -> 1.72 us
    ppermute x4, waiting for transfers between devices: 20.7 us -> 4.71 us  [on_line(): return lax.ppermute(value, 'gx', pairs)]
    ppermute x4, starting transfers between devices: 8.85 us -> 19.5 us  [on_line(): return lax.ppermute(value, 'gx', pairs)]
    ppermute x8, waiting for transfers between devices: 3.98 us -> 11.8 us  [in_plane(): return lax.ppermute(value, 'gx', [(i, i ^ step) for i in range(peers)])]
    ppermute x8, starting transfers between devices: 6.46 us -> 4.81 us  [in_plane(): return lax.ppermute(value, 'gx', [(i, i ^ step) for i in range(peers)])]
    pallas_call x1, Pallas kernels: 0.24 us -> 1.41 us  [grid_plan(): pl.pallas_call(functools.partial(last_kernel, last_moves), out_shape=[vec...]
    unnamed x4, local copies, waits for them, and re-layouts: 1.08 us -> 1.72 us
  transfers between devices with their start and end apart: 12 -> 12, of which waited for: 4 -> 6; matrix products, arithmetic and copies ran while one was open for 0% -> 0% of each run, Pallas kernels for 6% -> 5%
where the time goes in v8:
time: 47.3 us; the launch traced here: 47.1 us
  starting transfers between devices  24.3 us (51%)
  waiting for transfers between devices  16.5 us (35%)
  Pallas kernels  3.92 us (8%)
  local copies, waits for them, and re-layouts  1.72 us (4%)
  other arithmetic  0.58 us (1%)
    ppermute x4, starting transfers between devices, on_line(): return lax.ppermute(value, 'gx', pairs)  19.5 us
    ppermute x8, waiting for transfers between devices, in_plane(): return lax.ppermute(value, 'gx', [(i, i ^ step) for i in range(peers)])  11.8 us
    ppermute x8, starting transfers between devices, in_plane(): return lax.ppermute(value, 'gx', [(i, i ^ step) for i in range(peers)])  4.81 us
    ppermute x4, waiting for transfers between devices, on_line(): return lax.ppermute(value, 'gx', pairs)  4.71 us
    pallas_call x1, Pallas kernels, grid_plan(): pl.pallas_call(functools.partial(first_kernel, first_moves), out_shape=(l...  2.32 us
    unnamed x4, local copies, waits for them, and re-layouts  1.72 us
    pallas_call x1, Pallas kernels, grid_plan(): pl.pallas_call(functools.partial(last_kernel, last_moves), out_shape=[vec...  1.41 us
  transfers between devices with their start and end apart: 12, of which 6 were waited for; matrix products, arithmetic and copies ran while one was open for 0% of the time, Pallas kernels for 5%

profile of v8, /device:TPU:0, one launch (start us, length us, event | category | flops | bytes accessed | tf_op | source)
XLA Modules:
  0.0 47.1 jit_solution(18028145171954358228)
XLA Ops:
  0.0 0.0 copy-start.1
  0.0 0.7 %copy-done.1 = s32[256]{0:T(256)S(1)} copy-done((s32[256]{0:T(256)S(1)}, s32[256]{0:T(256)}, u32[]{:S(2)}) %copy-start.1) | copy-done | bytes 1048
  0.7 0.0 copy-start
  0.7 1.0 %copy-done = bf16[256,1024]{1,0:T(8,128)(2,1)S(1)} copy-done((bf16[256,1024]{1,0:T(8,128)(2,1)S(1)}, bf16[256,1024]{1,0:T(8,128)(2,1)}, u32[]{:S(2)}) %copy-start) | copy-done | bytes 524312
  1.7 0.2 shard_map.28
  1.9 3.1 %collective-permute-start.1 = (bf16[272,1024]{1,0:T(8,128)(2,1)S(1)}, bf16[272,1024]{1,0:T(8,128)(2,1)S(1)}, u32[]{:S(2)}, u32[]{:S(2)}) collective-permute-start(bf16[272,1024]{1,0:T(8,128)(2,1)S(1)} %get-tuple-element.19.refs_0_), channel_id=1, source_target_pairs={{0,4},{1,5},{2,6},{3,7},{4,8},{5,9},{6,10},{7,11},{8,12},{9,13},{1... | collective-permute-start | bytes 1671176 | tf_op jit(solution)/shard_map/ppermute | solution.py:211
  5.0 1.5 %collective-permute-start.2 = (bf16[176,1024]{1,0:T(8,128)(2,1)S(1)}, bf16[176,1024]{1,0:T(8,128)(2,1)S(1)}, u32[]{:S(2)}, u32[]{:S(2)}) collective-permute-start(bf16[176,1024]{1,0:T(8,128)(2,1)S(1)} %get-tuple-element.20), channel_id=1, source_target_pairs={{0,2},{1,3},{2,0},{3,1},{4,6},{5,7},{6,4},{7,5},{8,10},{9,11},{10,... | collective-permute-start | bytes 1081352 | tf_op jit(solution)/shard_map/ppermute | solution.py:207
  6.5 0.0 collective-permute-start.3
  6.5 1.3 %collective-permute-start = (bf16[272,1024]{1,0:T(8,128)(2,1)S(1)}, bf16[272,1024]{1,0:T(8,128)(2,1)S(1)}, u32[]{:S(2)}, u32[]{:S(2)}) collective-permute-start(bf16[272,1024]{1,0:T(8,128)(2,1)S(1)} %get-tuple-element.19.refs_0_), channel_id=1, source_target_pairs={{4,12},{5,13},{6,14},{7,15},{8,0},{9,1},{10,2},{11,3},{20,28},{21,... | collective-permute-start | bytes 1671176 | tf_op jit(solution)/shard_map/ppermute | solution.py:211
  7.8 0.6 %collective-permute-start.4 = (bf16[96,1024]{1,0:T(8,128)(2,1)S(1)}, bf16[96,1024]{1,0:T(8,128)(2,1)S(1)}, u32[]{:S(2)}, u32[]{:S(2)}) collective-permute-start(bf16[96,1024]{1,0:T(8,128)(2,1)S(1)} %get-tuple-element.22), channel_id=1, source_target_pairs={{0,2},{1,3},{2,0},{3,1},{4,6},{5,7},{6,4},{7,5},{8,10},{9,11},{10,... | collective-permute-start | bytes 589832 | tf_op jit(solution)/shard_map/ppermute | solution.py:207
  8.4 8.0 %collective-permute-done.2.refs_3_ = bf16[176,1024]{1,0:T(8,128)(2,1)S(1)} collective-permute-done((bf16[176,1024]{1,0:T(8,128)(2,1)S(1)}, bf16[176,1024]{1,0:T(8,128)(2,1)S(1)}, u32[]{:S(2)}, u32[]{:S(2)}) %collective-permute-start.2) | collective-permute-done | bytes 360480 | tf_op jit(solution)/shard_map/ppermute | solution.py:207
  16.3 3.4 %collective-permute-done.1.line_ref = bf16[272,1024]{1,0:T(8,128)(2,1)S(1)} collective-permute-done((bf16[272,1024]{1,0:T(8,128)(2,1)S(1)}, bf16[272,1024]{1,0:T(8,128)(2,1)S(1)}, u32[]{:S(2)}, u32[]{:S(2)}) %collective-permute-start.1) | collective-permute-done | bytes 557088 | tf_op jit(solution)/shard_map/ppermute | solution.py:211
  19.7 0.0 collective-permute-start.6
  19.7 0.0 collective-permute-done.4.refs_2_
  19.7 0.5 %collective-permute-start.5 = (bf16[96,1024]{1,0:T(8,128)(2,1)S(1)}, bf16[96,1024]{1,0:T(8,128)(2,1)S(1)}, u32[]{:S(2)}, u32[]{:S(2)}) collective-permute-start(bf16[96,1024]{1,0:T(8,128)(2,1)S(1)} %collective-permute-done.4.refs_2_), channel_id=1, source_target_pairs={{0,1},{1,0},{2,3},{3,2},{4,5},{5,4},{6,7},{7,6},{8,9},{9,8},{10,11... | collective-permute-start | bytes 589832 | tf_op jit(solution)/shard_map/ppermute | solution.py:207
  20.3 1.4 %collective-permute-done.5.refs_4_ = bf16[96,1024]{1,0:T(8,128)(2,1)S(1)} collective-permute-done((bf16[96,1024]{1,0:T(8,128)(2,1)S(1)}, bf16[96,1024]{1,0:T(8,128)(2,1)S(1)}, u32[]{:S(2)}, u32[]{:S(2)}) %collective-permute-start.5) | collective-permute-done | bytes 196640 | tf_op jit(solution)/shard_map/ppermute | solution.py:207
  21.7 0.0 collective-permute-done.3.refs_1_
  21.7 0.0 collective-permute-done.6.refs_5_
  21.7 2.3 %shard_map.29 = (f32[1024,128]{1,0:T(8,128)S(1)}, f32[1,256]{1,0:T(1,128)S(1)}, f32[1024,128]{1,0:T(8,128)S(1)}, f32[1,256]{1,0:T(1,128)S(1)}) custom-call(bf16[272,1024]{1,0:T(8,128)(2,1)S(1)} %collective-permute-done.1.line_ref, bf16[272,1024]{1,0:T(8,128)(2,1)S(1)} %get-tuple-element.19.refs_0_, bf16[272,1024]{1,0:T(8,128)(2,1)S(1)} %collective-permute-done.3.refs_1_, ...), custom_call_target="tpu_custom_call" | custom-call | flops 1 | bytes 1 | tf_op jit(solution)/shard_map/pallas_call | solution.py:236
  24.0 13.6 %collective-permute-start.7 = (f32[1,256]{1,0:T(1,128)S(1)}, f32[1,256]{1,0:T(1,128)S(1)}, u32[]{:S(2)}, u32[]{:S(2)}) collective-permute-start(f32[1,256]{1,0:T(1,128)S(1)} %get-tuple-element.27), channel_id=1, source_target_pairs={{4,0},{5,1},{6,2},{7,3},{8,4},{9,5},{10,6},{11,7},{12,8},{13,9},{1... | collective-permute-start | bytes 3080 | tf_op jit(solution)/shard_map/ppermute | solution.py:211
  37.7 0.0 collective-permute-done.line_ref
  37.7 1.3 %collective-permute-done.7.back_ref = f32[1,256]{1,0:T(1,128)S(1)} collective-permute-done((f32[1,256]{1,0:T(1,128)S(1)}, f32[1,256]{1,0:T(1,128)S(1)}, u32[]{:S(2)}, u32[]{:S(2)}) %collective-permute-start.7) | collective-permute-done | bytes 1056 | tf_op jit(solution)/shard_map/ppermute | solution.py:211
  39.0 1.4 %shard_map.30 = (f32[1,256]{1,0:T(1,128)S(1)}, f32[1,256]{1,0:T(1,128)S(1)}, f32[1,256]{1,0:T(1,128)S(1)}, f32[1,256]{1,0:T(1,128)S(1)}, f32[1,256]{1,0:T(1,128)S(1)}) custom-call(bf16[272,1024]{1,0:T(8,128)(2,1)S(1)} %collective-permute-done.line_ref, f32[1024,128]{1,0:T(8,128)S(1)} %get-tuple-element.24.ids_ref, ...), custom_call_target="tpu_custom_call" | custom-call | tf_op jit(solution)/shard_map/pallas_call | solution.py:243
  40.4 1.5 %collective-permute-start.8 = (f32[1,256]{1,0:T(1,128)S(1)}, f32[1,256]{1,0:T(1,128)S(1)}, u32[]{:S(2)}, u32[]{:S(2)}) collective-permute-start(f32[1,256]{1,0:T(1,128)S(1)} %get-tuple-element.29), channel_id=1, source_target_pairs={{12,4},{13,5},{14,6},{15,7},{0,8},{1,9},{2,10},{3,11},{28,20},{29,... | collective-permute-start | bytes 3080 | tf_op jit(solution)/shard_map/ppermute | solution.py:211
  41.9 1.6 %collective-permute-start.9 = (f32[1,256]{1,0:T(1,128)S(1)}, f32[1,256]{1,0:T(1,128)S(1)}, u32[]{:S(2)}, u32[]{:S(2)}) collective-permute-start(f32[1,256]{1,0:T(1,128)S(1)} %get-tuple-element.30), channel_id=1, source_target_pairs={{0,2},{1,3},{2,0},{3,1},{4,6},{5,7},{6,4},{7,5},{8,10},{9,11},{10,... | collective-permute-start | bytes 3080 | tf_op jit(solution)/shard_map/ppermute | solution.py:207
  43.5 0.0 collective-permute-start.10
  43.5 0.6 %collective-permute-start.11 = (f32[1,256]{1,0:T(1,128)S(1)}, f32[1,256]{1,0:T(1,128)S(1)}, u32[]{:S(2)}, u32[]{:S(2)}) collective-permute-start(f32[1,256]{1,0:T(1,128)S(1)} %get-tuple-element.32), channel_id=1, source_target_pairs={{0,1},{1,0},{2,3},{3,2},{4,5},{5,4},{6,7},{7,6},{8,9},{9,8},{10,11... | collective-permute-start | bytes 3080 | tf_op jit(solution)/shard_map/ppermute | solution.py:207
  44.1 0.0 collective-permute-done.8
  44.1 1.4 %collective-permute-done.9 = f32[1,256]{1,0:T(1,128)S(1)} collective-permute-done((f32[1,256]{1,0:T(1,128)S(1)}, f32[1,256]{1,0:T(1,128)S(1)}, u32[]{:S(2)}, u32[]{:S(2)}) %collective-permute-start.9) | collective-permute-done | bytes 1056 | tf_op jit(solution)/shard_map/ppermute | solution.py:207
  45.6 0.9 %collective-permute-done.10 = f32[1,256]{1,0:T(1,128)S(1)} collective-permute-done((f32[1,256]{1,0:T(1,128)S(1)}, f32[1,256]{1,0:T(1,128)S(1)}, u32[]{:S(2)}, u32[]{:S(2)}) %collective-permute-start.10) | collective-permute-done | bytes 1056 | tf_op jit(solution)/shard_map/ppermute | solution.py:207
  46.5 0.0 collective-permute-done.11
  46.5 0.6 %add_log-plus-one_fusion = f32[1,256]{1,0:T(1,128)} fusion(f32[1,256]{1,0:T(1,128)S(1)} %collective-permute-done.11, f32[1,256]{1,0:T(1,128)S(1)} %collective-permute-done.10, f32[1,256]{1,0:T(1,128)S(1)} %collective-permute-done.9, f32[1,256]{1,0:T(1,128)S(1)} %get-tuple-element.28, f32[1,256]{1,0:T(1,128)S(1)} %collective-permute-done.8), kind=kLoop, calls=%fused_computation | loop fusion | flops 1024 | bytes 6144 | tf_op jit(solution)/shard_map/log1p | solution.py:251
Async XLA Ops:
  0.0 0.7 %copy-start.1 = (s32[256]{0:T(256)S(1)}, s32[256]{0:T(256)}, u32[]{:S(2)}) copy-start(s32[256]{0:T(256)} %param.3) | copy-start | bytes 3076
  0.7 1.0 %copy-start = (bf16[256,1024]{1,0:T(8,128)(2,1)S(1)}, bf16[256,1024]{1,0:T(8,128)(2,1)}, u32[]{:S(2)}) copy-start(bf16[256,1024]{1,0:T(8,128)(2,1)} %rows_ref.1) | copy-start | bytes 1572868
  1.9 17.8 %collective-permute-start.1 = (bf16[272,1024]{1,0:T(8,128)(2,1)S(1)}, bf16[272,1024]{1,0:T(8,128)(2,1)S(1)}, u32[]{:S(2)}, u32[]{:S(2)}) collective-permute-start(bf16[272,1024]{1,0:T(8,128)(2,1)S(1)} %get-tuple-element.19.refs_0_), channel_id=1, source_target_pairs={{0,4},{1,5},{2,6},{3,7},{4,8},{5,9},{6,10},{7,11},{8,12},{9,13},{1... | collective-permute-start | bytes 1671176 | tf_op jit(solution)/shard_map/ppermute | solution.py:211
  5.0 11.3 %collective-permute-start.2 = (bf16[176,1024]{1,0:T(8,128)(2,1)S(1)}, bf16[176,1024]{1,0:T(8,128)(2,1)S(1)}, u32[]{:S(2)}, u32[]{:S(2)}) collective-permute-start(bf16[176,1024]{1,0:T(8,128)(2,1)S(1)} %get-tuple-element.20), channel_id=1, source_target_pairs={{0,2},{1,3},{2,0},{3,1},{4,6},{5,7},{6,4},{7,5},{8,10},{9,11},{10,... | collective-permute-start | bytes 1081352 | tf_op jit(solution)/shard_map/ppermute | solution.py:207
  6.5 15.2 %collective-permute-start.3 = (bf16[272,1024]{1,0:T(8,128)(2,1)S(1)}, bf16[272,1024]{1,0:T(8,128)(2,1)S(1)}, u32[]{:S(2)}, u32[]{:S(2)}) collective-permute-start(bf16[272,1024]{1,0:T(8,128)(2,1)S(1)} %get-tuple-element.19.refs_0_), channel_id=1, source_target_pairs={{0,1},{1,0},{2,3},{3,2},{4,5},{5,4},{6,7},{7,6},{8,9},{9,8},{10,11... | collective-permute-start | bytes 1671176 | tf_op jit(solution)/shard_map/ppermute | solution.py:207
  6.5 31.2 %collective-permute-start = (bf16[272,1024]{1,0:T(8,128)(2,1)S(1)}, bf16[272,1024]{1,0:T(8,128)(2,1)S(1)}, u32[]{:S(2)}, u32[]{:S(2)}) collective-permute-start(bf16[272,1024]{1,0:T(8,128)(2,1)S(1)} %get-tuple-element.19.refs_0_), channel_id=1, source_target_pairs={{4,12},{5,13},{6,14},{7,15},{8,0},{9,1},{10,2},{11,3},{20,28},{21,... | collective-permute-start | bytes 1671176 | tf_op jit(solution)/shard_map/ppermute | solution.py:211
  7.8 12.0 %collective-permute-start.4 = (bf16[96,1024]{1,0:T(8,128)(2,1)S(1)}, bf16[96,1024]{1,0:T(8,128)(2,1)S(1)}, u32[]{:S(2)}, u32[]{:S(2)}) collective-permute-start(bf16[96,1024]{1,0:T(8,128)(2,1)S(1)} %get-tuple-element.22), channel_id=1, source_target_pairs={{0,2},{1,3},{2,0},{3,1},{4,6},{5,7},{6,4},{7,5},{8,10},{9,11},{10,... | collective-permute-start | bytes 589832 | tf_op jit(solution)/shard_map/ppermute | solution.py:207
  19.7 2.0 %collective-permute-start.6 = (bf16[176,1024]{1,0:T(8,128)(2,1)S(1)}, bf16[176,1024]{1,0:T(8,128)(2,1)S(1)}, u32[]{:S(2)}, u32[]{:S(2)}) collective-permute-start(bf16[176,1024]{1,0:T(8,128)(2,1)S(1)} %collective-permute-done.2.refs_3_), channel_id=1, source_target_pairs={{0,1},{1,0},{2,3},{3,2},{4,5},{5,4},{6,7},{7,6},{8,9},{9,8},{10,11... | collective-permute-start | bytes 1081352 | tf_op jit(solution)/shard_map/ppermute | solution.py:207
  19.7 2.0 %collective-permute-start.5 = (bf16[96,1024]{1,0:T(8,128)(2,1)S(1)}, bf16[96,1024]{1,0:T(8,128)(2,1)S(1)}, u32[]{:S(2)}, u32[]{:S(2)}) collective-permute-start(bf16[96,1024]{1,0:T(8,128)(2,1)S(1)} %collective-permute-done.4.refs_2_), channel_id=1, source_target_pairs={{0,1},{1,0},{2,3},{3,2},{4,5},{5,4},{6,7},{7,6},{8,9},{9,8},{10,11... | collective-permute-start | bytes 589832 | tf_op jit(solution)/shard_map/ppermute | solution.py:207
  24.0 14.9 %collective-permute-start.7 = (f32[1,256]{1,0:T(1,128)S(1)}, f32[1,256]{1,0:T(1,128)S(1)}, u32[]{:S(2)}, u32[]{:S(2)}) collective-permute-start(f32[1,256]{1,0:T(1,128)S(1)} %get-tuple-element.27), channel_id=1, source_target_pairs={{4,0},{5,1},{6,2},{7,3},{8,4},{9,5},{10,6},{11,7},{12,8},{13,9},{1... | collective-permute-start | bytes 3080 | tf_op jit(solution)/shard_map/ppermute | solution.py:211
  40.4 3.8 %collective-permute-start.8 = (f32[1,256]{1,0:T(1,128)S(1)}, f32[1,256]{1,0:T(1,128)S(1)}, u32[]{:S(2)}, u32[]{:S(2)}) collective-permute-start(f32[1,256]{1,0:T(1,128)S(1)} %get-tuple-element.29), channel_id=1, source_target_pairs={{12,4},{13,5},{14,6},{15,7},{0,8},{1,9},{2,10},{3,11},{28,20},{29,... | collective-permute-start | bytes 3080 | tf_op jit(solution)/shard_map/ppermute | solution.py:211
  41.9 3.6 %collective-permute-start.9 = (f32[1,256]{1,0:T(1,128)S(1)}, f32[1,256]{1,0:T(1,128)S(1)}, u32[]{:S(2)}, u32[]{:S(2)}) collective-permute-start(f32[1,256]{1,0:T(1,128)S(1)} %get-tuple-element.30), channel_id=1, source_target_pairs={{0,2},{1,3},{2,0},{3,1},{4,6},{5,7},{6,4},{7,5},{8,10},{9,11},{10,... | collective-permute-start | bytes 3080 | tf_op jit(solution)/shard_map/ppermute | solution.py:207
  43.5 3.0 %collective-permute-start.10 = (f32[1,256]{1,0:T(1,128)S(1)}, f32[1,256]{1,0:T(1,128)S(1)}, u32[]{:S(2)}, u32[]{:S(2)}) collective-permute-start(f32[1,256]{1,0:T(1,128)S(1)} %get-tuple-element.31), channel_id=1, source_target_pairs={{0,3},{1,2},{2,1},{3,0},{4,7},{5,6},{6,5},{7,4},{8,11},{9,10},{10,... | collective-permute-start | bytes 3080 | tf_op jit(solution)/shard_map/ppermute | solution.py:207
  43.5 3.0 %collective-permute-start.11 = (f32[1,256]{1,0:T(1,128)S(1)}, f32[1,256]{1,0:T(1,128)S(1)}, u32[]{:S(2)}, u32[]{:S(2)}) collective-permute-start(f32[1,256]{1,0:T(1,128)S(1)} %get-tuple-element.32), channel_id=1, source_target_pairs={{0,1},{1,0},{2,3},{3,2},{4,5},{5,4},{6,7},{7,6},{8,9},{9,8},{10,11... | collective-permute-start | bytes 3080 | tf_op jit(solution)/shard_map/ppermute | solution.py:207

commit v9 on v8

--- a/solution.py
+++ b/solution.py
@@ -211,11 +211,11 @@
         return lax.ppermute(value, "gx", pairs)
 
     first_moves = [(0, 1), (1, 2), (2, 3), (3, 0)]
-    last_moves = [(1, 3), (2, 0)]
+    last_moves = [(0, 2), (3, 1)]
     first_back = [(b, a) for a, b in first_moves]
     last_back = [(b, a) for a, b in last_moves]
 
-    head = 3 * row_count // 8
+    head = 7 * row_count // 16
     block, *pieces = pl.pallas_call(
         unit_kernel,
         out_shape=(
@@ -227,9 +227,10 @@
         compiler_params=params,
     )(embeddings, cluster_ids.reshape(1, row_count))
     first_line = on_line(block, first_moves)
-    last_line = on_line(block, last_moves)
     across = [in_plane(piece, 2) for piece in pieces]
     sibling = in_plane(block, 1)
+    across[0], late_block = lax.optimization_barrier((across[0], block))
+    last_line = on_line(late_block, last_moves)
     first_line, across[1] = lax.optimization_barrier((first_line, across[1]))
     corner = [in_plane(piece, 1) for piece in across]
     queries = (block, sibling, *across, *corner)

time: 47.3 us -> 47 us (level)
  waiting for transfers between devices: 16.5 us -> 26.9 us
  starting transfers between devices: 24.3 us -> 14.7 us
  Pallas kernels: 3.92 us -> 2.79 us
    ppermute x4, waiting for transfers between devices: 4.71 us -> 17.9 us  [on_line(): return lax.ppermute(value, 'gx', pairs)]
    ppermute x4, starting transfers between devices: 19.5 us -> 9.92 us  [on_line(): return lax.ppermute(value, 'gx', pairs)]
    ppermute x8, waiting for transfers between devices: 11.8 us -> 8.99 us  [in_plane(): return lax.ppermute(value, 'gx', [(i, i ^ step) for i in range(peers)])]
    pallas_call x1, Pallas kernels: 1.41 us -> 0.24 us  [grid_plan(): pl.pallas_call(functools.partial(last_kernel, last_moves), out_shape=[vec...]
where the time goes in v9:
time: 47 us; the launch traced here: 46.8 us
  waiting for transfers between devices  26.9 us (57%)
  starting transfers between devices  14.7 us (31%)
  Pallas kernels  2.79 us (6%)
  local copies, waits for them, and re-layouts  1.72 us (4%)
  other arithmetic  0.58 us (1%)
    ppermute x4, waiting for transfers between devices, on_line(): return lax.ppermute(value, 'gx', pairs)  17.9 us
    ppermute x4, starting transfers between devices, on_line(): return lax.ppermute(value, 'gx', pairs)  9.92 us
    ppermute x8, waiting for transfers between devices, in_plane(): return lax.ppermute(value, 'gx', [(i, i ^ step) for i in range(peers)])  8.99 us
    ppermute x8, starting transfers between devices, in_plane(): return lax.ppermute(value, 'gx', [(i, i ^ step) for i in range(peers)])  4.8 us
    pallas_call x1, Pallas kernels, grid_plan(): pl.pallas_call(functools.partial(first_kernel, first_moves), out_shape=(l...  2.36 us
    unnamed x4, local copies, waits for them, and re-layouts  1.72 us
  transfers between devices with their start and end apart: 12, of which 6 were waited for; matrix products, arithmetic and copies ran while one was open for 0% of the time, Pallas kernels for 5%

profile of v9, /device:TPU:0, one launch (start us, length us, event | category | flops | bytes accessed | tf_op | source)
XLA Modules:
  0.0 46.8 jit_solution(14909080979235562545)
XLA Ops:
  0.0 0.0 copy-start.1
  0.0 0.7 %copy-done.1 = s32[256]{0:T(256)S(1)} copy-done((s32[256]{0:T(256)S(1)}, s32[256]{0:T(256)}, u32[]{:S(2)}) %copy-start.1) | copy-done | bytes 1048
  0.7 0.0 copy-start
  0.7 1.0 %copy-done = bf16[256,1024]{1,0:T(8,128)(2,1)S(1)} copy-done((bf16[256,1024]{1,0:T(8,128)(2,1)S(1)}, bf16[256,1024]{1,0:T(8,128)(2,1)}, u32[]{:S(2)}) %copy-start) | copy-done | bytes 524312
  1.7 0.2 shard_map.28
  1.9 3.1 %collective-permute-start.2 = (bf16[272,1024]{1,0:T(8,128)(2,1)S(1)}, bf16[272,1024]{1,0:T(8,128)(2,1)S(1)}, u32[]{:S(2)}, u32[]{:S(2)}) collective-permute-start(bf16[272,1024]{1,0:T(8,128)(2,1)S(1)} %get-tuple-element.23.refs_0_), channel_id=1, source_target_pairs={{0,4},{1,5},{2,6},{3,7},{4,8},{5,9},{6,10},{7,11},{8,12},{9,13},{1... | collective-permute-start | bytes 1671176 | tf_op jit(solution)/shard_map/ppermute | solution.py:211
  5.0 1.5 %collective-permute-start = (bf16[112,1024]{1,0:T(8,128)(2,1)S(1)}, bf16[112,1024]{1,0:T(8,128)(2,1)S(1)}, u32[]{:S(2)}, u32[]{:S(2)}) collective-permute-start(bf16[112,1024]{1,0:T(8,128)(2,1)S(1)} %get-tuple-element.21), channel_id=1, source_target_pairs={{0,2},{1,3},{2,0},{3,1},{4,6},{5,7},{6,4},{7,5},{8,10},{9,11},{10,... | collective-permute-start | bytes 688136 | tf_op jit(solution)/shard_map/ppermute | solution.py:207
  6.5 0.5 %collective-permute-start.3 = (bf16[160,1024]{1,0:T(8,128)(2,1)S(1)}, bf16[160,1024]{1,0:T(8,128)(2,1)S(1)}, u32[]{:S(2)}, u32[]{:S(2)}) collective-permute-start(bf16[160,1024]{1,0:T(8,128)(2,1)S(1)} %get-tuple-element.24), channel_id=1, source_target_pairs={{0,2},{1,3},{2,0},{3,1},{4,6},{5,7},{6,4},{7,5},{8,10},{9,11},{10,... | collective-permute-start | bytes 983048 | tf_op jit(solution)/shard_map/ppermute | solution.py:207
  7.0 0.0 collective-permute-start.4
  7.0 6.5 %collective-permute-done.refs_2_ = bf16[112,1024]{1,0:T(8,128)(2,1)S(1)} collective-permute-done((bf16[112,1024]{1,0:T(8,128)(2,1)S(1)}, bf16[112,1024]{1,0:T(8,128)(2,1)S(1)}, u32[]{:S(2)}, u32[]{:S(2)}) %collective-permute-start) | collective-permute-done | bytes 229408 | tf_op jit(solution)/shard_map/ppermute | solution.py:207
  13.5 4.5 %collective-permute-start.1 = (bf16[272,1024]{1,0:T(8,128)(2,1)S(1)}, bf16[272,1024]{1,0:T(8,128)(2,1)S(1)}, u32[]{:S(2)}, u32[]{:S(2)}) collective-permute-start(bf16[272,1024]{1,0:T(8,128)(2,1)S(1)} %get-tuple-element.23.refs_0_), channel_id=1, source_target_pairs={{0,8},{1,9},{2,10},{3,11},{12,4},{13,5},{14,6},{15,7},{16,24},{17,... | collective-permute-start | bytes 1671176 | tf_op jit(solution)/shard_map/ppermute | solution.py:211
  18.0 1.0 %collective-permute-done.3.refs_3_ = bf16[160,1024]{1,0:T(8,128)(2,1)S(1)} collective-permute-done((bf16[160,1024]{1,0:T(8,128)(2,1)S(1)}, bf16[160,1024]{1,0:T(8,128)(2,1)S(1)}, u32[]{:S(2)}, u32[]{:S(2)}) %collective-permute-start.3) | collective-permute-done | bytes 327712 | tf_op jit(solution)/shard_map/ppermute | solution.py:207
  19.1 1.4 %collective-permute-done.2.line_ref = bf16[272,1024]{1,0:T(8,128)(2,1)S(1)} collective-permute-done((bf16[272,1024]{1,0:T(8,128)(2,1)S(1)}, bf16[272,1024]{1,0:T(8,128)(2,1)S(1)}, u32[]{:S(2)}, u32[]{:S(2)}) %collective-permute-start.2) | collective-permute-done | bytes 557088 | tf_op jit(solution)/shard_map/ppermute | solution.py:211
  20.5 0.0 collective-permute-start.6
  20.5 0.5 %collective-permute-start.5 = (bf16[112,1024]{1,0:T(8,128)(2,1)S(1)}, bf16[112,1024]{1,0:T(8,128)(2,1)S(1)}, u32[]{:S(2)}, u32[]{:S(2)}) collective-permute-start(bf16[112,1024]{1,0:T(8,128)(2,1)S(1)} %collective-permute-done.refs_2_), channel_id=1, source_target_pairs={{0,1},{1,0},{2,3},{3,2},{4,5},{5,4},{6,7},{7,6},{8,9},{9,8},{10,11... | collective-permute-start | bytes 688136 | tf_op jit(solution)/shard_map/ppermute | solution.py:207
  21.0 1.4 %collective-permute-done.5.refs_4_ = bf16[112,1024]{1,0:T(8,128)(2,1)S(1)} collective-permute-done((bf16[112,1024]{1,0:T(8,128)(2,1)S(1)}, bf16[112,1024]{1,0:T(8,128)(2,1)S(1)}, u32[]{:S(2)}, u32[]{:S(2)}) %collective-permute-start.5) | collective-permute-done | bytes 229408 | tf_op jit(solution)/shard_map/ppermute | solution.py:207
  22.4 0.0 collective-permute-done.4.refs_1_
  22.4 0.0 collective-permute-done.6.refs_5_
  22.4 2.4 %shard_map.29 = (f32[1024,128]{1,0:T(8,128)S(1)}, f32[1,256]{1,0:T(1,128)S(1)}, f32[1024,128]{1,0:T(8,128)S(1)}, f32[1,256]{1,0:T(1,128)S(1)}) custom-call(bf16[272,1024]{1,0:T(8,128)(2,1)S(1)} %collective-permute-done.2.line_ref, bf16[272,1024]{1,0:T(8,128)(2,1)S(1)} %get-tuple-element.23.refs_0_, bf16[272,1024]{1,0:T(8,128)(2,1)S(1)} %collective-permute-done.4.refs_1_, ...), custom_call_target="tpu_custom_call" | custom-call | flops 1 | bytes 1 | tf_op jit(solution)/shard_map/pallas_call | solution.py:237
  24.8 1.0 %collective-permute-start.7 = (f32[1,256]{1,0:T(1,128)S(1)}, f32[1,256]{1,0:T(1,128)S(1)}, u32[]{:S(2)}, u32[]{:S(2)}) collective-permute-start(f32[1,256]{1,0:T(1,128)S(1)} %get-tuple-element.31), channel_id=1, source_target_pairs={{4,0},{5,1},{6,2},{7,3},{8,4},{9,5},{10,6},{11,7},{12,8},{13,9},{1... | collective-permute-start | bytes 3080 | tf_op jit(solution)/shard_map/ppermute | solution.py:211
  25.8 3.0 %collective-permute-done.1.line_ref = bf16[272,1024]{1,0:T(8,128)(2,1)S(1)} collective-permute-done((bf16[272,1024]{1,0:T(8,128)(2,1)S(1)}, bf16[272,1024]{1,0:T(8,128)(2,1)S(1)}, u32[]{:S(2)}, u32[]{:S(2)}) %collective-permute-start.1) | collective-permute-done | bytes 557088 | tf_op jit(solution)/shard_map/ppermute | solution.py:211
  28.9 0.0 collective-permute-done.7.back_ref
  28.9 0.2 shard_map.30
  29.2 0.1 collective-permute-start.10
  29.2 1.6 %collective-permute-start.11 = (f32[1,256]{1,0:T(1,128)S(1)}, f32[1,256]{1,0:T(1,128)S(1)}, u32[]{:S(2)}, u32[]{:S(2)}) collective-permute-start(f32[1,256]{1,0:T(1,128)S(1)} %get-tuple-element.36), channel_id=1, source_target_pairs={{0,1},{1,0},{2,3},{3,2},{4,5},{5,4},{6,7},{7,6},{8,9},{9,8},{10,11... | collective-permute-start | bytes 3080 | tf_op jit(solution)/shard_map/ppermute | solution.py:207
  30.8 1.3 %collective-permute-start.8 = (f32[1,256]{1,0:T(1,128)S(1)}, f32[1,256]{1,0:T(1,128)S(1)}, u32[]{:S(2)}, u32[]{:S(2)}) collective-permute-start(f32[1,256]{1,0:T(1,128)S(1)} %get-tuple-element.33), channel_id=1, source_target_pairs={{8,0},{9,1},{10,2},{11,3},{4,12},{5,13},{6,14},{7,15},{24,16},{25,... | collective-permute-start | bytes 3080 | tf_op jit(solution)/shard_map/ppermute | solution.py:211
  32.1 0.6 %collective-permute-start.9 = (f32[1,256]{1,0:T(1,128)S(1)}, f32[1,256]{1,0:T(1,128)S(1)}, u32[]{:S(2)}, u32[]{:S(2)}) collective-permute-start(f32[1,256]{1,0:T(1,128)S(1)} %get-tuple-element.34), channel_id=1, source_target_pairs={{0,2},{1,3},{2,0},{3,1},{4,6},{5,7},{6,4},{7,5},{8,10},{9,11},{10,... | collective-permute-start | bytes 3080 | tf_op jit(solution)/shard_map/ppermute | solution.py:207
  32.7 0.0 collective-permute-done.10
  32.7 0.0 collective-permute-done.11
  32.7 13.5 %collective-permute-done.8 = f32[1,256]{1,0:T(1,128)S(1)} collective-permute-done((f32[1,256]{1,0:T(1,128)S(1)}, f32[1,256]{1,0:T(1,128)S(1)}, u32[]{:S(2)}, u32[]{:S(2)}) %collective-permute-start.8) | collective-permute-done | bytes 1056 | tf_op jit(solution)/shard_map/ppermute | solution.py:211
  46.2 0.0 collective-permute-done.9
  46.2 0.6 %add_log-plus-one_fusion = f32[1,256]{1,0:T(1,128)} fusion(f32[1,256]{1,0:T(1,128)S(1)} %collective-permute-done.11, f32[1,256]{1,0:T(1,128)S(1)} %collective-permute-done.10, f32[1,256]{1,0:T(1,128)S(1)} %collective-permute-done.9, f32[1,256]{1,0:T(1,128)S(1)} %get-tuple-element.32, f32[1,256]{1,0:T(1,128)S(1)} %collective-permute-done.8), kind=kLoop, calls=%fused_computation | loop fusion | flops 1024 | bytes 6144 | tf_op jit(solution)/shard_map/log1p | solution.py:252
Async XLA Ops:
  0.0 0.7 %copy-start.1 = (s32[256]{0:T(256)S(1)}, s32[256]{0:T(256)}, u32[]{:S(2)}) copy-start(s32[256]{0:T(256)} %param.3) | copy-start | bytes 3076
  0.7 1.0 %copy-start = (bf16[256,1024]{1,0:T(8,128)(2,1)S(1)}, bf16[256,1024]{1,0:T(8,128)(2,1)}, u32[]{:S(2)}) copy-start(bf16[256,1024]{1,0:T(8,128)(2,1)} %rows_ref.1) | copy-start | bytes 1572868
  1.9 18.6 %collective-permute-start.2 = (bf16[272,1024]{1,0:T(8,128)(2,1)S(1)}, bf16[272,1024]{1,0:T(8,128)(2,1)S(1)}, u32[]{:S(2)}, u32[]{:S(2)}) collective-permute-start(bf16[272,1024]{1,0:T(8,128)(2,1)S(1)} %get-tuple-element.23.refs_0_), channel_id=1, source_target_pairs={{0,4},{1,5},{2,6},{3,7},{4,8},{5,9},{6,10},{7,11},{8,12},{9,13},{1... | collective-permute-start | bytes 1671176 | tf_op jit(solution)/shard_map/ppermute | solution.py:211
  5.0 8.5 %collective-permute-start = (bf16[112,1024]{1,0:T(8,128)(2,1)S(1)}, bf16[112,1024]{1,0:T(8,128)(2,1)S(1)}, u32[]{:S(2)}, u32[]{:S(2)}) collective-permute-start(bf16[112,1024]{1,0:T(8,128)(2,1)S(1)} %get-tuple-element.21), channel_id=1, source_target_pairs={{0,2},{1,3},{2,0},{3,1},{4,6},{5,7},{6,4},{7,5},{8,10},{9,11},{10,... | collective-permute-start | bytes 688136 | tf_op jit(solution)/shard_map/ppermute | solution.py:207
  6.5 12.6 %collective-permute-start.3 = (bf16[160,1024]{1,0:T(8,128)(2,1)S(1)}, bf16[160,1024]{1,0:T(8,128)(2,1)S(1)}, u32[]{:S(2)}, u32[]{:S(2)}) collective-permute-start(bf16[160,1024]{1,0:T(8,128)(2,1)S(1)} %get-tuple-element.24), channel_id=1, source_target_pairs={{0,2},{1,3},{2,0},{3,1},{4,6},{5,7},{6,4},{7,5},{8,10},{9,11},{10,... | collective-permute-start | bytes 983048 | tf_op jit(solution)/shard_map/ppermute | solution.py:207
  7.0 15.4 %collective-permute-start.4 = (bf16[272,1024]{1,0:T(8,128)(2,1)S(1)}, bf16[272,1024]{1,0:T(8,128)(2,1)S(1)}, u32[]{:S(2)}, u32[]{:S(2)}) collective-permute-start(bf16[272,1024]{1,0:T(8,128)(2,1)S(1)} %get-tuple-element.23.refs_0_), channel_id=1, source_target_pairs={{0,1},{1,0},{2,3},{3,2},{4,5},{5,4},{6,7},{7,6},{8,9},{9,8},{10,11... | collective-permute-start | bytes 1671176 | tf_op jit(solution)/shard_map/ppermute | solution.py:207
  13.5 15.4 %collective-permute-start.1 = (bf16[272,1024]{1,0:T(8,128)(2,1)S(1)}, bf16[272,1024]{1,0:T(8,128)(2,1)S(1)}, u32[]{:S(2)}, u32[]{:S(2)}) collective-permute-start(bf16[272,1024]{1,0:T(8,128)(2,1)S(1)} %get-tuple-element.23.refs_0_), channel_id=1, source_target_pairs={{0,8},{1,9},{2,10},{3,11},{12,4},{13,5},{14,6},{15,7},{16,24},{17,... | collective-permute-start | bytes 1671176 | tf_op jit(solution)/shard_map/ppermute | solution.py:211
  20.5 2.0 %collective-permute-start.6 = (bf16[160,1024]{1,0:T(8,128)(2,1)S(1)}, bf16[160,1024]{1,0:T(8,128)(2,1)S(1)}, u32[]{:S(2)}, u32[]{:S(2)}) collective-permute-start(bf16[160,1024]{1,0:T(8,128)(2,1)S(1)} %collective-permute-done.3.refs_3_), channel_id=1, source_target_pairs={{0,1},{1,0},{2,3},{3,2},{4,5},{5,4},{6,7},{7,6},{8,9},{9,8},{10,11... | collective-permute-start | bytes 983048 | tf_op jit(solution)/shard_map/ppermute | solution.py:207
  20.5 2.0 %collective-permute-start.5 = (bf16[112,1024]{1,0:T(8,128)(2,1)S(1)}, bf16[112,1024]{1,0:T(8,128)(2,1)S(1)}, u32[]{:S(2)}, u32[]{:S(2)}) collective-permute-start(bf16[112,1024]{1,0:T(8,128)(2,1)S(1)} %collective-permute-done.refs_2_), channel_id=1, source_target_pairs={{0,1},{1,0},{2,3},{3,2},{4,5},{5,4},{6,7},{7,6},{8,9},{9,8},{10,11... | collective-permute-start | bytes 688136 | tf_op jit(solution)/shard_map/ppermute | solution.py:207
  24.8 4.1 %collective-permute-start.7 = (f32[1,256]{1,0:T(1,128)S(1)}, f32[1,256]{1,0:T(1,128)S(1)}, u32[]{:S(2)}, u32[]{:S(2)}) collective-permute-start(f32[1,256]{1,0:T(1,128)S(1)} %get-tuple-element.31), channel_id=1, source_target_pairs={{4,0},{5,1},{6,2},{7,3},{8,4},{9,5},{10,6},{11,7},{12,8},{13,9},{1... | collective-permute-start | bytes 3080 | tf_op jit(solution)/shard_map/ppermute | solution.py:211
  29.2 3.6 %collective-permute-start.10 = (f32[1,256]{1,0:T(1,128)S(1)}, f32[1,256]{1,0:T(1,128)S(1)}, u32[]{:S(2)}, u32[]{:S(2)}) collective-permute-start(f32[1,256]{1,0:T(1,128)S(1)} %get-tuple-element.35), channel_id=1, source_target_pairs={{0,3},{1,2},{2,1},{3,0},{4,7},{5,6},{6,5},{7,4},{8,11},{9,10},{10,... | collective-permute-start | bytes 3080 | tf_op jit(solution)/shard_map/ppermute | solution.py:207
  29.2 3.5 %collective-permute-start.11 = (f32[1,256]{1,0:T(1,128)S(1)}, f32[1,256]{1,0:T(1,128)S(1)}, u32[]{:S(2)}, u32[]{:S(2)}) collective-permute-start(f32[1,256]{1,0:T(1,128)S(1)} %get-tuple-element.36), channel_id=1, source_target_pairs={{0,1},{1,0},{2,3},{3,2},{4,5},{5,4},{6,7},{7,6},{8,9},{9,8},{10,11... | collective-permute-start | bytes 3080 | tf_op jit(solution)/shard_map/ppermute | solution.py:207
  30.8 15.4 %collective-permute-start.8 = (f32[1,256]{1,0:T(1,128)S(1)}, f32[1,256]{1,0:T(1,128)S(1)}, u32[]{:S(2)}, u32[]{:S(2)}) collective-permute-start(f32[1,256]{1,0:T(1,128)S(1)} %get-tuple-element.33), channel_id=1, source_target_pairs={{8,0},{9,1},{10,2},{11,3},{4,12},{5,13},{6,14},{7,15},{24,16},{25,... | collective-permute-start | bytes 3080 | tf_op jit(solution)/shard_map/ppermute | solution.py:211
  32.1 14.1 %collective-permute-start.9 = (f32[1,256]{1,0:T(1,128)S(1)}, f32[1,256]{1,0:T(1,128)S(1)}, u32[]{:S(2)}, u32[]{:S(2)}) collective-permute-start(f32[1,256]{1,0:T(1,128)S(1)} %get-tuple-element.34), channel_id=1, source_target_pairs={{0,2},{1,3},{2,0},{3,1},{4,6},{5,7},{6,4},{7,5},{8,10},{9,11},{10,... | collective-permute-start | bytes 3080 | tf_op jit(solution)/shard_map/ppermute | solution.py:207

commit v10 on v8

--- a/solution.py
+++ b/solution.py
@@ -150,8 +150,8 @@
 
 
 def query_parts_of(refs, rows):
-    head = refs[2].shape[0]
-    sizes = [rows, rows] + [head, rows - head] * (PLANE - 2)
+    head = refs[1].shape[0]
+    sizes = [rows] + [head, rows - head] * (PLANE - 1)
     return list(zip(refs, sizes))
 
 
@@ -161,7 +161,7 @@
     query_parts = query_parts_of(query_refs, rows)
     own_ref = query_refs[0]
     own_ids = ids_of(own_ref)[:, :rows]
-    for m, ref in enumerate((*query_refs[:2], query_refs[3], query_refs[5])):
+    for m, ref in enumerate(query_refs[::2]):
         ids_ref[pl.ds(m * rows, rows), :] = along_rows(ids_of(ref)[:, :rows])
     mass = jnp.zeros((1, rows), jnp.float32)
     first = 0
@@ -177,13 +177,18 @@
     line_sums(moves, query_parts, ids_ref, line_ref, column_ref, sums_ref)
 
 
-def last_kernel(moves, line_ref, ids_ref, earlier_ref, mass_ref, back_ref, *refs):
-    query_refs, refs = refs[: -PLANE - 2], refs[-PLANE - 2 :]
-    column_ref, row_refs, sums_ref = refs[0], refs[1:-1], refs[-1]
-    rows = column_ref.shape[1]
+def last_kernel(all_moves, *refs):
+    count = len(all_moves)
+    line_refs, refs = refs[:count], refs[count:]
+    (ids_ref, earlier_ref, mass_ref, back_ref), refs = refs[:4], refs[4:]
+    out_count = count + PLANE
+    query_refs, column_refs = refs[: -out_count - 1], refs[-out_count - 1 : -PLANE - 1]
+    row_refs, sums_ref = refs[-PLANE - 1 : -1], refs[-1]
+    rows = mass_ref.shape[1]
     sums_ref[...] = earlier_ref[...]
     query_parts = query_parts_of(query_refs, rows)
-    line_sums(moves, query_parts, ids_ref, line_ref, column_ref, sums_ref)
+    for moves, line_ref, column_ref in zip(all_moves, line_refs, column_refs):
+        line_sums(moves, query_parts, ids_ref, line_ref, column_ref, sums_ref)
     for m in range(PLANE):
         row_sum = jnp.sum(sums_ref[pl.ds(m * rows, rows), :].T, axis=0, keepdims=True)
         if m == 0:
@@ -210,11 +215,11 @@
         pairs = [(a * PLANE + n, b * PLANE + n) for a, b in moves for n in range(PLANE)]
         return lax.ppermute(value, "gx", pairs)
 
-    first_moves = [(0, 1), (1, 2), (2, 3), (3, 0)]
-    last_moves = [(1, 3), (2, 0)]
-    first_back = [(b, a) for a, b in first_moves]
-    last_back = [(b, a) for a, b in last_moves]
-
+    def back(moves):
+        return [(b, a) for a, b in moves]
+
+    first_moves = [(0, 3), (3, 1), (1, 0)]
+    last_moves = [[(1, 2), (2, 0)], [(2, 3)]]
     head = 3 * row_count // 8
     block, *pieces = pl.pallas_call(
         unit_kernel,
@@ -227,26 +232,27 @@
         compiler_params=params,
     )(embeddings, cluster_ids.reshape(1, row_count))
     first_line = on_line(block, first_moves)
-    last_line = on_line(block, last_moves)
+    last_lines = [on_line(block, moves) for moves in last_moves]
     across = [in_plane(piece, 2) for piece in pieces]
-    sibling = in_plane(block, 1)
+    sibling = [in_plane(piece, 1) for piece in pieces]
     first_line, across[1] = lax.optimization_barrier((first_line, across[1]))
     corner = [in_plane(piece, 1) for piece in across]
-    queries = (block, sibling, *across, *corner)
+    queries = (block, *sibling, *across, *corner)
     ids, first_column, first_sums, mass = pl.pallas_call(
         functools.partial(first_kernel, first_moves),
         out_shape=(lanes, vector, lanes, vector),
         cost_estimate=small,
         compiler_params=params,
     )(first_line, *queries)
-    returned_first = on_line(first_column, first_back)
-    last_column, *row_sums = pl.pallas_call(
+    returned_first = on_line(first_column, back(first_moves))
+    sums = pl.pallas_call(
         functools.partial(last_kernel, last_moves),
-        out_shape=[vector] * (1 + PLANE),
+        out_shape=[vector] * (len(last_moves) + PLANE),
         scratch_shapes=[pltpu.VMEM(lanes.shape, lanes.dtype)],
         compiler_params=params,
-    )(last_line, ids, first_sums, mass, returned_first, *queries)
-    returned = [on_line(last_column, last_back)]
+    )(*last_lines, ids, first_sums, mass, returned_first, *queries)
+    columns, row_sums = sums[: len(last_moves)], sums[len(last_moves) :]
+    returned = [on_line(column, back(moves)) for column, moves in zip(columns, last_moves)]
     returned += [in_plane(row_sums[step], step) for step in (2, 3, 1)]
     return jnp.log1p(sum(returned, row_sums[0])).reshape(row_count)
 

time: 47.3 us -> 45.7 us (0.966)
  starting transfers between devices: 24.3 us -> 19.5 us
  waiting for transfers between devices: 16.5 us -> 19.2 us
  Pallas kernels: 3.92 us -> 4.41 us
    ppermute x4 -> x6, starting transfers between devices: 19.5 us -> 14.6 us  [on_line(): return lax.ppermute(value, 'gx', pairs)]
    ppermute x8 -> x9, waiting for transfers between devices: 11.8 us -> 13.3 us  [in_plane(): return lax.ppermute(value, 'gx', [(i, i ^ step) for i in range(peers)])]
    ppermute x4 -> x6, waiting for transfers between devices: 4.71 us -> 5.87 us  [on_line(): return lax.ppermute(value, 'gx', pairs)]
    ppermute x8 -> x9, starting transfers between devices: 4.81 us -> 4.81 us  [in_plane(): return lax.ppermute(value, 'gx', [(i, i ^ step) for i in range(peers)])]
  transfers between devices with their start and end apart: 12 -> 15, of which waited for: 6 -> 8; matrix products, arithmetic and copies ran while one was open for 0% -> 0% of each run, Pallas kernels for 5% -> 6%
where the time goes in v10:
time: 45.7 us; the launch traced here: 45.4 us
  starting transfers between devices  19.5 us (43%)
  waiting for transfers between devices  19.2 us (42%)
  Pallas kernels  4.41 us (10%)
  local copies, waits for them, and re-layouts  1.72 us (4%)
  other arithmetic  0.58 us (1%)
    ppermute x6, starting transfers between devices, on_line(): return lax.ppermute(value, 'gx', pairs)  14.6 us
    ppermute x9, waiting for transfers between devices, in_plane(): return lax.ppermute(value, 'gx', [(i, i ^ step) for i in range(peers)])  13.3 us
    ppermute x6, waiting for transfers between devices, on_line(): return lax.ppermute(value, 'gx', pairs)  5.87 us
    ppermute x9, starting transfers between devices, in_plane(): return lax.ppermute(value, 'gx', [(i, i ^ step) for i in range(peers)])  4.81 us
    pallas_call x1, Pallas kernels, grid_plan(): pl.pallas_call(functools.partial(first_kernel, first_moves), out_shape=(l...  2.64 us
    unnamed x4, local copies, waits for them, and re-layouts  1.72 us
    pallas_call x1, Pallas kernels, grid_plan(): pl.pallas_call(functools.partial(last_kernel, last_moves), out_shape=[vec...  1.58 us
  transfers between devices with their start and end apart: 15, of which 8 were waited for; matrix products, arithmetic and copies ran while one was open for 0% of the time, Pallas kernels for 6%

profile of v10, /device:TPU:0, one launch (start us, length us, event | category | flops | bytes accessed | tf_op | source)
XLA Modules:
  0.0 45.4 jit_solution(13298939684351711740)
XLA Ops:
  0.0 0.0 copy-start.1
  0.0 0.7 %copy-done.1 = s32[256]{0:T(256)S(1)} copy-done((s32[256]{0:T(256)S(1)}, s32[256]{0:T(256)}, u32[]{:S(2)}) %copy-start.1) | copy-done | bytes 1048
  0.7 0.0 copy-start
  0.7 1.0 %copy-done = bf16[256,1024]{1,0:T(8,128)(2,1)S(1)} copy-done((bf16[256,1024]{1,0:T(8,128)(2,1)S(1)}, bf16[256,1024]{1,0:T(8,128)(2,1)}, u32[]{:S(2)}) %copy-start) | copy-done | bytes 524312
  1.7 0.2 shard_map.28
  1.9 7.0 %collective-permute-start.2 = (bf16[272,1024]{1,0:T(8,128)(2,1)S(1)}, bf16[272,1024]{1,0:T(8,128)(2,1)S(1)}, u32[]{:S(2)}, u32[]{:S(2)}) collective-permute-start(bf16[272,1024]{1,0:T(8,128)(2,1)S(1)} %get-tuple-element.20.refs_0_.refs_6_), channel_id=1, source_target_pairs={{0,12},{1,13},{2,14},{3,15},{12,4},{13,5},{14,6},{15,7},{4,0},{5,1... | collective-permute-start | bytes 1671176 | tf_op jit(solution)/shard_map/ppermute | solution.py:216
  8.9 1.6 %collective-permute-start.3 = (bf16[176,1024]{1,0:T(8,128)(2,1)S(1)}, bf16[176,1024]{1,0:T(8,128)(2,1)S(1)}, u32[]{:S(2)}, u32[]{:S(2)}) collective-permute-start(bf16[176,1024]{1,0:T(8,128)(2,1)S(1)} %get-tuple-element.21), channel_id=1, source_target_pairs={{0,2},{1,3},{2,0},{3,1},{4,6},{5,7},{6,4},{7,5},{8,10},{9,11},{10,... | collective-permute-start | bytes 1081352 | tf_op jit(solution)/shard_map/ppermute | solution.py:212
  10.4 0.5 %collective-permute-start.6 = (bf16[96,1024]{1,0:T(8,128)(2,1)S(1)}, bf16[96,1024]{1,0:T(8,128)(2,1)S(1)}, u32[]{:S(2)}, u32[]{:S(2)}) collective-permute-start(bf16[96,1024]{1,0:T(8,128)(2,1)S(1)} %get-tuple-element.23), channel_id=1, source_target_pairs={{0,2},{1,3},{2,0},{3,1},{4,6},{5,7},{6,4},{7,5},{8,10},{9,11},{10,... | collective-permute-start | bytes 589832 | tf_op jit(solution)/shard_map/ppermute | solution.py:212
  11.0 0.7 %collective-permute-start.1 = (bf16[272,1024]{1,0:T(8,128)(2,1)S(1)}, bf16[272,1024]{1,0:T(8,128)(2,1)S(1)}, u32[]{:S(2)}, u32[]{:S(2)}) collective-permute-start(bf16[272,1024]{1,0:T(8,128)(2,1)S(1)} %get-tuple-element.20.refs_0_.refs_6_), channel_id=1, source_target_pairs={{8,12},{9,13},{10,14},{11,15},{24,28},{25,29},{26,30},{27,31}} | collective-permute-start | bytes 1671176 | tf_op jit(solution)/shard_map/ppermute | solution.py:216
  11.7 1.3 %collective-permute-start = (bf16[272,1024]{1,0:T(8,128)(2,1)S(1)}, bf16[272,1024]{1,0:T(8,128)(2,1)S(1)}, u32[]{:S(2)}, u32[]{:S(2)}) collective-permute-start(bf16[272,1024]{1,0:T(8,128)(2,1)S(1)} %get-tuple-element.20.refs_0_.refs_6_), channel_id=1, source_target_pairs={{4,8},{5,9},{6,10},{7,11},{8,0},{9,1},{10,2},{11,3},{20,24},{21,25... | collective-permute-start | bytes 1671176 | tf_op jit(solution)/shard_map/ppermute | solution.py:216
  13.0 7.3 %collective-permute-done.3.refs_4_.refs_10_ = bf16[176,1024]{1,0:T(8,128)(2,1)S(1)} collective-permute-done((bf16[176,1024]{1,0:T(8,128)(2,1)S(1)}, bf16[176,1024]{1,0:T(8,128)(2,1)S(1)}, u32[]{:S(2)}, u32[]{:S(2)}) %collective-permute-start.3) | collective-permute-done | bytes 360480 | tf_op jit(solution)/shard_map/ppermute | solution.py:212
  20.3 0.0 collective-permute-start.4
  20.3 0.5 %collective-permute-done.2.line_ref = bf16[272,1024]{1,0:T(8,128)(2,1)S(1)} collective-permute-done((bf16[272,1024]{1,0:T(8,128)(2,1)S(1)}, bf16[272,1024]{1,0:T(8,128)(2,1)S(1)}, u32[]{:S(2)}, u32[]{:S(2)}) %collective-permute-start.2) | collective-permute-done | bytes 557088 | tf_op jit(solution)/shard_map/ppermute | solution.py:216
  20.8 0.0 collective-permute-start.5
  20.8 2.2 %collective-permute-done.6.refs_3_.refs_9_ = bf16[96,1024]{1,0:T(8,128)(2,1)S(1)} collective-permute-done((bf16[96,1024]{1,0:T(8,128)(2,1)S(1)}, bf16[96,1024]{1,0:T(8,128)(2,1)S(1)}, u32[]{:S(2)}, u32[]{:S(2)}) %collective-permute-start.6) | collective-permute-done | bytes 196640 | tf_op jit(solution)/shard_map/ppermute | solution.py:212
  23.0 0.0 collective-permute-start.8
  23.0 0.0 collective-permute-done.4.refs_1_.refs_7_
  23.0 0.5 %collective-permute-start.7 = (bf16[96,1024]{1,0:T(8,128)(2,1)S(1)}, bf16[96,1024]{1,0:T(8,128)(2,1)S(1)}, u32[]{:S(2)}, u32[]{:S(2)}) collective-permute-start(bf16[96,1024]{1,0:T(8,128)(2,1)S(1)} %collective-permute-done.6.refs_3_.refs_9_), channel_id=1, source_target_pairs={{0,1},{1,0},{2,3},{3,2},{4,5},{5,4},{6,7},{7,6},{8,9},{9,8},{10,11... | collective-permute-start | bytes 589832 | tf_op jit(solution)/shard_map/ppermute | solution.py:212
  23.5 0.0 collective-permute-done.5.refs_2_.refs_8_
  23.6 1.4 %collective-permute-done.7.refs_5_.refs_11_ = bf16[96,1024]{1,0:T(8,128)(2,1)S(1)} collective-permute-done((bf16[96,1024]{1,0:T(8,128)(2,1)S(1)}, bf16[96,1024]{1,0:T(8,128)(2,1)S(1)}, u32[]{:S(2)}, u32[]{:S(2)}) %collective-permute-start.7) | collective-permute-done | bytes 196640 | tf_op jit(solution)/shard_map/ppermute | solution.py:212
  25.0 0.0 collective-permute-done.8.refs_6_.refs_12_
  25.0 2.6 %shard_map.29 = (f32[1024,128]{1,0:T(8,128)S(1)}, f32[1,256]{1,0:T(1,128)S(1)}, f32[1024,128]{1,0:T(8,128)S(1)}, f32[1,256]{1,0:T(1,128)S(1)}) custom-call(bf16[272,1024]{1,0:T(8,128)(2,1)S(1)} %collective-permute-done.2.line_ref, bf16[272,1024]{1,0:T(8,128)(2,1)S(1)} %get-tuple-element.20.refs_0_.refs_6_, ...), custom_call_target="tpu_custom_call" | custom-call | flops 1 | bytes 1 | tf_op jit(solution)/shard_map/pallas_call | solution.py:241
  27.6 1.9 %collective-permute-start.9 = (f32[1,256]{1,0:T(1,128)S(1)}, f32[1,256]{1,0:T(1,128)S(1)}, u32[]{:S(2)}, u32[]{:S(2)}) collective-permute-start(f32[1,256]{1,0:T(1,128)S(1)} %get-tuple-element.28), channel_id=1, source_target_pairs={{12,0},{13,1},{14,2},{15,3},{4,12},{5,13},{6,14},{7,15},{0,4},{1,5... | collective-permute-start | bytes 3080 | tf_op jit(solution)/shard_map/ppermute | solution.py:216
  29.6 0.0 collective-permute-done.1.refs_1_
  29.6 3.9 %collective-permute-done.refs_0_ = bf16[272,1024]{1,0:T(8,128)(2,1)S(1)} collective-permute-done((bf16[272,1024]{1,0:T(8,128)(2,1)S(1)}, bf16[272,1024]{1,0:T(8,128)(2,1)S(1)}, u32[]{:S(2)}, u32[]{:S(2)}) %collective-permute-start) | collective-permute-done | bytes 557088 | tf_op jit(solution)/shard_map/ppermute | solution.py:216
  33.5 1.4 %collective-permute-done.9.refs_5_ = f32[1,256]{1,0:T(1,128)S(1)} collective-permute-done((f32[1,256]{1,0:T(1,128)S(1)}, f32[1,256]{1,0:T(1,128)S(1)}, u32[]{:S(2)}, u32[]{:S(2)}) %collective-permute-start.9) | collective-permute-done | bytes 1056 | tf_op jit(solution)/shard_map/ppermute | solution.py:216
  34.9 1.6 %shard_map.30 = (f32[1,256]{1,0:T(1,128)S(1)}, f32[1,256]{1,0:T(1,128)S(1)}, f32[1,256]{1,0:T(1,128)S(1)}, f32[1,256]{1,0:T(1,128)S(1)}, f32[1,256]{1,0:T(1,128)S(1)}, /*index=5*/f32[1,256]{1,0:T(1,128)S(1)}) custom-call(bf16[272,1024]{1,0:T(8,128)(2,1)S(1)} %collective-permute-done.refs_0_, bf16[272,1024]{1,0:T(8,128)(2,1)S(1)} %collective-permute-done.1.refs_1_, ...), custom_call_target="tpu_custom_call" | custom-call | tf_op jit(solution)/shard_map/pallas_call | solution.py:248
  36.5 3.1 %collective-permute-start.10 = (f32[1,256]{1,0:T(1,128)S(1)}, f32[1,256]{1,0:T(1,128)S(1)}, u32[]{:S(2)}, u32[]{:S(2)}) collective-permute-start(f32[1,256]{1,0:T(1,128)S(1)} %get-tuple-element.30), channel_id=1, source_target_pairs={{8,4},{9,5},{10,6},{11,7},{0,8},{1,9},{2,10},{3,11},{24,20},{25,21... | collective-permute-start | bytes 3080 | tf_op jit(solution)/shard_map/ppermute | solution.py:216
  39.6 0.7 %collective-permute-start.11 = (f32[1,256]{1,0:T(1,128)S(1)}, f32[1,256]{1,0:T(1,128)S(1)}, u32[]{:S(2)}, u32[]{:S(2)}) collective-permute-start(f32[1,256]{1,0:T(1,128)S(1)} %get-tuple-element.31), channel_id=1, source_target_pairs={{12,8},{13,9},{14,10},{15,11},{28,24},{29,25},{30,26},{31,27}} | collective-permute-start | bytes 3080 | tf_op jit(solution)/shard_map/ppermute | solution.py:216
  40.3 1.6 %collective-permute-start.12 = (f32[1,256]{1,0:T(1,128)S(1)}, f32[1,256]{1,0:T(1,128)S(1)}, u32[]{:S(2)}, u32[]{:S(2)}) collective-permute-start(f32[1,256]{1,0:T(1,128)S(1)} %get-tuple-element.32), channel_id=1, source_target_pairs={{0,2},{1,3},{2,0},{3,1},{4,6},{5,7},{6,4},{7,5},{8,10},{9,11},{10,... | collective-permute-start | bytes 3080 | tf_op jit(solution)/shard_map/ppermute | solution.py:212
  41.8 0.0 collective-permute-start.13
  41.8 0.6 %collective-permute-start.14 = (f32[1,256]{1,0:T(1,128)S(1)}, f32[1,256]{1,0:T(1,128)S(1)}, u32[]{:S(2)}, u32[]{:S(2)}) collective-permute-start(f32[1,256]{1,0:T(1,128)S(1)} %get-tuple-element.34), channel_id=1, source_target_pairs={{0,1},{1,0},{2,3},{3,2},{4,5},{5,4},{6,7},{7,6},{8,9},{9,8},{10,11... | collective-permute-start | bytes 3080 | tf_op jit(solution)/shard_map/ppermute | solution.py:212
  42.5 0.0 collective-permute-done.10
  42.5 0.0 collective-permute-done.11
  42.5 1.4 %collective-permute-done.12 = f32[1,256]{1,0:T(1,128)S(1)} collective-permute-done((f32[1,256]{1,0:T(1,128)S(1)}, f32[1,256]{1,0:T(1,128)S(1)}, u32[]{:S(2)}, u32[]{:S(2)}) %collective-permute-start.12) | collective-permute-done | bytes 1056 | tf_op jit(solution)/shard_map/ppermute | solution.py:212
  43.9 0.9 %collective-permute-done.13 = f32[1,256]{1,0:T(1,128)S(1)} collective-permute-done((f32[1,256]{1,0:T(1,128)S(1)}, f32[1,256]{1,0:T(1,128)S(1)}, u32[]{:S(2)}, u32[]{:S(2)}) %collective-permute-start.13) | collective-permute-done | bytes 1056 | tf_op jit(solution)/shard_map/ppermute | solution.py:212
  44.8 0.0 collective-permute-done.14
  44.8 0.6 %add_log-plus-one_fusion = f32[1,256]{1,0:T(1,128)} fusion(f32[1,256]{1,0:T(1,128)S(1)} %collective-permute-done.14, f32[1,256]{1,0:T(1,128)S(1)} %collective-permute-done.13, f32[1,256]{1,0:T(1,128)S(1)} %collective-permute-done.12, f32[1,256]{1,0:T(1,128)S(1)} %collective-permute-done.11, f32[1,256]{1,0:T(1,128)S(1)} %get-tuple-element.29, ...), kind=kLoop, calls=%fused_computation | loop fusion | flops 1280 | bytes 7168 | tf_op jit(solution)/shard_map/log1p | solution.py:257
Async XLA Ops:
  0.0 0.7 %copy-start.1 = (s32[256]{0:T(256)S(1)}, s32[256]{0:T(256)}, u32[]{:S(2)}) copy-start(s32[256]{0:T(256)} %param.3) | copy-start | bytes 3076
  0.7 1.0 %copy-start = (bf16[256,1024]{1,0:T(8,128)(2,1)S(1)}, bf16[256,1024]{1,0:T(8,128)(2,1)}, u32[]{:S(2)}) copy-start(bf16[256,1024]{1,0:T(8,128)(2,1)} %rows_ref.1) | copy-start | bytes 1572868
  1.9 18.9 %collective-permute-start.2 = (bf16[272,1024]{1,0:T(8,128)(2,1)S(1)}, bf16[272,1024]{1,0:T(8,128)(2,1)S(1)}, u32[]{:S(2)}, u32[]{:S(2)}) collective-permute-start(bf16[272,1024]{1,0:T(8,128)(2,1)S(1)} %get-tuple-element.20.refs_0_.refs_6_), channel_id=1, source_target_pairs={{0,12},{1,13},{2,14},{3,15},{12,4},{13,5},{14,6},{15,7},{4,0},{5,1... | collective-permute-start | bytes 1671176 | tf_op jit(solution)/shard_map/ppermute | solution.py:216
  8.9 11.4 %collective-permute-start.3 = (bf16[176,1024]{1,0:T(8,128)(2,1)S(1)}, bf16[176,1024]{1,0:T(8,128)(2,1)S(1)}, u32[]{:S(2)}, u32[]{:S(2)}) collective-permute-start(bf16[176,1024]{1,0:T(8,128)(2,1)S(1)} %get-tuple-element.21), channel_id=1, source_target_pairs={{0,2},{1,3},{2,0},{3,1},{4,6},{5,7},{6,4},{7,5},{8,10},{9,11},{10,... | collective-permute-start | bytes 1081352 | tf_op jit(solution)/shard_map/ppermute | solution.py:212
  10.4 12.6 %collective-permute-start.6 = (bf16[96,1024]{1,0:T(8,128)(2,1)S(1)}, bf16[96,1024]{1,0:T(8,128)(2,1)S(1)}, u32[]{:S(2)}, u32[]{:S(2)}) collective-permute-start(bf16[96,1024]{1,0:T(8,128)(2,1)S(1)} %get-tuple-element.23), channel_id=1, source_target_pairs={{0,2},{1,3},{2,0},{3,1},{4,6},{5,7},{6,4},{7,5},{8,10},{9,11},{10,... | collective-permute-start | bytes 589832 | tf_op jit(solution)/shard_map/ppermute | solution.py:212
  11.0 18.6 %collective-permute-start.1 = (bf16[272,1024]{1,0:T(8,128)(2,1)S(1)}, bf16[272,1024]{1,0:T(8,128)(2,1)S(1)}, u32[]{:S(2)}, u32[]{:S(2)}) collective-permute-start(bf16[272,1024]{1,0:T(8,128)(2,1)S(1)} %get-tuple-element.20.refs_0_.refs_6_), channel_id=1, source_target_pairs={{8,12},{9,13},{10,14},{11,15},{24,28},{25,29},{26,30},{27,31}} | collective-permute-start | bytes 1671176 | tf_op jit(solution)/shard_map/ppermute | solution.py:216
  11.7 21.8 %collective-permute-start = (bf16[272,1024]{1,0:T(8,128)(2,1)S(1)}, bf16[272,1024]{1,0:T(8,128)(2,1)S(1)}, u32[]{:S(2)}, u32[]{:S(2)}) collective-permute-start(bf16[272,1024]{1,0:T(8,128)(2,1)S(1)} %get-tuple-element.20.refs_0_.refs_6_), channel_id=1, source_target_pairs={{4,8},{5,9},{6,10},{7,11},{8,0},{9,1},{10,2},{11,3},{20,24},{21,25... | collective-permute-start | bytes 1671176 | tf_op jit(solution)/shard_map/ppermute | solution.py:216
  20.3 2.8 %collective-permute-start.4 = (bf16[96,1024]{1,0:T(8,128)(2,1)S(1)}, bf16[96,1024]{1,0:T(8,128)(2,1)S(1)}, u32[]{:S(2)}, u32[]{:S(2)}) collective-permute-start(bf16[96,1024]{1,0:T(8,128)(2,1)S(1)} %get-tuple-element.23), channel_id=1, source_target_pairs={{0,1},{1,0},{2,3},{3,2},{4,5},{5,4},{6,7},{7,6},{8,9},{9,8},{10,11... | collective-permute-start | bytes 589832 | tf_op jit(solution)/shard_map/ppermute | solution.py:212
  20.8 2.7 %collective-permute-start.5 = (bf16[176,1024]{1,0:T(8,128)(2,1)S(1)}, bf16[176,1024]{1,0:T(8,128)(2,1)S(1)}, u32[]{:S(2)}, u32[]{:S(2)}) collective-permute-start(bf16[176,1024]{1,0:T(8,128)(2,1)S(1)} %get-tuple-element.21), channel_id=1, source_target_pairs={{0,1},{1,0},{2,3},{3,2},{4,5},{5,4},{6,7},{7,6},{8,9},{9,8},{10,11... | collective-permute-start | bytes 1081352 | tf_op jit(solution)/shard_map/ppermute | solution.py:212
  23.0 2.0 %collective-permute-start.8 = (bf16[176,1024]{1,0:T(8,128)(2,1)S(1)}, bf16[176,1024]{1,0:T(8,128)(2,1)S(1)}, u32[]{:S(2)}, u32[]{:S(2)}) collective-permute-start(bf16[176,1024]{1,0:T(8,128)(2,1)S(1)} %collective-permute-done.3.refs_4_.refs_10_), channel_id=1, source_target_pairs={{0,1},{1,0},{2,3},{3,2},{4,5},{5,4},{6,7},{7,6},{8,9},{9,8},{10,11... | collective-permute-start | bytes 1081352 | tf_op jit(solution)/shard_map/ppermute | solution.py:212
  23.0 2.0 %collective-permute-start.7 = (bf16[96,1024]{1,0:T(8,128)(2,1)S(1)}, bf16[96,1024]{1,0:T(8,128)(2,1)S(1)}, u32[]{:S(2)}, u32[]{:S(2)}) collective-permute-start(bf16[96,1024]{1,0:T(8,128)(2,1)S(1)} %collective-permute-done.6.refs_3_.refs_9_), channel_id=1, source_target_pairs={{0,1},{1,0},{2,3},{3,2},{4,5},{5,4},{6,7},{7,6},{8,9},{9,8},{10,11... | collective-permute-start | bytes 589832 | tf_op jit(solution)/shard_map/ppermute | solution.py:212
  27.6 7.3 %collective-permute-start.9 = (f32[1,256]{1,0:T(1,128)S(1)}, f32[1,256]{1,0:T(1,128)S(1)}, u32[]{:S(2)}, u32[]{:S(2)}) collective-permute-start(f32[1,256]{1,0:T(1,128)S(1)} %get-tuple-element.28), channel_id=1, source_target_pairs={{12,0},{13,1},{14,2},{15,3},{4,12},{5,13},{6,14},{7,15},{0,4},{1,5... | collective-permute-start | bytes 3080 | tf_op jit(solution)/shard_map/ppermute | solution.py:216
  36.5 6.0 %collective-permute-start.10 = (f32[1,256]{1,0:T(1,128)S(1)}, f32[1,256]{1,0:T(1,128)S(1)}, u32[]{:S(2)}, u32[]{:S(2)}) collective-permute-start(f32[1,256]{1,0:T(1,128)S(1)} %get-tuple-element.30), channel_id=1, source_target_pairs={{8,4},{9,5},{10,6},{11,7},{0,8},{1,9},{2,10},{3,11},{24,20},{25,21... | collective-permute-start | bytes 3080 | tf_op jit(solution)/shard_map/ppermute | solution.py:216
  39.6 2.9 %collective-permute-start.11 = (f32[1,256]{1,0:T(1,128)S(1)}, f32[1,256]{1,0:T(1,128)S(1)}, u32[]{:S(2)}, u32[]{:S(2)}) collective-permute-start(f32[1,256]{1,0:T(1,128)S(1)} %get-tuple-element.31), channel_id=1, source_target_pairs={{12,8},{13,9},{14,10},{15,11},{28,24},{29,25},{30,26},{31,27}} | collective-permute-start | bytes 3080 | tf_op jit(solution)/shard_map/ppermute | solution.py:216
  40.3 3.6 %collective-permute-start.12 = (f32[1,256]{1,0:T(1,128)S(1)}, f32[1,256]{1,0:T(1,128)S(1)}, u32[]{:S(2)}, u32[]{:S(2)}) collective-permute-start(f32[1,256]{1,0:T(1,128)S(1)} %get-tuple-element.32), channel_id=1, source_target_pairs={{0,2},{1,3},{2,0},{3,1},{4,6},{5,7},{6,4},{7,5},{8,10},{9,11},{10,... | collective-permute-start | bytes 3080 | tf_op jit(solution)/shard_map/ppermute | solution.py:212
  41.8 3.0 %collective-permute-start.13 = (f32[1,256]{1,0:T(1,128)S(1)}, f32[1,256]{1,0:T(1,128)S(1)}, u32[]{:S(2)}, u32[]{:S(2)}) collective-permute-start(f32[1,256]{1,0:T(1,128)S(1)} %get-tuple-element.33), channel_id=1, source_target_pairs={{0,3},{1,2},{2,1},{3,0},{4,7},{5,6},{6,5},{7,4},{8,11},{9,10},{10,... | collective-permute-start | bytes 3080 | tf_op jit(solution)/shard_map/ppermute | solution.py:212
  41.8 3.0 %collective-permute-start.14 = (f32[1,256]{1,0:T(1,128)S(1)}, f32[1,256]{1,0:T(1,128)S(1)}, u32[]{:S(2)}, u32[]{:S(2)}) collective-permute-start(f32[1,256]{1,0:T(1,128)S(1)} %get-tuple-element.34), channel_id=1, source_target_pairs={{0,1},{1,0},{2,3},{3,2},{4,5},{5,4},{6,7},{7,6},{8,9},{9,8},{10,11... | collective-permute-start | bytes 3080 | tf_op jit(solution)/shard_map/ppermute | solution.py:212

commit v11 on v8

--- a/solution.py
+++ b/solution.py
@@ -210,8 +210,8 @@
         pairs = [(a * PLANE + n, b * PLANE + n) for a, b in moves for n in range(PLANE)]
         return lax.ppermute(value, "gx", pairs)
 
-    first_moves = [(0, 1), (1, 2), (2, 3), (3, 0)]
-    last_moves = [(1, 3), (2, 0)]
+    first_moves = [(0, 1), (1, 2), (3, 0)]
+    last_moves = [(1, 3), (3, 2), (2, 0)]
     first_back = [(b, a) for a, b in first_moves]
     last_back = [(b, a) for a, b in last_moves]
 

time: 47.3 us -> 42.7 us (0.903)
  starting transfers between devices: 24.3 us -> 15.6 us
  waiting for transfers between devices: 16.5 us -> 20.6 us
    ppermute x4, starting transfers between devices: 19.5 us -> 10.6 us  [on_line(): return lax.ppermute(value, 'gx', pairs)]
    ppermute x4, waiting for transfers between devices: 4.71 us -> 8.35 us  [on_line(): return lax.ppermute(value, 'gx', pairs)]
where the time goes in v11:
time: 42.7 us; the launch traced here: 42.4 us
  waiting for transfers between devices  20.6 us (48%)
  starting transfers between devices  15.6 us (37%)
  Pallas kernels  3.92 us (9%)
  local copies, waits for them, and re-layouts  1.72 us (4%)
  other arithmetic  0.58 us (1%)
    ppermute x8, waiting for transfers between devices, in_plane(): return lax.ppermute(value, 'gx', [(i, i ^ step) for i in range(peers)])  12.2 us
    ppermute x4, starting transfers between devices, on_line(): return lax.ppermute(value, 'gx', pairs)  10.6 us
    ppermute x4, waiting for transfers between devices, on_line(): return lax.ppermute(value, 'gx', pairs)  8.35 us
    ppermute x8, starting transfers between devices, in_plane(): return lax.ppermute(value, 'gx', [(i, i ^ step) for i in range(peers)])  4.97 us
    pallas_call x1, Pallas kernels, grid_plan(): pl.pallas_call(functools.partial(first_kernel, first_moves), out_shape=(l...  2.32 us
    unnamed x4, local copies, waits for them, and re-layouts  1.72 us
    pallas_call x1, Pallas kernels, grid_plan(): pl.pallas_call(functools.partial(last_kernel, last_moves), out_shape=[vec...  1.41 us
  transfers between devices with their start and end apart: 12, of which 6 were waited for; matrix products, arithmetic and copies ran while one was open for 0% of the time, Pallas kernels for 5%

profile of v11, /device:TPU:0, one launch (start us, length us, event | category | flops | bytes accessed | tf_op | source)
XLA Modules:
  0.0 42.4 jit_solution(8924056422221487237)
XLA Ops:
  0.0 0.0 copy-start.1
  0.0 0.7 %copy-done.1 = s32[256]{0:T(256)S(1)} copy-done((s32[256]{0:T(256)S(1)}, s32[256]{0:T(256)}, u32[]{:S(2)}) %copy-start.1) | copy-done | bytes 1048
  0.7 0.0 copy-start
  0.7 1.0 %copy-done = bf16[256,1024]{1,0:T(8,128)(2,1)S(1)} copy-done((bf16[256,1024]{1,0:T(8,128)(2,1)S(1)}, bf16[256,1024]{1,0:T(8,128)(2,1)}, u32[]{:S(2)}) %copy-start) | copy-done | bytes 524312
  1.7 0.2 shard_map.28
  1.9 4.9 %collective-permute-start.1 = (bf16[272,1024]{1,0:T(8,128)(2,1)S(1)}, bf16[272,1024]{1,0:T(8,128)(2,1)S(1)}, u32[]{:S(2)}, u32[]{:S(2)}) collective-permute-start(bf16[272,1024]{1,0:T(8,128)(2,1)S(1)} %get-tuple-element.19.refs_0_), channel_id=1, source_target_pairs={{0,4},{1,5},{2,6},{3,7},{4,8},{5,9},{6,10},{7,11},{12,0},{13,1},{1... | collective-permute-start | bytes 1671176 | tf_op jit(solution)/shard_map/ppermute | solution.py:211
  6.9 1.6 %collective-permute-start.2 = (bf16[176,1024]{1,0:T(8,128)(2,1)S(1)}, bf16[176,1024]{1,0:T(8,128)(2,1)S(1)}, u32[]{:S(2)}, u32[]{:S(2)}) collective-permute-start(bf16[176,1024]{1,0:T(8,128)(2,1)S(1)} %get-tuple-element.20), channel_id=1, source_target_pairs={{0,2},{1,3},{2,0},{3,1},{4,6},{5,7},{6,4},{7,5},{8,10},{9,11},{10,... | collective-permute-start | bytes 1081352 | tf_op jit(solution)/shard_map/ppermute | solution.py:207
  8.4 0.0 collective-permute-start.3
  8.4 1.3 %collective-permute-start = (bf16[272,1024]{1,0:T(8,128)(2,1)S(1)}, bf16[272,1024]{1,0:T(8,128)(2,1)S(1)}, u32[]{:S(2)}, u32[]{:S(2)}) collective-permute-start(bf16[272,1024]{1,0:T(8,128)(2,1)S(1)} %get-tuple-element.19.refs_0_), channel_id=1, source_target_pairs={{4,12},{5,13},{6,14},{7,15},{12,8},{13,9},{14,10},{15,11},{8,0},{9... | collective-permute-start | bytes 1671176 | tf_op jit(solution)/shard_map/ppermute | solution.py:211
  9.7 0.6 %collective-permute-start.4 = (bf16[96,1024]{1,0:T(8,128)(2,1)S(1)}, bf16[96,1024]{1,0:T(8,128)(2,1)S(1)}, u32[]{:S(2)}, u32[]{:S(2)}) collective-permute-start(bf16[96,1024]{1,0:T(8,128)(2,1)S(1)} %get-tuple-element.22), channel_id=1, source_target_pairs={{0,2},{1,3},{2,0},{3,1},{4,6},{5,7},{6,4},{7,5},{8,10},{9,11},{10,... | collective-permute-start | bytes 589832 | tf_op jit(solution)/shard_map/ppermute | solution.py:207
  10.3 8.0 %collective-permute-done.2.refs_3_ = bf16[176,1024]{1,0:T(8,128)(2,1)S(1)} collective-permute-done((bf16[176,1024]{1,0:T(8,128)(2,1)S(1)}, bf16[176,1024]{1,0:T(8,128)(2,1)S(1)}, u32[]{:S(2)}, u32[]{:S(2)}) %collective-permute-start.2) | collective-permute-done | bytes 360480 | tf_op jit(solution)/shard_map/ppermute | solution.py:207
  18.3 3.5 %collective-permute-done.1.line_ref = bf16[272,1024]{1,0:T(8,128)(2,1)S(1)} collective-permute-done((bf16[272,1024]{1,0:T(8,128)(2,1)S(1)}, bf16[272,1024]{1,0:T(8,128)(2,1)S(1)}, u32[]{:S(2)}, u32[]{:S(2)}) %collective-permute-start.1) | collective-permute-done | bytes 557088 | tf_op jit(solution)/shard_map/ppermute | solution.py:211
  21.7 0.0 collective-permute-start.6
  21.7 0.0 collective-permute-done.4.refs_2_
  21.7 0.5 %collective-permute-start.5 = (bf16[96,1024]{1,0:T(8,128)(2,1)S(1)}, bf16[96,1024]{1,0:T(8,128)(2,1)S(1)}, u32[]{:S(2)}, u32[]{:S(2)}) collective-permute-start(bf16[96,1024]{1,0:T(8,128)(2,1)S(1)} %collective-permute-done.4.refs_2_), channel_id=1, source_target_pairs={{0,1},{1,0},{2,3},{3,2},{4,5},{5,4},{6,7},{7,6},{8,9},{9,8},{10,11... | collective-permute-start | bytes 589832 | tf_op jit(solution)/shard_map/ppermute | solution.py:207
  22.3 1.4 %collective-permute-done.5.refs_4_ = bf16[96,1024]{1,0:T(8,128)(2,1)S(1)} collective-permute-done((bf16[96,1024]{1,0:T(8,128)(2,1)S(1)}, bf16[96,1024]{1,0:T(8,128)(2,1)S(1)}, u32[]{:S(2)}, u32[]{:S(2)}) %collective-permute-start.5) | collective-permute-done | bytes 196640 | tf_op jit(solution)/shard_map/ppermute | solution.py:207
  23.7 0.0 collective-permute-done.3.refs_1_
  23.7 0.0 collective-permute-done.6.refs_5_
  23.7 2.3 %shard_map.29 = (f32[1024,128]{1,0:T(8,128)S(1)}, f32[1,256]{1,0:T(1,128)S(1)}, f32[1024,128]{1,0:T(8,128)S(1)}, f32[1,256]{1,0:T(1,128)S(1)}) custom-call(bf16[272,1024]{1,0:T(8,128)(2,1)S(1)} %collective-permute-done.1.line_ref, bf16[272,1024]{1,0:T(8,128)(2,1)S(1)} %get-tuple-element.19.refs_0_, bf16[272,1024]{1,0:T(8,128)(2,1)S(1)} %collective-permute-done.3.refs_1_, ...), custom_call_target="tpu_custom_call" | custom-call | flops 1 | bytes 1 | tf_op jit(solution)/shard_map/pallas_call | solution.py:236
  26.0 1.9 %collective-permute-start.7 = (f32[1,256]{1,0:T(1,128)S(1)}, f32[1,256]{1,0:T(1,128)S(1)}, u32[]{:S(2)}, u32[]{:S(2)}) collective-permute-start(f32[1,256]{1,0:T(1,128)S(1)} %get-tuple-element.27), channel_id=1, source_target_pairs={{4,0},{5,1},{6,2},{7,3},{8,4},{9,5},{10,6},{11,7},{0,12},{1,13},{2... | collective-permute-start | bytes 3080 | tf_op jit(solution)/shard_map/ppermute | solution.py:211
  28.0 4.9 %collective-permute-done.line_ref = bf16[272,1024]{1,0:T(8,128)(2,1)S(1)} collective-permute-done((bf16[272,1024]{1,0:T(8,128)(2,1)S(1)}, bf16[272,1024]{1,0:T(8,128)(2,1)S(1)}, u32[]{:S(2)}, u32[]{:S(2)}) %collective-permute-start) | collective-permute-done | bytes 557088 | tf_op jit(solution)/shard_map/ppermute | solution.py:211
  32.8 0.0 collective-permute-done.7.back_ref
  32.8 1.4 %shard_map.30 = (f32[1,256]{1,0:T(1,128)S(1)}, f32[1,256]{1,0:T(1,128)S(1)}, f32[1,256]{1,0:T(1,128)S(1)}, f32[1,256]{1,0:T(1,128)S(1)}, f32[1,256]{1,0:T(1,128)S(1)}) custom-call(bf16[272,1024]{1,0:T(8,128)(2,1)S(1)} %collective-permute-done.line_ref, f32[1024,128]{1,0:T(8,128)S(1)} %get-tuple-element.24.ids_ref, ...), custom_call_target="tpu_custom_call" | custom-call | tf_op jit(solution)/shard_map/pallas_call | solution.py:243
  34.2 2.5 %collective-permute-start.8 = (f32[1,256]{1,0:T(1,128)S(1)}, f32[1,256]{1,0:T(1,128)S(1)}, u32[]{:S(2)}, u32[]{:S(2)}) collective-permute-start(f32[1,256]{1,0:T(1,128)S(1)} %get-tuple-element.29), channel_id=1, source_target_pairs={{12,4},{13,5},{14,6},{15,7},{8,12},{9,13},{10,14},{11,15},{0,8},{1... | collective-permute-start | bytes 3080 | tf_op jit(solution)/shard_map/ppermute | solution.py:211
  36.8 2.1 %collective-permute-start.9 = (f32[1,256]{1,0:T(1,128)S(1)}, f32[1,256]{1,0:T(1,128)S(1)}, u32[]{:S(2)}, u32[]{:S(2)}) collective-permute-start(f32[1,256]{1,0:T(1,128)S(1)} %get-tuple-element.30), channel_id=1, source_target_pairs={{0,2},{1,3},{2,0},{3,1},{4,6},{5,7},{6,4},{7,5},{8,10},{9,11},{10,... | collective-permute-start | bytes 3080 | tf_op jit(solution)/shard_map/ppermute | solution.py:207
  38.9 0.0 collective-permute-start.10
  38.9 0.2 collective-permute-start.11
  39.1 0.0 collective-permute-done.8
  39.1 1.4 %collective-permute-done.9 = f32[1,256]{1,0:T(1,128)S(1)} collective-permute-done((f32[1,256]{1,0:T(1,128)S(1)}, f32[1,256]{1,0:T(1,128)S(1)}, u32[]{:S(2)}, u32[]{:S(2)}) %collective-permute-start.9) | collective-permute-done | bytes 1056 | tf_op jit(solution)/shard_map/ppermute | solution.py:207
  40.4 1.4 %collective-permute-done.10 = f32[1,256]{1,0:T(1,128)S(1)} collective-permute-done((f32[1,256]{1,0:T(1,128)S(1)}, f32[1,256]{1,0:T(1,128)S(1)}, u32[]{:S(2)}, u32[]{:S(2)}) %collective-permute-start.10) | collective-permute-done | bytes 1056 | tf_op jit(solution)/shard_map/ppermute | solution.py:207
  41.9 0.0 collective-permute-done.11
  41.9 0.6 %add_log-plus-one_fusion = f32[1,256]{1,0:T(1,128)} fusion(f32[1,256]{1,0:T(1,128)S(1)} %collective-permute-done.11, f32[1,256]{1,0:T(1,128)S(1)} %collective-permute-done.10, f32[1,256]{1,0:T(1,128)S(1)} %collective-permute-done.9, f32[1,256]{1,0:T(1,128)S(1)} %get-tuple-element.28, f32[1,256]{1,0:T(1,128)S(1)} %collective-permute-done.8), kind=kLoop, calls=%fused_computation | loop fusion | flops 1024 | bytes 6144 | tf_op jit(solution)/shard_map/log1p | solution.py:251
Async XLA Ops:
  0.0 0.7 %copy-start.1 = (s32[256]{0:T(256)S(1)}, s32[256]{0:T(256)}, u32[]{:S(2)}) copy-start(s32[256]{0:T(256)} %param.3) | copy-start | bytes 3076
  0.7 1.0 %copy-start = (bf16[256,1024]{1,0:T(8,128)(2,1)S(1)}, bf16[256,1024]{1,0:T(8,128)(2,1)}, u32[]{:S(2)}) copy-start(bf16[256,1024]{1,0:T(8,128)(2,1)} %rows_ref.1) | copy-start | bytes 1572868
  1.9 19.8 %collective-permute-start.1 = (bf16[272,1024]{1,0:T(8,128)(2,1)S(1)}, bf16[272,1024]{1,0:T(8,128)(2,1)S(1)}, u32[]{:S(2)}, u32[]{:S(2)}) collective-permute-start(bf16[272,1024]{1,0:T(8,128)(2,1)S(1)} %get-tuple-element.19.refs_0_), channel_id=1, source_target_pairs={{0,4},{1,5},{2,6},{3,7},{4,8},{5,9},{6,10},{7,11},{12,0},{13,1},{1... | collective-permute-start | bytes 1671176 | tf_op jit(solution)/shard_map/ppermute | solution.py:211
  6.9 11.4 %collective-permute-start.2 = (bf16[176,1024]{1,0:T(8,128)(2,1)S(1)}, bf16[176,1024]{1,0:T(8,128)(2,1)S(1)}, u32[]{:S(2)}, u32[]{:S(2)}) collective-permute-start(bf16[176,1024]{1,0:T(8,128)(2,1)S(1)} %get-tuple-element.20), channel_id=1, source_target_pairs={{0,2},{1,3},{2,0},{3,1},{4,6},{5,7},{6,4},{7,5},{8,10},{9,11},{10,... | collective-permute-start | bytes 1081352 | tf_op jit(solution)/shard_map/ppermute | solution.py:207
  8.4 15.3 %collective-permute-start.3 = (bf16[272,1024]{1,0:T(8,128)(2,1)S(1)}, bf16[272,1024]{1,0:T(8,128)(2,1)S(1)}, u32[]{:S(2)}, u32[]{:S(2)}) collective-permute-start(bf16[272,1024]{1,0:T(8,128)(2,1)S(1)} %get-tuple-element.19.refs_0_), channel_id=1, source_target_pairs={{0,1},{1,0},{2,3},{3,2},{4,5},{5,4},{6,7},{7,6},{8,9},{9,8},{10,11... | collective-permute-start | bytes 1671176 | tf_op jit(solution)/shard_map/ppermute | solution.py:207
  8.4 24.4 %collective-permute-start = (bf16[272,1024]{1,0:T(8,128)(2,1)S(1)}, bf16[272,1024]{1,0:T(8,128)(2,1)S(1)}, u32[]{:S(2)}, u32[]{:S(2)}) collective-permute-start(bf16[272,1024]{1,0:T(8,128)(2,1)S(1)} %get-tuple-element.19.refs_0_), channel_id=1, source_target_pairs={{4,12},{5,13},{6,14},{7,15},{12,8},{13,9},{14,10},{15,11},{8,0},{9... | collective-permute-start | bytes 1671176 | tf_op jit(solution)/shard_map/ppermute | solution.py:211
  9.7 12.0 %collective-permute-start.4 = (bf16[96,1024]{1,0:T(8,128)(2,1)S(1)}, bf16[96,1024]{1,0:T(8,128)(2,1)S(1)}, u32[]{:S(2)}, u32[]{:S(2)}) collective-permute-start(bf16[96,1024]{1,0:T(8,128)(2,1)S(1)} %get-tuple-element.22), channel_id=1, source_target_pairs={{0,2},{1,3},{2,0},{3,1},{4,6},{5,7},{6,4},{7,5},{8,10},{9,11},{10,... | collective-permute-start | bytes 589832 | tf_op jit(solution)/shard_map/ppermute | solution.py:207
  21.7 2.0 %collective-permute-start.6 = (bf16[176,1024]{1,0:T(8,128)(2,1)S(1)}, bf16[176,1024]{1,0:T(8,128)(2,1)S(1)}, u32[]{:S(2)}, u32[]{:S(2)}) collective-permute-start(bf16[176,1024]{1,0:T(8,128)(2,1)S(1)} %collective-permute-done.2.refs_3_), channel_id=1, source_target_pairs={{0,1},{1,0},{2,3},{3,2},{4,5},{5,4},{6,7},{7,6},{8,9},{9,8},{10,11... | collective-permute-start | bytes 1081352 | tf_op jit(solution)/shard_map/ppermute | solution.py:207
  21.7 2.0 %collective-permute-start.5 = (bf16[96,1024]{1,0:T(8,128)(2,1)S(1)}, bf16[96,1024]{1,0:T(8,128)(2,1)S(1)}, u32[]{:S(2)}, u32[]{:S(2)}) collective-permute-start(bf16[96,1024]{1,0:T(8,128)(2,1)S(1)} %collective-permute-done.4.refs_2_), channel_id=1, source_target_pairs={{0,1},{1,0},{2,3},{3,2},{4,5},{5,4},{6,7},{7,6},{8,9},{9,8},{10,11... | collective-permute-start | bytes 589832 | tf_op jit(solution)/shard_map/ppermute | solution.py:207
  26.0 6.8 %collective-permute-start.7 = (f32[1,256]{1,0:T(1,128)S(1)}, f32[1,256]{1,0:T(1,128)S(1)}, u32[]{:S(2)}, u32[]{:S(2)}) collective-permute-start(f32[1,256]{1,0:T(1,128)S(1)} %get-tuple-element.27), channel_id=1, source_target_pairs={{4,0},{5,1},{6,2},{7,3},{8,4},{9,5},{10,6},{11,7},{0,12},{1,13},{2... | collective-permute-start | bytes 3080 | tf_op jit(solution)/shard_map/ppermute | solution.py:211
  34.2 4.8 %collective-permute-start.8 = (f32[1,256]{1,0:T(1,128)S(1)}, f32[1,256]{1,0:T(1,128)S(1)}, u32[]{:S(2)}, u32[]{:S(2)}) collective-permute-start(f32[1,256]{1,0:T(1,128)S(1)} %get-tuple-element.29), channel_id=1, source_target_pairs={{12,4},{13,5},{14,6},{15,7},{8,12},{9,13},{10,14},{11,15},{0,8},{1... | collective-permute-start | bytes 3080 | tf_op jit(solution)/shard_map/ppermute | solution.py:211
  36.8 3.7 %collective-permute-start.9 = (f32[1,256]{1,0:T(1,128)S(1)}, f32[1,256]{1,0:T(1,128)S(1)}, u32[]{:S(2)}, u32[]{:S(2)}) collective-permute-start(f32[1,256]{1,0:T(1,128)S(1)} %get-tuple-element.30), channel_id=1, source_target_pairs={{0,2},{1,3},{2,0},{3,1},{4,6},{5,7},{6,4},{7,5},{8,10},{9,11},{10,... | collective-permute-start | bytes 3080 | tf_op jit(solution)/shard_map/ppermute | solution.py:207
  38.9 3.0 %collective-permute-start.10 = (f32[1,256]{1,0:T(1,128)S(1)}, f32[1,256]{1,0:T(1,128)S(1)}, u32[]{:S(2)}, u32[]{:S(2)}) collective-permute-start(f32[1,256]{1,0:T(1,128)S(1)} %get-tuple-element.31), channel_id=1, source_target_pairs={{0,3},{1,2},{2,1},{3,0},{4,7},{5,6},{6,5},{7,4},{8,11},{9,10},{10,... | collective-permute-start | bytes 3080 | tf_op jit(solution)/shard_map/ppermute | solution.py:207
  38.9 3.0 %collective-permute-start.11 = (f32[1,256]{1,0:T(1,128)S(1)}, f32[1,256]{1,0:T(1,128)S(1)}, u32[]{:S(2)}, u32[]{:S(2)}) collective-permute-start(f32[1,256]{1,0:T(1,128)S(1)} %get-tuple-element.32), channel_id=1, source_target_pairs={{0,1},{1,0},{2,3},{3,2},{4,5},{5,4},{6,7},{7,6},{8,9},{9,8},{10,11... | collective-permute-start | bytes 3080 | tf_op jit(solution)/shard_map/ppermute | solution.py:207

commit v12 on v7

--- a/solution.py
+++ b/solution.py
@@ -185,7 +185,7 @@
     line_sums(moves, query_parts, ids_ref, info_ref, line_ref, True, column_ref, sums_ref)
 
 
-def last_kernel(moves, info_ref, line_ref, ids_ref, earlier_ref, mass_ref, back_ref, *refs):
+def last_kernel(moves, info_ref, line_ref, ids_ref, earlier_ref, mass_ref, *refs):
     query_refs, refs = refs[: -PLANE - 2], refs[-PLANE - 2 :]
     column_ref, row_refs, sums_ref = refs[0], refs[1:-1], refs[-1]
     rows = column_ref.shape[1]
@@ -195,7 +195,7 @@
     for m in range(PLANE):
         row_sum = jnp.sum(sums_ref[pl.ds(m * rows, rows), :].T, axis=0, keepdims=True)
         if m == 0:
-            row_sum = row_sum + mass_ref[...] + back_ref[...]
+            row_sum = row_sum + mass_ref[...]
         row_refs[m][...] = row_sum
 
 
@@ -256,10 +256,11 @@
         out_shape=[vector] * (1 + PLANE),
         scratch_shapes=[pltpu.VMEM(lanes.shape, lanes.dtype)],
         compiler_params=params,
-    )(last_info, last_line, ids, first_sums, mass, returned_first, *queries)
+    )(last_info, last_line, ids, first_sums, mass, *queries)
+    returned_first, row_sums[1] = lax.optimization_barrier((returned_first, row_sums[1]))
     returned = [on_line(last_column, last_back)]
     returned += [in_plane(row_sums[step], step) for step in (2, 3, 1)]
-    return jnp.log1p(sum(returned, row_sums[0])).reshape(row_count)
+    return jnp.log1p(sum(returned, row_sums[0] + returned_first)).reshape(row_count)
 
 
 def on_device(embeddings, cluster_ids):

time: 39.5 us -> 38.4 us (0.972)
  the two profiles are of different devices: /device:TPU:8 before, /device:TPU:0 now
where the time goes in v12:
time: 38.4 us; the launch traced here: 38.2 us
  starting transfers between devices  18.1 us (47%)
  waiting for transfers between devices  15.8 us (41%)
  Pallas kernels  2.5 us (7%)
  local copies, waits for them, and re-layouts  1.12 us (3%)
  other arithmetic  0.58 us (2%)
    ppermute x6, waiting for transfers between devices, on_line(): return lax.ppermute(value, 'gx', pairs)  14.4 us
    ppermute x6, starting transfers between devices, on_line(): return lax.ppermute(value, 'gx', pairs)  13.7 us
    ppermute x7, starting transfers between devices, in_plane(): return lax.ppermute(value, 'gx', [(i, i ^ step) for i in range(peers)])  4.37 us
    pallas_call x1, Pallas kernels, grid_plan(): pl.pallas_call(functools.partial(first_kernel, first_moves), out_shape=(l...  2.03 us
    ppermute x7, waiting for transfers between devices, in_plane(): return lax.ppermute(value, 'gx', [(i, i ^ step) for i in range(peers)])  1.37 us
    unnamed x4, local copies, waits for them, and re-layouts  1.08 us
  transfers between devices with their start and end apart: 13, of which 5 were waited for; matrix products, arithmetic and copies ran while one was open for 0% of the time, Pallas kernels for 7%

profile of v12, /device:TPU:0, one launch (start us, length us, event | category | flops | bytes accessed | tf_op | source)
XLA Modules:
  0.0 38.2 jit_solution(4591522157167137566)
XLA Ops:
  0.0 0.0 copy-start.1
  0.0 3.0 %collective-permute-start = (bf16[256,1024]{1,0:T(8,128)(2,1)}, bf16[256,1024]{1,0:T(8,128)(2,1)S(1)}, u32[]{:S(2)}, u32[]{:S(2)}) collective-permute-start(bf16[256,1024]{1,0:T(8,128)(2,1)} %rows_ref.1), channel_id=1, source_target_pairs={{0,4},{1,5},{2,6},{3,7},{4,8},{5,9},{6,10},{7,11},{8,12},{9,13},{1... | collective-permute-start | bytes 1572872 | tf_op jit(solution)/shard_map/ppermute | solution.py:219
  3.0 0.0 copy-done.1
  3.0 0.0 copy-start
  3.0 1.1 %copy-done = bf16[256,1024]{1,0:T(8,128)(2,1)S(1)} copy-done((bf16[256,1024]{1,0:T(8,128)(2,1)S(1)}, bf16[256,1024]{1,0:T(8,128)(2,1)}, u32[]{:S(2)}) %copy-start) | copy-done | bytes 524312
  4.1 0.2 shard_map.28
  4.3 1.5 %collective-permute-start.5 = (bf16[272,1024]{1,0:T(8,128)(2,1)S(1)}, bf16[272,1024]{1,0:T(8,128)(2,1)S(1)}, u32[]{:S(2)}, u32[]{:S(2)}) collective-permute-start(bf16[272,1024]{1,0:T(8,128)(2,1)S(1)} %get-tuple-element.29.refs_0_), channel_id=1, source_target_pairs={{0,2},{1,3},{2,0},{3,1},{4,6},{5,7},{6,4},{7,5},{8,10},{9,11},{10,... | collective-permute-start | bytes 1671176 | tf_op jit(solution)/shard_map/ppermute | solution.py:215
  5.9 0.0 collective-permute-start.4
  5.9 4.5 %collective-permute-start.2 = (f32[1,512]{1,0:T(1,128)S(1)}, f32[1,512]{1,0:T(1,128)S(1)}, u32[]{:S(2)}, u32[]{:S(2)}) collective-permute-start(f32[1,512]{1,0:T(1,128)S(1)} %get-tuple-element.23), channel_id=1, source_target_pairs={{0,8},{1,9},{2,10},{3,11},{12,4},{13,5},{14,6},{15,7},{16,24},{17,... | collective-permute-start | bytes 6152 | tf_op jit(solution)/shard_map/ppermute | solution.py:219
  10.3 0.1 collective-permute-start.1
  10.4 4.2 %collective-permute-done.2.info_ref = f32[1,512]{1,0:T(1,128)S(1)} collective-permute-done((f32[1,512]{1,0:T(1,128)S(1)}, f32[1,512]{1,0:T(1,128)S(1)}, u32[]{:S(2)}, u32[]{:S(2)}) %collective-permute-start.2) | collective-permute-done | bytes 2080 | tf_op jit(solution)/shard_map/ppermute | solution.py:219
  14.6 2.7 %collective-permute-done.1.info_ref = f32[1,512]{1,0:T(1,128)S(1)} collective-permute-done((f32[1,512]{1,0:T(1,128)S(1)}, f32[1,512]{1,0:T(1,128)S(1)}, u32[]{:S(2)}, u32[]{:S(2)}) %collective-permute-start.1) | collective-permute-done | bytes 2080 | tf_op jit(solution)/shard_map/ppermute | solution.py:219
  17.3 0.0 collective-permute-done.line_ref
  17.3 2.7 %collective-permute-start.3 = (bf16[256,1024]{1,0:T(8,128)(2,1)S(1)}, bf16[256,1024]{1,0:T(8,128)(2,1)S(1)}, u32[]{:S(2)}, u32[]{:S(2)}) collective-permute-start(bf16[256,1024]{1,0:T(8,128)(2,1)S(1)} %get-tuple-element.26), channel_id=1, source_target_pairs={{0,8},{1,9},{2,10},{3,11},{12,4},{13,5},{14,6},{15,7},{16,24},{17,... | collective-permute-start | bytes 1572872 | tf_op jit(solution)/shard_map/ppermute | solution.py:219
  19.9 0.0 collective-permute-done.5.refs_2_
  20.0 0.1 collective-permute-start.7
  20.1 0.6 %collective-permute-start.6 = (bf16[128,1024]{1,0:T(8,128)(2,1)S(1)}, bf16[128,1024]{1,0:T(8,128)(2,1)S(1)}, u32[]{:S(2)}, u32[]{:S(2)}) collective-permute-start(bf16[128,1024]{1,0:T(8,128)(2,1)S(1)} %slice.8), channel_id=1, source_target_pairs={{0,1},{1,0},{2,3},{3,2},{4,5},{5,4},{6,7},{7,6},{8,9},{9,8},{10,11... | collective-permute-start | bytes 786440 | tf_op jit(solution)/shard_map/ppermute | solution.py:215
  20.6 0.0 collective-permute-done.4.refs_1_
  20.6 1.4 %collective-permute-done.6.refs_3_ = bf16[128,1024]{1,0:T(8,128)(2,1)S(1)} collective-permute-done((bf16[128,1024]{1,0:T(8,128)(2,1)S(1)}, bf16[128,1024]{1,0:T(8,128)(2,1)S(1)}, u32[]{:S(2)}, u32[]{:S(2)}) %collective-permute-start.6) | collective-permute-done | bytes 262176 | tf_op jit(solution)/shard_map/ppermute | solution.py:215
  22.0 0.0 collective-permute-done.7.refs_4_
  22.0 2.0 %shard_map.29 = (f32[1024,128]{1,0:T(8,128)S(1)}, f32[1,256]{1,0:T(1,128)S(1)}, f32[1024,128]{1,0:T(8,128)S(1)}, f32[1,256]{1,0:T(1,128)S(1)}) custom-call(f32[1,512]{1,0:T(1,128)S(1)} %collective-permute-done.1.info_ref, bf16[256,1024]{1,0:T(8,128)(2,1)S(1)} %collective-permute-done.line_ref, bf16[272,1024]{1,0:T(8,128)(2,1)S(1)} %get-tuple-element.29.refs_0_, ...), custom_call_target="tpu_custom_call" | custom-call | flops 1 | bytes 1 | tf_op jit(solution)/shard_map/pallas_call | solution.py:247
  24.0 2.2 %collective-permute-start.8 = (f32[1,256]{1,0:T(1,128)S(1)}, f32[1,256]{1,0:T(1,128)S(1)}, u32[]{:S(2)}, u32[]{:S(2)}) collective-permute-start(f32[1,256]{1,0:T(1,128)S(1)} %get-tuple-element.34), channel_id=1, source_target_pairs={{4,0},{5,1},{6,2},{7,3},{8,4},{9,5},{10,6},{11,7},{12,8},{13,9},{1... | collective-permute-start | bytes 3080 | tf_op jit(solution)/shard_map/ppermute | solution.py:219
  26.3 3.9 %collective-permute-done.3.line_ref = bf16[256,1024]{1,0:T(8,128)(2,1)S(1)} collective-permute-done((bf16[256,1024]{1,0:T(8,128)(2,1)S(1)}, bf16[256,1024]{1,0:T(8,128)(2,1)S(1)}, u32[]{:S(2)}, u32[]{:S(2)}) %collective-permute-start.3) | collective-permute-done | bytes 524320 | tf_op jit(solution)/shard_map/ppermute | solution.py:219
  30.2 0.2 shard_map.30
  30.4 1.3 %collective-permute-start.9 = (f32[1,256]{1,0:T(1,128)S(1)}, f32[1,256]{1,0:T(1,128)S(1)}, u32[]{:S(2)}, u32[]{:S(2)}) collective-permute-start(f32[1,256]{1,0:T(1,128)S(1)} %get-tuple-element.37), channel_id=1, source_target_pairs={{8,0},{9,1},{10,2},{11,3},{4,12},{5,13},{6,14},{7,15},{24,16},{25,... | collective-permute-start | bytes 3080 | tf_op jit(solution)/shard_map/ppermute | solution.py:219
  31.7 1.6 %collective-permute-start.10 = (f32[1,256]{1,0:T(1,128)S(1)}, f32[1,256]{1,0:T(1,128)S(1)}, u32[]{:S(2)}, u32[]{:S(2)}) collective-permute-start(f32[1,256]{1,0:T(1,128)S(1)} %get-tuple-element.38), channel_id=1, source_target_pairs={{0,2},{1,3},{2,0},{3,1},{4,6},{5,7},{6,4},{7,5},{8,10},{9,11},{10,... | collective-permute-start | bytes 3080 | tf_op jit(solution)/shard_map/ppermute | solution.py:215
  33.3 0.0 collective-permute-start.11
  33.3 0.0 collective-permute-done.8
  33.3 0.6 %collective-permute-start.12 = (f32[1,256]{1,0:T(1,128)S(1)}, f32[1,256]{1,0:T(1,128)S(1)}, u32[]{:S(2)}, u32[]{:S(2)}) collective-permute-start(f32[1,256]{1,0:T(1,128)S(1)} %get-tuple-element.40), channel_id=1, source_target_pairs={{0,1},{1,0},{2,3},{3,2},{4,5},{5,4},{6,7},{7,6},{8,9},{9,8},{10,11... | collective-permute-start | bytes 3080 | tf_op jit(solution)/shard_map/ppermute | solution.py:215
  33.9 3.7 %collective-permute-done.9 = f32[1,256]{1,0:T(1,128)S(1)} collective-permute-done((f32[1,256]{1,0:T(1,128)S(1)}, f32[1,256]{1,0:T(1,128)S(1)}, u32[]{:S(2)}, u32[]{:S(2)}) %collective-permute-start.9) | collective-permute-done | bytes 1056 | tf_op jit(solution)/shard_map/ppermute | solution.py:219
  37.6 0.0 collective-permute-done.10
  37.6 0.0 collective-permute-done.11
  37.6 0.0 collective-permute-done.12
  37.6 0.6 %add_log-plus-one_fusion = f32[1,256]{1,0:T(1,128)} fusion(f32[1,256]{1,0:T(1,128)S(1)} %collective-permute-done.12, f32[1,256]{1,0:T(1,128)S(1)} %collective-permute-done.11, f32[1,256]{1,0:T(1,128)S(1)} %collective-permute-done.10, f32[1,256]{1,0:T(1,128)S(1)} %collective-permute-done.9, f32[1,256]{1,0:T(1,128)S(1)} %get-tuple-element.33, ...), kind=kLoop, calls=%fused_computation | loop fusion | flops 1280 | bytes 7168 | tf_op jit(solution)/shard_map/log1p | solution.py:263
  (2 shorter events, 0.0 us)
Async XLA Ops:
  0.0 3.0 %copy-start.1 = (s32[256]{0:T(256)S(1)}, s32[256]{0:T(256)}, u32[]{:S(2)}) copy-start(s32[256]{0:T(256)} %param.3) | copy-start | bytes 3076
  0.0 17.3 %collective-permute-start = (bf16[256,1024]{1,0:T(8,128)(2,1)}, bf16[256,1024]{1,0:T(8,128)(2,1)S(1)}, u32[]{:S(2)}, u32[]{:S(2)}) collective-permute-start(bf16[256,1024]{1,0:T(8,128)(2,1)} %rows_ref.1), channel_id=1, source_target_pairs={{0,4},{1,5},{2,6},{3,7},{4,8},{5,9},{6,10},{7,11},{8,12},{9,13},{1... | collective-permute-start | bytes 1572872 | tf_op jit(solution)/shard_map/ppermute | solution.py:219
  3.0 1.1 %copy-start = (bf16[256,1024]{1,0:T(8,128)(2,1)S(1)}, bf16[256,1024]{1,0:T(8,128)(2,1)}, u32[]{:S(2)}) copy-start(bf16[256,1024]{1,0:T(8,128)(2,1)} %rows_ref.1) | copy-start | bytes 1572868
  4.3 15.6 %collective-permute-start.5 = (bf16[272,1024]{1,0:T(8,128)(2,1)S(1)}, bf16[272,1024]{1,0:T(8,128)(2,1)S(1)}, u32[]{:S(2)}, u32[]{:S(2)}) collective-permute-start(bf16[272,1024]{1,0:T(8,128)(2,1)S(1)} %get-tuple-element.29.refs_0_), channel_id=1, source_target_pairs={{0,2},{1,3},{2,0},{3,1},{4,6},{5,7},{6,4},{7,5},{8,10},{9,11},{10,... | collective-permute-start | bytes 1671176 | tf_op jit(solution)/shard_map/ppermute | solution.py:215
  5.9 14.8 %collective-permute-start.4 = (bf16[272,1024]{1,0:T(8,128)(2,1)S(1)}, bf16[272,1024]{1,0:T(8,128)(2,1)S(1)}, u32[]{:S(2)}, u32[]{:S(2)}) collective-permute-start(bf16[272,1024]{1,0:T(8,128)(2,1)S(1)} %get-tuple-element.29.refs_0_), channel_id=1, source_target_pairs={{0,1},{1,0},{2,3},{3,2},{4,5},{5,4},{6,7},{7,6},{8,9},{9,8},{10,11... | collective-permute-start | bytes 1671176 | tf_op jit(solution)/shard_map/ppermute | solution.py:215
  5.9 8.7 %collective-permute-start.2 = (f32[1,512]{1,0:T(1,128)S(1)}, f32[1,512]{1,0:T(1,128)S(1)}, u32[]{:S(2)}, u32[]{:S(2)}) collective-permute-start(f32[1,512]{1,0:T(1,128)S(1)} %get-tuple-element.23), channel_id=1, source_target_pairs={{0,8},{1,9},{2,10},{3,11},{12,4},{13,5},{14,6},{15,7},{16,24},{17,... | collective-permute-start | bytes 6152 | tf_op jit(solution)/shard_map/ppermute | solution.py:219
  10.3 6.9 %collective-permute-start.1 = (f32[1,512]{1,0:T(1,128)S(1)}, f32[1,512]{1,0:T(1,128)S(1)}, u32[]{:S(2)}, u32[]{:S(2)}) collective-permute-start(f32[1,512]{1,0:T(1,128)S(1)} %get-tuple-element.23), channel_id=1, source_target_pairs={{0,4},{1,5},{2,6},{3,7},{4,8},{5,9},{6,10},{7,11},{8,12},{9,13},{1... | collective-permute-start | bytes 6152 | tf_op jit(solution)/shard_map/ppermute | solution.py:219
  17.3 12.9 %collective-permute-start.3 = (bf16[256,1024]{1,0:T(8,128)(2,1)S(1)}, bf16[256,1024]{1,0:T(8,128)(2,1)S(1)}, u32[]{:S(2)}, u32[]{:S(2)}) collective-permute-start(bf16[256,1024]{1,0:T(8,128)(2,1)S(1)} %get-tuple-element.26), channel_id=1, source_target_pairs={{0,8},{1,9},{2,10},{3,11},{12,4},{13,5},{14,6},{15,7},{16,24},{17,... | collective-permute-start | bytes 1572872 | tf_op jit(solution)/shard_map/ppermute | solution.py:219
  20.0 2.0 %collective-permute-start.7 = (bf16[144,1024]{1,0:T(8,128)(2,1)S(1)}, bf16[144,1024]{1,0:T(8,128)(2,1)S(1)}, u32[]{:S(2)}, u32[]{:S(2)}) collective-permute-start(bf16[144,1024]{1,0:T(8,128)(2,1)S(1)} %slice.9), channel_id=1, source_target_pairs={{0,1},{1,0},{2,3},{3,2},{4,5},{5,4},{6,7},{7,6},{8,9},{9,8},{10,11... | collective-permute-start | bytes 884744 | tf_op jit(solution)/shard_map/ppermute | solution.py:215
  20.1 1.9 %collective-permute-start.6 = (bf16[128,1024]{1,0:T(8,128)(2,1)S(1)}, bf16[128,1024]{1,0:T(8,128)(2,1)S(1)}, u32[]{:S(2)}, u32[]{:S(2)}) collective-permute-start(bf16[128,1024]{1,0:T(8,128)(2,1)S(1)} %slice.8), channel_id=1, source_target_pairs={{0,1},{1,0},{2,3},{3,2},{4,5},{5,4},{6,7},{7,6},{8,9},{9,8},{10,11... | collective-permute-start | bytes 786440 | tf_op jit(solution)/shard_map/ppermute | solution.py:215
  24.0 9.3 %collective-permute-start.8 = (f32[1,256]{1,0:T(1,128)S(1)}, f32[1,256]{1,0:T(1,128)S(1)}, u32[]{:S(2)}, u32[]{:S(2)}) collective-permute-start(f32[1,256]{1,0:T(1,128)S(1)} %get-tuple-element.34), channel_id=1, source_target_pairs={{4,0},{5,1},{6,2},{7,3},{8,4},{9,5},{10,6},{11,7},{12,8},{13,9},{1... | collective-permute-start | bytes 3080 | tf_op jit(solution)/shard_map/ppermute | solution.py:219
  30.4 7.2 %collective-permute-start.9 = (f32[1,256]{1,0:T(1,128)S(1)}, f32[1,256]{1,0:T(1,128)S(1)}, u32[]{:S(2)}, u32[]{:S(2)}) collective-permute-start(f32[1,256]{1,0:T(1,128)S(1)} %get-tuple-element.37), channel_id=1, source_target_pairs={{8,0},{9,1},{10,2},{11,3},{4,12},{5,13},{6,14},{7,15},{24,16},{25,... | collective-permute-start | bytes 3080 | tf_op jit(solution)/shard_map/ppermute | solution.py:219
  31.7 5.9 %collective-permute-start.10 = (f32[1,256]{1,0:T(1,128)S(1)}, f32[1,256]{1,0:T(1,128)S(1)}, u32[]{:S(2)}, u32[]{:S(2)}) collective-permute-start(f32[1,256]{1,0:T(1,128)S(1)} %get-tuple-element.38), channel_id=1, source_target_pairs={{0,2},{1,3},{2,0},{3,1},{4,6},{5,7},{6,4},{7,5},{8,10},{9,11},{10,... | collective-permute-start | bytes 3080 | tf_op jit(solution)/shard_map/ppermute | solution.py:215
  33.3 4.3 %collective-permute-start.11 = (f32[1,256]{1,0:T(1,128)S(1)}, f32[1,256]{1,0:T(1,128)S(1)}, u32[]{:S(2)}, u32[]{:S(2)}) collective-permute-start(f32[1,256]{1,0:T(1,128)S(1)} %get-tuple-element.39), channel_id=1, source_target_pairs={{0,3},{1,2},{2,1},{3,0},{4,7},{5,6},{6,5},{7,4},{8,11},{9,10},{10,... | collective-permute-start | bytes 3080 | tf_op jit(solution)/shard_map/ppermute | solution.py:215
  33.3 4.3 %collective-permute-start.12 = (f32[1,256]{1,0:T(1,128)S(1)}, f32[1,256]{1,0:T(1,128)S(1)}, u32[]{:S(2)}, u32[]{:S(2)}) collective-permute-start(f32[1,256]{1,0:T(1,128)S(1)} %get-tuple-element.40), channel_id=1, source_target_pairs={{0,1},{1,0},{2,3},{3,2},{4,5},{5,4},{6,7},{7,6},{8,9},{9,8},{10,11... | collective-permute-start | bytes 3080 | tf_op jit(solution)/shard_map/ppermute | solution.py:215

commit v13 on v12

--- a/solution.py
+++ b/solution.py
@@ -111,13 +111,12 @@
     return jnp.where(mates, jnp.exp(similar * inverse_temp), 0.0)
 
 
-def unit_kernel(rows_ref, ids_ref, units_ref, info_ref, *block_refs):
+def unit_kernel(rows_ref, ids_ref, info_ref, *block_refs):
     rows, width = rows_ref.shape
     features = rows_ref[...].astype(jnp.float32)
     scale = lax.rsqrt(jnp.sum(features * features, axis=1, keepdims=True) + 1e-06)
     ids = ids_ref[...].astype(jnp.float32)
     units = (features * scale).astype(jnp.bfloat16)
-    units_ref[...] = units
     info_ref[:, :rows] = ids
     info_ref[:, rows:] = jnp.broadcast_to(scale, (rows, LANES)).T[:1]
     first = 0
@@ -135,7 +134,7 @@
     return (rows_ref[...].astype(jnp.float32) * wide).astype(jnp.bfloat16)
 
 
-def line_sums(moves, query_parts, ids_ref, info_ref, line_ref, is_raw, column_ref, sums_ref):
+def line_sums(moves, query_parts, ids_ref, info_ref, line_ref, column_ref, sums_ref):
     rows = column_ref.shape[1]
     plane = lax.axis_index("gx") // PLANE
     arrived = functools.reduce(jnp.logical_or, [plane == receiver for _, receiver in moves])
@@ -144,7 +143,7 @@
     @pl.when(arrived)
     def _():
         key_ids = info_ref[:, :rows]
-        key_rows = scaled_rows(line_ref, info_ref) if is_raw else line_ref[...]
+        key_rows = scaled_rows(line_ref, info_ref)
         column = jnp.zeros((1, rows), jnp.float32)
         first = 0
         for query_ref, size in query_parts:
@@ -182,7 +181,7 @@
         first += size
     mass_ref[...] = mass
     sums_ref[...] = jnp.zeros_like(sums_ref)
-    line_sums(moves, query_parts, ids_ref, info_ref, line_ref, True, column_ref, sums_ref)
+    line_sums(moves, query_parts, ids_ref, info_ref, line_ref, column_ref, sums_ref)
 
 
 def last_kernel(moves, info_ref, line_ref, ids_ref, earlier_ref, mass_ref, *refs):
@@ -191,7 +190,7 @@
     rows = column_ref.shape[1]
     sums_ref[...] = earlier_ref[...]
     query_parts = query_parts_of(query_refs, rows)
-    line_sums(moves, query_parts, ids_ref, info_ref, line_ref, False, column_ref, sums_ref)
+    line_sums(moves, query_parts, ids_ref, info_ref, line_ref, column_ref, sums_ref)
     for m in range(PLANE):
         row_sum = jnp.sum(sums_ref[pl.ds(m * rows, rows), :].T, axis=0, keepdims=True)
         if m == 0:
@@ -219,16 +218,16 @@
         return lax.ppermute(value, "gx", pairs)
 
     first_moves = [(0, 1), (1, 2), (2, 3), (3, 0)]
-    last_moves = [(0, 2), (3, 1)]
+    last_moves = [(0, 2), (1, 3)]
+    forward_moves = [(1, 2), (2, 3)]
     first_back = [(b, a) for a, b in first_moves]
     last_back = [(b, a) for a, b in last_moves]
 
     half = row_count // 2
     first_line = on_line(embeddings, first_moves)
-    units, info, block = pl.pallas_call(
+    info, block = pl.pallas_call(
         unit_kernel,
         out_shape=(
-            rows_of(row_count),
             jax.ShapeDtypeStruct((1, 2 * row_count), jnp.float32),
             rows_of(row_count + ID_ROWS),
         ),
@@ -238,10 +237,10 @@
     across = in_plane(block, 2)
     sibling = in_plane(block, 1)
     first_info, last_info = on_line(info, first_moves), on_line(info, last_moves)
-    first_line, first_info, last_info, units = lax.optimization_barrier(
-        (first_line, first_info, last_info, units)
-    )
-    last_line = on_line(units, last_moves)
+    first_line, first_info, last_info = lax.optimization_barrier(
+        (first_line, first_info, last_info)
+    )
+    last_line = on_line(first_line, forward_moves)
     corner = [in_plane(piece, 1) for piece in (across[:half], across[half:])]
     queries = (block, sibling, across, *corner)
     ids, first_column, first_sums, mass = pl.pallas_call(

time: 38.4 us -> 37.7 us (0.982)
  starting transfers between devices: 18.1 us -> 17.5 us
    ppermute x6, waiting for transfers between devices: 14.4 us -> 13.7 us  [on_line(): return lax.ppermute(value, 'gx', pairs)]
    ppermute x6, starting transfers between devices: 13.7 us -> 13.2 us  [on_line(): return lax.ppermute(value, 'gx', pairs)]
    ppermute x7, waiting for transfers between devices: 1.37 us -> 1.9 us  [in_plane(): return lax.ppermute(value, 'gx', [(i, i ^ step) for i in range(peers)])]
where the time goes in v13:
time: 37.7 us; the launch traced here: 37.5 us
  starting transfers between devices  17.5 us (46%)
  waiting for transfers between devices  15.6 us (41%)
  Pallas kernels  2.51 us (7%)
  local copies, waits for them, and re-layouts  1.11 us (3%)
  other arithmetic  0.58 us (2%)
    ppermute x6, waiting for transfers between devices, on_line(): return lax.ppermute(value, 'gx', pairs)  13.7 us
    ppermute x6, starting transfers between devices, on_line(): return lax.ppermute(value, 'gx', pairs)  13.2 us
    ppermute x7, starting transfers between devices, in_plane(): return lax.ppermute(value, 'gx', [(i, i ^ step) for i in range(peers)])  4.37 us
    pallas_call x1, Pallas kernels, grid_plan(): pl.pallas_call(functools.partial(first_kernel, first_moves), out_shape=(l...  2.04 us
    ppermute x7, waiting for transfers between devices, in_plane(): return lax.ppermute(value, 'gx', [(i, i ^ step) for i in range(peers)])  1.9 us
    unnamed x4, local copies, waits for them, and re-layouts  1.08 us
  transfers between devices with their start and end apart: 13, of which 5 were waited for; matrix products, arithmetic and copies ran while one was open for 0% of the time, Pallas kernels for 7%

profile of v13, /device:TPU:0, one launch (start us, length us, event | category | flops | bytes accessed | tf_op | source)
XLA Modules:
  0.0 37.5 jit_solution(29073214875625875)
XLA Ops:
  0.0 0.0 copy-start.1
  0.0 3.0 %collective-permute-start = (bf16[256,1024]{1,0:T(8,128)(2,1)}, bf16[256,1024]{1,0:T(8,128)(2,1)S(1)}, u32[]{:S(2)}, u32[]{:S(2)}) collective-permute-start(bf16[256,1024]{1,0:T(8,128)(2,1)} %rows_ref.1), channel_id=1, source_target_pairs={{0,4},{1,5},{2,6},{3,7},{4,8},{5,9},{6,10},{7,11},{8,12},{9,13},{1... | collective-permute-start | bytes 1572872 | tf_op jit(solution)/shard_map/ppermute | solution.py:218
  3.0 0.0 copy-done.1
  3.0 0.0 copy-start
  3.0 1.1 %copy-done = bf16[256,1024]{1,0:T(8,128)(2,1)S(1)} copy-done((bf16[256,1024]{1,0:T(8,128)(2,1)S(1)}, bf16[256,1024]{1,0:T(8,128)(2,1)}, u32[]{:S(2)}) %copy-start) | copy-done | bytes 524312
  4.1 0.2 shard_map.28
  4.3 1.5 %collective-permute-start.5 = (bf16[272,1024]{1,0:T(8,128)(2,1)S(1)}, bf16[272,1024]{1,0:T(8,128)(2,1)S(1)}, u32[]{:S(2)}, u32[]{:S(2)}) collective-permute-start(bf16[272,1024]{1,0:T(8,128)(2,1)S(1)} %get-tuple-element.25.refs_0_), channel_id=1, source_target_pairs={{0,2},{1,3},{2,0},{3,1},{4,6},{5,7},{6,4},{7,5},{8,10},{9,11},{10,... | collective-permute-start | bytes 1671176 | tf_op jit(solution)/shard_map/ppermute | solution.py:214
  5.9 0.0 collective-permute-start.4
  5.9 4.5 %collective-permute-start.2 = (f32[1,512]{1,0:T(1,128)S(1)}, f32[1,512]{1,0:T(1,128)S(1)}, u32[]{:S(2)}, u32[]{:S(2)}) collective-permute-start(f32[1,512]{1,0:T(1,128)S(1)} %get-tuple-element.21), channel_id=1, source_target_pairs={{0,8},{1,9},{2,10},{3,11},{4,12},{5,13},{6,14},{7,15},{16,24},{17,... | collective-permute-start | bytes 6152 | tf_op jit(solution)/shard_map/ppermute | solution.py:218
  10.3 0.7 %collective-permute-start.1 = (f32[1,512]{1,0:T(1,128)S(1)}, f32[1,512]{1,0:T(1,128)S(1)}, u32[]{:S(2)}, u32[]{:S(2)}) collective-permute-start(f32[1,512]{1,0:T(1,128)S(1)} %get-tuple-element.21), channel_id=1, source_target_pairs={{0,4},{1,5},{2,6},{3,7},{4,8},{5,9},{6,10},{7,11},{8,12},{9,13},{1... | collective-permute-start | bytes 6152 | tf_op jit(solution)/shard_map/ppermute | solution.py:218
  11.0 3.5 %collective-permute-done.2.info_ref = f32[1,512]{1,0:T(1,128)S(1)} collective-permute-done((f32[1,512]{1,0:T(1,128)S(1)}, f32[1,512]{1,0:T(1,128)S(1)}, u32[]{:S(2)}, u32[]{:S(2)}) %collective-permute-start.2) | collective-permute-done | bytes 2080 | tf_op jit(solution)/shard_map/ppermute | solution.py:218
  14.6 2.7 %collective-permute-done.1.info_ref = f32[1,512]{1,0:T(1,128)S(1)} collective-permute-done((f32[1,512]{1,0:T(1,128)S(1)}, f32[1,512]{1,0:T(1,128)S(1)}, u32[]{:S(2)}, u32[]{:S(2)}) %collective-permute-start.1) | collective-permute-done | bytes 2080 | tf_op jit(solution)/shard_map/ppermute | solution.py:218
  17.2 0.0 collective-permute-done.line_ref
  17.2 0.7 %collective-permute-start.3 = (bf16[256,1024]{1,0:T(8,128)(2,1)S(1)}, bf16[256,1024]{1,0:T(8,128)(2,1)S(1)}, u32[]{:S(2)}, u32[]{:S(2)}) collective-permute-start(bf16[256,1024]{1,0:T(8,128)(2,1)S(1)} %collective-permute-done.line_ref), channel_id=1, source_target_pairs={{4,8},{5,9},{6,10},{7,11},{8,12},{9,13},{10,14},{11,15},{20,24},{2... | collective-permute-start | bytes 1572872 | tf_op jit(solution)/shard_map/ppermute | solution.py:218
  17.9 0.5 %collective-permute-done.5.refs_2_ = bf16[272,1024]{1,0:T(8,128)(2,1)S(1)} collective-permute-done((bf16[272,1024]{1,0:T(8,128)(2,1)S(1)}, bf16[272,1024]{1,0:T(8,128)(2,1)S(1)}, u32[]{:S(2)}, u32[]{:S(2)}) %collective-permute-start.5) | collective-permute-done | bytes 557088 | tf_op jit(solution)/shard_map/ppermute | solution.py:214
  18.5 0.1 collective-permute-start.7
  18.6 0.6 %collective-permute-start.6 = (bf16[128,1024]{1,0:T(8,128)(2,1)S(1)}, bf16[128,1024]{1,0:T(8,128)(2,1)S(1)}, u32[]{:S(2)}, u32[]{:S(2)}) collective-permute-start(bf16[128,1024]{1,0:T(8,128)(2,1)S(1)} %slice.8), channel_id=1, source_target_pairs={{0,1},{1,0},{2,3},{3,2},{4,5},{5,4},{6,7},{7,6},{8,9},{9,8},{10,11... | collective-permute-start | bytes 786440 | tf_op jit(solution)/shard_map/ppermute | solution.py:214
  19.1 0.0 collective-permute-done.4.refs_1_
  19.1 1.4 %collective-permute-done.6.refs_3_ = bf16[128,1024]{1,0:T(8,128)(2,1)S(1)} collective-permute-done((bf16[128,1024]{1,0:T(8,128)(2,1)S(1)}, bf16[128,1024]{1,0:T(8,128)(2,1)S(1)}, u32[]{:S(2)}, u32[]{:S(2)}) %collective-permute-start.6) | collective-permute-done | bytes 262176 | tf_op jit(solution)/shard_map/ppermute | solution.py:214
  20.5 0.0 collective-permute-done.7.refs_4_
  20.5 2.0 %shard_map.29 = (f32[1024,128]{1,0:T(8,128)S(1)}, f32[1,256]{1,0:T(1,128)S(1)}, f32[1024,128]{1,0:T(8,128)S(1)}, f32[1,256]{1,0:T(1,128)S(1)}) custom-call(f32[1,512]{1,0:T(1,128)S(1)} %collective-permute-done.1.info_ref, bf16[256,1024]{1,0:T(8,128)(2,1)S(1)} %collective-permute-done.line_ref, bf16[272,1024]{1,0:T(8,128)(2,1)S(1)} %get-tuple-element.25.refs_0_, ...), custom_call_target="tpu_custom_call" | custom-call | flops 1 | bytes 1 | tf_op jit(solution)/shard_map/pallas_call | solution.py:246
  22.5 3.0 %collective-permute-start.8 = (f32[1,256]{1,0:T(1,128)S(1)}, f32[1,256]{1,0:T(1,128)S(1)}, u32[]{:S(2)}, u32[]{:S(2)}) collective-permute-start(f32[1,256]{1,0:T(1,128)S(1)} %get-tuple-element.30), channel_id=1, source_target_pairs={{4,0},{5,1},{6,2},{7,3},{8,4},{9,5},{10,6},{11,7},{12,8},{13,9},{1... | collective-permute-start | bytes 3080 | tf_op jit(solution)/shard_map/ppermute | solution.py:218
  25.5 0.0 collective-permute-done.3.line_ref
  25.5 0.2 shard_map.30
  25.8 1.3 %collective-permute-start.9 = (f32[1,256]{1,0:T(1,128)S(1)}, f32[1,256]{1,0:T(1,128)S(1)}, u32[]{:S(2)}, u32[]{:S(2)}) collective-permute-start(f32[1,256]{1,0:T(1,128)S(1)} %get-tuple-element.33), channel_id=1, source_target_pairs={{8,0},{9,1},{10,2},{11,3},{12,4},{13,5},{14,6},{15,7},{24,16},{25,... | collective-permute-start | bytes 3080 | tf_op jit(solution)/shard_map/ppermute | solution.py:218
  27.1 1.6 %collective-permute-start.10 = (f32[1,256]{1,0:T(1,128)S(1)}, f32[1,256]{1,0:T(1,128)S(1)}, u32[]{:S(2)}, u32[]{:S(2)}) collective-permute-start(f32[1,256]{1,0:T(1,128)S(1)} %get-tuple-element.34), channel_id=1, source_target_pairs={{0,2},{1,3},{2,0},{3,1},{4,6},{5,7},{6,4},{7,5},{8,10},{9,11},{10,... | collective-permute-start | bytes 3080 | tf_op jit(solution)/shard_map/ppermute | solution.py:214
  28.7 0.0 collective-permute-start.11
  28.7 0.0 collective-permute-done.8
  28.7 0.6 %collective-permute-start.12 = (f32[1,256]{1,0:T(1,128)S(1)}, f32[1,256]{1,0:T(1,128)S(1)}, u32[]{:S(2)}, u32[]{:S(2)}) collective-permute-start(f32[1,256]{1,0:T(1,128)S(1)} %get-tuple-element.36), channel_id=1, source_target_pairs={{0,1},{1,0},{2,3},{3,2},{4,5},{5,4},{6,7},{7,6},{8,9},{9,8},{10,11... | collective-permute-start | bytes 3080 | tf_op jit(solution)/shard_map/ppermute | solution.py:214
  29.3 7.6 %collective-permute-done.9 = f32[1,256]{1,0:T(1,128)S(1)} collective-permute-done((f32[1,256]{1,0:T(1,128)S(1)}, f32[1,256]{1,0:T(1,128)S(1)}, u32[]{:S(2)}, u32[]{:S(2)}) %collective-permute-start.9) | collective-permute-done | bytes 1056 | tf_op jit(solution)/shard_map/ppermute | solution.py:218
  36.9 0.0 collective-permute-done.10
  36.9 0.0 collective-permute-done.11
  36.9 0.0 collective-permute-done.12
  36.9 0.6 %add_log-plus-one_fusion = f32[1,256]{1,0:T(1,128)} fusion(f32[1,256]{1,0:T(1,128)S(1)} %collective-permute-done.12, f32[1,256]{1,0:T(1,128)S(1)} %collective-permute-done.11, f32[1,256]{1,0:T(1,128)S(1)} %collective-permute-done.10, f32[1,256]{1,0:T(1,128)S(1)} %collective-permute-done.9, f32[1,256]{1,0:T(1,128)S(1)} %get-tuple-element.29, ...), kind=kLoop, calls=%fused_computation | loop fusion | flops 1280 | bytes 7168 | tf_op jit(solution)/shard_map/log1p | solution.py:262
  (2 shorter events, 0.0 us)
Async XLA Ops:
  0.0 3.0 %copy-start.1 = (s32[256]{0:T(256)S(1)}, s32[256]{0:T(256)}, u32[]{:S(2)}) copy-start(s32[256]{0:T(256)} %param.3) | copy-start | bytes 3076
  0.0 17.2 %collective-permute-start = (bf16[256,1024]{1,0:T(8,128)(2,1)}, bf16[256,1024]{1,0:T(8,128)(2,1)S(1)}, u32[]{:S(2)}, u32[]{:S(2)}) collective-permute-start(bf16[256,1024]{1,0:T(8,128)(2,1)} %rows_ref.1), channel_id=1, source_target_pairs={{0,4},{1,5},{2,6},{3,7},{4,8},{5,9},{6,10},{7,11},{8,12},{9,13},{1... | collective-permute-start | bytes 1572872 | tf_op jit(solution)/shard_map/ppermute | solution.py:218
  3.0 1.1 %copy-start = (bf16[256,1024]{1,0:T(8,128)(2,1)S(1)}, bf16[256,1024]{1,0:T(8,128)(2,1)}, u32[]{:S(2)}) copy-start(bf16[256,1024]{1,0:T(8,128)(2,1)} %rows_ref.1) | copy-start | bytes 1572868
  4.3 14.1 %collective-permute-start.5 = (bf16[272,1024]{1,0:T(8,128)(2,1)S(1)}, bf16[272,1024]{1,0:T(8,128)(2,1)S(1)}, u32[]{:S(2)}, u32[]{:S(2)}) collective-permute-start(bf16[272,1024]{1,0:T(8,128)(2,1)S(1)} %get-tuple-element.25.refs_0_), channel_id=1, source_target_pairs={{0,2},{1,3},{2,0},{3,1},{4,6},{5,7},{6,4},{7,5},{8,10},{9,11},{10,... | collective-permute-start | bytes 1671176 | tf_op jit(solution)/shard_map/ppermute | solution.py:214
  5.9 13.3 %collective-permute-start.4 = (bf16[272,1024]{1,0:T(8,128)(2,1)S(1)}, bf16[272,1024]{1,0:T(8,128)(2,1)S(1)}, u32[]{:S(2)}, u32[]{:S(2)}) collective-permute-start(bf16[272,1024]{1,0:T(8,128)(2,1)S(1)} %get-tuple-element.25.refs_0_), channel_id=1, source_target_pairs={{0,1},{1,0},{2,3},{3,2},{4,5},{5,4},{6,7},{7,6},{8,9},{9,8},{10,11... | collective-permute-start | bytes 1671176 | tf_op jit(solution)/shard_map/ppermute | solution.py:214
  5.9 8.7 %collective-permute-start.2 = (f32[1,512]{1,0:T(1,128)S(1)}, f32[1,512]{1,0:T(1,128)S(1)}, u32[]{:S(2)}, u32[]{:S(2)}) collective-permute-start(f32[1,512]{1,0:T(1,128)S(1)} %get-tuple-element.21), channel_id=1, source_target_pairs={{0,8},{1,9},{2,10},{3,11},{4,12},{5,13},{6,14},{7,15},{16,24},{17,... | collective-permute-start | bytes 6152 | tf_op jit(solution)/shard_map/ppermute | solution.py:218
  10.3 6.9 %collective-permute-start.1 = (f32[1,512]{1,0:T(1,128)S(1)}, f32[1,512]{1,0:T(1,128)S(1)}, u32[]{:S(2)}, u32[]{:S(2)}) collective-permute-start(f32[1,512]{1,0:T(1,128)S(1)} %get-tuple-element.21), channel_id=1, source_target_pairs={{0,4},{1,5},{2,6},{3,7},{4,8},{5,9},{6,10},{7,11},{8,12},{9,13},{1... | collective-permute-start | bytes 6152 | tf_op jit(solution)/shard_map/ppermute | solution.py:218
  17.2 8.3 %collective-permute-start.3 = (bf16[256,1024]{1,0:T(8,128)(2,1)S(1)}, bf16[256,1024]{1,0:T(8,128)(2,1)S(1)}, u32[]{:S(2)}, u32[]{:S(2)}) collective-permute-start(bf16[256,1024]{1,0:T(8,128)(2,1)S(1)} %collective-permute-done.line_ref), channel_id=1, source_target_pairs={{4,8},{5,9},{6,10},{7,11},{8,12},{9,13},{10,14},{11,15},{20,24},{2... | collective-permute-start | bytes 1572872 | tf_op jit(solution)/shard_map/ppermute | solution.py:218
  18.5 2.0 %collective-permute-start.7 = (bf16[144,1024]{1,0:T(8,128)(2,1)S(1)}, bf16[144,1024]{1,0:T(8,128)(2,1)S(1)}, u32[]{:S(2)}, u32[]{:S(2)}) collective-permute-start(bf16[144,1024]{1,0:T(8,128)(2,1)S(1)} %slice.9), channel_id=1, source_target_pairs={{0,1},{1,0},{2,3},{3,2},{4,5},{5,4},{6,7},{7,6},{8,9},{9,8},{10,11... | collective-permute-start | bytes 884744 | tf_op jit(solution)/shard_map/ppermute | solution.py:214
  18.6 1.9 %collective-permute-start.6 = (bf16[128,1024]{1,0:T(8,128)(2,1)S(1)}, bf16[128,1024]{1,0:T(8,128)(2,1)S(1)}, u32[]{:S(2)}, u32[]{:S(2)}) collective-permute-start(bf16[128,1024]{1,0:T(8,128)(2,1)S(1)} %slice.8), channel_id=1, source_target_pairs={{0,1},{1,0},{2,3},{3,2},{4,5},{5,4},{6,7},{7,6},{8,9},{9,8},{10,11... | collective-permute-start | bytes 786440 | tf_op jit(solution)/shard_map/ppermute | solution.py:214
  22.5 6.1 %collective-permute-start.8 = (f32[1,256]{1,0:T(1,128)S(1)}, f32[1,256]{1,0:T(1,128)S(1)}, u32[]{:S(2)}, u32[]{:S(2)}) collective-permute-start(f32[1,256]{1,0:T(1,128)S(1)} %get-tuple-element.30), channel_id=1, source_target_pairs={{4,0},{5,1},{6,2},{7,3},{8,4},{9,5},{10,6},{11,7},{12,8},{13,9},{1... | collective-permute-start | bytes 3080 | tf_op jit(solution)/shard_map/ppermute | solution.py:218
  25.8 11.1 %collective-permute-start.9 = (f32[1,256]{1,0:T(1,128)S(1)}, f32[1,256]{1,0:T(1,128)S(1)}, u32[]{:S(2)}, u32[]{:S(2)}) collective-permute-start(f32[1,256]{1,0:T(1,128)S(1)} %get-tuple-element.33), channel_id=1, source_target_pairs={{8,0},{9,1},{10,2},{11,3},{12,4},{13,5},{14,6},{15,7},{24,16},{25,... | collective-permute-start | bytes 3080 | tf_op jit(solution)/shard_map/ppermute | solution.py:218
  27.1 9.8 %collective-permute-start.10 = (f32[1,256]{1,0:T(1,128)S(1)}, f32[1,256]{1,0:T(1,128)S(1)}, u32[]{:S(2)}, u32[]{:S(2)}) collective-permute-start(f32[1,256]{1,0:T(1,128)S(1)} %get-tuple-element.34), channel_id=1, source_target_pairs={{0,2},{1,3},{2,0},{3,1},{4,6},{5,7},{6,4},{7,5},{8,10},{9,11},{10,... | collective-permute-start | bytes 3080 | tf_op jit(solution)/shard_map/ppermute | solution.py:214
  28.7 8.2 %collective-permute-start.11 = (f32[1,256]{1,0:T(1,128)S(1)}, f32[1,256]{1,0:T(1,128)S(1)}, u32[]{:S(2)}, u32[]{:S(2)}) collective-permute-start(f32[1,256]{1,0:T(1,128)S(1)} %get-tuple-element.35), channel_id=1, source_target_pairs={{0,3},{1,2},{2,1},{3,0},{4,7},{5,6},{6,5},{7,4},{8,11},{9,10},{10,... | collective-permute-start | bytes 3080 | tf_op jit(solution)/shard_map/ppermute | solution.py:214
  28.7 8.2 %collective-permute-start.12 = (f32[1,256]{1,0:T(1,128)S(1)}, f32[1,256]{1,0:T(1,128)S(1)}, u32[]{:S(2)}, u32[]{:S(2)}) collective-permute-start(f32[1,256]{1,0:T(1,128)S(1)} %get-tuple-element.36), channel_id=1, source_target_pairs={{0,1},{1,0},{2,3},{3,2},{4,5},{5,4},{6,7},{7,6},{8,9},{9,8},{10,11... | collective-permute-start | bytes 3080 | tf_op jit(solution)/shard_map/ppermute | solution.py:214

commit v14 on v13

--- a/solution.py
+++ b/solution.py
@@ -219,9 +219,9 @@
 
     first_moves = [(0, 1), (1, 2), (2, 3), (3, 0)]
     last_moves = [(0, 2), (1, 3)]
-    forward_moves = [(1, 2), (2, 3)]
+    swap_moves = last_moves + [(b, a) for a, b in last_moves]
+    forward_moves = [(1, 2), (2, 3), (3, 1), (0, 0)]
     first_back = [(b, a) for a, b in first_moves]
-    last_back = [(b, a) for a, b in last_moves]
 
     half = row_count // 2
     first_line = on_line(embeddings, first_moves)
@@ -236,7 +236,7 @@
     )(embeddings, cluster_ids.reshape(1, row_count))
     across = in_plane(block, 2)
     sibling = in_plane(block, 1)
-    first_info, last_info = on_line(info, first_moves), on_line(info, last_moves)
+    first_info, last_info = on_line(info, first_moves), on_line(info, swap_moves)
     first_line, first_info, last_info = lax.optimization_barrier(
         (first_line, first_info, last_info)
     )
@@ -257,7 +257,7 @@
         compiler_params=params,
     )(last_info, last_line, ids, first_sums, mass, *queries)
     returned_first, row_sums[1] = lax.optimization_barrier((returned_first, row_sums[1]))
-    returned = [on_line(last_column, last_back)]
+    returned = [on_line(last_column, swap_moves)]
     returned += [in_plane(row_sums[step], step) for step in (2, 3, 1)]
     return jnp.log1p(sum(returned, row_sums[0] + returned_first)).reshape(row_count)
 

time: 37.7 us -> 39.3 us (1.042)
  starting transfers between devices: 17.5 us -> 22.5 us
  waiting for transfers between devices: 15.6 us -> 12.4 us
    ppermute x6, waiting for transfers between devices: 13.7 us -> 8.23 us  [on_line(): return lax.ppermute(value, 'gx', pairs)]
    ppermute x6, starting transfers between devices: 13.2 us -> 18.2 us  [on_line(): return lax.ppermute(value, 'gx', pairs)]
    ppermute x7, waiting for transfers between devices: 1.9 us -> 4.13 us  [in_plane(): return lax.ppermute(value, 'gx', [(i, i ^ step) for i in range(peers)])]
  transfers between devices with their start and end apart: 13 -> 13, of which waited for: 5 -> 6; matrix products, arithmetic and copies ran while one was open for 0% -> 0% of each run, Pallas kernels for 7% -> 6%
where the time goes in v14:
time: 39.3 us; the launch traced here: 39.2 us
  starting transfers between devices  22.5 us (57%)
  waiting for transfers between devices  12.4 us (32%)
  Pallas kernels  2.51 us (6%)
  local copies, waits for them, and re-layouts  1.11 us (3%)
  other arithmetic  0.58 us (1%)
    ppermute x6, starting transfers between devices, on_line(): return lax.ppermute(value, 'gx', pairs)  18.2 us
    ppermute x6, waiting for transfers between devices, on_line(): return lax.ppermute(value, 'gx', pairs)  8.23 us
    ppermute x7, starting transfers between devices, in_plane(): return lax.ppermute(value, 'gx', [(i, i ^ step) for i in range(peers)])  4.3 us
    ppermute x7, waiting for transfers between devices, in_plane(): return lax.ppermute(value, 'gx', [(i, i ^ step) for i in range(peers)])  4.13 us
    pallas_call x1, Pallas kernels, grid_plan(): pl.pallas_call(functools.partial(first_kernel, first_moves), out_shape=(l...  2.04 us
    unnamed x4, local copies, waits for them, and re-layouts  1.08 us
  transfers between devices with their start and end apart: 13, of which 6 were waited for; matrix products, arithmetic and copies ran while one was open for 0% of the time, Pallas kernels for 6%

profile of v14, /device:TPU:0, one launch (start us, length us, event | category | flops | bytes accessed | tf_op | source)
XLA Modules:
  0.0 39.2 jit_solution(16418945481875842908)
XLA Ops:
  0.0 0.0 copy-start.1
  0.0 3.0 %collective-permute-start = (bf16[256,1024]{1,0:T(8,128)(2,1)}, bf16[256,1024]{1,0:T(8,128)(2,1)S(1)}, u32[]{:S(2)}, u32[]{:S(2)}) collective-permute-start(bf16[256,1024]{1,0:T(8,128)(2,1)} %rows_ref.1), channel_id=1, source_target_pairs={{0,4},{1,5},{2,6},{3,7},{4,8},{5,9},{6,10},{7,11},{8,12},{9,13},{1... | collective-permute-start | bytes 1572872 | tf_op jit(solution)/shard_map/ppermute | solution.py:218
  3.0 0.0 copy-done.1
  3.0 0.0 copy-start
  3.0 1.1 %copy-done = bf16[256,1024]{1,0:T(8,128)(2,1)S(1)} copy-done((bf16[256,1024]{1,0:T(8,128)(2,1)S(1)}, bf16[256,1024]{1,0:T(8,128)(2,1)}, u32[]{:S(2)}) %copy-start) | copy-done | bytes 524312
  4.1 0.2 shard_map.28
  4.3 1.5 %collective-permute-start.5 = (bf16[272,1024]{1,0:T(8,128)(2,1)S(1)}, bf16[272,1024]{1,0:T(8,128)(2,1)S(1)}, u32[]{:S(2)}, u32[]{:S(2)}) collective-permute-start(bf16[272,1024]{1,0:T(8,128)(2,1)S(1)} %get-tuple-element.25.refs_0_), channel_id=1, source_target_pairs={{0,2},{1,3},{2,0},{3,1},{4,6},{5,7},{6,4},{7,5},{8,10},{9,11},{10,... | collective-permute-start | bytes 1671176 | tf_op jit(solution)/shard_map/ppermute | solution.py:214
  5.9 0.0 collective-permute-start.4
  5.9 2.6 %collective-permute-start.2 = (f32[1,512]{1,0:T(1,128)S(1)}, f32[1,512]{1,0:T(1,128)S(1)}, u32[]{:S(2)}, u32[]{:S(2)}) collective-permute-start(f32[1,512]{1,0:T(1,128)S(1)} %get-tuple-element.21), channel_id=1, source_target_pairs={{0,8},{1,9},{2,10},{3,11},{4,12},{5,13},{6,14},{7,15},{8,0},{9,1},... | collective-permute-start | bytes 6152 | tf_op jit(solution)/shard_map/ppermute | solution.py:218
  8.4 0.6 %collective-permute-start.1 = (f32[1,512]{1,0:T(1,128)S(1)}, f32[1,512]{1,0:T(1,128)S(1)}, u32[]{:S(2)}, u32[]{:S(2)}) collective-permute-start(f32[1,512]{1,0:T(1,128)S(1)} %get-tuple-element.21), channel_id=1, source_target_pairs={{0,4},{1,5},{2,6},{3,7},{4,8},{5,9},{6,10},{7,11},{8,12},{9,13},{1... | collective-permute-start | bytes 6152 | tf_op jit(solution)/shard_map/ppermute | solution.py:218
  9.1 5.5 %collective-permute-done.2.info_ref = f32[1,512]{1,0:T(1,128)S(1)} collective-permute-done((f32[1,512]{1,0:T(1,128)S(1)}, f32[1,512]{1,0:T(1,128)S(1)}, u32[]{:S(2)}, u32[]{:S(2)}) %collective-permute-start.2) | collective-permute-done | bytes 2080 | tf_op jit(solution)/shard_map/ppermute | solution.py:218
  14.6 2.7 %collective-permute-done.1.info_ref = f32[1,512]{1,0:T(1,128)S(1)} collective-permute-done((f32[1,512]{1,0:T(1,128)S(1)}, f32[1,512]{1,0:T(1,128)S(1)}, u32[]{:S(2)}, u32[]{:S(2)}) %collective-permute-start.1) | collective-permute-done | bytes 2080 | tf_op jit(solution)/shard_map/ppermute | solution.py:218
  17.3 0.0 collective-permute-done.line_ref
  17.3 0.7 %collective-permute-start.3 = (bf16[256,1024]{1,0:T(8,128)(2,1)S(1)}, bf16[256,1024]{1,0:T(8,128)(2,1)S(1)}, u32[]{:S(2)}, u32[]{:S(2)}) collective-permute-start(bf16[256,1024]{1,0:T(8,128)(2,1)S(1)} %collective-permute-done.line_ref), channel_id=1, source_target_pairs={{4,8},{5,9},{6,10},{7,11},{8,12},{9,13},{10,14},{11,15},{12,4},{13... | collective-permute-start | bytes 1572872 | tf_op jit(solution)/shard_map/ppermute | solution.py:218
  18.0 0.4 %collective-permute-done.5.refs_2_ = bf16[272,1024]{1,0:T(8,128)(2,1)S(1)} collective-permute-done((bf16[272,1024]{1,0:T(8,128)(2,1)S(1)}, bf16[272,1024]{1,0:T(8,128)(2,1)S(1)}, u32[]{:S(2)}, u32[]{:S(2)}) %collective-permute-start.5) | collective-permute-done | bytes 557088 | tf_op jit(solution)/shard_map/ppermute | solution.py:214
  18.5 0.1 collective-permute-start.7
  18.6 0.6 %collective-permute-start.6 = (bf16[128,1024]{1,0:T(8,128)(2,1)S(1)}, bf16[128,1024]{1,0:T(8,128)(2,1)S(1)}, u32[]{:S(2)}, u32[]{:S(2)}) collective-permute-start(bf16[128,1024]{1,0:T(8,128)(2,1)S(1)} %slice.8), channel_id=1, source_target_pairs={{0,1},{1,0},{2,3},{3,2},{4,5},{5,4},{6,7},{7,6},{8,9},{9,8},{10,11... | collective-permute-start | bytes 786440 | tf_op jit(solution)/shard_map/ppermute | solution.py:214
  19.1 0.0 collective-permute-done.4.refs_1_
  19.1 1.4 %collective-permute-done.6.refs_3_ = bf16[128,1024]{1,0:T(8,128)(2,1)S(1)} collective-permute-done((bf16[128,1024]{1,0:T(8,128)(2,1)S(1)}, bf16[128,1024]{1,0:T(8,128)(2,1)S(1)}, u32[]{:S(2)}, u32[]{:S(2)}) %collective-permute-start.6) | collective-permute-done | bytes 262176 | tf_op jit(solution)/shard_map/ppermute | solution.py:214
  20.5 0.0 collective-permute-done.7.refs_4_
  20.5 2.0 %shard_map.29 = (f32[1024,128]{1,0:T(8,128)S(1)}, f32[1,256]{1,0:T(1,128)S(1)}, f32[1024,128]{1,0:T(8,128)S(1)}, f32[1,256]{1,0:T(1,128)S(1)}) custom-call(f32[1,512]{1,0:T(1,128)S(1)} %collective-permute-done.1.info_ref, bf16[256,1024]{1,0:T(8,128)(2,1)S(1)} %collective-permute-done.line_ref, bf16[272,1024]{1,0:T(8,128)(2,1)S(1)} %get-tuple-element.25.refs_0_, ...), custom_call_target="tpu_custom_call" | custom-call | flops 1 | bytes 1 | tf_op jit(solution)/shard_map/pallas_call | solution.py:246
  22.5 3.7 %collective-permute-start.8 = (f32[1,256]{1,0:T(1,128)S(1)}, f32[1,256]{1,0:T(1,128)S(1)}, u32[]{:S(2)}, u32[]{:S(2)}) collective-permute-start(f32[1,256]{1,0:T(1,128)S(1)} %get-tuple-element.30), channel_id=1, source_target_pairs={{4,0},{5,1},{6,2},{7,3},{8,4},{9,5},{10,6},{11,7},{12,8},{13,9},{1... | collective-permute-start | bytes 3080 | tf_op jit(solution)/shard_map/ppermute | solution.py:218
  26.3 0.0 collective-permute-done.3.line_ref
  26.3 0.2 shard_map.30
  26.5 7.6 %collective-permute-start.9 = (f32[1,256]{1,0:T(1,128)S(1)}, f32[1,256]{1,0:T(1,128)S(1)}, u32[]{:S(2)}, u32[]{:S(2)}) collective-permute-start(f32[1,256]{1,0:T(1,128)S(1)} %get-tuple-element.33), channel_id=1, source_target_pairs={{0,8},{1,9},{2,10},{3,11},{4,12},{5,13},{6,14},{7,15},{8,0},{9,1},... | collective-permute-start | bytes 3080 | tf_op jit(solution)/shard_map/ppermute | solution.py:218
  34.1 1.5 %collective-permute-start.10 = (f32[1,256]{1,0:T(1,128)S(1)}, f32[1,256]{1,0:T(1,128)S(1)}, u32[]{:S(2)}, u32[]{:S(2)}) collective-permute-start(f32[1,256]{1,0:T(1,128)S(1)} %get-tuple-element.34), channel_id=1, source_target_pairs={{0,2},{1,3},{2,0},{3,1},{4,6},{5,7},{6,4},{7,5},{8,10},{9,11},{10,... | collective-permute-start | bytes 3080 | tf_op jit(solution)/shard_map/ppermute | solution.py:214
  35.6 0.0 collective-permute-start.11
  35.6 0.0 collective-permute-done.8
  35.6 0.7 %collective-permute-start.12 = (f32[1,256]{1,0:T(1,128)S(1)}, f32[1,256]{1,0:T(1,128)S(1)}, u32[]{:S(2)}, u32[]{:S(2)}) collective-permute-start(f32[1,256]{1,0:T(1,128)S(1)} %get-tuple-element.36), channel_id=1, source_target_pairs={{0,1},{1,0},{2,3},{3,2},{4,5},{5,4},{6,7},{7,6},{8,9},{9,8},{10,11... | collective-permute-start | bytes 3080 | tf_op jit(solution)/shard_map/ppermute | solution.py:214
  36.3 0.0 collective-permute-done.9
  36.3 1.4 %collective-permute-done.10 = f32[1,256]{1,0:T(1,128)S(1)} collective-permute-done((f32[1,256]{1,0:T(1,128)S(1)}, f32[1,256]{1,0:T(1,128)S(1)}, u32[]{:S(2)}, u32[]{:S(2)}) %collective-permute-start.10) | collective-permute-done | bytes 1056 | tf_op jit(solution)/shard_map/ppermute | solution.py:214
  37.7 0.9 %collective-permute-done.11 = f32[1,256]{1,0:T(1,128)S(1)} collective-permute-done((f32[1,256]{1,0:T(1,128)S(1)}, f32[1,256]{1,0:T(1,128)S(1)}, u32[]{:S(2)}, u32[]{:S(2)}) %collective-permute-start.11) | collective-permute-done | bytes 1056 | tf_op jit(solution)/shard_map/ppermute | solution.py:214
  38.6 0.0 collective-permute-done.12
  38.6 0.6 %add_log-plus-one_fusion = f32[1,256]{1,0:T(1,128)} fusion(f32[1,256]{1,0:T(1,128)S(1)} %collective-permute-done.12, f32[1,256]{1,0:T(1,128)S(1)} %collective-permute-done.11, f32[1,256]{1,0:T(1,128)S(1)} %collective-permute-done.10, f32[1,256]{1,0:T(1,128)S(1)} %collective-permute-done.9, f32[1,256]{1,0:T(1,128)S(1)} %get-tuple-element.29, ...), kind=kLoop, calls=%fused_computation | loop fusion | flops 1280 | bytes 7168 | tf_op jit(solution)/shard_map/log1p | solution.py:262
  (2 shorter events, 0.0 us)
Async XLA Ops:
  0.0 3.0 %copy-start.1 = (s32[256]{0:T(256)S(1)}, s32[256]{0:T(256)}, u32[]{:S(2)}) copy-start(s32[256]{0:T(256)} %param.3) | copy-start | bytes 3076
  0.0 17.3 %collective-permute-start = (bf16[256,1024]{1,0:T(8,128)(2,1)}, bf16[256,1024]{1,0:T(8,128)(2,1)S(1)}, u32[]{:S(2)}, u32[]{:S(2)}) collective-permute-start(bf16[256,1024]{1,0:T(8,128)(2,1)} %rows_ref.1), channel_id=1, source_target_pairs={{0,4},{1,5},{2,6},{3,7},{4,8},{5,9},{6,10},{7,11},{8,12},{9,13},{1... | collective-permute-start | bytes 1572872 | tf_op jit(solution)/shard_map/ppermute | solution.py:218
  3.0 1.1 %copy-start = (bf16[256,1024]{1,0:T(8,128)(2,1)S(1)}, bf16[256,1024]{1,0:T(8,128)(2,1)}, u32[]{:S(2)}) copy-start(bf16[256,1024]{1,0:T(8,128)(2,1)} %rows_ref.1) | copy-start | bytes 1572868
  4.3 14.1 %collective-permute-start.5 = (bf16[272,1024]{1,0:T(8,128)(2,1)S(1)}, bf16[272,1024]{1,0:T(8,128)(2,1)S(1)}, u32[]{:S(2)}, u32[]{:S(2)}) collective-permute-start(bf16[272,1024]{1,0:T(8,128)(2,1)S(1)} %get-tuple-element.25.refs_0_), channel_id=1, source_target_pairs={{0,2},{1,3},{2,0},{3,1},{4,6},{5,7},{6,4},{7,5},{8,10},{9,11},{10,... | collective-permute-start | bytes 1671176 | tf_op jit(solution)/shard_map/ppermute | solution.py:214
  5.9 13.3 %collective-permute-start.4 = (bf16[272,1024]{1,0:T(8,128)(2,1)S(1)}, bf16[272,1024]{1,0:T(8,128)(2,1)S(1)}, u32[]{:S(2)}, u32[]{:S(2)}) collective-permute-start(bf16[272,1024]{1,0:T(8,128)(2,1)S(1)} %get-tuple-element.25.refs_0_), channel_id=1, source_target_pairs={{0,1},{1,0},{2,3},{3,2},{4,5},{5,4},{6,7},{7,6},{8,9},{9,8},{10,11... | collective-permute-start | bytes 1671176 | tf_op jit(solution)/shard_map/ppermute | solution.py:214
  5.9 8.7 %collective-permute-start.2 = (f32[1,512]{1,0:T(1,128)S(1)}, f32[1,512]{1,0:T(1,128)S(1)}, u32[]{:S(2)}, u32[]{:S(2)}) collective-permute-start(f32[1,512]{1,0:T(1,128)S(1)} %get-tuple-element.21), channel_id=1, source_target_pairs={{0,8},{1,9},{2,10},{3,11},{4,12},{5,13},{6,14},{7,15},{8,0},{9,1},... | collective-permute-start | bytes 6152 | tf_op jit(solution)/shard_map/ppermute | solution.py:218
  8.4 8.9 %collective-permute-start.1 = (f32[1,512]{1,0:T(1,128)S(1)}, f32[1,512]{1,0:T(1,128)S(1)}, u32[]{:S(2)}, u32[]{:S(2)}) collective-permute-start(f32[1,512]{1,0:T(1,128)S(1)} %get-tuple-element.21), channel_id=1, source_target_pairs={{0,4},{1,5},{2,6},{3,7},{4,8},{5,9},{6,10},{7,11},{8,12},{9,13},{1... | collective-permute-start | bytes 6152 | tf_op jit(solution)/shard_map/ppermute | solution.py:218
  17.3 9.0 %collective-permute-start.3 = (bf16[256,1024]{1,0:T(8,128)(2,1)S(1)}, bf16[256,1024]{1,0:T(8,128)(2,1)S(1)}, u32[]{:S(2)}, u32[]{:S(2)}) collective-permute-start(bf16[256,1024]{1,0:T(8,128)(2,1)S(1)} %collective-permute-done.line_ref), channel_id=1, source_target_pairs={{4,8},{5,9},{6,10},{7,11},{8,12},{9,13},{10,14},{11,15},{12,4},{13... | collective-permute-start | bytes 1572872 | tf_op jit(solution)/shard_map/ppermute | solution.py:218
  18.5 2.0 %collective-permute-start.7 = (bf16[144,1024]{1,0:T(8,128)(2,1)S(1)}, bf16[144,1024]{1,0:T(8,128)(2,1)S(1)}, u32[]{:S(2)}, u32[]{:S(2)}) collective-permute-start(bf16[144,1024]{1,0:T(8,128)(2,1)S(1)} %slice.9), channel_id=1, source_target_pairs={{0,1},{1,0},{2,3},{3,2},{4,5},{5,4},{6,7},{7,6},{8,9},{9,8},{10,11... | collective-permute-start | bytes 884744 | tf_op jit(solution)/shard_map/ppermute | solution.py:214
  18.6 1.9 %collective-permute-start.6 = (bf16[128,1024]{1,0:T(8,128)(2,1)S(1)}, bf16[128,1024]{1,0:T(8,128)(2,1)S(1)}, u32[]{:S(2)}, u32[]{:S(2)}) collective-permute-start(bf16[128,1024]{1,0:T(8,128)(2,1)S(1)} %slice.8), channel_id=1, source_target_pairs={{0,1},{1,0},{2,3},{3,2},{4,5},{5,4},{6,7},{7,6},{8,9},{9,8},{10,11... | collective-permute-start | bytes 786440 | tf_op jit(solution)/shard_map/ppermute | solution.py:214
  22.5 13.0 %collective-permute-start.8 = (f32[1,256]{1,0:T(1,128)S(1)}, f32[1,256]{1,0:T(1,128)S(1)}, u32[]{:S(2)}, u32[]{:S(2)}) collective-permute-start(f32[1,256]{1,0:T(1,128)S(1)} %get-tuple-element.30), channel_id=1, source_target_pairs={{4,0},{5,1},{6,2},{7,3},{8,4},{9,5},{10,6},{11,7},{12,8},{13,9},{1... | collective-permute-start | bytes 3080 | tf_op jit(solution)/shard_map/ppermute | solution.py:218
  26.5 9.7 %collective-permute-start.9 = (f32[1,256]{1,0:T(1,128)S(1)}, f32[1,256]{1,0:T(1,128)S(1)}, u32[]{:S(2)}, u32[]{:S(2)}) collective-permute-start(f32[1,256]{1,0:T(1,128)S(1)} %get-tuple-element.33), channel_id=1, source_target_pairs={{0,8},{1,9},{2,10},{3,11},{4,12},{5,13},{6,14},{7,15},{8,0},{9,1},... | collective-permute-start | bytes 3080 | tf_op jit(solution)/shard_map/ppermute | solution.py:218
  34.1 3.6 %collective-permute-start.10 = (f32[1,256]{1,0:T(1,128)S(1)}, f32[1,256]{1,0:T(1,128)S(1)}, u32[]{:S(2)}, u32[]{:S(2)}) collective-permute-start(f32[1,256]{1,0:T(1,128)S(1)} %get-tuple-element.34), channel_id=1, source_target_pairs={{0,2},{1,3},{2,0},{3,1},{4,6},{5,7},{6,4},{7,5},{8,10},{9,11},{10,... | collective-permute-start | bytes 3080 | tf_op jit(solution)/shard_map/ppermute | solution.py:214
  35.6 3.0 %collective-permute-start.11 = (f32[1,256]{1,0:T(1,128)S(1)}, f32[1,256]{1,0:T(1,128)S(1)}, u32[]{:S(2)}, u32[]{:S(2)}) collective-permute-start(f32[1,256]{1,0:T(1,128)S(1)} %get-tuple-element.35), channel_id=1, source_target_pairs={{0,3},{1,2},{2,1},{3,0},{4,7},{5,6},{6,5},{7,4},{8,11},{9,10},{10,... | collective-permute-start | bytes 3080 | tf_op jit(solution)/shard_map/ppermute | solution.py:214
  35.6 3.0 %collective-permute-start.12 = (f32[1,256]{1,0:T(1,128)S(1)}, f32[1,256]{1,0:T(1,128)S(1)}, u32[]{:S(2)}, u32[]{:S(2)}) collective-permute-start(f32[1,256]{1,0:T(1,128)S(1)} %get-tuple-element.36), channel_id=1, source_target_pairs={{0,1},{1,0},{2,3},{3,2},{4,5},{5,4},{6,7},{7,6},{8,9},{9,8},{10,11... | collective-permute-start | bytes 3080 | tf_op jit(solution)/shard_map/ppermute | solution.py:214

commit v15 on v8

--- a/solution.py
+++ b/solution.py
@@ -80,6 +80,7 @@
 
 LANES = 128
 PLANE = 4
+INVERSE_TEMP_BITS = 20.0 * 1.4426950408889634
 ID_ROWS = 16
 VMEM_BYTES = 16 * 1024 * 1024
 
@@ -108,25 +109,28 @@
         query_pos = lax.broadcasted_iota(jnp.int32, similar.shape, 0) + shift
         key_pos = lax.broadcasted_iota(jnp.int32, similar.shape, 1)
         mates = mates & (query_pos != key_pos)
-    return jnp.where(mates, jnp.exp(similar * inverse_temp), 0.0)
-
-
-def unit_kernel(rows_ref, ids_ref, *block_refs):
+    return jnp.where(mates, jnp.exp2(similar * INVERSE_TEMP_BITS), 0.0)
+
+
+def unit_rows(raw):
+    features = raw.astype(jnp.float32)
+    squares = jnp.sum(features * features, axis=1, keepdims=True)
+    return (features * lax.rsqrt(squares + 1e-06)).astype(jnp.bfloat16)
+
+
+def unit_kernel(ranges, rows_ref, ids_ref, *block_refs):
     rows, width = rows_ref.shape
-    features = rows_ref[...].astype(jnp.float32)
-    scale = lax.rsqrt(jnp.sum(features * features, axis=1, keepdims=True) + 1e-06)
-    units = (features * scale).astype(jnp.bfloat16)
+    units = unit_rows(rows_ref[...])
     ids = ids_block(ids_ref[...].astype(jnp.float32), width)
-    first = 0
-    for ref in block_refs:
-        size = min(ref.shape[0], rows - first)
-        ref[:size, :] = units[first : first + size]
+    for (first, last), ref in zip(ranges, block_refs):
+        size = last - first
+        ref[:size, :] = units[first:last]
         if ref.shape[0] > size:
             ref[size:, :] = ids
-        first = (first + size) % rows
-
-
-def line_sums(moves, query_parts, ids_ref, line_ref, column_ref, sums_ref):
+
+
+def line_sums(moves, query_parts, ids_ref, line_refs, column_ref, sums_ref):
+    raw_ref, tail_ref = line_refs
     rows = column_ref.shape[1]
     plane = lax.axis_index("gx") // PLANE
     arrived = functools.reduce(jnp.logical_or, [plane == receiver for _, receiver in moves])
@@ -134,12 +138,14 @@
 
     @pl.when(arrived)
     def _():
-        key_ids = ids_of(line_ref)[:, :rows]
+        key_ids = ids_of(tail_ref)[:, :rows]
+        tail = tail_ref[: rows - raw_ref.shape[0], :]
+        key_rows = jnp.concatenate([unit_rows(raw_ref[...]), tail], axis=0)
         column = jnp.zeros((1, rows), jnp.float32)
         first = 0
         for query_ref, size in query_parts:
             part = pl.ds(first, size)
-            masses = mate_mass(query_ref[:size, :], ids_ref[part, :], line_ref[:rows, :], key_ids)
+            masses = mate_mass(query_ref[:size, :], ids_ref[part, :], key_rows, key_ids)
             column = column + jnp.sum(masses, axis=0, keepdims=True)
             folded = masses[:, :LANES]
             for lane in range(LANES, rows, LANES):
@@ -155,7 +161,7 @@
     return list(zip(refs, sizes))
 
 
-def first_kernel(moves, line_ref, *refs):
+def first_kernel(moves, raw_ref, tail_ref, *refs):
     query_refs, (ids_ref, column_ref, sums_ref, mass_ref) = refs[:-4], refs[-4:]
     rows = mass_ref.shape[1]
     query_parts = query_parts_of(query_refs, rows)
@@ -174,20 +180,20 @@
         first += size
     mass_ref[...] = mass
     sums_ref[...] = jnp.zeros_like(sums_ref)
-    line_sums(moves, query_parts, ids_ref, line_ref, column_ref, sums_ref)
-
-
-def last_kernel(moves, line_ref, ids_ref, earlier_ref, mass_ref, back_ref, *refs):
+    line_sums(moves, query_parts, ids_ref, (raw_ref, tail_ref), column_ref, sums_ref)
+
+
+def last_kernel(moves, raw_ref, tail_ref, ids_ref, earlier_ref, mass_ref, *refs):
     query_refs, refs = refs[: -PLANE - 2], refs[-PLANE - 2 :]
     column_ref, row_refs, sums_ref = refs[0], refs[1:-1], refs[-1]
     rows = column_ref.shape[1]
     sums_ref[...] = earlier_ref[...]
     query_parts = query_parts_of(query_refs, rows)
-    line_sums(moves, query_parts, ids_ref, line_ref, column_ref, sums_ref)
+    line_sums(moves, query_parts, ids_ref, (raw_ref, tail_ref), column_ref, sums_ref)
     for m in range(PLANE):
         row_sum = jnp.sum(sums_ref[pl.ds(m * rows, rows), :].T, axis=0, keepdims=True)
         if m == 0:
-            row_sum = row_sum + mass_ref[...] + back_ref[...]
+            row_sum = row_sum + mass_ref[...]
         row_refs[m][...] = row_sum
 
 
@@ -211,26 +217,25 @@
         return lax.ppermute(value, "gx", pairs)
 
     first_moves = [(0, 1), (1, 2), (2, 3), (3, 0)]
-    last_moves = [(1, 3), (2, 0)]
+    last_moves = [(0, 2), (1, 3)]
+    forward_moves = [(1, 2), (2, 3)]
     first_back = [(b, a) for a, b in first_moves]
     last_back = [(b, a) for a, b in last_moves]
 
-    head = 3 * row_count // 8
-    block, *pieces = pl.pallas_call(
-        unit_kernel,
-        out_shape=(
-            rows_of(row_count + ID_ROWS),
-            rows_of(head),
-            rows_of(row_count - head + ID_ROWS),
-        ),
+    half, part = row_count // 2, 5 * row_count // 8
+    ranges = [(0, row_count), (0, half), (half, row_count), (part, row_count)]
+    id_rows = [ID_ROWS, 0, ID_ROWS, ID_ROWS]
+    first_raw = on_line(embeddings[:part], first_moves)
+    block, *pieces, tail = pl.pallas_call(
+        functools.partial(unit_kernel, ranges),
+        out_shape=[rows_of(b - a + extra) for (a, b), extra in zip(ranges, id_rows)],
         cost_estimate=small,
         compiler_params=params,
     )(embeddings, cluster_ids.reshape(1, row_count))
-    first_line = on_line(block, first_moves)
-    last_line = on_line(block, last_moves)
+    first_tail = on_line(tail, first_moves)
     across = [in_plane(piece, 2) for piece in pieces]
     sibling = in_plane(block, 1)
-    first_line, across[1] = lax.optimization_barrier((first_line, across[1]))
+    last_line = [on_line(got, forward_moves) for got in (first_raw, first_tail)]
     corner = [in_plane(piece, 1) for piece in across]
     queries = (block, sibling, *across, *corner)
     ids, first_column, first_sums, mass = pl.pallas_call(
@@ -238,17 +243,18 @@
         out_shape=(lanes, vector, lanes, vector),
         cost_estimate=small,
         compiler_params=params,
-    )(first_line, *queries)
+    )(first_raw, first_tail, *queries)
     returned_first = on_line(first_column, first_back)
     last_column, *row_sums = pl.pallas_call(
         functools.partial(last_kernel, last_moves),
         out_shape=[vector] * (1 + PLANE),
         scratch_shapes=[pltpu.VMEM(lanes.shape, lanes.dtype)],
         compiler_params=params,
-    )(last_line, ids, first_sums, mass, returned_first, *queries)
+    )(*last_line, ids, first_sums, mass, *queries)
+    returned_first, row_sums[1] = lax.optimization_barrier((returned_first, row_sums[1]))
     returned = [on_line(last_column, last_back)]
     returned += [in_plane(row_sums[step], step) for step in (2, 3, 1)]
-    return jnp.log1p(sum(returned, row_sums[0])).reshape(row_count)
+    return jnp.log1p(sum(returned, row_sums[0] + returned_first)).reshape(row_count)
 
 
 def on_device(embeddings, cluster_ids):

time: 47.3 us -> 36.7 us (0.78)
  starting transfers between devices: 24.3 us -> 14.4 us
  waiting for transfers between devices: 16.5 us -> 17.6 us
  Pallas kernels: 3.92 us -> 2.84 us
  local copies, waits for them, and re-layouts: 1.72 us -> 1.08 us
    ppermute x4 -> x6, starting transfers between devices: 19.5 us -> 10.3 us  [on_line(): return lax.ppermute(value, 'gx', pairs)]
    ppermute x4 -> x6, waiting for transfers between devices: 4.71 us -> 13.9 us  [on_line(): return lax.ppermute(value, 'gx', pairs)]
    ppermute x8, waiting for transfers between devices: 11.8 us -> 3.61 us  [in_plane(): return lax.ppermute(value, 'gx', [(i, i ^ step) for i in range(peers)])]
    unnamed x4, local copies, waits for them, and re-layouts: 1.72 us -> 0.01 us
    pallas_call x1, Pallas kernels: 1.41 us -> 0.24 us  [grid_plan(): pl.pallas_call(functools.partial(last_kernel, last_moves), out_shape=[vec...]
    slice x0 -> x1, local copies, waits for them, and re-layouts: none -> 1.07 us  [grid_plan(): first_raw = on_line(embeddings[:part], first_moves)]
    ppermute x8, starting transfers between devices: 4.81 us -> 4.09 us  [in_plane(): return lax.ppermute(value, 'gx', [(i, i ^ step) for i in range(peers)])]
  transfers between devices with their start and end apart: 12 -> 14, of which waited for: 6 -> 6; matrix products, arithmetic and copies ran while one was open for 0% -> 0% of each run, Pallas kernels for 5% -> 8%
where the time goes in v15:
time: 36.7 us; the launch traced here: 36.5 us
  waiting for transfers between devices  17.6 us (48%)
  starting transfers between devices  14.4 us (39%)
  Pallas kernels  2.84 us (8%)
  local copies, waits for them, and re-layouts  1.08 us (3%)
  other arithmetic  0.58 us (2%)
    ppermute x6, waiting for transfers between devices, on_line(): return lax.ppermute(value, 'gx', pairs)  13.9 us
    ppermute x6, starting transfers between devices, on_line(): return lax.ppermute(value, 'gx', pairs)  10.3 us
    ppermute x8, starting transfers between devices, in_plane(): return lax.ppermute(value, 'gx', [(i, i ^ step) for i in range(peers)])  4.09 us
    ppermute x8, waiting for transfers between devices, in_plane(): return lax.ppermute(value, 'gx', [(i, i ^ step) for i in range(peers)])  3.61 us
    pallas_call x1, Pallas kernels, grid_plan(): pl.pallas_call(functools.partial(first_kernel, first_moves), out_shape=(l...  2.4 us
    slice x1, local copies, waits for them, and re-layouts, grid_plan(): first_raw = on_line(embeddings[:part], first_moves)  1.07 us
  transfers between devices with their start and end apart: 14, of which 6 were waited for; matrix products, arithmetic and copies ran while one was open for 0% of the time, Pallas kernels for 8%

profile of v15, /device:TPU:0, one launch (start us, length us, event | category | flops | bytes accessed | tf_op | source)
XLA Modules:
  0.0 36.5 jit_solution(17091752686139823629)
XLA Ops:
  0.0 0.0 copy-start
  0.0 1.1 %slice.3 = bf16[160,1024]{1,0:T(8,128)(2,1)S(1)} slice(bf16[256,1024]{1,0:T(8,128)(2,1)} %rows_ref.1), slice={[0:160], [0:1024]} | slice | bytes 655360 | tf_op jit(solution)/shard_map/slice | solution.py:228
  1.1 0.0 copy-start.1
  1.1 3.1 %collective-permute-start = (bf16[160,1024]{1,0:T(8,128)(2,1)S(1)}, bf16[160,1024]{1,0:T(8,128)(2,1)S(1)}, u32[]{:S(2)}, u32[]{:S(2)}) collective-permute-start(bf16[160,1024]{1,0:T(8,128)(2,1)S(1)} %slice.3), channel_id=1, source_target_pairs={{0,4},{1,5},{2,6},{3,7},{4,8},{5,9},{6,10},{7,11},{8,12},{9,13},{1... | collective-permute-start | bytes 983048 | tf_op jit(solution)/shard_map/ppermute | solution.py:217
  4.2 0.0 copy-done
  4.2 0.0 copy-done.1
  4.2 0.2 shard_map.28
  4.4 1.6 %collective-permute-start.6 = (bf16[144,1024]{1,0:T(8,128)(2,1)S(1)}, bf16[144,1024]{1,0:T(8,128)(2,1)S(1)}, u32[]{:S(2)}, u32[]{:S(2)}) collective-permute-start(bf16[144,1024]{1,0:T(8,128)(2,1)S(1)} %get-tuple-element.23), channel_id=1, source_target_pairs={{0,2},{1,3},{2,0},{3,1},{4,6},{5,7},{6,4},{7,5},{8,10},{9,11},{10,... | collective-permute-start | bytes 884744 | tf_op jit(solution)/shard_map/ppermute | solution.py:213
  5.9 0.0 collective-permute-start.4
  5.9 0.5 %collective-permute-start.5 = (bf16[128,1024]{1,0:T(8,128)(2,1)S(1)}, bf16[128,1024]{1,0:T(8,128)(2,1)S(1)}, u32[]{:S(2)}, u32[]{:S(2)}) collective-permute-start(bf16[128,1024]{1,0:T(8,128)(2,1)S(1)} %get-tuple-element.22), channel_id=1, source_target_pairs={{0,2},{1,3},{2,0},{3,1},{4,6},{5,7},{6,4},{7,5},{8,10},{9,11},{10,... | collective-permute-start | bytes 786440 | tf_op jit(solution)/shard_map/ppermute | solution.py:213
  6.5 1.6 %collective-permute-start.2 = (bf16[112,1024]{1,0:T(8,128)(2,1)S(1)}, bf16[112,1024]{1,0:T(8,128)(2,1)S(1)}, u32[]{:S(2)}, u32[]{:S(2)}) collective-permute-start(bf16[112,1024]{1,0:T(8,128)(2,1)S(1)} %get-tuple-element.20), channel_id=1, source_target_pairs={{0,4},{1,5},{2,6},{3,7},{4,8},{5,9},{6,10},{7,11},{8,12},{9,13},{1... | collective-permute-start | bytes 688136 | tf_op jit(solution)/shard_map/ppermute | solution.py:217
  8.0 6.7 %collective-permute-done.raw_ref = bf16[160,1024]{1,0:T(8,128)(2,1)S(1)} collective-permute-done((bf16[160,1024]{1,0:T(8,128)(2,1)S(1)}, bf16[160,1024]{1,0:T(8,128)(2,1)S(1)}, u32[]{:S(2)}, u32[]{:S(2)}) %collective-permute-start) | collective-permute-done | bytes 327712 | tf_op jit(solution)/shard_map/ppermute | solution.py:217
  14.7 0.7 %collective-permute-start.1 = (bf16[160,1024]{1,0:T(8,128)(2,1)S(1)}, bf16[160,1024]{1,0:T(8,128)(2,1)S(1)}, u32[]{:S(2)}, u32[]{:S(2)}) collective-permute-start(bf16[160,1024]{1,0:T(8,128)(2,1)S(1)} %collective-permute-done.raw_ref), channel_id=1, source_target_pairs={{4,8},{5,9},{6,10},{7,11},{8,12},{9,13},{10,14},{11,15},{20,24},{2... | collective-permute-start | bytes 983048 | tf_op jit(solution)/shard_map/ppermute | solution.py:217
  15.4 0.0 collective-permute-done.6.refs_3_
  15.4 0.1 collective-permute-start.8
  15.5 3.0 %collective-permute-done.5.refs_2_ = bf16[128,1024]{1,0:T(8,128)(2,1)S(1)} collective-permute-done((bf16[128,1024]{1,0:T(8,128)(2,1)S(1)}, bf16[128,1024]{1,0:T(8,128)(2,1)S(1)}, u32[]{:S(2)}, u32[]{:S(2)}) %collective-permute-start.5) | collective-permute-done | bytes 262176 | tf_op jit(solution)/shard_map/ppermute | solution.py:213
  18.5 0.0 collective-permute-start.7
  18.5 0.3 collective-permute-done.2.tail_ref
  18.8 0.7 %collective-permute-start.3 = (bf16[112,1024]{1,0:T(8,128)(2,1)S(1)}, bf16[112,1024]{1,0:T(8,128)(2,1)S(1)}, u32[]{:S(2)}, u32[]{:S(2)}) collective-permute-start(bf16[112,1024]{1,0:T(8,128)(2,1)S(1)} %collective-permute-done.2.tail_ref), channel_id=1, source_target_pairs={{4,8},{5,9},{6,10},{7,11},{8,12},{9,13},{10,14},{11,15},{20,24},{2... | collective-permute-start | bytes 688136 | tf_op jit(solution)/shard_map/ppermute | solution.py:217
  19.5 0.6 %collective-permute-done.7.refs_4_ = bf16[128,1024]{1,0:T(8,128)(2,1)S(1)} collective-permute-done((bf16[128,1024]{1,0:T(8,128)(2,1)S(1)}, bf16[128,1024]{1,0:T(8,128)(2,1)S(1)}, u32[]{:S(2)}, u32[]{:S(2)}) %collective-permute-start.7) | collective-permute-done | bytes 262176 | tf_op jit(solution)/shard_map/ppermute | solution.py:213
  20.1 0.0 collective-permute-done.4.refs_1_
  20.1 0.0 collective-permute-done.8.refs_5_
  20.1 2.4 %shard_map.29 = (f32[1024,128]{1,0:T(8,128)S(1)}, f32[1,256]{1,0:T(1,128)S(1)}, f32[1024,128]{1,0:T(8,128)S(1)}, f32[1,256]{1,0:T(1,128)S(1)}) custom-call(bf16[160,1024]{1,0:T(8,128)(2,1)S(1)} %collective-permute-done.raw_ref, bf16[112,1024]{1,0:T(8,128)(2,1)S(1)} %collective-permute-done.2.tail_ref, bf16[272,1024]{1,0:T(8,128)(2,1)S(1)} %get-tuple-element.21.refs_0_, ...), custom_call_target="tpu_custom_call" | custom-call | flops 1 | bytes 1 | tf_op jit(solution)/shard_map/pallas_call | solution.py:241
  22.5 3.0 %collective-permute-start.9 = (f32[1,256]{1,0:T(1,128)S(1)}, f32[1,256]{1,0:T(1,128)S(1)}, u32[]{:S(2)}, u32[]{:S(2)}) collective-permute-start(f32[1,256]{1,0:T(1,128)S(1)} %get-tuple-element.28), channel_id=1, source_target_pairs={{4,0},{5,1},{6,2},{7,3},{8,4},{9,5},{10,6},{11,7},{12,8},{13,9},{1... | collective-permute-start | bytes 3080 | tf_op jit(solution)/shard_map/ppermute | solution.py:217
  25.5 0.0 collective-permute-done.3.tail_ref
  25.5 0.0 collective-permute-done.1.raw_ref
  25.5 0.2 shard_map.30
  25.7 1.9 %collective-permute-done.9 = f32[1,256]{1,0:T(1,128)S(1)} collective-permute-done((f32[1,256]{1,0:T(1,128)S(1)}, f32[1,256]{1,0:T(1,128)S(1)}, u32[]{:S(2)}, u32[]{:S(2)}) %collective-permute-start.9) | collective-permute-done | bytes 1056 | tf_op jit(solution)/shard_map/ppermute | solution.py:217
  27.6 0.0 collective-permute-start.13
  27.6 1.3 %collective-permute-start.10 = (f32[1,256]{1,0:T(1,128)S(1)}, f32[1,256]{1,0:T(1,128)S(1)}, u32[]{:S(2)}, u32[]{:S(2)}) collective-permute-start(f32[1,256]{1,0:T(1,128)S(1)} %get-tuple-element.31), channel_id=1, source_target_pairs={{8,0},{9,1},{10,2},{11,3},{12,4},{13,5},{14,6},{15,7},{24,16},{25,... | collective-permute-start | bytes 3080 | tf_op jit(solution)/shard_map/ppermute | solution.py:217
  28.9 1.6 %collective-permute-start.11 = (f32[1,256]{1,0:T(1,128)S(1)}, f32[1,256]{1,0:T(1,128)S(1)}, u32[]{:S(2)}, u32[]{:S(2)}) collective-permute-start(f32[1,256]{1,0:T(1,128)S(1)} %get-tuple-element.32), channel_id=1, source_target_pairs={{0,2},{1,3},{2,0},{3,1},{4,6},{5,7},{6,4},{7,5},{8,10},{9,11},{10,... | collective-permute-start | bytes 3080 | tf_op jit(solution)/shard_map/ppermute | solution.py:213
  30.5 0.4 %collective-permute-start.12 = (f32[1,256]{1,0:T(1,128)S(1)}, f32[1,256]{1,0:T(1,128)S(1)}, u32[]{:S(2)}, u32[]{:S(2)}) collective-permute-start(f32[1,256]{1,0:T(1,128)S(1)} %get-tuple-element.33), channel_id=1, source_target_pairs={{0,3},{1,2},{2,1},{3,0},{4,7},{5,6},{6,5},{7,4},{8,11},{9,10},{10,... | collective-permute-start | bytes 3080 | tf_op jit(solution)/shard_map/ppermute | solution.py:213
  30.8 0.0 collective-permute-done.13
  30.8 5.1 %collective-permute-done.10 = f32[1,256]{1,0:T(1,128)S(1)} collective-permute-done((f32[1,256]{1,0:T(1,128)S(1)}, f32[1,256]{1,0:T(1,128)S(1)}, u32[]{:S(2)}, u32[]{:S(2)}) %collective-permute-start.10) | collective-permute-done | bytes 1056 | tf_op jit(solution)/shard_map/ppermute | solution.py:217
  35.9 0.0 collective-permute-done.11
  35.9 0.0 collective-permute-done.12
  35.9 0.6 %add_log-plus-one_fusion = f32[1,256]{1,0:T(1,128)} fusion(f32[1,256]{1,0:T(1,128)S(1)} %collective-permute-done.13, f32[1,256]{1,0:T(1,128)S(1)} %collective-permute-done.12, f32[1,256]{1,0:T(1,128)S(1)} %collective-permute-done.11, f32[1,256]{1,0:T(1,128)S(1)} %collective-permute-done.10, f32[1,256]{1,0:T(1,128)S(1)} %get-tuple-element.27, ...), kind=kLoop, calls=%fused_computation | loop fusion | flops 1280 | bytes 7168 | tf_op jit(solution)/shard_map/log1p | solution.py:257
Async XLA Ops:
  0.0 4.2 %copy-start = (bf16[256,1024]{1,0:T(8,128)(2,1)S(1)}, bf16[256,1024]{1,0:T(8,128)(2,1)}, u32[]{:S(2)}) copy-start(bf16[256,1024]{1,0:T(8,128)(2,1)} %rows_ref.1) | copy-start | bytes 1572868
  1.1 3.1 %copy-start.1 = (s32[256]{0:T(256)S(1)}, s32[256]{0:T(256)}, u32[]{:S(2)}) copy-start(s32[256]{0:T(256)} %param.3) | copy-start | bytes 3076
  1.1 13.6 %collective-permute-start = (bf16[160,1024]{1,0:T(8,128)(2,1)S(1)}, bf16[160,1024]{1,0:T(8,128)(2,1)S(1)}, u32[]{:S(2)}, u32[]{:S(2)}) collective-permute-start(bf16[160,1024]{1,0:T(8,128)(2,1)S(1)} %slice.3), channel_id=1, source_target_pairs={{0,4},{1,5},{2,6},{3,7},{4,8},{5,9},{6,10},{7,11},{8,12},{9,13},{1... | collective-permute-start | bytes 983048 | tf_op jit(solution)/shard_map/ppermute | solution.py:217
  4.4 11.0 %collective-permute-start.6 = (bf16[144,1024]{1,0:T(8,128)(2,1)S(1)}, bf16[144,1024]{1,0:T(8,128)(2,1)S(1)}, u32[]{:S(2)}, u32[]{:S(2)}) collective-permute-start(bf16[144,1024]{1,0:T(8,128)(2,1)S(1)} %get-tuple-element.23), channel_id=1, source_target_pairs={{0,2},{1,3},{2,0},{3,1},{4,6},{5,7},{6,4},{7,5},{8,10},{9,11},{10,... | collective-permute-start | bytes 884744 | tf_op jit(solution)/shard_map/ppermute | solution.py:213
  5.9 14.1 %collective-permute-start.4 = (bf16[272,1024]{1,0:T(8,128)(2,1)S(1)}, bf16[272,1024]{1,0:T(8,128)(2,1)S(1)}, u32[]{:S(2)}, u32[]{:S(2)}) collective-permute-start(bf16[272,1024]{1,0:T(8,128)(2,1)S(1)} %get-tuple-element.21.refs_0_), channel_id=1, source_target_pairs={{0,1},{1,0},{2,3},{3,2},{4,5},{5,4},{6,7},{7,6},{8,9},{9,8},{10,11... | collective-permute-start | bytes 1671176 | tf_op jit(solution)/shard_map/ppermute | solution.py:213
  5.9 12.6 %collective-permute-start.5 = (bf16[128,1024]{1,0:T(8,128)(2,1)S(1)}, bf16[128,1024]{1,0:T(8,128)(2,1)S(1)}, u32[]{:S(2)}, u32[]{:S(2)}) collective-permute-start(bf16[128,1024]{1,0:T(8,128)(2,1)S(1)} %get-tuple-element.22), channel_id=1, source_target_pairs={{0,2},{1,3},{2,0},{3,1},{4,6},{5,7},{6,4},{7,5},{8,10},{9,11},{10,... | collective-permute-start | bytes 786440 | tf_op jit(solution)/shard_map/ppermute | solution.py:213
  6.5 12.3 %collective-permute-start.2 = (bf16[112,1024]{1,0:T(8,128)(2,1)S(1)}, bf16[112,1024]{1,0:T(8,128)(2,1)S(1)}, u32[]{:S(2)}, u32[]{:S(2)}) collective-permute-start(bf16[112,1024]{1,0:T(8,128)(2,1)S(1)} %get-tuple-element.20), channel_id=1, source_target_pairs={{0,4},{1,5},{2,6},{3,7},{4,8},{5,9},{6,10},{7,11},{8,12},{9,13},{1... | collective-permute-start | bytes 688136 | tf_op jit(solution)/shard_map/ppermute | solution.py:217
  14.7 10.8 %collective-permute-start.1 = (bf16[160,1024]{1,0:T(8,128)(2,1)S(1)}, bf16[160,1024]{1,0:T(8,128)(2,1)S(1)}, u32[]{:S(2)}, u32[]{:S(2)}) collective-permute-start(bf16[160,1024]{1,0:T(8,128)(2,1)S(1)} %collective-permute-done.raw_ref), channel_id=1, source_target_pairs={{4,8},{5,9},{6,10},{7,11},{8,12},{9,13},{10,14},{11,15},{20,24},{2... | collective-permute-start | bytes 983048 | tf_op jit(solution)/shard_map/ppermute | solution.py:217
  15.4 4.6 %collective-permute-start.8 = (bf16[144,1024]{1,0:T(8,128)(2,1)S(1)}, bf16[144,1024]{1,0:T(8,128)(2,1)S(1)}, u32[]{:S(2)}, u32[]{:S(2)}) collective-permute-start(bf16[144,1024]{1,0:T(8,128)(2,1)S(1)} %collective-permute-done.6.refs_3_), channel_id=1, source_target_pairs={{0,1},{1,0},{2,3},{3,2},{4,5},{5,4},{6,7},{7,6},{8,9},{9,8},{10,11... | collective-permute-start | bytes 884744 | tf_op jit(solution)/shard_map/ppermute | solution.py:213
  18.5 1.5 %collective-permute-start.7 = (bf16[128,1024]{1,0:T(8,128)(2,1)S(1)}, bf16[128,1024]{1,0:T(8,128)(2,1)S(1)}, u32[]{:S(2)}, u32[]{:S(2)}) collective-permute-start(bf16[128,1024]{1,0:T(8,128)(2,1)S(1)} %collective-permute-done.5.refs_2_), channel_id=1, source_target_pairs={{0,1},{1,0},{2,3},{3,2},{4,5},{5,4},{6,7},{7,6},{8,9},{9,8},{10,11... | collective-permute-start | bytes 786440 | tf_op jit(solution)/shard_map/ppermute | solution.py:213
  18.8 6.7 %collective-permute-start.3 = (bf16[112,1024]{1,0:T(8,128)(2,1)S(1)}, bf16[112,1024]{1,0:T(8,128)(2,1)S(1)}, u32[]{:S(2)}, u32[]{:S(2)}) collective-permute-start(bf16[112,1024]{1,0:T(8,128)(2,1)S(1)} %collective-permute-done.2.tail_ref), channel_id=1, source_target_pairs={{4,8},{5,9},{6,10},{7,11},{8,12},{9,13},{10,14},{11,15},{20,24},{2... | collective-permute-start | bytes 688136 | tf_op jit(solution)/shard_map/ppermute | solution.py:217
  22.5 5.2 %collective-permute-start.9 = (f32[1,256]{1,0:T(1,128)S(1)}, f32[1,256]{1,0:T(1,128)S(1)}, u32[]{:S(2)}, u32[]{:S(2)}) collective-permute-start(f32[1,256]{1,0:T(1,128)S(1)} %get-tuple-element.28), channel_id=1, source_target_pairs={{4,0},{5,1},{6,2},{7,3},{8,4},{9,5},{10,6},{11,7},{12,8},{13,9},{1... | collective-permute-start | bytes 3080 | tf_op jit(solution)/shard_map/ppermute | solution.py:217
  27.6 3.2 %collective-permute-start.13 = (f32[1,256]{1,0:T(1,128)S(1)}, f32[1,256]{1,0:T(1,128)S(1)}, u32[]{:S(2)}, u32[]{:S(2)}) collective-permute-start(f32[1,256]{1,0:T(1,128)S(1)} %get-tuple-element.34), channel_id=1, source_target_pairs={{0,1},{1,0},{2,3},{3,2},{4,5},{5,4},{6,7},{7,6},{8,9},{9,8},{10,11... | collective-permute-start | bytes 3080 | tf_op jit(solution)/shard_map/ppermute | solution.py:213
  27.6 8.3 %collective-permute-start.10 = (f32[1,256]{1,0:T(1,128)S(1)}, f32[1,256]{1,0:T(1,128)S(1)}, u32[]{:S(2)}, u32[]{:S(2)}) collective-permute-start(f32[1,256]{1,0:T(1,128)S(1)} %get-tuple-element.31), channel_id=1, source_target_pairs={{8,0},{9,1},{10,2},{11,3},{12,4},{13,5},{14,6},{15,7},{24,16},{25,... | collective-permute-start | bytes 3080 | tf_op jit(solution)/shard_map/ppermute | solution.py:217
  28.9 7.0 %collective-permute-start.11 = (f32[1,256]{1,0:T(1,128)S(1)}, f32[1,256]{1,0:T(1,128)S(1)}, u32[]{:S(2)}, u32[]{:S(2)}) collective-permute-start(f32[1,256]{1,0:T(1,128)S(1)} %get-tuple-element.32), channel_id=1, source_target_pairs={{0,2},{1,3},{2,0},{3,1},{4,6},{5,7},{6,4},{7,5},{8,10},{9,11},{10,... | collective-permute-start | bytes 3080 | tf_op jit(solution)/shard_map/ppermute | solution.py:213
  30.5 5.4 %collective-permute-start.12 = (f32[1,256]{1,0:T(1,128)S(1)}, f32[1,256]{1,0:T(1,128)S(1)}, u32[]{:S(2)}, u32[]{:S(2)}) collective-permute-start(f32[1,256]{1,0:T(1,128)S(1)} %get-tuple-element.33), channel_id=1, source_target_pairs={{0,3},{1,2},{2,1},{3,0},{4,7},{5,6},{6,5},{7,4},{8,11},{9,10},{10,... | collective-permute-start | bytes 3080 | tf_op jit(solution)/shard_map/ppermute | solution.py:213

commit v16 on v15

--- a/solution.py
+++ b/solution.py
@@ -218,7 +218,7 @@
 
     first_moves = [(0, 1), (1, 2), (2, 3), (3, 0)]
     last_moves = [(0, 2), (1, 3)]
-    forward_moves = [(1, 2), (2, 3)]
+    forward_moves = [(1, 2), (2, 3), (3, 1), (0, 0)]
     first_back = [(b, a) for a, b in first_moves]
     last_back = [(b, a) for a, b in last_moves]
 

time: 36.7 us -> 36.7 us (level)
  waiting for transfers between devices: 17.6 us -> 16.4 us
  starting transfers between devices: 14.4 us -> 15.5 us
    ppermute x6, starting transfers between devices: 10.3 us -> 11.4 us  [on_line(): return lax.ppermute(value, 'gx', pairs)]
    ppermute x8, waiting for transfers between devices: 3.61 us -> 3.04 us  [in_plane(): return lax.ppermute(value, 'gx', [(i, i ^ step) for i in range(peers)])]
    ppermute x6, waiting for transfers between devices: 13.9 us -> 13.4 us  [on_line(): return lax.ppermute(value, 'gx', pairs)]
  transfers between devices with their start and end apart: 14 -> 14, of which waited for: 6 -> 5; matrix products, arithmetic and copies ran while one was open for 0% -> 0% of each run, Pallas kernels for 8% -> 8%
where the time goes in v16:
time: 36.7 us; the launch traced here: 36.5 us
  waiting for transfers between devices  16.4 us (45%)
  starting transfers between devices  15.5 us (42%)
  Pallas kernels  2.85 us (8%)
  local copies, waits for them, and re-layouts  1.08 us (3%)
  other arithmetic  0.58 us (2%)
    ppermute x6, waiting for transfers between devices, on_line(): return lax.ppermute(value, 'gx', pairs)  13.4 us
    ppermute x6, starting transfers between devices, on_line(): return lax.ppermute(value, 'gx', pairs)  11.4 us
    ppermute x8, starting transfers between devices, in_plane(): return lax.ppermute(value, 'gx', [(i, i ^ step) for i in range(peers)])  4.09 us
    ppermute x8, waiting for transfers between devices, in_plane(): return lax.ppermute(value, 'gx', [(i, i ^ step) for i in range(peers)])  3.04 us
    pallas_call x1, Pallas kernels, grid_plan(): pl.pallas_call(functools.partial(first_kernel, first_moves), out_shape=(l...  2.41 us
    slice x1, local copies, waits for them, and re-layouts, grid_plan(): first_raw = on_line(embeddings[:part], first_moves)  1.07 us
  transfers between devices with their start and end apart: 14, of which 5 were waited for; matrix products, arithmetic and copies ran while one was open for 0% of the time, Pallas kernels for 8%

profile of v16, /device:TPU:0, one launch (start us, length us, event | category | flops | bytes accessed | tf_op | source)
XLA Modules:
  0.0 36.5 jit_solution(4512748929712071502)
XLA Ops:
  0.0 0.0 copy-start
  0.0 1.1 %slice.3 = bf16[160,1024]{1,0:T(8,128)(2,1)S(1)} slice(bf16[256,1024]{1,0:T(8,128)(2,1)} %rows_ref.1), slice={[0:160], [0:1024]} | slice | bytes 655360 | tf_op jit(solution)/shard_map/slice | solution.py:228
  1.1 0.0 copy-start.1
  1.1 3.1 %collective-permute-start = (bf16[160,1024]{1,0:T(8,128)(2,1)S(1)}, bf16[160,1024]{1,0:T(8,128)(2,1)S(1)}, u32[]{:S(2)}, u32[]{:S(2)}) collective-permute-start(bf16[160,1024]{1,0:T(8,128)(2,1)S(1)} %slice.3), channel_id=1, source_target_pairs={{0,4},{1,5},{2,6},{3,7},{4,8},{5,9},{6,10},{7,11},{8,12},{9,13},{1... | collective-permute-start | bytes 983048 | tf_op jit(solution)/shard_map/ppermute | solution.py:217
  4.2 0.0 copy-done
  4.2 0.0 copy-done.1
  4.2 0.2 shard_map.28
  4.4 1.6 %collective-permute-start.6 = (bf16[144,1024]{1,0:T(8,128)(2,1)S(1)}, bf16[144,1024]{1,0:T(8,128)(2,1)S(1)}, u32[]{:S(2)}, u32[]{:S(2)}) collective-permute-start(bf16[144,1024]{1,0:T(8,128)(2,1)S(1)} %get-tuple-element.23), channel_id=1, source_target_pairs={{0,2},{1,3},{2,0},{3,1},{4,6},{5,7},{6,4},{7,5},{8,10},{9,11},{10,... | collective-permute-start | bytes 884744 | tf_op jit(solution)/shard_map/ppermute | solution.py:213
  5.9 0.0 collective-permute-start.4
  5.9 0.5 %collective-permute-start.5 = (bf16[128,1024]{1,0:T(8,128)(2,1)S(1)}, bf16[128,1024]{1,0:T(8,128)(2,1)S(1)}, u32[]{:S(2)}, u32[]{:S(2)}) collective-permute-start(bf16[128,1024]{1,0:T(8,128)(2,1)S(1)} %get-tuple-element.22), channel_id=1, source_target_pairs={{0,2},{1,3},{2,0},{3,1},{4,6},{5,7},{6,4},{7,5},{8,10},{9,11},{10,... | collective-permute-start | bytes 786440 | tf_op jit(solution)/shard_map/ppermute | solution.py:213
  6.5 1.6 %collective-permute-start.2 = (bf16[112,1024]{1,0:T(8,128)(2,1)S(1)}, bf16[112,1024]{1,0:T(8,128)(2,1)S(1)}, u32[]{:S(2)}, u32[]{:S(2)}) collective-permute-start(bf16[112,1024]{1,0:T(8,128)(2,1)S(1)} %get-tuple-element.20), channel_id=1, source_target_pairs={{0,4},{1,5},{2,6},{3,7},{4,8},{5,9},{6,10},{7,11},{8,12},{9,13},{1... | collective-permute-start | bytes 688136 | tf_op jit(solution)/shard_map/ppermute | solution.py:217
  8.0 6.7 %collective-permute-done.raw_ref = bf16[160,1024]{1,0:T(8,128)(2,1)S(1)} collective-permute-done((bf16[160,1024]{1,0:T(8,128)(2,1)S(1)}, bf16[160,1024]{1,0:T(8,128)(2,1)S(1)}, u32[]{:S(2)}, u32[]{:S(2)}) %collective-permute-start) | collective-permute-done | bytes 327712 | tf_op jit(solution)/shard_map/ppermute | solution.py:217
  14.7 0.7 %collective-permute-start.1 = (bf16[160,1024]{1,0:T(8,128)(2,1)S(1)}, bf16[160,1024]{1,0:T(8,128)(2,1)S(1)}, u32[]{:S(2)}, u32[]{:S(2)}) collective-permute-start(bf16[160,1024]{1,0:T(8,128)(2,1)S(1)} %collective-permute-done.raw_ref), channel_id=1, source_target_pairs={{4,8},{5,9},{6,10},{7,11},{8,12},{9,13},{10,14},{11,15},{12,4},{13... | collective-permute-start | bytes 983048 | tf_op jit(solution)/shard_map/ppermute | solution.py:217
  15.4 0.0 collective-permute-done.6.refs_3_
  15.4 0.1 collective-permute-start.8
  15.5 3.0 %collective-permute-done.5.refs_2_ = bf16[128,1024]{1,0:T(8,128)(2,1)S(1)} collective-permute-done((bf16[128,1024]{1,0:T(8,128)(2,1)S(1)}, bf16[128,1024]{1,0:T(8,128)(2,1)S(1)}, u32[]{:S(2)}, u32[]{:S(2)}) %collective-permute-start.5) | collective-permute-done | bytes 262176 | tf_op jit(solution)/shard_map/ppermute | solution.py:213
  18.5 0.0 collective-permute-start.7
  18.5 1.1 %collective-permute-done.2.tail_ref = bf16[112,1024]{1,0:T(8,128)(2,1)S(1)} collective-permute-done((bf16[112,1024]{1,0:T(8,128)(2,1)S(1)}, bf16[112,1024]{1,0:T(8,128)(2,1)S(1)}, u32[]{:S(2)}, u32[]{:S(2)}) %collective-permute-start.2) | collective-permute-done | bytes 229408 | tf_op jit(solution)/shard_map/ppermute | solution.py:217
  19.6 0.7 %collective-permute-start.3 = (bf16[112,1024]{1,0:T(8,128)(2,1)S(1)}, bf16[112,1024]{1,0:T(8,128)(2,1)S(1)}, u32[]{:S(2)}, u32[]{:S(2)}) collective-permute-start(bf16[112,1024]{1,0:T(8,128)(2,1)S(1)} %collective-permute-done.2.tail_ref), channel_id=1, source_target_pairs={{4,8},{5,9},{6,10},{7,11},{8,12},{9,13},{10,14},{11,15},{12,4},{13... | collective-permute-start | bytes 688136 | tf_op jit(solution)/shard_map/ppermute | solution.py:217
  20.3 0.0 collective-permute-done.7.refs_4_
  20.3 0.0 collective-permute-done.4.refs_1_
  20.3 0.0 collective-permute-done.8.refs_5_
  20.3 2.4 %shard_map.29 = (f32[1024,128]{1,0:T(8,128)S(1)}, f32[1,256]{1,0:T(1,128)S(1)}, f32[1024,128]{1,0:T(8,128)S(1)}, f32[1,256]{1,0:T(1,128)S(1)}) custom-call(bf16[160,1024]{1,0:T(8,128)(2,1)S(1)} %collective-permute-done.raw_ref, bf16[112,1024]{1,0:T(8,128)(2,1)S(1)} %collective-permute-done.2.tail_ref, bf16[272,1024]{1,0:T(8,128)(2,1)S(1)} %get-tuple-element.21.refs_0_, ...), custom_call_target="tpu_custom_call" | custom-call | flops 1 | bytes 1 | tf_op jit(solution)/shard_map/pallas_call | solution.py:241
  22.8 4.1 %collective-permute-start.9 = (f32[1,256]{1,0:T(1,128)S(1)}, f32[1,256]{1,0:T(1,128)S(1)}, u32[]{:S(2)}, u32[]{:S(2)}) collective-permute-start(f32[1,256]{1,0:T(1,128)S(1)} %get-tuple-element.28), channel_id=1, source_target_pairs={{4,0},{5,1},{6,2},{7,3},{8,4},{9,5},{10,6},{11,7},{12,8},{13,9},{1... | collective-permute-start | bytes 3080 | tf_op jit(solution)/shard_map/ppermute | solution.py:217
  26.9 0.0 collective-permute-done.3.tail_ref
  26.9 0.0 collective-permute-done.1.raw_ref
  26.9 0.2 shard_map.30
  27.1 1.0 %collective-permute-done.9 = f32[1,256]{1,0:T(1,128)S(1)} collective-permute-done((f32[1,256]{1,0:T(1,128)S(1)}, f32[1,256]{1,0:T(1,128)S(1)}, u32[]{:S(2)}, u32[]{:S(2)}) %collective-permute-start.9) | collective-permute-done | bytes 1056 | tf_op jit(solution)/shard_map/ppermute | solution.py:217
  28.2 0.0 collective-permute-start.13
  28.2 1.3 %collective-permute-start.10 = (f32[1,256]{1,0:T(1,128)S(1)}, f32[1,256]{1,0:T(1,128)S(1)}, u32[]{:S(2)}, u32[]{:S(2)}) collective-permute-start(f32[1,256]{1,0:T(1,128)S(1)} %get-tuple-element.31), channel_id=1, source_target_pairs={{8,0},{9,1},{10,2},{11,3},{12,4},{13,5},{14,6},{15,7},{24,16},{25,... | collective-permute-start | bytes 3080 | tf_op jit(solution)/shard_map/ppermute | solution.py:217
  29.4 1.6 %collective-permute-start.11 = (f32[1,256]{1,0:T(1,128)S(1)}, f32[1,256]{1,0:T(1,128)S(1)}, u32[]{:S(2)}, u32[]{:S(2)}) collective-permute-start(f32[1,256]{1,0:T(1,128)S(1)} %get-tuple-element.32), channel_id=1, source_target_pairs={{0,2},{1,3},{2,0},{3,1},{4,6},{5,7},{6,4},{7,5},{8,10},{9,11},{10,... | collective-permute-start | bytes 3080 | tf_op jit(solution)/shard_map/ppermute | solution.py:213
  31.0 0.4 %collective-permute-start.12 = (f32[1,256]{1,0:T(1,128)S(1)}, f32[1,256]{1,0:T(1,128)S(1)}, u32[]{:S(2)}, u32[]{:S(2)}) collective-permute-start(f32[1,256]{1,0:T(1,128)S(1)} %get-tuple-element.33), channel_id=1, source_target_pairs={{0,3},{1,2},{2,1},{3,0},{4,7},{5,6},{6,5},{7,4},{8,11},{9,10},{10,... | collective-permute-start | bytes 3080 | tf_op jit(solution)/shard_map/ppermute | solution.py:213
  31.4 0.0 collective-permute-done.13
  31.4 4.5 %collective-permute-done.10 = f32[1,256]{1,0:T(1,128)S(1)} collective-permute-done((f32[1,256]{1,0:T(1,128)S(1)}, f32[1,256]{1,0:T(1,128)S(1)}, u32[]{:S(2)}, u32[]{:S(2)}) %collective-permute-start.10) | collective-permute-done | bytes 1056 | tf_op jit(solution)/shard_map/ppermute | solution.py:217
  35.9 0.0 collective-permute-done.11
  35.9 0.0 collective-permute-done.12
  35.9 0.6 %add_log-plus-one_fusion = f32[1,256]{1,0:T(1,128)} fusion(f32[1,256]{1,0:T(1,128)S(1)} %collective-permute-done.13, f32[1,256]{1,0:T(1,128)S(1)} %collective-permute-done.12, f32[1,256]{1,0:T(1,128)S(1)} %collective-permute-done.11, f32[1,256]{1,0:T(1,128)S(1)} %collective-permute-done.10, f32[1,256]{1,0:T(1,128)S(1)} %get-tuple-element.27, ...), kind=kLoop, calls=%fused_computation | loop fusion | flops 1280 | bytes 7168 | tf_op jit(solution)/shard_map/log1p | solution.py:257
Async XLA Ops:
  0.0 4.2 %copy-start = (bf16[256,1024]{1,0:T(8,128)(2,1)S(1)}, bf16[256,1024]{1,0:T(8,128)(2,1)}, u32[]{:S(2)}) copy-start(bf16[256,1024]{1,0:T(8,128)(2,1)} %rows_ref.1) | copy-start | bytes 1572868
  1.1 3.1 %copy-start.1 = (s32[256]{0:T(256)S(1)}, s32[256]{0:T(256)}, u32[]{:S(2)}) copy-start(s32[256]{0:T(256)} %param.3) | copy-start | bytes 3076
  1.1 13.6 %collective-permute-start = (bf16[160,1024]{1,0:T(8,128)(2,1)S(1)}, bf16[160,1024]{1,0:T(8,128)(2,1)S(1)}, u32[]{:S(2)}, u32[]{:S(2)}) collective-permute-start(bf16[160,1024]{1,0:T(8,128)(2,1)S(1)} %slice.3), channel_id=1, source_target_pairs={{0,4},{1,5},{2,6},{3,7},{4,8},{5,9},{6,10},{7,11},{8,12},{9,13},{1... | collective-permute-start | bytes 983048 | tf_op jit(solution)/shard_map/ppermute | solution.py:217
  4.4 11.0 %collective-permute-start.6 = (bf16[144,1024]{1,0:T(8,128)(2,1)S(1)}, bf16[144,1024]{1,0:T(8,128)(2,1)S(1)}, u32[]{:S(2)}, u32[]{:S(2)}) collective-permute-start(bf16[144,1024]{1,0:T(8,128)(2,1)S(1)} %get-tuple-element.23), channel_id=1, source_target_pairs={{0,2},{1,3},{2,0},{3,1},{4,6},{5,7},{6,4},{7,5},{8,10},{9,11},{10,... | collective-permute-start | bytes 884744 | tf_op jit(solution)/shard_map/ppermute | solution.py:213
  5.9 14.4 %collective-permute-start.4 = (bf16[272,1024]{1,0:T(8,128)(2,1)S(1)}, bf16[272,1024]{1,0:T(8,128)(2,1)S(1)}, u32[]{:S(2)}, u32[]{:S(2)}) collective-permute-start(bf16[272,1024]{1,0:T(8,128)(2,1)S(1)} %get-tuple-element.21.refs_0_), channel_id=1, source_target_pairs={{0,1},{1,0},{2,3},{3,2},{4,5},{5,4},{6,7},{7,6},{8,9},{9,8},{10,11... | collective-permute-start | bytes 1671176 | tf_op jit(solution)/shard_map/ppermute | solution.py:213
  5.9 12.6 %collective-permute-start.5 = (bf16[128,1024]{1,0:T(8,128)(2,1)S(1)}, bf16[128,1024]{1,0:T(8,128)(2,1)S(1)}, u32[]{:S(2)}, u32[]{:S(2)}) collective-permute-start(bf16[128,1024]{1,0:T(8,128)(2,1)S(1)} %get-tuple-element.22), channel_id=1, source_target_pairs={{0,2},{1,3},{2,0},{3,1},{4,6},{5,7},{6,4},{7,5},{8,10},{9,11},{10,... | collective-permute-start | bytes 786440 | tf_op jit(solution)/shard_map/ppermute | solution.py:213
  6.5 13.2 %collective-permute-start.2 = (bf16[112,1024]{1,0:T(8,128)(2,1)S(1)}, bf16[112,1024]{1,0:T(8,128)(2,1)S(1)}, u32[]{:S(2)}, u32[]{:S(2)}) collective-permute-start(bf16[112,1024]{1,0:T(8,128)(2,1)S(1)} %get-tuple-element.20), channel_id=1, source_target_pairs={{0,4},{1,5},{2,6},{3,7},{4,8},{5,9},{6,10},{7,11},{8,12},{9,13},{1... | collective-permute-start | bytes 688136 | tf_op jit(solution)/shard_map/ppermute | solution.py:217
  14.7 12.1 %collective-permute-start.1 = (bf16[160,1024]{1,0:T(8,128)(2,1)S(1)}, bf16[160,1024]{1,0:T(8,128)(2,1)S(1)}, u32[]{:S(2)}, u32[]{:S(2)}) collective-permute-start(bf16[160,1024]{1,0:T(8,128)(2,1)S(1)} %collective-permute-done.raw_ref), channel_id=1, source_target_pairs={{4,8},{5,9},{6,10},{7,11},{8,12},{9,13},{10,14},{11,15},{12,4},{13... | collective-permute-start | bytes 983048 | tf_op jit(solution)/shard_map/ppermute | solution.py:217
  15.4 4.9 %collective-permute-start.8 = (bf16[144,1024]{1,0:T(8,128)(2,1)S(1)}, bf16[144,1024]{1,0:T(8,128)(2,1)S(1)}, u32[]{:S(2)}, u32[]{:S(2)}) collective-permute-start(bf16[144,1024]{1,0:T(8,128)(2,1)S(1)} %collective-permute-done.6.refs_3_), channel_id=1, source_target_pairs={{0,1},{1,0},{2,3},{3,2},{4,5},{5,4},{6,7},{7,6},{8,9},{9,8},{10,11... | collective-permute-start | bytes 884744 | tf_op jit(solution)/shard_map/ppermute | solution.py:213
  18.5 1.8 %collective-permute-start.7 = (bf16[128,1024]{1,0:T(8,128)(2,1)S(1)}, bf16[128,1024]{1,0:T(8,128)(2,1)S(1)}, u32[]{:S(2)}, u32[]{:S(2)}) collective-permute-start(bf16[128,1024]{1,0:T(8,128)(2,1)S(1)} %collective-permute-done.5.refs_2_), channel_id=1, source_target_pairs={{0,1},{1,0},{2,3},{3,2},{4,5},{5,4},{6,7},{7,6},{8,9},{9,8},{10,11... | collective-permute-start | bytes 786440 | tf_op jit(solution)/shard_map/ppermute | solution.py:213
  19.6 7.2 %collective-permute-start.3 = (bf16[112,1024]{1,0:T(8,128)(2,1)S(1)}, bf16[112,1024]{1,0:T(8,128)(2,1)S(1)}, u32[]{:S(2)}, u32[]{:S(2)}) collective-permute-start(bf16[112,1024]{1,0:T(8,128)(2,1)S(1)} %collective-permute-done.2.tail_ref), channel_id=1, source_target_pairs={{4,8},{5,9},{6,10},{7,11},{8,12},{9,13},{10,14},{11,15},{12,4},{13... | collective-permute-start | bytes 688136 | tf_op jit(solution)/shard_map/ppermute | solution.py:217
  22.8 5.4 %collective-permute-start.9 = (f32[1,256]{1,0:T(1,128)S(1)}, f32[1,256]{1,0:T(1,128)S(1)}, u32[]{:S(2)}, u32[]{:S(2)}) collective-permute-start(f32[1,256]{1,0:T(1,128)S(1)} %get-tuple-element.28), channel_id=1, source_target_pairs={{4,0},{5,1},{6,2},{7,3},{8,4},{9,5},{10,6},{11,7},{12,8},{13,9},{1... | collective-permute-start | bytes 3080 | tf_op jit(solution)/shard_map/ppermute | solution.py:217
  28.2 3.2 %collective-permute-start.13 = (f32[1,256]{1,0:T(1,128)S(1)}, f32[1,256]{1,0:T(1,128)S(1)}, u32[]{:S(2)}, u32[]{:S(2)}) collective-permute-start(f32[1,256]{1,0:T(1,128)S(1)} %get-tuple-element.34), channel_id=1, source_target_pairs={{0,1},{1,0},{2,3},{3,2},{4,5},{5,4},{6,7},{7,6},{8,9},{9,8},{10,11... | collective-permute-start | bytes 3080 | tf_op jit(solution)/shard_map/ppermute | solution.py:213
  28.2 7.8 %collective-permute-start.10 = (f32[1,256]{1,0:T(1,128)S(1)}, f32[1,256]{1,0:T(1,128)S(1)}, u32[]{:S(2)}, u32[]{:S(2)}) collective-permute-start(f32[1,256]{1,0:T(1,128)S(1)} %get-tuple-element.31), channel_id=1, source_target_pairs={{8,0},{9,1},{10,2},{11,3},{12,4},{13,5},{14,6},{15,7},{24,16},{25,... | collective-permute-start | bytes 3080 | tf_op jit(solution)/shard_map/ppermute | solution.py:217
  29.4 6.5 %collective-permute-start.11 = (f32[1,256]{1,0:T(1,128)S(1)}, f32[1,256]{1,0:T(1,128)S(1)}, u32[]{:S(2)}, u32[]{:S(2)}) collective-permute-start(f32[1,256]{1,0:T(1,128)S(1)} %get-tuple-element.32), channel_id=1, source_target_pairs={{0,2},{1,3},{2,0},{3,1},{4,6},{5,7},{6,4},{7,5},{8,10},{9,11},{10,... | collective-permute-start | bytes 3080 | tf_op jit(solution)/shard_map/ppermute | solution.py:213
  31.0 4.9 %collective-permute-start.12 = (f32[1,256]{1,0:T(1,128)S(1)}, f32[1,256]{1,0:T(1,128)S(1)}, u32[]{:S(2)}, u32[]{:S(2)}) collective-permute-start(f32[1,256]{1,0:T(1,128)S(1)} %get-tuple-element.33), channel_id=1, source_target_pairs={{0,3},{1,2},{2,1},{3,0},{4,7},{5,6},{6,5},{7,4},{8,11},{9,10},{10,... | collective-permute-start | bytes 3080 | tf_op jit(solution)/shard_map/ppermute | solution.py:213

commit v17 on v15

--- a/solution.py
+++ b/solution.py
@@ -129,30 +129,41 @@
             ref[size:, :] = ids
 
 
-def line_sums(moves, query_parts, ids_ref, line_refs, column_ref, sums_ref):
-    raw_ref, tail_ref = line_refs
-    rows = column_ref.shape[1]
+def padded(values, count, fill):
+    rows, columns = values.shape
+    if rows == 1:
+        return jnp.concatenate([values, jnp.full((1, count - columns), fill, values.dtype)], axis=1)
+    return jnp.concatenate([values, jnp.full((count - rows, columns), fill, values.dtype)], axis=0)
+
+
+def arrived_at(moves):
     plane = lax.axis_index("gx") // PLANE
-    arrived = functools.reduce(jnp.logical_or, [plane == receiver for _, receiver in moves])
-    column_ref[...] = jnp.zeros_like(column_ref)
-
-    @pl.when(arrived)
-    def _():
-        key_ids = ids_of(tail_ref)[:, :rows]
-        tail = tail_ref[: rows - raw_ref.shape[0], :]
-        key_rows = jnp.concatenate([unit_rows(raw_ref[...]), tail], axis=0)
-        column = jnp.zeros((1, rows), jnp.float32)
-        first = 0
-        for query_ref, size in query_parts:
-            part = pl.ds(first, size)
-            masses = mate_mass(query_ref[:size, :], ids_ref[part, :], key_rows, key_ids)
-            column = column + jnp.sum(masses, axis=0, keepdims=True)
-            folded = masses[:, :LANES]
-            for lane in range(LANES, rows, LANES):
-                folded = folded + masses[:, lane : lane + LANES]
-            sums_ref[part, :] += folded
-            first += size
-        column_ref[...] = column
+    return functools.reduce(jnp.logical_or, [plane == receiver for _, receiver in moves])
+
+
+def add_line(query_parts, ids_ref, key_rows, key_ids, earlier_ref, sums_ref):
+    keys = key_rows.shape[0]
+    column = jnp.zeros((1, keys), jnp.float32)
+    first = 0
+    for query_ref, size in query_parts:
+        part = pl.ds(first, size)
+        masses = mate_mass(query_ref[:size, :], ids_ref[part, :], key_rows, key_ids)
+        column = column + jnp.sum(masses, axis=0, keepdims=True)
+        folded = masses[:, :LANES]
+        for lane in range(LANES, keys, LANES):
+            folded = folded + masses[:, lane : lane + LANES]
+        sums_ref[part, :] = folded if earlier_ref is None else earlier_ref[part, :] + folded
+        first += size
+    return column
+
+
+def add_masses(query_ids, key_ids, powers):
+    mates = jnp.concatenate([query_ids] * (powers.shape[1] // LANES), axis=1) == key_ids
+    masses = jnp.where(mates, powers, 0.0)
+    folded = masses[:, :LANES]
+    for lane in range(LANES, powers.shape[1], LANES):
+        folded = folded + masses[:, lane : lane + LANES]
+    return folded, jnp.sum(masses, axis=0, keepdims=True)
 
 
 def query_parts_of(refs, rows):
@@ -161,7 +172,7 @@
     return list(zip(refs, sizes))
 
 
-def first_kernel(moves, raw_ref, tail_ref, *refs):
+def first_kernel(moves, head_ref, tail_ref, *refs):
     query_refs, (ids_ref, column_ref, sums_ref, mass_ref) = refs[:-4], refs[-4:]
     rows = mass_ref.shape[1]
     query_parts = query_parts_of(query_refs, rows)
@@ -179,22 +190,72 @@
         mass = mass + jnp.sum(masses, axis=0, keepdims=True)
         first += size
     mass_ref[...] = mass
-    sums_ref[...] = jnp.zeros_like(sums_ref)
-    line_sums(moves, query_parts, ids_ref, (raw_ref, tail_ref), column_ref, sums_ref)
-
-
-def last_kernel(moves, raw_ref, tail_ref, ids_ref, earlier_ref, mass_ref, *refs):
+    tail = tail_ref[: rows - head_ref.shape[0], :]
+    key_rows = jnp.concatenate([unit_rows(head_ref[...]), tail], axis=0)
+    key_ids = ids_of(tail_ref)[:, :rows]
+    column_ref[...] = add_line(query_parts, ids_ref, key_rows, key_ids, None, sums_ref)
+
+
+def middle_kernel(moves, head_ref, *refs):
+    query_refs, powers_ref = refs[:-1], refs[-1]
+
+    @pl.when(arrived_at(moves))
+    def _():
+        keys = powers_ref.shape[1]
+        key_rows = padded(unit_rows(head_ref[...]), keys, 0.0)
+        first = 0
+        for query_ref, size in query_parts_of(query_refs, keys):
+            similar = lax.dot_general(
+                query_ref[:size, :], key_rows, (((1,), (1,)), ((), ())),
+                preferred_element_type=jnp.float32,
+            )
+            powers_ref[pl.ds(first, size), :] = jnp.exp2(similar * INVERSE_TEMP_BITS)
+            first += size
+
+
+def last_kernel(moves, powers_ref, tail_ref, ids_ref, earlier_ref, mass_ref, *refs):
     query_refs, refs = refs[: -PLANE - 2], refs[-PLANE - 2 :]
     column_ref, row_refs, sums_ref = refs[0], refs[1:-1], refs[-1]
     rows = column_ref.shape[1]
-    sums_ref[...] = earlier_ref[...]
-    query_parts = query_parts_of(query_refs, rows)
-    line_sums(moves, query_parts, ids_ref, (raw_ref, tail_ref), column_ref, sums_ref)
+    arrived = arrived_at(moves)
+
+    @pl.when(arrived)
+    def _():
+        tail = tail_ref.shape[0] - ID_ROWS
+        keys = LANES * ((tail + LANES - 1) // LANES)
+        key_ids = ids_of(tail_ref)[:, :rows]
+        head_ids = padded(key_ids[:, : rows - tail], rows, -1.0)
+        tail_ids = padded(key_ids[:, rows - tail :], keys, -1.0)
+        key_rows = padded(tail_ref[:tail, :], keys, 0.0)
+        head_column = jnp.zeros((1, rows), jnp.float32)
+        tail_column = jnp.zeros((1, keys), jnp.float32)
+        first = 0
+        for query_ref, size in query_parts_of(query_refs, rows):
+            part = pl.ds(first, size)
+            query_ids = ids_ref[part, :]
+            similar = lax.dot_general(
+                query_ref[:size, :], key_rows, (((1,), (1,)), ((), ())),
+                preferred_element_type=jnp.float32,
+            )
+            powers = jnp.exp2(similar * INVERSE_TEMP_BITS)
+            tail_part, column = add_masses(query_ids, tail_ids, powers)
+            tail_column = tail_column + column
+            head_part, column = add_masses(query_ids, head_ids, powers_ref[part, :])
+            head_column = head_column + column
+            sums_ref[part, :] = earlier_ref[part, :] + head_part + tail_part
+            first += size
+        column_ref[...] = jnp.concatenate(
+            [head_column[:, : rows - tail], tail_column[:, :tail]], axis=1
+        )
+
+    @pl.when(jnp.logical_not(arrived))
+    def _():
+        column_ref[...] = jnp.zeros_like(column_ref)
+        sums_ref[...] = earlier_ref[...]
+
     for m in range(PLANE):
         row_sum = jnp.sum(sums_ref[pl.ds(m * rows, rows), :].T, axis=0, keepdims=True)
-        if m == 0:
-            row_sum = row_sum + mass_ref[...]
-        row_refs[m][...] = row_sum
+        row_refs[m][...] = row_sum + mass_ref[...] if m == 0 else row_sum
 
 
 def grid_plan(embeddings, cluster_ids):
@@ -225,7 +286,7 @@
     half, part = row_count // 2, 5 * row_count // 8
     ranges = [(0, row_count), (0, half), (half, row_count), (part, row_count)]
     id_rows = [ID_ROWS, 0, ID_ROWS, ID_ROWS]
-    first_raw = on_line(embeddings[:part], first_moves)
+    first_head = on_line(embeddings[:part], first_moves)
     block, *pieces, tail = pl.pallas_call(
         functools.partial(unit_kernel, ranges),
         out_shape=[rows_of(b - a + extra) for (a, b), extra in zip(ranges, id_rows)],
@@ -235,7 +296,7 @@
     first_tail = on_line(tail, first_moves)
     across = [in_plane(piece, 2) for piece in pieces]
     sibling = in_plane(block, 1)
-    last_line = [on_line(got, forward_moves) for got in (first_raw, first_tail)]
+    last_head, last_tail = [on_line(got, forward_moves) for got in (first_head, first_tail)]
     corner = [in_plane(piece, 1) for piece in across]
     queries = (block, sibling, *across, *corner)
     ids, first_column, first_sums, mass = pl.pallas_call(
@@ -243,14 +304,20 @@
         out_shape=(lanes, vector, lanes, vector),
         cost_estimate=small,
         compiler_params=params,
-    )(first_raw, first_tail, *queries)
+    )(first_head, first_tail, *queries)
     returned_first = on_line(first_column, first_back)
+    powers = pl.pallas_call(
+        functools.partial(middle_kernel, last_moves),
+        out_shape=jax.ShapeDtypeStruct((plane_rows, row_count), jnp.float32),
+        cost_estimate=small,
+        compiler_params=params,
+    )(last_head, *queries)
     last_column, *row_sums = pl.pallas_call(
         functools.partial(last_kernel, last_moves),
         out_shape=[vector] * (1 + PLANE),
         scratch_shapes=[pltpu.VMEM(lanes.shape, lanes.dtype)],
         compiler_params=params,
-    )(*last_line, ids, first_sums, mass, *queries)
+    )(powers, last_tail, ids, first_sums, mass, *queries)
     returned_first, row_sums[1] = lax.optimization_barrier((returned_first, row_sums[1]))
     returned = [on_line(last_column, last_back)]
     returned += [in_plane(row_sums[step], step) for step in (2, 3, 1)]

time: 36.7 us -> 36.2 us (0.986)
  transfers between devices with their start and end apart: 14 -> 14, of which waited for: 6 -> 6; matrix products, arithmetic and copies ran while one was open for 0% -> 0% of each run, Pallas kernels for 8% -> 7%
where the time goes in v17:
time: 36.2 us; the launch traced here: 36.1 us
  waiting for transfers between devices  17.4 us (48%)
  starting transfers between devices  14.4 us (40%)
  Pallas kernels  2.59 us (7%)
  local copies, waits for them, and re-layouts  1.08 us (3%)
  other arithmetic  0.58 us (2%)
    ppermute x6, waiting for transfers between devices, on_line(): return lax.ppermute(value, 'gx', pairs)  13.8 us
    ppermute x6, starting transfers between devices, on_line(): return lax.ppermute(value, 'gx', pairs)  10.3 us
    ppermute x8, starting transfers between devices, in_plane(): return lax.ppermute(value, 'gx', [(i, i ^ step) for i in range(peers)])  4.09 us
    ppermute x8, waiting for transfers between devices, in_plane(): return lax.ppermute(value, 'gx', [(i, i ^ step) for i in range(peers)])  3.61 us
    pallas_call x1, Pallas kernels, grid_plan(): pl.pallas_call(functools.partial(first_kernel, first_moves), out_shape=(l...  2.15 us
    slice x1, local copies, waits for them, and re-layouts, grid_plan(): first_head = on_line(embeddings[:part], first_moves)  1.07 us
  transfers between devices with their start and end apart: 14, of which 6 were waited for; matrix products, arithmetic and copies ran while one was open for 0% of the time, Pallas kernels for 7%

profile of v17, /device:TPU:0, one launch (start us, length us, event | category | flops | bytes accessed | tf_op | source)
XLA Modules:
  0.0 36.1 jit_solution(12527019831656035637)
XLA Ops:
  0.0 0.0 copy-start
  0.0 1.1 %slice.3 = bf16[160,1024]{1,0:T(8,128)(2,1)S(1)} slice(bf16[256,1024]{1,0:T(8,128)(2,1)} %rows_ref.1), slice={[0:160], [0:1024]} | slice | bytes 655360 | tf_op jit(solution)/shard_map/slice | solution.py:289
  1.1 0.0 copy-start.1
  1.1 3.1 %collective-permute-start = (bf16[160,1024]{1,0:T(8,128)(2,1)S(1)}, bf16[160,1024]{1,0:T(8,128)(2,1)S(1)}, u32[]{:S(2)}, u32[]{:S(2)}) collective-permute-start(bf16[160,1024]{1,0:T(8,128)(2,1)S(1)} %slice.3), channel_id=1, source_target_pairs={{0,4},{1,5},{2,6},{3,7},{4,8},{5,9},{6,10},{7,11},{8,12},{9,13},{1... | collective-permute-start | bytes 983048 | tf_op jit(solution)/shard_map/ppermute | solution.py:278
  4.2 0.0 copy-done
  4.2 0.0 copy-done.1
  4.2 0.2 shard_map.28
  4.4 1.6 %collective-permute-start.4 = (bf16[144,1024]{1,0:T(8,128)(2,1)S(1)}, bf16[144,1024]{1,0:T(8,128)(2,1)S(1)}, u32[]{:S(2)}, u32[]{:S(2)}) collective-permute-start(bf16[144,1024]{1,0:T(8,128)(2,1)S(1)} %get-tuple-element.22), channel_id=1, source_target_pairs={{0,2},{1,3},{2,0},{3,1},{4,6},{5,7},{6,4},{7,5},{8,10},{9,11},{10,... | collective-permute-start | bytes 884744 | tf_op jit(solution)/shard_map/ppermute | solution.py:274
  5.9 0.0 collective-permute-start.2
  5.9 0.5 %collective-permute-start.3 = (bf16[128,1024]{1,0:T(8,128)(2,1)S(1)}, bf16[128,1024]{1,0:T(8,128)(2,1)S(1)}, u32[]{:S(2)}, u32[]{:S(2)}) collective-permute-start(bf16[128,1024]{1,0:T(8,128)(2,1)S(1)} %get-tuple-element.21), channel_id=1, source_target_pairs={{0,2},{1,3},{2,0},{3,1},{4,6},{5,7},{6,4},{7,5},{8,10},{9,11},{10,... | collective-permute-start | bytes 786440 | tf_op jit(solution)/shard_map/ppermute | solution.py:274
  6.5 1.6 %collective-permute-start.7 = (bf16[112,1024]{1,0:T(8,128)(2,1)S(1)}, bf16[112,1024]{1,0:T(8,128)(2,1)S(1)}, u32[]{:S(2)}, u32[]{:S(2)}) collective-permute-start(bf16[112,1024]{1,0:T(8,128)(2,1)S(1)} %get-tuple-element.23), channel_id=1, source_target_pairs={{0,4},{1,5},{2,6},{3,7},{4,8},{5,9},{6,10},{7,11},{8,12},{9,13},{1... | collective-permute-start | bytes 688136 | tf_op jit(solution)/shard_map/ppermute | solution.py:278
  8.0 6.7 %collective-permute-done.head_ref = bf16[160,1024]{1,0:T(8,128)(2,1)S(1)} collective-permute-done((bf16[160,1024]{1,0:T(8,128)(2,1)S(1)}, bf16[160,1024]{1,0:T(8,128)(2,1)S(1)}, u32[]{:S(2)}, u32[]{:S(2)}) %collective-permute-start) | collective-permute-done | bytes 327712 | tf_op jit(solution)/shard_map/ppermute | solution.py:278
  14.7 0.7 %collective-permute-start.1 = (bf16[160,1024]{1,0:T(8,128)(2,1)S(1)}, bf16[160,1024]{1,0:T(8,128)(2,1)S(1)}, u32[]{:S(2)}, u32[]{:S(2)}) collective-permute-start(bf16[160,1024]{1,0:T(8,128)(2,1)S(1)} %collective-permute-done.head_ref), channel_id=1, source_target_pairs={{4,8},{5,9},{6,10},{7,11},{8,12},{9,13},{10,14},{11,15},{20,24},{2... | collective-permute-start | bytes 983048 | tf_op jit(solution)/shard_map/ppermute | solution.py:278
  15.4 0.0 collective-permute-done.4.refs_3_
  15.4 0.1 collective-permute-start.6
  15.5 3.0 %collective-permute-done.3.refs_2_ = bf16[128,1024]{1,0:T(8,128)(2,1)S(1)} collective-permute-done((bf16[128,1024]{1,0:T(8,128)(2,1)S(1)}, bf16[128,1024]{1,0:T(8,128)(2,1)S(1)}, u32[]{:S(2)}, u32[]{:S(2)}) %collective-permute-start.3) | collective-permute-done | bytes 262176 | tf_op jit(solution)/shard_map/ppermute | solution.py:274
  18.5 0.0 collective-permute-start.5
  18.5 0.3 collective-permute-done.7.tail_ref
  18.8 0.7 %collective-permute-start.8 = (bf16[112,1024]{1,0:T(8,128)(2,1)S(1)}, bf16[112,1024]{1,0:T(8,128)(2,1)S(1)}, u32[]{:S(2)}, u32[]{:S(2)}) collective-permute-start(bf16[112,1024]{1,0:T(8,128)(2,1)S(1)} %collective-permute-done.7.tail_ref), channel_id=1, source_target_pairs={{4,8},{5,9},{6,10},{7,11},{8,12},{9,13},{10,14},{11,15},{20,24},{2... | collective-permute-start | bytes 688136 | tf_op jit(solution)/shard_map/ppermute | solution.py:278
  19.5 0.6 %collective-permute-done.5.refs_4_ = bf16[128,1024]{1,0:T(8,128)(2,1)S(1)} collective-permute-done((bf16[128,1024]{1,0:T(8,128)(2,1)S(1)}, bf16[128,1024]{1,0:T(8,128)(2,1)S(1)}, u32[]{:S(2)}, u32[]{:S(2)}) %collective-permute-start.5) | collective-permute-done | bytes 262176 | tf_op jit(solution)/shard_map/ppermute | solution.py:274
  20.1 0.0 collective-permute-done.2.refs_1_
  20.1 0.0 collective-permute-done.6.refs_5_
  20.1 2.2 %shard_map.30 = (f32[1024,128]{1,0:T(8,128)S(1)}, f32[1,256]{1,0:T(1,128)S(1)}, f32[1024,128]{1,0:T(8,128)S(1)}, f32[1,256]{1,0:T(1,128)S(1)}) custom-call(bf16[160,1024]{1,0:T(8,128)(2,1)S(1)} %collective-permute-done.head_ref, bf16[112,1024]{1,0:T(8,128)(2,1)S(1)} %collective-permute-done.7.tail_ref, bf16[272,1024]{1,0:T(8,128)(2,1)S(1)} %get-tuple-element.20.refs_0_, ...), custom_call_target="tpu_custom_call" | custom-call | flops 1 | bytes 1 | tf_op jit(solution)/shard_map/pallas_call | solution.py:302
  22.2 3.0 %collective-permute-start.9 = (f32[1,256]{1,0:T(1,128)S(1)}, f32[1,256]{1,0:T(1,128)S(1)}, u32[]{:S(2)}, u32[]{:S(2)}) collective-permute-start(f32[1,256]{1,0:T(1,128)S(1)} %get-tuple-element.28), channel_id=1, source_target_pairs={{4,0},{5,1},{6,2},{7,3},{8,4},{9,5},{10,6},{11,7},{12,8},{13,9},{1... | collective-permute-start | bytes 3080 | tf_op jit(solution)/shard_map/ppermute | solution.py:278
  25.2 0.0 collective-permute-done.1.head_ref
  25.2 0.0 collective-permute-done.8.tail_ref
  25.2 0.2 shard_map.31
  25.5 1.9 %collective-permute-done.9 = f32[1,256]{1,0:T(1,128)S(1)} collective-permute-done((f32[1,256]{1,0:T(1,128)S(1)}, f32[1,256]{1,0:T(1,128)S(1)}, u32[]{:S(2)}, u32[]{:S(2)}) %collective-permute-start.9) | collective-permute-done | bytes 1056 | tf_op jit(solution)/shard_map/ppermute | solution.py:278
  27.4 0.0 collective-permute-start.13
  27.4 1.3 %collective-permute-start.10 = (f32[1,256]{1,0:T(1,128)S(1)}, f32[1,256]{1,0:T(1,128)S(1)}, u32[]{:S(2)}, u32[]{:S(2)}) collective-permute-start(f32[1,256]{1,0:T(1,128)S(1)} %get-tuple-element.31), channel_id=1, source_target_pairs={{8,0},{9,1},{10,2},{11,3},{12,4},{13,5},{14,6},{15,7},{24,16},{25,... | collective-permute-start | bytes 3080 | tf_op jit(solution)/shard_map/ppermute | solution.py:278
  28.7 1.6 %collective-permute-start.11 = (f32[1,256]{1,0:T(1,128)S(1)}, f32[1,256]{1,0:T(1,128)S(1)}, u32[]{:S(2)}, u32[]{:S(2)}) collective-permute-start(f32[1,256]{1,0:T(1,128)S(1)} %get-tuple-element.32), channel_id=1, source_target_pairs={{0,2},{1,3},{2,0},{3,1},{4,6},{5,7},{6,4},{7,5},{8,10},{9,11},{10,... | collective-permute-start | bytes 3080 | tf_op jit(solution)/shard_map/ppermute | solution.py:274
  30.2 0.4 collective-permute-start.12
  30.6 0.0 collective-permute-done.13
  30.6 4.9 %collective-permute-done.10 = f32[1,256]{1,0:T(1,128)S(1)} collective-permute-done((f32[1,256]{1,0:T(1,128)S(1)}, f32[1,256]{1,0:T(1,128)S(1)}, u32[]{:S(2)}, u32[]{:S(2)}) %collective-permute-start.10) | collective-permute-done | bytes 1056 | tf_op jit(solution)/shard_map/ppermute | solution.py:278
  35.5 0.0 collective-permute-done.11
  35.5 0.0 collective-permute-done.12
  35.5 0.6 %add_log-plus-one_fusion = f32[1,256]{1,0:T(1,128)} fusion(f32[1,256]{1,0:T(1,128)S(1)} %collective-permute-done.13, f32[1,256]{1,0:T(1,128)S(1)} %collective-permute-done.12, f32[1,256]{1,0:T(1,128)S(1)} %collective-permute-done.11, f32[1,256]{1,0:T(1,128)S(1)} %collective-permute-done.10, f32[1,256]{1,0:T(1,128)S(1)} %get-tuple-element.27, ...), kind=kLoop, calls=%fused_computation | loop fusion | flops 1280 | bytes 7168 | tf_op jit(solution)/shard_map/log1p | solution.py:324
  (1 shorter events, 0.0 us)
Async XLA Ops:
  0.0 4.2 %copy-start = (bf16[256,1024]{1,0:T(8,128)(2,1)S(1)}, bf16[256,1024]{1,0:T(8,128)(2,1)}, u32[]{:S(2)}) copy-start(bf16[256,1024]{1,0:T(8,128)(2,1)} %rows_ref.1) | copy-start | bytes 1572868
  1.1 3.1 %copy-start.1 = (s32[256]{0:T(256)S(1)}, s32[256]{0:T(256)}, u32[]{:S(2)}) copy-start(s32[256]{0:T(256)} %param.3) | copy-start | bytes 3076
  1.1 13.6 %collective-permute-start = (bf16[160,1024]{1,0:T(8,128)(2,1)S(1)}, bf16[160,1024]{1,0:T(8,128)(2,1)S(1)}, u32[]{:S(2)}, u32[]{:S(2)}) collective-permute-start(bf16[160,1024]{1,0:T(8,128)(2,1)S(1)} %slice.3), channel_id=1, source_target_pairs={{0,4},{1,5},{2,6},{3,7},{4,8},{5,9},{6,10},{7,11},{8,12},{9,13},{1... | collective-permute-start | bytes 983048 | tf_op jit(solution)/shard_map/ppermute | solution.py:278
  4.4 11.0 %collective-permute-start.4 = (bf16[144,1024]{1,0:T(8,128)(2,1)S(1)}, bf16[144,1024]{1,0:T(8,128)(2,1)S(1)}, u32[]{:S(2)}, u32[]{:S(2)}) collective-permute-start(bf16[144,1024]{1,0:T(8,128)(2,1)S(1)} %get-tuple-element.22), channel_id=1, source_target_pairs={{0,2},{1,3},{2,0},{3,1},{4,6},{5,7},{6,4},{7,5},{8,10},{9,11},{10,... | collective-permute-start | bytes 884744 | tf_op jit(solution)/shard_map/ppermute | solution.py:274
  5.9 14.1 %collective-permute-start.2 = (bf16[272,1024]{1,0:T(8,128)(2,1)S(1)}, bf16[272,1024]{1,0:T(8,128)(2,1)S(1)}, u32[]{:S(2)}, u32[]{:S(2)}) collective-permute-start(bf16[272,1024]{1,0:T(8,128)(2,1)S(1)} %get-tuple-element.20.refs_0_), channel_id=1, source_target_pairs={{0,1},{1,0},{2,3},{3,2},{4,5},{5,4},{6,7},{7,6},{8,9},{9,8},{10,11... | collective-permute-start | bytes 1671176 | tf_op jit(solution)/shard_map/ppermute | solution.py:274
  5.9 12.6 %collective-permute-start.3 = (bf16[128,1024]{1,0:T(8,128)(2,1)S(1)}, bf16[128,1024]{1,0:T(8,128)(2,1)S(1)}, u32[]{:S(2)}, u32[]{:S(2)}) collective-permute-start(bf16[128,1024]{1,0:T(8,128)(2,1)S(1)} %get-tuple-element.21), channel_id=1, source_target_pairs={{0,2},{1,3},{2,0},{3,1},{4,6},{5,7},{6,4},{7,5},{8,10},{9,11},{10,... | collective-permute-start | bytes 786440 | tf_op jit(solution)/shard_map/ppermute | solution.py:274
  6.5 12.3 %collective-permute-start.7 = (bf16[112,1024]{1,0:T(8,128)(2,1)S(1)}, bf16[112,1024]{1,0:T(8,128)(2,1)S(1)}, u32[]{:S(2)}, u32[]{:S(2)}) collective-permute-start(bf16[112,1024]{1,0:T(8,128)(2,1)S(1)} %get-tuple-element.23), channel_id=1, source_target_pairs={{0,4},{1,5},{2,6},{3,7},{4,8},{5,9},{6,10},{7,11},{8,12},{9,13},{1... | collective-permute-start | bytes 688136 | tf_op jit(solution)/shard_map/ppermute | solution.py:278
  14.7 10.5 %collective-permute-start.1 = (bf16[160,1024]{1,0:T(8,128)(2,1)S(1)}, bf16[160,1024]{1,0:T(8,128)(2,1)S(1)}, u32[]{:S(2)}, u32[]{:S(2)}) collective-permute-start(bf16[160,1024]{1,0:T(8,128)(2,1)S(1)} %collective-permute-done.head_ref), channel_id=1, source_target_pairs={{4,8},{5,9},{6,10},{7,11},{8,12},{9,13},{10,14},{11,15},{20,24},{2... | collective-permute-start | bytes 983048 | tf_op jit(solution)/shard_map/ppermute | solution.py:278
  15.4 4.6 %collective-permute-start.6 = (bf16[144,1024]{1,0:T(8,128)(2,1)S(1)}, bf16[144,1024]{1,0:T(8,128)(2,1)S(1)}, u32[]{:S(2)}, u32[]{:S(2)}) collective-permute-start(bf16[144,1024]{1,0:T(8,128)(2,1)S(1)} %collective-permute-done.4.refs_3_), channel_id=1, source_target_pairs={{0,1},{1,0},{2,3},{3,2},{4,5},{5,4},{6,7},{7,6},{8,9},{9,8},{10,11... | collective-permute-start | bytes 884744 | tf_op jit(solution)/shard_map/ppermute | solution.py:274
  18.5 1.5 %collective-permute-start.5 = (bf16[128,1024]{1,0:T(8,128)(2,1)S(1)}, bf16[128,1024]{1,0:T(8,128)(2,1)S(1)}, u32[]{:S(2)}, u32[]{:S(2)}) collective-permute-start(bf16[128,1024]{1,0:T(8,128)(2,1)S(1)} %collective-permute-done.3.refs_2_), channel_id=1, source_target_pairs={{0,1},{1,0},{2,3},{3,2},{4,5},{5,4},{6,7},{7,6},{8,9},{9,8},{10,11... | collective-permute-start | bytes 786440 | tf_op jit(solution)/shard_map/ppermute | solution.py:274
  18.8 6.4 %collective-permute-start.8 = (bf16[112,1024]{1,0:T(8,128)(2,1)S(1)}, bf16[112,1024]{1,0:T(8,128)(2,1)S(1)}, u32[]{:S(2)}, u32[]{:S(2)}) collective-permute-start(bf16[112,1024]{1,0:T(8,128)(2,1)S(1)} %collective-permute-done.7.tail_ref), channel_id=1, source_target_pairs={{4,8},{5,9},{6,10},{7,11},{8,12},{9,13},{10,14},{11,15},{20,24},{2... | collective-permute-start | bytes 688136 | tf_op jit(solution)/shard_map/ppermute | solution.py:278
  22.2 5.1 %collective-permute-start.9 = (f32[1,256]{1,0:T(1,128)S(1)}, f32[1,256]{1,0:T(1,128)S(1)}, u32[]{:S(2)}, u32[]{:S(2)}) collective-permute-start(f32[1,256]{1,0:T(1,128)S(1)} %get-tuple-element.28), channel_id=1, source_target_pairs={{4,0},{5,1},{6,2},{7,3},{8,4},{9,5},{10,6},{11,7},{12,8},{13,9},{1... | collective-permute-start | bytes 3080 | tf_op jit(solution)/shard_map/ppermute | solution.py:278
  27.4 3.2 %collective-permute-start.13 = (f32[1,256]{1,0:T(1,128)S(1)}, f32[1,256]{1,0:T(1,128)S(1)}, u32[]{:S(2)}, u32[]{:S(2)}) collective-permute-start(f32[1,256]{1,0:T(1,128)S(1)} %get-tuple-element.34), channel_id=1, source_target_pairs={{0,1},{1,0},{2,3},{3,2},{4,5},{5,4},{6,7},{7,6},{8,9},{9,8},{10,11... | collective-permute-start | bytes 3080 | tf_op jit(solution)/shard_map/ppermute | solution.py:274
  27.4 8.1 %collective-permute-start.10 = (f32[1,256]{1,0:T(1,128)S(1)}, f32[1,256]{1,0:T(1,128)S(1)}, u32[]{:S(2)}, u32[]{:S(2)}) collective-permute-start(f32[1,256]{1,0:T(1,128)S(1)} %get-tuple-element.31), channel_id=1, source_target_pairs={{8,0},{9,1},{10,2},{11,3},{12,4},{13,5},{14,6},{15,7},{24,16},{25,... | collective-permute-start | bytes 3080 | tf_op jit(solution)/shard_map/ppermute | solution.py:278
  28.7 6.8 %collective-permute-start.11 = (f32[1,256]{1,0:T(1,128)S(1)}, f32[1,256]{1,0:T(1,128)S(1)}, u32[]{:S(2)}, u32[]{:S(2)}) collective-permute-start(f32[1,256]{1,0:T(1,128)S(1)} %get-tuple-element.32), channel_id=1, source_target_pairs={{0,2},{1,3},{2,0},{3,1},{4,6},{5,7},{6,4},{7,5},{8,10},{9,11},{10,... | collective-permute-start | bytes 3080 | tf_op jit(solution)/shard_map/ppermute | solution.py:274
  30.2 5.3 %collective-permute-start.12 = (f32[1,256]{1,0:T(1,128)S(1)}, f32[1,256]{1,0:T(1,128)S(1)}, u32[]{:S(2)}, u32[]{:S(2)}) collective-permute-start(f32[1,256]{1,0:T(1,128)S(1)} %get-tuple-element.33), channel_id=1, source_target_pairs={{0,3},{1,2},{2,1},{3,0},{4,7},{5,6},{6,5},{7,4},{8,11},{9,10},{10,... | collective-permute-start | bytes 3080 | tf_op jit(solution)/shard_map/ppermute | solution.py:274

commit v18 on v17

--- a/solution.py
+++ b/solution.py
@@ -81,7 +81,7 @@
 LANES = 128
 PLANE = 4
 INVERSE_TEMP_BITS = 20.0 * 1.4426950408889634
-ID_ROWS = 16
+ID_ROWS = 8
 VMEM_BYTES = 16 * 1024 * 1024
 
 
@@ -283,7 +283,7 @@
     first_back = [(b, a) for a, b in first_moves]
     last_back = [(b, a) for a, b in last_moves]
 
-    half, part = row_count // 2, 5 * row_count // 8
+    half, part = row_count // 2, 9 * row_count // 16
     ranges = [(0, row_count), (0, half), (half, row_count), (part, row_count)]
     id_rows = [ID_ROWS, 0, ID_ROWS, ID_ROWS]
     first_head = on_line(embeddings[:part], first_moves)

time: 36.2 us -> 35.8 us (0.989)
  waiting for transfers between devices: 17.4 us -> 16.9 us
    ppermute x6, waiting for transfers between devices: 13.8 us -> 13 us  [on_line(): return lax.ppermute(value, 'gx', pairs)]
where the time goes in v18:
time: 35.8 us; the launch traced here: 35.6 us
  waiting for transfers between devices  16.9 us (47%)
  starting transfers between devices  14.4 us (40%)
  Pallas kernels  2.57 us (7%)
  local copies, waits for them, and re-layouts  1.06 us (3%)
  other arithmetic  0.58 us (2%)
    ppermute x6, waiting for transfers between devices, on_line(): return lax.ppermute(value, 'gx', pairs)  13 us
    ppermute x6, starting transfers between devices, on_line(): return lax.ppermute(value, 'gx', pairs)  10.3 us
    ppermute x8, starting transfers between devices, in_plane(): return lax.ppermute(value, 'gx', [(i, i ^ step) for i in range(peers)])  4.09 us
    ppermute x8, waiting for transfers between devices, in_plane(): return lax.ppermute(value, 'gx', [(i, i ^ step) for i in range(peers)])  3.96 us
    pallas_call x1, Pallas kernels, grid_plan(): pl.pallas_call(functools.partial(first_kernel, first_moves), out_shape=(l...  2.13 us
    slice x1, local copies, waits for them, and re-layouts, grid_plan(): first_head = on_line(embeddings[:part], first_moves)  1.05 us
  transfers between devices with their start and end apart: 14, of which 6 were waited for; matrix products, arithmetic and copies ran while one was open for 0% of the time, Pallas kernels for 7%

profile of v18, /device:TPU:0, one launch (start us, length us, event | category | flops | bytes accessed | tf_op | source)
XLA Modules:
  0.0 35.6 jit_solution(12170774942416608183)
XLA Ops:
  0.0 0.0 copy-start
  0.0 1.1 %slice.3 = bf16[144,1024]{1,0:T(8,128)(2,1)S(1)} slice(bf16[256,1024]{1,0:T(8,128)(2,1)} %rows_ref.1), slice={[0:144], [0:1024]} | slice | bytes 589824 | tf_op jit(solution)/shard_map/slice | solution.py:289
  1.1 0.0 copy-start.1
  1.1 3.1 %collective-permute-start = (bf16[144,1024]{1,0:T(8,128)(2,1)S(1)}, bf16[144,1024]{1,0:T(8,128)(2,1)S(1)}, u32[]{:S(2)}, u32[]{:S(2)}) collective-permute-start(bf16[144,1024]{1,0:T(8,128)(2,1)S(1)} %slice.3), channel_id=1, source_target_pairs={{0,4},{1,5},{2,6},{3,7},{4,8},{5,9},{6,10},{7,11},{8,12},{9,13},{1... | collective-permute-start | bytes 884744 | tf_op jit(solution)/shard_map/ppermute | solution.py:278
  4.1 0.0 copy-done
  4.2 0.0 copy-done.1
  4.2 0.2 shard_map.28
  4.4 1.6 %collective-permute-start.4 = (bf16[136,1024]{1,0:T(8,128)(2,1)S(1)}, bf16[136,1024]{1,0:T(8,128)(2,1)S(1)}, u32[]{:S(2)}, u32[]{:S(2)}) collective-permute-start(bf16[136,1024]{1,0:T(8,128)(2,1)S(1)} %get-tuple-element.22), channel_id=1, source_target_pairs={{0,2},{1,3},{2,0},{3,1},{4,6},{5,7},{6,4},{7,5},{8,10},{9,11},{10,... | collective-permute-start | bytes 835592 | tf_op jit(solution)/shard_map/ppermute | solution.py:274
  5.9 0.0 collective-permute-start.2
  5.9 0.5 %collective-permute-start.3 = (bf16[128,1024]{1,0:T(8,128)(2,1)S(1)}, bf16[128,1024]{1,0:T(8,128)(2,1)S(1)}, u32[]{:S(2)}, u32[]{:S(2)}) collective-permute-start(bf16[128,1024]{1,0:T(8,128)(2,1)S(1)} %get-tuple-element.21), channel_id=1, source_target_pairs={{0,2},{1,3},{2,0},{3,1},{4,6},{5,7},{6,4},{7,5},{8,10},{9,11},{10,... | collective-permute-start | bytes 786440 | tf_op jit(solution)/shard_map/ppermute | solution.py:274
  6.4 1.6 %collective-permute-start.7 = (bf16[120,1024]{1,0:T(8,128)(2,1)S(1)}, bf16[120,1024]{1,0:T(8,128)(2,1)S(1)}, u32[]{:S(2)}, u32[]{:S(2)}) collective-permute-start(bf16[120,1024]{1,0:T(8,128)(2,1)S(1)} %get-tuple-element.23), channel_id=1, source_target_pairs={{0,4},{1,5},{2,6},{3,7},{4,8},{5,9},{6,10},{7,11},{8,12},{9,13},{1... | collective-permute-start | bytes 737288 | tf_op jit(solution)/shard_map/ppermute | solution.py:278
  8.0 6.0 %collective-permute-done.head_ref = bf16[144,1024]{1,0:T(8,128)(2,1)S(1)} collective-permute-done((bf16[144,1024]{1,0:T(8,128)(2,1)S(1)}, bf16[144,1024]{1,0:T(8,128)(2,1)S(1)}, u32[]{:S(2)}, u32[]{:S(2)}) %collective-permute-start) | collective-permute-done | bytes 294944 | tf_op jit(solution)/shard_map/ppermute | solution.py:278
  14.0 0.7 %collective-permute-start.1 = (bf16[144,1024]{1,0:T(8,128)(2,1)S(1)}, bf16[144,1024]{1,0:T(8,128)(2,1)S(1)}, u32[]{:S(2)}, u32[]{:S(2)}) collective-permute-start(bf16[144,1024]{1,0:T(8,128)(2,1)S(1)} %collective-permute-done.head_ref), channel_id=1, source_target_pairs={{4,8},{5,9},{6,10},{7,11},{8,12},{9,13},{10,14},{11,15},{20,24},{2... | collective-permute-start | bytes 884744 | tf_op jit(solution)/shard_map/ppermute | solution.py:278
  14.7 0.0 collective-permute-done.4.refs_3_
  14.7 0.1 collective-permute-start.6
  14.8 3.4 %collective-permute-done.3.refs_2_ = bf16[128,1024]{1,0:T(8,128)(2,1)S(1)} collective-permute-done((bf16[128,1024]{1,0:T(8,128)(2,1)S(1)}, bf16[128,1024]{1,0:T(8,128)(2,1)S(1)}, u32[]{:S(2)}, u32[]{:S(2)}) %collective-permute-start.3) | collective-permute-done | bytes 262176 | tf_op jit(solution)/shard_map/ppermute | solution.py:274
  18.2 0.0 collective-permute-start.5
  18.2 0.3 collective-permute-done.7.tail_ref
  18.4 0.7 %collective-permute-start.8 = (bf16[120,1024]{1,0:T(8,128)(2,1)S(1)}, bf16[120,1024]{1,0:T(8,128)(2,1)S(1)}, u32[]{:S(2)}, u32[]{:S(2)}) collective-permute-start(bf16[120,1024]{1,0:T(8,128)(2,1)S(1)} %collective-permute-done.7.tail_ref), channel_id=1, source_target_pairs={{4,8},{5,9},{6,10},{7,11},{8,12},{9,13},{10,14},{11,15},{20,24},{2... | collective-permute-start | bytes 737288 | tf_op jit(solution)/shard_map/ppermute | solution.py:278
  19.1 0.6 %collective-permute-done.5.refs_4_ = bf16[128,1024]{1,0:T(8,128)(2,1)S(1)} collective-permute-done((bf16[128,1024]{1,0:T(8,128)(2,1)S(1)}, bf16[128,1024]{1,0:T(8,128)(2,1)S(1)}, u32[]{:S(2)}, u32[]{:S(2)}) %collective-permute-start.5) | collective-permute-done | bytes 262176 | tf_op jit(solution)/shard_map/ppermute | solution.py:274
  19.7 0.0 collective-permute-done.2.refs_1_
  19.7 0.0 collective-permute-done.6.refs_5_
  19.7 2.1 %shard_map.30 = (f32[1024,128]{1,0:T(8,128)S(1)}, f32[1,256]{1,0:T(1,128)S(1)}, f32[1024,128]{1,0:T(8,128)S(1)}, f32[1,256]{1,0:T(1,128)S(1)}) custom-call(bf16[144,1024]{1,0:T(8,128)(2,1)S(1)} %collective-permute-done.head_ref, bf16[120,1024]{1,0:T(8,128)(2,1)S(1)} %collective-permute-done.7.tail_ref, bf16[264,1024]{1,0:T(8,128)(2,1)S(1)} %get-tuple-element.20.refs_0_, ...), custom_call_target="tpu_custom_call" | custom-call | flops 1 | bytes 1 | tf_op jit(solution)/shard_map/pallas_call | solution.py:302
  21.8 3.0 %collective-permute-start.9 = (f32[1,256]{1,0:T(1,128)S(1)}, f32[1,256]{1,0:T(1,128)S(1)}, u32[]{:S(2)}, u32[]{:S(2)}) collective-permute-start(f32[1,256]{1,0:T(1,128)S(1)} %get-tuple-element.28), channel_id=1, source_target_pairs={{4,0},{5,1},{6,2},{7,3},{8,4},{9,5},{10,6},{11,7},{12,8},{13,9},{1... | collective-permute-start | bytes 3080 | tf_op jit(solution)/shard_map/ppermute | solution.py:278
  24.8 0.0 collective-permute-done.1.head_ref
  24.8 0.0 collective-permute-done.8.tail_ref
  24.8 0.2 shard_map.31
  25.1 1.9 %collective-permute-done.9 = f32[1,256]{1,0:T(1,128)S(1)} collective-permute-done((f32[1,256]{1,0:T(1,128)S(1)}, f32[1,256]{1,0:T(1,128)S(1)}, u32[]{:S(2)}, u32[]{:S(2)}) %collective-permute-start.9) | collective-permute-done | bytes 1056 | tf_op jit(solution)/shard_map/ppermute | solution.py:278
  27.0 0.0 collective-permute-start.13
  27.0 1.3 %collective-permute-start.10 = (f32[1,256]{1,0:T(1,128)S(1)}, f32[1,256]{1,0:T(1,128)S(1)}, u32[]{:S(2)}, u32[]{:S(2)}) collective-permute-start(f32[1,256]{1,0:T(1,128)S(1)} %get-tuple-element.31), channel_id=1, source_target_pairs={{8,0},{9,1},{10,2},{11,3},{12,4},{13,5},{14,6},{15,7},{24,16},{25,... | collective-permute-start | bytes 3080 | tf_op jit(solution)/shard_map/ppermute | solution.py:278
  28.3 1.6 %collective-permute-start.11 = (f32[1,256]{1,0:T(1,128)S(1)}, f32[1,256]{1,0:T(1,128)S(1)}, u32[]{:S(2)}, u32[]{:S(2)}) collective-permute-start(f32[1,256]{1,0:T(1,128)S(1)} %get-tuple-element.32), channel_id=1, source_target_pairs={{0,2},{1,3},{2,0},{3,1},{4,6},{5,7},{6,4},{7,5},{8,10},{9,11},{10,... | collective-permute-start | bytes 3080 | tf_op jit(solution)/shard_map/ppermute | solution.py:274
  29.8 0.4 %collective-permute-start.12 = (f32[1,256]{1,0:T(1,128)S(1)}, f32[1,256]{1,0:T(1,128)S(1)}, u32[]{:S(2)}, u32[]{:S(2)}) collective-permute-start(f32[1,256]{1,0:T(1,128)S(1)} %get-tuple-element.33), channel_id=1, source_target_pairs={{0,3},{1,2},{2,1},{3,0},{4,7},{5,6},{6,5},{7,4},{8,11},{9,10},{10,... | collective-permute-start | bytes 3080 | tf_op jit(solution)/shard_map/ppermute | solution.py:274
  30.2 0.0 collective-permute-done.13
  30.2 4.8 %collective-permute-done.10 = f32[1,256]{1,0:T(1,128)S(1)} collective-permute-done((f32[1,256]{1,0:T(1,128)S(1)}, f32[1,256]{1,0:T(1,128)S(1)}, u32[]{:S(2)}, u32[]{:S(2)}) %collective-permute-start.10) | collective-permute-done | bytes 1056 | tf_op jit(solution)/shard_map/ppermute | solution.py:278
  35.0 0.0 collective-permute-done.11
  35.0 0.0 collective-permute-done.12
  35.0 0.6 %add_log-plus-one_fusion = f32[1,256]{1,0:T(1,128)} fusion(f32[1,256]{1,0:T(1,128)S(1)} %collective-permute-done.13, f32[1,256]{1,0:T(1,128)S(1)} %collective-permute-done.12, f32[1,256]{1,0:T(1,128)S(1)} %collective-permute-done.11, f32[1,256]{1,0:T(1,128)S(1)} %collective-permute-done.10, f32[1,256]{1,0:T(1,128)S(1)} %get-tuple-element.27, ...), kind=kLoop, calls=%fused_computation | loop fusion | flops 1280 | bytes 7168 | tf_op jit(solution)/shard_map/log1p | solution.py:324
  (1 shorter events, 0.0 us)
Async XLA Ops:
  0.0 4.1 %copy-start = (bf16[256,1024]{1,0:T(8,128)(2,1)S(1)}, bf16[256,1024]{1,0:T(8,128)(2,1)}, u32[]{:S(2)}) copy-start(bf16[256,1024]{1,0:T(8,128)(2,1)} %rows_ref.1) | copy-start | bytes 1572868
  1.1 3.1 %copy-start.1 = (s32[256]{0:T(256)S(1)}, s32[256]{0:T(256)}, u32[]{:S(2)}) copy-start(s32[256]{0:T(256)} %param.3) | copy-start | bytes 3076
  1.1 12.9 %collective-permute-start = (bf16[144,1024]{1,0:T(8,128)(2,1)S(1)}, bf16[144,1024]{1,0:T(8,128)(2,1)S(1)}, u32[]{:S(2)}, u32[]{:S(2)}) collective-permute-start(bf16[144,1024]{1,0:T(8,128)(2,1)S(1)} %slice.3), channel_id=1, source_target_pairs={{0,4},{1,5},{2,6},{3,7},{4,8},{5,9},{6,10},{7,11},{8,12},{9,13},{1... | collective-permute-start | bytes 884744 | tf_op jit(solution)/shard_map/ppermute | solution.py:278
  4.4 10.3 %collective-permute-start.4 = (bf16[136,1024]{1,0:T(8,128)(2,1)S(1)}, bf16[136,1024]{1,0:T(8,128)(2,1)S(1)}, u32[]{:S(2)}, u32[]{:S(2)}) collective-permute-start(bf16[136,1024]{1,0:T(8,128)(2,1)S(1)} %get-tuple-element.22), channel_id=1, source_target_pairs={{0,2},{1,3},{2,0},{3,1},{4,6},{5,7},{6,4},{7,5},{8,10},{9,11},{10,... | collective-permute-start | bytes 835592 | tf_op jit(solution)/shard_map/ppermute | solution.py:274
  5.9 13.8 %collective-permute-start.2 = (bf16[264,1024]{1,0:T(8,128)(2,1)S(1)}, bf16[264,1024]{1,0:T(8,128)(2,1)S(1)}, u32[]{:S(2)}, u32[]{:S(2)}) collective-permute-start(bf16[264,1024]{1,0:T(8,128)(2,1)S(1)} %get-tuple-element.20.refs_0_), channel_id=1, source_target_pairs={{0,1},{1,0},{2,3},{3,2},{4,5},{5,4},{6,7},{7,6},{8,9},{9,8},{10,11... | collective-permute-start | bytes 1622024 | tf_op jit(solution)/shard_map/ppermute | solution.py:274
  5.9 12.2 %collective-permute-start.3 = (bf16[128,1024]{1,0:T(8,128)(2,1)S(1)}, bf16[128,1024]{1,0:T(8,128)(2,1)S(1)}, u32[]{:S(2)}, u32[]{:S(2)}) collective-permute-start(bf16[128,1024]{1,0:T(8,128)(2,1)S(1)} %get-tuple-element.21), channel_id=1, source_target_pairs={{0,2},{1,3},{2,0},{3,1},{4,6},{5,7},{6,4},{7,5},{8,10},{9,11},{10,... | collective-permute-start | bytes 786440 | tf_op jit(solution)/shard_map/ppermute | solution.py:274
  6.4 12.0 %collective-permute-start.7 = (bf16[120,1024]{1,0:T(8,128)(2,1)S(1)}, bf16[120,1024]{1,0:T(8,128)(2,1)S(1)}, u32[]{:S(2)}, u32[]{:S(2)}) collective-permute-start(bf16[120,1024]{1,0:T(8,128)(2,1)S(1)} %get-tuple-element.23), channel_id=1, source_target_pairs={{0,4},{1,5},{2,6},{3,7},{4,8},{5,9},{6,10},{7,11},{8,12},{9,13},{1... | collective-permute-start | bytes 737288 | tf_op jit(solution)/shard_map/ppermute | solution.py:278
  14.0 10.8 %collective-permute-start.1 = (bf16[144,1024]{1,0:T(8,128)(2,1)S(1)}, bf16[144,1024]{1,0:T(8,128)(2,1)S(1)}, u32[]{:S(2)}, u32[]{:S(2)}) collective-permute-start(bf16[144,1024]{1,0:T(8,128)(2,1)S(1)} %collective-permute-done.head_ref), channel_id=1, source_target_pairs={{4,8},{5,9},{6,10},{7,11},{8,12},{9,13},{10,14},{11,15},{20,24},{2... | collective-permute-start | bytes 884744 | tf_op jit(solution)/shard_map/ppermute | solution.py:278
  14.7 5.0 %collective-permute-start.6 = (bf16[136,1024]{1,0:T(8,128)(2,1)S(1)}, bf16[136,1024]{1,0:T(8,128)(2,1)S(1)}, u32[]{:S(2)}, u32[]{:S(2)}) collective-permute-start(bf16[136,1024]{1,0:T(8,128)(2,1)S(1)} %collective-permute-done.4.refs_3_), channel_id=1, source_target_pairs={{0,1},{1,0},{2,3},{3,2},{4,5},{5,4},{6,7},{7,6},{8,9},{9,8},{10,11... | collective-permute-start | bytes 835592 | tf_op jit(solution)/shard_map/ppermute | solution.py:274
  18.2 1.5 %collective-permute-start.5 = (bf16[128,1024]{1,0:T(8,128)(2,1)S(1)}, bf16[128,1024]{1,0:T(8,128)(2,1)S(1)}, u32[]{:S(2)}, u32[]{:S(2)}) collective-permute-start(bf16[128,1024]{1,0:T(8,128)(2,1)S(1)} %collective-permute-done.3.refs_2_), channel_id=1, source_target_pairs={{0,1},{1,0},{2,3},{3,2},{4,5},{5,4},{6,7},{7,6},{8,9},{9,8},{10,11... | collective-permute-start | bytes 786440 | tf_op jit(solution)/shard_map/ppermute | solution.py:274
  18.4 6.4 %collective-permute-start.8 = (bf16[120,1024]{1,0:T(8,128)(2,1)S(1)}, bf16[120,1024]{1,0:T(8,128)(2,1)S(1)}, u32[]{:S(2)}, u32[]{:S(2)}) collective-permute-start(bf16[120,1024]{1,0:T(8,128)(2,1)S(1)} %collective-permute-done.7.tail_ref), channel_id=1, source_target_pairs={{4,8},{5,9},{6,10},{7,11},{8,12},{9,13},{10,14},{11,15},{20,24},{2... | collective-permute-start | bytes 737288 | tf_op jit(solution)/shard_map/ppermute | solution.py:278
  21.8 5.2 %collective-permute-start.9 = (f32[1,256]{1,0:T(1,128)S(1)}, f32[1,256]{1,0:T(1,128)S(1)}, u32[]{:S(2)}, u32[]{:S(2)}) collective-permute-start(f32[1,256]{1,0:T(1,128)S(1)} %get-tuple-element.28), channel_id=1, source_target_pairs={{4,0},{5,1},{6,2},{7,3},{8,4},{9,5},{10,6},{11,7},{12,8},{13,9},{1... | collective-permute-start | bytes 3080 | tf_op jit(solution)/shard_map/ppermute | solution.py:278
  27.0 3.2 %collective-permute-start.13 = (f32[1,256]{1,0:T(1,128)S(1)}, f32[1,256]{1,0:T(1,128)S(1)}, u32[]{:S(2)}, u32[]{:S(2)}) collective-permute-start(f32[1,256]{1,0:T(1,128)S(1)} %get-tuple-element.34), channel_id=1, source_target_pairs={{0,1},{1,0},{2,3},{3,2},{4,5},{5,4},{6,7},{7,6},{8,9},{9,8},{10,11... | collective-permute-start | bytes 3080 | tf_op jit(solution)/shard_map/ppermute | solution.py:274
  27.0 8.0 %collective-permute-start.10 = (f32[1,256]{1,0:T(1,128)S(1)}, f32[1,256]{1,0:T(1,128)S(1)}, u32[]{:S(2)}, u32[]{:S(2)}) collective-permute-start(f32[1,256]{1,0:T(1,128)S(1)} %get-tuple-element.31), channel_id=1, source_target_pairs={{8,0},{9,1},{10,2},{11,3},{12,4},{13,5},{14,6},{15,7},{24,16},{25,... | collective-permute-start | bytes 3080 | tf_op jit(solution)/shard_map/ppermute | solution.py:278
  28.3 6.7 %collective-permute-start.11 = (f32[1,256]{1,0:T(1,128)S(1)}, f32[1,256]{1,0:T(1,128)S(1)}, u32[]{:S(2)}, u32[]{:S(2)}) collective-permute-start(f32[1,256]{1,0:T(1,128)S(1)} %get-tuple-element.32), channel_id=1, source_target_pairs={{0,2},{1,3},{2,0},{3,1},{4,6},{5,7},{6,4},{7,5},{8,10},{9,11},{10,... | collective-permute-start | bytes 3080 | tf_op jit(solution)/shard_map/ppermute | solution.py:274
  29.8 5.2 %collective-permute-start.12 = (f32[1,256]{1,0:T(1,128)S(1)}, f32[1,256]{1,0:T(1,128)S(1)}, u32[]{:S(2)}, u32[]{:S(2)}) collective-permute-start(f32[1,256]{1,0:T(1,128)S(1)} %get-tuple-element.33), channel_id=1, source_target_pairs={{0,3},{1,2},{2,1},{3,0},{4,7},{5,6},{6,5},{7,4},{8,11},{9,10},{10,... | collective-permute-start | bytes 3080 | tf_op jit(solution)/shard_map/ppermute | solution.py:274

commit v19 on v18

--- a/solution.py
+++ b/solution.py
@@ -127,13 +127,6 @@
         ref[:size, :] = units[first:last]
         if ref.shape[0] > size:
             ref[size:, :] = ids
-
-
-def padded(values, count, fill):
-    rows, columns = values.shape
-    if rows == 1:
-        return jnp.concatenate([values, jnp.full((1, count - columns), fill, values.dtype)], axis=1)
-    return jnp.concatenate([values, jnp.full((count - rows, columns), fill, values.dtype)], axis=0)
 
 
 def arrived_at(moves):
@@ -172,7 +165,14 @@
     return list(zip(refs, sizes))
 
 
-def first_kernel(moves, head_ref, tail_ref, *refs):
+def own_kernel(own_ref, mass_ref):
+    rows = mass_ref.shape[1]
+    own_ids = ids_of(own_ref)[:, :rows]
+    masses = mate_mass(own_ref[:rows, :], along_rows(own_ids), own_ref[:rows, :], own_ids, 0)
+    mass_ref[...] = jnp.sum(masses, axis=0, keepdims=True)
+
+
+def first_kernel(moves, own_mass_ref, head_ref, tail_ref, *refs):
     query_refs, (ids_ref, column_ref, sums_ref, mass_ref) = refs[:-4], refs[-4:]
     rows = mass_ref.shape[1]
     query_parts = query_parts_of(query_refs, rows)
@@ -180,13 +180,11 @@
     own_ids = ids_of(own_ref)[:, :rows]
     for m, ref in enumerate((*query_refs[:2], query_refs[3], query_refs[5])):
         ids_ref[pl.ds(m * rows, rows), :] = along_rows(ids_of(ref)[:, :rows])
-    mass = jnp.zeros((1, rows), jnp.float32)
-    first = 0
-    for ref, size in query_parts:
-        shift = first if first < rows else None
-        masses = mate_mass(
-            ref[:size, :], ids_ref[pl.ds(first, size), :], own_ref[:rows, :], own_ids, shift
-        )
+    mass = own_mass_ref[...]
+    first = rows
+    for ref, size in query_parts[1:]:
+        query_ids = ids_ref[pl.ds(first, size), :]
+        masses = mate_mass(ref[:size, :], query_ids, own_ref[:rows, :], own_ids)
         mass = mass + jnp.sum(masses, axis=0, keepdims=True)
         first += size
     mass_ref[...] = mass
@@ -197,38 +195,36 @@
 
 
 def middle_kernel(moves, head_ref, *refs):
-    query_refs, powers_ref = refs[:-1], refs[-1]
+    query_refs, (powers_ref, rest_ref) = refs[:-2], refs[-2:]
 
     @pl.when(arrived_at(moves))
     def _():
         keys = powers_ref.shape[1]
-        key_rows = padded(unit_rows(head_ref[...]), keys, 0.0)
+        units = unit_rows(head_ref[...])
+        rest_ref[...] = units[keys:]
         first = 0
-        for query_ref, size in query_parts_of(query_refs, keys):
+        for query_ref, size in query_parts_of(query_refs, query_refs[0].shape[0] - ID_ROWS):
             similar = lax.dot_general(
-                query_ref[:size, :], key_rows, (((1,), (1,)), ((), ())),
+                query_ref[:size, :], units[:keys], (((1,), (1,)), ((), ())),
                 preferred_element_type=jnp.float32,
             )
             powers_ref[pl.ds(first, size), :] = jnp.exp2(similar * INVERSE_TEMP_BITS)
             first += size
 
 
-def last_kernel(moves, powers_ref, tail_ref, ids_ref, earlier_ref, mass_ref, *refs):
+def last_kernel(moves, powers_ref, rest_ref, tail_ref, ids_ref, earlier_ref, mass_ref, *refs):
     query_refs, refs = refs[: -PLANE - 2], refs[-PLANE - 2 :]
     column_ref, row_refs, sums_ref = refs[0], refs[1:-1], refs[-1]
     rows = column_ref.shape[1]
+    cut = powers_ref.shape[1]
     arrived = arrived_at(moves)
 
     @pl.when(arrived)
     def _():
-        tail = tail_ref.shape[0] - ID_ROWS
-        keys = LANES * ((tail + LANES - 1) // LANES)
         key_ids = ids_of(tail_ref)[:, :rows]
-        head_ids = padded(key_ids[:, : rows - tail], rows, -1.0)
-        tail_ids = padded(key_ids[:, rows - tail :], keys, -1.0)
-        key_rows = padded(tail_ref[:tail, :], keys, 0.0)
-        head_column = jnp.zeros((1, rows), jnp.float32)
-        tail_column = jnp.zeros((1, keys), jnp.float32)
+        key_rows = jnp.concatenate([rest_ref[...], tail_ref[: tail_ref.shape[0] - ID_ROWS, :]], axis=0)
+        early_column = jnp.zeros((1, cut), jnp.float32)
+        late_column = jnp.zeros((1, rows - cut), jnp.float32)
         first = 0
         for query_ref, size in query_parts_of(query_refs, rows):
             part = pl.ds(first, size)
@@ -238,15 +234,13 @@
                 preferred_element_type=jnp.float32,
             )
             powers = jnp.exp2(similar * INVERSE_TEMP_BITS)
-            tail_part, column = add_masses(query_ids, tail_ids, powers)
-            tail_column = tail_column + column
-            head_part, column = add_masses(query_ids, head_ids, powers_ref[part, :])
-            head_column = head_column + column
-            sums_ref[part, :] = earlier_ref[part, :] + head_part + tail_part
+            late, column = add_masses(query_ids, key_ids[:, cut:], powers)
+            late_column = late_column + column
+            early, column = add_masses(query_ids, key_ids[:, :cut], powers_ref[part, :])
+            early_column = early_column + column
+            sums_ref[part, :] = earlier_ref[part, :] + early + late
             first += size
-        column_ref[...] = jnp.concatenate(
-            [head_column[:, : rows - tail], tail_column[:, :tail]], axis=1
-        )
+        column_ref[...] = jnp.concatenate([early_column, late_column], axis=1)
 
     @pl.when(jnp.logical_not(arrived))
     def _():
@@ -293,6 +287,10 @@
         cost_estimate=small,
         compiler_params=params,
     )(embeddings, cluster_ids.reshape(1, row_count))
+    own_mass = pl.pallas_call(
+        own_kernel, out_shape=vector, cost_estimate=small, compiler_params=params
+    )(block)
+    own_mass, tail = lax.optimization_barrier((own_mass, tail))
     first_tail = on_line(tail, first_moves)
     across = [in_plane(piece, 2) for piece in pieces]
     sibling = in_plane(block, 1)
@@ -304,11 +302,13 @@
         out_shape=(lanes, vector, lanes, vector),
         cost_estimate=small,
         compiler_params=params,
-    )(first_head, first_tail, *queries)
+    )(own_mass, first_head, first_tail, *queries)
     returned_first = on_line(first_column, first_back)
-    powers = pl.pallas_call(
+    powers, rest = pl.pallas_call(
         functools.partial(middle_kernel, last_moves),
-        out_shape=jax.ShapeDtypeStruct((plane_rows, row_count), jnp.float32),
+        out_shape=(
+            jax.ShapeDtypeStruct((plane_rows, half), jnp.float32), rows_of(part - half)
+        ),
         cost_estimate=small,
         compiler_params=params,
     )(last_head, *queries)
@@ -317,7 +317,7 @@
         out_shape=[vector] * (1 + PLANE),
         scratch_shapes=[pltpu.VMEM(lanes.shape, lanes.dtype)],
         compiler_params=params,
-    )(powers, last_tail, ids, first_sums, mass, *queries)
+    )(powers, rest, last_tail, ids, first_sums, mass, *queries)
     returned_first, row_sums[1] = lax.optimization_barrier((returned_first, row_sums[1]))
     returned = [on_line(last_column, last_back)]
     returned += [in_plane(row_sums[step], step) for step in (2, 3, 1)]

time: 35.8 us -> 35.7 us (level)
  waiting for transfers between devices: 16.9 us -> 16.5 us
    ppermute x6, waiting for transfers between devices: 13 us -> 12.6 us  [on_line(): return lax.ppermute(value, 'gx', pairs)]
  transfers between devices with their start and end apart: 14 -> 14, of which waited for: 6 -> 6; matrix products, arithmetic and copies ran while one was open for 0% -> 0% of each run, Pallas kernels for 7% -> 8%
where the time goes in v19:
time: 35.7 us; the launch traced here: 35.5 us
  waiting for transfers between devices  16.5 us (46%)
  starting transfers between devices  14.4 us (40%)
  Pallas kernels  2.79 us (8%)
  local copies, waits for them, and re-layouts  1.06 us (3%)
  other arithmetic  0.58 us (2%)
    ppermute x6, waiting for transfers between devices, on_line(): return lax.ppermute(value, 'gx', pairs)  12.6 us
    ppermute x6, starting transfers between devices, on_line(): return lax.ppermute(value, 'gx', pairs)  10.3 us
    ppermute x8, starting transfers between devices, in_plane(): return lax.ppermute(value, 'gx', [(i, i ^ step) for i in range(peers)])  4.09 us
    ppermute x8, waiting for transfers between devices, in_plane(): return lax.ppermute(value, 'gx', [(i, i ^ step) for i in range(peers)])  3.96 us
    pallas_call x1, Pallas kernels, grid_plan(): pl.pallas_call(functools.partial(first_kernel, first_moves), out_shape=(l...  2 us
    slice x1, local copies, waits for them, and re-layouts, grid_plan(): first_head = on_line(embeddings[:part], first_moves)  1.05 us
  transfers between devices with their start and end apart: 14, of which 6 were waited for; matrix products, arithmetic and copies ran while one was open for 0% of the time, Pallas kernels for 8%

profile of v19, /device:TPU:0, one launch (start us, length us, event | category | flops | bytes accessed | tf_op | source)
XLA Modules:
  0.0 35.5 jit_solution(15583455966433598647)
XLA Ops:
  0.0 0.0 copy-start
  0.0 1.1 %slice.3 = bf16[144,1024]{1,0:T(8,128)(2,1)S(1)} slice(bf16[256,1024]{1,0:T(8,128)(2,1)} %rows_ref.1), slice={[0:144], [0:1024]} | slice | bytes 589824 | tf_op jit(solution)/shard_map/slice | solution.py:283
  1.1 0.0 copy-start.1
  1.1 3.1 %collective-permute-start = (bf16[144,1024]{1,0:T(8,128)(2,1)S(1)}, bf16[144,1024]{1,0:T(8,128)(2,1)S(1)}, u32[]{:S(2)}, u32[]{:S(2)}) collective-permute-start(bf16[144,1024]{1,0:T(8,128)(2,1)S(1)} %slice.3), channel_id=1, source_target_pairs={{0,4},{1,5},{2,6},{3,7},{4,8},{5,9},{6,10},{7,11},{8,12},{9,13},{1... | collective-permute-start | bytes 884744 | tf_op jit(solution)/shard_map/ppermute | solution.py:272
  4.1 0.0 copy-done
  4.2 0.0 copy-done.1
  4.2 0.2 shard_map.28
  4.4 1.6 %collective-permute-start.4 = (bf16[136,1024]{1,0:T(8,128)(2,1)S(1)}, bf16[136,1024]{1,0:T(8,128)(2,1)S(1)}, u32[]{:S(2)}, u32[]{:S(2)}) collective-permute-start(bf16[136,1024]{1,0:T(8,128)(2,1)S(1)} %get-tuple-element.26), channel_id=1, source_target_pairs={{0,2},{1,3},{2,0},{3,1},{4,6},{5,7},{6,4},{7,5},{8,10},{9,11},{10,... | collective-permute-start | bytes 835592 | tf_op jit(solution)/shard_map/ppermute | solution.py:268
  5.9 0.0 collective-permute-start.2
  5.9 0.5 %collective-permute-start.3 = (bf16[128,1024]{1,0:T(8,128)(2,1)S(1)}, bf16[128,1024]{1,0:T(8,128)(2,1)S(1)}, u32[]{:S(2)}, u32[]{:S(2)}) collective-permute-start(bf16[128,1024]{1,0:T(8,128)(2,1)S(1)} %get-tuple-element.25), channel_id=1, source_target_pairs={{0,2},{1,3},{2,0},{3,1},{4,6},{5,7},{6,4},{7,5},{8,10},{9,11},{10,... | collective-permute-start | bytes 786440 | tf_op jit(solution)/shard_map/ppermute | solution.py:268
  6.4 0.4 shard_map.30.own_mass_ref
  6.8 1.6 %collective-permute-start.7 = (bf16[120,1024]{1,0:T(8,128)(2,1)S(1)}, bf16[120,1024]{1,0:T(8,128)(2,1)S(1)}, u32[]{:S(2)}, u32[]{:S(2)}) collective-permute-start(bf16[120,1024]{1,0:T(8,128)(2,1)S(1)} %get-tuple-element.30), channel_id=1, source_target_pairs={{0,4},{1,5},{2,6},{3,7},{4,8},{5,9},{6,10},{7,11},{8,12},{9,13},{1... | collective-permute-start | bytes 737288 | tf_op jit(solution)/shard_map/ppermute | solution.py:272
  8.4 5.6 %collective-permute-done.head_ref = bf16[144,1024]{1,0:T(8,128)(2,1)S(1)} collective-permute-done((bf16[144,1024]{1,0:T(8,128)(2,1)S(1)}, bf16[144,1024]{1,0:T(8,128)(2,1)S(1)}, u32[]{:S(2)}, u32[]{:S(2)}) %collective-permute-start) | collective-permute-done | bytes 294944 | tf_op jit(solution)/shard_map/ppermute | solution.py:272
  14.0 0.7 %collective-permute-start.1 = (bf16[144,1024]{1,0:T(8,128)(2,1)S(1)}, bf16[144,1024]{1,0:T(8,128)(2,1)S(1)}, u32[]{:S(2)}, u32[]{:S(2)}) collective-permute-start(bf16[144,1024]{1,0:T(8,128)(2,1)S(1)} %collective-permute-done.head_ref), channel_id=1, source_target_pairs={{4,8},{5,9},{6,10},{7,11},{8,12},{9,13},{10,14},{11,15},{20,24},{2... | collective-permute-start | bytes 884744 | tf_op jit(solution)/shard_map/ppermute | solution.py:272
  14.7 0.0 collective-permute-done.4.refs_3_
  14.7 0.1 collective-permute-start.6
  14.8 3.4 %collective-permute-done.3.refs_2_ = bf16[128,1024]{1,0:T(8,128)(2,1)S(1)} collective-permute-done((bf16[128,1024]{1,0:T(8,128)(2,1)S(1)}, bf16[128,1024]{1,0:T(8,128)(2,1)S(1)}, u32[]{:S(2)}, u32[]{:S(2)}) %collective-permute-start.3) | collective-permute-done | bytes 262176 | tf_op jit(solution)/shard_map/ppermute | solution.py:268
  18.2 0.0 collective-permute-start.5
  18.2 0.3 collective-permute-done.7.tail_ref
  18.4 0.7 %collective-permute-start.8 = (bf16[120,1024]{1,0:T(8,128)(2,1)S(1)}, bf16[120,1024]{1,0:T(8,128)(2,1)S(1)}, u32[]{:S(2)}, u32[]{:S(2)}) collective-permute-start(bf16[120,1024]{1,0:T(8,128)(2,1)S(1)} %collective-permute-done.7.tail_ref), channel_id=1, source_target_pairs={{4,8},{5,9},{6,10},{7,11},{8,12},{9,13},{10,14},{11,15},{20,24},{2... | collective-permute-start | bytes 737288 | tf_op jit(solution)/shard_map/ppermute | solution.py:272
  19.1 0.6 %collective-permute-done.5.refs_4_ = bf16[128,1024]{1,0:T(8,128)(2,1)S(1)} collective-permute-done((bf16[128,1024]{1,0:T(8,128)(2,1)S(1)}, bf16[128,1024]{1,0:T(8,128)(2,1)S(1)}, u32[]{:S(2)}, u32[]{:S(2)}) %collective-permute-start.5) | collective-permute-done | bytes 262176 | tf_op jit(solution)/shard_map/ppermute | solution.py:268
  19.7 0.0 collective-permute-done.2.refs_1_
  19.7 0.0 collective-permute-done.6.refs_5_
  19.7 2.0 %shard_map.31 = (f32[1024,128]{1,0:T(8,128)S(1)}, f32[1,256]{1,0:T(1,128)S(1)}, f32[1024,128]{1,0:T(8,128)S(1)}, f32[1,256]{1,0:T(1,128)S(1)}) custom-call(f32[1,256]{1,0:T(1,128)S(1)} %shard_map.30.own_mass_ref, bf16[144,1024]{1,0:T(8,128)(2,1)S(1)} %collective-permute-done.head_ref, bf16[120,1024]{1,0:T(8,128)(2,1)S(1)} %collective-permute-done.7.tail_ref, ...), custom_call_target="tpu_custom_call" | custom-call | flops 1 | bytes 1 | tf_op jit(solution)/shard_map/pallas_call | solution.py:300
  21.7 3.0 %collective-permute-start.9 = (f32[1,256]{1,0:T(1,128)S(1)}, f32[1,256]{1,0:T(1,128)S(1)}, u32[]{:S(2)}, u32[]{:S(2)}) collective-permute-start(f32[1,256]{1,0:T(1,128)S(1)} %get-tuple-element.36), channel_id=1, source_target_pairs={{4,0},{5,1},{6,2},{7,3},{8,4},{9,5},{10,6},{11,7},{12,8},{13,9},{1... | collective-permute-start | bytes 3080 | tf_op jit(solution)/shard_map/ppermute | solution.py:272
  24.7 0.0 collective-permute-done.1.head_ref
  24.7 0.0 collective-permute-done.8.tail_ref
  24.7 0.2 shard_map.32
  25.0 1.9 %collective-permute-done.9 = f32[1,256]{1,0:T(1,128)S(1)} collective-permute-done((f32[1,256]{1,0:T(1,128)S(1)}, f32[1,256]{1,0:T(1,128)S(1)}, u32[]{:S(2)}, u32[]{:S(2)}) %collective-permute-start.9) | collective-permute-done | bytes 1056 | tf_op jit(solution)/shard_map/ppermute | solution.py:272
  26.9 0.0 collective-permute-start.13
  26.9 1.3 %collective-permute-start.10 = (f32[1,256]{1,0:T(1,128)S(1)}, f32[1,256]{1,0:T(1,128)S(1)}, u32[]{:S(2)}, u32[]{:S(2)}) collective-permute-start(f32[1,256]{1,0:T(1,128)S(1)} %get-tuple-element.39), channel_id=1, source_target_pairs={{8,0},{9,1},{10,2},{11,3},{12,4},{13,5},{14,6},{15,7},{24,16},{25,... | collective-permute-start | bytes 3080 | tf_op jit(solution)/shard_map/ppermute | solution.py:272
  28.2 1.6 %collective-permute-start.11 = (f32[1,256]{1,0:T(1,128)S(1)}, f32[1,256]{1,0:T(1,128)S(1)}, u32[]{:S(2)}, u32[]{:S(2)}) collective-permute-start(f32[1,256]{1,0:T(1,128)S(1)} %get-tuple-element.40), channel_id=1, source_target_pairs={{0,2},{1,3},{2,0},{3,1},{4,6},{5,7},{6,4},{7,5},{8,10},{9,11},{10,... | collective-permute-start | bytes 3080 | tf_op jit(solution)/shard_map/ppermute | solution.py:268
  29.7 0.4 %collective-permute-start.12 = (f32[1,256]{1,0:T(1,128)S(1)}, f32[1,256]{1,0:T(1,128)S(1)}, u32[]{:S(2)}, u32[]{:S(2)}) collective-permute-start(f32[1,256]{1,0:T(1,128)S(1)} %get-tuple-element.41), channel_id=1, source_target_pairs={{0,3},{1,2},{2,1},{3,0},{4,7},{5,6},{6,5},{7,4},{8,11},{9,10},{10,... | collective-permute-start | bytes 3080 | tf_op jit(solution)/shard_map/ppermute | solution.py:268
  30.1 0.0 collective-permute-done.13
  30.1 4.8 %collective-permute-done.10 = f32[1,256]{1,0:T(1,128)S(1)} collective-permute-done((f32[1,256]{1,0:T(1,128)S(1)}, f32[1,256]{1,0:T(1,128)S(1)}, u32[]{:S(2)}, u32[]{:S(2)}) %collective-permute-start.10) | collective-permute-done | bytes 1056 | tf_op jit(solution)/shard_map/ppermute | solution.py:272
  34.9 0.0 collective-permute-done.11
  34.9 0.0 collective-permute-done.12
  34.9 0.6 %add_log-plus-one_fusion = f32[1,256]{1,0:T(1,128)} fusion(f32[1,256]{1,0:T(1,128)S(1)} %collective-permute-done.13, f32[1,256]{1,0:T(1,128)S(1)} %collective-permute-done.12, f32[1,256]{1,0:T(1,128)S(1)} %collective-permute-done.11, f32[1,256]{1,0:T(1,128)S(1)} %collective-permute-done.10, f32[1,256]{1,0:T(1,128)S(1)} %get-tuple-element.35, ...), kind=kLoop, calls=%fused_computation | loop fusion | flops 1280 | bytes 7168 | tf_op jit(solution)/shard_map/log1p | solution.py:324
  (1 shorter events, 0.0 us)
Async XLA Ops:
  0.0 4.1 %copy-start = (bf16[256,1024]{1,0:T(8,128)(2,1)S(1)}, bf16[256,1024]{1,0:T(8,128)(2,1)}, u32[]{:S(2)}) copy-start(bf16[256,1024]{1,0:T(8,128)(2,1)} %rows_ref.1) | copy-start | bytes 1572868
  1.1 3.1 %copy-start.1 = (s32[256]{0:T(256)S(1)}, s32[256]{0:T(256)}, u32[]{:S(2)}) copy-start(s32[256]{0:T(256)} %param.3) | copy-start | bytes 3076
  1.1 12.9 %collective-permute-start = (bf16[144,1024]{1,0:T(8,128)(2,1)S(1)}, bf16[144,1024]{1,0:T(8,128)(2,1)S(1)}, u32[]{:S(2)}, u32[]{:S(2)}) collective-permute-start(bf16[144,1024]{1,0:T(8,128)(2,1)S(1)} %slice.3), channel_id=1, source_target_pairs={{0,4},{1,5},{2,6},{3,7},{4,8},{5,9},{6,10},{7,11},{8,12},{9,13},{1... | collective-permute-start | bytes 884744 | tf_op jit(solution)/shard_map/ppermute | solution.py:272
  4.4 10.3 %collective-permute-start.4 = (bf16[136,1024]{1,0:T(8,128)(2,1)S(1)}, bf16[136,1024]{1,0:T(8,128)(2,1)S(1)}, u32[]{:S(2)}, u32[]{:S(2)}) collective-permute-start(bf16[136,1024]{1,0:T(8,128)(2,1)S(1)} %get-tuple-element.26), channel_id=1, source_target_pairs={{0,2},{1,3},{2,0},{3,1},{4,6},{5,7},{6,4},{7,5},{8,10},{9,11},{10,... | collective-permute-start | bytes 835592 | tf_op jit(solution)/shard_map/ppermute | solution.py:268
  5.9 13.8 %collective-permute-start.2 = (bf16[264,1024]{1,0:T(8,128)(2,1)S(1)}, bf16[264,1024]{1,0:T(8,128)(2,1)S(1)}, u32[]{:S(2)}, u32[]{:S(2)}) collective-permute-start(bf16[264,1024]{1,0:T(8,128)(2,1)S(1)} %get-tuple-element.24.refs_0_.own_ref), channel_id=1, source_target_pairs={{0,1},{1,0},{2,3},{3,2},{4,5},{5,4},{6,7},{7,6},{8,9},{9,8},{10,11... | collective-permute-start | bytes 1622024 | tf_op jit(solution)/shard_map/ppermute | solution.py:268
  5.9 12.2 %collective-permute-start.3 = (bf16[128,1024]{1,0:T(8,128)(2,1)S(1)}, bf16[128,1024]{1,0:T(8,128)(2,1)S(1)}, u32[]{:S(2)}, u32[]{:S(2)}) collective-permute-start(bf16[128,1024]{1,0:T(8,128)(2,1)S(1)} %get-tuple-element.25), channel_id=1, source_target_pairs={{0,2},{1,3},{2,0},{3,1},{4,6},{5,7},{6,4},{7,5},{8,10},{9,11},{10,... | collective-permute-start | bytes 786440 | tf_op jit(solution)/shard_map/ppermute | solution.py:268
  6.8 11.6 %collective-permute-start.7 = (bf16[120,1024]{1,0:T(8,128)(2,1)S(1)}, bf16[120,1024]{1,0:T(8,128)(2,1)S(1)}, u32[]{:S(2)}, u32[]{:S(2)}) collective-permute-start(bf16[120,1024]{1,0:T(8,128)(2,1)S(1)} %get-tuple-element.30), channel_id=1, source_target_pairs={{0,4},{1,5},{2,6},{3,7},{4,8},{5,9},{6,10},{7,11},{8,12},{9,13},{1... | collective-permute-start | bytes 737288 | tf_op jit(solution)/shard_map/ppermute | solution.py:272
  14.0 10.7 %collective-permute-start.1 = (bf16[144,1024]{1,0:T(8,128)(2,1)S(1)}, bf16[144,1024]{1,0:T(8,128)(2,1)S(1)}, u32[]{:S(2)}, u32[]{:S(2)}) collective-permute-start(bf16[144,1024]{1,0:T(8,128)(2,1)S(1)} %collective-permute-done.head_ref), channel_id=1, source_target_pairs={{4,8},{5,9},{6,10},{7,11},{8,12},{9,13},{10,14},{11,15},{20,24},{2... | collective-permute-start | bytes 884744 | tf_op jit(solution)/shard_map/ppermute | solution.py:272
  14.7 5.0 %collective-permute-start.6 = (bf16[136,1024]{1,0:T(8,128)(2,1)S(1)}, bf16[136,1024]{1,0:T(8,128)(2,1)S(1)}, u32[]{:S(2)}, u32[]{:S(2)}) collective-permute-start(bf16[136,1024]{1,0:T(8,128)(2,1)S(1)} %collective-permute-done.4.refs_3_), channel_id=1, source_target_pairs={{0,1},{1,0},{2,3},{3,2},{4,5},{5,4},{6,7},{7,6},{8,9},{9,8},{10,11... | collective-permute-start | bytes 835592 | tf_op jit(solution)/shard_map/ppermute | solution.py:268
  18.2 1.5 %collective-permute-start.5 = (bf16[128,1024]{1,0:T(8,128)(2,1)S(1)}, bf16[128,1024]{1,0:T(8,128)(2,1)S(1)}, u32[]{:S(2)}, u32[]{:S(2)}) collective-permute-start(bf16[128,1024]{1,0:T(8,128)(2,1)S(1)} %collective-permute-done.3.refs_2_), channel_id=1, source_target_pairs={{0,1},{1,0},{2,3},{3,2},{4,5},{5,4},{6,7},{7,6},{8,9},{9,8},{10,11... | collective-permute-start | bytes 786440 | tf_op jit(solution)/shard_map/ppermute | solution.py:268
  18.4 6.3 %collective-permute-start.8 = (bf16[120,1024]{1,0:T(8,128)(2,1)S(1)}, bf16[120,1024]{1,0:T(8,128)(2,1)S(1)}, u32[]{:S(2)}, u32[]{:S(2)}) collective-permute-start(bf16[120,1024]{1,0:T(8,128)(2,1)S(1)} %collective-permute-done.7.tail_ref), channel_id=1, source_target_pairs={{4,8},{5,9},{6,10},{7,11},{8,12},{9,13},{10,14},{11,15},{20,24},{2... | collective-permute-start | bytes 737288 | tf_op jit(solution)/shard_map/ppermute | solution.py:272
  21.7 5.2 %collective-permute-start.9 = (f32[1,256]{1,0:T(1,128)S(1)}, f32[1,256]{1,0:T(1,128)S(1)}, u32[]{:S(2)}, u32[]{:S(2)}) collective-permute-start(f32[1,256]{1,0:T(1,128)S(1)} %get-tuple-element.36), channel_id=1, source_target_pairs={{4,0},{5,1},{6,2},{7,3},{8,4},{9,5},{10,6},{11,7},{12,8},{13,9},{1... | collective-permute-start | bytes 3080 | tf_op jit(solution)/shard_map/ppermute | solution.py:272
  26.9 3.2 %collective-permute-start.13 = (f32[1,256]{1,0:T(1,128)S(1)}, f32[1,256]{1,0:T(1,128)S(1)}, u32[]{:S(2)}, u32[]{:S(2)}) collective-permute-start(f32[1,256]{1,0:T(1,128)S(1)} %get-tuple-element.42), channel_id=1, source_target_pairs={{0,1},{1,0},{2,3},{3,2},{4,5},{5,4},{6,7},{7,6},{8,9},{9,8},{10,11... | collective-permute-start | bytes 3080 | tf_op jit(solution)/shard_map/ppermute | solution.py:268
  26.9 8.0 %collective-permute-start.10 = (f32[1,256]{1,0:T(1,128)S(1)}, f32[1,256]{1,0:T(1,128)S(1)}, u32[]{:S(2)}, u32[]{:S(2)}) collective-permute-start(f32[1,256]{1,0:T(1,128)S(1)} %get-tuple-element.39), channel_id=1, source_target_pairs={{8,0},{9,1},{10,2},{11,3},{12,4},{13,5},{14,6},{15,7},{24,16},{25,... | collective-permute-start | bytes 3080 | tf_op jit(solution)/shard_map/ppermute | solution.py:272
  28.2 6.7 %collective-permute-start.11 = (f32[1,256]{1,0:T(1,128)S(1)}, f32[1,256]{1,0:T(1,128)S(1)}, u32[]{:S(2)}, u32[]{:S(2)}) collective-permute-start(f32[1,256]{1,0:T(1,128)S(1)} %get-tuple-element.40), channel_id=1, source_target_pairs={{0,2},{1,3},{2,0},{3,1},{4,6},{5,7},{6,4},{7,5},{8,10},{9,11},{10,... | collective-permute-start | bytes 3080 | tf_op jit(solution)/shard_map/ppermute | solution.py:268
  29.7 5.2 %collective-permute-start.12 = (f32[1,256]{1,0:T(1,128)S(1)}, f32[1,256]{1,0:T(1,128)S(1)}, u32[]{:S(2)}, u32[]{:S(2)}) collective-permute-start(f32[1,256]{1,0:T(1,128)S(1)} %get-tuple-element.41), channel_id=1, source_target_pairs={{0,3},{1,2},{2,1},{3,0},{4,7},{5,6},{6,5},{7,4},{8,11},{9,10},{10,... | collective-permute-start | bytes 3080 | tf_op jit(solution)/shard_map/ppermute | solution.py:268

commit v20 on v19

--- a/solution.py
+++ b/solution.py
@@ -294,7 +294,8 @@
     first_tail = on_line(tail, first_moves)
     across = [in_plane(piece, 2) for piece in pieces]
     sibling = in_plane(block, 1)
-    last_head, last_tail = [on_line(got, forward_moves) for got in (first_head, first_tail)]
+    last_head = on_line(first_head, forward_moves + [(3, 1), (0, 0)])
+    last_tail = on_line(first_tail, forward_moves)
     corner = [in_plane(piece, 1) for piece in across]
     queries = (block, sibling, *across, *corner)
     ids, first_column, first_sums, mass = pl.pallas_call(

time: 35.7 us -> 35.7 us (level)
    ppermute x6, waiting for transfers between devices: 12.6 us -> 13.4 us  [on_line(): return lax.ppermute(value, 'gx', pairs)]
    ppermute x8, waiting for transfers between devices: 3.96 us -> 3.4 us  [in_plane(): return lax.ppermute(value, 'gx', [(i, i ^ step) for i in range(peers)])]
  transfers between devices with their start and end apart: 14 -> 14, of which waited for: 6 -> 5; matrix products, arithmetic and copies ran while one was open for 0% -> 0% of each run, Pallas kernels for 8% -> 8%
where the time goes in v20:
time: 35.7 us; the launch traced here: 35.5 us
  waiting for transfers between devices  16.8 us (47%)
  starting transfers between devices  14.1 us (39%)
  Pallas kernels  2.8 us (8%)
  local copies, waits for them, and re-layouts  1.06 us (3%)
  other arithmetic  0.58 us (2%)
    ppermute x6, waiting for transfers between devices, on_line(): return lax.ppermute(value, 'gx', pairs)  13.4 us
    ppermute x6, starting transfers between devices, on_line(): return lax.ppermute(value, 'gx', pairs)  10 us
    ppermute x8, starting transfers between devices, in_plane(): return lax.ppermute(value, 'gx', [(i, i ^ step) for i in range(peers)])  4.09 us
    ppermute x8, waiting for transfers between devices, in_plane(): return lax.ppermute(value, 'gx', [(i, i ^ step) for i in range(peers)])  3.4 us
    pallas_call x1, Pallas kernels, grid_plan(): pl.pallas_call(functools.partial(first_kernel, first_moves), out_shape=(l...  2.01 us
    slice x1, local copies, waits for them, and re-layouts, grid_plan(): first_head = on_line(embeddings[:part], first_moves)  1.05 us
  transfers between devices with their start and end apart: 14, of which 5 were waited for; matrix products, arithmetic and copies ran while one was open for 0% of the time, Pallas kernels for 8%

profile of v20, /device:TPU:0, one launch (start us, length us, event | category | flops | bytes accessed | tf_op | source)
XLA Modules:
  0.0 35.5 jit_solution(5360215254676636643)
XLA Ops:
  0.0 0.0 copy-start
  0.0 1.1 %slice.3 = bf16[144,1024]{1,0:T(8,128)(2,1)S(1)} slice(bf16[256,1024]{1,0:T(8,128)(2,1)} %rows_ref.1), slice={[0:144], [0:1024]} | slice | bytes 589824 | tf_op jit(solution)/shard_map/slice | solution.py:283
  1.1 0.0 copy-start.1
  1.1 3.1 %collective-permute-start = (bf16[144,1024]{1,0:T(8,128)(2,1)S(1)}, bf16[144,1024]{1,0:T(8,128)(2,1)S(1)}, u32[]{:S(2)}, u32[]{:S(2)}) collective-permute-start(bf16[144,1024]{1,0:T(8,128)(2,1)S(1)} %slice.3), channel_id=1, source_target_pairs={{0,4},{1,5},{2,6},{3,7},{4,8},{5,9},{6,10},{7,11},{8,12},{9,13},{1... | collective-permute-start | bytes 884744 | tf_op jit(solution)/shard_map/ppermute | solution.py:272
  4.1 0.0 copy-done
  4.2 0.0 copy-done.1
  4.2 0.2 shard_map.28
  4.4 1.6 %collective-permute-start.4 = (bf16[136,1024]{1,0:T(8,128)(2,1)S(1)}, bf16[136,1024]{1,0:T(8,128)(2,1)S(1)}, u32[]{:S(2)}, u32[]{:S(2)}) collective-permute-start(bf16[136,1024]{1,0:T(8,128)(2,1)S(1)} %get-tuple-element.26), channel_id=1, source_target_pairs={{0,2},{1,3},{2,0},{3,1},{4,6},{5,7},{6,4},{7,5},{8,10},{9,11},{10,... | collective-permute-start | bytes 835592 | tf_op jit(solution)/shard_map/ppermute | solution.py:268
  5.9 0.0 collective-permute-start.2
  5.9 0.5 %collective-permute-start.3 = (bf16[128,1024]{1,0:T(8,128)(2,1)S(1)}, bf16[128,1024]{1,0:T(8,128)(2,1)S(1)}, u32[]{:S(2)}, u32[]{:S(2)}) collective-permute-start(bf16[128,1024]{1,0:T(8,128)(2,1)S(1)} %get-tuple-element.25), channel_id=1, source_target_pairs={{0,2},{1,3},{2,0},{3,1},{4,6},{5,7},{6,4},{7,5},{8,10},{9,11},{10,... | collective-permute-start | bytes 786440 | tf_op jit(solution)/shard_map/ppermute | solution.py:268
  6.4 0.4 shard_map.30.own_mass_ref
  6.8 1.6 %collective-permute-start.7 = (bf16[120,1024]{1,0:T(8,128)(2,1)S(1)}, bf16[120,1024]{1,0:T(8,128)(2,1)S(1)}, u32[]{:S(2)}, u32[]{:S(2)}) collective-permute-start(bf16[120,1024]{1,0:T(8,128)(2,1)S(1)} %get-tuple-element.30), channel_id=1, source_target_pairs={{0,4},{1,5},{2,6},{3,7},{4,8},{5,9},{6,10},{7,11},{8,12},{9,13},{1... | collective-permute-start | bytes 737288 | tf_op jit(solution)/shard_map/ppermute | solution.py:272
  8.4 5.6 %collective-permute-done.head_ref = bf16[144,1024]{1,0:T(8,128)(2,1)S(1)} collective-permute-done((bf16[144,1024]{1,0:T(8,128)(2,1)S(1)}, bf16[144,1024]{1,0:T(8,128)(2,1)S(1)}, u32[]{:S(2)}, u32[]{:S(2)}) %collective-permute-start) | collective-permute-done | bytes 294944 | tf_op jit(solution)/shard_map/ppermute | solution.py:272
  14.0 0.7 %collective-permute-start.1 = (bf16[144,1024]{1,0:T(8,128)(2,1)S(1)}, bf16[144,1024]{1,0:T(8,128)(2,1)S(1)}, u32[]{:S(2)}, u32[]{:S(2)}) collective-permute-start(bf16[144,1024]{1,0:T(8,128)(2,1)S(1)} %collective-permute-done.head_ref), channel_id=1, source_target_pairs={{4,8},{5,9},{6,10},{7,11},{8,12},{9,13},{10,14},{11,15},{12,4},{13... | collective-permute-start | bytes 884744 | tf_op jit(solution)/shard_map/ppermute | solution.py:272
  14.7 0.0 collective-permute-done.4.refs_3_
  14.7 0.1 collective-permute-start.6
  14.8 3.4 %collective-permute-done.3.refs_2_ = bf16[128,1024]{1,0:T(8,128)(2,1)S(1)} collective-permute-done((bf16[128,1024]{1,0:T(8,128)(2,1)S(1)}, bf16[128,1024]{1,0:T(8,128)(2,1)S(1)}, u32[]{:S(2)}, u32[]{:S(2)}) %collective-permute-start.3) | collective-permute-done | bytes 262176 | tf_op jit(solution)/shard_map/ppermute | solution.py:268
  18.2 0.0 collective-permute-start.5
  18.2 1.1 %collective-permute-done.7.tail_ref = bf16[120,1024]{1,0:T(8,128)(2,1)S(1)} collective-permute-done((bf16[120,1024]{1,0:T(8,128)(2,1)S(1)}, bf16[120,1024]{1,0:T(8,128)(2,1)S(1)}, u32[]{:S(2)}, u32[]{:S(2)}) %collective-permute-start.7) | collective-permute-done | bytes 245792 | tf_op jit(solution)/shard_map/ppermute | solution.py:272
  19.3 0.7 %collective-permute-start.8 = (bf16[120,1024]{1,0:T(8,128)(2,1)S(1)}, bf16[120,1024]{1,0:T(8,128)(2,1)S(1)}, u32[]{:S(2)}, u32[]{:S(2)}) collective-permute-start(bf16[120,1024]{1,0:T(8,128)(2,1)S(1)} %collective-permute-done.7.tail_ref), channel_id=1, source_target_pairs={{4,8},{5,9},{6,10},{7,11},{8,12},{9,13},{10,14},{11,15},{20,24},{2... | collective-permute-start | bytes 737288 | tf_op jit(solution)/shard_map/ppermute | solution.py:272
  19.9 0.0 collective-permute-done.5.refs_4_
  20.0 0.0 collective-permute-done.2.refs_1_
  20.0 0.0 collective-permute-done.6.refs_5_
  20.0 2.0 %shard_map.31 = (f32[1024,128]{1,0:T(8,128)S(1)}, f32[1,256]{1,0:T(1,128)S(1)}, f32[1024,128]{1,0:T(8,128)S(1)}, f32[1,256]{1,0:T(1,128)S(1)}) custom-call(f32[1,256]{1,0:T(1,128)S(1)} %shard_map.30.own_mass_ref, bf16[144,1024]{1,0:T(8,128)(2,1)S(1)} %collective-permute-done.head_ref, bf16[120,1024]{1,0:T(8,128)(2,1)S(1)} %collective-permute-done.7.tail_ref, ...), custom_call_target="tpu_custom_call" | custom-call | flops 1 | bytes 1 | tf_op jit(solution)/shard_map/pallas_call | solution.py:301
  22.0 2.7 %collective-permute-start.9 = (f32[1,256]{1,0:T(1,128)S(1)}, f32[1,256]{1,0:T(1,128)S(1)}, u32[]{:S(2)}, u32[]{:S(2)}) collective-permute-start(f32[1,256]{1,0:T(1,128)S(1)} %get-tuple-element.36), channel_id=1, source_target_pairs={{4,0},{5,1},{6,2},{7,3},{8,4},{9,5},{10,6},{11,7},{12,8},{13,9},{1... | collective-permute-start | bytes 3080 | tf_op jit(solution)/shard_map/ppermute | solution.py:272
  24.7 0.0 collective-permute-done.1.head_ref
  24.7 0.0 collective-permute-done.8.tail_ref
  24.7 0.2 shard_map.32
  25.0 1.9 %collective-permute-done.9 = f32[1,256]{1,0:T(1,128)S(1)} collective-permute-done((f32[1,256]{1,0:T(1,128)S(1)}, f32[1,256]{1,0:T(1,128)S(1)}, u32[]{:S(2)}, u32[]{:S(2)}) %collective-permute-start.9) | collective-permute-done | bytes 1056 | tf_op jit(solution)/shard_map/ppermute | solution.py:272
  26.9 0.0 collective-permute-start.13
  26.9 1.3 %collective-permute-start.10 = (f32[1,256]{1,0:T(1,128)S(1)}, f32[1,256]{1,0:T(1,128)S(1)}, u32[]{:S(2)}, u32[]{:S(2)}) collective-permute-start(f32[1,256]{1,0:T(1,128)S(1)} %get-tuple-element.39), channel_id=1, source_target_pairs={{8,0},{9,1},{10,2},{11,3},{12,4},{13,5},{14,6},{15,7},{24,16},{25,... | collective-permute-start | bytes 3080 | tf_op jit(solution)/shard_map/ppermute | solution.py:272
  28.2 1.6 %collective-permute-start.11 = (f32[1,256]{1,0:T(1,128)S(1)}, f32[1,256]{1,0:T(1,128)S(1)}, u32[]{:S(2)}, u32[]{:S(2)}) collective-permute-start(f32[1,256]{1,0:T(1,128)S(1)} %get-tuple-element.40), channel_id=1, source_target_pairs={{0,2},{1,3},{2,0},{3,1},{4,6},{5,7},{6,4},{7,5},{8,10},{9,11},{10,... | collective-permute-start | bytes 3080 | tf_op jit(solution)/shard_map/ppermute | solution.py:268
  29.7 0.4 %collective-permute-start.12 = (f32[1,256]{1,0:T(1,128)S(1)}, f32[1,256]{1,0:T(1,128)S(1)}, u32[]{:S(2)}, u32[]{:S(2)}) collective-permute-start(f32[1,256]{1,0:T(1,128)S(1)} %get-tuple-element.41), channel_id=1, source_target_pairs={{0,3},{1,2},{2,1},{3,0},{4,7},{5,6},{6,5},{7,4},{8,11},{9,10},{10,... | collective-permute-start | bytes 3080 | tf_op jit(solution)/shard_map/ppermute | solution.py:268
  30.1 0.0 collective-permute-done.13
  30.1 4.8 %collective-permute-done.10 = f32[1,256]{1,0:T(1,128)S(1)} collective-permute-done((f32[1,256]{1,0:T(1,128)S(1)}, f32[1,256]{1,0:T(1,128)S(1)}, u32[]{:S(2)}, u32[]{:S(2)}) %collective-permute-start.10) | collective-permute-done | bytes 1056 | tf_op jit(solution)/shard_map/ppermute | solution.py:272
  34.9 0.0 collective-permute-done.11
  34.9 0.0 collective-permute-done.12
  34.9 0.6 %add_log-plus-one_fusion = f32[1,256]{1,0:T(1,128)} fusion(f32[1,256]{1,0:T(1,128)S(1)} %collective-permute-done.13, f32[1,256]{1,0:T(1,128)S(1)} %collective-permute-done.12, f32[1,256]{1,0:T(1,128)S(1)} %collective-permute-done.11, f32[1,256]{1,0:T(1,128)S(1)} %collective-permute-done.10, f32[1,256]{1,0:T(1,128)S(1)} %get-tuple-element.35, ...), kind=kLoop, calls=%fused_computation | loop fusion | flops 1280 | bytes 7168 | tf_op jit(solution)/shard_map/log1p | solution.py:325
  (1 shorter events, 0.0 us)
Async XLA Ops:
  0.0 4.1 %copy-start = (bf16[256,1024]{1,0:T(8,128)(2,1)S(1)}, bf16[256,1024]{1,0:T(8,128)(2,1)}, u32[]{:S(2)}) copy-start(bf16[256,1024]{1,0:T(8,128)(2,1)} %rows_ref.1) | copy-start | bytes 1572868
  1.1 3.1 %copy-start.1 = (s32[256]{0:T(256)S(1)}, s32[256]{0:T(256)}, u32[]{:S(2)}) copy-start(s32[256]{0:T(256)} %param.3) | copy-start | bytes 3076
  1.1 12.9 %collective-permute-start = (bf16[144,1024]{1,0:T(8,128)(2,1)S(1)}, bf16[144,1024]{1,0:T(8,128)(2,1)S(1)}, u32[]{:S(2)}, u32[]{:S(2)}) collective-permute-start(bf16[144,1024]{1,0:T(8,128)(2,1)S(1)} %slice.3), channel_id=1, source_target_pairs={{0,4},{1,5},{2,6},{3,7},{4,8},{5,9},{6,10},{7,11},{8,12},{9,13},{1... | collective-permute-start | bytes 884744 | tf_op jit(solution)/shard_map/ppermute | solution.py:272
  4.4 10.3 %collective-permute-start.4 = (bf16[136,1024]{1,0:T(8,128)(2,1)S(1)}, bf16[136,1024]{1,0:T(8,128)(2,1)S(1)}, u32[]{:S(2)}, u32[]{:S(2)}) collective-permute-start(bf16[136,1024]{1,0:T(8,128)(2,1)S(1)} %get-tuple-element.26), channel_id=1, source_target_pairs={{0,2},{1,3},{2,0},{3,1},{4,6},{5,7},{6,4},{7,5},{8,10},{9,11},{10,... | collective-permute-start | bytes 835592 | tf_op jit(solution)/shard_map/ppermute | solution.py:268
  5.9 14.1 %collective-permute-start.2 = (bf16[264,1024]{1,0:T(8,128)(2,1)S(1)}, bf16[264,1024]{1,0:T(8,128)(2,1)S(1)}, u32[]{:S(2)}, u32[]{:S(2)}) collective-permute-start(bf16[264,1024]{1,0:T(8,128)(2,1)S(1)} %get-tuple-element.24.refs_0_.own_ref), channel_id=1, source_target_pairs={{0,1},{1,0},{2,3},{3,2},{4,5},{5,4},{6,7},{7,6},{8,9},{9,8},{10,11... | collective-permute-start | bytes 1622024 | tf_op jit(solution)/shard_map/ppermute | solution.py:268
  5.9 12.2 %collective-permute-start.3 = (bf16[128,1024]{1,0:T(8,128)(2,1)S(1)}, bf16[128,1024]{1,0:T(8,128)(2,1)S(1)}, u32[]{:S(2)}, u32[]{:S(2)}) collective-permute-start(bf16[128,1024]{1,0:T(8,128)(2,1)S(1)} %get-tuple-element.25), channel_id=1, source_target_pairs={{0,2},{1,3},{2,0},{3,1},{4,6},{5,7},{6,4},{7,5},{8,10},{9,11},{10,... | collective-permute-start | bytes 786440 | tf_op jit(solution)/shard_map/ppermute | solution.py:268
  6.8 12.5 %collective-permute-start.7 = (bf16[120,1024]{1,0:T(8,128)(2,1)S(1)}, bf16[120,1024]{1,0:T(8,128)(2,1)S(1)}, u32[]{:S(2)}, u32[]{:S(2)}) collective-permute-start(bf16[120,1024]{1,0:T(8,128)(2,1)S(1)} %get-tuple-element.30), channel_id=1, source_target_pairs={{0,4},{1,5},{2,6},{3,7},{4,8},{5,9},{6,10},{7,11},{8,12},{9,13},{1... | collective-permute-start | bytes 737288 | tf_op jit(solution)/shard_map/ppermute | solution.py:272
  14.0 10.7 %collective-permute-start.1 = (bf16[144,1024]{1,0:T(8,128)(2,1)S(1)}, bf16[144,1024]{1,0:T(8,128)(2,1)S(1)}, u32[]{:S(2)}, u32[]{:S(2)}) collective-permute-start(bf16[144,1024]{1,0:T(8,128)(2,1)S(1)} %collective-permute-done.head_ref), channel_id=1, source_target_pairs={{4,8},{5,9},{6,10},{7,11},{8,12},{9,13},{10,14},{11,15},{12,4},{13... | collective-permute-start | bytes 884744 | tf_op jit(solution)/shard_map/ppermute | solution.py:272
  14.7 5.3 %collective-permute-start.6 = (bf16[136,1024]{1,0:T(8,128)(2,1)S(1)}, bf16[136,1024]{1,0:T(8,128)(2,1)S(1)}, u32[]{:S(2)}, u32[]{:S(2)}) collective-permute-start(bf16[136,1024]{1,0:T(8,128)(2,1)S(1)} %collective-permute-done.4.refs_3_), channel_id=1, source_target_pairs={{0,1},{1,0},{2,3},{3,2},{4,5},{5,4},{6,7},{7,6},{8,9},{9,8},{10,11... | collective-permute-start | bytes 835592 | tf_op jit(solution)/shard_map/ppermute | solution.py:268
  18.2 1.8 %collective-permute-start.5 = (bf16[128,1024]{1,0:T(8,128)(2,1)S(1)}, bf16[128,1024]{1,0:T(8,128)(2,1)S(1)}, u32[]{:S(2)}, u32[]{:S(2)}) collective-permute-start(bf16[128,1024]{1,0:T(8,128)(2,1)S(1)} %collective-permute-done.3.refs_2_), channel_id=1, source_target_pairs={{0,1},{1,0},{2,3},{3,2},{4,5},{5,4},{6,7},{7,6},{8,9},{9,8},{10,11... | collective-permute-start | bytes 786440 | tf_op jit(solution)/shard_map/ppermute | solution.py:268
  19.3 5.5 %collective-permute-start.8 = (bf16[120,1024]{1,0:T(8,128)(2,1)S(1)}, bf16[120,1024]{1,0:T(8,128)(2,1)S(1)}, u32[]{:S(2)}, u32[]{:S(2)}) collective-permute-start(bf16[120,1024]{1,0:T(8,128)(2,1)S(1)} %collective-permute-done.7.tail_ref), channel_id=1, source_target_pairs={{4,8},{5,9},{6,10},{7,11},{8,12},{9,13},{10,14},{11,15},{20,24},{2... | collective-permute-start | bytes 737288 | tf_op jit(solution)/shard_map/ppermute | solution.py:272
  22.0 4.9 %collective-permute-start.9 = (f32[1,256]{1,0:T(1,128)S(1)}, f32[1,256]{1,0:T(1,128)S(1)}, u32[]{:S(2)}, u32[]{:S(2)}) collective-permute-start(f32[1,256]{1,0:T(1,128)S(1)} %get-tuple-element.36), channel_id=1, source_target_pairs={{4,0},{5,1},{6,2},{7,3},{8,4},{9,5},{10,6},{11,7},{12,8},{13,9},{1... | collective-permute-start | bytes 3080 | tf_op jit(solution)/shard_map/ppermute | solution.py:272
  26.9 3.2 %collective-permute-start.13 = (f32[1,256]{1,0:T(1,128)S(1)}, f32[1,256]{1,0:T(1,128)S(1)}, u32[]{:S(2)}, u32[]{:S(2)}) collective-permute-start(f32[1,256]{1,0:T(1,128)S(1)} %get-tuple-element.42), channel_id=1, source_target_pairs={{0,1},{1,0},{2,3},{3,2},{4,5},{5,4},{6,7},{7,6},{8,9},{9,8},{10,11... | collective-permute-start | bytes 3080 | tf_op jit(solution)/shard_map/ppermute | solution.py:268
  26.9 8.0 %collective-permute-start.10 = (f32[1,256]{1,0:T(1,128)S(1)}, f32[1,256]{1,0:T(1,128)S(1)}, u32[]{:S(2)}, u32[]{:S(2)}) collective-permute-start(f32[1,256]{1,0:T(1,128)S(1)} %get-tuple-element.39), channel_id=1, source_target_pairs={{8,0},{9,1},{10,2},{11,3},{12,4},{13,5},{14,6},{15,7},{24,16},{25,... | collective-permute-start | bytes 3080 | tf_op jit(solution)/shard_map/ppermute | solution.py:272
  28.2 6.7 %collective-permute-start.11 = (f32[1,256]{1,0:T(1,128)S(1)}, f32[1,256]{1,0:T(1,128)S(1)}, u32[]{:S(2)}, u32[]{:S(2)}) collective-permute-start(f32[1,256]{1,0:T(1,128)S(1)} %get-tuple-element.40), channel_id=1, source_target_pairs={{0,2},{1,3},{2,0},{3,1},{4,6},{5,7},{6,4},{7,5},{8,10},{9,11},{10,... | collective-permute-start | bytes 3080 | tf_op jit(solution)/shard_map/ppermute | solution.py:268
  29.7 5.2 %collective-permute-start.12 = (f32[1,256]{1,0:T(1,128)S(1)}, f32[1,256]{1,0:T(1,128)S(1)}, u32[]{:S(2)}, u32[]{:S(2)}) collective-permute-start(f32[1,256]{1,0:T(1,128)S(1)} %get-tuple-element.41), channel_id=1, source_target_pairs={{0,3},{1,2},{2,1},{3,0},{4,7},{5,6},{6,5},{7,4},{8,11},{9,10},{10,... | collective-permute-start | bytes 3080 | tf_op jit(solution)/shard_map/ppermute | solution.py:268

commit v21 on v19

--- a/solution.py
+++ b/solution.py
@@ -127,11 +127,6 @@
         ref[:size, :] = units[first:last]
         if ref.shape[0] > size:
             ref[size:, :] = ids
-
-
-def arrived_at(moves):
-    plane = lax.axis_index("gx") // PLANE
-    return functools.reduce(jnp.logical_or, [plane == receiver for _, receiver in moves])
 
 
 def add_line(query_parts, ids_ref, key_rows, key_ids, earlier_ref, sums_ref):
@@ -150,15 +145,6 @@
     return column
 
 
-def add_masses(query_ids, key_ids, powers):
-    mates = jnp.concatenate([query_ids] * (powers.shape[1] // LANES), axis=1) == key_ids
-    masses = jnp.where(mates, powers, 0.0)
-    folded = masses[:, :LANES]
-    for lane in range(LANES, powers.shape[1], LANES):
-        folded = folded + masses[:, lane : lane + LANES]
-    return folded, jnp.sum(masses, axis=0, keepdims=True)
-
-
 def query_parts_of(refs, rows):
     head = refs[2].shape[0]
     sizes = [rows, rows] + [head, rows - head] * (PLANE - 2)
@@ -172,7 +158,7 @@
     mass_ref[...] = jnp.sum(masses, axis=0, keepdims=True)
 
 
-def first_kernel(moves, own_mass_ref, head_ref, tail_ref, *refs):
+def first_kernel(own_mass_ref, head_ref, tail_ref, *refs):
     query_refs, (ids_ref, column_ref, sums_ref, mass_ref) = refs[:-4], refs[-4:]
     rows = mass_ref.shape[1]
     query_parts = query_parts_of(query_refs, rows)
@@ -194,59 +180,41 @@
     column_ref[...] = add_line(query_parts, ids_ref, key_rows, key_ids, None, sums_ref)
 
 
-def middle_kernel(moves, head_ref, *refs):
+def middle_kernel(head_ref, *refs):
     query_refs, (powers_ref, rest_ref) = refs[:-2], refs[-2:]
-
-    @pl.when(arrived_at(moves))
-    def _():
-        keys = powers_ref.shape[1]
-        units = unit_rows(head_ref[...])
-        rest_ref[...] = units[keys:]
-        first = 0
-        for query_ref, size in query_parts_of(query_refs, query_refs[0].shape[0] - ID_ROWS):
-            similar = lax.dot_general(
-                query_ref[:size, :], units[:keys], (((1,), (1,)), ((), ())),
-                preferred_element_type=jnp.float32,
-            )
-            powers_ref[pl.ds(first, size), :] = jnp.exp2(similar * INVERSE_TEMP_BITS)
-            first += size
-
-
-def last_kernel(moves, powers_ref, rest_ref, tail_ref, ids_ref, earlier_ref, mass_ref, *refs):
-    query_refs, refs = refs[: -PLANE - 2], refs[-PLANE - 2 :]
-    column_ref, row_refs, sums_ref = refs[0], refs[1:-1], refs[-1]
-    rows = column_ref.shape[1]
+    keys = powers_ref.shape[1]
+    units = unit_rows(head_ref[...])
+    rest_ref[...] = units[keys:]
+    first = 0
+    for query_ref, size in query_parts_of(query_refs, query_refs[0].shape[0] - ID_ROWS):
+        similar = lax.dot_general(
+            query_ref[:size, :], units[:keys], (((1,), (1,)), ((), ())),
+            preferred_element_type=jnp.float32,
+        )
+        powers_ref[pl.ds(first, size), :] = jnp.exp2(similar * INVERSE_TEMP_BITS)
+        first += size
+
+
+def last_kernel(powers_ref, rest_ref, tail_ref, ids_ref, earlier_ref, mass_ref, *refs):
+    query_refs, row_refs, sums_ref = refs[: -PLANE - 1], refs[-PLANE - 1 : -1], refs[-1]
+    rows = mass_ref.shape[1]
     cut = powers_ref.shape[1]
-    arrived = arrived_at(moves)
-
-    @pl.when(arrived)
-    def _():
-        key_ids = ids_of(tail_ref)[:, :rows]
-        key_rows = jnp.concatenate([rest_ref[...], tail_ref[: tail_ref.shape[0] - ID_ROWS, :]], axis=0)
-        early_column = jnp.zeros((1, cut), jnp.float32)
-        late_column = jnp.zeros((1, rows - cut), jnp.float32)
-        first = 0
-        for query_ref, size in query_parts_of(query_refs, rows):
-            part = pl.ds(first, size)
-            query_ids = ids_ref[part, :]
-            similar = lax.dot_general(
-                query_ref[:size, :], key_rows, (((1,), (1,)), ((), ())),
-                preferred_element_type=jnp.float32,
-            )
-            powers = jnp.exp2(similar * INVERSE_TEMP_BITS)
-            late, column = add_masses(query_ids, key_ids[:, cut:], powers)
-            late_column = late_column + column
-            early, column = add_masses(query_ids, key_ids[:, :cut], powers_ref[part, :])
-            early_column = early_column + column
-            sums_ref[part, :] = earlier_ref[part, :] + early + late
-            first += size
-        column_ref[...] = jnp.concatenate([early_column, late_column], axis=1)
-
-    @pl.when(jnp.logical_not(arrived))
-    def _():
-        column_ref[...] = jnp.zeros_like(column_ref)
-        sums_ref[...] = earlier_ref[...]
-
+    key_ids = ids_of(tail_ref)[:, :rows]
+    tail = tail_ref.shape[0] - ID_ROWS
+    key_rows = jnp.concatenate([rest_ref[...], tail_ref[:tail, :]], axis=0)
+    first = 0
+    for query_ref, size in query_parts_of(query_refs, rows):
+        part = pl.ds(first, size)
+        query_ids = ids_ref[part, :]
+        similar = lax.dot_general(
+            query_ref[:size, :], key_rows, (((1,), (1,)), ((), ())),
+            preferred_element_type=jnp.float32,
+        )
+        powers = jnp.exp2(similar * INVERSE_TEMP_BITS)
+        late = jnp.where(query_ids == key_ids[:, cut:], powers, 0.0)
+        early = jnp.where(query_ids == key_ids[:, :cut], powers_ref[part, :], 0.0)
+        sums_ref[part, :] = earlier_ref[part, :] + early + late
+        first += size
     for m in range(PLANE):
         row_sum = jnp.sum(sums_ref[pl.ds(m * rows, rows), :].T, axis=0, keepdims=True)
         row_refs[m][...] = row_sum + mass_ref[...] if m == 0 else row_sum
@@ -272,10 +240,7 @@
         return lax.ppermute(value, "gx", pairs)
 
     first_moves = [(0, 1), (1, 2), (2, 3), (3, 0)]
-    last_moves = [(0, 2), (1, 3)]
-    forward_moves = [(1, 2), (2, 3)]
     first_back = [(b, a) for a, b in first_moves]
-    last_back = [(b, a) for a, b in last_moves]
 
     half, part = row_count // 2, 9 * row_count // 16
     ranges = [(0, row_count), (0, half), (half, row_count), (part, row_count)]
@@ -294,38 +259,37 @@
     first_tail = on_line(tail, first_moves)
     across = [in_plane(piece, 2) for piece in pieces]
     sibling = in_plane(block, 1)
-    last_head, last_tail = [on_line(got, forward_moves) for got in (first_head, first_tail)]
+    last_head, last_tail = [on_line(got, first_moves) for got in (first_head, first_tail)]
     corner = [in_plane(piece, 1) for piece in across]
     queries = (block, sibling, *across, *corner)
     ids, first_column, first_sums, mass = pl.pallas_call(
-        functools.partial(first_kernel, first_moves),
+        first_kernel,
         out_shape=(lanes, vector, lanes, vector),
         cost_estimate=small,
         compiler_params=params,
     )(own_mass, first_head, first_tail, *queries)
     returned_first = on_line(first_column, first_back)
     powers, rest = pl.pallas_call(
-        functools.partial(middle_kernel, last_moves),
+        middle_kernel,
         out_shape=(
             jax.ShapeDtypeStruct((plane_rows, half), jnp.float32), rows_of(part - half)
         ),
         cost_estimate=small,
         compiler_params=params,
     )(last_head, *queries)
-    last_column, *row_sums = pl.pallas_call(
-        functools.partial(last_kernel, last_moves),
-        out_shape=[vector] * (1 + PLANE),
+    row_sums = list(pl.pallas_call(
+        last_kernel,
+        out_shape=[vector] * PLANE,
         scratch_shapes=[pltpu.VMEM(lanes.shape, lanes.dtype)],
         compiler_params=params,
-    )(powers, rest, last_tail, ids, first_sums, mass, *queries)
+    )(powers, rest, last_tail, ids, first_sums, mass, *queries))
     returned_first, row_sums[1] = lax.optimization_barrier((returned_first, row_sums[1]))
-    returned = [on_line(last_column, last_back)]
-    returned += [in_plane(row_sums[step], step) for step in (2, 3, 1)]
+    returned = [in_plane(row_sums[step], step) for step in (2, 3, 1)]
     return jnp.log1p(sum(returned, row_sums[0] + returned_first)).reshape(row_count)
 
 
 def on_device(embeddings, cluster_ids):
-    if lax.axis_size("gx") == 4 * PLANE and embeddings.shape[0] % (2 * LANES) == 0:
+    if lax.axis_size("gx") == 4 * PLANE and embeddings.shape[0] == 2 * LANES:
         return grid_plan(embeddings, cluster_ids)
     return plain_plan(embeddings, cluster_ids)
 

time: 35.7 us -> 36.3 us (1.017)
  starting transfers between devices: 14.4 us -> 12.6 us
  Pallas kernels: 2.79 us -> 4.2 us
  waiting for transfers between devices: 16.5 us -> 17.6 us
    ppermute x8, waiting for transfers between devices: 3.96 us -> 6.82 us  [in_plane(): return lax.ppermute(value, 'gx', [(i, i ^ step) for i in range(peers)])]
    ppermute x6 -> x5, waiting for transfers between devices: 12.6 us -> 10.7 us  [on_line(): return lax.ppermute(value, 'gx', pairs)]
    ppermute x6 -> x5, starting transfers between devices: 10.3 us -> 8.61 us  [on_line(): return lax.ppermute(value, 'gx', pairs)]
    pallas_call x3, Pallas kernels: 2.24 us -> 3.65 us  [the longest x1 2.02 us: grid_plan(): pl.pallas_call(first_kernel, out_shape=(lanes, vector, lanes, vector), co...]
  transfers between devices with their start and end apart: 14 -> 13, of which waited for: 6 -> 7; matrix products, arithmetic and copies ran while one was open for 0% -> 0% of each run, Pallas kernels for 8% -> 12%
where the time goes in v21:
time: 36.3 us; the launch traced here: 36.1 us
  waiting for transfers between devices  17.6 us (48%)
  starting transfers between devices  12.6 us (35%)
  Pallas kernels  4.2 us (12%)
  local copies, waits for them, and re-layouts  1.06 us (3%)
  other arithmetic  0.58 us (2%)
    ppermute x5, waiting for transfers between devices, on_line(): return lax.ppermute(value, 'gx', pairs)  10.7 us
    ppermute x5, starting transfers between devices, on_line(): return lax.ppermute(value, 'gx', pairs)  8.61 us
    ppermute x8, waiting for transfers between devices, in_plane(): return lax.ppermute(value, 'gx', [(i, i ^ step) for i in range(peers)])  6.82 us
    ppermute x8, starting transfers between devices, in_plane(): return lax.ppermute(value, 'gx', [(i, i ^ step) for i in range(peers)])  4.03 us
    pallas_call x1, Pallas kernels, grid_plan(): pl.pallas_call(first_kernel, out_shape=(lanes, vector, lanes, vector), co...  2.02 us
    slice x1, local copies, waits for them, and re-layouts, grid_plan(): first_head = on_line(embeddings[:part], first_moves)  1.05 us
    pallas_call x1, Pallas kernels, grid_plan(): pl.pallas_call(last_kernel, out_shape=[vector] * PLANE, scratch_shapes=[p...  0.82 us
    pallas_call x1, Pallas kernels, grid_plan(): pl.pallas_call(middle_kernel, out_shape=(jax.ShapeDtypeStruct((plane_rows...  0.81 us
  transfers between devices with their start and end apart: 13, of which 7 were waited for; matrix products, arithmetic and copies ran while one was open for 0% of the time, Pallas kernels for 12%

profile of v21, /device:TPU:0, one launch (start us, length us, event | category | flops | bytes accessed | tf_op | source)
XLA Modules:
  0.0 36.1 jit_solution(12968887057042509156)
XLA Ops:
  0.0 0.0 copy-start
  0.0 1.1 %slice.3 = bf16[144,1024]{1,0:T(8,128)(2,1)S(1)} slice(bf16[256,1024]{1,0:T(8,128)(2,1)} %rows_ref.1), slice={[0:144], [0:1024]} | slice | bytes 589824 | tf_op jit(solution)/shard_map/slice | solution.py:248
  1.1 0.0 copy-start.1
  1.1 3.1 %collective-permute-start = (bf16[144,1024]{1,0:T(8,128)(2,1)S(1)}, bf16[144,1024]{1,0:T(8,128)(2,1)S(1)}, u32[]{:S(2)}, u32[]{:S(2)}) collective-permute-start(bf16[144,1024]{1,0:T(8,128)(2,1)S(1)} %slice.3), channel_id=1, source_target_pairs={{0,4},{1,5},{2,6},{3,7},{4,8},{5,9},{6,10},{7,11},{8,12},{9,13},{1... | collective-permute-start | bytes 884744 | tf_op jit(solution)/shard_map/ppermute | solution.py:240
  4.1 0.0 copy-done
  4.2 0.0 copy-done.1
  4.2 0.2 shard_map.28
  4.4 1.6 %collective-permute-start.4 = (bf16[136,1024]{1,0:T(8,128)(2,1)S(1)}, bf16[136,1024]{1,0:T(8,128)(2,1)S(1)}, u32[]{:S(2)}, u32[]{:S(2)}) collective-permute-start(bf16[136,1024]{1,0:T(8,128)(2,1)S(1)} %get-tuple-element.25), channel_id=1, source_target_pairs={{0,2},{1,3},{2,0},{3,1},{4,6},{5,7},{6,4},{7,5},{8,10},{9,11},{10,... | collective-permute-start | bytes 835592 | tf_op jit(solution)/shard_map/ppermute | solution.py:236
  5.9 0.0 collective-permute-start.2
  5.9 0.5 %collective-permute-start.3 = (bf16[128,1024]{1,0:T(8,128)(2,1)S(1)}, bf16[128,1024]{1,0:T(8,128)(2,1)S(1)}, u32[]{:S(2)}, u32[]{:S(2)}) collective-permute-start(bf16[128,1024]{1,0:T(8,128)(2,1)S(1)} %get-tuple-element.24), channel_id=1, source_target_pairs={{0,2},{1,3},{2,0},{3,1},{4,6},{5,7},{6,4},{7,5},{8,10},{9,11},{10,... | collective-permute-start | bytes 786440 | tf_op jit(solution)/shard_map/ppermute | solution.py:236
  6.4 0.4 shard_map.30.own_mass_ref
  6.8 1.6 %collective-permute-start.7 = (bf16[120,1024]{1,0:T(8,128)(2,1)S(1)}, bf16[120,1024]{1,0:T(8,128)(2,1)S(1)}, u32[]{:S(2)}, u32[]{:S(2)}) collective-permute-start(bf16[120,1024]{1,0:T(8,128)(2,1)S(1)} %get-tuple-element.29), channel_id=1, source_target_pairs={{0,4},{1,5},{2,6},{3,7},{4,8},{5,9},{6,10},{7,11},{8,12},{9,13},{1... | collective-permute-start | bytes 737288 | tf_op jit(solution)/shard_map/ppermute | solution.py:240
  8.4 5.6 %collective-permute-done.head_ref = bf16[144,1024]{1,0:T(8,128)(2,1)S(1)} collective-permute-done((bf16[144,1024]{1,0:T(8,128)(2,1)S(1)}, bf16[144,1024]{1,0:T(8,128)(2,1)S(1)}, u32[]{:S(2)}, u32[]{:S(2)}) %collective-permute-start) | collective-permute-done | bytes 294944 | tf_op jit(solution)/shard_map/ppermute | solution.py:240
  14.0 0.0 collective-permute-start.1
  14.0 0.0 collective-permute-done.4.refs_3_
  14.0 0.0 collective-permute-start.6
  14.0 4.1 %collective-permute-done.3.refs_2_ = bf16[128,1024]{1,0:T(8,128)(2,1)S(1)} collective-permute-done((bf16[128,1024]{1,0:T(8,128)(2,1)S(1)}, bf16[128,1024]{1,0:T(8,128)(2,1)S(1)}, u32[]{:S(2)}, u32[]{:S(2)}) %collective-permute-start.3) | collective-permute-done | bytes 262176 | tf_op jit(solution)/shard_map/ppermute | solution.py:236
  18.2 0.0 collective-permute-start.5
  18.2 1.1 %collective-permute-done.7.tail_ref = bf16[120,1024]{1,0:T(8,128)(2,1)S(1)} collective-permute-done((bf16[120,1024]{1,0:T(8,128)(2,1)S(1)}, bf16[120,1024]{1,0:T(8,128)(2,1)S(1)}, u32[]{:S(2)}, u32[]{:S(2)}) %collective-permute-start.7) | collective-permute-done | bytes 245792 | tf_op jit(solution)/shard_map/ppermute | solution.py:240
  19.3 0.5 %collective-permute-start.8 = (bf16[120,1024]{1,0:T(8,128)(2,1)S(1)}, bf16[120,1024]{1,0:T(8,128)(2,1)S(1)}, u32[]{:S(2)}, u32[]{:S(2)}) collective-permute-start(bf16[120,1024]{1,0:T(8,128)(2,1)S(1)} %collective-permute-done.7.tail_ref), channel_id=1, source_target_pairs={{0,4},{1,5},{2,6},{3,7},{4,8},{5,9},{6,10},{7,11},{8,12},{9,13},{1... | collective-permute-start | bytes 737288 | tf_op jit(solution)/shard_map/ppermute | solution.py:240
  19.7 0.0 collective-permute-done.5.refs_4_
  19.7 0.0 collective-permute-done.2.refs_1_
  19.7 0.0 collective-permute-done.6.refs_5_
  19.7 2.0 %shard_map.31 = (f32[1024,128]{1,0:T(8,128)S(1)}, f32[1,256]{1,0:T(1,128)S(1)}, f32[1024,128]{1,0:T(8,128)S(1)}, f32[1,256]{1,0:T(1,128)S(1)}) custom-call(f32[1,256]{1,0:T(1,128)S(1)} %shard_map.30.own_mass_ref, bf16[144,1024]{1,0:T(8,128)(2,1)S(1)} %collective-permute-done.head_ref, bf16[120,1024]{1,0:T(8,128)(2,1)S(1)} %collective-permute-done.7.tail_ref, ...), custom_call_target="tpu_custom_call" | custom-call | flops 1 | bytes 1 | tf_op jit(solution)/shard_map/pallas_call | solution.py:265
  21.8 3.4 %collective-permute-start.9 = (f32[1,256]{1,0:T(1,128)S(1)}, f32[1,256]{1,0:T(1,128)S(1)}, u32[]{:S(2)}, u32[]{:S(2)}) collective-permute-start(f32[1,256]{1,0:T(1,128)S(1)} %get-tuple-element.35), channel_id=1, source_target_pairs={{4,0},{5,1},{6,2},{7,3},{8,4},{9,5},{10,6},{11,7},{12,8},{13,9},{1... | collective-permute-start | bytes 3080 | tf_op jit(solution)/shard_map/ppermute | solution.py:240
  25.2 0.6 %collective-permute-done.1.head_ref = bf16[144,1024]{1,0:T(8,128)(2,1)S(1)} collective-permute-done((bf16[144,1024]{1,0:T(8,128)(2,1)S(1)}, bf16[144,1024]{1,0:T(8,128)(2,1)S(1)}, u32[]{:S(2)}, u32[]{:S(2)}) %collective-permute-start.1) | collective-permute-done | bytes 294944 | tf_op jit(solution)/shard_map/ppermute | solution.py:240
  25.8 0.8 %shard_map.29 = (f32[1024,128]{1,0:T(8,128)S(1)}, bf16[16,1024]{1,0:T(8,128)(2,1)S(1)}) custom-call(bf16[144,1024]{1,0:T(8,128)(2,1)S(1)} %collective-permute-done.1.head_ref, bf16[264,1024]{1,0:T(8,128)(2,1)S(1)} %get-tuple-element.23.refs_0_.own_ref, bf16[264,1024]{1,0:T(8,128)(2,1)S(1)} %collective-permute-done.2.refs_1_, ...), custom_call_target="tpu_custom_call" | custom-call | flops 1 | bytes 1 | tf_op jit(solution)/shard_map/pallas_call | solution.py:272
  26.6 3.5 %collective-permute-done.8.tail_ref = bf16[120,1024]{1,0:T(8,128)(2,1)S(1)} collective-permute-done((bf16[120,1024]{1,0:T(8,128)(2,1)S(1)}, bf16[120,1024]{1,0:T(8,128)(2,1)S(1)}, u32[]{:S(2)}, u32[]{:S(2)}) %collective-permute-start.8) | collective-permute-done | bytes 245792 | tf_op jit(solution)/shard_map/ppermute | solution.py:240
  30.1 0.8 %shard_map.32 = (f32[1,256]{1,0:T(1,128)S(1)}, f32[1,256]{1,0:T(1,128)S(1)}, f32[1,256]{1,0:T(1,128)S(1)}, f32[1,256]{1,0:T(1,128)S(1)}) custom-call(f32[1024,128]{1,0:T(8,128)S(1)} %get-tuple-element.26.powers_ref, bf16[16,1024]{1,0:T(8,128)(2,1)S(1)} %get-tuple-element.27.rest_ref, bf16[120,1024]{1,0:T(8,128)(2,1)S(1)} %collective-permute-done.8.tail_ref, ...), custom_call_target="tpu_custom_call" | custom-call | tf_op jit(solution)/shard_map/pallas_call | solution.py:280
  30.9 0.0 collective-permute-done.9
  30.9 0.1 collective-permute-start.12
  31.0 1.6 %collective-permute-start.10 = (f32[1,256]{1,0:T(1,128)S(1)}, f32[1,256]{1,0:T(1,128)S(1)}, u32[]{:S(2)}, u32[]{:S(2)}) collective-permute-start(f32[1,256]{1,0:T(1,128)S(1)} %get-tuple-element.38), channel_id=1, source_target_pairs={{0,2},{1,3},{2,0},{3,1},{4,6},{5,7},{6,4},{7,5},{8,10},{9,11},{10,... | collective-permute-start | bytes 3080 | tf_op jit(solution)/shard_map/ppermute | solution.py:236
  32.5 0.3 collective-permute-start.11
  32.8 0.0 collective-permute-done.12
  32.8 1.8 %collective-permute-done.10 = f32[1,256]{1,0:T(1,128)S(1)} collective-permute-done((f32[1,256]{1,0:T(1,128)S(1)}, f32[1,256]{1,0:T(1,128)S(1)}, u32[]{:S(2)}, u32[]{:S(2)}) %collective-permute-start.10) | collective-permute-done | bytes 1056 | tf_op jit(solution)/shard_map/ppermute | solution.py:236
  34.6 0.9 %collective-permute-done.11 = f32[1,256]{1,0:T(1,128)S(1)} collective-permute-done((f32[1,256]{1,0:T(1,128)S(1)}, f32[1,256]{1,0:T(1,128)S(1)}, u32[]{:S(2)}, u32[]{:S(2)}) %collective-permute-start.11) | collective-permute-done | bytes 1056 | tf_op jit(solution)/shard_map/ppermute | solution.py:236
  35.5 0.6 %add_log-plus-one_fusion = f32[1,256]{1,0:T(1,128)} fusion(f32[1,256]{1,0:T(1,128)S(1)} %collective-permute-done.12, f32[1,256]{1,0:T(1,128)S(1)} %collective-permute-done.11, f32[1,256]{1,0:T(1,128)S(1)} %collective-permute-done.10, f32[1,256]{1,0:T(1,128)S(1)} %get-tuple-element.34, f32[1,256]{1,0:T(1,128)S(1)} %collective-permute-done.9), kind=kLoop, calls=%fused_computation | loop fusion | flops 1024 | bytes 6144 | tf_op jit(solution)/shard_map/log1p | solution.py:288
Async XLA Ops:
  0.0 4.1 %copy-start = (bf16[256,1024]{1,0:T(8,128)(2,1)S(1)}, bf16[256,1024]{1,0:T(8,128)(2,1)}, u32[]{:S(2)}) copy-start(bf16[256,1024]{1,0:T(8,128)(2,1)} %rows_ref.1) | copy-start | bytes 1572868
  1.1 3.1 %copy-start.1 = (s32[256]{0:T(256)S(1)}, s32[256]{0:T(256)}, u32[]{:S(2)}) copy-start(s32[256]{0:T(256)} %param.3) | copy-start | bytes 3076
  1.1 12.9 %collective-permute-start = (bf16[144,1024]{1,0:T(8,128)(2,1)S(1)}, bf16[144,1024]{1,0:T(8,128)(2,1)S(1)}, u32[]{:S(2)}, u32[]{:S(2)}) collective-permute-start(bf16[144,1024]{1,0:T(8,128)(2,1)S(1)} %slice.3), channel_id=1, source_target_pairs={{0,4},{1,5},{2,6},{3,7},{4,8},{5,9},{6,10},{7,11},{8,12},{9,13},{1... | collective-permute-start | bytes 884744 | tf_op jit(solution)/shard_map/ppermute | solution.py:240
  4.4 9.7 %collective-permute-start.4 = (bf16[136,1024]{1,0:T(8,128)(2,1)S(1)}, bf16[136,1024]{1,0:T(8,128)(2,1)S(1)}, u32[]{:S(2)}, u32[]{:S(2)}) collective-permute-start(bf16[136,1024]{1,0:T(8,128)(2,1)S(1)} %get-tuple-element.25), channel_id=1, source_target_pairs={{0,2},{1,3},{2,0},{3,1},{4,6},{5,7},{6,4},{7,5},{8,10},{9,11},{10,... | collective-permute-start | bytes 835592 | tf_op jit(solution)/shard_map/ppermute | solution.py:236
  5.9 13.8 %collective-permute-start.2 = (bf16[264,1024]{1,0:T(8,128)(2,1)S(1)}, bf16[264,1024]{1,0:T(8,128)(2,1)S(1)}, u32[]{:S(2)}, u32[]{:S(2)}) collective-permute-start(bf16[264,1024]{1,0:T(8,128)(2,1)S(1)} %get-tuple-element.23.refs_0_.own_ref), channel_id=1, source_target_pairs={{0,1},{1,0},{2,3},{3,2},{4,5},{5,4},{6,7},{7,6},{8,9},{9,8},{10,11... | collective-permute-start | bytes 1622024 | tf_op jit(solution)/shard_map/ppermute | solution.py:236
  5.9 12.2 %collective-permute-start.3 = (bf16[128,1024]{1,0:T(8,128)(2,1)S(1)}, bf16[128,1024]{1,0:T(8,128)(2,1)S(1)}, u32[]{:S(2)}, u32[]{:S(2)}) collective-permute-start(bf16[128,1024]{1,0:T(8,128)(2,1)S(1)} %get-tuple-element.24), channel_id=1, source_target_pairs={{0,2},{1,3},{2,0},{3,1},{4,6},{5,7},{6,4},{7,5},{8,10},{9,11},{10,... | collective-permute-start | bytes 786440 | tf_op jit(solution)/shard_map/ppermute | solution.py:236
  6.8 12.5 %collective-permute-start.7 = (bf16[120,1024]{1,0:T(8,128)(2,1)S(1)}, bf16[120,1024]{1,0:T(8,128)(2,1)S(1)}, u32[]{:S(2)}, u32[]{:S(2)}) collective-permute-start(bf16[120,1024]{1,0:T(8,128)(2,1)S(1)} %get-tuple-element.29), channel_id=1, source_target_pairs={{0,4},{1,5},{2,6},{3,7},{4,8},{5,9},{6,10},{7,11},{8,12},{9,13},{1... | collective-permute-start | bytes 737288 | tf_op jit(solution)/shard_map/ppermute | solution.py:240
  14.0 11.8 %collective-permute-start.1 = (bf16[144,1024]{1,0:T(8,128)(2,1)S(1)}, bf16[144,1024]{1,0:T(8,128)(2,1)S(1)}, u32[]{:S(2)}, u32[]{:S(2)}) collective-permute-start(bf16[144,1024]{1,0:T(8,128)(2,1)S(1)} %collective-permute-done.head_ref), channel_id=1, source_target_pairs={{0,4},{1,5},{2,6},{3,7},{4,8},{5,9},{6,10},{7,11},{8,12},{9,13},{1... | collective-permute-start | bytes 884744 | tf_op jit(solution)/shard_map/ppermute | solution.py:240
  14.0 5.7 %collective-permute-start.6 = (bf16[136,1024]{1,0:T(8,128)(2,1)S(1)}, bf16[136,1024]{1,0:T(8,128)(2,1)S(1)}, u32[]{:S(2)}, u32[]{:S(2)}) collective-permute-start(bf16[136,1024]{1,0:T(8,128)(2,1)S(1)} %collective-permute-done.4.refs_3_), channel_id=1, source_target_pairs={{0,1},{1,0},{2,3},{3,2},{4,5},{5,4},{6,7},{7,6},{8,9},{9,8},{10,11... | collective-permute-start | bytes 835592 | tf_op jit(solution)/shard_map/ppermute | solution.py:236
  18.2 1.6 %collective-permute-start.5 = (bf16[128,1024]{1,0:T(8,128)(2,1)S(1)}, bf16[128,1024]{1,0:T(8,128)(2,1)S(1)}, u32[]{:S(2)}, u32[]{:S(2)}) collective-permute-start(bf16[128,1024]{1,0:T(8,128)(2,1)S(1)} %collective-permute-done.3.refs_2_), channel_id=1, source_target_pairs={{0,1},{1,0},{2,3},{3,2},{4,5},{5,4},{6,7},{7,6},{8,9},{9,8},{10,11... | collective-permute-start | bytes 786440 | tf_op jit(solution)/shard_map/ppermute | solution.py:236
  19.3 10.8 %collective-permute-start.8 = (bf16[120,1024]{1,0:T(8,128)(2,1)S(1)}, bf16[120,1024]{1,0:T(8,128)(2,1)S(1)}, u32[]{:S(2)}, u32[]{:S(2)}) collective-permute-start(bf16[120,1024]{1,0:T(8,128)(2,1)S(1)} %collective-permute-done.7.tail_ref), channel_id=1, source_target_pairs={{0,4},{1,5},{2,6},{3,7},{4,8},{5,9},{6,10},{7,11},{8,12},{9,13},{1... | collective-permute-start | bytes 737288 | tf_op jit(solution)/shard_map/ppermute | solution.py:240
  21.8 9.1 %collective-permute-start.9 = (f32[1,256]{1,0:T(1,128)S(1)}, f32[1,256]{1,0:T(1,128)S(1)}, u32[]{:S(2)}, u32[]{:S(2)}) collective-permute-start(f32[1,256]{1,0:T(1,128)S(1)} %get-tuple-element.35), channel_id=1, source_target_pairs={{4,0},{5,1},{6,2},{7,3},{8,4},{9,5},{10,6},{11,7},{12,8},{13,9},{1... | collective-permute-start | bytes 3080 | tf_op jit(solution)/shard_map/ppermute | solution.py:240
  30.9 1.9 %collective-permute-start.12 = (f32[1,256]{1,0:T(1,128)S(1)}, f32[1,256]{1,0:T(1,128)S(1)}, u32[]{:S(2)}, u32[]{:S(2)}) collective-permute-start(f32[1,256]{1,0:T(1,128)S(1)} %get-tuple-element.40), channel_id=1, source_target_pairs={{0,1},{1,0},{2,3},{3,2},{4,5},{5,4},{6,7},{7,6},{8,9},{9,8},{10,11... | collective-permute-start | bytes 3080 | tf_op jit(solution)/shard_map/ppermute | solution.py:236
  31.0 3.6 %collective-permute-start.10 = (f32[1,256]{1,0:T(1,128)S(1)}, f32[1,256]{1,0:T(1,128)S(1)}, u32[]{:S(2)}, u32[]{:S(2)}) collective-permute-start(f32[1,256]{1,0:T(1,128)S(1)} %get-tuple-element.38), channel_id=1, source_target_pairs={{0,2},{1,3},{2,0},{3,1},{4,6},{5,7},{6,4},{7,5},{8,10},{9,11},{10,... | collective-permute-start | bytes 3080 | tf_op jit(solution)/shard_map/ppermute | solution.py:236
  32.5 3.0 %collective-permute-start.11 = (f32[1,256]{1,0:T(1,128)S(1)}, f32[1,256]{1,0:T(1,128)S(1)}, u32[]{:S(2)}, u32[]{:S(2)}) collective-permute-start(f32[1,256]{1,0:T(1,128)S(1)} %get-tuple-element.39), channel_id=1, source_target_pairs={{0,3},{1,2},{2,1},{3,0},{4,7},{5,6},{6,5},{7,4},{8,11},{9,10},{10,... | collective-permute-start | bytes 3080 | tf_op jit(solution)/shard_map/ppermute | solution.py:236

commit v22 on v21

--- a/solution.py
+++ b/solution.py
@@ -239,7 +239,7 @@
         pairs = [(a * PLANE + n, b * PLANE + n) for a, b in moves for n in range(PLANE)]
         return lax.ppermute(value, "gx", pairs)
 
-    first_moves = [(0, 1), (1, 2), (2, 3), (3, 0)]
+    first_moves = [(1, 0), (2, 1), (3, 2), (0, 3)]
     first_back = [(b, a) for a, b in first_moves]
 
     half, part = row_count // 2, 9 * row_count // 16

time: 36.3 us -> 35.8 us (0.986)
  waiting for transfers between devices: 17.6 us -> 12.7 us
  starting transfers between devices: 12.6 us -> 17 us
    ppermute x5, starting transfers between devices: 8.61 us -> 13.1 us  [on_line(): return lax.ppermute(value, 'gx', pairs)]
    ppermute x5, waiting for transfers between devices: 10.7 us -> 7.78 us  [on_line(): return lax.ppermute(value, 'gx', pairs)]
    ppermute x8, waiting for transfers between devices: 6.82 us -> 4.95 us  [in_plane(): return lax.ppermute(value, 'gx', [(i, i ^ step) for i in range(peers)])]
where the time goes in v22:
time: 35.8 us; the launch traced here: 35.7 us
  starting transfers between devices  17 us (47%)
  waiting for transfers between devices  12.7 us (35%)
  Pallas kernels  4.2 us (12%)
  local copies, waits for them, and re-layouts  1.06 us (3%)
  other arithmetic  0.58 us (2%)
    ppermute x5, starting transfers between devices, on_line(): return lax.ppermute(value, 'gx', pairs)  13.1 us
    ppermute x5, waiting for transfers between devices, on_line(): return lax.ppermute(value, 'gx', pairs)  7.78 us
    ppermute x8, waiting for transfers between devices, in_plane(): return lax.ppermute(value, 'gx', [(i, i ^ step) for i in range(peers)])  4.95 us
    ppermute x8, starting transfers between devices, in_plane(): return lax.ppermute(value, 'gx', [(i, i ^ step) for i in range(peers)])  3.96 us
    pallas_call x1, Pallas kernels, grid_plan(): pl.pallas_call(first_kernel, out_shape=(lanes, vector, lanes, vector), co...  2.02 us
    slice x1, local copies, waits for them, and re-layouts, grid_plan(): first_head = on_line(embeddings[:part], first_moves)  1.05 us
    pallas_call x1, Pallas kernels, grid_plan(): pl.pallas_call(last_kernel, out_shape=[vector] * PLANE, scratch_shapes=[p...  0.82 us
    pallas_call x1, Pallas kernels, grid_plan(): pl.pallas_call(middle_kernel, out_shape=(jax.ShapeDtypeStruct((plane_rows...  0.81 us
  transfers between devices with their start and end apart: 13, of which 7 were waited for; matrix products, arithmetic and copies ran while one was open for 0% of the time, Pallas kernels for 12%

profile of v22, /device:TPU:0, one launch (start us, length us, event | category | flops | bytes accessed | tf_op | source)
XLA Modules:
  0.0 35.7 jit_solution(674322803476637157)
XLA Ops:
  0.0 0.0 copy-start
  0.0 1.1 %slice.3 = bf16[144,1024]{1,0:T(8,128)(2,1)S(1)} slice(bf16[256,1024]{1,0:T(8,128)(2,1)} %rows_ref.1), slice={[0:144], [0:1024]} | slice | bytes 589824 | tf_op jit(solution)/shard_map/slice | solution.py:248
  1.1 0.0 copy-start.1
  1.1 5.1 %collective-permute-start = (bf16[144,1024]{1,0:T(8,128)(2,1)S(1)}, bf16[144,1024]{1,0:T(8,128)(2,1)S(1)}, u32[]{:S(2)}, u32[]{:S(2)}) collective-permute-start(bf16[144,1024]{1,0:T(8,128)(2,1)S(1)} %slice.3), channel_id=1, source_target_pairs={{4,0},{5,1},{6,2},{7,3},{8,4},{9,5},{10,6},{11,7},{12,8},{13,9},{1... | collective-permute-start | bytes 884744 | tf_op jit(solution)/shard_map/ppermute | solution.py:240
  6.2 0.0 copy-done
  6.2 0.0 copy-done.1
  6.2 0.2 shard_map.28
  6.4 1.6 %collective-permute-start.4 = (bf16[136,1024]{1,0:T(8,128)(2,1)S(1)}, bf16[136,1024]{1,0:T(8,128)(2,1)S(1)}, u32[]{:S(2)}, u32[]{:S(2)}) collective-permute-start(bf16[136,1024]{1,0:T(8,128)(2,1)S(1)} %get-tuple-element.25), channel_id=1, source_target_pairs={{0,2},{1,3},{2,0},{3,1},{4,6},{5,7},{6,4},{7,5},{8,10},{9,11},{10,... | collective-permute-start | bytes 835592 | tf_op jit(solution)/shard_map/ppermute | solution.py:236
  7.9 0.0 collective-permute-start.2
  7.9 0.5 %collective-permute-start.3 = (bf16[128,1024]{1,0:T(8,128)(2,1)S(1)}, bf16[128,1024]{1,0:T(8,128)(2,1)S(1)}, u32[]{:S(2)}, u32[]{:S(2)}) collective-permute-start(bf16[128,1024]{1,0:T(8,128)(2,1)S(1)} %get-tuple-element.24), channel_id=1, source_target_pairs={{0,2},{1,3},{2,0},{3,1},{4,6},{5,7},{6,4},{7,5},{8,10},{9,11},{10,... | collective-permute-start | bytes 786440 | tf_op jit(solution)/shard_map/ppermute | solution.py:236
  8.5 0.3 shard_map.30.own_mass_ref
  8.8 0.7 %collective-permute-start.7 = (bf16[120,1024]{1,0:T(8,128)(2,1)S(1)}, bf16[120,1024]{1,0:T(8,128)(2,1)S(1)}, u32[]{:S(2)}, u32[]{:S(2)}) collective-permute-start(bf16[120,1024]{1,0:T(8,128)(2,1)S(1)} %get-tuple-element.29), channel_id=1, source_target_pairs={{4,0},{5,1},{6,2},{7,3},{8,4},{9,5},{10,6},{11,7},{12,8},{13,9},{1... | collective-permute-start | bytes 737288 | tf_op jit(solution)/shard_map/ppermute | solution.py:240
  9.5 4.1 %collective-permute-done.head_ref = bf16[144,1024]{1,0:T(8,128)(2,1)S(1)} collective-permute-done((bf16[144,1024]{1,0:T(8,128)(2,1)S(1)}, bf16[144,1024]{1,0:T(8,128)(2,1)S(1)}, u32[]{:S(2)}, u32[]{:S(2)}) %collective-permute-start) | collective-permute-done | bytes 294944 | tf_op jit(solution)/shard_map/ppermute | solution.py:240
  13.6 4.3 %collective-permute-start.1 = (bf16[144,1024]{1,0:T(8,128)(2,1)S(1)}, bf16[144,1024]{1,0:T(8,128)(2,1)S(1)}, u32[]{:S(2)}, u32[]{:S(2)}) collective-permute-start(bf16[144,1024]{1,0:T(8,128)(2,1)S(1)} %collective-permute-done.head_ref), channel_id=1, source_target_pairs={{4,0},{5,1},{6,2},{7,3},{8,4},{9,5},{10,6},{11,7},{12,8},{13,9},{1... | collective-permute-start | bytes 884744 | tf_op jit(solution)/shard_map/ppermute | solution.py:240
  17.9 0.0 collective-permute-done.4.refs_3_
  17.9 0.0 collective-permute-start.6
  17.9 2.3 %collective-permute-done.3.refs_2_ = bf16[128,1024]{1,0:T(8,128)(2,1)S(1)} collective-permute-done((bf16[128,1024]{1,0:T(8,128)(2,1)S(1)}, bf16[128,1024]{1,0:T(8,128)(2,1)S(1)}, u32[]{:S(2)}, u32[]{:S(2)}) %collective-permute-start.3) | collective-permute-done | bytes 262176 | tf_op jit(solution)/shard_map/ppermute | solution.py:236
  20.2 0.0 collective-permute-start.5
  20.2 0.0 collective-permute-done.7.tail_ref
  20.2 2.9 %collective-permute-start.8 = (bf16[120,1024]{1,0:T(8,128)(2,1)S(1)}, bf16[120,1024]{1,0:T(8,128)(2,1)S(1)}, u32[]{:S(2)}, u32[]{:S(2)}) collective-permute-start(bf16[120,1024]{1,0:T(8,128)(2,1)S(1)} %collective-permute-done.7.tail_ref), channel_id=1, source_target_pairs={{4,0},{5,1},{6,2},{7,3},{8,4},{9,5},{10,6},{11,7},{12,8},{13,9},{1... | collective-permute-start | bytes 737288 | tf_op jit(solution)/shard_map/ppermute | solution.py:240
  23.1 0.0 collective-permute-done.5.refs_4_
  23.1 0.0 collective-permute-done.2.refs_1_
  23.1 0.0 collective-permute-done.6.refs_5_
  23.1 2.0 %shard_map.31 = (f32[1024,128]{1,0:T(8,128)S(1)}, f32[1,256]{1,0:T(1,128)S(1)}, f32[1024,128]{1,0:T(8,128)S(1)}, f32[1,256]{1,0:T(1,128)S(1)}) custom-call(f32[1,256]{1,0:T(1,128)S(1)} %shard_map.30.own_mass_ref, bf16[144,1024]{1,0:T(8,128)(2,1)S(1)} %collective-permute-done.head_ref, bf16[120,1024]{1,0:T(8,128)(2,1)S(1)} %collective-permute-done.7.tail_ref, ...), custom_call_target="tpu_custom_call" | custom-call | flops 1 | bytes 1 | tf_op jit(solution)/shard_map/pallas_call | solution.py:265
  25.2 0.1 collective-permute-start.9
  25.2 0.1 collective-permute-done.1.head_ref
  25.3 0.8 %shard_map.29 = (f32[1024,128]{1,0:T(8,128)S(1)}, bf16[16,1024]{1,0:T(8,128)(2,1)S(1)}) custom-call(bf16[144,1024]{1,0:T(8,128)(2,1)S(1)} %collective-permute-done.1.head_ref, bf16[264,1024]{1,0:T(8,128)(2,1)S(1)} %get-tuple-element.23.refs_0_.own_ref, bf16[264,1024]{1,0:T(8,128)(2,1)S(1)} %collective-permute-done.2.refs_1_, ...), custom_call_target="tpu_custom_call" | custom-call | flops 1 | bytes 1 | tf_op jit(solution)/shard_map/pallas_call | solution.py:272
  26.2 3.2 %collective-permute-done.8.tail_ref = bf16[120,1024]{1,0:T(8,128)(2,1)S(1)} collective-permute-done((bf16[120,1024]{1,0:T(8,128)(2,1)S(1)}, bf16[120,1024]{1,0:T(8,128)(2,1)S(1)}, u32[]{:S(2)}, u32[]{:S(2)}) %collective-permute-start.8) | collective-permute-done | bytes 245792 | tf_op jit(solution)/shard_map/ppermute | solution.py:240
  29.3 0.8 %shard_map.32 = (f32[1,256]{1,0:T(1,128)S(1)}, f32[1,256]{1,0:T(1,128)S(1)}, f32[1,256]{1,0:T(1,128)S(1)}, f32[1,256]{1,0:T(1,128)S(1)}) custom-call(f32[1024,128]{1,0:T(8,128)S(1)} %get-tuple-element.26.powers_ref, bf16[16,1024]{1,0:T(8,128)(2,1)S(1)} %get-tuple-element.27.rest_ref, bf16[120,1024]{1,0:T(8,128)(2,1)S(1)} %collective-permute-done.8.tail_ref, ...), custom_call_target="tpu_custom_call" | custom-call | tf_op jit(solution)/shard_map/pallas_call | solution.py:280
  30.1 0.5 %collective-permute-done.9 = f32[1,256]{1,0:T(1,128)S(1)} collective-permute-done((f32[1,256]{1,0:T(1,128)S(1)}, f32[1,256]{1,0:T(1,128)S(1)}, u32[]{:S(2)}, u32[]{:S(2)}) %collective-permute-start.9) | collective-permute-done | bytes 1056 | tf_op jit(solution)/shard_map/ppermute | solution.py:240
  30.6 0.0 collective-permute-start.12
  30.6 1.5 %collective-permute-start.10 = (f32[1,256]{1,0:T(1,128)S(1)}, f32[1,256]{1,0:T(1,128)S(1)}, u32[]{:S(2)}, u32[]{:S(2)}) collective-permute-start(f32[1,256]{1,0:T(1,128)S(1)} %get-tuple-element.38), channel_id=1, source_target_pairs={{0,2},{1,3},{2,0},{3,1},{4,6},{5,7},{6,4},{7,5},{8,10},{9,11},{10,... | collective-permute-start | bytes 3080 | tf_op jit(solution)/shard_map/ppermute | solution.py:236
  32.1 0.4 %collective-permute-start.11 = (f32[1,256]{1,0:T(1,128)S(1)}, f32[1,256]{1,0:T(1,128)S(1)}, u32[]{:S(2)}, u32[]{:S(2)}) collective-permute-start(f32[1,256]{1,0:T(1,128)S(1)} %get-tuple-element.39), channel_id=1, source_target_pairs={{0,3},{1,2},{2,1},{3,0},{4,7},{5,6},{6,5},{7,4},{8,11},{9,10},{10,... | collective-permute-start | bytes 3080 | tf_op jit(solution)/shard_map/ppermute | solution.py:236
  32.4 0.0 collective-permute-done.12
  32.5 1.7 %collective-permute-done.10 = f32[1,256]{1,0:T(1,128)S(1)} collective-permute-done((f32[1,256]{1,0:T(1,128)S(1)}, f32[1,256]{1,0:T(1,128)S(1)}, u32[]{:S(2)}, u32[]{:S(2)}) %collective-permute-start.10) | collective-permute-done | bytes 1056 | tf_op jit(solution)/shard_map/ppermute | solution.py:236
  34.2 0.9 %collective-permute-done.11 = f32[1,256]{1,0:T(1,128)S(1)} collective-permute-done((f32[1,256]{1,0:T(1,128)S(1)}, f32[1,256]{1,0:T(1,128)S(1)}, u32[]{:S(2)}, u32[]{:S(2)}) %collective-permute-start.11) | collective-permute-done | bytes 1056 | tf_op jit(solution)/shard_map/ppermute | solution.py:236
  35.1 0.6 %add_log-plus-one_fusion = f32[1,256]{1,0:T(1,128)} fusion(f32[1,256]{1,0:T(1,128)S(1)} %collective-permute-done.12, f32[1,256]{1,0:T(1,128)S(1)} %collective-permute-done.11, f32[1,256]{1,0:T(1,128)S(1)} %collective-permute-done.10, f32[1,256]{1,0:T(1,128)S(1)} %get-tuple-element.34, f32[1,256]{1,0:T(1,128)S(1)} %collective-permute-done.9), kind=kLoop, calls=%fused_computation | loop fusion | flops 1024 | bytes 6144 | tf_op jit(solution)/shard_map/log1p | solution.py:288
Async XLA Ops:
  0.0 6.2 %copy-start = (bf16[256,1024]{1,0:T(8,128)(2,1)S(1)}, bf16[256,1024]{1,0:T(8,128)(2,1)}, u32[]{:S(2)}) copy-start(bf16[256,1024]{1,0:T(8,128)(2,1)} %rows_ref.1) | copy-start | bytes 1572868
  1.1 5.1 %copy-start.1 = (s32[256]{0:T(256)S(1)}, s32[256]{0:T(256)}, u32[]{:S(2)}) copy-start(s32[256]{0:T(256)} %param.3) | copy-start | bytes 3076
  1.1 12.5 %collective-permute-start = (bf16[144,1024]{1,0:T(8,128)(2,1)S(1)}, bf16[144,1024]{1,0:T(8,128)(2,1)S(1)}, u32[]{:S(2)}, u32[]{:S(2)}) collective-permute-start(bf16[144,1024]{1,0:T(8,128)(2,1)S(1)} %slice.3), channel_id=1, source_target_pairs={{4,0},{5,1},{6,2},{7,3},{8,4},{9,5},{10,6},{11,7},{12,8},{13,9},{1... | collective-permute-start | bytes 884744 | tf_op jit(solution)/shard_map/ppermute | solution.py:240
  6.4 11.5 %collective-permute-start.4 = (bf16[136,1024]{1,0:T(8,128)(2,1)S(1)}, bf16[136,1024]{1,0:T(8,128)(2,1)S(1)}, u32[]{:S(2)}, u32[]{:S(2)}) collective-permute-start(bf16[136,1024]{1,0:T(8,128)(2,1)S(1)} %get-tuple-element.25), channel_id=1, source_target_pairs={{0,2},{1,3},{2,0},{3,1},{4,6},{5,7},{6,4},{7,5},{8,10},{9,11},{10,... | collective-permute-start | bytes 835592 | tf_op jit(solution)/shard_map/ppermute | solution.py:236
  7.9 15.2 %collective-permute-start.2 = (bf16[264,1024]{1,0:T(8,128)(2,1)S(1)}, bf16[264,1024]{1,0:T(8,128)(2,1)S(1)}, u32[]{:S(2)}, u32[]{:S(2)}) collective-permute-start(bf16[264,1024]{1,0:T(8,128)(2,1)S(1)} %get-tuple-element.23.refs_0_.own_ref), channel_id=1, source_target_pairs={{0,1},{1,0},{2,3},{3,2},{4,5},{5,4},{6,7},{7,6},{8,9},{9,8},{10,11... | collective-permute-start | bytes 1622024 | tf_op jit(solution)/shard_map/ppermute | solution.py:236
  7.9 12.2 %collective-permute-start.3 = (bf16[128,1024]{1,0:T(8,128)(2,1)S(1)}, bf16[128,1024]{1,0:T(8,128)(2,1)S(1)}, u32[]{:S(2)}, u32[]{:S(2)}) collective-permute-start(bf16[128,1024]{1,0:T(8,128)(2,1)S(1)} %get-tuple-element.24), channel_id=1, source_target_pairs={{0,2},{1,3},{2,0},{3,1},{4,6},{5,7},{6,4},{7,5},{8,10},{9,11},{10,... | collective-permute-start | bytes 786440 | tf_op jit(solution)/shard_map/ppermute | solution.py:236
  8.8 11.4 %collective-permute-start.7 = (bf16[120,1024]{1,0:T(8,128)(2,1)S(1)}, bf16[120,1024]{1,0:T(8,128)(2,1)S(1)}, u32[]{:S(2)}, u32[]{:S(2)}) collective-permute-start(bf16[120,1024]{1,0:T(8,128)(2,1)S(1)} %get-tuple-element.29), channel_id=1, source_target_pairs={{4,0},{5,1},{6,2},{7,3},{8,4},{9,5},{10,6},{11,7},{12,8},{13,9},{1... | collective-permute-start | bytes 737288 | tf_op jit(solution)/shard_map/ppermute | solution.py:240
  13.6 11.7 %collective-permute-start.1 = (bf16[144,1024]{1,0:T(8,128)(2,1)S(1)}, bf16[144,1024]{1,0:T(8,128)(2,1)S(1)}, u32[]{:S(2)}, u32[]{:S(2)}) collective-permute-start(bf16[144,1024]{1,0:T(8,128)(2,1)S(1)} %collective-permute-done.head_ref), channel_id=1, source_target_pairs={{4,0},{5,1},{6,2},{7,3},{8,4},{9,5},{10,6},{11,7},{12,8},{13,9},{1... | collective-permute-start | bytes 884744 | tf_op jit(solution)/shard_map/ppermute | solution.py:240
  17.9 5.3 %collective-permute-start.6 = (bf16[136,1024]{1,0:T(8,128)(2,1)S(1)}, bf16[136,1024]{1,0:T(8,128)(2,1)S(1)}, u32[]{:S(2)}, u32[]{:S(2)}) collective-permute-start(bf16[136,1024]{1,0:T(8,128)(2,1)S(1)} %collective-permute-done.4.refs_3_), channel_id=1, source_target_pairs={{0,1},{1,0},{2,3},{3,2},{4,5},{5,4},{6,7},{7,6},{8,9},{9,8},{10,11... | collective-permute-start | bytes 835592 | tf_op jit(solution)/shard_map/ppermute | solution.py:236
  20.2 3.0 %collective-permute-start.5 = (bf16[128,1024]{1,0:T(8,128)(2,1)S(1)}, bf16[128,1024]{1,0:T(8,128)(2,1)S(1)}, u32[]{:S(2)}, u32[]{:S(2)}) collective-permute-start(bf16[128,1024]{1,0:T(8,128)(2,1)S(1)} %collective-permute-done.3.refs_2_), channel_id=1, source_target_pairs={{0,1},{1,0},{2,3},{3,2},{4,5},{5,4},{6,7},{7,6},{8,9},{9,8},{10,11... | collective-permute-start | bytes 786440 | tf_op jit(solution)/shard_map/ppermute | solution.py:236
  20.2 9.1 %collective-permute-start.8 = (bf16[120,1024]{1,0:T(8,128)(2,1)S(1)}, bf16[120,1024]{1,0:T(8,128)(2,1)S(1)}, u32[]{:S(2)}, u32[]{:S(2)}) collective-permute-start(bf16[120,1024]{1,0:T(8,128)(2,1)S(1)} %collective-permute-done.7.tail_ref), channel_id=1, source_target_pairs={{4,0},{5,1},{6,2},{7,3},{8,4},{9,5},{10,6},{11,7},{12,8},{13,9},{1... | collective-permute-start | bytes 737288 | tf_op jit(solution)/shard_map/ppermute | solution.py:240
  25.2 5.4 %collective-permute-start.9 = (f32[1,256]{1,0:T(1,128)S(1)}, f32[1,256]{1,0:T(1,128)S(1)}, u32[]{:S(2)}, u32[]{:S(2)}) collective-permute-start(f32[1,256]{1,0:T(1,128)S(1)} %get-tuple-element.35), channel_id=1, source_target_pairs={{0,4},{1,5},{2,6},{3,7},{4,8},{5,9},{6,10},{7,11},{8,12},{9,13},{1... | collective-permute-start | bytes 3080 | tf_op jit(solution)/shard_map/ppermute | solution.py:240
  30.6 1.9 %collective-permute-start.12 = (f32[1,256]{1,0:T(1,128)S(1)}, f32[1,256]{1,0:T(1,128)S(1)}, u32[]{:S(2)}, u32[]{:S(2)}) collective-permute-start(f32[1,256]{1,0:T(1,128)S(1)} %get-tuple-element.40), channel_id=1, source_target_pairs={{0,1},{1,0},{2,3},{3,2},{4,5},{5,4},{6,7},{7,6},{8,9},{9,8},{10,11... | collective-permute-start | bytes 3080 | tf_op jit(solution)/shard_map/ppermute | solution.py:236
  30.6 3.6 %collective-permute-start.10 = (f32[1,256]{1,0:T(1,128)S(1)}, f32[1,256]{1,0:T(1,128)S(1)}, u32[]{:S(2)}, u32[]{:S(2)}) collective-permute-start(f32[1,256]{1,0:T(1,128)S(1)} %get-tuple-element.38), channel_id=1, source_target_pairs={{0,2},{1,3},{2,0},{3,1},{4,6},{5,7},{6,4},{7,5},{8,10},{9,11},{10,... | collective-permute-start | bytes 3080 | tf_op jit(solution)/shard_map/ppermute | solution.py:236
  32.1 3.0 %collective-permute-start.11 = (f32[1,256]{1,0:T(1,128)S(1)}, f32[1,256]{1,0:T(1,128)S(1)}, u32[]{:S(2)}, u32[]{:S(2)}) collective-permute-start(f32[1,256]{1,0:T(1,128)S(1)} %get-tuple-element.39), channel_id=1, source_target_pairs={{0,3},{1,2},{2,1},{3,0},{4,7},{5,6},{6,5},{7,4},{8,11},{9,10},{10,... | collective-permute-start | bytes 3080 | tf_op jit(solution)/shard_map/ppermute | solution.py:236

commit v23 on v20

--- a/solution.py
+++ b/solution.py
@@ -294,7 +294,7 @@
     first_tail = on_line(tail, first_moves)
     across = [in_plane(piece, 2) for piece in pieces]
     sibling = in_plane(block, 1)
-    last_head = on_line(first_head, forward_moves + [(3, 1), (0, 0)])
+    last_head = on_line(first_head, first_moves)
     last_tail = on_line(first_tail, forward_moves)
     corner = [in_plane(piece, 1) for piece in across]
     queries = (block, sibling, *across, *corner)
@@ -326,7 +326,7 @@
 
 
 def on_device(embeddings, cluster_ids):
-    if lax.axis_size("gx") == 4 * PLANE and embeddings.shape[0] % (2 * LANES) == 0:
+    if lax.axis_size("gx") == 4 * PLANE and embeddings.shape[0] == 2 * LANES:
         return grid_plan(embeddings, cluster_ids)
     return plain_plan(embeddings, cluster_ids)
 

time: 35.7 us -> 35.7 us (level)
  starting transfers between devices: 14.1 us -> 13.4 us
  waiting for transfers between devices: 16.8 us -> 17.5 us
    ppermute x8, waiting for transfers between devices: 3.4 us -> 4.12 us  [in_plane(): return lax.ppermute(value, 'gx', [(i, i ^ step) for i in range(peers)])]
    ppermute x6, starting transfers between devices: 10 us -> 9.41 us  [on_line(): return lax.ppermute(value, 'gx', pairs)]
where the time goes in v23:
time: 35.7 us; the launch traced here: 35.5 us
  waiting for transfers between devices  17.5 us (49%)
  starting transfers between devices  13.4 us (38%)
  Pallas kernels  2.8 us (8%)
  local copies, waits for them, and re-layouts  1.06 us (3%)
  other arithmetic  0.58 us (2%)
    ppermute x6, waiting for transfers between devices, on_line(): return lax.ppermute(value, 'gx', pairs)  13.4 us
    ppermute x6, starting transfers between devices, on_line(): return lax.ppermute(value, 'gx', pairs)  9.41 us
    ppermute x8, waiting for transfers between devices, in_plane(): return lax.ppermute(value, 'gx', [(i, i ^ step) for i in range(peers)])  4.12 us
    ppermute x8, starting transfers between devices, in_plane(): return lax.ppermute(value, 'gx', [(i, i ^ step) for i in range(peers)])  4.02 us
    pallas_call x1, Pallas kernels, grid_plan(): pl.pallas_call(functools.partial(first_kernel, first_moves), out_shape=(l...  2.01 us
    slice x1, local copies, waits for them, and re-layouts, grid_plan(): first_head = on_line(embeddings[:part], first_moves)  1.05 us
  transfers between devices with their start and end apart: 14, of which 5 were waited for; matrix products, arithmetic and copies ran while one was open for 0% of the time, Pallas kernels for 8%

profile of v23, /device:TPU:0, one launch (start us, length us, event | category | flops | bytes accessed | tf_op | source)
XLA Modules:
  0.0 35.5 jit_solution(2934788607282959810)
XLA Ops:
  0.0 0.0 copy-start
  0.0 1.1 %slice.3 = bf16[144,1024]{1,0:T(8,128)(2,1)S(1)} slice(bf16[256,1024]{1,0:T(8,128)(2,1)} %rows_ref.1), slice={[0:144], [0:1024]} | slice | bytes 589824 | tf_op jit(solution)/shard_map/slice | solution.py:283
  1.1 0.0 copy-start.1
  1.1 3.1 %collective-permute-start = (bf16[144,1024]{1,0:T(8,128)(2,1)S(1)}, bf16[144,1024]{1,0:T(8,128)(2,1)S(1)}, u32[]{:S(2)}, u32[]{:S(2)}) collective-permute-start(bf16[144,1024]{1,0:T(8,128)(2,1)S(1)} %slice.3), channel_id=1, source_target_pairs={{0,4},{1,5},{2,6},{3,7},{4,8},{5,9},{6,10},{7,11},{8,12},{9,13},{1... | collective-permute-start | bytes 884744 | tf_op jit(solution)/shard_map/ppermute | solution.py:272
  4.1 0.0 copy-done
  4.2 0.0 copy-done.1
  4.2 0.2 shard_map.28
  4.4 1.6 %collective-permute-start.4 = (bf16[136,1024]{1,0:T(8,128)(2,1)S(1)}, bf16[136,1024]{1,0:T(8,128)(2,1)S(1)}, u32[]{:S(2)}, u32[]{:S(2)}) collective-permute-start(bf16[136,1024]{1,0:T(8,128)(2,1)S(1)} %get-tuple-element.26), channel_id=1, source_target_pairs={{0,2},{1,3},{2,0},{3,1},{4,6},{5,7},{6,4},{7,5},{8,10},{9,11},{10,... | collective-permute-start | bytes 835592 | tf_op jit(solution)/shard_map/ppermute | solution.py:268
  5.9 0.0 collective-permute-start.2
  5.9 0.5 %collective-permute-start.3 = (bf16[128,1024]{1,0:T(8,128)(2,1)S(1)}, bf16[128,1024]{1,0:T(8,128)(2,1)S(1)}, u32[]{:S(2)}, u32[]{:S(2)}) collective-permute-start(bf16[128,1024]{1,0:T(8,128)(2,1)S(1)} %get-tuple-element.25), channel_id=1, source_target_pairs={{0,2},{1,3},{2,0},{3,1},{4,6},{5,7},{6,4},{7,5},{8,10},{9,11},{10,... | collective-permute-start | bytes 786440 | tf_op jit(solution)/shard_map/ppermute | solution.py:268
  6.4 0.4 shard_map.30.own_mass_ref
  6.8 1.6 %collective-permute-start.7 = (bf16[120,1024]{1,0:T(8,128)(2,1)S(1)}, bf16[120,1024]{1,0:T(8,128)(2,1)S(1)}, u32[]{:S(2)}, u32[]{:S(2)}) collective-permute-start(bf16[120,1024]{1,0:T(8,128)(2,1)S(1)} %get-tuple-element.30), channel_id=1, source_target_pairs={{0,4},{1,5},{2,6},{3,7},{4,8},{5,9},{6,10},{7,11},{8,12},{9,13},{1... | collective-permute-start | bytes 737288 | tf_op jit(solution)/shard_map/ppermute | solution.py:272
  8.4 5.6 %collective-permute-done.head_ref = bf16[144,1024]{1,0:T(8,128)(2,1)S(1)} collective-permute-done((bf16[144,1024]{1,0:T(8,128)(2,1)S(1)}, bf16[144,1024]{1,0:T(8,128)(2,1)S(1)}, u32[]{:S(2)}, u32[]{:S(2)}) %collective-permute-start) | collective-permute-done | bytes 294944 | tf_op jit(solution)/shard_map/ppermute | solution.py:272
  14.0 0.0 collective-permute-start.1
  14.0 0.0 collective-permute-done.4.refs_3_
  14.0 0.0 collective-permute-start.6
  14.0 4.1 %collective-permute-done.3.refs_2_ = bf16[128,1024]{1,0:T(8,128)(2,1)S(1)} collective-permute-done((bf16[128,1024]{1,0:T(8,128)(2,1)S(1)}, bf16[128,1024]{1,0:T(8,128)(2,1)S(1)}, u32[]{:S(2)}, u32[]{:S(2)}) %collective-permute-start.3) | collective-permute-done | bytes 262176 | tf_op jit(solution)/shard_map/ppermute | solution.py:268
  18.2 0.0 collective-permute-start.5
  18.2 1.1 %collective-permute-done.7.tail_ref = bf16[120,1024]{1,0:T(8,128)(2,1)S(1)} collective-permute-done((bf16[120,1024]{1,0:T(8,128)(2,1)S(1)}, bf16[120,1024]{1,0:T(8,128)(2,1)S(1)}, u32[]{:S(2)}, u32[]{:S(2)}) %collective-permute-start.7) | collective-permute-done | bytes 245792 | tf_op jit(solution)/shard_map/ppermute | solution.py:272
  19.3 0.7 %collective-permute-start.8 = (bf16[120,1024]{1,0:T(8,128)(2,1)S(1)}, bf16[120,1024]{1,0:T(8,128)(2,1)S(1)}, u32[]{:S(2)}, u32[]{:S(2)}) collective-permute-start(bf16[120,1024]{1,0:T(8,128)(2,1)S(1)} %collective-permute-done.7.tail_ref), channel_id=1, source_target_pairs={{4,8},{5,9},{6,10},{7,11},{8,12},{9,13},{10,14},{11,15},{20,24},{2... | collective-permute-start | bytes 737288 | tf_op jit(solution)/shard_map/ppermute | solution.py:272
  19.9 0.0 collective-permute-done.5.refs_4_
  20.0 0.0 collective-permute-done.2.refs_1_
  20.0 0.0 collective-permute-done.6.refs_5_
  20.0 2.0 %shard_map.31 = (f32[1024,128]{1,0:T(8,128)S(1)}, f32[1,256]{1,0:T(1,128)S(1)}, f32[1024,128]{1,0:T(8,128)S(1)}, f32[1,256]{1,0:T(1,128)S(1)}) custom-call(f32[1,256]{1,0:T(1,128)S(1)} %shard_map.30.own_mass_ref, bf16[144,1024]{1,0:T(8,128)(2,1)S(1)} %collective-permute-done.head_ref, bf16[120,1024]{1,0:T(8,128)(2,1)S(1)} %collective-permute-done.7.tail_ref, ...), custom_call_target="tpu_custom_call" | custom-call | flops 1 | bytes 1 | tf_op jit(solution)/shard_map/pallas_call | solution.py:301
  22.0 2.7 %collective-permute-start.9 = (f32[1,256]{1,0:T(1,128)S(1)}, f32[1,256]{1,0:T(1,128)S(1)}, u32[]{:S(2)}, u32[]{:S(2)}) collective-permute-start(f32[1,256]{1,0:T(1,128)S(1)} %get-tuple-element.36), channel_id=1, source_target_pairs={{4,0},{5,1},{6,2},{7,3},{8,4},{9,5},{10,6},{11,7},{12,8},{13,9},{1... | collective-permute-start | bytes 3080 | tf_op jit(solution)/shard_map/ppermute | solution.py:272
  24.7 0.0 collective-permute-done.1.head_ref
  24.8 0.0 collective-permute-done.8.tail_ref
  24.8 0.2 shard_map.32
  25.0 1.9 %collective-permute-done.9 = f32[1,256]{1,0:T(1,128)S(1)} collective-permute-done((f32[1,256]{1,0:T(1,128)S(1)}, f32[1,256]{1,0:T(1,128)S(1)}, u32[]{:S(2)}, u32[]{:S(2)}) %collective-permute-start.9) | collective-permute-done | bytes 1056 | tf_op jit(solution)/shard_map/ppermute | solution.py:272
  26.9 0.0 collective-permute-start.13
  26.9 1.3 %collective-permute-start.10 = (f32[1,256]{1,0:T(1,128)S(1)}, f32[1,256]{1,0:T(1,128)S(1)}, u32[]{:S(2)}, u32[]{:S(2)}) collective-permute-start(f32[1,256]{1,0:T(1,128)S(1)} %get-tuple-element.39), channel_id=1, source_target_pairs={{8,0},{9,1},{10,2},{11,3},{12,4},{13,5},{14,6},{15,7},{24,16},{25,... | collective-permute-start | bytes 3080 | tf_op jit(solution)/shard_map/ppermute | solution.py:272
  28.2 1.6 %collective-permute-start.11 = (f32[1,256]{1,0:T(1,128)S(1)}, f32[1,256]{1,0:T(1,128)S(1)}, u32[]{:S(2)}, u32[]{:S(2)}) collective-permute-start(f32[1,256]{1,0:T(1,128)S(1)} %get-tuple-element.40), channel_id=1, source_target_pairs={{0,2},{1,3},{2,0},{3,1},{4,6},{5,7},{6,4},{7,5},{8,10},{9,11},{10,... | collective-permute-start | bytes 3080 | tf_op jit(solution)/shard_map/ppermute | solution.py:268
  29.7 0.4 %collective-permute-start.12 = (f32[1,256]{1,0:T(1,128)S(1)}, f32[1,256]{1,0:T(1,128)S(1)}, u32[]{:S(2)}, u32[]{:S(2)}) collective-permute-start(f32[1,256]{1,0:T(1,128)S(1)} %get-tuple-element.41), channel_id=1, source_target_pairs={{0,3},{1,2},{2,1},{3,0},{4,7},{5,6},{6,5},{7,4},{8,11},{9,10},{10,... | collective-permute-start | bytes 3080 | tf_op jit(solution)/shard_map/ppermute | solution.py:268
  30.1 0.0 collective-permute-done.13
  30.1 4.8 %collective-permute-done.10 = f32[1,256]{1,0:T(1,128)S(1)} collective-permute-done((f32[1,256]{1,0:T(1,128)S(1)}, f32[1,256]{1,0:T(1,128)S(1)}, u32[]{:S(2)}, u32[]{:S(2)}) %collective-permute-start.10) | collective-permute-done | bytes 1056 | tf_op jit(solution)/shard_map/ppermute | solution.py:272
  34.9 0.0 collective-permute-done.11
  34.9 0.0 collective-permute-done.12
  34.9 0.6 %add_log-plus-one_fusion = f32[1,256]{1,0:T(1,128)} fusion(f32[1,256]{1,0:T(1,128)S(1)} %collective-permute-done.13, f32[1,256]{1,0:T(1,128)S(1)} %collective-permute-done.12, f32[1,256]{1,0:T(1,128)S(1)} %collective-permute-done.11, f32[1,256]{1,0:T(1,128)S(1)} %collective-permute-done.10, f32[1,256]{1,0:T(1,128)S(1)} %get-tuple-element.35, ...), kind=kLoop, calls=%fused_computation | loop fusion | flops 1280 | bytes 7168 | tf_op jit(solution)/shard_map/log1p | solution.py:325
  (1 shorter events, 0.0 us)
Async XLA Ops:
  0.0 4.1 %copy-start = (bf16[256,1024]{1,0:T(8,128)(2,1)S(1)}, bf16[256,1024]{1,0:T(8,128)(2,1)}, u32[]{:S(2)}) copy-start(bf16[256,1024]{1,0:T(8,128)(2,1)} %rows_ref.1) | copy-start | bytes 1572868
  1.1 3.1 %copy-start.1 = (s32[256]{0:T(256)S(1)}, s32[256]{0:T(256)}, u32[]{:S(2)}) copy-start(s32[256]{0:T(256)} %param.3) | copy-start | bytes 3076
  1.1 12.9 %collective-permute-start = (bf16[144,1024]{1,0:T(8,128)(2,1)S(1)}, bf16[144,1024]{1,0:T(8,128)(2,1)S(1)}, u32[]{:S(2)}, u32[]{:S(2)}) collective-permute-start(bf16[144,1024]{1,0:T(8,128)(2,1)S(1)} %slice.3), channel_id=1, source_target_pairs={{0,4},{1,5},{2,6},{3,7},{4,8},{5,9},{6,10},{7,11},{8,12},{9,13},{1... | collective-permute-start | bytes 884744 | tf_op jit(solution)/shard_map/ppermute | solution.py:272
  4.4 9.7 %collective-permute-start.4 = (bf16[136,1024]{1,0:T(8,128)(2,1)S(1)}, bf16[136,1024]{1,0:T(8,128)(2,1)S(1)}, u32[]{:S(2)}, u32[]{:S(2)}) collective-permute-start(bf16[136,1024]{1,0:T(8,128)(2,1)S(1)} %get-tuple-element.26), channel_id=1, source_target_pairs={{0,2},{1,3},{2,0},{3,1},{4,6},{5,7},{6,4},{7,5},{8,10},{9,11},{10,... | collective-permute-start | bytes 835592 | tf_op jit(solution)/shard_map/ppermute | solution.py:268
  5.9 14.1 %collective-permute-start.2 = (bf16[264,1024]{1,0:T(8,128)(2,1)S(1)}, bf16[264,1024]{1,0:T(8,128)(2,1)S(1)}, u32[]{:S(2)}, u32[]{:S(2)}) collective-permute-start(bf16[264,1024]{1,0:T(8,128)(2,1)S(1)} %get-tuple-element.24.refs_0_.own_ref), channel_id=1, source_target_pairs={{0,1},{1,0},{2,3},{3,2},{4,5},{5,4},{6,7},{7,6},{8,9},{9,8},{10,11... | collective-permute-start | bytes 1622024 | tf_op jit(solution)/shard_map/ppermute | solution.py:268
  5.9 12.2 %collective-permute-start.3 = (bf16[128,1024]{1,0:T(8,128)(2,1)S(1)}, bf16[128,1024]{1,0:T(8,128)(2,1)S(1)}, u32[]{:S(2)}, u32[]{:S(2)}) collective-permute-start(bf16[128,1024]{1,0:T(8,128)(2,1)S(1)} %get-tuple-element.25), channel_id=1, source_target_pairs={{0,2},{1,3},{2,0},{3,1},{4,6},{5,7},{6,4},{7,5},{8,10},{9,11},{10,... | collective-permute-start | bytes 786440 | tf_op jit(solution)/shard_map/ppermute | solution.py:268
  6.8 12.5 %collective-permute-start.7 = (bf16[120,1024]{1,0:T(8,128)(2,1)S(1)}, bf16[120,1024]{1,0:T(8,128)(2,1)S(1)}, u32[]{:S(2)}, u32[]{:S(2)}) collective-permute-start(bf16[120,1024]{1,0:T(8,128)(2,1)S(1)} %get-tuple-element.30), channel_id=1, source_target_pairs={{0,4},{1,5},{2,6},{3,7},{4,8},{5,9},{6,10},{7,11},{8,12},{9,13},{1... | collective-permute-start | bytes 737288 | tf_op jit(solution)/shard_map/ppermute | solution.py:272
  14.0 10.8 %collective-permute-start.1 = (bf16[144,1024]{1,0:T(8,128)(2,1)S(1)}, bf16[144,1024]{1,0:T(8,128)(2,1)S(1)}, u32[]{:S(2)}, u32[]{:S(2)}) collective-permute-start(bf16[144,1024]{1,0:T(8,128)(2,1)S(1)} %collective-permute-done.head_ref), channel_id=1, source_target_pairs={{0,4},{1,5},{2,6},{3,7},{4,8},{5,9},{6,10},{7,11},{8,12},{9,13},{1... | collective-permute-start | bytes 884744 | tf_op jit(solution)/shard_map/ppermute | solution.py:272
  14.0 5.9 %collective-permute-start.6 = (bf16[136,1024]{1,0:T(8,128)(2,1)S(1)}, bf16[136,1024]{1,0:T(8,128)(2,1)S(1)}, u32[]{:S(2)}, u32[]{:S(2)}) collective-permute-start(bf16[136,1024]{1,0:T(8,128)(2,1)S(1)} %collective-permute-done.4.refs_3_), channel_id=1, source_target_pairs={{0,1},{1,0},{2,3},{3,2},{4,5},{5,4},{6,7},{7,6},{8,9},{9,8},{10,11... | collective-permute-start | bytes 835592 | tf_op jit(solution)/shard_map/ppermute | solution.py:268
  18.2 1.8 %collective-permute-start.5 = (bf16[128,1024]{1,0:T(8,128)(2,1)S(1)}, bf16[128,1024]{1,0:T(8,128)(2,1)S(1)}, u32[]{:S(2)}, u32[]{:S(2)}) collective-permute-start(bf16[128,1024]{1,0:T(8,128)(2,1)S(1)} %collective-permute-done.3.refs_2_), channel_id=1, source_target_pairs={{0,1},{1,0},{2,3},{3,2},{4,5},{5,4},{6,7},{7,6},{8,9},{9,8},{10,11... | collective-permute-start | bytes 786440 | tf_op jit(solution)/shard_map/ppermute | solution.py:268
  19.3 5.5 %collective-permute-start.8 = (bf16[120,1024]{1,0:T(8,128)(2,1)S(1)}, bf16[120,1024]{1,0:T(8,128)(2,1)S(1)}, u32[]{:S(2)}, u32[]{:S(2)}) collective-permute-start(bf16[120,1024]{1,0:T(8,128)(2,1)S(1)} %collective-permute-done.7.tail_ref), channel_id=1, source_target_pairs={{4,8},{5,9},{6,10},{7,11},{8,12},{9,13},{10,14},{11,15},{20,24},{2... | collective-permute-start | bytes 737288 | tf_op jit(solution)/shard_map/ppermute | solution.py:272
  22.0 4.9 %collective-permute-start.9 = (f32[1,256]{1,0:T(1,128)S(1)}, f32[1,256]{1,0:T(1,128)S(1)}, u32[]{:S(2)}, u32[]{:S(2)}) collective-permute-start(f32[1,256]{1,0:T(1,128)S(1)} %get-tuple-element.36), channel_id=1, source_target_pairs={{4,0},{5,1},{6,2},{7,3},{8,4},{9,5},{10,6},{11,7},{12,8},{13,9},{1... | collective-permute-start | bytes 3080 | tf_op jit(solution)/shard_map/ppermute | solution.py:272
  26.9 3.2 %collective-permute-start.13 = (f32[1,256]{1,0:T(1,128)S(1)}, f32[1,256]{1,0:T(1,128)S(1)}, u32[]{:S(2)}, u32[]{:S(2)}) collective-permute-start(f32[1,256]{1,0:T(1,128)S(1)} %get-tuple-element.42), channel_id=1, source_target_pairs={{0,1},{1,0},{2,3},{3,2},{4,5},{5,4},{6,7},{7,6},{8,9},{9,8},{10,11... | collective-permute-start | bytes 3080 | tf_op jit(solution)/shard_map/ppermute | solution.py:268
  26.9 8.0 %collective-permute-start.10 = (f32[1,256]{1,0:T(1,128)S(1)}, f32[1,256]{1,0:T(1,128)S(1)}, u32[]{:S(2)}, u32[]{:S(2)}) collective-permute-start(f32[1,256]{1,0:T(1,128)S(1)} %get-tuple-element.39), channel_id=1, source_target_pairs={{8,0},{9,1},{10,2},{11,3},{12,4},{13,5},{14,6},{15,7},{24,16},{25,... | collective-permute-start | bytes 3080 | tf_op jit(solution)/shard_map/ppermute | solution.py:272
  28.2 6.7 %collective-permute-start.11 = (f32[1,256]{1,0:T(1,128)S(1)}, f32[1,256]{1,0:T(1,128)S(1)}, u32[]{:S(2)}, u32[]{:S(2)}) collective-permute-start(f32[1,256]{1,0:T(1,128)S(1)} %get-tuple-element.40), channel_id=1, source_target_pairs={{0,2},{1,3},{2,0},{3,1},{4,6},{5,7},{6,4},{7,5},{8,10},{9,11},{10,... | collective-permute-start | bytes 3080 | tf_op jit(solution)/shard_map/ppermute | solution.py:268
  29.7 5.2 %collective-permute-start.12 = (f32[1,256]{1,0:T(1,128)S(1)}, f32[1,256]{1,0:T(1,128)S(1)}, u32[]{:S(2)}, u32[]{:S(2)}) collective-permute-start(f32[1,256]{1,0:T(1,128)S(1)} %get-tuple-element.41), channel_id=1, source_target_pairs={{0,3},{1,2},{2,1},{3,0},{4,7},{5,6},{6,5},{7,4},{8,11},{9,10},{10,... | collective-permute-start | bytes 3080 | tf_op jit(solution)/shard_map/ppermute | solution.py:268

commit v24 on v23

--- a/solution.py
+++ b/solution.py
@@ -212,9 +212,8 @@
             first += size
 
 
-def last_kernel(moves, powers_ref, rest_ref, tail_ref, ids_ref, earlier_ref, mass_ref, *refs):
-    query_refs, refs = refs[: -PLANE - 2], refs[-PLANE - 2 :]
-    column_ref, row_refs, sums_ref = refs[0], refs[1:-1], refs[-1]
+def last_kernel(moves, powers_ref, rest_ref, tail_ref, ids_ref, earlier_ref, *refs):
+    query_refs, (column_ref, sums_ref) = refs[:-2], refs[-2:]
     rows = column_ref.shape[1]
     cut = powers_ref.shape[1]
     arrived = arrived_at(moves)
@@ -247,6 +246,9 @@
         column_ref[...] = jnp.zeros_like(column_ref)
         sums_ref[...] = earlier_ref[...]
 
+
+def fold_kernel(sums_ref, mass_ref, *row_refs):
+    rows = mass_ref.shape[1]
     for m in range(PLANE):
         row_sum = jnp.sum(sums_ref[pl.ds(m * rows, rows), :].T, axis=0, keepdims=True)
         row_refs[m][...] = row_sum + mass_ref[...] if m == 0 else row_sum
@@ -313,13 +315,19 @@
         cost_estimate=small,
         compiler_params=params,
     )(last_head, *queries)
-    last_column, *row_sums = pl.pallas_call(
+    last_column, sums = pl.pallas_call(
         functools.partial(last_kernel, last_moves),
-        out_shape=[vector] * (1 + PLANE),
-        scratch_shapes=[pltpu.VMEM(lanes.shape, lanes.dtype)],
-        compiler_params=params,
-    )(powers, rest, last_tail, ids, first_sums, mass, *queries)
-    returned_first, row_sums[1] = lax.optimization_barrier((returned_first, row_sums[1]))
+        out_shape=(vector, lanes),
+        cost_estimate=small,
+        compiler_params=params,
+    )(powers, rest, last_tail, ids, first_sums, *queries)
+    returned_first, last_column = lax.optimization_barrier((returned_first, last_column))
+    row_sums = pl.pallas_call(
+        fold_kernel,
+        out_shape=[vector] * PLANE,
+        cost_estimate=small,
+        compiler_params=params,
+    )(sums, mass)
     returned = [on_line(last_column, last_back)]
     returned += [in_plane(row_sums[step], step) for step in (2, 3, 1)]
     return jnp.log1p(sum(returned, row_sums[0] + returned_first)).reshape(row_count)

time: 35.7 us -> 35.4 us (level)
  waiting for transfers between devices: 17.5 us -> 17 us
    ppermute x6, waiting for transfers between devices: 13.4 us -> 12.8 us  [on_line(): return lax.ppermute(value, 'gx', pairs)]
where the time goes in v24:
time: 35.4 us; the launch traced here: 35.2 us
  waiting for transfers between devices  17 us (48%)
  starting transfers between devices  13.7 us (39%)
  Pallas kernels  2.81 us (8%)
  local copies, waits for them, and re-layouts  1.06 us (3%)
  other arithmetic  0.58 us (2%)
    ppermute x6, waiting for transfers between devices, on_line(): return lax.ppermute(value, 'gx', pairs)  12.8 us
    ppermute x6, starting transfers between devices, on_line(): return lax.ppermute(value, 'gx', pairs)  9.41 us
    ppermute x8, starting transfers between devices, in_plane(): return lax.ppermute(value, 'gx', [(i, i ^ step) for i in range(peers)])  4.31 us
    ppermute x8, waiting for transfers between devices, in_plane(): return lax.ppermute(value, 'gx', [(i, i ^ step) for i in range(peers)])  4.12 us
    pallas_call x1, Pallas kernels, grid_plan(): pl.pallas_call(functools.partial(first_kernel, first_moves), out_shape=(l...  2.02 us
    slice x1, local copies, waits for them, and re-layouts, grid_plan(): first_head = on_line(embeddings[:part], first_moves)  1.05 us
  transfers between devices with their start and end apart: 14, of which 5 were waited for; matrix products, arithmetic and copies ran while one was open for 0% of the time, Pallas kernels for 8%

profile of v24, /device:TPU:0, one launch (start us, length us, event | category | flops | bytes accessed | tf_op | source)
XLA Modules:
  0.0 35.2 jit_solution(10166325214794034788)
XLA Ops:
  0.0 0.0 copy-start
  0.0 1.1 %slice.3 = bf16[144,1024]{1,0:T(8,128)(2,1)S(1)} slice(bf16[256,1024]{1,0:T(8,128)(2,1)} %rows_ref.1), slice={[0:144], [0:1024]} | slice | bytes 589824 | tf_op jit(solution)/shard_map/slice | solution.py:285
  1.1 0.0 copy-start.1
  1.1 3.1 %collective-permute-start = (bf16[144,1024]{1,0:T(8,128)(2,1)S(1)}, bf16[144,1024]{1,0:T(8,128)(2,1)S(1)}, u32[]{:S(2)}, u32[]{:S(2)}) collective-permute-start(bf16[144,1024]{1,0:T(8,128)(2,1)S(1)} %slice.3), channel_id=1, source_target_pairs={{0,4},{1,5},{2,6},{3,7},{4,8},{5,9},{6,10},{7,11},{8,12},{9,13},{1... | collective-permute-start | bytes 884744 | tf_op jit(solution)/shard_map/ppermute | solution.py:274
  4.1 0.0 copy-done
  4.2 0.0 copy-done.1
  4.2 0.2 shard_map.28
  4.4 1.6 %collective-permute-start.4 = (bf16[136,1024]{1,0:T(8,128)(2,1)S(1)}, bf16[136,1024]{1,0:T(8,128)(2,1)S(1)}, u32[]{:S(2)}, u32[]{:S(2)}) collective-permute-start(bf16[136,1024]{1,0:T(8,128)(2,1)S(1)} %get-tuple-element.27), channel_id=1, source_target_pairs={{0,2},{1,3},{2,0},{3,1},{4,6},{5,7},{6,4},{7,5},{8,10},{9,11},{10,... | collective-permute-start | bytes 835592 | tf_op jit(solution)/shard_map/ppermute | solution.py:270
  5.9 0.0 collective-permute-start.2
  5.9 0.5 %collective-permute-start.3 = (bf16[128,1024]{1,0:T(8,128)(2,1)S(1)}, bf16[128,1024]{1,0:T(8,128)(2,1)S(1)}, u32[]{:S(2)}, u32[]{:S(2)}) collective-permute-start(bf16[128,1024]{1,0:T(8,128)(2,1)S(1)} %get-tuple-element.26), channel_id=1, source_target_pairs={{0,2},{1,3},{2,0},{3,1},{4,6},{5,7},{6,4},{7,5},{8,10},{9,11},{10,... | collective-permute-start | bytes 786440 | tf_op jit(solution)/shard_map/ppermute | solution.py:270
  6.4 0.4 %shard_map.30.own_mass_ref = f32[1,256]{1,0:T(1,128)S(1)} custom-call(bf16[264,1024]{1,0:T(8,128)(2,1)S(1)} %get-tuple-element.25.refs_0_.own_ref), custom_call_target="tpu_custom_call" | custom-call | flops 1 | bytes 1 | tf_op jit(solution)/shard_map/pallas_call | solution.py:292
  6.8 1.6 %collective-permute-start.7 = (bf16[120,1024]{1,0:T(8,128)(2,1)S(1)}, bf16[120,1024]{1,0:T(8,128)(2,1)S(1)}, u32[]{:S(2)}, u32[]{:S(2)}) collective-permute-start(bf16[120,1024]{1,0:T(8,128)(2,1)S(1)} %get-tuple-element.31), channel_id=1, source_target_pairs={{0,4},{1,5},{2,6},{3,7},{4,8},{5,9},{6,10},{7,11},{8,12},{9,13},{1... | collective-permute-start | bytes 737288 | tf_op jit(solution)/shard_map/ppermute | solution.py:274
  8.4 5.6 %collective-permute-done.head_ref = bf16[144,1024]{1,0:T(8,128)(2,1)S(1)} collective-permute-done((bf16[144,1024]{1,0:T(8,128)(2,1)S(1)}, bf16[144,1024]{1,0:T(8,128)(2,1)S(1)}, u32[]{:S(2)}, u32[]{:S(2)}) %collective-permute-start) | collective-permute-done | bytes 294944 | tf_op jit(solution)/shard_map/ppermute | solution.py:274
  14.0 0.0 collective-permute-start.1
  14.0 0.0 collective-permute-done.4.refs_3_
  14.0 0.0 collective-permute-start.6
  14.0 4.1 %collective-permute-done.3.refs_2_ = bf16[128,1024]{1,0:T(8,128)(2,1)S(1)} collective-permute-done((bf16[128,1024]{1,0:T(8,128)(2,1)S(1)}, bf16[128,1024]{1,0:T(8,128)(2,1)S(1)}, u32[]{:S(2)}, u32[]{:S(2)}) %collective-permute-start.3) | collective-permute-done | bytes 262176 | tf_op jit(solution)/shard_map/ppermute | solution.py:270
  18.2 0.0 collective-permute-start.5
  18.2 1.1 %collective-permute-done.7.tail_ref = bf16[120,1024]{1,0:T(8,128)(2,1)S(1)} collective-permute-done((bf16[120,1024]{1,0:T(8,128)(2,1)S(1)}, bf16[120,1024]{1,0:T(8,128)(2,1)S(1)}, u32[]{:S(2)}, u32[]{:S(2)}) %collective-permute-start.7) | collective-permute-done | bytes 245792 | tf_op jit(solution)/shard_map/ppermute | solution.py:274
  19.3 0.7 %collective-permute-start.8 = (bf16[120,1024]{1,0:T(8,128)(2,1)S(1)}, bf16[120,1024]{1,0:T(8,128)(2,1)S(1)}, u32[]{:S(2)}, u32[]{:S(2)}) collective-permute-start(bf16[120,1024]{1,0:T(8,128)(2,1)S(1)} %collective-permute-done.7.tail_ref), channel_id=1, source_target_pairs={{4,8},{5,9},{6,10},{7,11},{8,12},{9,13},{10,14},{11,15},{20,24},{2... | collective-permute-start | bytes 737288 | tf_op jit(solution)/shard_map/ppermute | solution.py:274
  19.9 0.0 collective-permute-done.5.refs_4_
  20.0 0.0 collective-permute-done.2.refs_1_
  20.0 0.0 collective-permute-done.6.refs_5_
  20.0 2.0 %shard_map.31 = (f32[1024,128]{1,0:T(8,128)S(1)}, f32[1,256]{1,0:T(1,128)S(1)}, f32[1024,128]{1,0:T(8,128)S(1)}, f32[1,256]{1,0:T(1,128)S(1)}) custom-call(f32[1,256]{1,0:T(1,128)S(1)} %shard_map.30.own_mass_ref, bf16[144,1024]{1,0:T(8,128)(2,1)S(1)} %collective-permute-done.head_ref, bf16[120,1024]{1,0:T(8,128)(2,1)S(1)} %collective-permute-done.7.tail_ref, ...), custom_call_target="tpu_custom_call" | custom-call | flops 1 | bytes 1 | tf_op jit(solution)/shard_map/pallas_call | solution.py:303
  22.0 2.7 %collective-permute-start.9 = (f32[1,256]{1,0:T(1,128)S(1)}, f32[1,256]{1,0:T(1,128)S(1)}, u32[]{:S(2)}, u32[]{:S(2)}) collective-permute-start(f32[1,256]{1,0:T(1,128)S(1)} %get-tuple-element.38), channel_id=1, source_target_pairs={{4,0},{5,1},{6,2},{7,3},{8,4},{9,5},{10,6},{11,7},{12,8},{13,9},{1... | collective-permute-start | bytes 3080 | tf_op jit(solution)/shard_map/ppermute | solution.py:274
  24.7 0.0 collective-permute-done.1.head_ref
  24.8 0.0 collective-permute-done.8.tail_ref
  24.8 2.1 %collective-permute-done.9 = f32[1,256]{1,0:T(1,128)S(1)} collective-permute-done((f32[1,256]{1,0:T(1,128)S(1)}, f32[1,256]{1,0:T(1,128)S(1)}, u32[]{:S(2)}, u32[]{:S(2)}) %collective-permute-start.9) | collective-permute-done | bytes 1056 | tf_op jit(solution)/shard_map/ppermute | solution.py:274
  26.9 1.3 %collective-permute-start.10 = (f32[1,256]{1,0:T(1,128)S(1)}, f32[1,256]{1,0:T(1,128)S(1)}, u32[]{:S(2)}, u32[]{:S(2)}) collective-permute-start(f32[1,256]{1,0:T(1,128)S(1)} %get-tuple-element.41), channel_id=1, source_target_pairs={{8,0},{9,1},{10,2},{11,3},{12,4},{13,5},{14,6},{15,7},{24,16},{25,... | collective-permute-start | bytes 3080 | tf_op jit(solution)/shard_map/ppermute | solution.py:274
  28.2 0.2 shard_map.33
  28.4 1.6 %collective-permute-start.11 = (f32[1,256]{1,0:T(1,128)S(1)}, f32[1,256]{1,0:T(1,128)S(1)}, u32[]{:S(2)}, u32[]{:S(2)}) collective-permute-start(f32[1,256]{1,0:T(1,128)S(1)} %get-tuple-element.42), channel_id=1, source_target_pairs={{0,2},{1,3},{2,0},{3,1},{4,6},{5,7},{6,4},{7,5},{8,10},{9,11},{10,... | collective-permute-start | bytes 3080 | tf_op jit(solution)/shard_map/ppermute | solution.py:270
  29.9 0.0 collective-permute-start.12
  29.9 0.6 %collective-permute-start.13 = (f32[1,256]{1,0:T(1,128)S(1)}, f32[1,256]{1,0:T(1,128)S(1)}, u32[]{:S(2)}, u32[]{:S(2)}) collective-permute-start(f32[1,256]{1,0:T(1,128)S(1)} %get-tuple-element.44), channel_id=1, source_target_pairs={{0,1},{1,0},{2,3},{3,2},{4,5},{5,4},{6,7},{7,6},{8,9},{9,8},{10,11... | collective-permute-start | bytes 3080 | tf_op jit(solution)/shard_map/ppermute | solution.py:270
  30.6 4.0 %collective-permute-done.10 = f32[1,256]{1,0:T(1,128)S(1)} collective-permute-done((f32[1,256]{1,0:T(1,128)S(1)}, f32[1,256]{1,0:T(1,128)S(1)}, u32[]{:S(2)}, u32[]{:S(2)}) %collective-permute-start.10) | collective-permute-done | bytes 1056 | tf_op jit(solution)/shard_map/ppermute | solution.py:274
  34.6 0.0 collective-permute-done.11
  34.6 0.0 collective-permute-done.12
  34.6 0.0 collective-permute-done.13
  34.6 0.6 %add_log-plus-one_fusion = f32[1,256]{1,0:T(1,128)} fusion(f32[1,256]{1,0:T(1,128)S(1)} %collective-permute-done.13, f32[1,256]{1,0:T(1,128)S(1)} %collective-permute-done.12, f32[1,256]{1,0:T(1,128)S(1)} %collective-permute-done.11, f32[1,256]{1,0:T(1,128)S(1)} %collective-permute-done.10, f32[1,256]{1,0:T(1,128)S(1)} %get-tuple-element.37, ...), kind=kLoop, calls=%fused_computation | loop fusion | flops 1280 | bytes 7168 | tf_op jit(solution)/shard_map/log1p | solution.py:333
  (2 shorter events, 0.0 us)
Async XLA Ops:
  0.0 4.1 %copy-start = (bf16[256,1024]{1,0:T(8,128)(2,1)S(1)}, bf16[256,1024]{1,0:T(8,128)(2,1)}, u32[]{:S(2)}) copy-start(bf16[256,1024]{1,0:T(8,128)(2,1)} %rows_ref.1) | copy-start | bytes 1572868
  1.1 3.1 %copy-start.1 = (s32[256]{0:T(256)S(1)}, s32[256]{0:T(256)}, u32[]{:S(2)}) copy-start(s32[256]{0:T(256)} %param.3) | copy-start | bytes 3076
  1.1 12.9 %collective-permute-start = (bf16[144,1024]{1,0:T(8,128)(2,1)S(1)}, bf16[144,1024]{1,0:T(8,128)(2,1)S(1)}, u32[]{:S(2)}, u32[]{:S(2)}) collective-permute-start(bf16[144,1024]{1,0:T(8,128)(2,1)S(1)} %slice.3), channel_id=1, source_target_pairs={{0,4},{1,5},{2,6},{3,7},{4,8},{5,9},{6,10},{7,11},{8,12},{9,13},{1... | collective-permute-start | bytes 884744 | tf_op jit(solution)/shard_map/ppermute | solution.py:274
  4.4 9.7 %collective-permute-start.4 = (bf16[136,1024]{1,0:T(8,128)(2,1)S(1)}, bf16[136,1024]{1,0:T(8,128)(2,1)S(1)}, u32[]{:S(2)}, u32[]{:S(2)}) collective-permute-start(bf16[136,1024]{1,0:T(8,128)(2,1)S(1)} %get-tuple-element.27), channel_id=1, source_target_pairs={{0,2},{1,3},{2,0},{3,1},{4,6},{5,7},{6,4},{7,5},{8,10},{9,11},{10,... | collective-permute-start | bytes 835592 | tf_op jit(solution)/shard_map/ppermute | solution.py:270
  5.9 14.1 %collective-permute-start.2 = (bf16[264,1024]{1,0:T(8,128)(2,1)S(1)}, bf16[264,1024]{1,0:T(8,128)(2,1)S(1)}, u32[]{:S(2)}, u32[]{:S(2)}) collective-permute-start(bf16[264,1024]{1,0:T(8,128)(2,1)S(1)} %get-tuple-element.25.refs_0_.own_ref), channel_id=1, source_target_pairs={{0,1},{1,0},{2,3},{3,2},{4,5},{5,4},{6,7},{7,6},{8,9},{9,8},{10,11... | collective-permute-start | bytes 1622024 | tf_op jit(solution)/shard_map/ppermute | solution.py:270
  5.9 12.2 %collective-permute-start.3 = (bf16[128,1024]{1,0:T(8,128)(2,1)S(1)}, bf16[128,1024]{1,0:T(8,128)(2,1)S(1)}, u32[]{:S(2)}, u32[]{:S(2)}) collective-permute-start(bf16[128,1024]{1,0:T(8,128)(2,1)S(1)} %get-tuple-element.26), channel_id=1, source_target_pairs={{0,2},{1,3},{2,0},{3,1},{4,6},{5,7},{6,4},{7,5},{8,10},{9,11},{10,... | collective-permute-start | bytes 786440 | tf_op jit(solution)/shard_map/ppermute | solution.py:270
  6.8 12.5 %collective-permute-start.7 = (bf16[120,1024]{1,0:T(8,128)(2,1)S(1)}, bf16[120,1024]{1,0:T(8,128)(2,1)S(1)}, u32[]{:S(2)}, u32[]{:S(2)}) collective-permute-start(bf16[120,1024]{1,0:T(8,128)(2,1)S(1)} %get-tuple-element.31), channel_id=1, source_target_pairs={{0,4},{1,5},{2,6},{3,7},{4,8},{5,9},{6,10},{7,11},{8,12},{9,13},{1... | collective-permute-start | bytes 737288 | tf_op jit(solution)/shard_map/ppermute | solution.py:274
  14.0 10.8 %collective-permute-start.1 = (bf16[144,1024]{1,0:T(8,128)(2,1)S(1)}, bf16[144,1024]{1,0:T(8,128)(2,1)S(1)}, u32[]{:S(2)}, u32[]{:S(2)}) collective-permute-start(bf16[144,1024]{1,0:T(8,128)(2,1)S(1)} %collective-permute-done.head_ref), channel_id=1, source_target_pairs={{0,4},{1,5},{2,6},{3,7},{4,8},{5,9},{6,10},{7,11},{8,12},{9,13},{1... | collective-permute-start | bytes 884744 | tf_op jit(solution)/shard_map/ppermute | solution.py:274
  14.0 5.9 %collective-permute-start.6 = (bf16[136,1024]{1,0:T(8,128)(2,1)S(1)}, bf16[136,1024]{1,0:T(8,128)(2,1)S(1)}, u32[]{:S(2)}, u32[]{:S(2)}) collective-permute-start(bf16[136,1024]{1,0:T(8,128)(2,1)S(1)} %collective-permute-done.4.refs_3_), channel_id=1, source_target_pairs={{0,1},{1,0},{2,3},{3,2},{4,5},{5,4},{6,7},{7,6},{8,9},{9,8},{10,11... | collective-permute-start | bytes 835592 | tf_op jit(solution)/shard_map/ppermute | solution.py:270
  18.2 1.8 %collective-permute-start.5 = (bf16[128,1024]{1,0:T(8,128)(2,1)S(1)}, bf16[128,1024]{1,0:T(8,128)(2,1)S(1)}, u32[]{:S(2)}, u32[]{:S(2)}) collective-permute-start(bf16[128,1024]{1,0:T(8,128)(2,1)S(1)} %collective-permute-done.3.refs_2_), channel_id=1, source_target_pairs={{0,1},{1,0},{2,3},{3,2},{4,5},{5,4},{6,7},{7,6},{8,9},{9,8},{10,11... | collective-permute-start | bytes 786440 | tf_op jit(solution)/shard_map/ppermute | solution.py:270
  19.3 5.5 %collective-permute-start.8 = (bf16[120,1024]{1,0:T(8,128)(2,1)S(1)}, bf16[120,1024]{1,0:T(8,128)(2,1)S(1)}, u32[]{:S(2)}, u32[]{:S(2)}) collective-permute-start(bf16[120,1024]{1,0:T(8,128)(2,1)S(1)} %collective-permute-done.7.tail_ref), channel_id=1, source_target_pairs={{4,8},{5,9},{6,10},{7,11},{8,12},{9,13},{10,14},{11,15},{20,24},{2... | collective-permute-start | bytes 737288 | tf_op jit(solution)/shard_map/ppermute | solution.py:274
  22.0 4.9 %collective-permute-start.9 = (f32[1,256]{1,0:T(1,128)S(1)}, f32[1,256]{1,0:T(1,128)S(1)}, u32[]{:S(2)}, u32[]{:S(2)}) collective-permute-start(f32[1,256]{1,0:T(1,128)S(1)} %get-tuple-element.38), channel_id=1, source_target_pairs={{4,0},{5,1},{6,2},{7,3},{8,4},{9,5},{10,6},{11,7},{12,8},{13,9},{1... | collective-permute-start | bytes 3080 | tf_op jit(solution)/shard_map/ppermute | solution.py:274
  26.9 7.7 %collective-permute-start.10 = (f32[1,256]{1,0:T(1,128)S(1)}, f32[1,256]{1,0:T(1,128)S(1)}, u32[]{:S(2)}, u32[]{:S(2)}) collective-permute-start(f32[1,256]{1,0:T(1,128)S(1)} %get-tuple-element.41), channel_id=1, source_target_pairs={{8,0},{9,1},{10,2},{11,3},{12,4},{13,5},{14,6},{15,7},{24,16},{25,... | collective-permute-start | bytes 3080 | tf_op jit(solution)/shard_map/ppermute | solution.py:274
  28.4 6.2 %collective-permute-start.11 = (f32[1,256]{1,0:T(1,128)S(1)}, f32[1,256]{1,0:T(1,128)S(1)}, u32[]{:S(2)}, u32[]{:S(2)}) collective-permute-start(f32[1,256]{1,0:T(1,128)S(1)} %get-tuple-element.42), channel_id=1, source_target_pairs={{0,2},{1,3},{2,0},{3,1},{4,6},{5,7},{6,4},{7,5},{8,10},{9,11},{10,... | collective-permute-start | bytes 3080 | tf_op jit(solution)/shard_map/ppermute | solution.py:270
  29.9 4.7 %collective-permute-start.12 = (f32[1,256]{1,0:T(1,128)S(1)}, f32[1,256]{1,0:T(1,128)S(1)}, u32[]{:S(2)}, u32[]{:S(2)}) collective-permute-start(f32[1,256]{1,0:T(1,128)S(1)} %get-tuple-element.43), channel_id=1, source_target_pairs={{0,3},{1,2},{2,1},{3,0},{4,7},{5,6},{6,5},{7,4},{8,11},{9,10},{10,... | collective-permute-start | bytes 3080 | tf_op jit(solution)/shard_map/ppermute | solution.py:270
  29.9 4.7 %collective-permute-start.13 = (f32[1,256]{1,0:T(1,128)S(1)}, f32[1,256]{1,0:T(1,128)S(1)}, u32[]{:S(2)}, u32[]{:S(2)}) collective-permute-start(f32[1,256]{1,0:T(1,128)S(1)} %get-tuple-element.44), channel_id=1, source_target_pairs={{0,1},{1,0},{2,3},{3,2},{4,5},{5,4},{6,7},{7,6},{8,9},{9,8},{10,11... | collective-permute-start | bytes 3080 | tf_op jit(solution)/shard_map/ppermute | solution.py:270

commit v25 on v24

--- a/solution.py
+++ b/solution.py
@@ -173,7 +173,7 @@
 
 
 def first_kernel(moves, own_mass_ref, head_ref, tail_ref, *refs):
-    query_refs, (ids_ref, column_ref, sums_ref, mass_ref) = refs[:-4], refs[-4:]
+    query_refs, (key_ids_ref, ids_ref, column_ref, sums_ref, mass_ref) = refs[:-5], refs[-5:]
     rows = mass_ref.shape[1]
     query_parts = query_parts_of(query_refs, rows)
     own_ref = query_refs[0]
@@ -191,6 +191,7 @@
     tail = tail_ref[: rows - head_ref.shape[0], :]
     key_rows = jnp.concatenate([unit_rows(head_ref[...]), tail], axis=0)
     key_ids = ids_of(tail_ref)[:, :rows]
+    key_ids_ref[...] = key_ids
     column_ref[...] = add_line(query_parts, ids_ref, key_rows, key_ids, None, sums_ref)
 
 
@@ -212,7 +213,7 @@
             first += size
 
 
-def last_kernel(moves, powers_ref, rest_ref, tail_ref, ids_ref, earlier_ref, *refs):
+def last_kernel(moves, powers_ref, rest_ref, key_ids_ref, tail_ref, ids_ref, earlier_ref, *refs):
     query_refs, (column_ref, sums_ref) = refs[:-2], refs[-2:]
     rows = column_ref.shape[1]
     cut = powers_ref.shape[1]
@@ -220,8 +221,8 @@
 
     @pl.when(arrived)
     def _():
-        key_ids = ids_of(tail_ref)[:, :rows]
-        key_rows = jnp.concatenate([rest_ref[...], tail_ref[: tail_ref.shape[0] - ID_ROWS, :]], axis=0)
+        key_ids = key_ids_ref[...]
+        key_rows = jnp.concatenate([rest_ref[...], tail_ref[...]], axis=0)
         early_column = jnp.zeros((1, cut), jnp.float32)
         late_column = jnp.zeros((1, rows - cut), jnp.float32)
         first = 0
@@ -297,15 +298,16 @@
     across = [in_plane(piece, 2) for piece in pieces]
     sibling = in_plane(block, 1)
     last_head = on_line(first_head, first_moves)
-    last_tail = on_line(first_tail, forward_moves)
+    last_tail = on_line(first_tail[: row_count - part], forward_moves)
     corner = [in_plane(piece, 1) for piece in across]
     queries = (block, sibling, *across, *corner)
-    ids, first_column, first_sums, mass = pl.pallas_call(
+    first_ids, ids, first_column, first_sums, mass = pl.pallas_call(
         functools.partial(first_kernel, first_moves),
-        out_shape=(lanes, vector, lanes, vector),
+        out_shape=(vector, lanes, vector, lanes, vector),
         cost_estimate=small,
         compiler_params=params,
     )(own_mass, first_head, first_tail, *queries)
+    last_ids = on_line(first_ids, first_moves)
     returned_first = on_line(first_column, first_back)
     powers, rest = pl.pallas_call(
         functools.partial(middle_kernel, last_moves),
@@ -320,7 +322,7 @@
         out_shape=(vector, lanes),
         cost_estimate=small,
         compiler_params=params,
-    )(powers, rest, last_tail, ids, first_sums, *queries)
+    )(powers, rest, last_ids, last_tail, ids, first_sums, *queries)
     returned_first, last_column = lax.optimization_barrier((returned_first, last_column))
     row_sums = pl.pallas_call(
         fold_kernel,

time: 35.4 us -> 36 us (1.017)
  starting transfers between devices: 13.7 us -> 14.9 us
  waiting for transfers between devices: 17 us -> 16.4 us
    ppermute x6 -> x7, starting transfers between devices: 9.41 us -> 10.6 us  [on_line(): return lax.ppermute(value, 'gx', pairs)]
    ppermute x6 -> x7, waiting for transfers between devices: 12.8 us -> 12.3 us  [on_line(): return lax.ppermute(value, 'gx', pairs)]
  transfers between devices with their start and end apart: 14 -> 15, of which waited for: 5 -> 6; matrix products, arithmetic and copies ran while one was open for 0% -> 0% of each run, Pallas kernels for 8% -> 8%
where the time goes in v25:
time: 36 us; the launch traced here: 35.9 us
  waiting for transfers between devices  16.4 us (46%)
  starting transfers between devices  14.9 us (41%)
  Pallas kernels  2.8 us (8%)
  local copies, waits for them, and re-layouts  1.08 us (3%)
  other arithmetic  0.58 us (2%)
    ppermute x7, waiting for transfers between devices, on_line(): return lax.ppermute(value, 'gx', pairs)  12.3 us
    ppermute x7, starting transfers between devices, on_line(): return lax.ppermute(value, 'gx', pairs)  10.6 us
    ppermute x8, starting transfers between devices, in_plane(): return lax.ppermute(value, 'gx', [(i, i ^ step) for i in range(peers)])  4.31 us
    ppermute x8, waiting for transfers between devices, in_plane(): return lax.ppermute(value, 'gx', [(i, i ^ step) for i in range(peers)])  4.12 us
    pallas_call x1, Pallas kernels, grid_plan(): pl.pallas_call(functools.partial(first_kernel, first_moves), out_shape=(v...  2 us
    slice x1, local copies, waits for them, and re-layouts, grid_plan(): first_head = on_line(embeddings[:part], first_moves)  1.05 us
  transfers between devices with their start and end apart: 15, of which 6 were waited for; matrix products, arithmetic and copies ran while one was open for 0% of the time, Pallas kernels for 8%

profile of v25, /device:TPU:0, one launch (start us, length us, event | category | flops | bytes accessed | tf_op | source)
XLA Modules:
  0.0 35.9 jit_solution(4601018420217429616)
XLA Ops:
  0.0 0.0 copy-start
  0.0 1.1 %slice.6 = bf16[144,1024]{1,0:T(8,128)(2,1)S(1)} slice(bf16[256,1024]{1,0:T(8,128)(2,1)} %rows_ref.1), slice={[0:144], [0:1024]} | slice | bytes 589824 | tf_op jit(solution)/shard_map/slice | solution.py:286
  1.1 0.0 copy-start.1
  1.1 3.1 %collective-permute-start = (bf16[144,1024]{1,0:T(8,128)(2,1)S(1)}, bf16[144,1024]{1,0:T(8,128)(2,1)S(1)}, u32[]{:S(2)}, u32[]{:S(2)}) collective-permute-start(bf16[144,1024]{1,0:T(8,128)(2,1)S(1)} %slice.6), channel_id=1, source_target_pairs={{0,4},{1,5},{2,6},{3,7},{4,8},{5,9},{6,10},{7,11},{8,12},{9,13},{1... | collective-permute-start | bytes 884744 | tf_op jit(solution)/shard_map/ppermute | solution.py:275
  4.1 0.0 copy-done
  4.2 0.0 copy-done.1
  4.2 0.2 shard_map.28
  4.4 1.6 %collective-permute-start.4 = (bf16[136,1024]{1,0:T(8,128)(2,1)S(1)}, bf16[136,1024]{1,0:T(8,128)(2,1)S(1)}, u32[]{:S(2)}, u32[]{:S(2)}) collective-permute-start(bf16[136,1024]{1,0:T(8,128)(2,1)S(1)} %get-tuple-element.28), channel_id=1, source_target_pairs={{0,2},{1,3},{2,0},{3,1},{4,6},{5,7},{6,4},{7,5},{8,10},{9,11},{10,... | collective-permute-start | bytes 835592 | tf_op jit(solution)/shard_map/ppermute | solution.py:271
  5.9 0.0 collective-permute-start.2
  5.9 0.5 %collective-permute-start.3 = (bf16[128,1024]{1,0:T(8,128)(2,1)S(1)}, bf16[128,1024]{1,0:T(8,128)(2,1)S(1)}, u32[]{:S(2)}, u32[]{:S(2)}) collective-permute-start(bf16[128,1024]{1,0:T(8,128)(2,1)S(1)} %get-tuple-element.27), channel_id=1, source_target_pairs={{0,2},{1,3},{2,0},{3,1},{4,6},{5,7},{6,4},{7,5},{8,10},{9,11},{10,... | collective-permute-start | bytes 786440 | tf_op jit(solution)/shard_map/ppermute | solution.py:271
  6.4 0.4 shard_map.30.own_mass_ref
  6.8 1.6 %collective-permute-start.7 = (bf16[120,1024]{1,0:T(8,128)(2,1)S(1)}, bf16[120,1024]{1,0:T(8,128)(2,1)S(1)}, u32[]{:S(2)}, u32[]{:S(2)}) collective-permute-start(bf16[120,1024]{1,0:T(8,128)(2,1)S(1)} %get-tuple-element.33), channel_id=1, source_target_pairs={{0,4},{1,5},{2,6},{3,7},{4,8},{5,9},{6,10},{7,11},{8,12},{9,13},{1... | collective-permute-start | bytes 737288 | tf_op jit(solution)/shard_map/ppermute | solution.py:275
  8.4 5.6 %collective-permute-done.head_ref = bf16[144,1024]{1,0:T(8,128)(2,1)S(1)} collective-permute-done((bf16[144,1024]{1,0:T(8,128)(2,1)S(1)}, bf16[144,1024]{1,0:T(8,128)(2,1)S(1)}, u32[]{:S(2)}, u32[]{:S(2)}) %collective-permute-start) | collective-permute-done | bytes 294944 | tf_op jit(solution)/shard_map/ppermute | solution.py:275
  14.0 0.0 collective-permute-start.1
  14.0 0.0 collective-permute-done.4.refs_3_
  14.0 0.0 collective-permute-start.6
  14.0 4.1 %collective-permute-done.3.refs_2_ = bf16[128,1024]{1,0:T(8,128)(2,1)S(1)} collective-permute-done((bf16[128,1024]{1,0:T(8,128)(2,1)S(1)}, bf16[128,1024]{1,0:T(8,128)(2,1)S(1)}, u32[]{:S(2)}, u32[]{:S(2)}) %collective-permute-start.3) | collective-permute-done | bytes 262176 | tf_op jit(solution)/shard_map/ppermute | solution.py:271
  18.2 0.0 collective-permute-start.5
  18.2 1.1 %collective-permute-done.7.tail_ref = bf16[120,1024]{1,0:T(8,128)(2,1)S(1)} collective-permute-done((bf16[120,1024]{1,0:T(8,128)(2,1)S(1)}, bf16[120,1024]{1,0:T(8,128)(2,1)S(1)}, u32[]{:S(2)}, u32[]{:S(2)}) %collective-permute-start.7) | collective-permute-done | bytes 245792 | tf_op jit(solution)/shard_map/ppermute | solution.py:275
  19.3 0.7 %collective-permute-start.9 = (bf16[112,1024]{1,0:T(8,128)(2,1)S(1)}, bf16[112,1024]{1,0:T(8,128)(2,1)S(1)}, u32[]{:S(2)}, u32[]{:S(2)}) collective-permute-start(bf16[112,1024]{1,0:T(8,128)(2,1)S(1)} %slice.8), channel_id=1, source_target_pairs={{4,8},{5,9},{6,10},{7,11},{8,12},{9,13},{10,14},{11,15},{20,24},{2... | collective-permute-start | bytes 688136 | tf_op jit(solution)/shard_map/ppermute | solution.py:275
  20.0 0.0 collective-permute-done.5.refs_4_
  20.0 0.0 collective-permute-done.2.refs_1_
  20.0 0.0 collective-permute-done.6.refs_5_
  20.0 2.0 %shard_map.31 = (f32[1,256]{1,0:T(1,128)S(1)}, f32[1024,128]{1,0:T(8,128)S(1)}, f32[1,256]{1,0:T(1,128)S(1)}, f32[1024,128]{1,0:T(8,128)S(1)}, f32[1,256]{1,0:T(1,128)S(1)}) custom-call(f32[1,256]{1,0:T(1,128)S(1)} %shard_map.30.own_mass_ref, bf16[144,1024]{1,0:T(8,128)(2,1)S(1)} %collective-permute-done.head_ref, ...), custom_call_target="tpu_custom_call" | custom-call | flops 1 | bytes 1 | tf_op jit(solution)/shard_map/pallas_call | solution.py:304
  22.0 3.3 %collective-permute-start.8 = (f32[1,256]{1,0:T(1,128)S(1)}, f32[1,256]{1,0:T(1,128)S(1)}, u32[]{:S(2)}, u32[]{:S(2)}) collective-permute-start(f32[1,256]{1,0:T(1,128)S(1)} %get-tuple-element.34), channel_id=1, source_target_pairs={{0,4},{1,5},{2,6},{3,7},{4,8},{5,9},{6,10},{7,11},{8,12},{9,13},{1... | collective-permute-start | bytes 3080 | tf_op jit(solution)/shard_map/ppermute | solution.py:275
  25.3 0.5 %collective-permute-start.10 = (f32[1,256]{1,0:T(1,128)S(1)}, f32[1,256]{1,0:T(1,128)S(1)}, u32[]{:S(2)}, u32[]{:S(2)}) collective-permute-start(f32[1,256]{1,0:T(1,128)S(1)} %get-tuple-element.40), channel_id=1, source_target_pairs={{4,0},{5,1},{6,2},{7,3},{8,4},{9,5},{10,6},{11,7},{12,8},{13,9},{1... | collective-permute-start | bytes 3080 | tf_op jit(solution)/shard_map/ppermute | solution.py:275
  25.9 0.0 collective-permute-done.1.head_ref
  25.9 0.0 collective-permute-done.9.tail_ref
  25.9 1.5 %collective-permute-done.8.key_ids_ref = f32[1,256]{1,0:T(1,128)S(1)} collective-permute-done((f32[1,256]{1,0:T(1,128)S(1)}, f32[1,256]{1,0:T(1,128)S(1)}, u32[]{:S(2)}, u32[]{:S(2)}) %collective-permute-start.8) | collective-permute-done | bytes 1056 | tf_op jit(solution)/shard_map/ppermute | solution.py:275
  27.5 1.4 %collective-permute-done.10 = f32[1,256]{1,0:T(1,128)S(1)} collective-permute-done((f32[1,256]{1,0:T(1,128)S(1)}, f32[1,256]{1,0:T(1,128)S(1)}, u32[]{:S(2)}, u32[]{:S(2)}) %collective-permute-start.10) | collective-permute-done | bytes 1056 | tf_op jit(solution)/shard_map/ppermute | solution.py:275
  28.9 1.3 %collective-permute-start.11 = (f32[1,256]{1,0:T(1,128)S(1)}, f32[1,256]{1,0:T(1,128)S(1)}, u32[]{:S(2)}, u32[]{:S(2)}) collective-permute-start(f32[1,256]{1,0:T(1,128)S(1)} %get-tuple-element.43), channel_id=1, source_target_pairs={{8,0},{9,1},{10,2},{11,3},{12,4},{13,5},{14,6},{15,7},{24,16},{25,... | collective-permute-start | bytes 3080 | tf_op jit(solution)/shard_map/ppermute | solution.py:275
  30.2 0.2 shard_map.33
  30.4 1.6 %collective-permute-start.12 = (f32[1,256]{1,0:T(1,128)S(1)}, f32[1,256]{1,0:T(1,128)S(1)}, u32[]{:S(2)}, u32[]{:S(2)}) collective-permute-start(f32[1,256]{1,0:T(1,128)S(1)} %get-tuple-element.44), channel_id=1, source_target_pairs={{0,2},{1,3},{2,0},{3,1},{4,6},{5,7},{6,4},{7,5},{8,10},{9,11},{10,... | collective-permute-start | bytes 3080 | tf_op jit(solution)/shard_map/ppermute | solution.py:271
  32.0 0.0 collective-permute-start.13
  32.0 0.6 %collective-permute-start.14 = (f32[1,256]{1,0:T(1,128)S(1)}, f32[1,256]{1,0:T(1,128)S(1)}, u32[]{:S(2)}, u32[]{:S(2)}) collective-permute-start(f32[1,256]{1,0:T(1,128)S(1)} %get-tuple-element.46), channel_id=1, source_target_pairs={{0,1},{1,0},{2,3},{3,2},{4,5},{5,4},{6,7},{7,6},{8,9},{9,8},{10,11... | collective-permute-start | bytes 3080 | tf_op jit(solution)/shard_map/ppermute | solution.py:271
  32.6 2.6 %collective-permute-done.11 = f32[1,256]{1,0:T(1,128)S(1)} collective-permute-done((f32[1,256]{1,0:T(1,128)S(1)}, f32[1,256]{1,0:T(1,128)S(1)}, u32[]{:S(2)}, u32[]{:S(2)}) %collective-permute-start.11) | collective-permute-done | bytes 1056 | tf_op jit(solution)/shard_map/ppermute | solution.py:275
  35.3 0.0 collective-permute-done.12
  35.3 0.0 collective-permute-done.13
  35.3 0.0 collective-permute-done.14
  35.3 0.6 %add_log-plus-one_fusion = f32[1,256]{1,0:T(1,128)} fusion(f32[1,256]{1,0:T(1,128)S(1)} %collective-permute-done.14, f32[1,256]{1,0:T(1,128)S(1)} %collective-permute-done.13, f32[1,256]{1,0:T(1,128)S(1)} %collective-permute-done.12, f32[1,256]{1,0:T(1,128)S(1)} %collective-permute-done.11, f32[1,256]{1,0:T(1,128)S(1)} %get-tuple-element.39, ...), kind=kLoop, calls=%fused_computation | loop fusion | flops 1280 | bytes 7168 | tf_op jit(solution)/shard_map/log1p | solution.py:335
  (3 shorter events, 0.1 us)
Async XLA Ops:
  0.0 4.1 %copy-start = (bf16[256,1024]{1,0:T(8,128)(2,1)S(1)}, bf16[256,1024]{1,0:T(8,128)(2,1)}, u32[]{:S(2)}) copy-start(bf16[256,1024]{1,0:T(8,128)(2,1)} %rows_ref.1) | copy-start | bytes 1572868
  1.1 3.1 %copy-start.1 = (s32[256]{0:T(256)S(1)}, s32[256]{0:T(256)}, u32[]{:S(2)}) copy-start(s32[256]{0:T(256)} %param.3) | copy-start | bytes 3076
  1.1 12.9 %collective-permute-start = (bf16[144,1024]{1,0:T(8,128)(2,1)S(1)}, bf16[144,1024]{1,0:T(8,128)(2,1)S(1)}, u32[]{:S(2)}, u32[]{:S(2)}) collective-permute-start(bf16[144,1024]{1,0:T(8,128)(2,1)S(1)} %slice.6), channel_id=1, source_target_pairs={{0,4},{1,5},{2,6},{3,7},{4,8},{5,9},{6,10},{7,11},{8,12},{9,13},{1... | collective-permute-start | bytes 884744 | tf_op jit(solution)/shard_map/ppermute | solution.py:275
  4.4 9.7 %collective-permute-start.4 = (bf16[136,1024]{1,0:T(8,128)(2,1)S(1)}, bf16[136,1024]{1,0:T(8,128)(2,1)S(1)}, u32[]{:S(2)}, u32[]{:S(2)}) collective-permute-start(bf16[136,1024]{1,0:T(8,128)(2,1)S(1)} %get-tuple-element.28), channel_id=1, source_target_pairs={{0,2},{1,3},{2,0},{3,1},{4,6},{5,7},{6,4},{7,5},{8,10},{9,11},{10,... | collective-permute-start | bytes 835592 | tf_op jit(solution)/shard_map/ppermute | solution.py:271
  5.9 14.1 %collective-permute-start.2 = (bf16[264,1024]{1,0:T(8,128)(2,1)S(1)}, bf16[264,1024]{1,0:T(8,128)(2,1)S(1)}, u32[]{:S(2)}, u32[]{:S(2)}) collective-permute-start(bf16[264,1024]{1,0:T(8,128)(2,1)S(1)} %get-tuple-element.26.refs_0_.own_ref), channel_id=1, source_target_pairs={{0,1},{1,0},{2,3},{3,2},{4,5},{5,4},{6,7},{7,6},{8,9},{9,8},{10,11... | collective-permute-start | bytes 1622024 | tf_op jit(solution)/shard_map/ppermute | solution.py:271
  5.9 12.2 %collective-permute-start.3 = (bf16[128,1024]{1,0:T(8,128)(2,1)S(1)}, bf16[128,1024]{1,0:T(8,128)(2,1)S(1)}, u32[]{:S(2)}, u32[]{:S(2)}) collective-permute-start(bf16[128,1024]{1,0:T(8,128)(2,1)S(1)} %get-tuple-element.27), channel_id=1, source_target_pairs={{0,2},{1,3},{2,0},{3,1},{4,6},{5,7},{6,4},{7,5},{8,10},{9,11},{10,... | collective-permute-start | bytes 786440 | tf_op jit(solution)/shard_map/ppermute | solution.py:271
  6.8 12.5 %collective-permute-start.7 = (bf16[120,1024]{1,0:T(8,128)(2,1)S(1)}, bf16[120,1024]{1,0:T(8,128)(2,1)S(1)}, u32[]{:S(2)}, u32[]{:S(2)}) collective-permute-start(bf16[120,1024]{1,0:T(8,128)(2,1)S(1)} %get-tuple-element.33), channel_id=1, source_target_pairs={{0,4},{1,5},{2,6},{3,7},{4,8},{5,9},{6,10},{7,11},{8,12},{9,13},{1... | collective-permute-start | bytes 737288 | tf_op jit(solution)/shard_map/ppermute | solution.py:275
  14.0 11.9 %collective-permute-start.1 = (bf16[144,1024]{1,0:T(8,128)(2,1)S(1)}, bf16[144,1024]{1,0:T(8,128)(2,1)S(1)}, u32[]{:S(2)}, u32[]{:S(2)}) collective-permute-start(bf16[144,1024]{1,0:T(8,128)(2,1)S(1)} %collective-permute-done.head_ref), channel_id=1, source_target_pairs={{0,4},{1,5},{2,6},{3,7},{4,8},{5,9},{6,10},{7,11},{8,12},{9,13},{1... | collective-permute-start | bytes 884744 | tf_op jit(solution)/shard_map/ppermute | solution.py:275
  14.0 6.0 %collective-permute-start.6 = (bf16[136,1024]{1,0:T(8,128)(2,1)S(1)}, bf16[136,1024]{1,0:T(8,128)(2,1)S(1)}, u32[]{:S(2)}, u32[]{:S(2)}) collective-permute-start(bf16[136,1024]{1,0:T(8,128)(2,1)S(1)} %collective-permute-done.4.refs_3_), channel_id=1, source_target_pairs={{0,1},{1,0},{2,3},{3,2},{4,5},{5,4},{6,7},{7,6},{8,9},{9,8},{10,11... | collective-permute-start | bytes 835592 | tf_op jit(solution)/shard_map/ppermute | solution.py:271
  18.2 1.8 %collective-permute-start.5 = (bf16[128,1024]{1,0:T(8,128)(2,1)S(1)}, bf16[128,1024]{1,0:T(8,128)(2,1)S(1)}, u32[]{:S(2)}, u32[]{:S(2)}) collective-permute-start(bf16[128,1024]{1,0:T(8,128)(2,1)S(1)} %collective-permute-done.3.refs_2_), channel_id=1, source_target_pairs={{0,1},{1,0},{2,3},{3,2},{4,5},{5,4},{6,7},{7,6},{8,9},{9,8},{10,11... | collective-permute-start | bytes 786440 | tf_op jit(solution)/shard_map/ppermute | solution.py:271
  19.3 6.6 %collective-permute-start.9 = (bf16[112,1024]{1,0:T(8,128)(2,1)S(1)}, bf16[112,1024]{1,0:T(8,128)(2,1)S(1)}, u32[]{:S(2)}, u32[]{:S(2)}) collective-permute-start(bf16[112,1024]{1,0:T(8,128)(2,1)S(1)} %slice.8), channel_id=1, source_target_pairs={{4,8},{5,9},{6,10},{7,11},{8,12},{9,13},{10,14},{11,15},{20,24},{2... | collective-permute-start | bytes 688136 | tf_op jit(solution)/shard_map/ppermute | solution.py:275
  22.0 5.4 %collective-permute-start.8 = (f32[1,256]{1,0:T(1,128)S(1)}, f32[1,256]{1,0:T(1,128)S(1)}, u32[]{:S(2)}, u32[]{:S(2)}) collective-permute-start(f32[1,256]{1,0:T(1,128)S(1)} %get-tuple-element.34), channel_id=1, source_target_pairs={{0,4},{1,5},{2,6},{3,7},{4,8},{5,9},{6,10},{7,11},{8,12},{9,13},{1... | collective-permute-start | bytes 3080 | tf_op jit(solution)/shard_map/ppermute | solution.py:275
  25.3 3.6 %collective-permute-start.10 = (f32[1,256]{1,0:T(1,128)S(1)}, f32[1,256]{1,0:T(1,128)S(1)}, u32[]{:S(2)}, u32[]{:S(2)}) collective-permute-start(f32[1,256]{1,0:T(1,128)S(1)} %get-tuple-element.40), channel_id=1, source_target_pairs={{4,0},{5,1},{6,2},{7,3},{8,4},{9,5},{10,6},{11,7},{12,8},{13,9},{1... | collective-permute-start | bytes 3080 | tf_op jit(solution)/shard_map/ppermute | solution.py:275
  28.9 6.3 %collective-permute-start.11 = (f32[1,256]{1,0:T(1,128)S(1)}, f32[1,256]{1,0:T(1,128)S(1)}, u32[]{:S(2)}, u32[]{:S(2)}) collective-permute-start(f32[1,256]{1,0:T(1,128)S(1)} %get-tuple-element.43), channel_id=1, source_target_pairs={{8,0},{9,1},{10,2},{11,3},{12,4},{13,5},{14,6},{15,7},{24,16},{25,... | collective-permute-start | bytes 3080 | tf_op jit(solution)/shard_map/ppermute | solution.py:275
  30.4 4.8 %collective-permute-start.12 = (f32[1,256]{1,0:T(1,128)S(1)}, f32[1,256]{1,0:T(1,128)S(1)}, u32[]{:S(2)}, u32[]{:S(2)}) collective-permute-start(f32[1,256]{1,0:T(1,128)S(1)} %get-tuple-element.44), channel_id=1, source_target_pairs={{0,2},{1,3},{2,0},{3,1},{4,6},{5,7},{6,4},{7,5},{8,10},{9,11},{10,... | collective-permute-start | bytes 3080 | tf_op jit(solution)/shard_map/ppermute | solution.py:271
  32.0 3.3 %collective-permute-start.13 = (f32[1,256]{1,0:T(1,128)S(1)}, f32[1,256]{1,0:T(1,128)S(1)}, u32[]{:S(2)}, u32[]{:S(2)}) collective-permute-start(f32[1,256]{1,0:T(1,128)S(1)} %get-tuple-element.45), channel_id=1, source_target_pairs={{0,3},{1,2},{2,1},{3,0},{4,7},{5,6},{6,5},{7,4},{8,11},{9,10},{10,... | collective-permute-start | bytes 3080 | tf_op jit(solution)/shard_map/ppermute | solution.py:271
  32.0 3.3 %collective-permute-start.14 = (f32[1,256]{1,0:T(1,128)S(1)}, f32[1,256]{1,0:T(1,128)S(1)}, u32[]{:S(2)}, u32[]{:S(2)}) collective-permute-start(f32[1,256]{1,0:T(1,128)S(1)} %get-tuple-element.46), channel_id=1, source_target_pairs={{0,1},{1,0},{2,3},{3,2},{4,5},{5,4},{6,7},{7,6},{8,9},{9,8},{10,11... | collective-permute-start | bytes 3080 | tf_op jit(solution)/shard_map/ppermute | solution.py:271

commit v26 on v25

--- a/solution.py
+++ b/solution.py
@@ -173,7 +173,7 @@
 
 
 def first_kernel(moves, own_mass_ref, head_ref, tail_ref, *refs):
-    query_refs, (key_ids_ref, ids_ref, column_ref, sums_ref, mass_ref) = refs[:-5], refs[-5:]
+    query_refs, (ids_ref, column_ref, sums_ref, mass_ref) = refs[:-4], refs[-4:]
     rows = mass_ref.shape[1]
     query_parts = query_parts_of(query_refs, rows)
     own_ref = query_refs[0]
@@ -191,7 +191,6 @@
     tail = tail_ref[: rows - head_ref.shape[0], :]
     key_rows = jnp.concatenate([unit_rows(head_ref[...]), tail], axis=0)
     key_ids = ids_of(tail_ref)[:, :rows]
-    key_ids_ref[...] = key_ids
     column_ref[...] = add_line(query_parts, ids_ref, key_rows, key_ids, None, sums_ref)
 
 
@@ -221,7 +220,7 @@
 
     @pl.when(arrived)
     def _():
-        key_ids = key_ids_ref[...]
+        key_ids = key_ids_ref[...].astype(jnp.float32)
         key_rows = jnp.concatenate([rest_ref[...], tail_ref[...]], axis=0)
         early_column = jnp.zeros((1, cut), jnp.float32)
         late_column = jnp.zeros((1, rows - cut), jnp.float32)
@@ -299,15 +298,17 @@
     sibling = in_plane(block, 1)
     last_head = on_line(first_head, first_moves)
     last_tail = on_line(first_tail[: row_count - part], forward_moves)
+    last_ids = on_line(
+        cluster_ids.reshape(1, row_count), last_moves + [(b, a) for a, b in last_moves]
+    )
     corner = [in_plane(piece, 1) for piece in across]
     queries = (block, sibling, *across, *corner)
-    first_ids, ids, first_column, first_sums, mass = pl.pallas_call(
+    ids, first_column, first_sums, mass = pl.pallas_call(
         functools.partial(first_kernel, first_moves),
-        out_shape=(vector, lanes, vector, lanes, vector),
+        out_shape=(lanes, vector, lanes, vector),
         cost_estimate=small,
         compiler_params=params,
     )(own_mass, first_head, first_tail, *queries)
-    last_ids = on_line(first_ids, first_moves)
     returned_first = on_line(first_column, first_back)
     powers, rest = pl.pallas_call(
         functools.partial(middle_kernel, last_moves),

time: 36 us -> 36.7 us (1.019)
  starting transfers between devices: 14.9 us -> 16.8 us
  waiting for transfers between devices: 16.4 us -> 15.2 us
    ppermute x7, starting transfers between devices: 10.6 us -> 12.5 us  [on_line(): return lax.ppermute(value, 'gx', pairs)]
    ppermute x7, waiting for transfers between devices: 12.3 us -> 11 us  [on_line(): return lax.ppermute(value, 'gx', pairs)]
  transfers between devices with their start and end apart: 15 -> 15, of which waited for: 6 -> 5; matrix products, arithmetic and copies ran while one was open for 0% -> 0% of each run, Pallas kernels for 8% -> 8%
where the time goes in v26:
time: 36.7 us; the launch traced here: 36.5 us
  starting transfers between devices  16.8 us (46%)
  waiting for transfers between devices  15.2 us (41%)
  Pallas kernels  2.82 us (8%)
  local copies, waits for them, and re-layouts  1.08 us (3%)
  other arithmetic  0.58 us (2%)
    ppermute x7, starting transfers between devices, on_line(): return lax.ppermute(value, 'gx', pairs)  12.5 us
    ppermute x7, waiting for transfers between devices, on_line(): return lax.ppermute(value, 'gx', pairs)  11 us
    ppermute x8, starting transfers between devices, in_plane(): return lax.ppermute(value, 'gx', [(i, i ^ step) for i in range(peers)])  4.31 us
    ppermute x8, waiting for transfers between devices, in_plane(): return lax.ppermute(value, 'gx', [(i, i ^ step) for i in range(peers)])  4.12 us
    pallas_call x1, Pallas kernels, grid_plan(): pl.pallas_call(functools.partial(first_kernel, first_moves), out_shape=(l...  2.01 us
    slice x1, local copies, waits for them, and re-layouts, grid_plan(): first_head = on_line(embeddings[:part], first_moves)  1.05 us
  transfers between devices with their start and end apart: 15, of which 5 were waited for; matrix products, arithmetic and copies ran while one was open for 0% of the time, Pallas kernels for 8%

profile of v26, /device:TPU:0, one launch (start us, length us, event | category | flops | bytes accessed | tf_op | source)
XLA Modules:
  0.0 36.5 jit_solution(2918677058121643657)
XLA Ops:
  0.0 0.0 copy-start
  0.0 1.1 %slice.6 = bf16[144,1024]{1,0:T(8,128)(2,1)S(1)} slice(bf16[256,1024]{1,0:T(8,128)(2,1)} %rows_ref.1), slice={[0:144], [0:1024]} | slice | bytes 589824 | tf_op jit(solution)/shard_map/slice | solution.py:285
  1.1 0.0 copy-start.1
  1.1 3.1 %collective-permute-start = (bf16[144,1024]{1,0:T(8,128)(2,1)S(1)}, bf16[144,1024]{1,0:T(8,128)(2,1)S(1)}, u32[]{:S(2)}, u32[]{:S(2)}) collective-permute-start(bf16[144,1024]{1,0:T(8,128)(2,1)S(1)} %slice.6), channel_id=1, source_target_pairs={{0,4},{1,5},{2,6},{3,7},{4,8},{5,9},{6,10},{7,11},{8,12},{9,13},{1... | collective-permute-start | bytes 884744 | tf_op jit(solution)/shard_map/ppermute | solution.py:274
  4.1 0.0 copy-done
  4.2 0.0 copy-done.1
  4.2 0.2 shard_map.28
  4.4 1.6 %collective-permute-start.4 = (bf16[136,1024]{1,0:T(8,128)(2,1)S(1)}, bf16[136,1024]{1,0:T(8,128)(2,1)S(1)}, u32[]{:S(2)}, u32[]{:S(2)}) collective-permute-start(bf16[136,1024]{1,0:T(8,128)(2,1)S(1)} %get-tuple-element.27), channel_id=1, source_target_pairs={{0,2},{1,3},{2,0},{3,1},{4,6},{5,7},{6,4},{7,5},{8,10},{9,11},{10,... | collective-permute-start | bytes 835592 | tf_op jit(solution)/shard_map/ppermute | solution.py:270
  5.9 0.0 collective-permute-start.2
  5.9 0.5 %collective-permute-start.3 = (bf16[128,1024]{1,0:T(8,128)(2,1)S(1)}, bf16[128,1024]{1,0:T(8,128)(2,1)S(1)}, u32[]{:S(2)}, u32[]{:S(2)}) collective-permute-start(bf16[128,1024]{1,0:T(8,128)(2,1)S(1)} %get-tuple-element.26), channel_id=1, source_target_pairs={{0,2},{1,3},{2,0},{3,1},{4,6},{5,7},{6,4},{7,5},{8,10},{9,11},{10,... | collective-permute-start | bytes 786440 | tf_op jit(solution)/shard_map/ppermute | solution.py:270
  6.4 0.4 shard_map.30.own_mass_ref
  6.8 1.6 %collective-permute-start.8 = (bf16[120,1024]{1,0:T(8,128)(2,1)S(1)}, bf16[120,1024]{1,0:T(8,128)(2,1)S(1)}, u32[]{:S(2)}, u32[]{:S(2)}) collective-permute-start(bf16[120,1024]{1,0:T(8,128)(2,1)S(1)} %get-tuple-element.31), channel_id=1, source_target_pairs={{0,4},{1,5},{2,6},{3,7},{4,8},{5,9},{6,10},{7,11},{8,12},{9,13},{1... | collective-permute-start | bytes 737288 | tf_op jit(solution)/shard_map/ppermute | solution.py:274
  8.4 5.6 %collective-permute-done.head_ref = bf16[144,1024]{1,0:T(8,128)(2,1)S(1)} collective-permute-done((bf16[144,1024]{1,0:T(8,128)(2,1)S(1)}, bf16[144,1024]{1,0:T(8,128)(2,1)S(1)}, u32[]{:S(2)}, u32[]{:S(2)}) %collective-permute-start) | collective-permute-done | bytes 294944 | tf_op jit(solution)/shard_map/ppermute | solution.py:274
  14.0 0.0 collective-permute-start.1
  14.0 0.0 collective-permute-done.4.refs_3_
  14.0 0.0 collective-permute-start.6
  14.0 4.1 %collective-permute-done.3.refs_2_ = bf16[128,1024]{1,0:T(8,128)(2,1)S(1)} collective-permute-done((bf16[128,1024]{1,0:T(8,128)(2,1)S(1)}, bf16[128,1024]{1,0:T(8,128)(2,1)S(1)}, u32[]{:S(2)}, u32[]{:S(2)}) %collective-permute-start.3) | collective-permute-done | bytes 262176 | tf_op jit(solution)/shard_map/ppermute | solution.py:270
  18.2 0.0 collective-permute-start.5
  18.2 1.1 %collective-permute-done.8.tail_ref = bf16[120,1024]{1,0:T(8,128)(2,1)S(1)} collective-permute-done((bf16[120,1024]{1,0:T(8,128)(2,1)S(1)}, bf16[120,1024]{1,0:T(8,128)(2,1)S(1)}, u32[]{:S(2)}, u32[]{:S(2)}) %collective-permute-start.8) | collective-permute-done | bytes 245792 | tf_op jit(solution)/shard_map/ppermute | solution.py:274
  19.3 0.7 %collective-permute-start.9 = (bf16[112,1024]{1,0:T(8,128)(2,1)S(1)}, bf16[112,1024]{1,0:T(8,128)(2,1)S(1)}, u32[]{:S(2)}, u32[]{:S(2)}) collective-permute-start(bf16[112,1024]{1,0:T(8,128)(2,1)S(1)} %slice.8), channel_id=1, source_target_pairs={{4,8},{5,9},{6,10},{7,11},{8,12},{9,13},{10,14},{11,15},{20,24},{2... | collective-permute-start | bytes 688136 | tf_op jit(solution)/shard_map/ppermute | solution.py:274
  20.0 0.0 collective-permute-done.5.refs_4_
  20.0 3.9 %collective-permute-start.7 = (s32[1,256]{1,0:T(1,128)S(1)}, s32[1,256]{1,0:T(1,128)S(1)}, u32[]{:S(2)}, u32[]{:S(2)}) collective-permute-start(s32[1,256]{1,0:T(1,128)S(1)} %bitcast.3), channel_id=1, source_target_pairs={{0,8},{1,9},{2,10},{3,11},{4,12},{5,13},{6,14},{7,15},{8,0},{9,1},... | collective-permute-start | bytes 3080 | tf_op jit(solution)/shard_map/ppermute | solution.py:274
  23.9 0.0 collective-permute-done.2.refs_1_
  23.9 0.0 collective-permute-done.6.refs_5_
  23.9 2.0 %shard_map.31 = (f32[1024,128]{1,0:T(8,128)S(1)}, f32[1,256]{1,0:T(1,128)S(1)}, f32[1024,128]{1,0:T(8,128)S(1)}, f32[1,256]{1,0:T(1,128)S(1)}) custom-call(f32[1,256]{1,0:T(1,128)S(1)} %shard_map.30.own_mass_ref, bf16[144,1024]{1,0:T(8,128)(2,1)S(1)} %collective-permute-done.head_ref, bf16[120,1024]{1,0:T(8,128)(2,1)S(1)} %collective-permute-done.8.tail_ref, ...), custom_call_target="tpu_custom_call" | custom-call | flops 1 | bytes 1 | tf_op jit(solution)/shard_map/pallas_call | solution.py:306
  25.9 1.8 %collective-permute-start.10 = (f32[1,256]{1,0:T(1,128)S(1)}, f32[1,256]{1,0:T(1,128)S(1)}, u32[]{:S(2)}, u32[]{:S(2)}) collective-permute-start(f32[1,256]{1,0:T(1,128)S(1)} %get-tuple-element.38), channel_id=1, source_target_pairs={{4,0},{5,1},{6,2},{7,3},{8,4},{9,5},{10,6},{11,7},{12,8},{13,9},{1... | collective-permute-start | bytes 3080 | tf_op jit(solution)/shard_map/ppermute | solution.py:274
  27.8 0.0 collective-permute-done.1.head_ref
  27.8 0.0 collective-permute-done.7.key_ids_ref
  27.8 0.0 collective-permute-done.9.tail_ref
  27.8 0.1 shard_map.32
  27.8 1.7 %collective-permute-done.10 = f32[1,256]{1,0:T(1,128)S(1)} collective-permute-done((f32[1,256]{1,0:T(1,128)S(1)}, f32[1,256]{1,0:T(1,128)S(1)}, u32[]{:S(2)}, u32[]{:S(2)}) %collective-permute-start.10) | collective-permute-done | bytes 1056 | tf_op jit(solution)/shard_map/ppermute | solution.py:274
  29.5 1.3 %collective-permute-start.11 = (f32[1,256]{1,0:T(1,128)S(1)}, f32[1,256]{1,0:T(1,128)S(1)}, u32[]{:S(2)}, u32[]{:S(2)}) collective-permute-start(f32[1,256]{1,0:T(1,128)S(1)} %get-tuple-element.41), channel_id=1, source_target_pairs={{8,0},{9,1},{10,2},{11,3},{12,4},{13,5},{14,6},{15,7},{24,16},{25,... | collective-permute-start | bytes 3080 | tf_op jit(solution)/shard_map/ppermute | solution.py:274
  30.8 0.2 shard_map.33
  31.1 1.6 %collective-permute-start.12 = (f32[1,256]{1,0:T(1,128)S(1)}, f32[1,256]{1,0:T(1,128)S(1)}, u32[]{:S(2)}, u32[]{:S(2)}) collective-permute-start(f32[1,256]{1,0:T(1,128)S(1)} %get-tuple-element.42), channel_id=1, source_target_pairs={{0,2},{1,3},{2,0},{3,1},{4,6},{5,7},{6,4},{7,5},{8,10},{9,11},{10,... | collective-permute-start | bytes 3080 | tf_op jit(solution)/shard_map/ppermute | solution.py:270
  32.6 0.0 collective-permute-start.13
  32.6 0.6 %collective-permute-start.14 = (f32[1,256]{1,0:T(1,128)S(1)}, f32[1,256]{1,0:T(1,128)S(1)}, u32[]{:S(2)}, u32[]{:S(2)}) collective-permute-start(f32[1,256]{1,0:T(1,128)S(1)} %get-tuple-element.44), channel_id=1, source_target_pairs={{0,1},{1,0},{2,3},{3,2},{4,5},{5,4},{6,7},{7,6},{8,9},{9,8},{10,11... | collective-permute-start | bytes 3080 | tf_op jit(solution)/shard_map/ppermute | solution.py:270
  33.3 2.6 %collective-permute-done.11 = f32[1,256]{1,0:T(1,128)S(1)} collective-permute-done((f32[1,256]{1,0:T(1,128)S(1)}, f32[1,256]{1,0:T(1,128)S(1)}, u32[]{:S(2)}, u32[]{:S(2)}) %collective-permute-start.11) | collective-permute-done | bytes 1056 | tf_op jit(solution)/shard_map/ppermute | solution.py:274
  35.9 0.0 collective-permute-done.12
  35.9 0.0 collective-permute-done.13
  35.9 0.0 collective-permute-done.14
  35.9 0.6 %add_log-plus-one_fusion = f32[1,256]{1,0:T(1,128)} fusion(f32[1,256]{1,0:T(1,128)S(1)} %collective-permute-done.14, f32[1,256]{1,0:T(1,128)S(1)} %collective-permute-done.13, f32[1,256]{1,0:T(1,128)S(1)} %collective-permute-done.12, f32[1,256]{1,0:T(1,128)S(1)} %collective-permute-done.11, f32[1,256]{1,0:T(1,128)S(1)} %get-tuple-element.37, ...), kind=kLoop, calls=%fused_computation | loop fusion | flops 1280 | bytes 7168 | tf_op jit(solution)/shard_map/log1p | solution.py:336
  (2 shorter events, 0.0 us)
Async XLA Ops:
  0.0 4.1 %copy-start = (bf16[256,1024]{1,0:T(8,128)(2,1)S(1)}, bf16[256,1024]{1,0:T(8,128)(2,1)}, u32[]{:S(2)}) copy-start(bf16[256,1024]{1,0:T(8,128)(2,1)} %rows_ref.1) | copy-start | bytes 1572868
  1.1 3.1 %copy-start.1 = (s32[256]{0:T(256)S(1)}, s32[256]{0:T(256)}, u32[]{:S(2)}) copy-start(s32[256]{0:T(256)} %param.3) | copy-start | bytes 3076
  1.1 12.9 %collective-permute-start = (bf16[144,1024]{1,0:T(8,128)(2,1)S(1)}, bf16[144,1024]{1,0:T(8,128)(2,1)S(1)}, u32[]{:S(2)}, u32[]{:S(2)}) collective-permute-start(bf16[144,1024]{1,0:T(8,128)(2,1)S(1)} %slice.6), channel_id=1, source_target_pairs={{0,4},{1,5},{2,6},{3,7},{4,8},{5,9},{6,10},{7,11},{8,12},{9,13},{1... | collective-permute-start | bytes 884744 | tf_op jit(solution)/shard_map/ppermute | solution.py:274
  4.4 9.7 %collective-permute-start.4 = (bf16[136,1024]{1,0:T(8,128)(2,1)S(1)}, bf16[136,1024]{1,0:T(8,128)(2,1)S(1)}, u32[]{:S(2)}, u32[]{:S(2)}) collective-permute-start(bf16[136,1024]{1,0:T(8,128)(2,1)S(1)} %get-tuple-element.27), channel_id=1, source_target_pairs={{0,2},{1,3},{2,0},{3,1},{4,6},{5,7},{6,4},{7,5},{8,10},{9,11},{10,... | collective-permute-start | bytes 835592 | tf_op jit(solution)/shard_map/ppermute | solution.py:270
  5.9 18.0 %collective-permute-start.2 = (bf16[264,1024]{1,0:T(8,128)(2,1)S(1)}, bf16[264,1024]{1,0:T(8,128)(2,1)S(1)}, u32[]{:S(2)}, u32[]{:S(2)}) collective-permute-start(bf16[264,1024]{1,0:T(8,128)(2,1)S(1)} %get-tuple-element.25.refs_0_.own_ref), channel_id=1, source_target_pairs={{0,1},{1,0},{2,3},{3,2},{4,5},{5,4},{6,7},{7,6},{8,9},{9,8},{10,11... | collective-permute-start | bytes 1622024 | tf_op jit(solution)/shard_map/ppermute | solution.py:270
  5.9 12.2 %collective-permute-start.3 = (bf16[128,1024]{1,0:T(8,128)(2,1)S(1)}, bf16[128,1024]{1,0:T(8,128)(2,1)S(1)}, u32[]{:S(2)}, u32[]{:S(2)}) collective-permute-start(bf16[128,1024]{1,0:T(8,128)(2,1)S(1)} %get-tuple-element.26), channel_id=1, source_target_pairs={{0,2},{1,3},{2,0},{3,1},{4,6},{5,7},{6,4},{7,5},{8,10},{9,11},{10,... | collective-permute-start | bytes 786440 | tf_op jit(solution)/shard_map/ppermute | solution.py:270
  6.8 12.5 %collective-permute-start.8 = (bf16[120,1024]{1,0:T(8,128)(2,1)S(1)}, bf16[120,1024]{1,0:T(8,128)(2,1)S(1)}, u32[]{:S(2)}, u32[]{:S(2)}) collective-permute-start(bf16[120,1024]{1,0:T(8,128)(2,1)S(1)} %get-tuple-element.31), channel_id=1, source_target_pairs={{0,4},{1,5},{2,6},{3,7},{4,8},{5,9},{6,10},{7,11},{8,12},{9,13},{1... | collective-permute-start | bytes 737288 | tf_op jit(solution)/shard_map/ppermute | solution.py:274
  14.0 13.8 %collective-permute-start.1 = (bf16[144,1024]{1,0:T(8,128)(2,1)S(1)}, bf16[144,1024]{1,0:T(8,128)(2,1)S(1)}, u32[]{:S(2)}, u32[]{:S(2)}) collective-permute-start(bf16[144,1024]{1,0:T(8,128)(2,1)S(1)} %collective-permute-done.head_ref), channel_id=1, source_target_pairs={{0,4},{1,5},{2,6},{3,7},{4,8},{5,9},{6,10},{7,11},{8,12},{9,13},{1... | collective-permute-start | bytes 884744 | tf_op jit(solution)/shard_map/ppermute | solution.py:274
  14.0 9.9 %collective-permute-start.6 = (bf16[136,1024]{1,0:T(8,128)(2,1)S(1)}, bf16[136,1024]{1,0:T(8,128)(2,1)S(1)}, u32[]{:S(2)}, u32[]{:S(2)}) collective-permute-start(bf16[136,1024]{1,0:T(8,128)(2,1)S(1)} %collective-permute-done.4.refs_3_), channel_id=1, source_target_pairs={{0,1},{1,0},{2,3},{3,2},{4,5},{5,4},{6,7},{7,6},{8,9},{9,8},{10,11... | collective-permute-start | bytes 835592 | tf_op jit(solution)/shard_map/ppermute | solution.py:270
  18.2 1.8 %collective-permute-start.5 = (bf16[128,1024]{1,0:T(8,128)(2,1)S(1)}, bf16[128,1024]{1,0:T(8,128)(2,1)S(1)}, u32[]{:S(2)}, u32[]{:S(2)}) collective-permute-start(bf16[128,1024]{1,0:T(8,128)(2,1)S(1)} %collective-permute-done.3.refs_2_), channel_id=1, source_target_pairs={{0,1},{1,0},{2,3},{3,2},{4,5},{5,4},{6,7},{7,6},{8,9},{9,8},{10,11... | collective-permute-start | bytes 786440 | tf_op jit(solution)/shard_map/ppermute | solution.py:270
  19.3 8.5 %collective-permute-start.9 = (bf16[112,1024]{1,0:T(8,128)(2,1)S(1)}, bf16[112,1024]{1,0:T(8,128)(2,1)S(1)}, u32[]{:S(2)}, u32[]{:S(2)}) collective-permute-start(bf16[112,1024]{1,0:T(8,128)(2,1)S(1)} %slice.8), channel_id=1, source_target_pairs={{4,8},{5,9},{6,10},{7,11},{8,12},{9,13},{10,14},{11,15},{20,24},{2... | collective-permute-start | bytes 688136 | tf_op jit(solution)/shard_map/ppermute | solution.py:274
  20.0 7.8 %collective-permute-start.7 = (s32[1,256]{1,0:T(1,128)S(1)}, s32[1,256]{1,0:T(1,128)S(1)}, u32[]{:S(2)}, u32[]{:S(2)}) collective-permute-start(s32[1,256]{1,0:T(1,128)S(1)} %bitcast.3), channel_id=1, source_target_pairs={{0,8},{1,9},{2,10},{3,11},{4,12},{5,13},{6,14},{7,15},{8,0},{9,1},... | collective-permute-start | bytes 3080 | tf_op jit(solution)/shard_map/ppermute | solution.py:274
  25.9 3.6 %collective-permute-start.10 = (f32[1,256]{1,0:T(1,128)S(1)}, f32[1,256]{1,0:T(1,128)S(1)}, u32[]{:S(2)}, u32[]{:S(2)}) collective-permute-start(f32[1,256]{1,0:T(1,128)S(1)} %get-tuple-element.38), channel_id=1, source_target_pairs={{4,0},{5,1},{6,2},{7,3},{8,4},{9,5},{10,6},{11,7},{12,8},{13,9},{1... | collective-permute-start | bytes 3080 | tf_op jit(solution)/shard_map/ppermute | solution.py:274
  29.5 6.3 %collective-permute-start.11 = (f32[1,256]{1,0:T(1,128)S(1)}, f32[1,256]{1,0:T(1,128)S(1)}, u32[]{:S(2)}, u32[]{:S(2)}) collective-permute-start(f32[1,256]{1,0:T(1,128)S(1)} %get-tuple-element.41), channel_id=1, source_target_pairs={{8,0},{9,1},{10,2},{11,3},{12,4},{13,5},{14,6},{15,7},{24,16},{25,... | collective-permute-start | bytes 3080 | tf_op jit(solution)/shard_map/ppermute | solution.py:274
  31.1 4.8 %collective-permute-start.12 = (f32[1,256]{1,0:T(1,128)S(1)}, f32[1,256]{1,0:T(1,128)S(1)}, u32[]{:S(2)}, u32[]{:S(2)}) collective-permute-start(f32[1,256]{1,0:T(1,128)S(1)} %get-tuple-element.42), channel_id=1, source_target_pairs={{0,2},{1,3},{2,0},{3,1},{4,6},{5,7},{6,4},{7,5},{8,10},{9,11},{10,... | collective-permute-start | bytes 3080 | tf_op jit(solution)/shard_map/ppermute | solution.py:270
  32.6 3.3 %collective-permute-start.13 = (f32[1,256]{1,0:T(1,128)S(1)}, f32[1,256]{1,0:T(1,128)S(1)}, u32[]{:S(2)}, u32[]{:S(2)}) collective-permute-start(f32[1,256]{1,0:T(1,128)S(1)} %get-tuple-element.43), channel_id=1, source_target_pairs={{0,3},{1,2},{2,1},{3,0},{4,7},{5,6},{6,5},{7,4},{8,11},{9,10},{10,... | collective-permute-start | bytes 3080 | tf_op jit(solution)/shard_map/ppermute | solution.py:270
  32.6 3.3 %collective-permute-start.14 = (f32[1,256]{1,0:T(1,128)S(1)}, f32[1,256]{1,0:T(1,128)S(1)}, u32[]{:S(2)}, u32[]{:S(2)}) collective-permute-start(f32[1,256]{1,0:T(1,128)S(1)} %get-tuple-element.44), channel_id=1, source_target_pairs={{0,1},{1,0},{2,3},{3,2},{4,5},{5,4},{6,7},{7,6},{8,9},{9,8},{10,11... | collective-permute-start | bytes 3080 | tf_op jit(solution)/shard_map/ppermute | solution.py:270

commit v27 on v24

--- a/solution.py
+++ b/solution.py
@@ -279,7 +279,7 @@
     first_back = [(b, a) for a, b in first_moves]
     last_back = [(b, a) for a, b in last_moves]
 
-    half, part = row_count // 2, 9 * row_count // 16
+    half, part = row_count // 2, 5 * row_count // 8
     ranges = [(0, row_count), (0, half), (half, row_count), (part, row_count)]
     id_rows = [ID_ROWS, 0, ID_ROWS, ID_ROWS]
     first_head = on_line(embeddings[:part], first_moves)

time: 35.4 us -> 35.2 us (level)
    ppermute x8, waiting for transfers between devices: 4.12 us -> 3.42 us  [in_plane(): return lax.ppermute(value, 'gx', [(i, i ^ step) for i in range(peers)])]
    ppermute x6, waiting for transfers between devices: 12.8 us -> 13.3 us  [on_line(): return lax.ppermute(value, 'gx', pairs)]
  transfers between devices with their start and end apart: 14 -> 14, of which waited for: 5 -> 6; matrix products, arithmetic and copies ran while one was open for 0% -> 0% of each run, Pallas kernels for 8% -> 8%
where the time goes in v27:
time: 35.2 us; the launch traced here: 35 us
  waiting for transfers between devices  16.7 us (47%)
  starting transfers between devices  13.7 us (39%)
  Pallas kernels  2.81 us (8%)
  local copies, waits for them, and re-layouts  1.08 us (3%)
  other arithmetic  0.58 us (2%)
    ppermute x6, waiting for transfers between devices, on_line(): return lax.ppermute(value, 'gx', pairs)  13.3 us
    ppermute x6, starting transfers between devices, on_line(): return lax.ppermute(value, 'gx', pairs)  9.4 us
    ppermute x8, starting transfers between devices, in_plane(): return lax.ppermute(value, 'gx', [(i, i ^ step) for i in range(peers)])  4.31 us
    ppermute x8, waiting for transfers between devices, in_plane(): return lax.ppermute(value, 'gx', [(i, i ^ step) for i in range(peers)])  3.42 us
    pallas_call x1, Pallas kernels, grid_plan(): pl.pallas_call(functools.partial(first_kernel, first_moves), out_shape=(l...  2.02 us
    slice x1, local copies, waits for them, and re-layouts, grid_plan(): first_head = on_line(embeddings[:part], first_moves)  1.07 us
  transfers between devices with their start and end apart: 14, of which 6 were waited for; matrix products, arithmetic and copies ran while one was open for 0% of the time, Pallas kernels for 8%

profile of v27, /device:TPU:0, one launch (start us, length us, event | category | flops | bytes accessed | tf_op | source)
XLA Modules:
  0.0 35.0 jit_solution(9512514488670086352)
XLA Ops:
  0.0 0.0 copy-start
  0.0 1.1 %slice.3 = bf16[160,1024]{1,0:T(8,128)(2,1)S(1)} slice(bf16[256,1024]{1,0:T(8,128)(2,1)} %rows_ref.1), slice={[0:160], [0:1024]} | slice | bytes 655360 | tf_op jit(solution)/shard_map/slice | solution.py:285
  1.1 0.0 copy-start.1
  1.1 3.1 %collective-permute-start = (bf16[160,1024]{1,0:T(8,128)(2,1)S(1)}, bf16[160,1024]{1,0:T(8,128)(2,1)S(1)}, u32[]{:S(2)}, u32[]{:S(2)}) collective-permute-start(bf16[160,1024]{1,0:T(8,128)(2,1)S(1)} %slice.3), channel_id=1, source_target_pairs={{0,4},{1,5},{2,6},{3,7},{4,8},{5,9},{6,10},{7,11},{8,12},{9,13},{1... | collective-permute-start | bytes 983048 | tf_op jit(solution)/shard_map/ppermute | solution.py:274
  4.2 0.0 copy-done
  4.2 0.0 copy-done.1
  4.2 0.2 shard_map.28
  4.4 1.6 %collective-permute-start.4 = (bf16[136,1024]{1,0:T(8,128)(2,1)S(1)}, bf16[136,1024]{1,0:T(8,128)(2,1)S(1)}, u32[]{:S(2)}, u32[]{:S(2)}) collective-permute-start(bf16[136,1024]{1,0:T(8,128)(2,1)S(1)} %get-tuple-element.27), channel_id=1, source_target_pairs={{0,2},{1,3},{2,0},{3,1},{4,6},{5,7},{6,4},{7,5},{8,10},{9,11},{10,... | collective-permute-start | bytes 835592 | tf_op jit(solution)/shard_map/ppermute | solution.py:270
  5.9 0.0 collective-permute-start.2
  5.9 0.5 %collective-permute-start.3 = (bf16[128,1024]{1,0:T(8,128)(2,1)S(1)}, bf16[128,1024]{1,0:T(8,128)(2,1)S(1)}, u32[]{:S(2)}, u32[]{:S(2)}) collective-permute-start(bf16[128,1024]{1,0:T(8,128)(2,1)S(1)} %get-tuple-element.26), channel_id=1, source_target_pairs={{0,2},{1,3},{2,0},{3,1},{4,6},{5,7},{6,4},{7,5},{8,10},{9,11},{10,... | collective-permute-start | bytes 786440 | tf_op jit(solution)/shard_map/ppermute | solution.py:270
  6.5 0.3 shard_map.30.own_mass_ref
  6.8 1.6 %collective-permute-start.7 = (bf16[104,1024]{1,0:T(8,128)(2,1)S(1)}, bf16[104,1024]{1,0:T(8,128)(2,1)S(1)}, u32[]{:S(2)}, u32[]{:S(2)}) collective-permute-start(bf16[104,1024]{1,0:T(8,128)(2,1)S(1)} %get-tuple-element.31), channel_id=1, source_target_pairs={{0,4},{1,5},{2,6},{3,7},{4,8},{5,9},{6,10},{7,11},{8,12},{9,13},{1... | collective-permute-start | bytes 638984 | tf_op jit(solution)/shard_map/ppermute | solution.py:274
  8.4 6.3 %collective-permute-done.head_ref = bf16[160,1024]{1,0:T(8,128)(2,1)S(1)} collective-permute-done((bf16[160,1024]{1,0:T(8,128)(2,1)S(1)}, bf16[160,1024]{1,0:T(8,128)(2,1)S(1)}, u32[]{:S(2)}, u32[]{:S(2)}) %collective-permute-start) | collective-permute-done | bytes 327712 | tf_op jit(solution)/shard_map/ppermute | solution.py:274
  14.7 0.0 collective-permute-start.1
  14.8 0.0 collective-permute-done.4.refs_3_
  14.8 0.0 collective-permute-start.6
  14.8 3.4 %collective-permute-done.3.refs_2_ = bf16[128,1024]{1,0:T(8,128)(2,1)S(1)} collective-permute-done((bf16[128,1024]{1,0:T(8,128)(2,1)S(1)}, bf16[128,1024]{1,0:T(8,128)(2,1)S(1)}, u32[]{:S(2)}, u32[]{:S(2)}) %collective-permute-start.3) | collective-permute-done | bytes 262176 | tf_op jit(solution)/shard_map/ppermute | solution.py:270
  18.2 0.0 collective-permute-start.5
  18.2 1.1 %collective-permute-done.7.tail_ref = bf16[104,1024]{1,0:T(8,128)(2,1)S(1)} collective-permute-done((bf16[104,1024]{1,0:T(8,128)(2,1)S(1)}, bf16[104,1024]{1,0:T(8,128)(2,1)S(1)}, u32[]{:S(2)}, u32[]{:S(2)}) %collective-permute-start.7) | collective-permute-done | bytes 213024 | tf_op jit(solution)/shard_map/ppermute | solution.py:274
  19.3 0.7 %collective-permute-start.8 = (bf16[104,1024]{1,0:T(8,128)(2,1)S(1)}, bf16[104,1024]{1,0:T(8,128)(2,1)S(1)}, u32[]{:S(2)}, u32[]{:S(2)}) collective-permute-start(bf16[104,1024]{1,0:T(8,128)(2,1)S(1)} %collective-permute-done.7.tail_ref), channel_id=1, source_target_pairs={{4,8},{5,9},{6,10},{7,11},{8,12},{9,13},{10,14},{11,15},{20,24},{2... | collective-permute-start | bytes 638984 | tf_op jit(solution)/shard_map/ppermute | solution.py:274
  20.0 0.0 collective-permute-done.5.refs_4_
  20.0 0.0 collective-permute-done.2.refs_1_
  20.0 0.0 collective-permute-done.6.refs_5_
  20.0 2.0 %shard_map.31 = (f32[1024,128]{1,0:T(8,128)S(1)}, f32[1,256]{1,0:T(1,128)S(1)}, f32[1024,128]{1,0:T(8,128)S(1)}, f32[1,256]{1,0:T(1,128)S(1)}) custom-call(f32[1,256]{1,0:T(1,128)S(1)} %shard_map.30.own_mass_ref, bf16[160,1024]{1,0:T(8,128)(2,1)S(1)} %collective-permute-done.head_ref, bf16[104,1024]{1,0:T(8,128)(2,1)S(1)} %collective-permute-done.7.tail_ref, ...), custom_call_target="tpu_custom_call" | custom-call | flops 1 | bytes 1 | tf_op jit(solution)/shard_map/pallas_call | solution.py:303
  22.0 2.7 %collective-permute-start.9 = (f32[1,256]{1,0:T(1,128)S(1)}, f32[1,256]{1,0:T(1,128)S(1)}, u32[]{:S(2)}, u32[]{:S(2)}) collective-permute-start(f32[1,256]{1,0:T(1,128)S(1)} %get-tuple-element.38), channel_id=1, source_target_pairs={{4,0},{5,1},{6,2},{7,3},{8,4},{9,5},{10,6},{11,7},{12,8},{13,9},{1... | collective-permute-start | bytes 3080 | tf_op jit(solution)/shard_map/ppermute | solution.py:274
  24.7 0.7 %collective-permute-done.1.head_ref = bf16[160,1024]{1,0:T(8,128)(2,1)S(1)} collective-permute-done((bf16[160,1024]{1,0:T(8,128)(2,1)S(1)}, bf16[160,1024]{1,0:T(8,128)(2,1)S(1)}, u32[]{:S(2)}, u32[]{:S(2)}) %collective-permute-start.1) | collective-permute-done | bytes 327712 | tf_op jit(solution)/shard_map/ppermute | solution.py:274
  25.5 0.0 collective-permute-done.8.tail_ref
  25.5 1.4 %collective-permute-done.9 = f32[1,256]{1,0:T(1,128)S(1)} collective-permute-done((f32[1,256]{1,0:T(1,128)S(1)}, f32[1,256]{1,0:T(1,128)S(1)}, u32[]{:S(2)}, u32[]{:S(2)}) %collective-permute-start.9) | collective-permute-done | bytes 1056 | tf_op jit(solution)/shard_map/ppermute | solution.py:274
  26.9 1.3 %collective-permute-start.10 = (f32[1,256]{1,0:T(1,128)S(1)}, f32[1,256]{1,0:T(1,128)S(1)}, u32[]{:S(2)}, u32[]{:S(2)}) collective-permute-start(f32[1,256]{1,0:T(1,128)S(1)} %get-tuple-element.41), channel_id=1, source_target_pairs={{8,0},{9,1},{10,2},{11,3},{12,4},{13,5},{14,6},{15,7},{24,16},{25,... | collective-permute-start | bytes 3080 | tf_op jit(solution)/shard_map/ppermute | solution.py:274
  28.2 0.2 shard_map.33
  28.4 1.6 %collective-permute-start.11 = (f32[1,256]{1,0:T(1,128)S(1)}, f32[1,256]{1,0:T(1,128)S(1)}, u32[]{:S(2)}, u32[]{:S(2)}) collective-permute-start(f32[1,256]{1,0:T(1,128)S(1)} %get-tuple-element.42), channel_id=1, source_target_pairs={{0,2},{1,3},{2,0},{3,1},{4,6},{5,7},{6,4},{7,5},{8,10},{9,11},{10,... | collective-permute-start | bytes 3080 | tf_op jit(solution)/shard_map/ppermute | solution.py:270
  30.0 0.0 collective-permute-start.12
  30.0 0.6 %collective-permute-start.13 = (f32[1,256]{1,0:T(1,128)S(1)}, f32[1,256]{1,0:T(1,128)S(1)}, u32[]{:S(2)}, u32[]{:S(2)}) collective-permute-start(f32[1,256]{1,0:T(1,128)S(1)} %get-tuple-element.44), channel_id=1, source_target_pairs={{0,1},{1,0},{2,3},{3,2},{4,5},{5,4},{6,7},{7,6},{8,9},{9,8},{10,11... | collective-permute-start | bytes 3080 | tf_op jit(solution)/shard_map/ppermute | solution.py:270
  30.6 3.8 %collective-permute-done.10 = f32[1,256]{1,0:T(1,128)S(1)} collective-permute-done((f32[1,256]{1,0:T(1,128)S(1)}, f32[1,256]{1,0:T(1,128)S(1)}, u32[]{:S(2)}, u32[]{:S(2)}) %collective-permute-start.10) | collective-permute-done | bytes 1056 | tf_op jit(solution)/shard_map/ppermute | solution.py:274
  34.4 0.0 collective-permute-done.11
  34.4 0.0 collective-permute-done.12
  34.4 0.0 collective-permute-done.13
  34.4 0.6 %add_log-plus-one_fusion = f32[1,256]{1,0:T(1,128)} fusion(f32[1,256]{1,0:T(1,128)S(1)} %collective-permute-done.13, f32[1,256]{1,0:T(1,128)S(1)} %collective-permute-done.12, f32[1,256]{1,0:T(1,128)S(1)} %collective-permute-done.11, f32[1,256]{1,0:T(1,128)S(1)} %collective-permute-done.10, f32[1,256]{1,0:T(1,128)S(1)} %get-tuple-element.37, ...), kind=kLoop, calls=%fused_computation | loop fusion | flops 1280 | bytes 7168 | tf_op jit(solution)/shard_map/log1p | solution.py:333
  (2 shorter events, 0.0 us)
Async XLA Ops:
  0.0 4.2 %copy-start = (bf16[256,1024]{1,0:T(8,128)(2,1)S(1)}, bf16[256,1024]{1,0:T(8,128)(2,1)}, u32[]{:S(2)}) copy-start(bf16[256,1024]{1,0:T(8,128)(2,1)} %rows_ref.1) | copy-start | bytes 1572868
  1.1 3.1 %copy-start.1 = (s32[256]{0:T(256)S(1)}, s32[256]{0:T(256)}, u32[]{:S(2)}) copy-start(s32[256]{0:T(256)} %param.3) | copy-start | bytes 3076
  1.1 13.6 %collective-permute-start = (bf16[160,1024]{1,0:T(8,128)(2,1)S(1)}, bf16[160,1024]{1,0:T(8,128)(2,1)S(1)}, u32[]{:S(2)}, u32[]{:S(2)}) collective-permute-start(bf16[160,1024]{1,0:T(8,128)(2,1)S(1)} %slice.3), channel_id=1, source_target_pairs={{0,4},{1,5},{2,6},{3,7},{4,8},{5,9},{6,10},{7,11},{8,12},{9,13},{1... | collective-permute-start | bytes 983048 | tf_op jit(solution)/shard_map/ppermute | solution.py:274
  4.4 10.4 %collective-permute-start.4 = (bf16[136,1024]{1,0:T(8,128)(2,1)S(1)}, bf16[136,1024]{1,0:T(8,128)(2,1)S(1)}, u32[]{:S(2)}, u32[]{:S(2)}) collective-permute-start(bf16[136,1024]{1,0:T(8,128)(2,1)S(1)} %get-tuple-element.27), channel_id=1, source_target_pairs={{0,2},{1,3},{2,0},{3,1},{4,6},{5,7},{6,4},{7,5},{8,10},{9,11},{10,... | collective-permute-start | bytes 835592 | tf_op jit(solution)/shard_map/ppermute | solution.py:270
  5.9 14.1 %collective-permute-start.2 = (bf16[264,1024]{1,0:T(8,128)(2,1)S(1)}, bf16[264,1024]{1,0:T(8,128)(2,1)S(1)}, u32[]{:S(2)}, u32[]{:S(2)}) collective-permute-start(bf16[264,1024]{1,0:T(8,128)(2,1)S(1)} %get-tuple-element.25.refs_0_.own_ref), channel_id=1, source_target_pairs={{0,1},{1,0},{2,3},{3,2},{4,5},{5,4},{6,7},{7,6},{8,9},{9,8},{10,11... | collective-permute-start | bytes 1622024 | tf_op jit(solution)/shard_map/ppermute | solution.py:270
  5.9 12.2 %collective-permute-start.3 = (bf16[128,1024]{1,0:T(8,128)(2,1)S(1)}, bf16[128,1024]{1,0:T(8,128)(2,1)S(1)}, u32[]{:S(2)}, u32[]{:S(2)}) collective-permute-start(bf16[128,1024]{1,0:T(8,128)(2,1)S(1)} %get-tuple-element.26), channel_id=1, source_target_pairs={{0,2},{1,3},{2,0},{3,1},{4,6},{5,7},{6,4},{7,5},{8,10},{9,11},{10,... | collective-permute-start | bytes 786440 | tf_op jit(solution)/shard_map/ppermute | solution.py:270
  6.8 12.5 %collective-permute-start.7 = (bf16[104,1024]{1,0:T(8,128)(2,1)S(1)}, bf16[104,1024]{1,0:T(8,128)(2,1)S(1)}, u32[]{:S(2)}, u32[]{:S(2)}) collective-permute-start(bf16[104,1024]{1,0:T(8,128)(2,1)S(1)} %get-tuple-element.31), channel_id=1, source_target_pairs={{0,4},{1,5},{2,6},{3,7},{4,8},{5,9},{6,10},{7,11},{8,12},{9,13},{1... | collective-permute-start | bytes 638984 | tf_op jit(solution)/shard_map/ppermute | solution.py:274
  14.7 10.8 %collective-permute-start.1 = (bf16[160,1024]{1,0:T(8,128)(2,1)S(1)}, bf16[160,1024]{1,0:T(8,128)(2,1)S(1)}, u32[]{:S(2)}, u32[]{:S(2)}) collective-permute-start(bf16[160,1024]{1,0:T(8,128)(2,1)S(1)} %collective-permute-done.head_ref), channel_id=1, source_target_pairs={{0,4},{1,5},{2,6},{3,7},{4,8},{5,9},{6,10},{7,11},{8,12},{9,13},{1... | collective-permute-start | bytes 983048 | tf_op jit(solution)/shard_map/ppermute | solution.py:274
  14.8 5.2 %collective-permute-start.6 = (bf16[136,1024]{1,0:T(8,128)(2,1)S(1)}, bf16[136,1024]{1,0:T(8,128)(2,1)S(1)}, u32[]{:S(2)}, u32[]{:S(2)}) collective-permute-start(bf16[136,1024]{1,0:T(8,128)(2,1)S(1)} %collective-permute-done.4.refs_3_), channel_id=1, source_target_pairs={{0,1},{1,0},{2,3},{3,2},{4,5},{5,4},{6,7},{7,6},{8,9},{9,8},{10,11... | collective-permute-start | bytes 835592 | tf_op jit(solution)/shard_map/ppermute | solution.py:270
  18.2 1.8 %collective-permute-start.5 = (bf16[128,1024]{1,0:T(8,128)(2,1)S(1)}, bf16[128,1024]{1,0:T(8,128)(2,1)S(1)}, u32[]{:S(2)}, u32[]{:S(2)}) collective-permute-start(bf16[128,1024]{1,0:T(8,128)(2,1)S(1)} %collective-permute-done.3.refs_2_), channel_id=1, source_target_pairs={{0,1},{1,0},{2,3},{3,2},{4,5},{5,4},{6,7},{7,6},{8,9},{9,8},{10,11... | collective-permute-start | bytes 786440 | tf_op jit(solution)/shard_map/ppermute | solution.py:270
  19.3 6.2 %collective-permute-start.8 = (bf16[104,1024]{1,0:T(8,128)(2,1)S(1)}, bf16[104,1024]{1,0:T(8,128)(2,1)S(1)}, u32[]{:S(2)}, u32[]{:S(2)}) collective-permute-start(bf16[104,1024]{1,0:T(8,128)(2,1)S(1)} %collective-permute-done.7.tail_ref), channel_id=1, source_target_pairs={{4,8},{5,9},{6,10},{7,11},{8,12},{9,13},{10,14},{11,15},{20,24},{2... | collective-permute-start | bytes 638984 | tf_op jit(solution)/shard_map/ppermute | solution.py:274
  22.0 4.9 %collective-permute-start.9 = (f32[1,256]{1,0:T(1,128)S(1)}, f32[1,256]{1,0:T(1,128)S(1)}, u32[]{:S(2)}, u32[]{:S(2)}) collective-permute-start(f32[1,256]{1,0:T(1,128)S(1)} %get-tuple-element.38), channel_id=1, source_target_pairs={{4,0},{5,1},{6,2},{7,3},{8,4},{9,5},{10,6},{11,7},{12,8},{13,9},{1... | collective-permute-start | bytes 3080 | tf_op jit(solution)/shard_map/ppermute | solution.py:274
  26.9 7.5 %collective-permute-start.10 = (f32[1,256]{1,0:T(1,128)S(1)}, f32[1,256]{1,0:T(1,128)S(1)}, u32[]{:S(2)}, u32[]{:S(2)}) collective-permute-start(f32[1,256]{1,0:T(1,128)S(1)} %get-tuple-element.41), channel_id=1, source_target_pairs={{8,0},{9,1},{10,2},{11,3},{12,4},{13,5},{14,6},{15,7},{24,16},{25,... | collective-permute-start | bytes 3080 | tf_op jit(solution)/shard_map/ppermute | solution.py:274
  28.4 6.0 %collective-permute-start.11 = (f32[1,256]{1,0:T(1,128)S(1)}, f32[1,256]{1,0:T(1,128)S(1)}, u32[]{:S(2)}, u32[]{:S(2)}) collective-permute-start(f32[1,256]{1,0:T(1,128)S(1)} %get-tuple-element.42), channel_id=1, source_target_pairs={{0,2},{1,3},{2,0},{3,1},{4,6},{5,7},{6,4},{7,5},{8,10},{9,11},{10,... | collective-permute-start | bytes 3080 | tf_op jit(solution)/shard_map/ppermute | solution.py:270
  30.0 4.5 %collective-permute-start.12 = (f32[1,256]{1,0:T(1,128)S(1)}, f32[1,256]{1,0:T(1,128)S(1)}, u32[]{:S(2)}, u32[]{:S(2)}) collective-permute-start(f32[1,256]{1,0:T(1,128)S(1)} %get-tuple-element.43), channel_id=1, source_target_pairs={{0,3},{1,2},{2,1},{3,0},{4,7},{5,6},{6,5},{7,4},{8,11},{9,10},{10,... | collective-permute-start | bytes 3080 | tf_op jit(solution)/shard_map/ppermute | solution.py:270
  30.0 4.5 %collective-permute-start.13 = (f32[1,256]{1,0:T(1,128)S(1)}, f32[1,256]{1,0:T(1,128)S(1)}, u32[]{:S(2)}, u32[]{:S(2)}) collective-permute-start(f32[1,256]{1,0:T(1,128)S(1)} %get-tuple-element.44), channel_id=1, source_target_pairs={{0,1},{1,0},{2,3},{3,2},{4,5},{5,4},{6,7},{7,6},{8,9},{9,8},{10,11... | collective-permute-start | bytes 3080 | tf_op jit(solution)/shard_map/ppermute | solution.py:270

commit v28 on v27

--- a/solution.py
+++ b/solution.py
@@ -269,8 +269,8 @@
     def in_plane(value, step):
         return lax.ppermute(value, "gx", [(i, i ^ step) for i in range(peers)])
 
-    def on_line(value, moves):
-        pairs = [(a * PLANE + n, b * PLANE + n) for a, b in moves for n in range(PLANE)]
+    def on_line(value, moves, flip):
+        pairs = [(a * PLANE + n, b * PLANE + (n ^ flip)) for a, b in moves for n in range(PLANE)]
         return lax.ppermute(value, "gx", pairs)
 
     first_moves = [(0, 1), (1, 2), (2, 3), (3, 0)]
@@ -282,7 +282,7 @@
     half, part = row_count // 2, 5 * row_count // 8
     ranges = [(0, row_count), (0, half), (half, row_count), (part, row_count)]
     id_rows = [ID_ROWS, 0, ID_ROWS, ID_ROWS]
-    first_head = on_line(embeddings[:part], first_moves)
+    first_head = on_line(embeddings[:part], first_moves, 1)
     block, *pieces, tail = pl.pallas_call(
         functools.partial(unit_kernel, ranges),
         out_shape=[rows_of(b - a + extra) for (a, b), extra in zip(ranges, id_rows)],
@@ -293,11 +293,11 @@
         own_kernel, out_shape=vector, cost_estimate=small, compiler_params=params
     )(block)
     own_mass, tail = lax.optimization_barrier((own_mass, tail))
-    first_tail = on_line(tail, first_moves)
+    first_tail = on_line(tail, first_moves, 1)
     across = [in_plane(piece, 2) for piece in pieces]
     sibling = in_plane(block, 1)
-    last_head = on_line(first_head, first_moves)
-    last_tail = on_line(first_tail, forward_moves)
+    last_head = on_line(first_head, first_moves, 1)
+    last_tail = on_line(first_tail, forward_moves, 1)
     corner = [in_plane(piece, 1) for piece in across]
     queries = (block, sibling, *across, *corner)
     ids, first_column, first_sums, mass = pl.pallas_call(
@@ -306,7 +306,7 @@
         cost_estimate=small,
         compiler_params=params,
     )(own_mass, first_head, first_tail, *queries)
-    returned_first = on_line(first_column, first_back)
+    returned_first = on_line(first_column, first_back, 1)
     powers, rest = pl.pallas_call(
         functools.partial(middle_kernel, last_moves),
         out_shape=(
@@ -328,7 +328,7 @@
         cost_estimate=small,
         compiler_params=params,
     )(sums, mass)
-    returned = [on_line(last_column, last_back)]
+    returned = [on_line(last_column, last_back, 0)]
     returned += [in_plane(row_sums[step], step) for step in (2, 3, 1)]
     return jnp.log1p(sum(returned, row_sums[0] + returned_first)).reshape(row_count)
 

time: 35.2 us -> 35.5 us (level)
  starting transfers between devices: 13.7 us -> 14.3 us
    ppermute x6, waiting for transfers between devices: 13.3 us -> 11.8 us  [on_line(): return lax.ppermute(value, 'gx', pairs)]
    ppermute x8, starting transfers between devices: 4.31 us -> 5.64 us  [in_plane(): return lax.ppermute(value, 'gx', [(i, i ^ step) for i in range(peers)])]
    ppermute x8, waiting for transfers between devices: 3.42 us -> 4.75 us  [in_plane(): return lax.ppermute(value, 'gx', [(i, i ^ step) for i in range(peers)])]
    ppermute x6, starting transfers between devices: 9.4 us -> 8.69 us  [on_line(): return lax.ppermute(value, 'gx', pairs)]
  transfers between devices with their start and end apart: 14 -> 14, of which waited for: 6 -> 5; matrix products, arithmetic and copies ran while one was open for 0% -> 0% of each run, Pallas kernels for 8% -> 8%
where the time goes in v28:
time: 35.5 us; the launch traced here: 35.4 us
  waiting for transfers between devices  16.5 us (46%)
  starting transfers between devices  14.3 us (40%)
  Pallas kernels  2.8 us (8%)
  local copies, waits for them, and re-layouts  1.08 us (3%)
  other arithmetic  0.58 us (2%)
    ppermute x6, waiting for transfers between devices, on_line(): return lax.ppermute(value, 'gx', pairs)  11.8 us
    ppermute x6, starting transfers between devices, on_line(): return lax.ppermute(value, 'gx', pairs)  8.69 us
    ppermute x8, starting transfers between devices, in_plane(): return lax.ppermute(value, 'gx', [(i, i ^ step) for i in range(peers)])  5.64 us
    ppermute x8, waiting for transfers between devices, in_plane(): return lax.ppermute(value, 'gx', [(i, i ^ step) for i in range(peers)])  4.75 us
    pallas_call x1, Pallas kernels, grid_plan(): pl.pallas_call(functools.partial(first_kernel, first_moves), out_shape=(l...  2.01 us
    slice x1, local copies, waits for them, and re-layouts, grid_plan(): first_head = on_line(embeddings[:part], first_moves, 1)  1.07 us
  transfers between devices with their start and end apart: 14, of which 5 were waited for; matrix products, arithmetic and copies ran while one was open for 0% of the time, Pallas kernels for 8%

profile of v28, /device:TPU:0, one launch (start us, length us, event | category | flops | bytes accessed | tf_op | source)
XLA Modules:
  0.0 35.4 jit_solution(6103235597679467204)
XLA Ops:
  0.0 0.0 copy-start
  0.0 1.1 %slice.3 = bf16[160,1024]{1,0:T(8,128)(2,1)S(1)} slice(bf16[256,1024]{1,0:T(8,128)(2,1)} %rows_ref.1), slice={[0:160], [0:1024]} | slice | bytes 655360 | tf_op jit(solution)/shard_map/slice | solution.py:285
  1.1 0.0 copy-start.1
  1.1 2.5 %collective-permute-start = (bf16[160,1024]{1,0:T(8,128)(2,1)S(1)}, bf16[160,1024]{1,0:T(8,128)(2,1)S(1)}, u32[]{:S(2)}, u32[]{:S(2)}) collective-permute-start(bf16[160,1024]{1,0:T(8,128)(2,1)S(1)} %slice.3), channel_id=1, source_target_pairs={{0,5},{1,4},{2,7},{3,6},{4,9},{5,8},{6,11},{7,10},{8,13},{9,12},{1... | collective-permute-start | bytes 983048 | tf_op jit(solution)/shard_map/ppermute | solution.py:274
  3.6 0.0 copy-done
  3.6 0.0 copy-done.1
  3.6 0.2 shard_map.28
  3.8 1.6 %collective-permute-start.4 = (bf16[136,1024]{1,0:T(8,128)(2,1)S(1)}, bf16[136,1024]{1,0:T(8,128)(2,1)S(1)}, u32[]{:S(2)}, u32[]{:S(2)}) collective-permute-start(bf16[136,1024]{1,0:T(8,128)(2,1)S(1)} %get-tuple-element.27), channel_id=1, source_target_pairs={{0,2},{1,3},{2,0},{3,1},{4,6},{5,7},{6,4},{7,5},{8,10},{9,11},{10,... | collective-permute-start | bytes 835592 | tf_op jit(solution)/shard_map/ppermute | solution.py:270
  5.4 0.4 %collective-permute-start.2 = (bf16[264,1024]{1,0:T(8,128)(2,1)S(1)}, bf16[264,1024]{1,0:T(8,128)(2,1)S(1)}, u32[]{:S(2)}, u32[]{:S(2)}) collective-permute-start(bf16[264,1024]{1,0:T(8,128)(2,1)S(1)} %get-tuple-element.25.refs_0_.own_ref), channel_id=1, source_target_pairs={{0,1},{1,0},{2,3},{3,2},{4,5},{5,4},{6,7},{7,6},{8,9},{9,8},{10,11... | collective-permute-start | bytes 1622024 | tf_op jit(solution)/shard_map/ppermute | solution.py:270
  5.8 0.5 %collective-permute-start.3 = (bf16[128,1024]{1,0:T(8,128)(2,1)S(1)}, bf16[128,1024]{1,0:T(8,128)(2,1)S(1)}, u32[]{:S(2)}, u32[]{:S(2)}) collective-permute-start(bf16[128,1024]{1,0:T(8,128)(2,1)S(1)} %get-tuple-element.26), channel_id=1, source_target_pairs={{0,2},{1,3},{2,0},{3,1},{4,6},{5,7},{6,4},{7,5},{8,10},{9,11},{10,... | collective-permute-start | bytes 786440 | tf_op jit(solution)/shard_map/ppermute | solution.py:270
  6.3 0.3 shard_map.30.own_mass_ref
  6.6 1.1 %collective-permute-start.7 = (bf16[104,1024]{1,0:T(8,128)(2,1)S(1)}, bf16[104,1024]{1,0:T(8,128)(2,1)S(1)}, u32[]{:S(2)}, u32[]{:S(2)}) collective-permute-start(bf16[104,1024]{1,0:T(8,128)(2,1)S(1)} %get-tuple-element.31), channel_id=1, source_target_pairs={{0,5},{1,4},{2,7},{3,6},{4,9},{5,8},{6,11},{7,10},{8,13},{9,12},{1... | collective-permute-start | bytes 638984 | tf_op jit(solution)/shard_map/ppermute | solution.py:274
  7.7 5.3 %collective-permute-done.head_ref = bf16[160,1024]{1,0:T(8,128)(2,1)S(1)} collective-permute-done((bf16[160,1024]{1,0:T(8,128)(2,1)S(1)}, bf16[160,1024]{1,0:T(8,128)(2,1)S(1)}, u32[]{:S(2)}, u32[]{:S(2)}) %collective-permute-start) | collective-permute-done | bytes 327712 | tf_op jit(solution)/shard_map/ppermute | solution.py:274
  13.1 0.8 %collective-permute-start.1 = (bf16[160,1024]{1,0:T(8,128)(2,1)S(1)}, bf16[160,1024]{1,0:T(8,128)(2,1)S(1)}, u32[]{:S(2)}, u32[]{:S(2)}) collective-permute-start(bf16[160,1024]{1,0:T(8,128)(2,1)S(1)} %collective-permute-done.head_ref), channel_id=1, source_target_pairs={{0,5},{1,4},{2,7},{3,6},{4,9},{5,8},{6,11},{7,10},{8,13},{9,12},{1... | collective-permute-start | bytes 983048 | tf_op jit(solution)/shard_map/ppermute | solution.py:274
  13.9 0.0 collective-permute-done.4.refs_3_
  13.9 0.9 %collective-permute-start.6 = (bf16[136,1024]{1,0:T(8,128)(2,1)S(1)}, bf16[136,1024]{1,0:T(8,128)(2,1)S(1)}, u32[]{:S(2)}, u32[]{:S(2)}) collective-permute-start(bf16[136,1024]{1,0:T(8,128)(2,1)S(1)} %collective-permute-done.4.refs_3_), channel_id=1, source_target_pairs={{0,1},{1,0},{2,3},{3,2},{4,5},{5,4},{6,7},{7,6},{8,9},{9,8},{10,11... | collective-permute-start | bytes 835592 | tf_op jit(solution)/shard_map/ppermute | solution.py:270
  14.8 3.9 %collective-permute-done.3.refs_2_ = bf16[128,1024]{1,0:T(8,128)(2,1)S(1)} collective-permute-done((bf16[128,1024]{1,0:T(8,128)(2,1)S(1)}, bf16[128,1024]{1,0:T(8,128)(2,1)S(1)}, u32[]{:S(2)}, u32[]{:S(2)}) %collective-permute-start.3) | collective-permute-done | bytes 262176 | tf_op jit(solution)/shard_map/ppermute | solution.py:270
  18.7 0.0 collective-permute-start.5
  18.7 0.0 collective-permute-done.7.tail_ref
  18.7 0.7 %collective-permute-start.8 = (bf16[104,1024]{1,0:T(8,128)(2,1)S(1)}, bf16[104,1024]{1,0:T(8,128)(2,1)S(1)}, u32[]{:S(2)}, u32[]{:S(2)}) collective-permute-start(bf16[104,1024]{1,0:T(8,128)(2,1)S(1)} %collective-permute-done.7.tail_ref), channel_id=1, source_target_pairs={{4,9},{5,8},{6,11},{7,10},{8,13},{9,12},{10,15},{11,14},{20,25},{2... | collective-permute-start | bytes 638984 | tf_op jit(solution)/shard_map/ppermute | solution.py:274
  19.4 0.9 %collective-permute-done.5.refs_4_ = bf16[128,1024]{1,0:T(8,128)(2,1)S(1)} collective-permute-done((bf16[128,1024]{1,0:T(8,128)(2,1)S(1)}, bf16[128,1024]{1,0:T(8,128)(2,1)S(1)}, u32[]{:S(2)}, u32[]{:S(2)}) %collective-permute-start.5) | collective-permute-done | bytes 262176 | tf_op jit(solution)/shard_map/ppermute | solution.py:270
  20.3 0.0 collective-permute-done.2.refs_1_
  20.3 0.0 collective-permute-done.6.refs_5_
  20.3 2.0 %shard_map.31 = (f32[1024,128]{1,0:T(8,128)S(1)}, f32[1,256]{1,0:T(1,128)S(1)}, f32[1024,128]{1,0:T(8,128)S(1)}, f32[1,256]{1,0:T(1,128)S(1)}) custom-call(f32[1,256]{1,0:T(1,128)S(1)} %shard_map.30.own_mass_ref, bf16[160,1024]{1,0:T(8,128)(2,1)S(1)} %collective-permute-done.head_ref, bf16[104,1024]{1,0:T(8,128)(2,1)S(1)} %collective-permute-done.7.tail_ref, ...), custom_call_target="tpu_custom_call" | custom-call | flops 1 | bytes 1 | tf_op jit(solution)/shard_map/pallas_call | solution.py:303
  22.3 2.3 %collective-permute-start.9 = (f32[1,256]{1,0:T(1,128)S(1)}, f32[1,256]{1,0:T(1,128)S(1)}, u32[]{:S(2)}, u32[]{:S(2)}) collective-permute-start(f32[1,256]{1,0:T(1,128)S(1)} %get-tuple-element.38), channel_id=1, source_target_pairs={{4,1},{5,0},{6,3},{7,2},{8,5},{9,4},{10,7},{11,6},{12,9},{13,8},{1... | collective-permute-start | bytes 3080 | tf_op jit(solution)/shard_map/ppermute | solution.py:274
  24.6 0.0 collective-permute-done.1.head_ref
  24.6 0.0 collective-permute-done.8.tail_ref
  24.7 2.2 %collective-permute-done.9 = f32[1,256]{1,0:T(1,128)S(1)} collective-permute-done((f32[1,256]{1,0:T(1,128)S(1)}, f32[1,256]{1,0:T(1,128)S(1)}, u32[]{:S(2)}, u32[]{:S(2)}) %collective-permute-start.9) | collective-permute-done | bytes 1056 | tf_op jit(solution)/shard_map/ppermute | solution.py:274
  26.9 1.3 %collective-permute-start.10 = (f32[1,256]{1,0:T(1,128)S(1)}, f32[1,256]{1,0:T(1,128)S(1)}, u32[]{:S(2)}, u32[]{:S(2)}) collective-permute-start(f32[1,256]{1,0:T(1,128)S(1)} %get-tuple-element.41), channel_id=1, source_target_pairs={{8,0},{9,1},{10,2},{11,3},{12,4},{13,5},{14,6},{15,7},{24,16},{25,... | collective-permute-start | bytes 3080 | tf_op jit(solution)/shard_map/ppermute | solution.py:274
  28.2 0.2 shard_map.33
  28.4 1.6 %collective-permute-start.11 = (f32[1,256]{1,0:T(1,128)S(1)}, f32[1,256]{1,0:T(1,128)S(1)}, u32[]{:S(2)}, u32[]{:S(2)}) collective-permute-start(f32[1,256]{1,0:T(1,128)S(1)} %get-tuple-element.42), channel_id=1, source_target_pairs={{0,2},{1,3},{2,0},{3,1},{4,6},{5,7},{6,4},{7,5},{8,10},{9,11},{10,... | collective-permute-start | bytes 3080 | tf_op jit(solution)/shard_map/ppermute | solution.py:270
  29.9 0.4 %collective-permute-start.12 = (f32[1,256]{1,0:T(1,128)S(1)}, f32[1,256]{1,0:T(1,128)S(1)}, u32[]{:S(2)}, u32[]{:S(2)}) collective-permute-start(f32[1,256]{1,0:T(1,128)S(1)} %get-tuple-element.43), channel_id=1, source_target_pairs={{0,3},{1,2},{2,1},{3,0},{4,7},{5,6},{6,5},{7,4},{8,11},{9,10},{10,... | collective-permute-start | bytes 3080 | tf_op jit(solution)/shard_map/ppermute | solution.py:270
  30.3 0.3 collective-permute-start.13
  30.6 4.2 %collective-permute-done.10 = f32[1,256]{1,0:T(1,128)S(1)} collective-permute-done((f32[1,256]{1,0:T(1,128)S(1)}, f32[1,256]{1,0:T(1,128)S(1)}, u32[]{:S(2)}, u32[]{:S(2)}) %collective-permute-start.10) | collective-permute-done | bytes 1056 | tf_op jit(solution)/shard_map/ppermute | solution.py:274
  34.8 0.0 collective-permute-done.11
  34.8 0.0 collective-permute-done.12
  34.8 0.0 collective-permute-done.13
  34.8 0.6 %add_log-plus-one_fusion = f32[1,256]{1,0:T(1,128)} fusion(f32[1,256]{1,0:T(1,128)S(1)} %collective-permute-done.13, f32[1,256]{1,0:T(1,128)S(1)} %collective-permute-done.12, f32[1,256]{1,0:T(1,128)S(1)} %collective-permute-done.11, f32[1,256]{1,0:T(1,128)S(1)} %collective-permute-done.10, f32[1,256]{1,0:T(1,128)S(1)} %get-tuple-element.37, ...), kind=kLoop, calls=%fused_computation | loop fusion | flops 1280 | bytes 7168 | tf_op jit(solution)/shard_map/log1p | solution.py:333
  (2 shorter events, 0.0 us)
Async XLA Ops:
  0.0 3.6 %copy-start = (bf16[256,1024]{1,0:T(8,128)(2,1)S(1)}, bf16[256,1024]{1,0:T(8,128)(2,1)}, u32[]{:S(2)}) copy-start(bf16[256,1024]{1,0:T(8,128)(2,1)} %rows_ref.1) | copy-start | bytes 1572868
  1.1 2.5 %copy-start.1 = (s32[256]{0:T(256)S(1)}, s32[256]{0:T(256)}, u32[]{:S(2)}) copy-start(s32[256]{0:T(256)} %param.3) | copy-start | bytes 3076
  1.1 12.0 %collective-permute-start = (bf16[160,1024]{1,0:T(8,128)(2,1)S(1)}, bf16[160,1024]{1,0:T(8,128)(2,1)S(1)}, u32[]{:S(2)}, u32[]{:S(2)}) collective-permute-start(bf16[160,1024]{1,0:T(8,128)(2,1)S(1)} %slice.3), channel_id=1, source_target_pairs={{0,5},{1,4},{2,7},{3,6},{4,9},{5,8},{6,11},{7,10},{8,13},{9,12},{1... | collective-permute-start | bytes 983048 | tf_op jit(solution)/shard_map/ppermute | solution.py:274
  3.8 10.1 %collective-permute-start.4 = (bf16[136,1024]{1,0:T(8,128)(2,1)S(1)}, bf16[136,1024]{1,0:T(8,128)(2,1)S(1)}, u32[]{:S(2)}, u32[]{:S(2)}) collective-permute-start(bf16[136,1024]{1,0:T(8,128)(2,1)S(1)} %get-tuple-element.27), channel_id=1, source_target_pairs={{0,2},{1,3},{2,0},{3,1},{4,6},{5,7},{6,4},{7,5},{8,10},{9,11},{10,... | collective-permute-start | bytes 835592 | tf_op jit(solution)/shard_map/ppermute | solution.py:270
  5.4 14.9 %collective-permute-start.2 = (bf16[264,1024]{1,0:T(8,128)(2,1)S(1)}, bf16[264,1024]{1,0:T(8,128)(2,1)S(1)}, u32[]{:S(2)}, u32[]{:S(2)}) collective-permute-start(bf16[264,1024]{1,0:T(8,128)(2,1)S(1)} %get-tuple-element.25.refs_0_.own_ref), channel_id=1, source_target_pairs={{0,1},{1,0},{2,3},{3,2},{4,5},{5,4},{6,7},{7,6},{8,9},{9,8},{10,11... | collective-permute-start | bytes 1622024 | tf_op jit(solution)/shard_map/ppermute | solution.py:270
  5.8 13.0 %collective-permute-start.3 = (bf16[128,1024]{1,0:T(8,128)(2,1)S(1)}, bf16[128,1024]{1,0:T(8,128)(2,1)S(1)}, u32[]{:S(2)}, u32[]{:S(2)}) collective-permute-start(bf16[128,1024]{1,0:T(8,128)(2,1)S(1)} %get-tuple-element.26), channel_id=1, source_target_pairs={{0,2},{1,3},{2,0},{3,1},{4,6},{5,7},{6,4},{7,5},{8,10},{9,11},{10,... | collective-permute-start | bytes 786440 | tf_op jit(solution)/shard_map/ppermute | solution.py:270
  6.6 12.1 %collective-permute-start.7 = (bf16[104,1024]{1,0:T(8,128)(2,1)S(1)}, bf16[104,1024]{1,0:T(8,128)(2,1)S(1)}, u32[]{:S(2)}, u32[]{:S(2)}) collective-permute-start(bf16[104,1024]{1,0:T(8,128)(2,1)S(1)} %get-tuple-element.31), channel_id=1, source_target_pairs={{0,5},{1,4},{2,7},{3,6},{4,9},{5,8},{6,11},{7,10},{8,13},{9,12},{1... | collective-permute-start | bytes 638984 | tf_op jit(solution)/shard_map/ppermute | solution.py:274
  13.1 11.6 %collective-permute-start.1 = (bf16[160,1024]{1,0:T(8,128)(2,1)S(1)}, bf16[160,1024]{1,0:T(8,128)(2,1)S(1)}, u32[]{:S(2)}, u32[]{:S(2)}) collective-permute-start(bf16[160,1024]{1,0:T(8,128)(2,1)S(1)} %collective-permute-done.head_ref), channel_id=1, source_target_pairs={{0,5},{1,4},{2,7},{3,6},{4,9},{5,8},{6,11},{7,10},{8,13},{9,12},{1... | collective-permute-start | bytes 983048 | tf_op jit(solution)/shard_map/ppermute | solution.py:274
  13.9 6.4 %collective-permute-start.6 = (bf16[136,1024]{1,0:T(8,128)(2,1)S(1)}, bf16[136,1024]{1,0:T(8,128)(2,1)S(1)}, u32[]{:S(2)}, u32[]{:S(2)}) collective-permute-start(bf16[136,1024]{1,0:T(8,128)(2,1)S(1)} %collective-permute-done.4.refs_3_), channel_id=1, source_target_pairs={{0,1},{1,0},{2,3},{3,2},{4,5},{5,4},{6,7},{7,6},{8,9},{9,8},{10,11... | collective-permute-start | bytes 835592 | tf_op jit(solution)/shard_map/ppermute | solution.py:270
  18.7 1.5 %collective-permute-start.5 = (bf16[128,1024]{1,0:T(8,128)(2,1)S(1)}, bf16[128,1024]{1,0:T(8,128)(2,1)S(1)}, u32[]{:S(2)}, u32[]{:S(2)}) collective-permute-start(bf16[128,1024]{1,0:T(8,128)(2,1)S(1)} %collective-permute-done.3.refs_2_), channel_id=1, source_target_pairs={{0,1},{1,0},{2,3},{3,2},{4,5},{5,4},{6,7},{7,6},{8,9},{9,8},{10,11... | collective-permute-start | bytes 786440 | tf_op jit(solution)/shard_map/ppermute | solution.py:270
  18.7 5.9 %collective-permute-start.8 = (bf16[104,1024]{1,0:T(8,128)(2,1)S(1)}, bf16[104,1024]{1,0:T(8,128)(2,1)S(1)}, u32[]{:S(2)}, u32[]{:S(2)}) collective-permute-start(bf16[104,1024]{1,0:T(8,128)(2,1)S(1)} %collective-permute-done.7.tail_ref), channel_id=1, source_target_pairs={{4,9},{5,8},{6,11},{7,10},{8,13},{9,12},{10,15},{11,14},{20,25},{2... | collective-permute-start | bytes 638984 | tf_op jit(solution)/shard_map/ppermute | solution.py:274
  22.3 4.6 %collective-permute-start.9 = (f32[1,256]{1,0:T(1,128)S(1)}, f32[1,256]{1,0:T(1,128)S(1)}, u32[]{:S(2)}, u32[]{:S(2)}) collective-permute-start(f32[1,256]{1,0:T(1,128)S(1)} %get-tuple-element.38), channel_id=1, source_target_pairs={{4,1},{5,0},{6,3},{7,2},{8,5},{9,4},{10,7},{11,6},{12,9},{13,8},{1... | collective-permute-start | bytes 3080 | tf_op jit(solution)/shard_map/ppermute | solution.py:274
  26.9 7.9 %collective-permute-start.10 = (f32[1,256]{1,0:T(1,128)S(1)}, f32[1,256]{1,0:T(1,128)S(1)}, u32[]{:S(2)}, u32[]{:S(2)}) collective-permute-start(f32[1,256]{1,0:T(1,128)S(1)} %get-tuple-element.41), channel_id=1, source_target_pairs={{8,0},{9,1},{10,2},{11,3},{12,4},{13,5},{14,6},{15,7},{24,16},{25,... | collective-permute-start | bytes 3080 | tf_op jit(solution)/shard_map/ppermute | solution.py:274
  28.4 6.4 %collective-permute-start.11 = (f32[1,256]{1,0:T(1,128)S(1)}, f32[1,256]{1,0:T(1,128)S(1)}, u32[]{:S(2)}, u32[]{:S(2)}) collective-permute-start(f32[1,256]{1,0:T(1,128)S(1)} %get-tuple-element.42), channel_id=1, source_target_pairs={{0,2},{1,3},{2,0},{3,1},{4,6},{5,7},{6,4},{7,5},{8,10},{9,11},{10,... | collective-permute-start | bytes 3080 | tf_op jit(solution)/shard_map/ppermute | solution.py:270
  29.9 4.8 %collective-permute-start.12 = (f32[1,256]{1,0:T(1,128)S(1)}, f32[1,256]{1,0:T(1,128)S(1)}, u32[]{:S(2)}, u32[]{:S(2)}) collective-permute-start(f32[1,256]{1,0:T(1,128)S(1)} %get-tuple-element.43), channel_id=1, source_target_pairs={{0,3},{1,2},{2,1},{3,0},{4,7},{5,6},{6,5},{7,4},{8,11},{9,10},{10,... | collective-permute-start | bytes 3080 | tf_op jit(solution)/shard_map/ppermute | solution.py:270
  30.3 4.5 %collective-permute-start.13 = (f32[1,256]{1,0:T(1,128)S(1)}, f32[1,256]{1,0:T(1,128)S(1)}, u32[]{:S(2)}, u32[]{:S(2)}) collective-permute-start(f32[1,256]{1,0:T(1,128)S(1)} %get-tuple-element.44), channel_id=1, source_target_pairs={{0,1},{1,0},{2,3},{3,2},{4,5},{5,4},{6,7},{7,6},{8,9},{9,8},{10,11... | collective-permute-start | bytes 3080 | tf_op jit(solution)/shard_map/ppermute | solution.py:270

commit v29 on v28

--- a/solution.py
+++ b/solution.py
@@ -282,7 +282,7 @@
     half, part = row_count // 2, 5 * row_count // 8
     ranges = [(0, row_count), (0, half), (half, row_count), (part, row_count)]
     id_rows = [ID_ROWS, 0, ID_ROWS, ID_ROWS]
-    first_head = on_line(embeddings[:part], first_moves, 1)
+    first_head = on_line(embeddings[:part], first_moves, 0)
     block, *pieces, tail = pl.pallas_call(
         functools.partial(unit_kernel, ranges),
         out_shape=[rows_of(b - a + extra) for (a, b), extra in zip(ranges, id_rows)],
@@ -293,7 +293,7 @@
         own_kernel, out_shape=vector, cost_estimate=small, compiler_params=params
     )(block)
     own_mass, tail = lax.optimization_barrier((own_mass, tail))
-    first_tail = on_line(tail, first_moves, 1)
+    first_tail = on_line(tail, first_moves, 0)
     across = [in_plane(piece, 2) for piece in pieces]
     sibling = in_plane(block, 1)
     last_head = on_line(first_head, first_moves, 1)
@@ -306,7 +306,7 @@
         cost_estimate=small,
         compiler_params=params,
     )(own_mass, first_head, first_tail, *queries)
-    returned_first = on_line(first_column, first_back, 1)
+    returned_first = on_line(first_column, first_back, 0)
     powers, rest = pl.pallas_call(
         functools.partial(middle_kernel, last_moves),
         out_shape=(
@@ -328,7 +328,7 @@
         cost_estimate=small,
         compiler_params=params,
     )(sums, mass)
-    returned = [on_line(last_column, last_back, 0)]
+    returned = [on_line(last_column, last_back, 1)]
     returned += [in_plane(row_sums[step], step) for step in (2, 3, 1)]
     return jnp.log1p(sum(returned, row_sums[0] + returned_first)).reshape(row_count)
 

time: 35.5 us -> 34.3 us (0.966)
  waiting for transfers between devices: 16.5 us -> 15.5 us
    ppermute x8, starting transfers between devices: 5.64 us -> 4.45 us  [in_plane(): return lax.ppermute(value, 'gx', [(i, i ^ step) for i in range(peers)])]
    ppermute x6, starting transfers between devices: 8.69 us -> 9.63 us  [on_line(): return lax.ppermute(value, 'gx', pairs)]
    ppermute x8, waiting for transfers between devices: 4.75 us -> 3.87 us  [in_plane(): return lax.ppermute(value, 'gx', [(i, i ^ step) for i in range(peers)])]
  transfers between devices with their start and end apart: 14 -> 14, of which waited for: 5 -> 7; matrix products, arithmetic and copies ran while one was open for 0% -> 0% of each run, Pallas kernels for 8% -> 8%
where the time goes in v29:
time: 34.3 us; the launch traced here: 34.1 us
  waiting for transfers between devices  15.5 us (45%)
  starting transfers between devices  14.1 us (41%)
  Pallas kernels  2.81 us (8%)
  local copies, waits for them, and re-layouts  1.08 us (3%)
  other arithmetic  0.58 us (2%)
    ppermute x6, waiting for transfers between devices, on_line(): return lax.ppermute(value, 'gx', pairs)  11.6 us
    ppermute x6, starting transfers between devices, on_line(): return lax.ppermute(value, 'gx', pairs)  9.63 us
    ppermute x8, starting transfers between devices, in_plane(): return lax.ppermute(value, 'gx', [(i, i ^ step) for i in range(peers)])  4.45 us
    ppermute x8, waiting for transfers between devices, in_plane(): return lax.ppermute(value, 'gx', [(i, i ^ step) for i in range(peers)])  3.87 us
    pallas_call x1, Pallas kernels, grid_plan(): pl.pallas_call(functools.partial(first_kernel, first_moves), out_shape=(l...  2.02 us
    slice x1, local copies, waits for them, and re-layouts, grid_plan(): first_head = on_line(embeddings[:part], first_moves, 0)  1.07 us
  transfers between devices with their start and end apart: 14, of which 7 were waited for; matrix products, arithmetic and copies ran while one was open for 0% of the time, Pallas kernels for 8%

profile of v29, /device:TPU:0, one launch (start us, length us, event | category | flops | bytes accessed | tf_op | source)
XLA Modules:
  0.0 34.1 jit_solution(10547351617339658005)
XLA Ops:
  0.0 0.0 copy-start
  0.0 1.1 %slice.3 = bf16[160,1024]{1,0:T(8,128)(2,1)S(1)} slice(bf16[256,1024]{1,0:T(8,128)(2,1)} %rows_ref.1), slice={[0:160], [0:1024]} | slice | bytes 655360 | tf_op jit(solution)/shard_map/slice | solution.py:285
  1.1 0.0 copy-start.1
  1.1 3.1 %collective-permute-start = (bf16[160,1024]{1,0:T(8,128)(2,1)S(1)}, bf16[160,1024]{1,0:T(8,128)(2,1)S(1)}, u32[]{:S(2)}, u32[]{:S(2)}) collective-permute-start(bf16[160,1024]{1,0:T(8,128)(2,1)S(1)} %slice.3), channel_id=1, source_target_pairs={{0,4},{1,5},{2,6},{3,7},{4,8},{5,9},{6,10},{7,11},{8,12},{9,13},{1... | collective-permute-start | bytes 983048 | tf_op jit(solution)/shard_map/ppermute | solution.py:274
  4.2 0.0 copy-done
  4.2 0.0 copy-done.1
  4.2 0.2 shard_map.28
  4.4 1.6 %collective-permute-start.4 = (bf16[136,1024]{1,0:T(8,128)(2,1)S(1)}, bf16[136,1024]{1,0:T(8,128)(2,1)S(1)}, u32[]{:S(2)}, u32[]{:S(2)}) collective-permute-start(bf16[136,1024]{1,0:T(8,128)(2,1)S(1)} %get-tuple-element.27), channel_id=1, source_target_pairs={{0,2},{1,3},{2,0},{3,1},{4,6},{5,7},{6,4},{7,5},{8,10},{9,11},{10,... | collective-permute-start | bytes 835592 | tf_op jit(solution)/shard_map/ppermute | solution.py:270
  5.9 0.0 collective-permute-start.2
  5.9 0.5 %collective-permute-start.3 = (bf16[128,1024]{1,0:T(8,128)(2,1)S(1)}, bf16[128,1024]{1,0:T(8,128)(2,1)S(1)}, u32[]{:S(2)}, u32[]{:S(2)}) collective-permute-start(bf16[128,1024]{1,0:T(8,128)(2,1)S(1)} %get-tuple-element.26), channel_id=1, source_target_pairs={{0,2},{1,3},{2,0},{3,1},{4,6},{5,7},{6,4},{7,5},{8,10},{9,11},{10,... | collective-permute-start | bytes 786440 | tf_op jit(solution)/shard_map/ppermute | solution.py:270
  6.5 0.3 %shard_map.30.own_mass_ref = f32[1,256]{1,0:T(1,128)S(1)} custom-call(bf16[264,1024]{1,0:T(8,128)(2,1)S(1)} %get-tuple-element.25.refs_0_.own_ref), custom_call_target="tpu_custom_call" | custom-call | flops 1 | bytes 1 | tf_op jit(solution)/shard_map/pallas_call | solution.py:292
  6.8 1.6 %collective-permute-start.7 = (bf16[104,1024]{1,0:T(8,128)(2,1)S(1)}, bf16[104,1024]{1,0:T(8,128)(2,1)S(1)}, u32[]{:S(2)}, u32[]{:S(2)}) collective-permute-start(bf16[104,1024]{1,0:T(8,128)(2,1)S(1)} %get-tuple-element.31), channel_id=1, source_target_pairs={{0,4},{1,5},{2,6},{3,7},{4,8},{5,9},{6,10},{7,11},{8,12},{9,13},{1... | collective-permute-start | bytes 638984 | tf_op jit(solution)/shard_map/ppermute | solution.py:274
  8.4 6.3 %collective-permute-done.head_ref = bf16[160,1024]{1,0:T(8,128)(2,1)S(1)} collective-permute-done((bf16[160,1024]{1,0:T(8,128)(2,1)S(1)}, bf16[160,1024]{1,0:T(8,128)(2,1)S(1)}, u32[]{:S(2)}, u32[]{:S(2)}) %collective-permute-start) | collective-permute-done | bytes 327712 | tf_op jit(solution)/shard_map/ppermute | solution.py:274
  14.7 0.0 collective-permute-start.1
  14.7 0.0 collective-permute-done.4.refs_3_
  14.7 0.1 collective-permute-start.6
  14.9 3.3 %collective-permute-done.3.refs_2_ = bf16[128,1024]{1,0:T(8,128)(2,1)S(1)} collective-permute-done((bf16[128,1024]{1,0:T(8,128)(2,1)S(1)}, bf16[128,1024]{1,0:T(8,128)(2,1)S(1)}, u32[]{:S(2)}, u32[]{:S(2)}) %collective-permute-start.3) | collective-permute-done | bytes 262176 | tf_op jit(solution)/shard_map/ppermute | solution.py:270
  18.2 0.0 collective-permute-start.5
  18.2 0.3 collective-permute-done.7.tail_ref
  18.5 0.7 %collective-permute-start.8 = (bf16[104,1024]{1,0:T(8,128)(2,1)S(1)}, bf16[104,1024]{1,0:T(8,128)(2,1)S(1)}, u32[]{:S(2)}, u32[]{:S(2)}) collective-permute-start(bf16[104,1024]{1,0:T(8,128)(2,1)S(1)} %collective-permute-done.7.tail_ref), channel_id=1, source_target_pairs={{4,9},{5,8},{6,11},{7,10},{8,13},{9,12},{10,15},{11,14},{20,25},{2... | collective-permute-start | bytes 638984 | tf_op jit(solution)/shard_map/ppermute | solution.py:274
  19.1 0.6 %collective-permute-done.5.refs_4_ = bf16[128,1024]{1,0:T(8,128)(2,1)S(1)} collective-permute-done((bf16[128,1024]{1,0:T(8,128)(2,1)S(1)}, bf16[128,1024]{1,0:T(8,128)(2,1)S(1)}, u32[]{:S(2)}, u32[]{:S(2)}) %collective-permute-start.5) | collective-permute-done | bytes 262176 | tf_op jit(solution)/shard_map/ppermute | solution.py:270
  19.7 0.0 collective-permute-done.2.refs_1_
  19.7 0.0 collective-permute-done.6.refs_5_
  19.7 2.0 %shard_map.31 = (f32[1024,128]{1,0:T(8,128)S(1)}, f32[1,256]{1,0:T(1,128)S(1)}, f32[1024,128]{1,0:T(8,128)S(1)}, f32[1,256]{1,0:T(1,128)S(1)}) custom-call(f32[1,256]{1,0:T(1,128)S(1)} %shard_map.30.own_mass_ref, bf16[160,1024]{1,0:T(8,128)(2,1)S(1)} %collective-permute-done.head_ref, bf16[104,1024]{1,0:T(8,128)(2,1)S(1)} %collective-permute-done.7.tail_ref, ...), custom_call_target="tpu_custom_call" | custom-call | flops 1 | bytes 1 | tf_op jit(solution)/shard_map/pallas_call | solution.py:303
  21.7 3.0 %collective-permute-start.9 = (f32[1,256]{1,0:T(1,128)S(1)}, f32[1,256]{1,0:T(1,128)S(1)}, u32[]{:S(2)}, u32[]{:S(2)}) collective-permute-start(f32[1,256]{1,0:T(1,128)S(1)} %get-tuple-element.38), channel_id=1, source_target_pairs={{4,0},{5,1},{6,2},{7,3},{8,4},{9,5},{10,6},{11,7},{12,8},{13,9},{1... | collective-permute-start | bytes 3080 | tf_op jit(solution)/shard_map/ppermute | solution.py:274
  24.7 0.8 %collective-permute-done.1.head_ref = bf16[160,1024]{1,0:T(8,128)(2,1)S(1)} collective-permute-done((bf16[160,1024]{1,0:T(8,128)(2,1)S(1)}, bf16[160,1024]{1,0:T(8,128)(2,1)S(1)}, u32[]{:S(2)}, u32[]{:S(2)}) %collective-permute-start.1) | collective-permute-done | bytes 327712 | tf_op jit(solution)/shard_map/ppermute | solution.py:274
  25.5 0.0 collective-permute-done.8.tail_ref
  25.5 1.5 %collective-permute-done.9 = f32[1,256]{1,0:T(1,128)S(1)} collective-permute-done((f32[1,256]{1,0:T(1,128)S(1)}, f32[1,256]{1,0:T(1,128)S(1)}, u32[]{:S(2)}, u32[]{:S(2)}) %collective-permute-start.9) | collective-permute-done | bytes 1056 | tf_op jit(solution)/shard_map/ppermute | solution.py:274
  27.0 1.3 %collective-permute-start.10 = (f32[1,256]{1,0:T(1,128)S(1)}, f32[1,256]{1,0:T(1,128)S(1)}, u32[]{:S(2)}, u32[]{:S(2)}) collective-permute-start(f32[1,256]{1,0:T(1,128)S(1)} %get-tuple-element.41), channel_id=1, source_target_pairs={{8,1},{9,0},{10,3},{11,2},{12,5},{13,4},{14,7},{15,6},{24,17},{25,... | collective-permute-start | bytes 3080 | tf_op jit(solution)/shard_map/ppermute | solution.py:274
  28.3 0.2 shard_map.33
  28.5 1.6 %collective-permute-start.11 = (f32[1,256]{1,0:T(1,128)S(1)}, f32[1,256]{1,0:T(1,128)S(1)}, u32[]{:S(2)}, u32[]{:S(2)}) collective-permute-start(f32[1,256]{1,0:T(1,128)S(1)} %get-tuple-element.42), channel_id=1, source_target_pairs={{0,2},{1,3},{2,0},{3,1},{4,6},{5,7},{6,4},{7,5},{8,10},{9,11},{10,... | collective-permute-start | bytes 3080 | tf_op jit(solution)/shard_map/ppermute | solution.py:270
  30.1 0.0 collective-permute-start.12
  30.1 0.6 %collective-permute-start.13 = (f32[1,256]{1,0:T(1,128)S(1)}, f32[1,256]{1,0:T(1,128)S(1)}, u32[]{:S(2)}, u32[]{:S(2)}) collective-permute-start(f32[1,256]{1,0:T(1,128)S(1)} %get-tuple-element.44), channel_id=1, source_target_pairs={{0,1},{1,0},{2,3},{3,2},{4,5},{5,4},{6,7},{7,6},{8,9},{9,8},{10,11... | collective-permute-start | bytes 3080 | tf_op jit(solution)/shard_map/ppermute | solution.py:270
  30.7 2.8 %collective-permute-done.10 = f32[1,256]{1,0:T(1,128)S(1)} collective-permute-done((f32[1,256]{1,0:T(1,128)S(1)}, f32[1,256]{1,0:T(1,128)S(1)}, u32[]{:S(2)}, u32[]{:S(2)}) %collective-permute-start.10) | collective-permute-done | bytes 1056 | tf_op jit(solution)/shard_map/ppermute | solution.py:274
  33.5 0.0 collective-permute-done.11
  33.5 0.0 collective-permute-done.12
  33.5 0.0 collective-permute-done.13
  33.5 0.6 %add_log-plus-one_fusion = f32[1,256]{1,0:T(1,128)} fusion(f32[1,256]{1,0:T(1,128)S(1)} %collective-permute-done.13, f32[1,256]{1,0:T(1,128)S(1)} %collective-permute-done.12, f32[1,256]{1,0:T(1,128)S(1)} %collective-permute-done.11, f32[1,256]{1,0:T(1,128)S(1)} %collective-permute-done.10, f32[1,256]{1,0:T(1,128)S(1)} %get-tuple-element.37, ...), kind=kLoop, calls=%fused_computation | loop fusion | flops 1280 | bytes 7168 | tf_op jit(solution)/shard_map/log1p | solution.py:333
  (2 shorter events, 0.0 us)
Async XLA Ops:
  0.0 4.2 %copy-start = (bf16[256,1024]{1,0:T(8,128)(2,1)S(1)}, bf16[256,1024]{1,0:T(8,128)(2,1)}, u32[]{:S(2)}) copy-start(bf16[256,1024]{1,0:T(8,128)(2,1)} %rows_ref.1) | copy-start | bytes 1572868
  1.1 3.1 %copy-start.1 = (s32[256]{0:T(256)S(1)}, s32[256]{0:T(256)}, u32[]{:S(2)}) copy-start(s32[256]{0:T(256)} %param.3) | copy-start | bytes 3076
  1.1 13.6 %collective-permute-start = (bf16[160,1024]{1,0:T(8,128)(2,1)S(1)}, bf16[160,1024]{1,0:T(8,128)(2,1)S(1)}, u32[]{:S(2)}, u32[]{:S(2)}) collective-permute-start(bf16[160,1024]{1,0:T(8,128)(2,1)S(1)} %slice.3), channel_id=1, source_target_pairs={{0,4},{1,5},{2,6},{3,7},{4,8},{5,9},{6,10},{7,11},{8,12},{9,13},{1... | collective-permute-start | bytes 983048 | tf_op jit(solution)/shard_map/ppermute | solution.py:274
  4.4 10.4 %collective-permute-start.4 = (bf16[136,1024]{1,0:T(8,128)(2,1)S(1)}, bf16[136,1024]{1,0:T(8,128)(2,1)S(1)}, u32[]{:S(2)}, u32[]{:S(2)}) collective-permute-start(bf16[136,1024]{1,0:T(8,128)(2,1)S(1)} %get-tuple-element.27), channel_id=1, source_target_pairs={{0,2},{1,3},{2,0},{3,1},{4,6},{5,7},{6,4},{7,5},{8,10},{9,11},{10,... | collective-permute-start | bytes 835592 | tf_op jit(solution)/shard_map/ppermute | solution.py:270
  5.9 13.8 %collective-permute-start.2 = (bf16[264,1024]{1,0:T(8,128)(2,1)S(1)}, bf16[264,1024]{1,0:T(8,128)(2,1)S(1)}, u32[]{:S(2)}, u32[]{:S(2)}) collective-permute-start(bf16[264,1024]{1,0:T(8,128)(2,1)S(1)} %get-tuple-element.25.refs_0_.own_ref), channel_id=1, source_target_pairs={{0,1},{1,0},{2,3},{3,2},{4,5},{5,4},{6,7},{7,6},{8,9},{9,8},{10,11... | collective-permute-start | bytes 1622024 | tf_op jit(solution)/shard_map/ppermute | solution.py:270
  5.9 12.2 %collective-permute-start.3 = (bf16[128,1024]{1,0:T(8,128)(2,1)S(1)}, bf16[128,1024]{1,0:T(8,128)(2,1)S(1)}, u32[]{:S(2)}, u32[]{:S(2)}) collective-permute-start(bf16[128,1024]{1,0:T(8,128)(2,1)S(1)} %get-tuple-element.26), channel_id=1, source_target_pairs={{0,2},{1,3},{2,0},{3,1},{4,6},{5,7},{6,4},{7,5},{8,10},{9,11},{10,... | collective-permute-start | bytes 786440 | tf_op jit(solution)/shard_map/ppermute | solution.py:270
  6.8 11.6 %collective-permute-start.7 = (bf16[104,1024]{1,0:T(8,128)(2,1)S(1)}, bf16[104,1024]{1,0:T(8,128)(2,1)S(1)}, u32[]{:S(2)}, u32[]{:S(2)}) collective-permute-start(bf16[104,1024]{1,0:T(8,128)(2,1)S(1)} %get-tuple-element.31), channel_id=1, source_target_pairs={{0,4},{1,5},{2,6},{3,7},{4,8},{5,9},{6,10},{7,11},{8,12},{9,13},{1... | collective-permute-start | bytes 638984 | tf_op jit(solution)/shard_map/ppermute | solution.py:274
  14.7 10.8 %collective-permute-start.1 = (bf16[160,1024]{1,0:T(8,128)(2,1)S(1)}, bf16[160,1024]{1,0:T(8,128)(2,1)S(1)}, u32[]{:S(2)}, u32[]{:S(2)}) collective-permute-start(bf16[160,1024]{1,0:T(8,128)(2,1)S(1)} %collective-permute-done.head_ref), channel_id=1, source_target_pairs={{0,5},{1,4},{2,7},{3,6},{4,9},{5,8},{6,11},{7,10},{8,13},{9,12},{1... | collective-permute-start | bytes 983048 | tf_op jit(solution)/shard_map/ppermute | solution.py:274
  14.7 5.0 %collective-permute-start.6 = (bf16[136,1024]{1,0:T(8,128)(2,1)S(1)}, bf16[136,1024]{1,0:T(8,128)(2,1)S(1)}, u32[]{:S(2)}, u32[]{:S(2)}) collective-permute-start(bf16[136,1024]{1,0:T(8,128)(2,1)S(1)} %collective-permute-done.4.refs_3_), channel_id=1, source_target_pairs={{0,1},{1,0},{2,3},{3,2},{4,5},{5,4},{6,7},{7,6},{8,9},{9,8},{10,11... | collective-permute-start | bytes 835592 | tf_op jit(solution)/shard_map/ppermute | solution.py:270
  18.2 1.5 %collective-permute-start.5 = (bf16[128,1024]{1,0:T(8,128)(2,1)S(1)}, bf16[128,1024]{1,0:T(8,128)(2,1)S(1)}, u32[]{:S(2)}, u32[]{:S(2)}) collective-permute-start(bf16[128,1024]{1,0:T(8,128)(2,1)S(1)} %collective-permute-done.3.refs_2_), channel_id=1, source_target_pairs={{0,1},{1,0},{2,3},{3,2},{4,5},{5,4},{6,7},{7,6},{8,9},{9,8},{10,11... | collective-permute-start | bytes 786440 | tf_op jit(solution)/shard_map/ppermute | solution.py:270
  18.5 7.0 %collective-permute-start.8 = (bf16[104,1024]{1,0:T(8,128)(2,1)S(1)}, bf16[104,1024]{1,0:T(8,128)(2,1)S(1)}, u32[]{:S(2)}, u32[]{:S(2)}) collective-permute-start(bf16[104,1024]{1,0:T(8,128)(2,1)S(1)} %collective-permute-done.7.tail_ref), channel_id=1, source_target_pairs={{4,9},{5,8},{6,11},{7,10},{8,13},{9,12},{10,15},{11,14},{20,25},{2... | collective-permute-start | bytes 638984 | tf_op jit(solution)/shard_map/ppermute | solution.py:274
  21.7 5.3 %collective-permute-start.9 = (f32[1,256]{1,0:T(1,128)S(1)}, f32[1,256]{1,0:T(1,128)S(1)}, u32[]{:S(2)}, u32[]{:S(2)}) collective-permute-start(f32[1,256]{1,0:T(1,128)S(1)} %get-tuple-element.38), channel_id=1, source_target_pairs={{4,0},{5,1},{6,2},{7,3},{8,4},{9,5},{10,6},{11,7},{12,8},{13,9},{1... | collective-permute-start | bytes 3080 | tf_op jit(solution)/shard_map/ppermute | solution.py:274
  27.0 6.5 %collective-permute-start.10 = (f32[1,256]{1,0:T(1,128)S(1)}, f32[1,256]{1,0:T(1,128)S(1)}, u32[]{:S(2)}, u32[]{:S(2)}) collective-permute-start(f32[1,256]{1,0:T(1,128)S(1)} %get-tuple-element.41), channel_id=1, source_target_pairs={{8,1},{9,0},{10,3},{11,2},{12,5},{13,4},{14,7},{15,6},{24,17},{25,... | collective-permute-start | bytes 3080 | tf_op jit(solution)/shard_map/ppermute | solution.py:274
  28.5 5.0 %collective-permute-start.11 = (f32[1,256]{1,0:T(1,128)S(1)}, f32[1,256]{1,0:T(1,128)S(1)}, u32[]{:S(2)}, u32[]{:S(2)}) collective-permute-start(f32[1,256]{1,0:T(1,128)S(1)} %get-tuple-element.42), channel_id=1, source_target_pairs={{0,2},{1,3},{2,0},{3,1},{4,6},{5,7},{6,4},{7,5},{8,10},{9,11},{10,... | collective-permute-start | bytes 3080 | tf_op jit(solution)/shard_map/ppermute | solution.py:270
  30.1 3.5 %collective-permute-start.12 = (f32[1,256]{1,0:T(1,128)S(1)}, f32[1,256]{1,0:T(1,128)S(1)}, u32[]{:S(2)}, u32[]{:S(2)}) collective-permute-start(f32[1,256]{1,0:T(1,128)S(1)} %get-tuple-element.43), channel_id=1, source_target_pairs={{0,3},{1,2},{2,1},{3,0},{4,7},{5,6},{6,5},{7,4},{8,11},{9,10},{10,... | collective-permute-start | bytes 3080 | tf_op jit(solution)/shard_map/ppermute | solution.py:270
  30.1 3.5 %collective-permute-start.13 = (f32[1,256]{1,0:T(1,128)S(1)}, f32[1,256]{1,0:T(1,128)S(1)}, u32[]{:S(2)}, u32[]{:S(2)}) collective-permute-start(f32[1,256]{1,0:T(1,128)S(1)} %get-tuple-element.44), channel_id=1, source_target_pairs={{0,1},{1,0},{2,3},{3,2},{4,5},{5,4},{6,7},{7,6},{8,9},{9,8},{10,11... | collective-permute-start | bytes 3080 | tf_op jit(solution)/shard_map/ppermute | solution.py:270

commit v30 on v29

--- a/solution.py
+++ b/solution.py
@@ -195,7 +195,7 @@
 
 
 def middle_kernel(moves, head_ref, *refs):
-    query_refs, (powers_ref, rest_ref) = refs[:-2], refs[-2:]
+    query_refs, (queries_ref, powers_ref, rest_ref) = refs[:-3], refs[-3:]
 
     @pl.when(arrived_at(moves))
     def _():
@@ -204,16 +204,17 @@
         rest_ref[...] = units[keys:]
         first = 0
         for query_ref, size in query_parts_of(query_refs, query_refs[0].shape[0] - ID_ROWS):
-            similar = lax.dot_general(
-                query_ref[:size, :], units[:keys], (((1,), (1,)), ((), ())),
-                preferred_element_type=jnp.float32,
-            )
-            powers_ref[pl.ds(first, size), :] = jnp.exp2(similar * INVERSE_TEMP_BITS)
+            queries_ref[pl.ds(first, size), :] = query_ref[:size, :]
             first += size
-
-
-def last_kernel(moves, powers_ref, rest_ref, tail_ref, ids_ref, earlier_ref, *refs):
-    query_refs, (column_ref, sums_ref) = refs[:-2], refs[-2:]
+        similar = lax.dot_general(
+            queries_ref[...], units[:keys], (((1,), (1,)), ((), ())),
+            preferred_element_type=jnp.float32,
+        )
+        powers_ref[...] = jnp.exp2(similar * INVERSE_TEMP_BITS)
+
+
+def last_kernel(moves, queries_ref, powers_ref, rest_ref, tail_ref, ids_ref, earlier_ref, *refs):
+    column_ref, sums_ref = refs
     rows = column_ref.shape[1]
     cut = powers_ref.shape[1]
     arrived = arrived_at(moves)
@@ -221,24 +222,17 @@
     @pl.when(arrived)
     def _():
         key_ids = ids_of(tail_ref)[:, :rows]
-        key_rows = jnp.concatenate([rest_ref[...], tail_ref[: tail_ref.shape[0] - ID_ROWS, :]], axis=0)
-        early_column = jnp.zeros((1, cut), jnp.float32)
-        late_column = jnp.zeros((1, rows - cut), jnp.float32)
-        first = 0
-        for query_ref, size in query_parts_of(query_refs, rows):
-            part = pl.ds(first, size)
-            query_ids = ids_ref[part, :]
-            similar = lax.dot_general(
-                query_ref[:size, :], key_rows, (((1,), (1,)), ((), ())),
-                preferred_element_type=jnp.float32,
-            )
-            powers = jnp.exp2(similar * INVERSE_TEMP_BITS)
-            late, column = add_masses(query_ids, key_ids[:, cut:], powers)
-            late_column = late_column + column
-            early, column = add_masses(query_ids, key_ids[:, :cut], powers_ref[part, :])
-            early_column = early_column + column
-            sums_ref[part, :] = earlier_ref[part, :] + early + late
-            first += size
+        tail = tail_ref[: tail_ref.shape[0] - ID_ROWS, :]
+        key_rows = jnp.concatenate([rest_ref[...], tail], axis=0)
+        similar = lax.dot_general(
+            queries_ref[...], key_rows, (((1,), (1,)), ((), ())),
+            preferred_element_type=jnp.float32,
+        )
+        query_ids = ids_ref[...]
+        powers = jnp.exp2(similar * INVERSE_TEMP_BITS)
+        late, late_column = add_masses(query_ids, key_ids[:, cut:], powers)
+        early, early_column = add_masses(query_ids, key_ids[:, :cut], powers_ref[...])
+        sums_ref[...] = earlier_ref[...] + early + late
         column_ref[...] = jnp.concatenate([early_column, late_column], axis=1)
 
     @pl.when(jnp.logical_not(arrived))
@@ -307,10 +301,12 @@
         compiler_params=params,
     )(own_mass, first_head, first_tail, *queries)
     returned_first = on_line(first_column, first_back, 0)
-    powers, rest = pl.pallas_call(
+    plane_queries, powers, rest = pl.pallas_call(
         functools.partial(middle_kernel, last_moves),
         out_shape=(
-            jax.ShapeDtypeStruct((plane_rows, half), jnp.float32), rows_of(part - half)
+            rows_of(plane_rows),
+            jax.ShapeDtypeStruct((plane_rows, half), jnp.float32),
+            rows_of(part - half),
         ),
         cost_estimate=small,
         compiler_params=params,
@@ -320,7 +316,7 @@
         out_shape=(vector, lanes),
         cost_estimate=small,
         compiler_params=params,
-    )(powers, rest, last_tail, ids, first_sums, *queries)
+    )(plane_queries, powers, rest, last_tail, ids, first_sums)
     returned_first, last_column = lax.optimization_barrier((returned_first, last_column))
     row_sums = pl.pallas_call(
         fold_kernel,

time: 34.3 us -> 35.5 us (1.035)
  local copies, waits for them, and re-layouts: 1.08 us -> 2.71 us
  starting transfers between devices: 14.1 us -> 13.3 us
    ppermute x8, waiting for transfers between devices: 3.87 us -> 6.33 us  [in_plane(): return lax.ppermute(value, 'gx', [(i, i ^ step) for i in range(peers)])]
    ppermute x6, waiting for transfers between devices: 11.6 us -> 9.45 us  [on_line(): return lax.ppermute(value, 'gx', pairs)]
    unnamed x4, local copies, waits for them, and re-layouts: 0.01 us -> 1.72 us
    ppermute x6, starting transfers between devices: 9.63 us -> 9.04 us  [on_line(): return lax.ppermute(value, 'gx', pairs)]
where the time goes in v30:
time: 35.5 us; the launch traced here: 35.3 us
  waiting for transfers between devices  15.8 us (45%)
  starting transfers between devices  13.3 us (37%)
  Pallas kernels  2.79 us (8%)
  local copies, waits for them, and re-layouts  2.71 us (8%)
  other arithmetic  0.58 us (2%)
    ppermute x6, waiting for transfers between devices, on_line(): return lax.ppermute(value, 'gx', pairs)  9.45 us
    ppermute x6, starting transfers between devices, on_line(): return lax.ppermute(value, 'gx', pairs)  9.04 us
    ppermute x8, waiting for transfers between devices, in_plane(): return lax.ppermute(value, 'gx', [(i, i ^ step) for i in range(peers)])  6.33 us
    ppermute x8, starting transfers between devices, in_plane(): return lax.ppermute(value, 'gx', [(i, i ^ step) for i in range(peers)])  4.31 us
    pallas_call x1, Pallas kernels, grid_plan(): pl.pallas_call(functools.partial(first_kernel, first_moves), out_shape=(l...  2 us
    unnamed x4, local copies, waits for them, and re-layouts  1.72 us
    slice x1, local copies, waits for them, and re-layouts, grid_plan(): first_head = on_line(embeddings[:part], first_moves, 0)  0.99 us
  transfers between devices with their start and end apart: 14, of which 7 were waited for; matrix products, arithmetic and copies ran while one was open for 0% of the time, Pallas kernels for 8%

profile of v30, /device:TPU:0, one launch (start us, length us, event | category | flops | bytes accessed | tf_op | source)
XLA Modules:
  0.0 35.3 jit_solution(14003064366089287396)
XLA Ops:
  0.0 1.0 %slice.3 = bf16[160,1024]{1,0:T(8,128)(2,1)S(1)} slice(bf16[256,1024]{1,0:T(8,128)(2,1)} %rows_ref.1), slice={[0:160], [0:1024]} | slice | bytes 655360 | tf_op jit(solution)/shard_map/slice | solution.py:279
  1.0 3.1 %collective-permute-start = (bf16[160,1024]{1,0:T(8,128)(2,1)S(1)}, bf16[160,1024]{1,0:T(8,128)(2,1)S(1)}, u32[]{:S(2)}, u32[]{:S(2)}) collective-permute-start(bf16[160,1024]{1,0:T(8,128)(2,1)S(1)} %slice.3), channel_id=1, source_target_pairs={{0,4},{1,5},{2,6},{3,7},{4,8},{5,9},{6,10},{7,11},{8,12},{9,13},{1... | collective-permute-start | bytes 983048 | tf_op jit(solution)/shard_map/ppermute | solution.py:268
  4.1 0.0 copy-start
  4.1 1.0 %copy-done = bf16[256,1024]{1,0:T(8,128)(2,1)S(1)} copy-done((bf16[256,1024]{1,0:T(8,128)(2,1)S(1)}, bf16[256,1024]{1,0:T(8,128)(2,1)}, u32[]{:S(2)}) %copy-start) | copy-done | bytes 524312
  5.1 0.0 copy-start.1
  5.1 0.7 %copy-done.1 = s32[256]{0:T(256)S(1)} copy-done((s32[256]{0:T(256)S(1)}, s32[256]{0:T(256)}, u32[]{:S(2)}) %copy-start.1) | copy-done | bytes 1048
  5.8 0.2 shard_map.28
  6.0 1.6 %collective-permute-start.4 = (bf16[136,1024]{1,0:T(8,128)(2,1)S(1)}, bf16[136,1024]{1,0:T(8,128)(2,1)S(1)}, u32[]{:S(2)}, u32[]{:S(2)}) collective-permute-start(bf16[136,1024]{1,0:T(8,128)(2,1)S(1)} %get-tuple-element.28), channel_id=1, source_target_pairs={{0,2},{1,3},{2,0},{3,1},{4,6},{5,7},{6,4},{7,5},{8,10},{9,11},{10,... | collective-permute-start | bytes 835592 | tf_op jit(solution)/shard_map/ppermute | solution.py:264
  7.5 0.0 collective-permute-start.2
  7.6 0.5 %collective-permute-start.3 = (bf16[128,1024]{1,0:T(8,128)(2,1)S(1)}, bf16[128,1024]{1,0:T(8,128)(2,1)S(1)}, u32[]{:S(2)}, u32[]{:S(2)}) collective-permute-start(bf16[128,1024]{1,0:T(8,128)(2,1)S(1)} %get-tuple-element.27), channel_id=1, source_target_pairs={{0,2},{1,3},{2,0},{3,1},{4,6},{5,7},{6,4},{7,5},{8,10},{9,11},{10,... | collective-permute-start | bytes 786440 | tf_op jit(solution)/shard_map/ppermute | solution.py:264
  8.1 0.4 %shard_map.30.own_mass_ref = f32[1,256]{1,0:T(1,128)S(1)} custom-call(bf16[264,1024]{1,0:T(8,128)(2,1)S(1)} %get-tuple-element.26.refs_0_.own_ref), custom_call_target="tpu_custom_call" | custom-call | flops 1 | bytes 1 | tf_op jit(solution)/shard_map/pallas_call | solution.py:286
  8.4 1.6 %collective-permute-start.7 = (bf16[104,1024]{1,0:T(8,128)(2,1)S(1)}, bf16[104,1024]{1,0:T(8,128)(2,1)S(1)}, u32[]{:S(2)}, u32[]{:S(2)}) collective-permute-start(bf16[104,1024]{1,0:T(8,128)(2,1)S(1)} %get-tuple-element.33), channel_id=1, source_target_pairs={{0,4},{1,5},{2,6},{3,7},{4,8},{5,9},{6,10},{7,11},{8,12},{9,13},{1... | collective-permute-start | bytes 638984 | tf_op jit(solution)/shard_map/ppermute | solution.py:268
  10.1 4.4 %collective-permute-done.head_ref = bf16[160,1024]{1,0:T(8,128)(2,1)S(1)} collective-permute-done((bf16[160,1024]{1,0:T(8,128)(2,1)S(1)}, bf16[160,1024]{1,0:T(8,128)(2,1)S(1)}, u32[]{:S(2)}, u32[]{:S(2)}) %collective-permute-start) | collective-permute-done | bytes 327712 | tf_op jit(solution)/shard_map/ppermute | solution.py:268
  14.4 0.0 collective-permute-start.1
  14.4 1.2 %collective-permute-done.4.refs_3_ = bf16[136,1024]{1,0:T(8,128)(2,1)S(1)} collective-permute-done((bf16[136,1024]{1,0:T(8,128)(2,1)S(1)}, bf16[136,1024]{1,0:T(8,128)(2,1)S(1)}, u32[]{:S(2)}, u32[]{:S(2)}) %collective-permute-start.4) | collective-permute-done | bytes 278560 | tf_op jit(solution)/shard_map/ppermute | solution.py:264
  15.6 0.0 collective-permute-start.6
  15.6 4.1 %collective-permute-done.3.refs_2_ = bf16[128,1024]{1,0:T(8,128)(2,1)S(1)} collective-permute-done((bf16[128,1024]{1,0:T(8,128)(2,1)S(1)}, bf16[128,1024]{1,0:T(8,128)(2,1)S(1)}, u32[]{:S(2)}, u32[]{:S(2)}) %collective-permute-start.3) | collective-permute-done | bytes 262176 | tf_op jit(solution)/shard_map/ppermute | solution.py:264
  19.8 0.0 collective-permute-start.5
  19.8 0.0 collective-permute-done.7.tail_ref
  19.8 0.7 %collective-permute-start.8 = (bf16[104,1024]{1,0:T(8,128)(2,1)S(1)}, bf16[104,1024]{1,0:T(8,128)(2,1)S(1)}, u32[]{:S(2)}, u32[]{:S(2)}) collective-permute-start(bf16[104,1024]{1,0:T(8,128)(2,1)S(1)} %collective-permute-done.7.tail_ref), channel_id=1, source_target_pairs={{4,9},{5,8},{6,11},{7,10},{8,13},{9,12},{10,15},{11,14},{20,25},{2... | collective-permute-start | bytes 638984 | tf_op jit(solution)/shard_map/ppermute | solution.py:268
  20.5 0.9 %collective-permute-done.5.refs_4_ = bf16[128,1024]{1,0:T(8,128)(2,1)S(1)} collective-permute-done((bf16[128,1024]{1,0:T(8,128)(2,1)S(1)}, bf16[128,1024]{1,0:T(8,128)(2,1)S(1)}, u32[]{:S(2)}, u32[]{:S(2)}) %collective-permute-start.5) | collective-permute-done | bytes 262176 | tf_op jit(solution)/shard_map/ppermute | solution.py:264
  21.3 0.0 collective-permute-done.2.refs_1_
  21.3 0.0 collective-permute-done.6.refs_5_
  21.3 2.0 %shard_map.31 = (f32[1024,128]{1,0:T(8,128)S(1)}, f32[1,256]{1,0:T(1,128)S(1)}, f32[1024,128]{1,0:T(8,128)S(1)}, f32[1,256]{1,0:T(1,128)S(1)}) custom-call(f32[1,256]{1,0:T(1,128)S(1)} %shard_map.30.own_mass_ref, bf16[160,1024]{1,0:T(8,128)(2,1)S(1)} %collective-permute-done.head_ref, bf16[104,1024]{1,0:T(8,128)(2,1)S(1)} %collective-permute-done.7.tail_ref, ...), custom_call_target="tpu_custom_call" | custom-call | flops 1 | bytes 1 | tf_op jit(solution)/shard_map/pallas_call | solution.py:297
  23.3 2.4 %collective-permute-start.9 = (f32[1,256]{1,0:T(1,128)S(1)}, f32[1,256]{1,0:T(1,128)S(1)}, u32[]{:S(2)}, u32[]{:S(2)}) collective-permute-start(f32[1,256]{1,0:T(1,128)S(1)} %get-tuple-element.40), channel_id=1, source_target_pairs={{4,0},{5,1},{6,2},{7,3},{8,4},{9,5},{10,6},{11,7},{12,8},{13,9},{1... | collective-permute-start | bytes 3080 | tf_op jit(solution)/shard_map/ppermute | solution.py:268
  25.7 0.0 collective-permute-done.1.head_ref
  25.7 0.0 collective-permute-done.8.tail_ref
  25.8 2.9 %collective-permute-done.9 = f32[1,256]{1,0:T(1,128)S(1)} collective-permute-done((f32[1,256]{1,0:T(1,128)S(1)}, f32[1,256]{1,0:T(1,128)S(1)}, u32[]{:S(2)}, u32[]{:S(2)}) %collective-permute-start.9) | collective-permute-done | bytes 1056 | tf_op jit(solution)/shard_map/ppermute | solution.py:268
  28.6 1.3 %collective-permute-start.10 = (f32[1,256]{1,0:T(1,128)S(1)}, f32[1,256]{1,0:T(1,128)S(1)}, u32[]{:S(2)}, u32[]{:S(2)}) collective-permute-start(f32[1,256]{1,0:T(1,128)S(1)} %get-tuple-element.43), channel_id=1, source_target_pairs={{8,1},{9,0},{10,3},{11,2},{12,5},{13,4},{14,7},{15,6},{24,17},{25,... | collective-permute-start | bytes 3080 | tf_op jit(solution)/shard_map/ppermute | solution.py:268
  29.9 0.2 shard_map.33
  30.1 1.6 %collective-permute-start.11 = (f32[1,256]{1,0:T(1,128)S(1)}, f32[1,256]{1,0:T(1,128)S(1)}, u32[]{:S(2)}, u32[]{:S(2)}) collective-permute-start(f32[1,256]{1,0:T(1,128)S(1)} %get-tuple-element.44), channel_id=1, source_target_pairs={{0,2},{1,3},{2,0},{3,1},{4,6},{5,7},{6,4},{7,5},{8,10},{9,11},{10,... | collective-permute-start | bytes 3080 | tf_op jit(solution)/shard_map/ppermute | solution.py:264
  31.7 0.0 collective-permute-start.12
  31.7 0.6 %collective-permute-start.13 = (f32[1,256]{1,0:T(1,128)S(1)}, f32[1,256]{1,0:T(1,128)S(1)}, u32[]{:S(2)}, u32[]{:S(2)}) collective-permute-start(f32[1,256]{1,0:T(1,128)S(1)} %get-tuple-element.46), channel_id=1, source_target_pairs={{0,1},{1,0},{2,3},{3,2},{4,5},{5,4},{6,7},{7,6},{8,9},{9,8},{10,11... | collective-permute-start | bytes 3080 | tf_op jit(solution)/shard_map/ppermute | solution.py:264
  32.4 2.2 %collective-permute-done.10 = f32[1,256]{1,0:T(1,128)S(1)} collective-permute-done((f32[1,256]{1,0:T(1,128)S(1)}, f32[1,256]{1,0:T(1,128)S(1)}, u32[]{:S(2)}, u32[]{:S(2)}) %collective-permute-start.10) | collective-permute-done | bytes 1056 | tf_op jit(solution)/shard_map/ppermute | solution.py:268
  34.6 0.0 collective-permute-done.11
  34.6 0.1 collective-permute-done.12
  34.7 0.0 collective-permute-done.13
  34.7 0.6 %add_log-plus-one_fusion = f32[1,256]{1,0:T(1,128)} fusion(f32[1,256]{1,0:T(1,128)S(1)} %collective-permute-done.13, f32[1,256]{1,0:T(1,128)S(1)} %collective-permute-done.12, f32[1,256]{1,0:T(1,128)S(1)} %collective-permute-done.11, f32[1,256]{1,0:T(1,128)S(1)} %collective-permute-done.10, f32[1,256]{1,0:T(1,128)S(1)} %get-tuple-element.39, ...), kind=kLoop, calls=%fused_computation | loop fusion | flops 1280 | bytes 7168 | tf_op jit(solution)/shard_map/log1p | solution.py:329
  (2 shorter events, 0.0 us)
Async XLA Ops:
  1.0 13.4 %collective-permute-start = (bf16[160,1024]{1,0:T(8,128)(2,1)S(1)}, bf16[160,1024]{1,0:T(8,128)(2,1)S(1)}, u32[]{:S(2)}, u32[]{:S(2)}) collective-permute-start(bf16[160,1024]{1,0:T(8,128)(2,1)S(1)} %slice.3), channel_id=1, source_target_pairs={{0,4},{1,5},{2,6},{3,7},{4,8},{5,9},{6,10},{7,11},{8,12},{9,13},{1... | collective-permute-start | bytes 983048 | tf_op jit(solution)/shard_map/ppermute | solution.py:268
  4.1 1.0 %copy-start = (bf16[256,1024]{1,0:T(8,128)(2,1)S(1)}, bf16[256,1024]{1,0:T(8,128)(2,1)}, u32[]{:S(2)}) copy-start(bf16[256,1024]{1,0:T(8,128)(2,1)} %rows_ref.1) | copy-start | bytes 1572868
  5.1 0.7 %copy-start.1 = (s32[256]{0:T(256)S(1)}, s32[256]{0:T(256)}, u32[]{:S(2)}) copy-start(s32[256]{0:T(256)} %param.3) | copy-start | bytes 3076
  6.0 9.6 %collective-permute-start.4 = (bf16[136,1024]{1,0:T(8,128)(2,1)S(1)}, bf16[136,1024]{1,0:T(8,128)(2,1)S(1)}, u32[]{:S(2)}, u32[]{:S(2)}) collective-permute-start(bf16[136,1024]{1,0:T(8,128)(2,1)S(1)} %get-tuple-element.28), channel_id=1, source_target_pairs={{0,2},{1,3},{2,0},{3,1},{4,6},{5,7},{6,4},{7,5},{8,10},{9,11},{10,... | collective-permute-start | bytes 835592 | tf_op jit(solution)/shard_map/ppermute | solution.py:264
  7.5 13.8 %collective-permute-start.2 = (bf16[264,1024]{1,0:T(8,128)(2,1)S(1)}, bf16[264,1024]{1,0:T(8,128)(2,1)S(1)}, u32[]{:S(2)}, u32[]{:S(2)}) collective-permute-start(bf16[264,1024]{1,0:T(8,128)(2,1)S(1)} %get-tuple-element.26.refs_0_.own_ref), channel_id=1, source_target_pairs={{0,1},{1,0},{2,3},{3,2},{4,5},{5,4},{6,7},{7,6},{8,9},{9,8},{10,11... | collective-permute-start | bytes 1622024 | tf_op jit(solution)/shard_map/ppermute | solution.py:264
  7.6 12.2 %collective-permute-start.3 = (bf16[128,1024]{1,0:T(8,128)(2,1)S(1)}, bf16[128,1024]{1,0:T(8,128)(2,1)S(1)}, u32[]{:S(2)}, u32[]{:S(2)}) collective-permute-start(bf16[128,1024]{1,0:T(8,128)(2,1)S(1)} %get-tuple-element.27), channel_id=1, source_target_pairs={{0,2},{1,3},{2,0},{3,1},{4,6},{5,7},{6,4},{7,5},{8,10},{9,11},{10,... | collective-permute-start | bytes 786440 | tf_op jit(solution)/shard_map/ppermute | solution.py:264
  8.4 11.4 %collective-permute-start.7 = (bf16[104,1024]{1,0:T(8,128)(2,1)S(1)}, bf16[104,1024]{1,0:T(8,128)(2,1)S(1)}, u32[]{:S(2)}, u32[]{:S(2)}) collective-permute-start(bf16[104,1024]{1,0:T(8,128)(2,1)S(1)} %get-tuple-element.33), channel_id=1, source_target_pairs={{0,4},{1,5},{2,6},{3,7},{4,8},{5,9},{6,10},{7,11},{8,12},{9,13},{1... | collective-permute-start | bytes 638984 | tf_op jit(solution)/shard_map/ppermute | solution.py:268
  14.4 11.3 %collective-permute-start.1 = (bf16[160,1024]{1,0:T(8,128)(2,1)S(1)}, bf16[160,1024]{1,0:T(8,128)(2,1)S(1)}, u32[]{:S(2)}, u32[]{:S(2)}) collective-permute-start(bf16[160,1024]{1,0:T(8,128)(2,1)S(1)} %collective-permute-done.head_ref), channel_id=1, source_target_pairs={{0,5},{1,4},{2,7},{3,6},{4,9},{5,8},{6,11},{7,10},{8,13},{9,12},{1... | collective-permute-start | bytes 983048 | tf_op jit(solution)/shard_map/ppermute | solution.py:268
  15.6 5.7 %collective-permute-start.6 = (bf16[136,1024]{1,0:T(8,128)(2,1)S(1)}, bf16[136,1024]{1,0:T(8,128)(2,1)S(1)}, u32[]{:S(2)}, u32[]{:S(2)}) collective-permute-start(bf16[136,1024]{1,0:T(8,128)(2,1)S(1)} %collective-permute-done.4.refs_3_), channel_id=1, source_target_pairs={{0,1},{1,0},{2,3},{3,2},{4,5},{5,4},{6,7},{7,6},{8,9},{9,8},{10,11... | collective-permute-start | bytes 835592 | tf_op jit(solution)/shard_map/ppermute | solution.py:264
  19.8 1.5 %collective-permute-start.5 = (bf16[128,1024]{1,0:T(8,128)(2,1)S(1)}, bf16[128,1024]{1,0:T(8,128)(2,1)S(1)}, u32[]{:S(2)}, u32[]{:S(2)}) collective-permute-start(bf16[128,1024]{1,0:T(8,128)(2,1)S(1)} %collective-permute-done.3.refs_2_), channel_id=1, source_target_pairs={{0,1},{1,0},{2,3},{3,2},{4,5},{5,4},{6,7},{7,6},{8,9},{9,8},{10,11... | collective-permute-start | bytes 786440 | tf_op jit(solution)/shard_map/ppermute | solution.py:264
  19.8 5.9 %collective-permute-start.8 = (bf16[104,1024]{1,0:T(8,128)(2,1)S(1)}, bf16[104,1024]{1,0:T(8,128)(2,1)S(1)}, u32[]{:S(2)}, u32[]{:S(2)}) collective-permute-start(bf16[104,1024]{1,0:T(8,128)(2,1)S(1)} %collective-permute-done.7.tail_ref), channel_id=1, source_target_pairs={{4,9},{5,8},{6,11},{7,10},{8,13},{9,12},{10,15},{11,14},{20,25},{2... | collective-permute-start | bytes 638984 | tf_op jit(solution)/shard_map/ppermute | solution.py:268
  23.3 5.3 %collective-permute-start.9 = (f32[1,256]{1,0:T(1,128)S(1)}, f32[1,256]{1,0:T(1,128)S(1)}, u32[]{:S(2)}, u32[]{:S(2)}) collective-permute-start(f32[1,256]{1,0:T(1,128)S(1)} %get-tuple-element.40), channel_id=1, source_target_pairs={{4,0},{5,1},{6,2},{7,3},{8,4},{9,5},{10,6},{11,7},{12,8},{13,9},{1... | collective-permute-start | bytes 3080 | tf_op jit(solution)/shard_map/ppermute | solution.py:268
  28.6 5.9 %collective-permute-start.10 = (f32[1,256]{1,0:T(1,128)S(1)}, f32[1,256]{1,0:T(1,128)S(1)}, u32[]{:S(2)}, u32[]{:S(2)}) collective-permute-start(f32[1,256]{1,0:T(1,128)S(1)} %get-tuple-element.43), channel_id=1, source_target_pairs={{8,1},{9,0},{10,3},{11,2},{12,5},{13,4},{14,7},{15,6},{24,17},{25,... | collective-permute-start | bytes 3080 | tf_op jit(solution)/shard_map/ppermute | solution.py:268
  30.1 4.4 %collective-permute-start.11 = (f32[1,256]{1,0:T(1,128)S(1)}, f32[1,256]{1,0:T(1,128)S(1)}, u32[]{:S(2)}, u32[]{:S(2)}) collective-permute-start(f32[1,256]{1,0:T(1,128)S(1)} %get-tuple-element.44), channel_id=1, source_target_pairs={{0,2},{1,3},{2,0},{3,1},{4,6},{5,7},{6,4},{7,5},{8,10},{9,11},{10,... | collective-permute-start | bytes 3080 | tf_op jit(solution)/shard_map/ppermute | solution.py:264
  31.7 3.0 %collective-permute-start.12 = (f32[1,256]{1,0:T(1,128)S(1)}, f32[1,256]{1,0:T(1,128)S(1)}, u32[]{:S(2)}, u32[]{:S(2)}) collective-permute-start(f32[1,256]{1,0:T(1,128)S(1)} %get-tuple-element.45), channel_id=1, source_target_pairs={{0,3},{1,2},{2,1},{3,0},{4,7},{5,6},{6,5},{7,4},{8,11},{9,10},{10,... | collective-permute-start | bytes 3080 | tf_op jit(solution)/shard_map/ppermute | solution.py:264
  31.7 3.0 %collective-permute-start.13 = (f32[1,256]{1,0:T(1,128)S(1)}, f32[1,256]{1,0:T(1,128)S(1)}, u32[]{:S(2)}, u32[]{:S(2)}) collective-permute-start(f32[1,256]{1,0:T(1,128)S(1)} %get-tuple-element.46), channel_id=1, source_target_pairs={{0,1},{1,0},{2,3},{3,2},{4,5},{5,4},{6,7},{7,6},{8,9},{9,8},{10,11... | collective-permute-start | bytes 3080 | tf_op jit(solution)/shard_map/ppermute | solution.py:264

commit v31 on v29

--- a/solution.py
+++ b/solution.py
@@ -329,7 +329,7 @@
         compiler_params=params,
     )(sums, mass)
     returned = [on_line(last_column, last_back, 1)]
-    returned += [in_plane(row_sums[step], step) for step in (2, 3, 1)]
+    returned += [in_plane(row_sums[step], step) for step in (3, 2, 1)]
     return jnp.log1p(sum(returned, row_sums[0] + returned_first)).reshape(row_count)
 
 

time: 34.3 us -> 34.4 us (level)
  no operation moved by 1% of the time
where the time goes in v31:
time: 34.4 us; the launch traced here: 34.1 us
  waiting for transfers between devices  15.8 us (46%)
  starting transfers between devices  13.8 us (40%)
  Pallas kernels  2.81 us (8%)
  local copies, waits for them, and re-layouts  1.08 us (3%)
  other arithmetic  0.58 us (2%)
    ppermute x6, waiting for transfers between devices, on_line(): return lax.ppermute(value, 'gx', pairs)  11.9 us
    ppermute x6, starting transfers between devices, on_line(): return lax.ppermute(value, 'gx', pairs)  9.63 us
    ppermute x8, starting transfers between devices, in_plane(): return lax.ppermute(value, 'gx', [(i, i ^ step) for i in range(peers)])  4.17 us
    ppermute x8, waiting for transfers between devices, in_plane(): return lax.ppermute(value, 'gx', [(i, i ^ step) for i in range(peers)])  3.87 us
    pallas_call x1, Pallas kernels, grid_plan(): pl.pallas_call(functools.partial(first_kernel, first_moves), out_shape=(l...  2.02 us
    slice x1, local copies, waits for them, and re-layouts, grid_plan(): first_head = on_line(embeddings[:part], first_moves, 0)  1.07 us
  transfers between devices with their start and end apart: 14, of which 7 were waited for; matrix products, arithmetic and copies ran while one was open for 0% of the time, Pallas kernels for 8%

profile of v31, /device:TPU:0, one launch (start us, length us, event | category | flops | bytes accessed | tf_op | source)
XLA Modules:
  0.0 34.1 jit_solution(3817611152258208862)
XLA Ops:
  0.0 0.0 copy-start
  0.0 1.1 %slice.3 = bf16[160,1024]{1,0:T(8,128)(2,1)S(1)} slice(bf16[256,1024]{1,0:T(8,128)(2,1)} %rows_ref.1), slice={[0:160], [0:1024]} | slice | bytes 655360 | tf_op jit(solution)/shard_map/slice | solution.py:285
  1.1 0.0 copy-start.1
  1.1 3.1 %collective-permute-start = (bf16[160,1024]{1,0:T(8,128)(2,1)S(1)}, bf16[160,1024]{1,0:T(8,128)(2,1)S(1)}, u32[]{:S(2)}, u32[]{:S(2)}) collective-permute-start(bf16[160,1024]{1,0:T(8,128)(2,1)S(1)} %slice.3), channel_id=1, source_target_pairs={{0,4},{1,5},{2,6},{3,7},{4,8},{5,9},{6,10},{7,11},{8,12},{9,13},{1... | collective-permute-start | bytes 983048 | tf_op jit(solution)/shard_map/ppermute | solution.py:274
  4.2 0.0 copy-done
  4.2 0.0 copy-done.1
  4.2 0.2 shard_map.28
  4.4 1.6 %collective-permute-start.4 = (bf16[136,1024]{1,0:T(8,128)(2,1)S(1)}, bf16[136,1024]{1,0:T(8,128)(2,1)S(1)}, u32[]{:S(2)}, u32[]{:S(2)}) collective-permute-start(bf16[136,1024]{1,0:T(8,128)(2,1)S(1)} %get-tuple-element.27), channel_id=1, source_target_pairs={{0,2},{1,3},{2,0},{3,1},{4,6},{5,7},{6,4},{7,5},{8,10},{9,11},{10,... | collective-permute-start | bytes 835592 | tf_op jit(solution)/shard_map/ppermute | solution.py:270
  5.9 0.0 collective-permute-start.2
  5.9 0.5 %collective-permute-start.3 = (bf16[128,1024]{1,0:T(8,128)(2,1)S(1)}, bf16[128,1024]{1,0:T(8,128)(2,1)S(1)}, u32[]{:S(2)}, u32[]{:S(2)}) collective-permute-start(bf16[128,1024]{1,0:T(8,128)(2,1)S(1)} %get-tuple-element.26), channel_id=1, source_target_pairs={{0,2},{1,3},{2,0},{3,1},{4,6},{5,7},{6,4},{7,5},{8,10},{9,11},{10,... | collective-permute-start | bytes 786440 | tf_op jit(solution)/shard_map/ppermute | solution.py:270
  6.5 0.3 %shard_map.30.own_mass_ref = f32[1,256]{1,0:T(1,128)S(1)} custom-call(bf16[264,1024]{1,0:T(8,128)(2,1)S(1)} %get-tuple-element.25.refs_0_.own_ref), custom_call_target="tpu_custom_call" | custom-call | flops 1 | bytes 1 | tf_op jit(solution)/shard_map/pallas_call | solution.py:292
  6.8 1.6 %collective-permute-start.7 = (bf16[104,1024]{1,0:T(8,128)(2,1)S(1)}, bf16[104,1024]{1,0:T(8,128)(2,1)S(1)}, u32[]{:S(2)}, u32[]{:S(2)}) collective-permute-start(bf16[104,1024]{1,0:T(8,128)(2,1)S(1)} %get-tuple-element.31), channel_id=1, source_target_pairs={{0,4},{1,5},{2,6},{3,7},{4,8},{5,9},{6,10},{7,11},{8,12},{9,13},{1... | collective-permute-start | bytes 638984 | tf_op jit(solution)/shard_map/ppermute | solution.py:274
  8.4 6.3 %collective-permute-done.head_ref = bf16[160,1024]{1,0:T(8,128)(2,1)S(1)} collective-permute-done((bf16[160,1024]{1,0:T(8,128)(2,1)S(1)}, bf16[160,1024]{1,0:T(8,128)(2,1)S(1)}, u32[]{:S(2)}, u32[]{:S(2)}) %collective-permute-start) | collective-permute-done | bytes 327712 | tf_op jit(solution)/shard_map/ppermute | solution.py:274
  14.7 0.0 collective-permute-start.1
  14.7 0.0 collective-permute-done.4.refs_3_
  14.7 0.1 collective-permute-start.6
  14.9 3.3 %collective-permute-done.3.refs_2_ = bf16[128,1024]{1,0:T(8,128)(2,1)S(1)} collective-permute-done((bf16[128,1024]{1,0:T(8,128)(2,1)S(1)}, bf16[128,1024]{1,0:T(8,128)(2,1)S(1)}, u32[]{:S(2)}, u32[]{:S(2)}) %collective-permute-start.3) | collective-permute-done | bytes 262176 | tf_op jit(solution)/shard_map/ppermute | solution.py:270
  18.2 0.0 collective-permute-start.5
  18.2 0.3 collective-permute-done.7.tail_ref
  18.5 0.7 %collective-permute-start.8 = (bf16[104,1024]{1,0:T(8,128)(2,1)S(1)}, bf16[104,1024]{1,0:T(8,128)(2,1)S(1)}, u32[]{:S(2)}, u32[]{:S(2)}) collective-permute-start(bf16[104,1024]{1,0:T(8,128)(2,1)S(1)} %collective-permute-done.7.tail_ref), channel_id=1, source_target_pairs={{4,9},{5,8},{6,11},{7,10},{8,13},{9,12},{10,15},{11,14},{20,25},{2... | collective-permute-start | bytes 638984 | tf_op jit(solution)/shard_map/ppermute | solution.py:274
  19.1 0.6 %collective-permute-done.5.refs_4_ = bf16[128,1024]{1,0:T(8,128)(2,1)S(1)} collective-permute-done((bf16[128,1024]{1,0:T(8,128)(2,1)S(1)}, bf16[128,1024]{1,0:T(8,128)(2,1)S(1)}, u32[]{:S(2)}, u32[]{:S(2)}) %collective-permute-start.5) | collective-permute-done | bytes 262176 | tf_op jit(solution)/shard_map/ppermute | solution.py:270
  19.7 0.0 collective-permute-done.2.refs_1_
  19.7 0.0 collective-permute-done.6.refs_5_
  19.7 2.0 %shard_map.31 = (f32[1024,128]{1,0:T(8,128)S(1)}, f32[1,256]{1,0:T(1,128)S(1)}, f32[1024,128]{1,0:T(8,128)S(1)}, f32[1,256]{1,0:T(1,128)S(1)}) custom-call(f32[1,256]{1,0:T(1,128)S(1)} %shard_map.30.own_mass_ref, bf16[160,1024]{1,0:T(8,128)(2,1)S(1)} %collective-permute-done.head_ref, bf16[104,1024]{1,0:T(8,128)(2,1)S(1)} %collective-permute-done.7.tail_ref, ...), custom_call_target="tpu_custom_call" | custom-call | flops 1 | bytes 1 | tf_op jit(solution)/shard_map/pallas_call | solution.py:303
  21.7 3.0 %collective-permute-start.9 = (f32[1,256]{1,0:T(1,128)S(1)}, f32[1,256]{1,0:T(1,128)S(1)}, u32[]{:S(2)}, u32[]{:S(2)}) collective-permute-start(f32[1,256]{1,0:T(1,128)S(1)} %get-tuple-element.38), channel_id=1, source_target_pairs={{4,0},{5,1},{6,2},{7,3},{8,4},{9,5},{10,6},{11,7},{12,8},{13,9},{1... | collective-permute-start | bytes 3080 | tf_op jit(solution)/shard_map/ppermute | solution.py:274
  24.7 0.8 %collective-permute-done.1.head_ref = bf16[160,1024]{1,0:T(8,128)(2,1)S(1)} collective-permute-done((bf16[160,1024]{1,0:T(8,128)(2,1)S(1)}, bf16[160,1024]{1,0:T(8,128)(2,1)S(1)}, u32[]{:S(2)}, u32[]{:S(2)}) %collective-permute-start.1) | collective-permute-done | bytes 327712 | tf_op jit(solution)/shard_map/ppermute | solution.py:274
  25.5 0.0 collective-permute-done.8.tail_ref
  25.5 1.5 %collective-permute-done.9 = f32[1,256]{1,0:T(1,128)S(1)} collective-permute-done((f32[1,256]{1,0:T(1,128)S(1)}, f32[1,256]{1,0:T(1,128)S(1)}, u32[]{:S(2)}, u32[]{:S(2)}) %collective-permute-start.9) | collective-permute-done | bytes 1056 | tf_op jit(solution)/shard_map/ppermute | solution.py:274
  27.0 1.3 %collective-permute-start.10 = (f32[1,256]{1,0:T(1,128)S(1)}, f32[1,256]{1,0:T(1,128)S(1)}, u32[]{:S(2)}, u32[]{:S(2)}) collective-permute-start(f32[1,256]{1,0:T(1,128)S(1)} %get-tuple-element.41), channel_id=1, source_target_pairs={{8,1},{9,0},{10,3},{11,2},{12,5},{13,4},{14,7},{15,6},{24,17},{25,... | collective-permute-start | bytes 3080 | tf_op jit(solution)/shard_map/ppermute | solution.py:274
  28.3 0.2 shard_map.33
  28.5 0.3 collective-permute-start.11
  28.8 1.3 %collective-permute-start.12 = (f32[1,256]{1,0:T(1,128)S(1)}, f32[1,256]{1,0:T(1,128)S(1)}, u32[]{:S(2)}, u32[]{:S(2)}) collective-permute-start(f32[1,256]{1,0:T(1,128)S(1)} %get-tuple-element.43), channel_id=1, source_target_pairs={{0,2},{1,3},{2,0},{3,1},{4,6},{5,7},{6,4},{7,5},{8,10},{9,11},{10,... | collective-permute-start | bytes 3080 | tf_op jit(solution)/shard_map/ppermute | solution.py:270
  30.1 0.3 collective-permute-start.13
  30.4 3.1 %collective-permute-done.10 = f32[1,256]{1,0:T(1,128)S(1)} collective-permute-done((f32[1,256]{1,0:T(1,128)S(1)}, f32[1,256]{1,0:T(1,128)S(1)}, u32[]{:S(2)}, u32[]{:S(2)}) %collective-permute-start.10) | collective-permute-done | bytes 1056 | tf_op jit(solution)/shard_map/ppermute | solution.py:274
  33.5 0.0 collective-permute-done.11
  33.5 0.0 collective-permute-done.12
  33.5 0.0 collective-permute-done.13
  33.5 0.6 %add_log-plus-one_fusion = f32[1,256]{1,0:T(1,128)} fusion(f32[1,256]{1,0:T(1,128)S(1)} %collective-permute-done.13, f32[1,256]{1,0:T(1,128)S(1)} %collective-permute-done.12, f32[1,256]{1,0:T(1,128)S(1)} %collective-permute-done.11, f32[1,256]{1,0:T(1,128)S(1)} %collective-permute-done.10, f32[1,256]{1,0:T(1,128)S(1)} %get-tuple-element.37, ...), kind=kLoop, calls=%fused_computation | loop fusion | flops 1280 | bytes 7168 | tf_op jit(solution)/shard_map/log1p | solution.py:333
  (2 shorter events, 0.0 us)
Async XLA Ops:
  0.0 4.2 %copy-start = (bf16[256,1024]{1,0:T(8,128)(2,1)S(1)}, bf16[256,1024]{1,0:T(8,128)(2,1)}, u32[]{:S(2)}) copy-start(bf16[256,1024]{1,0:T(8,128)(2,1)} %rows_ref.1) | copy-start | bytes 1572868
  1.1 3.1 %copy-start.1 = (s32[256]{0:T(256)S(1)}, s32[256]{0:T(256)}, u32[]{:S(2)}) copy-start(s32[256]{0:T(256)} %param.3) | copy-start | bytes 3076
  1.1 13.6 %collective-permute-start = (bf16[160,1024]{1,0:T(8,128)(2,1)S(1)}, bf16[160,1024]{1,0:T(8,128)(2,1)S(1)}, u32[]{:S(2)}, u32[]{:S(2)}) collective-permute-start(bf16[160,1024]{1,0:T(8,128)(2,1)S(1)} %slice.3), channel_id=1, source_target_pairs={{0,4},{1,5},{2,6},{3,7},{4,8},{5,9},{6,10},{7,11},{8,12},{9,13},{1... | collective-permute-start | bytes 983048 | tf_op jit(solution)/shard_map/ppermute | solution.py:274
  4.4 10.4 %collective-permute-start.4 = (bf16[136,1024]{1,0:T(8,128)(2,1)S(1)}, bf16[136,1024]{1,0:T(8,128)(2,1)S(1)}, u32[]{:S(2)}, u32[]{:S(2)}) collective-permute-start(bf16[136,1024]{1,0:T(8,128)(2,1)S(1)} %get-tuple-element.27), channel_id=1, source_target_pairs={{0,2},{1,3},{2,0},{3,1},{4,6},{5,7},{6,4},{7,5},{8,10},{9,11},{10,... | collective-permute-start | bytes 835592 | tf_op jit(solution)/shard_map/ppermute | solution.py:270
  5.9 13.8 %collective-permute-start.2 = (bf16[264,1024]{1,0:T(8,128)(2,1)S(1)}, bf16[264,1024]{1,0:T(8,128)(2,1)S(1)}, u32[]{:S(2)}, u32[]{:S(2)}) collective-permute-start(bf16[264,1024]{1,0:T(8,128)(2,1)S(1)} %get-tuple-element.25.refs_0_.own_ref), channel_id=1, source_target_pairs={{0,1},{1,0},{2,3},{3,2},{4,5},{5,4},{6,7},{7,6},{8,9},{9,8},{10,11... | collective-permute-start | bytes 1622024 | tf_op jit(solution)/shard_map/ppermute | solution.py:270
  5.9 12.2 %collective-permute-start.3 = (bf16[128,1024]{1,0:T(8,128)(2,1)S(1)}, bf16[128,1024]{1,0:T(8,128)(2,1)S(1)}, u32[]{:S(2)}, u32[]{:S(2)}) collective-permute-start(bf16[128,1024]{1,0:T(8,128)(2,1)S(1)} %get-tuple-element.26), channel_id=1, source_target_pairs={{0,2},{1,3},{2,0},{3,1},{4,6},{5,7},{6,4},{7,5},{8,10},{9,11},{10,... | collective-permute-start | bytes 786440 | tf_op jit(solution)/shard_map/ppermute | solution.py:270
  6.8 11.6 %collective-permute-start.7 = (bf16[104,1024]{1,0:T(8,128)(2,1)S(1)}, bf16[104,1024]{1,0:T(8,128)(2,1)S(1)}, u32[]{:S(2)}, u32[]{:S(2)}) collective-permute-start(bf16[104,1024]{1,0:T(8,128)(2,1)S(1)} %get-tuple-element.31), channel_id=1, source_target_pairs={{0,4},{1,5},{2,6},{3,7},{4,8},{5,9},{6,10},{7,11},{8,12},{9,13},{1... | collective-permute-start | bytes 638984 | tf_op jit(solution)/shard_map/ppermute | solution.py:274
  14.7 10.8 %collective-permute-start.1 = (bf16[160,1024]{1,0:T(8,128)(2,1)S(1)}, bf16[160,1024]{1,0:T(8,128)(2,1)S(1)}, u32[]{:S(2)}, u32[]{:S(2)}) collective-permute-start(bf16[160,1024]{1,0:T(8,128)(2,1)S(1)} %collective-permute-done.head_ref), channel_id=1, source_target_pairs={{0,5},{1,4},{2,7},{3,6},{4,9},{5,8},{6,11},{7,10},{8,13},{9,12},{1... | collective-permute-start | bytes 983048 | tf_op jit(solution)/shard_map/ppermute | solution.py:274
  14.7 5.0 %collective-permute-start.6 = (bf16[136,1024]{1,0:T(8,128)(2,1)S(1)}, bf16[136,1024]{1,0:T(8,128)(2,1)S(1)}, u32[]{:S(2)}, u32[]{:S(2)}) collective-permute-start(bf16[136,1024]{1,0:T(8,128)(2,1)S(1)} %collective-permute-done.4.refs_3_), channel_id=1, source_target_pairs={{0,1},{1,0},{2,3},{3,2},{4,5},{5,4},{6,7},{7,6},{8,9},{9,8},{10,11... | collective-permute-start | bytes 835592 | tf_op jit(solution)/shard_map/ppermute | solution.py:270
  18.2 1.5 %collective-permute-start.5 = (bf16[128,1024]{1,0:T(8,128)(2,1)S(1)}, bf16[128,1024]{1,0:T(8,128)(2,1)S(1)}, u32[]{:S(2)}, u32[]{:S(2)}) collective-permute-start(bf16[128,1024]{1,0:T(8,128)(2,1)S(1)} %collective-permute-done.3.refs_2_), channel_id=1, source_target_pairs={{0,1},{1,0},{2,3},{3,2},{4,5},{5,4},{6,7},{7,6},{8,9},{9,8},{10,11... | collective-permute-start | bytes 786440 | tf_op jit(solution)/shard_map/ppermute | solution.py:270
  18.5 7.0 %collective-permute-start.8 = (bf16[104,1024]{1,0:T(8,128)(2,1)S(1)}, bf16[104,1024]{1,0:T(8,128)(2,1)S(1)}, u32[]{:S(2)}, u32[]{:S(2)}) collective-permute-start(bf16[104,1024]{1,0:T(8,128)(2,1)S(1)} %collective-permute-done.7.tail_ref), channel_id=1, source_target_pairs={{4,9},{5,8},{6,11},{7,10},{8,13},{9,12},{10,15},{11,14},{20,25},{2... | collective-permute-start | bytes 638984 | tf_op jit(solution)/shard_map/ppermute | solution.py:274
  21.7 5.3 %collective-permute-start.9 = (f32[1,256]{1,0:T(1,128)S(1)}, f32[1,256]{1,0:T(1,128)S(1)}, u32[]{:S(2)}, u32[]{:S(2)}) collective-permute-start(f32[1,256]{1,0:T(1,128)S(1)} %get-tuple-element.38), channel_id=1, source_target_pairs={{4,0},{5,1},{6,2},{7,3},{8,4},{9,5},{10,6},{11,7},{12,8},{13,9},{1... | collective-permute-start | bytes 3080 | tf_op jit(solution)/shard_map/ppermute | solution.py:274
  27.0 6.5 %collective-permute-start.10 = (f32[1,256]{1,0:T(1,128)S(1)}, f32[1,256]{1,0:T(1,128)S(1)}, u32[]{:S(2)}, u32[]{:S(2)}) collective-permute-start(f32[1,256]{1,0:T(1,128)S(1)} %get-tuple-element.41), channel_id=1, source_target_pairs={{8,1},{9,0},{10,3},{11,2},{12,5},{13,4},{14,7},{15,6},{24,17},{25,... | collective-permute-start | bytes 3080 | tf_op jit(solution)/shard_map/ppermute | solution.py:274
  28.5 5.0 %collective-permute-start.11 = (f32[1,256]{1,0:T(1,128)S(1)}, f32[1,256]{1,0:T(1,128)S(1)}, u32[]{:S(2)}, u32[]{:S(2)}) collective-permute-start(f32[1,256]{1,0:T(1,128)S(1)} %get-tuple-element.42), channel_id=1, source_target_pairs={{0,3},{1,2},{2,1},{3,0},{4,7},{5,6},{6,5},{7,4},{8,11},{9,10},{10,... | collective-permute-start | bytes 3080 | tf_op jit(solution)/shard_map/ppermute | solution.py:270
  28.8 4.7 %collective-permute-start.12 = (f32[1,256]{1,0:T(1,128)S(1)}, f32[1,256]{1,0:T(1,128)S(1)}, u32[]{:S(2)}, u32[]{:S(2)}) collective-permute-start(f32[1,256]{1,0:T(1,128)S(1)} %get-tuple-element.43), channel_id=1, source_target_pairs={{0,2},{1,3},{2,0},{3,1},{4,6},{5,7},{6,4},{7,5},{8,10},{9,11},{10,... | collective-permute-start | bytes 3080 | tf_op jit(solution)/shard_map/ppermute | solution.py:270
  30.1 3.4 %collective-permute-start.13 = (f32[1,256]{1,0:T(1,128)S(1)}, f32[1,256]{1,0:T(1,128)S(1)}, u32[]{:S(2)}, u32[]{:S(2)}) collective-permute-start(f32[1,256]{1,0:T(1,128)S(1)} %get-tuple-element.44), channel_id=1, source_target_pairs={{0,1},{1,0},{2,3},{3,2},{4,5},{5,4},{6,7},{7,6},{8,9},{9,8},{10,11... | collective-permute-start | bytes 3080 | tf_op jit(solution)/shard_map/ppermute | solution.py:270

commit v32 on v31

--- a/solution.py
+++ b/solution.py
@@ -279,7 +279,7 @@
     first_back = [(b, a) for a, b in first_moves]
     last_back = [(b, a) for a, b in last_moves]
 
-    half, part = row_count // 2, 5 * row_count // 8
+    half, part = row_count // 2, 11 * row_count // 16
     ranges = [(0, row_count), (0, half), (half, row_count), (part, row_count)]
     id_rows = [ID_ROWS, 0, ID_ROWS, ID_ROWS]
     first_head = on_line(embeddings[:part], first_moves, 0)

time: 34.4 us -> 42.8 us (1.24)
  waiting for transfers between devices: 15.8 us -> 27.7 us
  starting transfers between devices: 13.8 us -> 10.4 us
    ppermute x6, waiting for transfers between devices: 11.9 us -> 25.3 us  [on_line(): return lax.ppermute(value, 'gx', pairs)]
    ppermute x6, starting transfers between devices: 9.63 us -> 5.24 us  [on_line(): return lax.ppermute(value, 'gx', pairs)]
    ppermute x8, waiting for transfers between devices: 3.87 us -> 2.45 us  [in_plane(): return lax.ppermute(value, 'gx', [(i, i ^ step) for i in range(peers)])]
    ppermute x8, starting transfers between devices: 4.17 us -> 5.13 us  [in_plane(): return lax.ppermute(value, 'gx', [(i, i ^ step) for i in range(peers)])]
  transfers between devices with their start and end apart: 14 -> 14, of which waited for: 7 -> 5; matrix products, arithmetic and copies ran while one was open for 0% -> 0% of each run, Pallas kernels for 8% -> 7%
where the time goes in v32:
time: 42.8 us; the launch traced here: 42.7 us
  waiting for transfers between devices  27.7 us (65%)
  starting transfers between devices  10.4 us (24%)
  Pallas kernels  2.8 us (7%)
  local copies, waits for them, and re-layouts  1.09 us (3%)
  other arithmetic  0.58 us (1%)
    ppermute x6, waiting for transfers between devices, on_line(): return lax.ppermute(value, 'gx', pairs)  25.3 us
    ppermute x6, starting transfers between devices, on_line(): return lax.ppermute(value, 'gx', pairs)  5.24 us
    ppermute x8, starting transfers between devices, in_plane(): return lax.ppermute(value, 'gx', [(i, i ^ step) for i in range(peers)])  5.13 us
    ppermute x8, waiting for transfers between devices, in_plane(): return lax.ppermute(value, 'gx', [(i, i ^ step) for i in range(peers)])  2.45 us
    pallas_call x1, Pallas kernels, grid_plan(): pl.pallas_call(functools.partial(first_kernel, first_moves), out_shape=(l...  2.01 us
    slice x1, local copies, waits for them, and re-layouts, grid_plan(): first_head = on_line(embeddings[:part], first_moves, 0)  1.08 us
  transfers between devices with their start and end apart: 14, of which 5 were waited for; matrix products, arithmetic and copies ran while one was open for 0% of the time, Pallas kernels for 7%

profile of v32, /device:TPU:0, one launch (start us, length us, event | category | flops | bytes accessed | tf_op | source)
XLA Modules:
  0.0 42.7 jit_solution(14846002029565866388)
XLA Ops:
  0.0 0.0 copy-start
  0.0 1.1 %slice.3 = bf16[176,1024]{1,0:T(8,128)(2,1)S(1)} slice(bf16[256,1024]{1,0:T(8,128)(2,1)} %rows_ref.1), slice={[0:176], [0:1024]} | slice | bytes 720896 | tf_op jit(solution)/shard_map/slice | solution.py:285
  1.1 0.0 copy-start.1
  1.1 3.1 %collective-permute-start = (bf16[176,1024]{1,0:T(8,128)(2,1)S(1)}, bf16[176,1024]{1,0:T(8,128)(2,1)S(1)}, u32[]{:S(2)}, u32[]{:S(2)}) collective-permute-start(bf16[176,1024]{1,0:T(8,128)(2,1)S(1)} %slice.3), channel_id=1, source_target_pairs={{0,4},{1,5},{2,6},{3,7},{4,8},{5,9},{6,10},{7,11},{8,12},{9,13},{1... | collective-permute-start | bytes 1081352 | tf_op jit(solution)/shard_map/ppermute | solution.py:274
  4.2 0.0 copy-done
  4.2 0.0 copy-done.1
  4.2 0.2 shard_map.28
  4.4 1.6 %collective-permute-start.4 = (bf16[136,1024]{1,0:T(8,128)(2,1)S(1)}, bf16[136,1024]{1,0:T(8,128)(2,1)S(1)}, u32[]{:S(2)}, u32[]{:S(2)}) collective-permute-start(bf16[136,1024]{1,0:T(8,128)(2,1)S(1)} %get-tuple-element.27), channel_id=1, source_target_pairs={{0,2},{1,3},{2,0},{3,1},{4,6},{5,7},{6,4},{7,5},{8,10},{9,11},{10,... | collective-permute-start | bytes 835592 | tf_op jit(solution)/shard_map/ppermute | solution.py:270
  5.9 0.0 collective-permute-start.2
  5.9 0.5 %collective-permute-start.3 = (bf16[128,1024]{1,0:T(8,128)(2,1)S(1)}, bf16[128,1024]{1,0:T(8,128)(2,1)S(1)}, u32[]{:S(2)}, u32[]{:S(2)}) collective-permute-start(bf16[128,1024]{1,0:T(8,128)(2,1)S(1)} %get-tuple-element.26), channel_id=1, source_target_pairs={{0,2},{1,3},{2,0},{3,1},{4,6},{5,7},{6,4},{7,5},{8,10},{9,11},{10,... | collective-permute-start | bytes 786440 | tf_op jit(solution)/shard_map/ppermute | solution.py:270
  6.5 0.4 shard_map.30.own_mass_ref
  6.8 7.8 %collective-permute-done.head_ref = bf16[176,1024]{1,0:T(8,128)(2,1)S(1)} collective-permute-done((bf16[176,1024]{1,0:T(8,128)(2,1)S(1)}, bf16[176,1024]{1,0:T(8,128)(2,1)S(1)}, u32[]{:S(2)}, u32[]{:S(2)}) %collective-permute-start) | collective-permute-done | bytes 360480 | tf_op jit(solution)/shard_map/ppermute | solution.py:274
  14.6 0.0 collective-permute-start.1
  14.6 0.0 collective-permute-start.7
  14.6 0.0 collective-permute-done.4.refs_3_
  14.6 1.1 %collective-permute-start.6 = (bf16[136,1024]{1,0:T(8,128)(2,1)S(1)}, bf16[136,1024]{1,0:T(8,128)(2,1)S(1)}, u32[]{:S(2)}, u32[]{:S(2)}) collective-permute-start(bf16[136,1024]{1,0:T(8,128)(2,1)S(1)} %collective-permute-done.4.refs_3_), channel_id=1, source_target_pairs={{0,1},{1,0},{2,3},{3,2},{4,5},{5,4},{6,7},{7,6},{8,9},{9,8},{10,11... | collective-permute-start | bytes 835592 | tf_op jit(solution)/shard_map/ppermute | solution.py:270
  15.7 2.4 %collective-permute-done.3.refs_2_ = bf16[128,1024]{1,0:T(8,128)(2,1)S(1)} collective-permute-done((bf16[128,1024]{1,0:T(8,128)(2,1)S(1)}, bf16[128,1024]{1,0:T(8,128)(2,1)S(1)}, u32[]{:S(2)}, u32[]{:S(2)}) %collective-permute-start.3) | collective-permute-done | bytes 262176 | tf_op jit(solution)/shard_map/ppermute | solution.py:270
  18.2 0.0 collective-permute-start.5
  18.2 11.8 %collective-permute-done.7.tail_ref = bf16[88,1024]{1,0:T(8,128)(2,1)S(1)} collective-permute-done((bf16[88,1024]{1,0:T(8,128)(2,1)S(1)}, bf16[88,1024]{1,0:T(8,128)(2,1)S(1)}, u32[]{:S(2)}, u32[]{:S(2)}) %collective-permute-start.7) | collective-permute-done | bytes 180256 | tf_op jit(solution)/shard_map/ppermute | solution.py:274
  30.0 0.7 %collective-permute-start.8 = (bf16[88,1024]{1,0:T(8,128)(2,1)S(1)}, bf16[88,1024]{1,0:T(8,128)(2,1)S(1)}, u32[]{:S(2)}, u32[]{:S(2)}) collective-permute-start(bf16[88,1024]{1,0:T(8,128)(2,1)S(1)} %collective-permute-done.7.tail_ref), channel_id=1, source_target_pairs={{4,9},{5,8},{6,11},{7,10},{8,13},{9,12},{10,15},{11,14},{20,25},{2... | collective-permute-start | bytes 540680 | tf_op jit(solution)/shard_map/ppermute | solution.py:274
  30.6 0.0 collective-permute-done.5.refs_4_
  30.6 0.0 collective-permute-done.2.refs_1_
  30.7 0.0 collective-permute-done.6.refs_5_
  30.7 2.0 %shard_map.31 = (f32[1024,128]{1,0:T(8,128)S(1)}, f32[1,256]{1,0:T(1,128)S(1)}, f32[1024,128]{1,0:T(8,128)S(1)}, f32[1,256]{1,0:T(1,128)S(1)}) custom-call(f32[1,256]{1,0:T(1,128)S(1)} %shard_map.30.own_mass_ref, bf16[176,1024]{1,0:T(8,128)(2,1)S(1)} %collective-permute-done.head_ref, bf16[88,1024]{1,0:T(8,128)(2,1)S(1)} %collective-permute-done.7.tail_ref, ...), custom_call_target="tpu_custom_call" | custom-call | flops 1 | bytes 1 | tf_op jit(solution)/shard_map/pallas_call | solution.py:303
  32.7 0.2 collective-permute-start.9
  32.9 0.0 collective-permute-done.1.head_ref
  32.9 0.0 collective-permute-done.8.tail_ref
  32.9 3.4 %collective-permute-done.9 = f32[1,256]{1,0:T(1,128)S(1)} collective-permute-done((f32[1,256]{1,0:T(1,128)S(1)}, f32[1,256]{1,0:T(1,128)S(1)}, u32[]{:S(2)}, u32[]{:S(2)}) %collective-permute-start.9) | collective-permute-done | bytes 1056 | tf_op jit(solution)/shard_map/ppermute | solution.py:274
  36.3 1.3 %collective-permute-start.10 = (f32[1,256]{1,0:T(1,128)S(1)}, f32[1,256]{1,0:T(1,128)S(1)}, u32[]{:S(2)}, u32[]{:S(2)}) collective-permute-start(f32[1,256]{1,0:T(1,128)S(1)} %get-tuple-element.41), channel_id=1, source_target_pairs={{8,1},{9,0},{10,3},{11,2},{12,5},{13,4},{14,7},{15,6},{24,17},{25,... | collective-permute-start | bytes 3080 | tf_op jit(solution)/shard_map/ppermute | solution.py:274
  37.6 0.2 shard_map.33
  37.8 0.1 collective-permute-start.11
  37.9 1.0 %collective-permute-start.12 = (f32[1,256]{1,0:T(1,128)S(1)}, f32[1,256]{1,0:T(1,128)S(1)}, u32[]{:S(2)}, u32[]{:S(2)}) collective-permute-start(f32[1,256]{1,0:T(1,128)S(1)} %get-tuple-element.43), channel_id=1, source_target_pairs={{0,2},{1,3},{2,0},{3,1},{4,6},{5,7},{6,4},{7,5},{8,10},{9,11},{10,... | collective-permute-start | bytes 3080 | tf_op jit(solution)/shard_map/ppermute | solution.py:270
  38.9 0.8 %collective-permute-start.13 = (f32[1,256]{1,0:T(1,128)S(1)}, f32[1,256]{1,0:T(1,128)S(1)}, u32[]{:S(2)}, u32[]{:S(2)}) collective-permute-start(f32[1,256]{1,0:T(1,128)S(1)} %get-tuple-element.44), channel_id=1, source_target_pairs={{0,1},{1,0},{2,3},{3,2},{4,5},{5,4},{6,7},{7,6},{8,9},{9,8},{10,11... | collective-permute-start | bytes 3080 | tf_op jit(solution)/shard_map/ppermute | solution.py:270
  39.7 2.3 %collective-permute-done.10 = f32[1,256]{1,0:T(1,128)S(1)} collective-permute-done((f32[1,256]{1,0:T(1,128)S(1)}, f32[1,256]{1,0:T(1,128)S(1)}, u32[]{:S(2)}, u32[]{:S(2)}) %collective-permute-start.10) | collective-permute-done | bytes 1056 | tf_op jit(solution)/shard_map/ppermute | solution.py:274
  42.1 0.0 collective-permute-done.11
  42.1 0.0 collective-permute-done.12
  42.1 0.0 collective-permute-done.13
  42.1 0.6 %add_log-plus-one_fusion = f32[1,256]{1,0:T(1,128)} fusion(f32[1,256]{1,0:T(1,128)S(1)} %collective-permute-done.13, f32[1,256]{1,0:T(1,128)S(1)} %collective-permute-done.12, f32[1,256]{1,0:T(1,128)S(1)} %collective-permute-done.11, f32[1,256]{1,0:T(1,128)S(1)} %collective-permute-done.10, f32[1,256]{1,0:T(1,128)S(1)} %get-tuple-element.37, ...), kind=kLoop, calls=%fused_computation | loop fusion | flops 1280 | bytes 7168 | tf_op jit(solution)/shard_map/log1p | solution.py:333
  (2 shorter events, 0.0 us)
Async XLA Ops:
  0.0 4.2 %copy-start = (bf16[256,1024]{1,0:T(8,128)(2,1)S(1)}, bf16[256,1024]{1,0:T(8,128)(2,1)}, u32[]{:S(2)}) copy-start(bf16[256,1024]{1,0:T(8,128)(2,1)} %rows_ref.1) | copy-start | bytes 1572868
  1.1 3.1 %copy-start.1 = (s32[256]{0:T(256)S(1)}, s32[256]{0:T(256)}, u32[]{:S(2)}) copy-start(s32[256]{0:T(256)} %param.3) | copy-start | bytes 3076
  1.1 13.5 %collective-permute-start = (bf16[176,1024]{1,0:T(8,128)(2,1)S(1)}, bf16[176,1024]{1,0:T(8,128)(2,1)S(1)}, u32[]{:S(2)}, u32[]{:S(2)}) collective-permute-start(bf16[176,1024]{1,0:T(8,128)(2,1)S(1)} %slice.3), channel_id=1, source_target_pairs={{0,4},{1,5},{2,6},{3,7},{4,8},{5,9},{6,10},{7,11},{8,12},{9,13},{1... | collective-permute-start | bytes 1081352 | tf_op jit(solution)/shard_map/ppermute | solution.py:274
  4.4 10.2 %collective-permute-start.4 = (bf16[136,1024]{1,0:T(8,128)(2,1)S(1)}, bf16[136,1024]{1,0:T(8,128)(2,1)S(1)}, u32[]{:S(2)}, u32[]{:S(2)}) collective-permute-start(bf16[136,1024]{1,0:T(8,128)(2,1)S(1)} %get-tuple-element.27), channel_id=1, source_target_pairs={{0,2},{1,3},{2,0},{3,1},{4,6},{5,7},{6,4},{7,5},{8,10},{9,11},{10,... | collective-permute-start | bytes 835592 | tf_op jit(solution)/shard_map/ppermute | solution.py:270
  5.9 24.7 %collective-permute-start.2 = (bf16[264,1024]{1,0:T(8,128)(2,1)S(1)}, bf16[264,1024]{1,0:T(8,128)(2,1)S(1)}, u32[]{:S(2)}, u32[]{:S(2)}) collective-permute-start(bf16[264,1024]{1,0:T(8,128)(2,1)S(1)} %get-tuple-element.25.refs_0_.own_ref), channel_id=1, source_target_pairs={{0,1},{1,0},{2,3},{3,2},{4,5},{5,4},{6,7},{7,6},{8,9},{9,8},{10,11... | collective-permute-start | bytes 1622024 | tf_op jit(solution)/shard_map/ppermute | solution.py:270
  5.9 12.2 %collective-permute-start.3 = (bf16[128,1024]{1,0:T(8,128)(2,1)S(1)}, bf16[128,1024]{1,0:T(8,128)(2,1)S(1)}, u32[]{:S(2)}, u32[]{:S(2)}) collective-permute-start(bf16[128,1024]{1,0:T(8,128)(2,1)S(1)} %get-tuple-element.26), channel_id=1, source_target_pairs={{0,2},{1,3},{2,0},{3,1},{4,6},{5,7},{6,4},{7,5},{8,10},{9,11},{10,... | collective-permute-start | bytes 786440 | tf_op jit(solution)/shard_map/ppermute | solution.py:270
  14.6 18.3 %collective-permute-start.1 = (bf16[176,1024]{1,0:T(8,128)(2,1)S(1)}, bf16[176,1024]{1,0:T(8,128)(2,1)S(1)}, u32[]{:S(2)}, u32[]{:S(2)}) collective-permute-start(bf16[176,1024]{1,0:T(8,128)(2,1)S(1)} %collective-permute-done.head_ref), channel_id=1, source_target_pairs={{0,5},{1,4},{2,7},{3,6},{4,9},{5,8},{6,11},{7,10},{8,13},{9,12},{1... | collective-permute-start | bytes 1081352 | tf_op jit(solution)/shard_map/ppermute | solution.py:274
  14.6 15.4 %collective-permute-start.7 = (bf16[88,1024]{1,0:T(8,128)(2,1)S(1)}, bf16[88,1024]{1,0:T(8,128)(2,1)S(1)}, u32[]{:S(2)}, u32[]{:S(2)}) collective-permute-start(bf16[88,1024]{1,0:T(8,128)(2,1)S(1)} %get-tuple-element.31), channel_id=1, source_target_pairs={{0,4},{1,5},{2,6},{3,7},{4,8},{5,9},{6,10},{7,11},{8,12},{9,13},{1... | collective-permute-start | bytes 540680 | tf_op jit(solution)/shard_map/ppermute | solution.py:274
  14.6 16.0 %collective-permute-start.6 = (bf16[136,1024]{1,0:T(8,128)(2,1)S(1)}, bf16[136,1024]{1,0:T(8,128)(2,1)S(1)}, u32[]{:S(2)}, u32[]{:S(2)}) collective-permute-start(bf16[136,1024]{1,0:T(8,128)(2,1)S(1)} %collective-permute-done.4.refs_3_), channel_id=1, source_target_pairs={{0,1},{1,0},{2,3},{3,2},{4,5},{5,4},{6,7},{7,6},{8,9},{9,8},{10,11... | collective-permute-start | bytes 835592 | tf_op jit(solution)/shard_map/ppermute | solution.py:270
  18.2 12.5 %collective-permute-start.5 = (bf16[128,1024]{1,0:T(8,128)(2,1)S(1)}, bf16[128,1024]{1,0:T(8,128)(2,1)S(1)}, u32[]{:S(2)}, u32[]{:S(2)}) collective-permute-start(bf16[128,1024]{1,0:T(8,128)(2,1)S(1)} %collective-permute-done.3.refs_2_), channel_id=1, source_target_pairs={{0,1},{1,0},{2,3},{3,2},{4,5},{5,4},{6,7},{7,6},{8,9},{9,8},{10,11... | collective-permute-start | bytes 786440 | tf_op jit(solution)/shard_map/ppermute | solution.py:270
  30.0 2.9 %collective-permute-start.8 = (bf16[88,1024]{1,0:T(8,128)(2,1)S(1)}, bf16[88,1024]{1,0:T(8,128)(2,1)S(1)}, u32[]{:S(2)}, u32[]{:S(2)}) collective-permute-start(bf16[88,1024]{1,0:T(8,128)(2,1)S(1)} %collective-permute-done.7.tail_ref), channel_id=1, source_target_pairs={{4,9},{5,8},{6,11},{7,10},{8,13},{9,12},{10,15},{11,14},{20,25},{2... | collective-permute-start | bytes 540680 | tf_op jit(solution)/shard_map/ppermute | solution.py:274
  32.7 3.6 %collective-permute-start.9 = (f32[1,256]{1,0:T(1,128)S(1)}, f32[1,256]{1,0:T(1,128)S(1)}, u32[]{:S(2)}, u32[]{:S(2)}) collective-permute-start(f32[1,256]{1,0:T(1,128)S(1)} %get-tuple-element.38), channel_id=1, source_target_pairs={{4,0},{5,1},{6,2},{7,3},{8,4},{9,5},{10,6},{11,7},{12,8},{13,9},{1... | collective-permute-start | bytes 3080 | tf_op jit(solution)/shard_map/ppermute | solution.py:274
  36.3 5.8 %collective-permute-start.10 = (f32[1,256]{1,0:T(1,128)S(1)}, f32[1,256]{1,0:T(1,128)S(1)}, u32[]{:S(2)}, u32[]{:S(2)}) collective-permute-start(f32[1,256]{1,0:T(1,128)S(1)} %get-tuple-element.41), channel_id=1, source_target_pairs={{8,1},{9,0},{10,3},{11,2},{12,5},{13,4},{14,7},{15,6},{24,17},{25,... | collective-permute-start | bytes 3080 | tf_op jit(solution)/shard_map/ppermute | solution.py:274
  37.8 4.3 %collective-permute-start.11 = (f32[1,256]{1,0:T(1,128)S(1)}, f32[1,256]{1,0:T(1,128)S(1)}, u32[]{:S(2)}, u32[]{:S(2)}) collective-permute-start(f32[1,256]{1,0:T(1,128)S(1)} %get-tuple-element.42), channel_id=1, source_target_pairs={{0,3},{1,2},{2,1},{3,0},{4,7},{5,6},{6,5},{7,4},{8,11},{9,10},{10,... | collective-permute-start | bytes 3080 | tf_op jit(solution)/shard_map/ppermute | solution.py:270
  37.9 4.2 %collective-permute-start.12 = (f32[1,256]{1,0:T(1,128)S(1)}, f32[1,256]{1,0:T(1,128)S(1)}, u32[]{:S(2)}, u32[]{:S(2)}) collective-permute-start(f32[1,256]{1,0:T(1,128)S(1)} %get-tuple-element.43), channel_id=1, source_target_pairs={{0,2},{1,3},{2,0},{3,1},{4,6},{5,7},{6,4},{7,5},{8,10},{9,11},{10,... | collective-permute-start | bytes 3080 | tf_op jit(solution)/shard_map/ppermute | solution.py:270
  38.9 3.2 %collective-permute-start.13 = (f32[1,256]{1,0:T(1,128)S(1)}, f32[1,256]{1,0:T(1,128)S(1)}, u32[]{:S(2)}, u32[]{:S(2)}) collective-permute-start(f32[1,256]{1,0:T(1,128)S(1)} %get-tuple-element.44), channel_id=1, source_target_pairs={{0,1},{1,0},{2,3},{3,2},{4,5},{5,4},{6,7},{7,6},{8,9},{9,8},{10,11... | collective-permute-start | bytes 3080 | tf_op jit(solution)/shard_map/ppermute | solution.py:270

commit v33 on v29

--- a/solution.py
+++ b/solution.py
@@ -80,7 +80,6 @@
 
 LANES = 128
 PLANE = 4
-INVERSE_TEMP_BITS = 20.0 * 1.4426950408889634
 ID_ROWS = 8
 VMEM_BYTES = 16 * 1024 * 1024
 
@@ -109,7 +108,7 @@
         query_pos = lax.broadcasted_iota(jnp.int32, similar.shape, 0) + shift
         key_pos = lax.broadcasted_iota(jnp.int32, similar.shape, 1)
         mates = mates & (query_pos != key_pos)
-    return jnp.where(mates, jnp.exp2(similar * INVERSE_TEMP_BITS), 0.0)
+    return jnp.where(mates, jnp.exp(similar * inverse_temp), 0.0)
 
 
 def unit_rows(raw):
@@ -150,15 +149,6 @@
     return column
 
 
-def add_masses(query_ids, key_ids, powers):
-    mates = jnp.concatenate([query_ids] * (powers.shape[1] // LANES), axis=1) == key_ids
-    masses = jnp.where(mates, powers, 0.0)
-    folded = masses[:, :LANES]
-    for lane in range(LANES, powers.shape[1], LANES):
-        folded = folded + masses[:, lane : lane + LANES]
-    return folded, jnp.sum(masses, axis=0, keepdims=True)
-
-
 def query_parts_of(refs, rows):
     head = refs[2].shape[0]
     sizes = [rows, rows] + [head, rows - head] * (PLANE - 2)
@@ -173,7 +163,7 @@
 
 
 def first_kernel(moves, own_mass_ref, head_ref, tail_ref, *refs):
-    query_refs, (ids_ref, column_ref, sums_ref, mass_ref) = refs[:-4], refs[-4:]
+    query_refs, (column_ref, sums_ref, mass_ref, ids_ref) = refs[:-4], refs[-4:]
     rows = mass_ref.shape[1]
     query_parts = query_parts_of(query_refs, rows)
     own_ref = query_refs[0]
@@ -194,64 +184,84 @@
     column_ref[...] = add_line(query_parts, ids_ref, key_rows, key_ids, None, sums_ref)
 
 
-def middle_kernel(moves, head_ref, *refs):
-    query_refs, (powers_ref, rest_ref) = refs[:-2], refs[-2:]
+def transposed_powers(key_rows, query_rows):
+    similar = lax.dot_general(
+        key_rows, query_rows, (((1,), (1,)), ((), ())), preferred_element_type=jnp.float32
+    )
+    return jnp.exp(similar * inverse_temp)
+
+
+def middle_kernel(moves, head_ref, sums_ref, mass_ref, *refs):
+    query_refs, (row_ref, query_ids_ref, powers_ref, rest_ref) = refs[:-4], refs[-4:]
+    rows = mass_ref.shape[1]
+    for m, ref in enumerate((*query_refs[:2], query_refs[3], query_refs[5])):
+        part = pl.ds(m * rows, rows)
+        row_sum = jnp.sum(sums_ref[part, :].T, axis=0, keepdims=True)
+        row_ref[:, part] = row_sum + mass_ref[...] if m == 0 else row_sum
+        query_ids_ref[:, part] = ids_of(ref)[:, :rows]
 
     @pl.when(arrived_at(moves))
     def _():
-        keys = powers_ref.shape[1]
+        keys = powers_ref.shape[0]
         units = unit_rows(head_ref[...])
         rest_ref[...] = units[keys:]
         first = 0
-        for query_ref, size in query_parts_of(query_refs, query_refs[0].shape[0] - ID_ROWS):
-            similar = lax.dot_general(
-                query_ref[:size, :], units[:keys], (((1,), (1,)), ((), ())),
-                preferred_element_type=jnp.float32,
+        for query_ref, size in query_parts_of(query_refs, rows):
+            powers_ref[:, pl.ds(first, size)] = transposed_powers(
+                units[:keys], query_ref[:size, :]
             )
-            powers_ref[pl.ds(first, size), :] = jnp.exp2(similar * INVERSE_TEMP_BITS)
             first += size
 
 
-def last_kernel(moves, powers_ref, rest_ref, tail_ref, ids_ref, earlier_ref, *refs):
-    query_refs, (column_ref, sums_ref) = refs[:-2], refs[-2:]
+def fold_lanes(values):
+    folded = values[:, :LANES]
+    for lane in range(LANES, values.shape[1], LANES):
+        folded = folded + values[:, lane : lane + LANES]
+    return folded
+
+
+def last_kernel(moves, row_ref, query_ids_ref, powers_ref, rest_ref, tail_ref, *refs):
+    query_refs, (column_ref, *row_refs) = refs[: -PLANE - 1], refs[-PLANE - 1 :]
     rows = column_ref.shape[1]
-    cut = powers_ref.shape[1]
+    cut = powers_ref.shape[0]
     arrived = arrived_at(moves)
 
     @pl.when(arrived)
     def _():
         key_ids = ids_of(tail_ref)[:, :rows]
-        key_rows = jnp.concatenate([rest_ref[...], tail_ref[: tail_ref.shape[0] - ID_ROWS, :]], axis=0)
-        early_column = jnp.zeros((1, cut), jnp.float32)
-        late_column = jnp.zeros((1, rows - cut), jnp.float32)
+        early_ids, late_ids = along_rows(key_ids[:, :cut]), along_rows(key_ids[:, cut:])
+        tail = tail_ref[: tail_ref.shape[0] - ID_ROWS, :]
+        key_rows = jnp.concatenate([rest_ref[...], tail], axis=0)
+        early_column = jnp.zeros((cut, LANES), jnp.float32)
+        late_column = jnp.zeros((rows - cut, LANES), jnp.float32)
         first = 0
         for query_ref, size in query_parts_of(query_refs, rows):
             part = pl.ds(first, size)
-            query_ids = ids_ref[part, :]
-            similar = lax.dot_general(
-                query_ref[:size, :], key_rows, (((1,), (1,)), ((), ())),
-                preferred_element_type=jnp.float32,
+            query_ids = query_ids_ref[:, part]
+            repeats = size // LANES
+            late = jnp.where(
+                jnp.concatenate([late_ids] * repeats, axis=1) == query_ids,
+                transposed_powers(key_rows, query_ref[:size, :]), 0.0,
             )
-            powers = jnp.exp2(similar * INVERSE_TEMP_BITS)
-            late, column = add_masses(query_ids, key_ids[:, cut:], powers)
-            late_column = late_column + column
-            early, column = add_masses(query_ids, key_ids[:, :cut], powers_ref[part, :])
-            early_column = early_column + column
-            sums_ref[part, :] = earlier_ref[part, :] + early + late
+            early = jnp.where(
+                jnp.concatenate([early_ids] * repeats, axis=1) == query_ids,
+                powers_ref[:, part], 0.0,
+            )
+            early_column = early_column + fold_lanes(early)
+            late_column = late_column + fold_lanes(late)
+            inside = first % rows
+            row_refs[first // rows][:, inside : inside + size] = row_ref[:, part] + jnp.sum(
+                early + late, axis=0, keepdims=True
+            )
             first += size
-        column_ref[...] = jnp.concatenate([early_column, late_column], axis=1)
+        column_ref[:, :cut] = jnp.sum(early_column.T, axis=0, keepdims=True)
+        column_ref[:, cut:] = jnp.sum(late_column.T, axis=0, keepdims=True)
 
     @pl.when(jnp.logical_not(arrived))
     def _():
         column_ref[...] = jnp.zeros_like(column_ref)
-        sums_ref[...] = earlier_ref[...]
-
-
-def fold_kernel(sums_ref, mass_ref, *row_refs):
-    rows = mass_ref.shape[1]
-    for m in range(PLANE):
-        row_sum = jnp.sum(sums_ref[pl.ds(m * rows, rows), :].T, axis=0, keepdims=True)
-        row_refs[m][...] = row_sum + mass_ref[...] if m == 0 else row_sum
+        for m in range(PLANE):
+            row_refs[m][...] = row_ref[:, m * rows : (m + 1) * rows]
 
 
 def grid_plan(embeddings, cluster_ids):
@@ -300,34 +310,33 @@
     last_tail = on_line(first_tail, forward_moves, 1)
     corner = [in_plane(piece, 1) for piece in across]
     queries = (block, sibling, *across, *corner)
-    ids, first_column, first_sums, mass = pl.pallas_call(
+    first_column, first_sums, mass = pl.pallas_call(
         functools.partial(first_kernel, first_moves),
-        out_shape=(lanes, vector, lanes, vector),
+        out_shape=(vector, lanes, vector),
+        scratch_shapes=[pltpu.VMEM(lanes.shape, lanes.dtype)],
         cost_estimate=small,
         compiler_params=params,
     )(own_mass, first_head, first_tail, *queries)
     returned_first = on_line(first_column, first_back, 0)
-    powers, rest = pl.pallas_call(
+    plane_vector = jax.ShapeDtypeStruct((1, plane_rows), jnp.float32)
+    rows_before, query_ids, powers, rest = pl.pallas_call(
         functools.partial(middle_kernel, last_moves),
         out_shape=(
-            jax.ShapeDtypeStruct((plane_rows, half), jnp.float32), rows_of(part - half)
+            plane_vector,
+            plane_vector,
+            jax.ShapeDtypeStruct((half, plane_rows), jnp.float32),
+            rows_of(part - half),
         ),
         cost_estimate=small,
         compiler_params=params,
-    )(last_head, *queries)
-    last_column, sums = pl.pallas_call(
+    )(last_head, first_sums, mass, *queries)
+    last_column, *row_sums = pl.pallas_call(
         functools.partial(last_kernel, last_moves),
-        out_shape=(vector, lanes),
+        out_shape=[vector] * (1 + PLANE),
         cost_estimate=small,
         compiler_params=params,
-    )(powers, rest, last_tail, ids, first_sums, *queries)
+    )(rows_before, query_ids, powers, rest, last_tail, *queries)
     returned_first, last_column = lax.optimization_barrier((returned_first, last_column))
-    row_sums = pl.pallas_call(
-        fold_kernel,
-        out_shape=[vector] * PLANE,
-        cost_estimate=small,
-        compiler_params=params,
-    )(sums, mass)
     returned = [on_line(last_column, last_back, 1)]
     returned += [in_plane(row_sums[step], step) for step in (2, 3, 1)]
     return jnp.log1p(sum(returned, row_sums[0] + returned_first)).reshape(row_count)

time: 34.3 us -> 36.5 us (1.064)
  waiting for transfers between devices: 15.5 us -> 17.6 us
    ppermute x6, waiting for transfers between devices: 11.6 us -> 12.7 us  [on_line(): return lax.ppermute(value, 'gx', pairs)]
    ppermute x8, waiting for transfers between devices: 3.87 us -> 4.92 us  [in_plane(): return lax.ppermute(value, 'gx', [(i, i ^ step) for i in range(peers)])]
    pallas_call x4 -> x3, Pallas kernels: 2.26 us -> 2.25 us  [the longest x1 2.01 us: grid_plan(): pl.pallas_call(functools.partial(first_kernel, first_moves), out_shape=(v...]
  transfers between devices with their start and end apart: 14 -> 14, of which waited for: 7 -> 8; matrix products, arithmetic and copies ran while one was open for 0% -> 0% of each run, Pallas kernels for 8% -> 8%
where the time goes in v33:
time: 36.5 us; the launch traced here: 36.2 us
  waiting for transfers between devices  17.6 us (48%)
  starting transfers between devices  14.1 us (39%)
  Pallas kernels  2.8 us (8%)
  local copies, waits for them, and re-layouts  1.08 us (3%)
  other arithmetic  0.58 us (2%)
    ppermute x6, waiting for transfers between devices, on_line(): return lax.ppermute(value, 'gx', pairs)  12.7 us
    ppermute x6, starting transfers between devices, on_line(): return lax.ppermute(value, 'gx', pairs)  9.64 us
    ppermute x8, waiting for transfers between devices, in_plane(): return lax.ppermute(value, 'gx', [(i, i ^ step) for i in range(peers)])  4.92 us
    ppermute x8, starting transfers between devices, in_plane(): return lax.ppermute(value, 'gx', [(i, i ^ step) for i in range(peers)])  4.45 us
    pallas_call x1, Pallas kernels, grid_plan(): pl.pallas_call(functools.partial(first_kernel, first_moves), out_shape=(v...  2.01 us
    slice x1, local copies, waits for them, and re-layouts, grid_plan(): first_head = on_line(embeddings[:part], first_moves, 0)  1.07 us
  transfers between devices with their start and end apart: 14, of which 8 were waited for; matrix products, arithmetic and copies ran while one was open for 0% of the time, Pallas kernels for 8%

profile of v33, /device:TPU:0, one launch (start us, length us, event | category | flops | bytes accessed | tf_op | source)
XLA Modules:
  0.0 36.2 jit_solution(17915591199677227803)
XLA Ops:
  0.0 0.0 copy-start
  0.0 1.1 %slice.3 = bf16[160,1024]{1,0:T(8,128)(2,1)S(1)} slice(bf16[256,1024]{1,0:T(8,128)(2,1)} %rows_ref.1), slice={[0:160], [0:1024]} | slice | bytes 655360 | tf_op jit(solution)/shard_map/slice | solution.py:295
  1.1 0.0 copy-start.1
  1.1 3.1 %collective-permute-start = (bf16[160,1024]{1,0:T(8,128)(2,1)S(1)}, bf16[160,1024]{1,0:T(8,128)(2,1)S(1)}, u32[]{:S(2)}, u32[]{:S(2)}) collective-permute-start(bf16[160,1024]{1,0:T(8,128)(2,1)S(1)} %slice.3), channel_id=1, source_target_pairs={{0,4},{1,5},{2,6},{3,7},{4,8},{5,9},{6,10},{7,11},{8,12},{9,13},{1... | collective-permute-start | bytes 983048 | tf_op jit(solution)/shard_map/ppermute | solution.py:284
  4.2 0.0 copy-done
  4.2 0.0 copy-done.1
  4.2 0.2 shard_map.28
  4.4 1.6 %collective-permute-start.5 = (bf16[136,1024]{1,0:T(8,128)(2,1)S(1)}, bf16[136,1024]{1,0:T(8,128)(2,1)S(1)}, u32[]{:S(2)}, u32[]{:S(2)}) collective-permute-start(bf16[136,1024]{1,0:T(8,128)(2,1)S(1)} %get-tuple-element.30), channel_id=1, source_target_pairs={{0,2},{1,3},{2,0},{3,1},{4,6},{5,7},{6,4},{7,5},{8,10},{9,11},{10,... | collective-permute-start | bytes 835592 | tf_op jit(solution)/shard_map/ppermute | solution.py:280
  5.9 0.0 collective-permute-start.3
  5.9 0.5 %collective-permute-start.4 = (bf16[128,1024]{1,0:T(8,128)(2,1)S(1)}, bf16[128,1024]{1,0:T(8,128)(2,1)S(1)}, u32[]{:S(2)}, u32[]{:S(2)}) collective-permute-start(bf16[128,1024]{1,0:T(8,128)(2,1)S(1)} %get-tuple-element.29), channel_id=1, source_target_pairs={{0,2},{1,3},{2,0},{3,1},{4,6},{5,7},{6,4},{7,5},{8,10},{9,11},{10,... | collective-permute-start | bytes 786440 | tf_op jit(solution)/shard_map/ppermute | solution.py:280
  6.5 0.4 shard_map.29.own_mass_ref
  6.8 1.6 %collective-permute-start.2 = (bf16[104,1024]{1,0:T(8,128)(2,1)S(1)}, bf16[104,1024]{1,0:T(8,128)(2,1)S(1)}, u32[]{:S(2)}, u32[]{:S(2)}) collective-permute-start(bf16[104,1024]{1,0:T(8,128)(2,1)S(1)} %get-tuple-element.28), channel_id=1, source_target_pairs={{0,4},{1,5},{2,6},{3,7},{4,8},{5,9},{6,10},{7,11},{8,12},{9,13},{1... | collective-permute-start | bytes 638984 | tf_op jit(solution)/shard_map/ppermute | solution.py:284
  8.4 6.3 %collective-permute-done.head_ref = bf16[160,1024]{1,0:T(8,128)(2,1)S(1)} collective-permute-done((bf16[160,1024]{1,0:T(8,128)(2,1)S(1)}, bf16[160,1024]{1,0:T(8,128)(2,1)S(1)}, u32[]{:S(2)}, u32[]{:S(2)}) %collective-permute-start) | collective-permute-done | bytes 327712 | tf_op jit(solution)/shard_map/ppermute | solution.py:284
  14.7 0.0 collective-permute-start.1
  14.7 0.0 collective-permute-done.5.refs_3_
  14.7 0.1 collective-permute-start.7
  14.9 3.3 %collective-permute-done.4.refs_2_ = bf16[128,1024]{1,0:T(8,128)(2,1)S(1)} collective-permute-done((bf16[128,1024]{1,0:T(8,128)(2,1)S(1)}, bf16[128,1024]{1,0:T(8,128)(2,1)S(1)}, u32[]{:S(2)}, u32[]{:S(2)}) %collective-permute-start.4) | collective-permute-done | bytes 262176 | tf_op jit(solution)/shard_map/ppermute | solution.py:280
  18.2 0.0 collective-permute-start.6
  18.2 0.3 collective-permute-done.2.tail_ref
  18.5 0.7 %collective-permute-start.8 = (bf16[104,1024]{1,0:T(8,128)(2,1)S(1)}, bf16[104,1024]{1,0:T(8,128)(2,1)S(1)}, u32[]{:S(2)}, u32[]{:S(2)}) collective-permute-start(bf16[104,1024]{1,0:T(8,128)(2,1)S(1)} %collective-permute-done.2.tail_ref), channel_id=1, source_target_pairs={{4,9},{5,8},{6,11},{7,10},{8,13},{9,12},{10,15},{11,14},{20,25},{2... | collective-permute-start | bytes 638984 | tf_op jit(solution)/shard_map/ppermute | solution.py:284
  19.1 0.6 %collective-permute-done.6.refs_4_ = bf16[128,1024]{1,0:T(8,128)(2,1)S(1)} collective-permute-done((bf16[128,1024]{1,0:T(8,128)(2,1)S(1)}, bf16[128,1024]{1,0:T(8,128)(2,1)S(1)}, u32[]{:S(2)}, u32[]{:S(2)}) %collective-permute-start.6) | collective-permute-done | bytes 262176 | tf_op jit(solution)/shard_map/ppermute | solution.py:280
  19.7 0.0 collective-permute-done.3.refs_1_
  19.7 0.0 collective-permute-done.7.refs_5_
  19.7 2.0 %shard_map.30 = (f32[1,256]{1,0:T(1,128)S(1)}, f32[1024,128]{1,0:T(8,128)S(1)}, f32[1,256]{1,0:T(1,128)S(1)}) custom-call(f32[1,256]{1,0:T(1,128)S(1)} %shard_map.29.own_mass_ref, bf16[160,1024]{1,0:T(8,128)(2,1)S(1)} %collective-permute-done.head_ref, bf16[104,1024]{1,0:T(8,128)(2,1)S(1)} %collective-permute-done.2.tail_ref, ...), custom_call_target="tpu_custom_call" | custom-call | flops 1 | bytes 1 | tf_op jit(solution)/shard_map/pallas_call | solution.py:313
  21.7 3.0 %collective-permute-start.9 = (f32[1,256]{1,0:T(1,128)S(1)}, f32[1,256]{1,0:T(1,128)S(1)}, u32[]{:S(2)}, u32[]{:S(2)}) collective-permute-start(f32[1,256]{1,0:T(1,128)S(1)} %get-tuple-element.38), channel_id=1, source_target_pairs={{4,0},{5,1},{6,2},{7,3},{8,4},{9,5},{10,6},{11,7},{12,8},{13,9},{1... | collective-permute-start | bytes 3080 | tf_op jit(solution)/shard_map/ppermute | solution.py:284
  24.7 0.8 %collective-permute-done.1.head_ref = bf16[160,1024]{1,0:T(8,128)(2,1)S(1)} collective-permute-done((bf16[160,1024]{1,0:T(8,128)(2,1)S(1)}, bf16[160,1024]{1,0:T(8,128)(2,1)S(1)}, u32[]{:S(2)}, u32[]{:S(2)}) %collective-permute-start.1) | collective-permute-done | bytes 327712 | tf_op jit(solution)/shard_map/ppermute | solution.py:284
  25.5 0.2 shard_map.31
  25.7 0.0 collective-permute-done.8.tail_ref
  25.7 1.6 %collective-permute-start.11 = (f32[1,256]{1,0:T(1,128)S(1)}, f32[1,256]{1,0:T(1,128)S(1)}, u32[]{:S(2)}, u32[]{:S(2)}) collective-permute-start(f32[1,256]{1,0:T(1,128)S(1)} %get-tuple-element.42), channel_id=1, source_target_pairs={{0,2},{1,3},{2,0},{3,1},{4,6},{5,7},{6,4},{7,5},{8,10},{9,11},{10,... | collective-permute-start | bytes 3080 | tf_op jit(solution)/shard_map/ppermute | solution.py:280
  27.3 0.0 collective-permute-start.12
  27.3 0.6 %collective-permute-start.13 = (f32[1,256]{1,0:T(1,128)S(1)}, f32[1,256]{1,0:T(1,128)S(1)}, u32[]{:S(2)}, u32[]{:S(2)}) collective-permute-start(f32[1,256]{1,0:T(1,128)S(1)} %get-tuple-element.44), channel_id=1, source_target_pairs={{0,1},{1,0},{2,3},{3,2},{4,5},{5,4},{6,7},{7,6},{8,9},{9,8},{10,11... | collective-permute-start | bytes 3080 | tf_op jit(solution)/shard_map/ppermute | solution.py:280
  28.0 0.0 collective-permute-done.9
  28.0 1.3 %collective-permute-start.10 = (f32[1,256]{1,0:T(1,128)S(1)}, f32[1,256]{1,0:T(1,128)S(1)}, u32[]{:S(2)}, u32[]{:S(2)}) collective-permute-start(f32[1,256]{1,0:T(1,128)S(1)} %get-tuple-element.41), channel_id=1, source_target_pairs={{8,1},{9,0},{10,3},{11,2},{12,5},{13,4},{14,7},{15,6},{24,17},{25,... | collective-permute-start | bytes 3080 | tf_op jit(solution)/shard_map/ppermute | solution.py:284
  29.2 0.1 collective-permute-done.11
  29.4 0.9 %collective-permute-done.12 = f32[1,256]{1,0:T(1,128)S(1)} collective-permute-done((f32[1,256]{1,0:T(1,128)S(1)}, f32[1,256]{1,0:T(1,128)S(1)}, u32[]{:S(2)}, u32[]{:S(2)}) %collective-permute-start.12) | collective-permute-done | bytes 1056 | tf_op jit(solution)/shard_map/ppermute | solution.py:280
  30.3 0.0 collective-permute-done.13
  30.3 5.3 %collective-permute-done.10 = f32[1,256]{1,0:T(1,128)S(1)} collective-permute-done((f32[1,256]{1,0:T(1,128)S(1)}, f32[1,256]{1,0:T(1,128)S(1)}, u32[]{:S(2)}, u32[]{:S(2)}) %collective-permute-start.10) | collective-permute-done | bytes 1056 | tf_op jit(solution)/shard_map/ppermute | solution.py:284
  35.6 0.6 %add_log-plus-one_fusion = f32[1,256]{1,0:T(1,128)} fusion(f32[1,256]{1,0:T(1,128)S(1)} %collective-permute-done.13, f32[1,256]{1,0:T(1,128)S(1)} %collective-permute-done.12, f32[1,256]{1,0:T(1,128)S(1)} %collective-permute-done.11, f32[1,256]{1,0:T(1,128)S(1)} %collective-permute-done.10, f32[1,256]{1,0:T(1,128)S(1)} %get-tuple-element.37, ...), kind=kLoop, calls=%fused_computation | loop fusion | flops 1280 | bytes 7168 | tf_op jit(solution)/shard_map/log1p | solution.py:342
  (1 shorter events, 0.0 us)
Async XLA Ops:
  0.0 4.2 %copy-start = (bf16[256,1024]{1,0:T(8,128)(2,1)S(1)}, bf16[256,1024]{1,0:T(8,128)(2,1)}, u32[]{:S(2)}) copy-start(bf16[256,1024]{1,0:T(8,128)(2,1)} %rows_ref.1) | copy-start | bytes 1572868
  1.1 3.1 %copy-start.1 = (s32[256]{0:T(256)S(1)}, s32[256]{0:T(256)}, u32[]{:S(2)}) copy-start(s32[256]{0:T(256)} %param.3) | copy-start | bytes 3076
  1.1 13.6 %collective-permute-start = (bf16[160,1024]{1,0:T(8,128)(2,1)S(1)}, bf16[160,1024]{1,0:T(8,128)(2,1)S(1)}, u32[]{:S(2)}, u32[]{:S(2)}) collective-permute-start(bf16[160,1024]{1,0:T(8,128)(2,1)S(1)} %slice.3), channel_id=1, source_target_pairs={{0,4},{1,5},{2,6},{3,7},{4,8},{5,9},{6,10},{7,11},{8,12},{9,13},{1... | collective-permute-start | bytes 983048 | tf_op jit(solution)/shard_map/ppermute | solution.py:284
  4.4 10.4 %collective-permute-start.5 = (bf16[136,1024]{1,0:T(8,128)(2,1)S(1)}, bf16[136,1024]{1,0:T(8,128)(2,1)S(1)}, u32[]{:S(2)}, u32[]{:S(2)}) collective-permute-start(bf16[136,1024]{1,0:T(8,128)(2,1)S(1)} %get-tuple-element.30), channel_id=1, source_target_pairs={{0,2},{1,3},{2,0},{3,1},{4,6},{5,7},{6,4},{7,5},{8,10},{9,11},{10,... | collective-permute-start | bytes 835592 | tf_op jit(solution)/shard_map/ppermute | solution.py:280
  5.9 13.8 %collective-permute-start.3 = (bf16[264,1024]{1,0:T(8,128)(2,1)S(1)}, bf16[264,1024]{1,0:T(8,128)(2,1)S(1)}, u32[]{:S(2)}, u32[]{:S(2)}) collective-permute-start(bf16[264,1024]{1,0:T(8,128)(2,1)S(1)} %get-tuple-element.25.own_ref.refs_0_), channel_id=1, source_target_pairs={{0,1},{1,0},{2,3},{3,2},{4,5},{5,4},{6,7},{7,6},{8,9},{9,8},{10,11... | collective-permute-start | bytes 1622024 | tf_op jit(solution)/shard_map/ppermute | solution.py:280
  5.9 12.2 %collective-permute-start.4 = (bf16[128,1024]{1,0:T(8,128)(2,1)S(1)}, bf16[128,1024]{1,0:T(8,128)(2,1)S(1)}, u32[]{:S(2)}, u32[]{:S(2)}) collective-permute-start(bf16[128,1024]{1,0:T(8,128)(2,1)S(1)} %get-tuple-element.29), channel_id=1, source_target_pairs={{0,2},{1,3},{2,0},{3,1},{4,6},{5,7},{6,4},{7,5},{8,10},{9,11},{10,... | collective-permute-start | bytes 786440 | tf_op jit(solution)/shard_map/ppermute | solution.py:280
  6.8 11.6 %collective-permute-start.2 = (bf16[104,1024]{1,0:T(8,128)(2,1)S(1)}, bf16[104,1024]{1,0:T(8,128)(2,1)S(1)}, u32[]{:S(2)}, u32[]{:S(2)}) collective-permute-start(bf16[104,1024]{1,0:T(8,128)(2,1)S(1)} %get-tuple-element.28), channel_id=1, source_target_pairs={{0,4},{1,5},{2,6},{3,7},{4,8},{5,9},{6,10},{7,11},{8,12},{9,13},{1... | collective-permute-start | bytes 638984 | tf_op jit(solution)/shard_map/ppermute | solution.py:284
  14.7 10.8 %collective-permute-start.1 = (bf16[160,1024]{1,0:T(8,128)(2,1)S(1)}, bf16[160,1024]{1,0:T(8,128)(2,1)S(1)}, u32[]{:S(2)}, u32[]{:S(2)}) collective-permute-start(bf16[160,1024]{1,0:T(8,128)(2,1)S(1)} %collective-permute-done.head_ref), channel_id=1, source_target_pairs={{0,5},{1,4},{2,7},{3,6},{4,9},{5,8},{6,11},{7,10},{8,13},{9,12},{1... | collective-permute-start | bytes 983048 | tf_op jit(solution)/shard_map/ppermute | solution.py:284
  14.7 5.0 %collective-permute-start.7 = (bf16[136,1024]{1,0:T(8,128)(2,1)S(1)}, bf16[136,1024]{1,0:T(8,128)(2,1)S(1)}, u32[]{:S(2)}, u32[]{:S(2)}) collective-permute-start(bf16[136,1024]{1,0:T(8,128)(2,1)S(1)} %collective-permute-done.5.refs_3_), channel_id=1, source_target_pairs={{0,1},{1,0},{2,3},{3,2},{4,5},{5,4},{6,7},{7,6},{8,9},{9,8},{10,11... | collective-permute-start | bytes 835592 | tf_op jit(solution)/shard_map/ppermute | solution.py:280
  18.2 1.5 %collective-permute-start.6 = (bf16[128,1024]{1,0:T(8,128)(2,1)S(1)}, bf16[128,1024]{1,0:T(8,128)(2,1)S(1)}, u32[]{:S(2)}, u32[]{:S(2)}) collective-permute-start(bf16[128,1024]{1,0:T(8,128)(2,1)S(1)} %collective-permute-done.4.refs_2_), channel_id=1, source_target_pairs={{0,1},{1,0},{2,3},{3,2},{4,5},{5,4},{6,7},{7,6},{8,9},{9,8},{10,11... | collective-permute-start | bytes 786440 | tf_op jit(solution)/shard_map/ppermute | solution.py:280
  18.5 7.2 %collective-permute-start.8 = (bf16[104,1024]{1,0:T(8,128)(2,1)S(1)}, bf16[104,1024]{1,0:T(8,128)(2,1)S(1)}, u32[]{:S(2)}, u32[]{:S(2)}) collective-permute-start(bf16[104,1024]{1,0:T(8,128)(2,1)S(1)} %collective-permute-done.2.tail_ref), channel_id=1, source_target_pairs={{4,9},{5,8},{6,11},{7,10},{8,13},{9,12},{10,15},{11,14},{20,25},{2... | collective-permute-start | bytes 638984 | tf_op jit(solution)/shard_map/ppermute | solution.py:284
  21.7 6.2 %collective-permute-start.9 = (f32[1,256]{1,0:T(1,128)S(1)}, f32[1,256]{1,0:T(1,128)S(1)}, u32[]{:S(2)}, u32[]{:S(2)}) collective-permute-start(f32[1,256]{1,0:T(1,128)S(1)} %get-tuple-element.38), channel_id=1, source_target_pairs={{4,0},{5,1},{6,2},{7,3},{8,4},{9,5},{10,6},{11,7},{12,8},{13,9},{1... | collective-permute-start | bytes 3080 | tf_op jit(solution)/shard_map/ppermute | solution.py:284
  25.7 3.6 %collective-permute-start.11 = (f32[1,256]{1,0:T(1,128)S(1)}, f32[1,256]{1,0:T(1,128)S(1)}, u32[]{:S(2)}, u32[]{:S(2)}) collective-permute-start(f32[1,256]{1,0:T(1,128)S(1)} %get-tuple-element.42), channel_id=1, source_target_pairs={{0,2},{1,3},{2,0},{3,1},{4,6},{5,7},{6,4},{7,5},{8,10},{9,11},{10,... | collective-permute-start | bytes 3080 | tf_op jit(solution)/shard_map/ppermute | solution.py:280
  27.3 3.0 %collective-permute-start.12 = (f32[1,256]{1,0:T(1,128)S(1)}, f32[1,256]{1,0:T(1,128)S(1)}, u32[]{:S(2)}, u32[]{:S(2)}) collective-permute-start(f32[1,256]{1,0:T(1,128)S(1)} %get-tuple-element.43), channel_id=1, source_target_pairs={{0,3},{1,2},{2,1},{3,0},{4,7},{5,6},{6,5},{7,4},{8,11},{9,10},{10,... | collective-permute-start | bytes 3080 | tf_op jit(solution)/shard_map/ppermute | solution.py:280
  27.3 3.0 %collective-permute-start.13 = (f32[1,256]{1,0:T(1,128)S(1)}, f32[1,256]{1,0:T(1,128)S(1)}, u32[]{:S(2)}, u32[]{:S(2)}) collective-permute-start(f32[1,256]{1,0:T(1,128)S(1)} %get-tuple-element.44), channel_id=1, source_target_pairs={{0,1},{1,0},{2,3},{3,2},{4,5},{5,4},{6,7},{7,6},{8,9},{9,8},{10,11... | collective-permute-start | bytes 3080 | tf_op jit(solution)/shard_map/ppermute | solution.py:280
  28.0 7.7 %collective-permute-start.10 = (f32[1,256]{1,0:T(1,128)S(1)}, f32[1,256]{1,0:T(1,128)S(1)}, u32[]{:S(2)}, u32[]{:S(2)}) collective-permute-start(f32[1,256]{1,0:T(1,128)S(1)} %get-tuple-element.41), channel_id=1, source_target_pairs={{8,1},{9,0},{10,3},{11,2},{12,5},{13,4},{14,7},{15,6},{24,17},{25,... | collective-permute-start | bytes 3080 | tf_op jit(solution)/shard_map/ppermute | solution.py:284

commit v34 on v33

--- a/solution.py
+++ b/solution.py
@@ -163,7 +163,7 @@
 
 
 def first_kernel(moves, own_mass_ref, head_ref, tail_ref, *refs):
-    query_refs, (column_ref, sums_ref, mass_ref, ids_ref) = refs[:-4], refs[-4:]
+    query_refs, (ids_ref, column_ref, sums_ref, mass_ref) = refs[:-4], refs[-4:]
     rows = mass_ref.shape[1]
     query_parts = query_parts_of(query_refs, rows)
     own_ref = query_refs[0]
@@ -310,10 +310,9 @@
     last_tail = on_line(first_tail, forward_moves, 1)
     corner = [in_plane(piece, 1) for piece in across]
     queries = (block, sibling, *across, *corner)
-    first_column, first_sums, mass = pl.pallas_call(
+    _, first_column, first_sums, mass = pl.pallas_call(
         functools.partial(first_kernel, first_moves),
-        out_shape=(vector, lanes, vector),
-        scratch_shapes=[pltpu.VMEM(lanes.shape, lanes.dtype)],
+        out_shape=(lanes, vector, lanes, vector),
         cost_estimate=small,
         compiler_params=params,
     )(own_mass, first_head, first_tail, *queries)

time: 36.5 us -> 34.4 us (0.942)
  waiting for transfers between devices: 17.6 us -> 15.1 us
  Pallas kernels: 2.8 us -> 3.41 us
    ppermute x6, waiting for transfers between devices: 12.7 us -> 11.2 us  [on_line(): return lax.ppermute(value, 'gx', pairs)]
    ppermute x8, waiting for transfers between devices: 4.92 us -> 3.87 us  [in_plane(): return lax.ppermute(value, 'gx', [(i, i ^ step) for i in range(peers)])]
    pallas_call x1, Pallas kernels: 2.01 us -> 2.63 us  [grid_plan(): pl.pallas_call(functools.partial(first_kernel, first_moves), out_shape=(l...]
  transfers between devices with their start and end apart: 14 -> 14, of which waited for: 8 -> 7; matrix products, arithmetic and copies ran while one was open for 0% -> 0% of each run, Pallas kernels for 8% -> 10%
where the time goes in v34:
time: 34.4 us; the launch traced here: 34.2 us
  waiting for transfers between devices  15.1 us (44%)
  starting transfers between devices  14 us (41%)
  Pallas kernels  3.41 us (10%)
  local copies, waits for them, and re-layouts  1.08 us (3%)
  other arithmetic  0.58 us (2%)
    ppermute x6, waiting for transfers between devices, on_line(): return lax.ppermute(value, 'gx', pairs)  11.2 us
    ppermute x6, starting transfers between devices, on_line(): return lax.ppermute(value, 'gx', pairs)  9.58 us
    ppermute x8, starting transfers between devices, in_plane(): return lax.ppermute(value, 'gx', [(i, i ^ step) for i in range(peers)])  4.45 us
    ppermute x8, waiting for transfers between devices, in_plane(): return lax.ppermute(value, 'gx', [(i, i ^ step) for i in range(peers)])  3.87 us
    pallas_call x1, Pallas kernels, grid_plan(): pl.pallas_call(functools.partial(first_kernel, first_moves), out_shape=(l...  2.63 us
    slice x1, local copies, waits for them, and re-layouts, grid_plan(): first_head = on_line(embeddings[:part], first_moves, 0)  1.07 us
  transfers between devices with their start and end apart: 14, of which 7 were waited for; matrix products, arithmetic and copies ran while one was open for 0% of the time, Pallas kernels for 10%

profile of v34, /device:TPU:0, one launch (start us, length us, event | category | flops | bytes accessed | tf_op | source)
XLA Modules:
  0.0 34.2 jit_solution(16168459483674164505)
XLA Ops:
  0.0 0.0 copy-start
  0.0 1.1 %slice.3 = bf16[160,1024]{1,0:T(8,128)(2,1)S(1)} slice(bf16[256,1024]{1,0:T(8,128)(2,1)} %rows_ref.1), slice={[0:160], [0:1024]} | slice | bytes 655360 | tf_op jit(solution)/shard_map/slice | solution.py:295
  1.1 0.0 copy-start.1
  1.1 3.1 %collective-permute-start = (bf16[160,1024]{1,0:T(8,128)(2,1)S(1)}, bf16[160,1024]{1,0:T(8,128)(2,1)S(1)}, u32[]{:S(2)}, u32[]{:S(2)}) collective-permute-start(bf16[160,1024]{1,0:T(8,128)(2,1)S(1)} %slice.3), channel_id=1, source_target_pairs={{0,4},{1,5},{2,6},{3,7},{4,8},{5,9},{6,10},{7,11},{8,12},{9,13},{1... | collective-permute-start | bytes 983048 | tf_op jit(solution)/shard_map/ppermute | solution.py:284
  4.2 0.0 copy-done
  4.2 0.0 copy-done.1
  4.2 0.2 shard_map.28
  4.4 1.6 %collective-permute-start.5 = (bf16[136,1024]{1,0:T(8,128)(2,1)S(1)}, bf16[136,1024]{1,0:T(8,128)(2,1)S(1)}, u32[]{:S(2)}, u32[]{:S(2)}) collective-permute-start(bf16[136,1024]{1,0:T(8,128)(2,1)S(1)} %get-tuple-element.30), channel_id=1, source_target_pairs={{0,2},{1,3},{2,0},{3,1},{4,6},{5,7},{6,4},{7,5},{8,10},{9,11},{10,... | collective-permute-start | bytes 835592 | tf_op jit(solution)/shard_map/ppermute | solution.py:280
  5.9 0.0 collective-permute-start.3
  5.9 0.5 %collective-permute-start.4 = (bf16[128,1024]{1,0:T(8,128)(2,1)S(1)}, bf16[128,1024]{1,0:T(8,128)(2,1)S(1)}, u32[]{:S(2)}, u32[]{:S(2)}) collective-permute-start(bf16[128,1024]{1,0:T(8,128)(2,1)S(1)} %get-tuple-element.29), channel_id=1, source_target_pairs={{0,2},{1,3},{2,0},{3,1},{4,6},{5,7},{6,4},{7,5},{8,10},{9,11},{10,... | collective-permute-start | bytes 786440 | tf_op jit(solution)/shard_map/ppermute | solution.py:280
  6.5 0.4 %shard_map.29.own_mass_ref = f32[1,256]{1,0:T(1,128)S(1)} custom-call(bf16[264,1024]{1,0:T(8,128)(2,1)S(1)} %get-tuple-element.25.own_ref.refs_0_), custom_call_target="tpu_custom_call" | custom-call | flops 1 | bytes 1 | tf_op jit(solution)/shard_map/pallas_call | solution.py:302
  6.8 1.6 %collective-permute-start.2 = (bf16[104,1024]{1,0:T(8,128)(2,1)S(1)}, bf16[104,1024]{1,0:T(8,128)(2,1)S(1)}, u32[]{:S(2)}, u32[]{:S(2)}) collective-permute-start(bf16[104,1024]{1,0:T(8,128)(2,1)S(1)} %get-tuple-element.28), channel_id=1, source_target_pairs={{0,4},{1,5},{2,6},{3,7},{4,8},{5,9},{6,10},{7,11},{8,12},{9,13},{1... | collective-permute-start | bytes 638984 | tf_op jit(solution)/shard_map/ppermute | solution.py:284
  8.4 6.3 %collective-permute-done.head_ref = bf16[160,1024]{1,0:T(8,128)(2,1)S(1)} collective-permute-done((bf16[160,1024]{1,0:T(8,128)(2,1)S(1)}, bf16[160,1024]{1,0:T(8,128)(2,1)S(1)}, u32[]{:S(2)}, u32[]{:S(2)}) %collective-permute-start) | collective-permute-done | bytes 327712 | tf_op jit(solution)/shard_map/ppermute | solution.py:284
  14.7 0.0 collective-permute-start.1
  14.7 0.0 collective-permute-done.5.refs_3_
  14.7 0.1 collective-permute-start.7
  14.9 3.3 %collective-permute-done.4.refs_2_ = bf16[128,1024]{1,0:T(8,128)(2,1)S(1)} collective-permute-done((bf16[128,1024]{1,0:T(8,128)(2,1)S(1)}, bf16[128,1024]{1,0:T(8,128)(2,1)S(1)}, u32[]{:S(2)}, u32[]{:S(2)}) %collective-permute-start.4) | collective-permute-done | bytes 262176 | tf_op jit(solution)/shard_map/ppermute | solution.py:280
  18.2 0.0 collective-permute-start.6
  18.2 0.3 collective-permute-done.2.tail_ref
  18.5 0.7 %collective-permute-start.8 = (bf16[104,1024]{1,0:T(8,128)(2,1)S(1)}, bf16[104,1024]{1,0:T(8,128)(2,1)S(1)}, u32[]{:S(2)}, u32[]{:S(2)}) collective-permute-start(bf16[104,1024]{1,0:T(8,128)(2,1)S(1)} %collective-permute-done.2.tail_ref), channel_id=1, source_target_pairs={{4,9},{5,8},{6,11},{7,10},{8,13},{9,12},{10,15},{11,14},{20,25},{2... | collective-permute-start | bytes 638984 | tf_op jit(solution)/shard_map/ppermute | solution.py:284
  19.1 0.6 %collective-permute-done.6.refs_4_ = bf16[128,1024]{1,0:T(8,128)(2,1)S(1)} collective-permute-done((bf16[128,1024]{1,0:T(8,128)(2,1)S(1)}, bf16[128,1024]{1,0:T(8,128)(2,1)S(1)}, u32[]{:S(2)}, u32[]{:S(2)}) %collective-permute-start.6) | collective-permute-done | bytes 262176 | tf_op jit(solution)/shard_map/ppermute | solution.py:280
  19.7 0.0 collective-permute-done.3.refs_1_
  19.7 0.0 collective-permute-done.7.refs_5_
  19.7 2.6 %shard_map.30 = (f32[1024,128]{1,0:T(8,128)}, f32[1,256]{1,0:T(1,128)S(1)}, f32[1024,128]{1,0:T(8,128)S(1)}, f32[1,256]{1,0:T(1,128)S(1)}) custom-call(f32[1,256]{1,0:T(1,128)S(1)} %shard_map.29.own_mass_ref, bf16[160,1024]{1,0:T(8,128)(2,1)S(1)} %collective-permute-done.head_ref, bf16[104,1024]{1,0:T(8,128)(2,1)S(1)} %collective-permute-done.2.tail_ref, ...), custom_call_target="tpu_custom_call" | custom-call | flops 1 | bytes 1 | tf_op jit(solution)/shard_map/pallas_call | solution.py:313
  22.3 2.9 %collective-permute-start.9 = (f32[1,256]{1,0:T(1,128)S(1)}, f32[1,256]{1,0:T(1,128)S(1)}, u32[]{:S(2)}, u32[]{:S(2)}) collective-permute-start(f32[1,256]{1,0:T(1,128)S(1)} %get-tuple-element.38), channel_id=1, source_target_pairs={{4,0},{5,1},{6,2},{7,3},{8,4},{9,5},{10,6},{11,7},{12,8},{13,9},{1... | collective-permute-start | bytes 3080 | tf_op jit(solution)/shard_map/ppermute | solution.py:284
  25.3 0.2 collective-permute-done.1.head_ref
  25.5 0.2 shard_map.31
  25.7 0.0 collective-permute-done.8.tail_ref
  25.7 1.8 %collective-permute-done.9 = f32[1,256]{1,0:T(1,128)S(1)} collective-permute-done((f32[1,256]{1,0:T(1,128)S(1)}, f32[1,256]{1,0:T(1,128)S(1)}, u32[]{:S(2)}, u32[]{:S(2)}) %collective-permute-start.9) | collective-permute-done | bytes 1056 | tf_op jit(solution)/shard_map/ppermute | solution.py:284
  27.6 1.3 %collective-permute-start.10 = (f32[1,256]{1,0:T(1,128)S(1)}, f32[1,256]{1,0:T(1,128)S(1)}, u32[]{:S(2)}, u32[]{:S(2)}) collective-permute-start(f32[1,256]{1,0:T(1,128)S(1)} %get-tuple-element.41), channel_id=1, source_target_pairs={{8,1},{9,0},{10,3},{11,2},{12,5},{13,4},{14,7},{15,6},{24,17},{25,... | collective-permute-start | bytes 3080 | tf_op jit(solution)/shard_map/ppermute | solution.py:284
  28.8 1.6 %collective-permute-start.11 = (f32[1,256]{1,0:T(1,128)S(1)}, f32[1,256]{1,0:T(1,128)S(1)}, u32[]{:S(2)}, u32[]{:S(2)}) collective-permute-start(f32[1,256]{1,0:T(1,128)S(1)} %get-tuple-element.42), channel_id=1, source_target_pairs={{0,2},{1,3},{2,0},{3,1},{4,6},{5,7},{6,4},{7,5},{8,10},{9,11},{10,... | collective-permute-start | bytes 3080 | tf_op jit(solution)/shard_map/ppermute | solution.py:280
  30.4 0.0 collective-permute-start.12
  30.4 0.6 %collective-permute-start.13 = (f32[1,256]{1,0:T(1,128)S(1)}, f32[1,256]{1,0:T(1,128)S(1)}, u32[]{:S(2)}, u32[]{:S(2)}) collective-permute-start(f32[1,256]{1,0:T(1,128)S(1)} %get-tuple-element.44), channel_id=1, source_target_pairs={{0,1},{1,0},{2,3},{3,2},{4,5},{5,4},{6,7},{7,6},{8,9},{9,8},{10,11... | collective-permute-start | bytes 3080 | tf_op jit(solution)/shard_map/ppermute | solution.py:280
  31.1 2.6 %collective-permute-done.10 = f32[1,256]{1,0:T(1,128)S(1)} collective-permute-done((f32[1,256]{1,0:T(1,128)S(1)}, f32[1,256]{1,0:T(1,128)S(1)}, u32[]{:S(2)}, u32[]{:S(2)}) %collective-permute-start.10) | collective-permute-done | bytes 1056 | tf_op jit(solution)/shard_map/ppermute | solution.py:284
  33.6 0.0 collective-permute-done.11
  33.6 0.0 collective-permute-done.12
  33.7 0.0 collective-permute-done.13
  33.7 0.6 %add_log-plus-one_fusion = f32[1,256]{1,0:T(1,128)} fusion(f32[1,256]{1,0:T(1,128)S(1)} %collective-permute-done.13, f32[1,256]{1,0:T(1,128)S(1)} %collective-permute-done.12, f32[1,256]{1,0:T(1,128)S(1)} %collective-permute-done.11, f32[1,256]{1,0:T(1,128)S(1)} %collective-permute-done.10, f32[1,256]{1,0:T(1,128)S(1)} %get-tuple-element.37, ...), kind=kLoop, calls=%fused_computation | loop fusion | flops 1280 | bytes 7168 | tf_op jit(solution)/shard_map/log1p | solution.py:341
  (1 shorter events, 0.0 us)
Async XLA Ops:
  0.0 4.2 %copy-start = (bf16[256,1024]{1,0:T(8,128)(2,1)S(1)}, bf16[256,1024]{1,0:T(8,128)(2,1)}, u32[]{:S(2)}) copy-start(bf16[256,1024]{1,0:T(8,128)(2,1)} %rows_ref.1) | copy-start | bytes 1572868
  1.1 3.1 %copy-start.1 = (s32[256]{0:T(256)S(1)}, s32[256]{0:T(256)}, u32[]{:S(2)}) copy-start(s32[256]{0:T(256)} %param.3) | copy-start | bytes 3076
  1.1 13.6 %collective-permute-start = (bf16[160,1024]{1,0:T(8,128)(2,1)S(1)}, bf16[160,1024]{1,0:T(8,128)(2,1)S(1)}, u32[]{:S(2)}, u32[]{:S(2)}) collective-permute-start(bf16[160,1024]{1,0:T(8,128)(2,1)S(1)} %slice.3), channel_id=1, source_target_pairs={{0,4},{1,5},{2,6},{3,7},{4,8},{5,9},{6,10},{7,11},{8,12},{9,13},{1... | collective-permute-start | bytes 983048 | tf_op jit(solution)/shard_map/ppermute | solution.py:284
  4.4 10.4 %collective-permute-start.5 = (bf16[136,1024]{1,0:T(8,128)(2,1)S(1)}, bf16[136,1024]{1,0:T(8,128)(2,1)S(1)}, u32[]{:S(2)}, u32[]{:S(2)}) collective-permute-start(bf16[136,1024]{1,0:T(8,128)(2,1)S(1)} %get-tuple-element.30), channel_id=1, source_target_pairs={{0,2},{1,3},{2,0},{3,1},{4,6},{5,7},{6,4},{7,5},{8,10},{9,11},{10,... | collective-permute-start | bytes 835592 | tf_op jit(solution)/shard_map/ppermute | solution.py:280
  5.9 13.8 %collective-permute-start.3 = (bf16[264,1024]{1,0:T(8,128)(2,1)S(1)}, bf16[264,1024]{1,0:T(8,128)(2,1)S(1)}, u32[]{:S(2)}, u32[]{:S(2)}) collective-permute-start(bf16[264,1024]{1,0:T(8,128)(2,1)S(1)} %get-tuple-element.25.own_ref.refs_0_), channel_id=1, source_target_pairs={{0,1},{1,0},{2,3},{3,2},{4,5},{5,4},{6,7},{7,6},{8,9},{9,8},{10,11... | collective-permute-start | bytes 1622024 | tf_op jit(solution)/shard_map/ppermute | solution.py:280
  5.9 12.2 %collective-permute-start.4 = (bf16[128,1024]{1,0:T(8,128)(2,1)S(1)}, bf16[128,1024]{1,0:T(8,128)(2,1)S(1)}, u32[]{:S(2)}, u32[]{:S(2)}) collective-permute-start(bf16[128,1024]{1,0:T(8,128)(2,1)S(1)} %get-tuple-element.29), channel_id=1, source_target_pairs={{0,2},{1,3},{2,0},{3,1},{4,6},{5,7},{6,4},{7,5},{8,10},{9,11},{10,... | collective-permute-start | bytes 786440 | tf_op jit(solution)/shard_map/ppermute | solution.py:280
  6.8 11.6 %collective-permute-start.2 = (bf16[104,1024]{1,0:T(8,128)(2,1)S(1)}, bf16[104,1024]{1,0:T(8,128)(2,1)S(1)}, u32[]{:S(2)}, u32[]{:S(2)}) collective-permute-start(bf16[104,1024]{1,0:T(8,128)(2,1)S(1)} %get-tuple-element.28), channel_id=1, source_target_pairs={{0,4},{1,5},{2,6},{3,7},{4,8},{5,9},{6,10},{7,11},{8,12},{9,13},{1... | collective-permute-start | bytes 638984 | tf_op jit(solution)/shard_map/ppermute | solution.py:284
  14.7 10.8 %collective-permute-start.1 = (bf16[160,1024]{1,0:T(8,128)(2,1)S(1)}, bf16[160,1024]{1,0:T(8,128)(2,1)S(1)}, u32[]{:S(2)}, u32[]{:S(2)}) collective-permute-start(bf16[160,1024]{1,0:T(8,128)(2,1)S(1)} %collective-permute-done.head_ref), channel_id=1, source_target_pairs={{0,5},{1,4},{2,7},{3,6},{4,9},{5,8},{6,11},{7,10},{8,13},{9,12},{1... | collective-permute-start | bytes 983048 | tf_op jit(solution)/shard_map/ppermute | solution.py:284
  14.7 5.0 %collective-permute-start.7 = (bf16[136,1024]{1,0:T(8,128)(2,1)S(1)}, bf16[136,1024]{1,0:T(8,128)(2,1)S(1)}, u32[]{:S(2)}, u32[]{:S(2)}) collective-permute-start(bf16[136,1024]{1,0:T(8,128)(2,1)S(1)} %collective-permute-done.5.refs_3_), channel_id=1, source_target_pairs={{0,1},{1,0},{2,3},{3,2},{4,5},{5,4},{6,7},{7,6},{8,9},{9,8},{10,11... | collective-permute-start | bytes 835592 | tf_op jit(solution)/shard_map/ppermute | solution.py:280
  18.2 1.5 %collective-permute-start.6 = (bf16[128,1024]{1,0:T(8,128)(2,1)S(1)}, bf16[128,1024]{1,0:T(8,128)(2,1)S(1)}, u32[]{:S(2)}, u32[]{:S(2)}) collective-permute-start(bf16[128,1024]{1,0:T(8,128)(2,1)S(1)} %collective-permute-done.4.refs_2_), channel_id=1, source_target_pairs={{0,1},{1,0},{2,3},{3,2},{4,5},{5,4},{6,7},{7,6},{8,9},{9,8},{10,11... | collective-permute-start | bytes 786440 | tf_op jit(solution)/shard_map/ppermute | solution.py:280
  18.5 7.2 %collective-permute-start.8 = (bf16[104,1024]{1,0:T(8,128)(2,1)S(1)}, bf16[104,1024]{1,0:T(8,128)(2,1)S(1)}, u32[]{:S(2)}, u32[]{:S(2)}) collective-permute-start(bf16[104,1024]{1,0:T(8,128)(2,1)S(1)} %collective-permute-done.2.tail_ref), channel_id=1, source_target_pairs={{4,9},{5,8},{6,11},{7,10},{8,13},{9,12},{10,15},{11,14},{20,25},{2... | collective-permute-start | bytes 638984 | tf_op jit(solution)/shard_map/ppermute | solution.py:284
  22.3 5.2 %collective-permute-start.9 = (f32[1,256]{1,0:T(1,128)S(1)}, f32[1,256]{1,0:T(1,128)S(1)}, u32[]{:S(2)}, u32[]{:S(2)}) collective-permute-start(f32[1,256]{1,0:T(1,128)S(1)} %get-tuple-element.38), channel_id=1, source_target_pairs={{4,0},{5,1},{6,2},{7,3},{8,4},{9,5},{10,6},{11,7},{12,8},{13,9},{1... | collective-permute-start | bytes 3080 | tf_op jit(solution)/shard_map/ppermute | solution.py:284
  27.6 6.1 %collective-permute-start.10 = (f32[1,256]{1,0:T(1,128)S(1)}, f32[1,256]{1,0:T(1,128)S(1)}, u32[]{:S(2)}, u32[]{:S(2)}) collective-permute-start(f32[1,256]{1,0:T(1,128)S(1)} %get-tuple-element.41), channel_id=1, source_target_pairs={{8,1},{9,0},{10,3},{11,2},{12,5},{13,4},{14,7},{15,6},{24,17},{25,... | collective-permute-start | bytes 3080 | tf_op jit(solution)/shard_map/ppermute | solution.py:284
  28.8 4.8 %collective-permute-start.11 = (f32[1,256]{1,0:T(1,128)S(1)}, f32[1,256]{1,0:T(1,128)S(1)}, u32[]{:S(2)}, u32[]{:S(2)}) collective-permute-start(f32[1,256]{1,0:T(1,128)S(1)} %get-tuple-element.42), channel_id=1, source_target_pairs={{0,2},{1,3},{2,0},{3,1},{4,6},{5,7},{6,4},{7,5},{8,10},{9,11},{10,... | collective-permute-start | bytes 3080 | tf_op jit(solution)/shard_map/ppermute | solution.py:280
  30.4 3.2 %collective-permute-start.12 = (f32[1,256]{1,0:T(1,128)S(1)}, f32[1,256]{1,0:T(1,128)S(1)}, u32[]{:S(2)}, u32[]{:S(2)}) collective-permute-start(f32[1,256]{1,0:T(1,128)S(1)} %get-tuple-element.43), channel_id=1, source_target_pairs={{0,3},{1,2},{2,1},{3,0},{4,7},{5,6},{6,5},{7,4},{8,11},{9,10},{10,... | collective-permute-start | bytes 3080 | tf_op jit(solution)/shard_map/ppermute | solution.py:280
  30.4 3.2 %collective-permute-start.13 = (f32[1,256]{1,0:T(1,128)S(1)}, f32[1,256]{1,0:T(1,128)S(1)}, u32[]{:S(2)}, u32[]{:S(2)}) collective-permute-start(f32[1,256]{1,0:T(1,128)S(1)} %get-tuple-element.44), channel_id=1, source_target_pairs={{0,1},{1,0},{2,3},{3,2},{4,5},{5,4},{6,7},{7,6},{8,9},{9,8},{10,11... | collective-permute-start | bytes 3080 | tf_op jit(solution)/shard_map/ppermute | solution.py:280

commit v35 on v29

--- a/solution.py
+++ b/solution.py
@@ -80,7 +80,6 @@
 
 LANES = 128
 PLANE = 4
-INVERSE_TEMP_BITS = 20.0 * 1.4426950408889634
 ID_ROWS = 8
 VMEM_BYTES = 16 * 1024 * 1024
 
@@ -109,7 +108,7 @@
         query_pos = lax.broadcasted_iota(jnp.int32, similar.shape, 0) + shift
         key_pos = lax.broadcasted_iota(jnp.int32, similar.shape, 1)
         mates = mates & (query_pos != key_pos)
-    return jnp.where(mates, jnp.exp2(similar * INVERSE_TEMP_BITS), 0.0)
+    return jnp.where(mates, jnp.exp(similar * inverse_temp), 0.0)
 
 
 def unit_rows(raw):
@@ -208,7 +207,7 @@
                 query_ref[:size, :], units[:keys], (((1,), (1,)), ((), ())),
                 preferred_element_type=jnp.float32,
             )
-            powers_ref[pl.ds(first, size), :] = jnp.exp2(similar * INVERSE_TEMP_BITS)
+            powers_ref[pl.ds(first, size), :] = jnp.exp(similar * inverse_temp)
             first += size
 
 
@@ -232,7 +231,7 @@
                 query_ref[:size, :], key_rows, (((1,), (1,)), ((), ())),
                 preferred_element_type=jnp.float32,
             )
-            powers = jnp.exp2(similar * INVERSE_TEMP_BITS)
+            powers = jnp.exp(similar * inverse_temp)
             late, column = add_masses(query_ids, key_ids[:, cut:], powers)
             late_column = late_column + column
             early, column = add_masses(query_ids, key_ids[:, :cut], powers_ref[part, :])
@@ -292,7 +291,6 @@
     own_mass = pl.pallas_call(
         own_kernel, out_shape=vector, cost_estimate=small, compiler_params=params
     )(block)
-    own_mass, tail = lax.optimization_barrier((own_mass, tail))
     first_tail = on_line(tail, first_moves, 0)
     across = [in_plane(piece, 2) for piece in pieces]
     sibling = in_plane(block, 1)

time: 34.3 us -> 34.3 us (level)
    ppermute x8, waiting for transfers between devices: 3.87 us -> 3.51 us  [in_plane(): return lax.ppermute(value, 'gx', [(i, i ^ step) for i in range(peers)])]
where the time goes in v35:
time: 34.3 us; the launch traced here: 34.1 us
  waiting for transfers between devices  15.4 us (45%)
  starting transfers between devices  14.2 us (41%)
  Pallas kernels  2.82 us (8%)
  local copies, waits for them, and re-layouts  1.08 us (3%)
  other arithmetic  0.58 us (2%)
    ppermute x6, waiting for transfers between devices, on_line(): return lax.ppermute(value, 'gx', pairs)  11.9 us
    ppermute x6, starting transfers between devices, on_line(): return lax.ppermute(value, 'gx', pairs)  9.72 us
    ppermute x8, starting transfers between devices, in_plane(): return lax.ppermute(value, 'gx', [(i, i ^ step) for i in range(peers)])  4.45 us
    ppermute x8, waiting for transfers between devices, in_plane(): return lax.ppermute(value, 'gx', [(i, i ^ step) for i in range(peers)])  3.51 us
    pallas_call x1, Pallas kernels, grid_plan(): pl.pallas_call(functools.partial(first_kernel, first_moves), out_shape=(l...  2.03 us
    slice x1, local copies, waits for them, and re-layouts, grid_plan(): first_head = on_line(embeddings[:part], first_moves, 0)  1.07 us
  transfers between devices with their start and end apart: 14, of which 7 were waited for; matrix products, arithmetic and copies ran while one was open for 0% of the time, Pallas kernels for 8%

profile of v35, /device:TPU:0, one launch (start us, length us, event | category | flops | bytes accessed | tf_op | source)
XLA Modules:
  0.0 34.1 jit_solution(12868413842805622961)
XLA Ops:
  0.0 0.0 copy-start
  0.0 1.1 %slice.3 = bf16[160,1024]{1,0:T(8,128)(2,1)S(1)} slice(bf16[256,1024]{1,0:T(8,128)(2,1)} %rows_ref.1), slice={[0:160], [0:1024]} | slice | bytes 655360 | tf_op jit(solution)/shard_map/slice | solution.py:284
  1.1 0.0 copy-start.1
  1.1 3.1 %collective-permute-start = (bf16[160,1024]{1,0:T(8,128)(2,1)S(1)}, bf16[160,1024]{1,0:T(8,128)(2,1)S(1)}, u32[]{:S(2)}, u32[]{:S(2)}) collective-permute-start(bf16[160,1024]{1,0:T(8,128)(2,1)S(1)} %slice.3), channel_id=1, source_target_pairs={{0,4},{1,5},{2,6},{3,7},{4,8},{5,9},{6,10},{7,11},{8,12},{9,13},{1... | collective-permute-start | bytes 983048 | tf_op jit(solution)/shard_map/ppermute | solution.py:273
  4.2 0.0 copy-done
  4.2 0.0 copy-done.1
  4.2 0.2 shard_map.28
  4.4 1.6 %collective-permute-start.4 = (bf16[136,1024]{1,0:T(8,128)(2,1)S(1)}, bf16[136,1024]{1,0:T(8,128)(2,1)S(1)}, u32[]{:S(2)}, u32[]{:S(2)}) collective-permute-start(bf16[136,1024]{1,0:T(8,128)(2,1)S(1)} %get-tuple-element.25), channel_id=1, source_target_pairs={{0,2},{1,3},{2,0},{3,1},{4,6},{5,7},{6,4},{7,5},{8,10},{9,11},{10,... | collective-permute-start | bytes 835592 | tf_op jit(solution)/shard_map/ppermute | solution.py:269
  5.9 0.0 collective-permute-start.2
  5.9 0.5 %collective-permute-start.3 = (bf16[128,1024]{1,0:T(8,128)(2,1)S(1)}, bf16[128,1024]{1,0:T(8,128)(2,1)S(1)}, u32[]{:S(2)}, u32[]{:S(2)}) collective-permute-start(bf16[128,1024]{1,0:T(8,128)(2,1)S(1)} %get-tuple-element.24), channel_id=1, source_target_pairs={{0,2},{1,3},{2,0},{3,1},{4,6},{5,7},{6,4},{7,5},{8,10},{9,11},{10,... | collective-permute-start | bytes 786440 | tf_op jit(solution)/shard_map/ppermute | solution.py:269
  6.5 1.6 %collective-permute-start.7 = (bf16[104,1024]{1,0:T(8,128)(2,1)S(1)}, bf16[104,1024]{1,0:T(8,128)(2,1)S(1)}, u32[]{:S(2)}, u32[]{:S(2)}) collective-permute-start(bf16[104,1024]{1,0:T(8,128)(2,1)S(1)} %get-tuple-element.28), channel_id=1, source_target_pairs={{0,4},{1,5},{2,6},{3,7},{4,8},{5,9},{6,10},{7,11},{8,12},{9,13},{1... | collective-permute-start | bytes 638984 | tf_op jit(solution)/shard_map/ppermute | solution.py:273
  8.0 6.7 %collective-permute-done.head_ref = bf16[160,1024]{1,0:T(8,128)(2,1)S(1)} collective-permute-done((bf16[160,1024]{1,0:T(8,128)(2,1)S(1)}, bf16[160,1024]{1,0:T(8,128)(2,1)S(1)}, u32[]{:S(2)}, u32[]{:S(2)}) %collective-permute-start) | collective-permute-done | bytes 327712 | tf_op jit(solution)/shard_map/ppermute | solution.py:273
  14.7 0.0 collective-permute-start.1
  14.7 0.0 collective-permute-done.4.refs_3_
  14.7 0.1 collective-permute-start.6
  14.9 3.3 %collective-permute-done.3.refs_2_ = bf16[128,1024]{1,0:T(8,128)(2,1)S(1)} collective-permute-done((bf16[128,1024]{1,0:T(8,128)(2,1)S(1)}, bf16[128,1024]{1,0:T(8,128)(2,1)S(1)}, u32[]{:S(2)}, u32[]{:S(2)}) %collective-permute-start.3) | collective-permute-done | bytes 262176 | tf_op jit(solution)/shard_map/ppermute | solution.py:269
  18.2 0.0 collective-permute-start.5
  18.2 0.3 collective-permute-done.7.tail_ref
  18.5 0.7 %collective-permute-start.8 = (bf16[104,1024]{1,0:T(8,128)(2,1)S(1)}, bf16[104,1024]{1,0:T(8,128)(2,1)S(1)}, u32[]{:S(2)}, u32[]{:S(2)}) collective-permute-start(bf16[104,1024]{1,0:T(8,128)(2,1)S(1)} %collective-permute-done.7.tail_ref), channel_id=1, source_target_pairs={{4,9},{5,8},{6,11},{7,10},{8,13},{9,12},{10,15},{11,14},{20,25},{2... | collective-permute-start | bytes 638984 | tf_op jit(solution)/shard_map/ppermute | solution.py:273
  19.1 0.4 %shard_map.30.own_mass_ref = f32[1,256]{1,0:T(1,128)S(1)} custom-call(bf16[264,1024]{1,0:T(8,128)(2,1)S(1)} %get-tuple-element.23.refs_0_.own_ref), custom_call_target="tpu_custom_call" | custom-call | flops 1 | bytes 1 | tf_op jit(solution)/shard_map/pallas_call | solution.py:291
  19.5 0.2 collective-permute-done.5.refs_4_
  19.7 0.0 collective-permute-done.2.refs_1_
  19.7 0.0 collective-permute-done.6.refs_5_
  19.7 2.0 %shard_map.31 = (f32[1024,128]{1,0:T(8,128)S(1)}, f32[1,256]{1,0:T(1,128)S(1)}, f32[1024,128]{1,0:T(8,128)S(1)}, f32[1,256]{1,0:T(1,128)S(1)}) custom-call(f32[1,256]{1,0:T(1,128)S(1)} %shard_map.30.own_mass_ref, bf16[160,1024]{1,0:T(8,128)(2,1)S(1)} %collective-permute-done.head_ref, bf16[104,1024]{1,0:T(8,128)(2,1)S(1)} %collective-permute-done.7.tail_ref, ...), custom_call_target="tpu_custom_call" | custom-call | flops 1 | bytes 1 | tf_op jit(solution)/shard_map/pallas_call | solution.py:301
  21.7 3.1 %collective-permute-start.9 = (f32[1,256]{1,0:T(1,128)S(1)}, f32[1,256]{1,0:T(1,128)S(1)}, u32[]{:S(2)}, u32[]{:S(2)}) collective-permute-start(f32[1,256]{1,0:T(1,128)S(1)} %get-tuple-element.34), channel_id=1, source_target_pairs={{4,0},{5,1},{6,2},{7,3},{8,4},{9,5},{10,6},{11,7},{12,8},{13,9},{1... | collective-permute-start | bytes 3080 | tf_op jit(solution)/shard_map/ppermute | solution.py:273
  24.9 0.6 %collective-permute-done.1.head_ref = bf16[160,1024]{1,0:T(8,128)(2,1)S(1)} collective-permute-done((bf16[160,1024]{1,0:T(8,128)(2,1)S(1)}, bf16[160,1024]{1,0:T(8,128)(2,1)S(1)}, u32[]{:S(2)}, u32[]{:S(2)}) %collective-permute-start.1) | collective-permute-done | bytes 327712 | tf_op jit(solution)/shard_map/ppermute | solution.py:273
  25.5 0.0 collective-permute-done.8.tail_ref
  25.5 1.8 %collective-permute-done.9 = f32[1,256]{1,0:T(1,128)S(1)} collective-permute-done((f32[1,256]{1,0:T(1,128)S(1)}, f32[1,256]{1,0:T(1,128)S(1)}, u32[]{:S(2)}, u32[]{:S(2)}) %collective-permute-start.9) | collective-permute-done | bytes 1056 | tf_op jit(solution)/shard_map/ppermute | solution.py:273
  27.4 1.3 %collective-permute-start.10 = (f32[1,256]{1,0:T(1,128)S(1)}, f32[1,256]{1,0:T(1,128)S(1)}, u32[]{:S(2)}, u32[]{:S(2)}) collective-permute-start(f32[1,256]{1,0:T(1,128)S(1)} %get-tuple-element.37), channel_id=1, source_target_pairs={{8,1},{9,0},{10,3},{11,2},{12,5},{13,4},{14,7},{15,6},{24,17},{25,... | collective-permute-start | bytes 3080 | tf_op jit(solution)/shard_map/ppermute | solution.py:273
  28.7 0.2 shard_map.33
  28.9 1.6 %collective-permute-start.11 = (f32[1,256]{1,0:T(1,128)S(1)}, f32[1,256]{1,0:T(1,128)S(1)}, u32[]{:S(2)}, u32[]{:S(2)}) collective-permute-start(f32[1,256]{1,0:T(1,128)S(1)} %get-tuple-element.38), channel_id=1, source_target_pairs={{0,2},{1,3},{2,0},{3,1},{4,6},{5,7},{6,4},{7,5},{8,10},{9,11},{10,... | collective-permute-start | bytes 3080 | tf_op jit(solution)/shard_map/ppermute | solution.py:269
  30.4 0.0 collective-permute-start.12
  30.4 0.6 %collective-permute-start.13 = (f32[1,256]{1,0:T(1,128)S(1)}, f32[1,256]{1,0:T(1,128)S(1)}, u32[]{:S(2)}, u32[]{:S(2)}) collective-permute-start(f32[1,256]{1,0:T(1,128)S(1)} %get-tuple-element.40), channel_id=1, source_target_pairs={{0,1},{1,0},{2,3},{3,2},{4,5},{5,4},{6,7},{7,6},{8,9},{9,8},{10,11... | collective-permute-start | bytes 3080 | tf_op jit(solution)/shard_map/ppermute | solution.py:269
  31.1 2.5 %collective-permute-done.10 = f32[1,256]{1,0:T(1,128)S(1)} collective-permute-done((f32[1,256]{1,0:T(1,128)S(1)}, f32[1,256]{1,0:T(1,128)S(1)}, u32[]{:S(2)}, u32[]{:S(2)}) %collective-permute-start.10) | collective-permute-done | bytes 1056 | tf_op jit(solution)/shard_map/ppermute | solution.py:273
  33.5 0.0 collective-permute-done.11
  33.5 0.0 collective-permute-done.12
  33.6 0.0 collective-permute-done.13
  33.6 0.6 %add_log-plus-one_fusion = f32[1,256]{1,0:T(1,128)} fusion(f32[1,256]{1,0:T(1,128)S(1)} %collective-permute-done.13, f32[1,256]{1,0:T(1,128)S(1)} %collective-permute-done.12, f32[1,256]{1,0:T(1,128)S(1)} %collective-permute-done.11, f32[1,256]{1,0:T(1,128)S(1)} %collective-permute-done.10, f32[1,256]{1,0:T(1,128)S(1)} %get-tuple-element.33, ...), kind=kLoop, calls=%fused_computation | loop fusion | flops 1280 | bytes 7168 | tf_op jit(solution)/shard_map/log1p | solution.py:331
  (2 shorter events, 0.0 us)
Async XLA Ops:
  0.0 4.2 %copy-start = (bf16[256,1024]{1,0:T(8,128)(2,1)S(1)}, bf16[256,1024]{1,0:T(8,128)(2,1)}, u32[]{:S(2)}) copy-start(bf16[256,1024]{1,0:T(8,128)(2,1)} %rows_ref.1) | copy-start | bytes 1572868
  1.1 3.1 %copy-start.1 = (s32[256]{0:T(256)S(1)}, s32[256]{0:T(256)}, u32[]{:S(2)}) copy-start(s32[256]{0:T(256)} %param.3) | copy-start | bytes 3076
  1.1 13.6 %collective-permute-start = (bf16[160,1024]{1,0:T(8,128)(2,1)S(1)}, bf16[160,1024]{1,0:T(8,128)(2,1)S(1)}, u32[]{:S(2)}, u32[]{:S(2)}) collective-permute-start(bf16[160,1024]{1,0:T(8,128)(2,1)S(1)} %slice.3), channel_id=1, source_target_pairs={{0,4},{1,5},{2,6},{3,7},{4,8},{5,9},{6,10},{7,11},{8,12},{9,13},{1... | collective-permute-start | bytes 983048 | tf_op jit(solution)/shard_map/ppermute | solution.py:273
  4.4 10.4 %collective-permute-start.4 = (bf16[136,1024]{1,0:T(8,128)(2,1)S(1)}, bf16[136,1024]{1,0:T(8,128)(2,1)S(1)}, u32[]{:S(2)}, u32[]{:S(2)}) collective-permute-start(bf16[136,1024]{1,0:T(8,128)(2,1)S(1)} %get-tuple-element.25), channel_id=1, source_target_pairs={{0,2},{1,3},{2,0},{3,1},{4,6},{5,7},{6,4},{7,5},{8,10},{9,11},{10,... | collective-permute-start | bytes 835592 | tf_op jit(solution)/shard_map/ppermute | solution.py:269
  5.9 13.8 %collective-permute-start.2 = (bf16[264,1024]{1,0:T(8,128)(2,1)S(1)}, bf16[264,1024]{1,0:T(8,128)(2,1)S(1)}, u32[]{:S(2)}, u32[]{:S(2)}) collective-permute-start(bf16[264,1024]{1,0:T(8,128)(2,1)S(1)} %get-tuple-element.23.refs_0_.own_ref), channel_id=1, source_target_pairs={{0,1},{1,0},{2,3},{3,2},{4,5},{5,4},{6,7},{7,6},{8,9},{9,8},{10,11... | collective-permute-start | bytes 1622024 | tf_op jit(solution)/shard_map/ppermute | solution.py:269
  5.9 12.2 %collective-permute-start.3 = (bf16[128,1024]{1,0:T(8,128)(2,1)S(1)}, bf16[128,1024]{1,0:T(8,128)(2,1)S(1)}, u32[]{:S(2)}, u32[]{:S(2)}) collective-permute-start(bf16[128,1024]{1,0:T(8,128)(2,1)S(1)} %get-tuple-element.24), channel_id=1, source_target_pairs={{0,2},{1,3},{2,0},{3,1},{4,6},{5,7},{6,4},{7,5},{8,10},{9,11},{10,... | collective-permute-start | bytes 786440 | tf_op jit(solution)/shard_map/ppermute | solution.py:269
  6.5 12.0 %collective-permute-start.7 = (bf16[104,1024]{1,0:T(8,128)(2,1)S(1)}, bf16[104,1024]{1,0:T(8,128)(2,1)S(1)}, u32[]{:S(2)}, u32[]{:S(2)}) collective-permute-start(bf16[104,1024]{1,0:T(8,128)(2,1)S(1)} %get-tuple-element.28), channel_id=1, source_target_pairs={{0,4},{1,5},{2,6},{3,7},{4,8},{5,9},{6,10},{7,11},{8,12},{9,13},{1... | collective-permute-start | bytes 638984 | tf_op jit(solution)/shard_map/ppermute | solution.py:273
  14.7 10.8 %collective-permute-start.1 = (bf16[160,1024]{1,0:T(8,128)(2,1)S(1)}, bf16[160,1024]{1,0:T(8,128)(2,1)S(1)}, u32[]{:S(2)}, u32[]{:S(2)}) collective-permute-start(bf16[160,1024]{1,0:T(8,128)(2,1)S(1)} %collective-permute-done.head_ref), channel_id=1, source_target_pairs={{0,5},{1,4},{2,7},{3,6},{4,9},{5,8},{6,11},{7,10},{8,13},{9,12},{1... | collective-permute-start | bytes 983048 | tf_op jit(solution)/shard_map/ppermute | solution.py:273
  14.7 5.0 %collective-permute-start.6 = (bf16[136,1024]{1,0:T(8,128)(2,1)S(1)}, bf16[136,1024]{1,0:T(8,128)(2,1)S(1)}, u32[]{:S(2)}, u32[]{:S(2)}) collective-permute-start(bf16[136,1024]{1,0:T(8,128)(2,1)S(1)} %collective-permute-done.4.refs_3_), channel_id=1, source_target_pairs={{0,1},{1,0},{2,3},{3,2},{4,5},{5,4},{6,7},{7,6},{8,9},{9,8},{10,11... | collective-permute-start | bytes 835592 | tf_op jit(solution)/shard_map/ppermute | solution.py:269
  18.2 1.5 %collective-permute-start.5 = (bf16[128,1024]{1,0:T(8,128)(2,1)S(1)}, bf16[128,1024]{1,0:T(8,128)(2,1)S(1)}, u32[]{:S(2)}, u32[]{:S(2)}) collective-permute-start(bf16[128,1024]{1,0:T(8,128)(2,1)S(1)} %collective-permute-done.3.refs_2_), channel_id=1, source_target_pairs={{0,1},{1,0},{2,3},{3,2},{4,5},{5,4},{6,7},{7,6},{8,9},{9,8},{10,11... | collective-permute-start | bytes 786440 | tf_op jit(solution)/shard_map/ppermute | solution.py:269
  18.5 7.0 %collective-permute-start.8 = (bf16[104,1024]{1,0:T(8,128)(2,1)S(1)}, bf16[104,1024]{1,0:T(8,128)(2,1)S(1)}, u32[]{:S(2)}, u32[]{:S(2)}) collective-permute-start(bf16[104,1024]{1,0:T(8,128)(2,1)S(1)} %collective-permute-done.7.tail_ref), channel_id=1, source_target_pairs={{4,9},{5,8},{6,11},{7,10},{8,13},{9,12},{10,15},{11,14},{20,25},{2... | collective-permute-start | bytes 638984 | tf_op jit(solution)/shard_map/ppermute | solution.py:273
  21.7 5.6 %collective-permute-start.9 = (f32[1,256]{1,0:T(1,128)S(1)}, f32[1,256]{1,0:T(1,128)S(1)}, u32[]{:S(2)}, u32[]{:S(2)}) collective-permute-start(f32[1,256]{1,0:T(1,128)S(1)} %get-tuple-element.34), channel_id=1, source_target_pairs={{4,0},{5,1},{6,2},{7,3},{8,4},{9,5},{10,6},{11,7},{12,8},{13,9},{1... | collective-permute-start | bytes 3080 | tf_op jit(solution)/shard_map/ppermute | solution.py:273
  27.4 6.2 %collective-permute-start.10 = (f32[1,256]{1,0:T(1,128)S(1)}, f32[1,256]{1,0:T(1,128)S(1)}, u32[]{:S(2)}, u32[]{:S(2)}) collective-permute-start(f32[1,256]{1,0:T(1,128)S(1)} %get-tuple-element.37), channel_id=1, source_target_pairs={{8,1},{9,0},{10,3},{11,2},{12,5},{13,4},{14,7},{15,6},{24,17},{25,... | collective-permute-start | bytes 3080 | tf_op jit(solution)/shard_map/ppermute | solution.py:273
  28.9 4.7 %collective-permute-start.11 = (f32[1,256]{1,0:T(1,128)S(1)}, f32[1,256]{1,0:T(1,128)S(1)}, u32[]{:S(2)}, u32[]{:S(2)}) collective-permute-start(f32[1,256]{1,0:T(1,128)S(1)} %get-tuple-element.38), channel_id=1, source_target_pairs={{0,2},{1,3},{2,0},{3,1},{4,6},{5,7},{6,4},{7,5},{8,10},{9,11},{10,... | collective-permute-start | bytes 3080 | tf_op jit(solution)/shard_map/ppermute | solution.py:269
  30.4 3.1 %collective-permute-start.12 = (f32[1,256]{1,0:T(1,128)S(1)}, f32[1,256]{1,0:T(1,128)S(1)}, u32[]{:S(2)}, u32[]{:S(2)}) collective-permute-start(f32[1,256]{1,0:T(1,128)S(1)} %get-tuple-element.39), channel_id=1, source_target_pairs={{0,3},{1,2},{2,1},{3,0},{4,7},{5,6},{6,5},{7,4},{8,11},{9,10},{10,... | collective-permute-start | bytes 3080 | tf_op jit(solution)/shard_map/ppermute | solution.py:269
  30.4 3.1 %collective-permute-start.13 = (f32[1,256]{1,0:T(1,128)S(1)}, f32[1,256]{1,0:T(1,128)S(1)}, u32[]{:S(2)}, u32[]{:S(2)}) collective-permute-start(f32[1,256]{1,0:T(1,128)S(1)} %get-tuple-element.40), channel_id=1, source_target_pairs={{0,1},{1,0},{2,3},{3,2},{4,5},{5,4},{6,7},{7,6},{8,9},{9,8},{10,11... | collective-permute-start | bytes 3080 | tf_op jit(solution)/shard_map/ppermute | solution.py:269

commit v36 on v35

--- a/solution.py
+++ b/solution.py
@@ -171,9 +171,13 @@
     mass_ref[...] = jnp.sum(masses, axis=0, keepdims=True)
 
 
+def folded_rows(sums_ref, m, rows):
+    return jnp.sum(sums_ref[pl.ds(m * rows, rows), :].T, axis=0, keepdims=True)
+
+
 def first_kernel(moves, own_mass_ref, head_ref, tail_ref, *refs):
     query_refs, (ids_ref, column_ref, sums_ref, mass_ref) = refs[:-4], refs[-4:]
-    rows = mass_ref.shape[1]
+    rows = mass_ref.shape[1] // PLANE
     query_parts = query_parts_of(query_refs, rows)
     own_ref = query_refs[0]
     own_ids = ids_of(own_ref)[:, :rows]
@@ -186,11 +190,13 @@
         masses = mate_mass(ref[:size, :], query_ids, own_ref[:rows, :], own_ids)
         mass = mass + jnp.sum(masses, axis=0, keepdims=True)
         first += size
-    mass_ref[...] = mass
     tail = tail_ref[: rows - head_ref.shape[0], :]
     key_rows = jnp.concatenate([unit_rows(head_ref[...]), tail], axis=0)
     key_ids = ids_of(tail_ref)[:, :rows]
     column_ref[...] = add_line(query_parts, ids_ref, key_rows, key_ids, None, sums_ref)
+    for m in range(PLANE):
+        row_sum = folded_rows(sums_ref, m, rows)
+        mass_ref[:, m * rows : (m + 1) * rows] = row_sum + mass if m == 0 else row_sum
 
 
 def middle_kernel(moves, head_ref, *refs):
@@ -211,7 +217,7 @@
             first += size
 
 
-def last_kernel(moves, powers_ref, rest_ref, tail_ref, ids_ref, earlier_ref, *refs):
+def last_kernel(moves, powers_ref, rest_ref, tail_ref, ids_ref, *refs):
     query_refs, (column_ref, sums_ref) = refs[:-2], refs[-2:]
     rows = column_ref.shape[1]
     cut = powers_ref.shape[1]
@@ -236,21 +242,20 @@
             late_column = late_column + column
             early, column = add_masses(query_ids, key_ids[:, :cut], powers_ref[part, :])
             early_column = early_column + column
-            sums_ref[part, :] = earlier_ref[part, :] + early + late
+            sums_ref[part, :] = early + late
             first += size
         column_ref[...] = jnp.concatenate([early_column, late_column], axis=1)
 
     @pl.when(jnp.logical_not(arrived))
     def _():
         column_ref[...] = jnp.zeros_like(column_ref)
-        sums_ref[...] = earlier_ref[...]
-
-
-def fold_kernel(sums_ref, mass_ref, *row_refs):
-    rows = mass_ref.shape[1]
+        sums_ref[...] = jnp.zeros_like(sums_ref)
+
+
+def fold_kernel(sums_ref, row_ref, *row_refs):
+    rows = row_refs[0].shape[1]
     for m in range(PLANE):
-        row_sum = jnp.sum(sums_ref[pl.ds(m * rows, rows), :].T, axis=0, keepdims=True)
-        row_refs[m][...] = row_sum + mass_ref[...] if m == 0 else row_sum
+        row_refs[m][...] = row_ref[:, m * rows : (m + 1) * rows] + folded_rows(sums_ref, m, rows)
 
 
 def grid_plan(embeddings, cluster_ids):
@@ -298,9 +303,11 @@
     last_tail = on_line(first_tail, forward_moves, 1)
     corner = [in_plane(piece, 1) for piece in across]
     queries = (block, sibling, *across, *corner)
-    ids, first_column, first_sums, mass = pl.pallas_call(
+    ids, first_column, _, rows_before = pl.pallas_call(
         functools.partial(first_kernel, first_moves),
-        out_shape=(lanes, vector, lanes, vector),
+        out_shape=(
+            lanes, vector, lanes, jax.ShapeDtypeStruct((1, plane_rows), jnp.float32)
+        ),
         cost_estimate=small,
         compiler_params=params,
     )(own_mass, first_head, first_tail, *queries)
@@ -308,7 +315,8 @@
     powers, rest = pl.pallas_call(
         functools.partial(middle_kernel, last_moves),
         out_shape=(
-            jax.ShapeDtypeStruct((plane_rows, half), jnp.float32), rows_of(part - half)
+            jax.ShapeDtypeStruct((plane_rows, half), jnp.float32),
+            rows_of(part - half),
         ),
         cost_estimate=small,
         compiler_params=params,
@@ -318,14 +326,14 @@
         out_shape=(vector, lanes),
         cost_estimate=small,
         compiler_params=params,
-    )(powers, rest, last_tail, ids, first_sums, *queries)
+    )(powers, rest, last_tail, ids, *queries)
     returned_first, last_column = lax.optimization_barrier((returned_first, last_column))
     row_sums = pl.pallas_call(
         fold_kernel,
         out_shape=[vector] * PLANE,
         cost_estimate=small,
         compiler_params=params,
-    )(sums, mass)
+    )(sums, rows_before)
     returned = [on_line(last_column, last_back, 1)]
     returned += [in_plane(row_sums[step], step) for step in (2, 3, 1)]
     return jnp.log1p(sum(returned, row_sums[0] + returned_first)).reshape(row_count)

time: 34.3 us -> 34.9 us (1.017)
  Pallas kernels: 2.82 us -> 3.62 us
    pallas_call x1, Pallas kernels: 2.03 us -> 2.83 us  [grid_plan(): pl.pallas_call(functools.partial(first_kernel, first_moves), out_shape=(l...]
    ppermute x6, waiting for transfers between devices: 11.9 us -> 11.5 us  [on_line(): return lax.ppermute(value, 'gx', pairs)]
  transfers between devices with their start and end apart: 14 -> 14, of which waited for: 7 -> 7; matrix products, arithmetic and copies ran while one was open for 0% -> 0% of each run, Pallas kernels for 8% -> 10%
where the time goes in v36:
time: 34.9 us; the launch traced here: 34.7 us
  waiting for transfers between devices  15.3 us (44%)
  starting transfers between devices  14.1 us (40%)
  Pallas kernels  3.62 us (10%)
  local copies, waits for them, and re-layouts  1.08 us (3%)
  other arithmetic  0.58 us (2%)
    ppermute x6, waiting for transfers between devices, on_line(): return lax.ppermute(value, 'gx', pairs)  11.5 us
    ppermute x6, starting transfers between devices, on_line(): return lax.ppermute(value, 'gx', pairs)  9.67 us
    ppermute x8, starting transfers between devices, in_plane(): return lax.ppermute(value, 'gx', [(i, i ^ step) for i in range(peers)])  4.45 us
    ppermute x8, waiting for transfers between devices, in_plane(): return lax.ppermute(value, 'gx', [(i, i ^ step) for i in range(peers)])  3.79 us
    pallas_call x1, Pallas kernels, grid_plan(): pl.pallas_call(functools.partial(first_kernel, first_moves), out_shape=(l...  2.83 us
    slice x1, local copies, waits for them, and re-layouts, grid_plan(): first_head = on_line(embeddings[:part], first_moves, 0)  1.07 us
  transfers between devices with their start and end apart: 14, of which 7 were waited for; matrix products, arithmetic and copies ran while one was open for 0% of the time, Pallas kernels for 10%

profile of v36, /device:TPU:0, one launch (start us, length us, event | category | flops | bytes accessed | tf_op | source)
XLA Modules:
  0.0 34.7 jit_solution(4831001181712499392)
XLA Ops:
  0.0 0.0 copy-start
  0.0 1.1 %slice.3 = bf16[160,1024]{1,0:T(8,128)(2,1)S(1)} slice(bf16[256,1024]{1,0:T(8,128)(2,1)} %rows_ref.1), slice={[0:160], [0:1024]} | slice | bytes 655360 | tf_op jit(solution)/shard_map/slice | solution.py:289
  1.1 0.0 copy-start.1
  1.1 3.1 %collective-permute-start = (bf16[160,1024]{1,0:T(8,128)(2,1)S(1)}, bf16[160,1024]{1,0:T(8,128)(2,1)S(1)}, u32[]{:S(2)}, u32[]{:S(2)}) collective-permute-start(bf16[160,1024]{1,0:T(8,128)(2,1)S(1)} %slice.3), channel_id=1, source_target_pairs={{0,4},{1,5},{2,6},{3,7},{4,8},{5,9},{6,10},{7,11},{8,12},{9,13},{1... | collective-permute-start | bytes 983048 | tf_op jit(solution)/shard_map/ppermute | solution.py:278
  4.2 0.0 copy-done
  4.2 0.0 copy-done.1
  4.2 0.2 shard_map.28
  4.4 1.6 %collective-permute-start.4 = (bf16[136,1024]{1,0:T(8,128)(2,1)S(1)}, bf16[136,1024]{1,0:T(8,128)(2,1)S(1)}, u32[]{:S(2)}, u32[]{:S(2)}) collective-permute-start(bf16[136,1024]{1,0:T(8,128)(2,1)S(1)} %get-tuple-element.24), channel_id=1, source_target_pairs={{0,2},{1,3},{2,0},{3,1},{4,6},{5,7},{6,4},{7,5},{8,10},{9,11},{10,... | collective-permute-start | bytes 835592 | tf_op jit(solution)/shard_map/ppermute | solution.py:274
  5.9 0.0 collective-permute-start.2
  5.9 0.5 %collective-permute-start.3 = (bf16[128,1024]{1,0:T(8,128)(2,1)S(1)}, bf16[128,1024]{1,0:T(8,128)(2,1)S(1)}, u32[]{:S(2)}, u32[]{:S(2)}) collective-permute-start(bf16[128,1024]{1,0:T(8,128)(2,1)S(1)} %get-tuple-element.23), channel_id=1, source_target_pairs={{0,2},{1,3},{2,0},{3,1},{4,6},{5,7},{6,4},{7,5},{8,10},{9,11},{10,... | collective-permute-start | bytes 786440 | tf_op jit(solution)/shard_map/ppermute | solution.py:274
  6.5 1.6 %collective-permute-start.7 = (bf16[104,1024]{1,0:T(8,128)(2,1)S(1)}, bf16[104,1024]{1,0:T(8,128)(2,1)S(1)}, u32[]{:S(2)}, u32[]{:S(2)}) collective-permute-start(bf16[104,1024]{1,0:T(8,128)(2,1)S(1)} %get-tuple-element.27), channel_id=1, source_target_pairs={{0,4},{1,5},{2,6},{3,7},{4,8},{5,9},{6,10},{7,11},{8,12},{9,13},{1... | collective-permute-start | bytes 638984 | tf_op jit(solution)/shard_map/ppermute | solution.py:278
  8.0 6.7 %collective-permute-done.head_ref = bf16[160,1024]{1,0:T(8,128)(2,1)S(1)} collective-permute-done((bf16[160,1024]{1,0:T(8,128)(2,1)S(1)}, bf16[160,1024]{1,0:T(8,128)(2,1)S(1)}, u32[]{:S(2)}, u32[]{:S(2)}) %collective-permute-start) | collective-permute-done | bytes 327712 | tf_op jit(solution)/shard_map/ppermute | solution.py:278
  14.7 0.0 collective-permute-start.1
  14.7 0.0 collective-permute-done.4.refs_3_
  14.7 0.1 collective-permute-start.6
  14.9 3.3 %collective-permute-done.3.refs_2_ = bf16[128,1024]{1,0:T(8,128)(2,1)S(1)} collective-permute-done((bf16[128,1024]{1,0:T(8,128)(2,1)S(1)}, bf16[128,1024]{1,0:T(8,128)(2,1)S(1)}, u32[]{:S(2)}, u32[]{:S(2)}) %collective-permute-start.3) | collective-permute-done | bytes 262176 | tf_op jit(solution)/shard_map/ppermute | solution.py:274
  18.2 0.0 collective-permute-start.5
  18.2 0.3 collective-permute-done.7.tail_ref
  18.5 0.7 %collective-permute-start.8 = (bf16[104,1024]{1,0:T(8,128)(2,1)S(1)}, bf16[104,1024]{1,0:T(8,128)(2,1)S(1)}, u32[]{:S(2)}, u32[]{:S(2)}) collective-permute-start(bf16[104,1024]{1,0:T(8,128)(2,1)S(1)} %collective-permute-done.7.tail_ref), channel_id=1, source_target_pairs={{4,9},{5,8},{6,11},{7,10},{8,13},{9,12},{10,15},{11,14},{20,25},{2... | collective-permute-start | bytes 638984 | tf_op jit(solution)/shard_map/ppermute | solution.py:278
  19.1 0.4 %shard_map.30.own_mass_ref = f32[1,256]{1,0:T(1,128)S(1)} custom-call(bf16[264,1024]{1,0:T(8,128)(2,1)S(1)} %get-tuple-element.22.refs_0_.own_ref), custom_call_target="tpu_custom_call" | custom-call | flops 1 | bytes 1 | tf_op jit(solution)/shard_map/pallas_call | solution.py:296
  19.5 0.2 collective-permute-done.5.refs_4_
  19.7 0.0 collective-permute-done.2.refs_1_
  19.7 0.0 collective-permute-done.6.refs_5_
  19.7 2.8 %shard_map.31 = (f32[1024,128]{1,0:T(8,128)S(1)}, f32[1,256]{1,0:T(1,128)S(1)}, f32[1024,128]{1,0:T(8,128)}, f32[1,1024]{1,0:T(1,128)S(1)}) custom-call(f32[1,256]{1,0:T(1,128)S(1)} %shard_map.30.own_mass_ref, bf16[160,1024]{1,0:T(8,128)(2,1)S(1)} %collective-permute-done.head_ref, bf16[104,1024]{1,0:T(8,128)(2,1)S(1)} %collective-permute-done.7.tail_ref, ...), custom_call_target="tpu_custom_call" | custom-call | flops 1 | bytes 1 | tf_op jit(solution)/shard_map/pallas_call | solution.py:306
  22.5 3.1 %collective-permute-start.9 = (f32[1,256]{1,0:T(1,128)S(1)}, f32[1,256]{1,0:T(1,128)S(1)}, u32[]{:S(2)}, u32[]{:S(2)}) collective-permute-start(f32[1,256]{1,0:T(1,128)S(1)} %get-tuple-element.32), channel_id=1, source_target_pairs={{4,0},{5,1},{6,2},{7,3},{8,4},{9,5},{10,6},{11,7},{12,8},{13,9},{1... | collective-permute-start | bytes 3080 | tf_op jit(solution)/shard_map/ppermute | solution.py:278
  25.6 0.0 collective-permute-done.1.head_ref
  25.6 0.0 collective-permute-done.8.tail_ref
  25.7 2.4 %collective-permute-done.9 = f32[1,256]{1,0:T(1,128)S(1)} collective-permute-done((f32[1,256]{1,0:T(1,128)S(1)}, f32[1,256]{1,0:T(1,128)S(1)}, u32[]{:S(2)}, u32[]{:S(2)}) %collective-permute-start.9) | collective-permute-done | bytes 1056 | tf_op jit(solution)/shard_map/ppermute | solution.py:278
  28.1 1.3 %collective-permute-start.10 = (f32[1,256]{1,0:T(1,128)S(1)}, f32[1,256]{1,0:T(1,128)S(1)}, u32[]{:S(2)}, u32[]{:S(2)}) collective-permute-start(f32[1,256]{1,0:T(1,128)S(1)} %get-tuple-element.35), channel_id=1, source_target_pairs={{8,1},{9,0},{10,3},{11,2},{12,5},{13,4},{14,7},{15,6},{24,17},{25,... | collective-permute-start | bytes 3080 | tf_op jit(solution)/shard_map/ppermute | solution.py:278
  29.4 0.2 shard_map.33
  29.6 1.6 %collective-permute-start.11 = (f32[1,256]{1,0:T(1,128)S(1)}, f32[1,256]{1,0:T(1,128)S(1)}, u32[]{:S(2)}, u32[]{:S(2)}) collective-permute-start(f32[1,256]{1,0:T(1,128)S(1)} %get-tuple-element.36), channel_id=1, source_target_pairs={{0,2},{1,3},{2,0},{3,1},{4,6},{5,7},{6,4},{7,5},{8,10},{9,11},{10,... | collective-permute-start | bytes 3080 | tf_op jit(solution)/shard_map/ppermute | solution.py:274
  31.2 0.0 collective-permute-start.12
  31.2 0.6 %collective-permute-start.13 = (f32[1,256]{1,0:T(1,128)S(1)}, f32[1,256]{1,0:T(1,128)S(1)}, u32[]{:S(2)}, u32[]{:S(2)}) collective-permute-start(f32[1,256]{1,0:T(1,128)S(1)} %get-tuple-element.38), channel_id=1, source_target_pairs={{0,1},{1,0},{2,3},{3,2},{4,5},{5,4},{6,7},{7,6},{8,9},{9,8},{10,11... | collective-permute-start | bytes 3080 | tf_op jit(solution)/shard_map/ppermute | solution.py:274
  31.8 2.1 %collective-permute-done.10 = f32[1,256]{1,0:T(1,128)S(1)} collective-permute-done((f32[1,256]{1,0:T(1,128)S(1)}, f32[1,256]{1,0:T(1,128)S(1)}, u32[]{:S(2)}, u32[]{:S(2)}) %collective-permute-start.10) | collective-permute-done | bytes 1056 | tf_op jit(solution)/shard_map/ppermute | solution.py:278
  33.9 0.0 collective-permute-done.11
  33.9 0.3 collective-permute-done.12
  34.2 0.0 collective-permute-done.13
  34.2 0.6 %add_log-plus-one_fusion = f32[1,256]{1,0:T(1,128)} fusion(f32[1,256]{1,0:T(1,128)S(1)} %collective-permute-done.13, f32[1,256]{1,0:T(1,128)S(1)} %collective-permute-done.12, f32[1,256]{1,0:T(1,128)S(1)} %collective-permute-done.11, f32[1,256]{1,0:T(1,128)S(1)} %collective-permute-done.10, f32[1,256]{1,0:T(1,128)S(1)} %get-tuple-element.31, ...), kind=kLoop, calls=%fused_computation | loop fusion | flops 1280 | bytes 7168 | tf_op jit(solution)/shard_map/log1p | solution.py:339
  (2 shorter events, 0.0 us)
Async XLA Ops:
  0.0 4.2 %copy-start = (bf16[256,1024]{1,0:T(8,128)(2,1)S(1)}, bf16[256,1024]{1,0:T(8,128)(2,1)}, u32[]{:S(2)}) copy-start(bf16[256,1024]{1,0:T(8,128)(2,1)} %rows_ref.1) | copy-start | bytes 1572868
  1.1 3.1 %copy-start.1 = (s32[256]{0:T(256)S(1)}, s32[256]{0:T(256)}, u32[]{:S(2)}) copy-start(s32[256]{0:T(256)} %param.3) | copy-start | bytes 3076
  1.1 13.6 %collective-permute-start = (bf16[160,1024]{1,0:T(8,128)(2,1)S(1)}, bf16[160,1024]{1,0:T(8,128)(2,1)S(1)}, u32[]{:S(2)}, u32[]{:S(2)}) collective-permute-start(bf16[160,1024]{1,0:T(8,128)(2,1)S(1)} %slice.3), channel_id=1, source_target_pairs={{0,4},{1,5},{2,6},{3,7},{4,8},{5,9},{6,10},{7,11},{8,12},{9,13},{1... | collective-permute-start | bytes 983048 | tf_op jit(solution)/shard_map/ppermute | solution.py:278
  4.4 10.4 %collective-permute-start.4 = (bf16[136,1024]{1,0:T(8,128)(2,1)S(1)}, bf16[136,1024]{1,0:T(8,128)(2,1)S(1)}, u32[]{:S(2)}, u32[]{:S(2)}) collective-permute-start(bf16[136,1024]{1,0:T(8,128)(2,1)S(1)} %get-tuple-element.24), channel_id=1, source_target_pairs={{0,2},{1,3},{2,0},{3,1},{4,6},{5,7},{6,4},{7,5},{8,10},{9,11},{10,... | collective-permute-start | bytes 835592 | tf_op jit(solution)/shard_map/ppermute | solution.py:274
  5.9 13.8 %collective-permute-start.2 = (bf16[264,1024]{1,0:T(8,128)(2,1)S(1)}, bf16[264,1024]{1,0:T(8,128)(2,1)S(1)}, u32[]{:S(2)}, u32[]{:S(2)}) collective-permute-start(bf16[264,1024]{1,0:T(8,128)(2,1)S(1)} %get-tuple-element.22.refs_0_.own_ref), channel_id=1, source_target_pairs={{0,1},{1,0},{2,3},{3,2},{4,5},{5,4},{6,7},{7,6},{8,9},{9,8},{10,11... | collective-permute-start | bytes 1622024 | tf_op jit(solution)/shard_map/ppermute | solution.py:274
  5.9 12.2 %collective-permute-start.3 = (bf16[128,1024]{1,0:T(8,128)(2,1)S(1)}, bf16[128,1024]{1,0:T(8,128)(2,1)S(1)}, u32[]{:S(2)}, u32[]{:S(2)}) collective-permute-start(bf16[128,1024]{1,0:T(8,128)(2,1)S(1)} %get-tuple-element.23), channel_id=1, source_target_pairs={{0,2},{1,3},{2,0},{3,1},{4,6},{5,7},{6,4},{7,5},{8,10},{9,11},{10,... | collective-permute-start | bytes 786440 | tf_op jit(solution)/shard_map/ppermute | solution.py:274
  6.5 12.0 %collective-permute-start.7 = (bf16[104,1024]{1,0:T(8,128)(2,1)S(1)}, bf16[104,1024]{1,0:T(8,128)(2,1)S(1)}, u32[]{:S(2)}, u32[]{:S(2)}) collective-permute-start(bf16[104,1024]{1,0:T(8,128)(2,1)S(1)} %get-tuple-element.27), channel_id=1, source_target_pairs={{0,4},{1,5},{2,6},{3,7},{4,8},{5,9},{6,10},{7,11},{8,12},{9,13},{1... | collective-permute-start | bytes 638984 | tf_op jit(solution)/shard_map/ppermute | solution.py:278
  14.7 10.9 %collective-permute-start.1 = (bf16[160,1024]{1,0:T(8,128)(2,1)S(1)}, bf16[160,1024]{1,0:T(8,128)(2,1)S(1)}, u32[]{:S(2)}, u32[]{:S(2)}) collective-permute-start(bf16[160,1024]{1,0:T(8,128)(2,1)S(1)} %collective-permute-done.head_ref), channel_id=1, source_target_pairs={{0,5},{1,4},{2,7},{3,6},{4,9},{5,8},{6,11},{7,10},{8,13},{9,12},{1... | collective-permute-start | bytes 983048 | tf_op jit(solution)/shard_map/ppermute | solution.py:278
  14.7 5.0 %collective-permute-start.6 = (bf16[136,1024]{1,0:T(8,128)(2,1)S(1)}, bf16[136,1024]{1,0:T(8,128)(2,1)S(1)}, u32[]{:S(2)}, u32[]{:S(2)}) collective-permute-start(bf16[136,1024]{1,0:T(8,128)(2,1)S(1)} %collective-permute-done.4.refs_3_), channel_id=1, source_target_pairs={{0,1},{1,0},{2,3},{3,2},{4,5},{5,4},{6,7},{7,6},{8,9},{9,8},{10,11... | collective-permute-start | bytes 835592 | tf_op jit(solution)/shard_map/ppermute | solution.py:274
  18.2 1.5 %collective-permute-start.5 = (bf16[128,1024]{1,0:T(8,128)(2,1)S(1)}, bf16[128,1024]{1,0:T(8,128)(2,1)S(1)}, u32[]{:S(2)}, u32[]{:S(2)}) collective-permute-start(bf16[128,1024]{1,0:T(8,128)(2,1)S(1)} %collective-permute-done.3.refs_2_), channel_id=1, source_target_pairs={{0,1},{1,0},{2,3},{3,2},{4,5},{5,4},{6,7},{7,6},{8,9},{9,8},{10,11... | collective-permute-start | bytes 786440 | tf_op jit(solution)/shard_map/ppermute | solution.py:274
  18.5 7.2 %collective-permute-start.8 = (bf16[104,1024]{1,0:T(8,128)(2,1)S(1)}, bf16[104,1024]{1,0:T(8,128)(2,1)S(1)}, u32[]{:S(2)}, u32[]{:S(2)}) collective-permute-start(bf16[104,1024]{1,0:T(8,128)(2,1)S(1)} %collective-permute-done.7.tail_ref), channel_id=1, source_target_pairs={{4,9},{5,8},{6,11},{7,10},{8,13},{9,12},{10,15},{11,14},{20,25},{2... | collective-permute-start | bytes 638984 | tf_op jit(solution)/shard_map/ppermute | solution.py:278
  22.5 5.6 %collective-permute-start.9 = (f32[1,256]{1,0:T(1,128)S(1)}, f32[1,256]{1,0:T(1,128)S(1)}, u32[]{:S(2)}, u32[]{:S(2)}) collective-permute-start(f32[1,256]{1,0:T(1,128)S(1)} %get-tuple-element.32), channel_id=1, source_target_pairs={{4,0},{5,1},{6,2},{7,3},{8,4},{9,5},{10,6},{11,7},{12,8},{13,9},{1... | collective-permute-start | bytes 3080 | tf_op jit(solution)/shard_map/ppermute | solution.py:278
  28.1 5.8 %collective-permute-start.10 = (f32[1,256]{1,0:T(1,128)S(1)}, f32[1,256]{1,0:T(1,128)S(1)}, u32[]{:S(2)}, u32[]{:S(2)}) collective-permute-start(f32[1,256]{1,0:T(1,128)S(1)} %get-tuple-element.35), channel_id=1, source_target_pairs={{8,1},{9,0},{10,3},{11,2},{12,5},{13,4},{14,7},{15,6},{24,17},{25,... | collective-permute-start | bytes 3080 | tf_op jit(solution)/shard_map/ppermute | solution.py:278
  29.6 4.3 %collective-permute-start.11 = (f32[1,256]{1,0:T(1,128)S(1)}, f32[1,256]{1,0:T(1,128)S(1)}, u32[]{:S(2)}, u32[]{:S(2)}) collective-permute-start(f32[1,256]{1,0:T(1,128)S(1)} %get-tuple-element.36), channel_id=1, source_target_pairs={{0,2},{1,3},{2,0},{3,1},{4,6},{5,7},{6,4},{7,5},{8,10},{9,11},{10,... | collective-permute-start | bytes 3080 | tf_op jit(solution)/shard_map/ppermute | solution.py:274
  31.2 3.0 %collective-permute-start.12 = (f32[1,256]{1,0:T(1,128)S(1)}, f32[1,256]{1,0:T(1,128)S(1)}, u32[]{:S(2)}, u32[]{:S(2)}) collective-permute-start(f32[1,256]{1,0:T(1,128)S(1)} %get-tuple-element.37), channel_id=1, source_target_pairs={{0,3},{1,2},{2,1},{3,0},{4,7},{5,6},{6,5},{7,4},{8,11},{9,10},{10,... | collective-permute-start | bytes 3080 | tf_op jit(solution)/shard_map/ppermute | solution.py:274
  31.2 3.0 %collective-permute-start.13 = (f32[1,256]{1,0:T(1,128)S(1)}, f32[1,256]{1,0:T(1,128)S(1)}, u32[]{:S(2)}, u32[]{:S(2)}) collective-permute-start(f32[1,256]{1,0:T(1,128)S(1)} %get-tuple-element.38), channel_id=1, source_target_pairs={{0,1},{1,0},{2,3},{3,2},{4,5},{5,4},{6,7},{7,6},{8,9},{9,8},{10,11... | collective-permute-start | bytes 3080 | tf_op jit(solution)/shard_map/ppermute | solution.py:274

commit v37 on v35

--- a/solution.py
+++ b/solution.py
@@ -211,7 +211,7 @@
             first += size
 
 
-def last_kernel(moves, powers_ref, rest_ref, tail_ref, ids_ref, earlier_ref, *refs):
+def last_kernel(moves, powers_ref, rest_ref, tail_ref, ids_ref, *refs):
     query_refs, (column_ref, sums_ref) = refs[:-2], refs[-2:]
     rows = column_ref.shape[1]
     cut = powers_ref.shape[1]
@@ -236,21 +236,22 @@
             late_column = late_column + column
             early, column = add_masses(query_ids, key_ids[:, :cut], powers_ref[part, :])
             early_column = early_column + column
-            sums_ref[part, :] = earlier_ref[part, :] + early + late
+            sums_ref[part, :] = early + late
             first += size
         column_ref[...] = jnp.concatenate([early_column, late_column], axis=1)
 
     @pl.when(jnp.logical_not(arrived))
     def _():
         column_ref[...] = jnp.zeros_like(column_ref)
-        sums_ref[...] = earlier_ref[...]
-
-
-def fold_kernel(sums_ref, mass_ref, *row_refs):
-    rows = mass_ref.shape[1]
+        sums_ref[...] = jnp.zeros_like(sums_ref)
+
+
+def fold_kernel(sums_ref, *refs):
+    before_refs, row_refs = refs[:-PLANE], refs[-PLANE:]
+    rows = row_refs[0].shape[1]
     for m in range(PLANE):
         row_sum = jnp.sum(sums_ref[pl.ds(m * rows, rows), :].T, axis=0, keepdims=True)
-        row_refs[m][...] = row_sum + mass_ref[...] if m == 0 else row_sum
+        row_refs[m][...] = row_sum + before_refs[m][...] if m < len(before_refs) else row_sum
 
 
 def grid_plan(embeddings, cluster_ids):
@@ -318,14 +319,15 @@
         out_shape=(vector, lanes),
         cost_estimate=small,
         compiler_params=params,
-    )(powers, rest, last_tail, ids, first_sums, *queries)
+    )(powers, rest, last_tail, ids, *queries)
     returned_first, last_column = lax.optimization_barrier((returned_first, last_column))
-    row_sums = pl.pallas_call(
+    fold = pl.pallas_call(
         fold_kernel,
         out_shape=[vector] * PLANE,
         cost_estimate=small,
         compiler_params=params,
-    )(sums, mass)
+    )
+    row_sums = fold(sums, *fold(first_sums, mass))
     returned = [on_line(last_column, last_back, 1)]
     returned += [in_plane(row_sums[step], step) for step in (2, 3, 1)]
     return jnp.log1p(sum(returned, row_sums[0] + returned_first)).reshape(row_count)

time: 34.3 us -> 34.3 us (level)
  transfers between devices with their start and end apart: 14 -> 14, of which waited for: 7 -> 7; matrix products, arithmetic and copies ran while one was open for 0% -> 0% of each run, Pallas kernels for 8% -> 9%
where the time goes in v37:
time: 34.3 us; the launch traced here: 34.1 us
  waiting for transfers between devices  15.2 us (44%)
  starting transfers between devices  14.2 us (41%)
  Pallas kernels  3.02 us (9%)
  local copies, waits for them, and re-layouts  1.08 us (3%)
  other arithmetic  0.58 us (2%)
    ppermute x6, waiting for transfers between devices, on_line(): return lax.ppermute(value, 'gx', pairs)  11.7 us
    ppermute x6, starting transfers between devices, on_line(): return lax.ppermute(value, 'gx', pairs)  9.73 us
    ppermute x8, starting transfers between devices, in_plane(): return lax.ppermute(value, 'gx', [(i, i ^ step) for i in range(peers)])  4.45 us
    ppermute x8, waiting for transfers between devices, in_plane(): return lax.ppermute(value, 'gx', [(i, i ^ step) for i in range(peers)])  3.51 us
    pallas_call x1, Pallas kernels, grid_plan(): pl.pallas_call(functools.partial(first_kernel, first_moves), out_shape=(l...  2.02 us
    slice x1, local copies, waits for them, and re-layouts, grid_plan(): first_head = on_line(embeddings[:part], first_moves, 0)  1.07 us
  transfers between devices with their start and end apart: 14, of which 7 were waited for; matrix products, arithmetic and copies ran while one was open for 0% of the time, Pallas kernels for 9%

profile of v37, /device:TPU:0, one launch (start us, length us, event | category | flops | bytes accessed | tf_op | source)
XLA Modules:
  0.0 34.1 jit_solution(930448092735464456)
XLA Ops:
  0.0 0.0 copy-start
  0.0 1.1 %slice.3 = bf16[160,1024]{1,0:T(8,128)(2,1)S(1)} slice(bf16[256,1024]{1,0:T(8,128)(2,1)} %rows_ref.1), slice={[0:160], [0:1024]} | slice | bytes 655360 | tf_op jit(solution)/shard_map/slice | solution.py:285
  1.1 0.0 copy-start.1
  1.1 3.1 %collective-permute-start = (bf16[160,1024]{1,0:T(8,128)(2,1)S(1)}, bf16[160,1024]{1,0:T(8,128)(2,1)S(1)}, u32[]{:S(2)}, u32[]{:S(2)}) collective-permute-start(bf16[160,1024]{1,0:T(8,128)(2,1)S(1)} %slice.3), channel_id=1, source_target_pairs={{0,4},{1,5},{2,6},{3,7},{4,8},{5,9},{6,10},{7,11},{8,12},{9,13},{1... | collective-permute-start | bytes 983048 | tf_op jit(solution)/shard_map/ppermute | solution.py:274
  4.2 0.0 copy-done
  4.2 0.0 copy-done.1
  4.2 0.2 shard_map.28
  4.4 1.6 %collective-permute-start.4 = (bf16[136,1024]{1,0:T(8,128)(2,1)S(1)}, bf16[136,1024]{1,0:T(8,128)(2,1)S(1)}, u32[]{:S(2)}, u32[]{:S(2)}) collective-permute-start(bf16[136,1024]{1,0:T(8,128)(2,1)S(1)} %get-tuple-element.29), channel_id=1, source_target_pairs={{0,2},{1,3},{2,0},{3,1},{4,6},{5,7},{6,4},{7,5},{8,10},{9,11},{10,... | collective-permute-start | bytes 835592 | tf_op jit(solution)/shard_map/ppermute | solution.py:270
  5.9 0.0 collective-permute-start.2
  5.9 0.5 %collective-permute-start.3 = (bf16[128,1024]{1,0:T(8,128)(2,1)S(1)}, bf16[128,1024]{1,0:T(8,128)(2,1)S(1)}, u32[]{:S(2)}, u32[]{:S(2)}) collective-permute-start(bf16[128,1024]{1,0:T(8,128)(2,1)S(1)} %get-tuple-element.28), channel_id=1, source_target_pairs={{0,2},{1,3},{2,0},{3,1},{4,6},{5,7},{6,4},{7,5},{8,10},{9,11},{10,... | collective-permute-start | bytes 786440 | tf_op jit(solution)/shard_map/ppermute | solution.py:270
  6.5 1.6 %collective-permute-start.7 = (bf16[104,1024]{1,0:T(8,128)(2,1)S(1)}, bf16[104,1024]{1,0:T(8,128)(2,1)S(1)}, u32[]{:S(2)}, u32[]{:S(2)}) collective-permute-start(bf16[104,1024]{1,0:T(8,128)(2,1)S(1)} %get-tuple-element.32), channel_id=1, source_target_pairs={{0,4},{1,5},{2,6},{3,7},{4,8},{5,9},{6,10},{7,11},{8,12},{9,13},{1... | collective-permute-start | bytes 638984 | tf_op jit(solution)/shard_map/ppermute | solution.py:274
  8.0 6.7 %collective-permute-done.head_ref = bf16[160,1024]{1,0:T(8,128)(2,1)S(1)} collective-permute-done((bf16[160,1024]{1,0:T(8,128)(2,1)S(1)}, bf16[160,1024]{1,0:T(8,128)(2,1)S(1)}, u32[]{:S(2)}, u32[]{:S(2)}) %collective-permute-start) | collective-permute-done | bytes 327712 | tf_op jit(solution)/shard_map/ppermute | solution.py:274
  14.7 0.0 collective-permute-start.1
  14.7 0.0 collective-permute-done.4.refs_3_
  14.7 0.1 collective-permute-start.6
  14.9 3.3 %collective-permute-done.3.refs_2_ = bf16[128,1024]{1,0:T(8,128)(2,1)S(1)} collective-permute-done((bf16[128,1024]{1,0:T(8,128)(2,1)S(1)}, bf16[128,1024]{1,0:T(8,128)(2,1)S(1)}, u32[]{:S(2)}, u32[]{:S(2)}) %collective-permute-start.3) | collective-permute-done | bytes 262176 | tf_op jit(solution)/shard_map/ppermute | solution.py:270
  18.2 0.0 collective-permute-start.5
  18.2 0.3 collective-permute-done.7.tail_ref
  18.5 0.7 %collective-permute-start.8 = (bf16[104,1024]{1,0:T(8,128)(2,1)S(1)}, bf16[104,1024]{1,0:T(8,128)(2,1)S(1)}, u32[]{:S(2)}, u32[]{:S(2)}) collective-permute-start(bf16[104,1024]{1,0:T(8,128)(2,1)S(1)} %collective-permute-done.7.tail_ref), channel_id=1, source_target_pairs={{4,9},{5,8},{6,11},{7,10},{8,13},{9,12},{10,15},{11,14},{20,25},{2... | collective-permute-start | bytes 638984 | tf_op jit(solution)/shard_map/ppermute | solution.py:274
  19.1 0.4 %shard_map.30.own_mass_ref = f32[1,256]{1,0:T(1,128)S(1)} custom-call(bf16[264,1024]{1,0:T(8,128)(2,1)S(1)} %get-tuple-element.27.refs_0_.own_ref), custom_call_target="tpu_custom_call" | custom-call | flops 1 | bytes 1 | tf_op jit(solution)/shard_map/pallas_call | solution.py:292
  19.5 0.2 collective-permute-done.5.refs_4_
  19.7 0.0 collective-permute-done.2.refs_1_
  19.7 0.0 collective-permute-done.6.refs_5_
  19.7 2.0 %shard_map.31 = (f32[1024,128]{1,0:T(8,128)S(1)}, f32[1,256]{1,0:T(1,128)S(1)}, f32[1024,128]{1,0:T(8,128)S(1)}, f32[1,256]{1,0:T(1,128)S(1)}) custom-call(f32[1,256]{1,0:T(1,128)S(1)} %shard_map.30.own_mass_ref, bf16[160,1024]{1,0:T(8,128)(2,1)S(1)} %collective-permute-done.head_ref, bf16[104,1024]{1,0:T(8,128)(2,1)S(1)} %collective-permute-done.7.tail_ref, ...), custom_call_target="tpu_custom_call" | custom-call | flops 1 | bytes 1 | tf_op jit(solution)/shard_map/pallas_call | solution.py:302
  21.7 3.1 %collective-permute-start.9 = (f32[1,256]{1,0:T(1,128)S(1)}, f32[1,256]{1,0:T(1,128)S(1)}, u32[]{:S(2)}, u32[]{:S(2)}) collective-permute-start(f32[1,256]{1,0:T(1,128)S(1)} %get-tuple-element.42), channel_id=1, source_target_pairs={{4,0},{5,1},{6,2},{7,3},{8,4},{9,5},{10,6},{11,7},{12,8},{13,9},{1... | collective-permute-start | bytes 3080 | tf_op jit(solution)/shard_map/ppermute | solution.py:274
  24.9 0.2 shard_map.33
  25.1 0.4 %collective-permute-done.1.head_ref = bf16[160,1024]{1,0:T(8,128)(2,1)S(1)} collective-permute-done((bf16[160,1024]{1,0:T(8,128)(2,1)S(1)}, bf16[160,1024]{1,0:T(8,128)(2,1)S(1)}, u32[]{:S(2)}, u32[]{:S(2)}) %collective-permute-start.1) | collective-permute-done | bytes 327712 | tf_op jit(solution)/shard_map/ppermute | solution.py:274
  25.5 0.0 collective-permute-done.8.tail_ref
  25.5 1.8 %collective-permute-done.9 = f32[1,256]{1,0:T(1,128)S(1)} collective-permute-done((f32[1,256]{1,0:T(1,128)S(1)}, f32[1,256]{1,0:T(1,128)S(1)}, u32[]{:S(2)}, u32[]{:S(2)}) %collective-permute-start.9) | collective-permute-done | bytes 1056 | tf_op jit(solution)/shard_map/ppermute | solution.py:274
  27.4 1.3 %collective-permute-start.10 = (f32[1,256]{1,0:T(1,128)S(1)}, f32[1,256]{1,0:T(1,128)S(1)}, u32[]{:S(2)}, u32[]{:S(2)}) collective-permute-start(f32[1,256]{1,0:T(1,128)S(1)} %get-tuple-element.45), channel_id=1, source_target_pairs={{8,1},{9,0},{10,3},{11,2},{12,5},{13,4},{14,7},{15,6},{24,17},{25,... | collective-permute-start | bytes 3080 | tf_op jit(solution)/shard_map/ppermute | solution.py:274
  28.7 0.2 shard_map.34
  28.9 1.6 %collective-permute-start.11 = (f32[1,256]{1,0:T(1,128)S(1)}, f32[1,256]{1,0:T(1,128)S(1)}, u32[]{:S(2)}, u32[]{:S(2)}) collective-permute-start(f32[1,256]{1,0:T(1,128)S(1)} %get-tuple-element.46), channel_id=1, source_target_pairs={{0,2},{1,3},{2,0},{3,1},{4,6},{5,7},{6,4},{7,5},{8,10},{9,11},{10,... | collective-permute-start | bytes 3080 | tf_op jit(solution)/shard_map/ppermute | solution.py:270
  30.4 0.0 collective-permute-start.12
  30.4 0.6 %collective-permute-start.13 = (f32[1,256]{1,0:T(1,128)S(1)}, f32[1,256]{1,0:T(1,128)S(1)}, u32[]{:S(2)}, u32[]{:S(2)}) collective-permute-start(f32[1,256]{1,0:T(1,128)S(1)} %get-tuple-element.48), channel_id=1, source_target_pairs={{0,1},{1,0},{2,3},{3,2},{4,5},{5,4},{6,7},{7,6},{8,9},{9,8},{10,11... | collective-permute-start | bytes 3080 | tf_op jit(solution)/shard_map/ppermute | solution.py:270
  31.1 2.4 %collective-permute-done.10 = f32[1,256]{1,0:T(1,128)S(1)} collective-permute-done((f32[1,256]{1,0:T(1,128)S(1)}, f32[1,256]{1,0:T(1,128)S(1)}, u32[]{:S(2)}, u32[]{:S(2)}) %collective-permute-start.10) | collective-permute-done | bytes 1056 | tf_op jit(solution)/shard_map/ppermute | solution.py:274
  33.5 0.0 collective-permute-done.11
  33.5 0.0 collective-permute-done.12
  33.5 0.0 collective-permute-done.13
  33.5 0.6 %add_log-plus-one_fusion = f32[1,256]{1,0:T(1,128)} fusion(f32[1,256]{1,0:T(1,128)S(1)} %collective-permute-done.13, f32[1,256]{1,0:T(1,128)S(1)} %collective-permute-done.12, f32[1,256]{1,0:T(1,128)S(1)} %collective-permute-done.11, f32[1,256]{1,0:T(1,128)S(1)} %collective-permute-done.10, f32[1,256]{1,0:T(1,128)S(1)} %get-tuple-element.41, ...), kind=kLoop, calls=%fused_computation | loop fusion | flops 1280 | bytes 7168 | tf_op jit(solution)/shard_map/log1p | solution.py:333
  (2 shorter events, 0.0 us)
Async XLA Ops:
  0.0 4.2 %copy-start = (bf16[256,1024]{1,0:T(8,128)(2,1)S(1)}, bf16[256,1024]{1,0:T(8,128)(2,1)}, u32[]{:S(2)}) copy-start(bf16[256,1024]{1,0:T(8,128)(2,1)} %rows_ref.1) | copy-start | bytes 1572868
  1.1 3.1 %copy-start.1 = (s32[256]{0:T(256)S(1)}, s32[256]{0:T(256)}, u32[]{:S(2)}) copy-start(s32[256]{0:T(256)} %param.3) | copy-start | bytes 3076
  1.1 13.6 %collective-permute-start = (bf16[160,1024]{1,0:T(8,128)(2,1)S(1)}, bf16[160,1024]{1,0:T(8,128)(2,1)S(1)}, u32[]{:S(2)}, u32[]{:S(2)}) collective-permute-start(bf16[160,1024]{1,0:T(8,128)(2,1)S(1)} %slice.3), channel_id=1, source_target_pairs={{0,4},{1,5},{2,6},{3,7},{4,8},{5,9},{6,10},{7,11},{8,12},{9,13},{1... | collective-permute-start | bytes 983048 | tf_op jit(solution)/shard_map/ppermute | solution.py:274
  4.4 10.4 %collective-permute-start.4 = (bf16[136,1024]{1,0:T(8,128)(2,1)S(1)}, bf16[136,1024]{1,0:T(8,128)(2,1)S(1)}, u32[]{:S(2)}, u32[]{:S(2)}) collective-permute-start(bf16[136,1024]{1,0:T(8,128)(2,1)S(1)} %get-tuple-element.29), channel_id=1, source_target_pairs={{0,2},{1,3},{2,0},{3,1},{4,6},{5,7},{6,4},{7,5},{8,10},{9,11},{10,... | collective-permute-start | bytes 835592 | tf_op jit(solution)/shard_map/ppermute | solution.py:270
  5.9 13.8 %collective-permute-start.2 = (bf16[264,1024]{1,0:T(8,128)(2,1)S(1)}, bf16[264,1024]{1,0:T(8,128)(2,1)S(1)}, u32[]{:S(2)}, u32[]{:S(2)}) collective-permute-start(bf16[264,1024]{1,0:T(8,128)(2,1)S(1)} %get-tuple-element.27.refs_0_.own_ref), channel_id=1, source_target_pairs={{0,1},{1,0},{2,3},{3,2},{4,5},{5,4},{6,7},{7,6},{8,9},{9,8},{10,11... | collective-permute-start | bytes 1622024 | tf_op jit(solution)/shard_map/ppermute | solution.py:270
  5.9 12.2 %collective-permute-start.3 = (bf16[128,1024]{1,0:T(8,128)(2,1)S(1)}, bf16[128,1024]{1,0:T(8,128)(2,1)S(1)}, u32[]{:S(2)}, u32[]{:S(2)}) collective-permute-start(bf16[128,1024]{1,0:T(8,128)(2,1)S(1)} %get-tuple-element.28), channel_id=1, source_target_pairs={{0,2},{1,3},{2,0},{3,1},{4,6},{5,7},{6,4},{7,5},{8,10},{9,11},{10,... | collective-permute-start | bytes 786440 | tf_op jit(solution)/shard_map/ppermute | solution.py:270
  6.5 12.0 %collective-permute-start.7 = (bf16[104,1024]{1,0:T(8,128)(2,1)S(1)}, bf16[104,1024]{1,0:T(8,128)(2,1)S(1)}, u32[]{:S(2)}, u32[]{:S(2)}) collective-permute-start(bf16[104,1024]{1,0:T(8,128)(2,1)S(1)} %get-tuple-element.32), channel_id=1, source_target_pairs={{0,4},{1,5},{2,6},{3,7},{4,8},{5,9},{6,10},{7,11},{8,12},{9,13},{1... | collective-permute-start | bytes 638984 | tf_op jit(solution)/shard_map/ppermute | solution.py:274
  14.7 10.8 %collective-permute-start.1 = (bf16[160,1024]{1,0:T(8,128)(2,1)S(1)}, bf16[160,1024]{1,0:T(8,128)(2,1)S(1)}, u32[]{:S(2)}, u32[]{:S(2)}) collective-permute-start(bf16[160,1024]{1,0:T(8,128)(2,1)S(1)} %collective-permute-done.head_ref), channel_id=1, source_target_pairs={{0,5},{1,4},{2,7},{3,6},{4,9},{5,8},{6,11},{7,10},{8,13},{9,12},{1... | collective-permute-start | bytes 983048 | tf_op jit(solution)/shard_map/ppermute | solution.py:274
  14.7 5.0 %collective-permute-start.6 = (bf16[136,1024]{1,0:T(8,128)(2,1)S(1)}, bf16[136,1024]{1,0:T(8,128)(2,1)S(1)}, u32[]{:S(2)}, u32[]{:S(2)}) collective-permute-start(bf16[136,1024]{1,0:T(8,128)(2,1)S(1)} %collective-permute-done.4.refs_3_), channel_id=1, source_target_pairs={{0,1},{1,0},{2,3},{3,2},{4,5},{5,4},{6,7},{7,6},{8,9},{9,8},{10,11... | collective-permute-start | bytes 835592 | tf_op jit(solution)/shard_map/ppermute | solution.py:270
  18.2 1.5 %collective-permute-start.5 = (bf16[128,1024]{1,0:T(8,128)(2,1)S(1)}, bf16[128,1024]{1,0:T(8,128)(2,1)S(1)}, u32[]{:S(2)}, u32[]{:S(2)}) collective-permute-start(bf16[128,1024]{1,0:T(8,128)(2,1)S(1)} %collective-permute-done.3.refs_2_), channel_id=1, source_target_pairs={{0,1},{1,0},{2,3},{3,2},{4,5},{5,4},{6,7},{7,6},{8,9},{9,8},{10,11... | collective-permute-start | bytes 786440 | tf_op jit(solution)/shard_map/ppermute | solution.py:270
  18.5 7.0 %collective-permute-start.8 = (bf16[104,1024]{1,0:T(8,128)(2,1)S(1)}, bf16[104,1024]{1,0:T(8,128)(2,1)S(1)}, u32[]{:S(2)}, u32[]{:S(2)}) collective-permute-start(bf16[104,1024]{1,0:T(8,128)(2,1)S(1)} %collective-permute-done.7.tail_ref), channel_id=1, source_target_pairs={{4,9},{5,8},{6,11},{7,10},{8,13},{9,12},{10,15},{11,14},{20,25},{2... | collective-permute-start | bytes 638984 | tf_op jit(solution)/shard_map/ppermute | solution.py:274
  21.7 5.6 %collective-permute-start.9 = (f32[1,256]{1,0:T(1,128)S(1)}, f32[1,256]{1,0:T(1,128)S(1)}, u32[]{:S(2)}, u32[]{:S(2)}) collective-permute-start(f32[1,256]{1,0:T(1,128)S(1)} %get-tuple-element.42), channel_id=1, source_target_pairs={{4,0},{5,1},{6,2},{7,3},{8,4},{9,5},{10,6},{11,7},{12,8},{13,9},{1... | collective-permute-start | bytes 3080 | tf_op jit(solution)/shard_map/ppermute | solution.py:274
  27.4 6.2 %collective-permute-start.10 = (f32[1,256]{1,0:T(1,128)S(1)}, f32[1,256]{1,0:T(1,128)S(1)}, u32[]{:S(2)}, u32[]{:S(2)}) collective-permute-start(f32[1,256]{1,0:T(1,128)S(1)} %get-tuple-element.45), channel_id=1, source_target_pairs={{8,1},{9,0},{10,3},{11,2},{12,5},{13,4},{14,7},{15,6},{24,17},{25,... | collective-permute-start | bytes 3080 | tf_op jit(solution)/shard_map/ppermute | solution.py:274
  28.9 4.7 %collective-permute-start.11 = (f32[1,256]{1,0:T(1,128)S(1)}, f32[1,256]{1,0:T(1,128)S(1)}, u32[]{:S(2)}, u32[]{:S(2)}) collective-permute-start(f32[1,256]{1,0:T(1,128)S(1)} %get-tuple-element.46), channel_id=1, source_target_pairs={{0,2},{1,3},{2,0},{3,1},{4,6},{5,7},{6,4},{7,5},{8,10},{9,11},{10,... | collective-permute-start | bytes 3080 | tf_op jit(solution)/shard_map/ppermute | solution.py:270
  30.4 3.1 %collective-permute-start.12 = (f32[1,256]{1,0:T(1,128)S(1)}, f32[1,256]{1,0:T(1,128)S(1)}, u32[]{:S(2)}, u32[]{:S(2)}) collective-permute-start(f32[1,256]{1,0:T(1,128)S(1)} %get-tuple-element.47), channel_id=1, source_target_pairs={{0,3},{1,2},{2,1},{3,0},{4,7},{5,6},{6,5},{7,4},{8,11},{9,10},{10,... | collective-permute-start | bytes 3080 | tf_op jit(solution)/shard_map/ppermute | solution.py:270
  30.4 3.1 %collective-permute-start.13 = (f32[1,256]{1,0:T(1,128)S(1)}, f32[1,256]{1,0:T(1,128)S(1)}, u32[]{:S(2)}, u32[]{:S(2)}) collective-permute-start(f32[1,256]{1,0:T(1,128)S(1)} %get-tuple-element.48), channel_id=1, source_target_pairs={{0,1},{1,0},{2,3},{3,2},{4,5},{5,4},{6,7},{7,6},{8,9},{9,8},{10,11... | collective-permute-start | bytes 3080 | tf_op jit(solution)/shard_map/ppermute | solution.py:270

commit v38 on v37

--- a/solution.py
+++ b/solution.py
@@ -329,7 +329,7 @@
     )
     row_sums = fold(sums, *fold(first_sums, mass))
     returned = [on_line(last_column, last_back, 1)]
-    returned += [in_plane(row_sums[step], step) for step in (2, 3, 1)]
+    returned += [in_plane(row_sums[step], step) for step in (3, 2, 1)]
     return jnp.log1p(sum(returned, row_sums[0] + returned_first)).reshape(row_count)
 
 

time: 34.3 us -> 34.4 us (level)
  no operation moved by 1% of the time
where the time goes in v38:
time: 34.4 us; the launch traced here: 34.1 us
  waiting for transfers between devices  15.5 us (45%)
  starting transfers between devices  13.9 us (40%)
  Pallas kernels  3.02 us (9%)
  local copies, waits for them, and re-layouts  1.08 us (3%)
  other arithmetic  0.58 us (2%)
    ppermute x6, waiting for transfers between devices, on_line(): return lax.ppermute(value, 'gx', pairs)  11.9 us
    ppermute x6, starting transfers between devices, on_line(): return lax.ppermute(value, 'gx', pairs)  9.73 us
    ppermute x8, starting transfers between devices, in_plane(): return lax.ppermute(value, 'gx', [(i, i ^ step) for i in range(peers)])  4.17 us
    ppermute x8, waiting for transfers between devices, in_plane(): return lax.ppermute(value, 'gx', [(i, i ^ step) for i in range(peers)])  3.51 us
    pallas_call x1, Pallas kernels, grid_plan(): pl.pallas_call(functools.partial(first_kernel, first_moves), out_shape=(l...  2.02 us
    slice x1, local copies, waits for them, and re-layouts, grid_plan(): first_head = on_line(embeddings[:part], first_moves, 0)  1.07 us
  transfers between devices with their start and end apart: 14, of which 7 were waited for; matrix products, arithmetic and copies ran while one was open for 0% of the time, Pallas kernels for 9%

profile of v38, /device:TPU:0, one launch (start us, length us, event | category | flops | bytes accessed | tf_op | source)
XLA Modules:
  0.0 34.1 jit_solution(16879212421309887112)
XLA Ops:
  0.0 0.0 copy-start
  0.0 1.1 %slice.3 = bf16[160,1024]{1,0:T(8,128)(2,1)S(1)} slice(bf16[256,1024]{1,0:T(8,128)(2,1)} %rows_ref.1), slice={[0:160], [0:1024]} | slice | bytes 655360 | tf_op jit(solution)/shard_map/slice | solution.py:285
  1.1 0.0 copy-start.1
  1.1 3.1 %collective-permute-start = (bf16[160,1024]{1,0:T(8,128)(2,1)S(1)}, bf16[160,1024]{1,0:T(8,128)(2,1)S(1)}, u32[]{:S(2)}, u32[]{:S(2)}) collective-permute-start(bf16[160,1024]{1,0:T(8,128)(2,1)S(1)} %slice.3), channel_id=1, source_target_pairs={{0,4},{1,5},{2,6},{3,7},{4,8},{5,9},{6,10},{7,11},{8,12},{9,13},{1... | collective-permute-start | bytes 983048 | tf_op jit(solution)/shard_map/ppermute | solution.py:274
  4.2 0.0 copy-done
  4.2 0.0 copy-done.1
  4.2 0.2 shard_map.28
  4.4 1.6 %collective-permute-start.4 = (bf16[136,1024]{1,0:T(8,128)(2,1)S(1)}, bf16[136,1024]{1,0:T(8,128)(2,1)S(1)}, u32[]{:S(2)}, u32[]{:S(2)}) collective-permute-start(bf16[136,1024]{1,0:T(8,128)(2,1)S(1)} %get-tuple-element.29), channel_id=1, source_target_pairs={{0,2},{1,3},{2,0},{3,1},{4,6},{5,7},{6,4},{7,5},{8,10},{9,11},{10,... | collective-permute-start | bytes 835592 | tf_op jit(solution)/shard_map/ppermute | solution.py:270
  5.9 0.0 collective-permute-start.2
  5.9 0.5 %collective-permute-start.3 = (bf16[128,1024]{1,0:T(8,128)(2,1)S(1)}, bf16[128,1024]{1,0:T(8,128)(2,1)S(1)}, u32[]{:S(2)}, u32[]{:S(2)}) collective-permute-start(bf16[128,1024]{1,0:T(8,128)(2,1)S(1)} %get-tuple-element.28), channel_id=1, source_target_pairs={{0,2},{1,3},{2,0},{3,1},{4,6},{5,7},{6,4},{7,5},{8,10},{9,11},{10,... | collective-permute-start | bytes 786440 | tf_op jit(solution)/shard_map/ppermute | solution.py:270
  6.5 1.6 %collective-permute-start.7 = (bf16[104,1024]{1,0:T(8,128)(2,1)S(1)}, bf16[104,1024]{1,0:T(8,128)(2,1)S(1)}, u32[]{:S(2)}, u32[]{:S(2)}) collective-permute-start(bf16[104,1024]{1,0:T(8,128)(2,1)S(1)} %get-tuple-element.32), channel_id=1, source_target_pairs={{0,4},{1,5},{2,6},{3,7},{4,8},{5,9},{6,10},{7,11},{8,12},{9,13},{1... | collective-permute-start | bytes 638984 | tf_op jit(solution)/shard_map/ppermute | solution.py:274
  8.0 6.7 %collective-permute-done.head_ref = bf16[160,1024]{1,0:T(8,128)(2,1)S(1)} collective-permute-done((bf16[160,1024]{1,0:T(8,128)(2,1)S(1)}, bf16[160,1024]{1,0:T(8,128)(2,1)S(1)}, u32[]{:S(2)}, u32[]{:S(2)}) %collective-permute-start) | collective-permute-done | bytes 327712 | tf_op jit(solution)/shard_map/ppermute | solution.py:274
  14.7 0.0 collective-permute-start.1
  14.7 0.0 collective-permute-done.4.refs_3_
  14.7 0.1 collective-permute-start.6
  14.9 3.3 %collective-permute-done.3.refs_2_ = bf16[128,1024]{1,0:T(8,128)(2,1)S(1)} collective-permute-done((bf16[128,1024]{1,0:T(8,128)(2,1)S(1)}, bf16[128,1024]{1,0:T(8,128)(2,1)S(1)}, u32[]{:S(2)}, u32[]{:S(2)}) %collective-permute-start.3) | collective-permute-done | bytes 262176 | tf_op jit(solution)/shard_map/ppermute | solution.py:270
  18.2 0.0 collective-permute-start.5
  18.2 0.3 collective-permute-done.7.tail_ref
  18.5 0.7 %collective-permute-start.8 = (bf16[104,1024]{1,0:T(8,128)(2,1)S(1)}, bf16[104,1024]{1,0:T(8,128)(2,1)S(1)}, u32[]{:S(2)}, u32[]{:S(2)}) collective-permute-start(bf16[104,1024]{1,0:T(8,128)(2,1)S(1)} %collective-permute-done.7.tail_ref), channel_id=1, source_target_pairs={{4,9},{5,8},{6,11},{7,10},{8,13},{9,12},{10,15},{11,14},{20,25},{2... | collective-permute-start | bytes 638984 | tf_op jit(solution)/shard_map/ppermute | solution.py:274
  19.1 0.4 %shard_map.30.own_mass_ref = f32[1,256]{1,0:T(1,128)S(1)} custom-call(bf16[264,1024]{1,0:T(8,128)(2,1)S(1)} %get-tuple-element.27.refs_0_.own_ref), custom_call_target="tpu_custom_call" | custom-call | flops 1 | bytes 1 | tf_op jit(solution)/shard_map/pallas_call | solution.py:292
  19.5 0.2 collective-permute-done.5.refs_4_
  19.7 0.0 collective-permute-done.2.refs_1_
  19.7 0.0 collective-permute-done.6.refs_5_
  19.7 2.0 %shard_map.31 = (f32[1024,128]{1,0:T(8,128)S(1)}, f32[1,256]{1,0:T(1,128)S(1)}, f32[1024,128]{1,0:T(8,128)S(1)}, f32[1,256]{1,0:T(1,128)S(1)}) custom-call(f32[1,256]{1,0:T(1,128)S(1)} %shard_map.30.own_mass_ref, bf16[160,1024]{1,0:T(8,128)(2,1)S(1)} %collective-permute-done.head_ref, bf16[104,1024]{1,0:T(8,128)(2,1)S(1)} %collective-permute-done.7.tail_ref, ...), custom_call_target="tpu_custom_call" | custom-call | flops 1 | bytes 1 | tf_op jit(solution)/shard_map/pallas_call | solution.py:302
  21.7 3.1 %collective-permute-start.9 = (f32[1,256]{1,0:T(1,128)S(1)}, f32[1,256]{1,0:T(1,128)S(1)}, u32[]{:S(2)}, u32[]{:S(2)}) collective-permute-start(f32[1,256]{1,0:T(1,128)S(1)} %get-tuple-element.42), channel_id=1, source_target_pairs={{4,0},{5,1},{6,2},{7,3},{8,4},{9,5},{10,6},{11,7},{12,8},{13,9},{1... | collective-permute-start | bytes 3080 | tf_op jit(solution)/shard_map/ppermute | solution.py:274
  24.9 0.2 shard_map.33
  25.1 0.4 %collective-permute-done.1.head_ref = bf16[160,1024]{1,0:T(8,128)(2,1)S(1)} collective-permute-done((bf16[160,1024]{1,0:T(8,128)(2,1)S(1)}, bf16[160,1024]{1,0:T(8,128)(2,1)S(1)}, u32[]{:S(2)}, u32[]{:S(2)}) %collective-permute-start.1) | collective-permute-done | bytes 327712 | tf_op jit(solution)/shard_map/ppermute | solution.py:274
  25.5 0.0 collective-permute-done.8.tail_ref
  25.5 1.8 %collective-permute-done.9 = f32[1,256]{1,0:T(1,128)S(1)} collective-permute-done((f32[1,256]{1,0:T(1,128)S(1)}, f32[1,256]{1,0:T(1,128)S(1)}, u32[]{:S(2)}, u32[]{:S(2)}) %collective-permute-start.9) | collective-permute-done | bytes 1056 | tf_op jit(solution)/shard_map/ppermute | solution.py:274
  27.4 1.3 %collective-permute-start.10 = (f32[1,256]{1,0:T(1,128)S(1)}, f32[1,256]{1,0:T(1,128)S(1)}, u32[]{:S(2)}, u32[]{:S(2)}) collective-permute-start(f32[1,256]{1,0:T(1,128)S(1)} %get-tuple-element.45), channel_id=1, source_target_pairs={{8,1},{9,0},{10,3},{11,2},{12,5},{13,4},{14,7},{15,6},{24,17},{25,... | collective-permute-start | bytes 3080 | tf_op jit(solution)/shard_map/ppermute | solution.py:274
  28.7 0.2 shard_map.34
  28.9 0.3 collective-permute-start.11
  29.2 1.3 %collective-permute-start.12 = (f32[1,256]{1,0:T(1,128)S(1)}, f32[1,256]{1,0:T(1,128)S(1)}, u32[]{:S(2)}, u32[]{:S(2)}) collective-permute-start(f32[1,256]{1,0:T(1,128)S(1)} %get-tuple-element.47), channel_id=1, source_target_pairs={{0,2},{1,3},{2,0},{3,1},{4,6},{5,7},{6,4},{7,5},{8,10},{9,11},{10,... | collective-permute-start | bytes 3080 | tf_op jit(solution)/shard_map/ppermute | solution.py:270
  30.5 0.3 collective-permute-start.13
  30.8 2.7 %collective-permute-done.10 = f32[1,256]{1,0:T(1,128)S(1)} collective-permute-done((f32[1,256]{1,0:T(1,128)S(1)}, f32[1,256]{1,0:T(1,128)S(1)}, u32[]{:S(2)}, u32[]{:S(2)}) %collective-permute-start.10) | collective-permute-done | bytes 1056 | tf_op jit(solution)/shard_map/ppermute | solution.py:274
  33.5 0.0 collective-permute-done.11
  33.5 0.0 collective-permute-done.12
  33.5 0.0 collective-permute-done.13
  33.5 0.6 %add_log-plus-one_fusion = f32[1,256]{1,0:T(1,128)} fusion(f32[1,256]{1,0:T(1,128)S(1)} %collective-permute-done.13, f32[1,256]{1,0:T(1,128)S(1)} %collective-permute-done.12, f32[1,256]{1,0:T(1,128)S(1)} %collective-permute-done.11, f32[1,256]{1,0:T(1,128)S(1)} %collective-permute-done.10, f32[1,256]{1,0:T(1,128)S(1)} %get-tuple-element.41, ...), kind=kLoop, calls=%fused_computation | loop fusion | flops 1280 | bytes 7168 | tf_op jit(solution)/shard_map/log1p | solution.py:333
  (2 shorter events, 0.0 us)
Async XLA Ops:
  0.0 4.2 %copy-start = (bf16[256,1024]{1,0:T(8,128)(2,1)S(1)}, bf16[256,1024]{1,0:T(8,128)(2,1)}, u32[]{:S(2)}) copy-start(bf16[256,1024]{1,0:T(8,128)(2,1)} %rows_ref.1) | copy-start | bytes 1572868
  1.1 3.1 %copy-start.1 = (s32[256]{0:T(256)S(1)}, s32[256]{0:T(256)}, u32[]{:S(2)}) copy-start(s32[256]{0:T(256)} %param.3) | copy-start | bytes 3076
  1.1 13.6 %collective-permute-start = (bf16[160,1024]{1,0:T(8,128)(2,1)S(1)}, bf16[160,1024]{1,0:T(8,128)(2,1)S(1)}, u32[]{:S(2)}, u32[]{:S(2)}) collective-permute-start(bf16[160,1024]{1,0:T(8,128)(2,1)S(1)} %slice.3), channel_id=1, source_target_pairs={{0,4},{1,5},{2,6},{3,7},{4,8},{5,9},{6,10},{7,11},{8,12},{9,13},{1... | collective-permute-start | bytes 983048 | tf_op jit(solution)/shard_map/ppermute | solution.py:274
  4.4 10.4 %collective-permute-start.4 = (bf16[136,1024]{1,0:T(8,128)(2,1)S(1)}, bf16[136,1024]{1,0:T(8,128)(2,1)S(1)}, u32[]{:S(2)}, u32[]{:S(2)}) collective-permute-start(bf16[136,1024]{1,0:T(8,128)(2,1)S(1)} %get-tuple-element.29), channel_id=1, source_target_pairs={{0,2},{1,3},{2,0},{3,1},{4,6},{5,7},{6,4},{7,5},{8,10},{9,11},{10,... | collective-permute-start | bytes 835592 | tf_op jit(solution)/shard_map/ppermute | solution.py:270
  5.9 13.8 %collective-permute-start.2 = (bf16[264,1024]{1,0:T(8,128)(2,1)S(1)}, bf16[264,1024]{1,0:T(8,128)(2,1)S(1)}, u32[]{:S(2)}, u32[]{:S(2)}) collective-permute-start(bf16[264,1024]{1,0:T(8,128)(2,1)S(1)} %get-tuple-element.27.refs_0_.own_ref), channel_id=1, source_target_pairs={{0,1},{1,0},{2,3},{3,2},{4,5},{5,4},{6,7},{7,6},{8,9},{9,8},{10,11... | collective-permute-start | bytes 1622024 | tf_op jit(solution)/shard_map/ppermute | solution.py:270
  5.9 12.2 %collective-permute-start.3 = (bf16[128,1024]{1,0:T(8,128)(2,1)S(1)}, bf16[128,1024]{1,0:T(8,128)(2,1)S(1)}, u32[]{:S(2)}, u32[]{:S(2)}) collective-permute-start(bf16[128,1024]{1,0:T(8,128)(2,1)S(1)} %get-tuple-element.28), channel_id=1, source_target_pairs={{0,2},{1,3},{2,0},{3,1},{4,6},{5,7},{6,4},{7,5},{8,10},{9,11},{10,... | collective-permute-start | bytes 786440 | tf_op jit(solution)/shard_map/ppermute | solution.py:270
  6.5 12.0 %collective-permute-start.7 = (bf16[104,1024]{1,0:T(8,128)(2,1)S(1)}, bf16[104,1024]{1,0:T(8,128)(2,1)S(1)}, u32[]{:S(2)}, u32[]{:S(2)}) collective-permute-start(bf16[104,1024]{1,0:T(8,128)(2,1)S(1)} %get-tuple-element.32), channel_id=1, source_target_pairs={{0,4},{1,5},{2,6},{3,7},{4,8},{5,9},{6,10},{7,11},{8,12},{9,13},{1... | collective-permute-start | bytes 638984 | tf_op jit(solution)/shard_map/ppermute | solution.py:274
  14.7 10.8 %collective-permute-start.1 = (bf16[160,1024]{1,0:T(8,128)(2,1)S(1)}, bf16[160,1024]{1,0:T(8,128)(2,1)S(1)}, u32[]{:S(2)}, u32[]{:S(2)}) collective-permute-start(bf16[160,1024]{1,0:T(8,128)(2,1)S(1)} %collective-permute-done.head_ref), channel_id=1, source_target_pairs={{0,5},{1,4},{2,7},{3,6},{4,9},{5,8},{6,11},{7,10},{8,13},{9,12},{1... | collective-permute-start | bytes 983048 | tf_op jit(solution)/shard_map/ppermute | solution.py:274
  14.7 5.0 %collective-permute-start.6 = (bf16[136,1024]{1,0:T(8,128)(2,1)S(1)}, bf16[136,1024]{1,0:T(8,128)(2,1)S(1)}, u32[]{:S(2)}, u32[]{:S(2)}) collective-permute-start(bf16[136,1024]{1,0:T(8,128)(2,1)S(1)} %collective-permute-done.4.refs_3_), channel_id=1, source_target_pairs={{0,1},{1,0},{2,3},{3,2},{4,5},{5,4},{6,7},{7,6},{8,9},{9,8},{10,11... | collective-permute-start | bytes 835592 | tf_op jit(solution)/shard_map/ppermute | solution.py:270
  18.2 1.5 %collective-permute-start.5 = (bf16[128,1024]{1,0:T(8,128)(2,1)S(1)}, bf16[128,1024]{1,0:T(8,128)(2,1)S(1)}, u32[]{:S(2)}, u32[]{:S(2)}) collective-permute-start(bf16[128,1024]{1,0:T(8,128)(2,1)S(1)} %collective-permute-done.3.refs_2_), channel_id=1, source_target_pairs={{0,1},{1,0},{2,3},{3,2},{4,5},{5,4},{6,7},{7,6},{8,9},{9,8},{10,11... | collective-permute-start | bytes 786440 | tf_op jit(solution)/shard_map/ppermute | solution.py:270
  18.5 7.0 %collective-permute-start.8 = (bf16[104,1024]{1,0:T(8,128)(2,1)S(1)}, bf16[104,1024]{1,0:T(8,128)(2,1)S(1)}, u32[]{:S(2)}, u32[]{:S(2)}) collective-permute-start(bf16[104,1024]{1,0:T(8,128)(2,1)S(1)} %collective-permute-done.7.tail_ref), channel_id=1, source_target_pairs={{4,9},{5,8},{6,11},{7,10},{8,13},{9,12},{10,15},{11,14},{20,25},{2... | collective-permute-start | bytes 638984 | tf_op jit(solution)/shard_map/ppermute | solution.py:274
  21.7 5.6 %collective-permute-start.9 = (f32[1,256]{1,0:T(1,128)S(1)}, f32[1,256]{1,0:T(1,128)S(1)}, u32[]{:S(2)}, u32[]{:S(2)}) collective-permute-start(f32[1,256]{1,0:T(1,128)S(1)} %get-tuple-element.42), channel_id=1, source_target_pairs={{4,0},{5,1},{6,2},{7,3},{8,4},{9,5},{10,6},{11,7},{12,8},{13,9},{1... | collective-permute-start | bytes 3080 | tf_op jit(solution)/shard_map/ppermute | solution.py:274
  27.4 6.2 %collective-permute-start.10 = (f32[1,256]{1,0:T(1,128)S(1)}, f32[1,256]{1,0:T(1,128)S(1)}, u32[]{:S(2)}, u32[]{:S(2)}) collective-permute-start(f32[1,256]{1,0:T(1,128)S(1)} %get-tuple-element.45), channel_id=1, source_target_pairs={{8,1},{9,0},{10,3},{11,2},{12,5},{13,4},{14,7},{15,6},{24,17},{25,... | collective-permute-start | bytes 3080 | tf_op jit(solution)/shard_map/ppermute | solution.py:274
  28.9 4.7 %collective-permute-start.11 = (f32[1,256]{1,0:T(1,128)S(1)}, f32[1,256]{1,0:T(1,128)S(1)}, u32[]{:S(2)}, u32[]{:S(2)}) collective-permute-start(f32[1,256]{1,0:T(1,128)S(1)} %get-tuple-element.46), channel_id=1, source_target_pairs={{0,3},{1,2},{2,1},{3,0},{4,7},{5,6},{6,5},{7,4},{8,11},{9,10},{10,... | collective-permute-start | bytes 3080 | tf_op jit(solution)/shard_map/ppermute | solution.py:270
  29.2 4.4 %collective-permute-start.12 = (f32[1,256]{1,0:T(1,128)S(1)}, f32[1,256]{1,0:T(1,128)S(1)}, u32[]{:S(2)}, u32[]{:S(2)}) collective-permute-start(f32[1,256]{1,0:T(1,128)S(1)} %get-tuple-element.47), channel_id=1, source_target_pairs={{0,2},{1,3},{2,0},{3,1},{4,6},{5,7},{6,4},{7,5},{8,10},{9,11},{10,... | collective-permute-start | bytes 3080 | tf_op jit(solution)/shard_map/ppermute | solution.py:270
  30.5 3.0 %collective-permute-start.13 = (f32[1,256]{1,0:T(1,128)S(1)}, f32[1,256]{1,0:T(1,128)S(1)}, u32[]{:S(2)}, u32[]{:S(2)}) collective-permute-start(f32[1,256]{1,0:T(1,128)S(1)} %get-tuple-element.48), channel_id=1, source_target_pairs={{0,1},{1,0},{2,3},{3,2},{4,5},{5,4},{6,7},{7,6},{8,9},{9,8},{10,11... | collective-permute-start | bytes 3080 | tf_op jit(solution)/shard_map/ppermute | solution.py:270

commit v39 on v29

--- a/solution.py
+++ b/solution.py
@@ -82,7 +82,7 @@
 PLANE = 4
 INVERSE_TEMP_BITS = 20.0 * 1.4426950408889634
 ID_ROWS = 8
-VMEM_BYTES = 16 * 1024 * 1024
+VMEM_BYTES = 8 * 1024 * 1024
 
 
 def along_rows(values):

time: 34.3 us -> 34.3 us (level)
  no operation moved by 1% of the time
where the time goes in v39:
time: 34.3 us; the launch traced here: 34.1 us
  waiting for transfers between devices  15.5 us (45%)
  starting transfers between devices  14.1 us (41%)
  Pallas kernels  2.81 us (8%)
  local copies, waits for them, and re-layouts  1.08 us (3%)
  other arithmetic  0.58 us (2%)
    ppermute x6, waiting for transfers between devices, on_line(): return lax.ppermute(value, 'gx', pairs)  11.6 us
    ppermute x6, starting transfers between devices, on_line(): return lax.ppermute(value, 'gx', pairs)  9.63 us
    ppermute x8, starting transfers between devices, in_plane(): return lax.ppermute(value, 'gx', [(i, i ^ step) for i in range(peers)])  4.45 us
    ppermute x8, waiting for transfers between devices, in_plane(): return lax.ppermute(value, 'gx', [(i, i ^ step) for i in range(peers)])  3.87 us
    pallas_call x1, Pallas kernels, grid_plan(): pl.pallas_call(functools.partial(first_kernel, first_moves), out_shape=(l...  2.02 us
    slice x1, local copies, waits for them, and re-layouts, grid_plan(): first_head = on_line(embeddings[:part], first_moves, 0)  1.07 us
  transfers between devices with their start and end apart: 14, of which 7 were waited for; matrix products, arithmetic and copies ran while one was open for 0% of the time, Pallas kernels for 8%

profile of v39, /device:TPU:0, one launch (start us, length us, event | category | flops | bytes accessed | tf_op | source)
XLA Modules:
  0.0 34.1 jit_solution(3535285724224350910)
XLA Ops:
  0.0 0.0 copy-start
  0.0 1.1 %slice.3 = bf16[160,1024]{1,0:T(8,128)(2,1)S(1)} slice(bf16[256,1024]{1,0:T(8,128)(2,1)} %rows_ref.1), slice={[0:160], [0:1024]} | slice | bytes 655360 | tf_op jit(solution)/shard_map/slice | solution.py:285
  1.1 0.0 copy-start.1
  1.1 3.1 %collective-permute-start = (bf16[160,1024]{1,0:T(8,128)(2,1)S(1)}, bf16[160,1024]{1,0:T(8,128)(2,1)S(1)}, u32[]{:S(2)}, u32[]{:S(2)}) collective-permute-start(bf16[160,1024]{1,0:T(8,128)(2,1)S(1)} %slice.3), channel_id=1, source_target_pairs={{0,4},{1,5},{2,6},{3,7},{4,8},{5,9},{6,10},{7,11},{8,12},{9,13},{1... | collective-permute-start | bytes 983048 | tf_op jit(solution)/shard_map/ppermute | solution.py:274
  4.2 0.0 copy-done
  4.2 0.0 copy-done.1
  4.2 0.2 shard_map.28
  4.4 1.6 %collective-permute-start.4 = (bf16[136,1024]{1,0:T(8,128)(2,1)S(1)}, bf16[136,1024]{1,0:T(8,128)(2,1)S(1)}, u32[]{:S(2)}, u32[]{:S(2)}) collective-permute-start(bf16[136,1024]{1,0:T(8,128)(2,1)S(1)} %get-tuple-element.27), channel_id=1, source_target_pairs={{0,2},{1,3},{2,0},{3,1},{4,6},{5,7},{6,4},{7,5},{8,10},{9,11},{10,... | collective-permute-start | bytes 835592 | tf_op jit(solution)/shard_map/ppermute | solution.py:270
  5.9 0.0 collective-permute-start.2
  5.9 0.5 %collective-permute-start.3 = (bf16[128,1024]{1,0:T(8,128)(2,1)S(1)}, bf16[128,1024]{1,0:T(8,128)(2,1)S(1)}, u32[]{:S(2)}, u32[]{:S(2)}) collective-permute-start(bf16[128,1024]{1,0:T(8,128)(2,1)S(1)} %get-tuple-element.26), channel_id=1, source_target_pairs={{0,2},{1,3},{2,0},{3,1},{4,6},{5,7},{6,4},{7,5},{8,10},{9,11},{10,... | collective-permute-start | bytes 786440 | tf_op jit(solution)/shard_map/ppermute | solution.py:270
  6.5 0.3 %shard_map.30.own_mass_ref = f32[1,256]{1,0:T(1,128)S(1)} custom-call(bf16[264,1024]{1,0:T(8,128)(2,1)S(1)} %get-tuple-element.25.refs_0_.own_ref), custom_call_target="tpu_custom_call" | custom-call | flops 1 | bytes 1 | tf_op jit(solution)/shard_map/pallas_call | solution.py:292
  6.8 1.6 %collective-permute-start.7 = (bf16[104,1024]{1,0:T(8,128)(2,1)S(1)}, bf16[104,1024]{1,0:T(8,128)(2,1)S(1)}, u32[]{:S(2)}, u32[]{:S(2)}) collective-permute-start(bf16[104,1024]{1,0:T(8,128)(2,1)S(1)} %get-tuple-element.31), channel_id=1, source_target_pairs={{0,4},{1,5},{2,6},{3,7},{4,8},{5,9},{6,10},{7,11},{8,12},{9,13},{1... | collective-permute-start | bytes 638984 | tf_op jit(solution)/shard_map/ppermute | solution.py:274
  8.4 6.3 %collective-permute-done.head_ref = bf16[160,1024]{1,0:T(8,128)(2,1)S(1)} collective-permute-done((bf16[160,1024]{1,0:T(8,128)(2,1)S(1)}, bf16[160,1024]{1,0:T(8,128)(2,1)S(1)}, u32[]{:S(2)}, u32[]{:S(2)}) %collective-permute-start) | collective-permute-done | bytes 327712 | tf_op jit(solution)/shard_map/ppermute | solution.py:274
  14.7 0.0 collective-permute-start.1
  14.7 0.0 collective-permute-done.4.refs_3_
  14.7 0.1 collective-permute-start.6
  14.9 3.3 %collective-permute-done.3.refs_2_ = bf16[128,1024]{1,0:T(8,128)(2,1)S(1)} collective-permute-done((bf16[128,1024]{1,0:T(8,128)(2,1)S(1)}, bf16[128,1024]{1,0:T(8,128)(2,1)S(1)}, u32[]{:S(2)}, u32[]{:S(2)}) %collective-permute-start.3) | collective-permute-done | bytes 262176 | tf_op jit(solution)/shard_map/ppermute | solution.py:270
  18.2 0.0 collective-permute-start.5
  18.2 0.3 collective-permute-done.7.tail_ref
  18.5 0.7 %collective-permute-start.8 = (bf16[104,1024]{1,0:T(8,128)(2,1)S(1)}, bf16[104,1024]{1,0:T(8,128)(2,1)S(1)}, u32[]{:S(2)}, u32[]{:S(2)}) collective-permute-start(bf16[104,1024]{1,0:T(8,128)(2,1)S(1)} %collective-permute-done.7.tail_ref), channel_id=1, source_target_pairs={{4,9},{5,8},{6,11},{7,10},{8,13},{9,12},{10,15},{11,14},{20,25},{2... | collective-permute-start | bytes 638984 | tf_op jit(solution)/shard_map/ppermute | solution.py:274
  19.1 0.6 %collective-permute-done.5.refs_4_ = bf16[128,1024]{1,0:T(8,128)(2,1)S(1)} collective-permute-done((bf16[128,1024]{1,0:T(8,128)(2,1)S(1)}, bf16[128,1024]{1,0:T(8,128)(2,1)S(1)}, u32[]{:S(2)}, u32[]{:S(2)}) %collective-permute-start.5) | collective-permute-done | bytes 262176 | tf_op jit(solution)/shard_map/ppermute | solution.py:270
  19.7 0.0 collective-permute-done.2.refs_1_
  19.7 0.0 collective-permute-done.6.refs_5_
  19.7 2.0 %shard_map.31 = (f32[1024,128]{1,0:T(8,128)S(1)}, f32[1,256]{1,0:T(1,128)S(1)}, f32[1024,128]{1,0:T(8,128)S(1)}, f32[1,256]{1,0:T(1,128)S(1)}) custom-call(f32[1,256]{1,0:T(1,128)S(1)} %shard_map.30.own_mass_ref, bf16[160,1024]{1,0:T(8,128)(2,1)S(1)} %collective-permute-done.head_ref, bf16[104,1024]{1,0:T(8,128)(2,1)S(1)} %collective-permute-done.7.tail_ref, ...), custom_call_target="tpu_custom_call" | custom-call | flops 1 | bytes 1 | tf_op jit(solution)/shard_map/pallas_call | solution.py:303
  21.7 3.0 %collective-permute-start.9 = (f32[1,256]{1,0:T(1,128)S(1)}, f32[1,256]{1,0:T(1,128)S(1)}, u32[]{:S(2)}, u32[]{:S(2)}) collective-permute-start(f32[1,256]{1,0:T(1,128)S(1)} %get-tuple-element.38), channel_id=1, source_target_pairs={{4,0},{5,1},{6,2},{7,3},{8,4},{9,5},{10,6},{11,7},{12,8},{13,9},{1... | collective-permute-start | bytes 3080 | tf_op jit(solution)/shard_map/ppermute | solution.py:274
  24.7 0.8 %collective-permute-done.1.head_ref = bf16[160,1024]{1,0:T(8,128)(2,1)S(1)} collective-permute-done((bf16[160,1024]{1,0:T(8,128)(2,1)S(1)}, bf16[160,1024]{1,0:T(8,128)(2,1)S(1)}, u32[]{:S(2)}, u32[]{:S(2)}) %collective-permute-start.1) | collective-permute-done | bytes 327712 | tf_op jit(solution)/shard_map/ppermute | solution.py:274
  25.5 0.0 collective-permute-done.8.tail_ref
  25.5 1.5 %collective-permute-done.9 = f32[1,256]{1,0:T(1,128)S(1)} collective-permute-done((f32[1,256]{1,0:T(1,128)S(1)}, f32[1,256]{1,0:T(1,128)S(1)}, u32[]{:S(2)}, u32[]{:S(2)}) %collective-permute-start.9) | collective-permute-done | bytes 1056 | tf_op jit(solution)/shard_map/ppermute | solution.py:274
  27.0 1.3 %collective-permute-start.10 = (f32[1,256]{1,0:T(1,128)S(1)}, f32[1,256]{1,0:T(1,128)S(1)}, u32[]{:S(2)}, u32[]{:S(2)}) collective-permute-start(f32[1,256]{1,0:T(1,128)S(1)} %get-tuple-element.41), channel_id=1, source_target_pairs={{8,1},{9,0},{10,3},{11,2},{12,5},{13,4},{14,7},{15,6},{24,17},{25,... | collective-permute-start | bytes 3080 | tf_op jit(solution)/shard_map/ppermute | solution.py:274
  28.3 0.2 shard_map.33
  28.5 1.6 %collective-permute-start.11 = (f32[1,256]{1,0:T(1,128)S(1)}, f32[1,256]{1,0:T(1,128)S(1)}, u32[]{:S(2)}, u32[]{:S(2)}) collective-permute-start(f32[1,256]{1,0:T(1,128)S(1)} %get-tuple-element.42), channel_id=1, source_target_pairs={{0,2},{1,3},{2,0},{3,1},{4,6},{5,7},{6,4},{7,5},{8,10},{9,11},{10,... | collective-permute-start | bytes 3080 | tf_op jit(solution)/shard_map/ppermute | solution.py:270
  30.1 0.0 collective-permute-start.12
  30.1 0.6 %collective-permute-start.13 = (f32[1,256]{1,0:T(1,128)S(1)}, f32[1,256]{1,0:T(1,128)S(1)}, u32[]{:S(2)}, u32[]{:S(2)}) collective-permute-start(f32[1,256]{1,0:T(1,128)S(1)} %get-tuple-element.44), channel_id=1, source_target_pairs={{0,1},{1,0},{2,3},{3,2},{4,5},{5,4},{6,7},{7,6},{8,9},{9,8},{10,11... | collective-permute-start | bytes 3080 | tf_op jit(solution)/shard_map/ppermute | solution.py:270
  30.7 2.8 %collective-permute-done.10 = f32[1,256]{1,0:T(1,128)S(1)} collective-permute-done((f32[1,256]{1,0:T(1,128)S(1)}, f32[1,256]{1,0:T(1,128)S(1)}, u32[]{:S(2)}, u32[]{:S(2)}) %collective-permute-start.10) | collective-permute-done | bytes 1056 | tf_op jit(solution)/shard_map/ppermute | solution.py:274
  33.5 0.0 collective-permute-done.11
  33.5 0.0 collective-permute-done.12
  33.5 0.0 collective-permute-done.13
  33.5 0.6 %add_log-plus-one_fusion = f32[1,256]{1,0:T(1,128)} fusion(f32[1,256]{1,0:T(1,128)S(1)} %collective-permute-done.13, f32[1,256]{1,0:T(1,128)S(1)} %collective-permute-done.12, f32[1,256]{1,0:T(1,128)S(1)} %collective-permute-done.11, f32[1,256]{1,0:T(1,128)S(1)} %collective-permute-done.10, f32[1,256]{1,0:T(1,128)S(1)} %get-tuple-element.37, ...), kind=kLoop, calls=%fused_computation | loop fusion | flops 1280 | bytes 7168 | tf_op jit(solution)/shard_map/log1p | solution.py:333
  (2 shorter events, 0.0 us)
Async XLA Ops:
  0.0 4.2 %copy-start = (bf16[256,1024]{1,0:T(8,128)(2,1)S(1)}, bf16[256,1024]{1,0:T(8,128)(2,1)}, u32[]{:S(2)}) copy-start(bf16[256,1024]{1,0:T(8,128)(2,1)} %rows_ref.1) | copy-start | bytes 1572868
  1.1 3.1 %copy-start.1 = (s32[256]{0:T(256)S(1)}, s32[256]{0:T(256)}, u32[]{:S(2)}) copy-start(s32[256]{0:T(256)} %param.3) | copy-start | bytes 3076
  1.1 13.6 %collective-permute-start = (bf16[160,1024]{1,0:T(8,128)(2,1)S(1)}, bf16[160,1024]{1,0:T(8,128)(2,1)S(1)}, u32[]{:S(2)}, u32[]{:S(2)}) collective-permute-start(bf16[160,1024]{1,0:T(8,128)(2,1)S(1)} %slice.3), channel_id=1, source_target_pairs={{0,4},{1,5},{2,6},{3,7},{4,8},{5,9},{6,10},{7,11},{8,12},{9,13},{1... | collective-permute-start | bytes 983048 | tf_op jit(solution)/shard_map/ppermute | solution.py:274
  4.4 10.4 %collective-permute-start.4 = (bf16[136,1024]{1,0:T(8,128)(2,1)S(1)}, bf16[136,1024]{1,0:T(8,128)(2,1)S(1)}, u32[]{:S(2)}, u32[]{:S(2)}) collective-permute-start(bf16[136,1024]{1,0:T(8,128)(2,1)S(1)} %get-tuple-element.27), channel_id=1, source_target_pairs={{0,2},{1,3},{2,0},{3,1},{4,6},{5,7},{6,4},{7,5},{8,10},{9,11},{10,... | collective-permute-start | bytes 835592 | tf_op jit(solution)/shard_map/ppermute | solution.py:270
  5.9 13.8 %collective-permute-start.2 = (bf16[264,1024]{1,0:T(8,128)(2,1)S(1)}, bf16[264,1024]{1,0:T(8,128)(2,1)S(1)}, u32[]{:S(2)}, u32[]{:S(2)}) collective-permute-start(bf16[264,1024]{1,0:T(8,128)(2,1)S(1)} %get-tuple-element.25.refs_0_.own_ref), channel_id=1, source_target_pairs={{0,1},{1,0},{2,3},{3,2},{4,5},{5,4},{6,7},{7,6},{8,9},{9,8},{10,11... | collective-permute-start | bytes 1622024 | tf_op jit(solution)/shard_map/ppermute | solution.py:270
  5.9 12.2 %collective-permute-start.3 = (bf16[128,1024]{1,0:T(8,128)(2,1)S(1)}, bf16[128,1024]{1,0:T(8,128)(2,1)S(1)}, u32[]{:S(2)}, u32[]{:S(2)}) collective-permute-start(bf16[128,1024]{1,0:T(8,128)(2,1)S(1)} %get-tuple-element.26), channel_id=1, source_target_pairs={{0,2},{1,3},{2,0},{3,1},{4,6},{5,7},{6,4},{7,5},{8,10},{9,11},{10,... | collective-permute-start | bytes 786440 | tf_op jit(solution)/shard_map/ppermute | solution.py:270
  6.8 11.6 %collective-permute-start.7 = (bf16[104,1024]{1,0:T(8,128)(2,1)S(1)}, bf16[104,1024]{1,0:T(8,128)(2,1)S(1)}, u32[]{:S(2)}, u32[]{:S(2)}) collective-permute-start(bf16[104,1024]{1,0:T(8,128)(2,1)S(1)} %get-tuple-element.31), channel_id=1, source_target_pairs={{0,4},{1,5},{2,6},{3,7},{4,8},{5,9},{6,10},{7,11},{8,12},{9,13},{1... | collective-permute-start | bytes 638984 | tf_op jit(solution)/shard_map/ppermute | solution.py:274
  14.7 10.8 %collective-permute-start.1 = (bf16[160,1024]{1,0:T(8,128)(2,1)S(1)}, bf16[160,1024]{1,0:T(8,128)(2,1)S(1)}, u32[]{:S(2)}, u32[]{:S(2)}) collective-permute-start(bf16[160,1024]{1,0:T(8,128)(2,1)S(1)} %collective-permute-done.head_ref), channel_id=1, source_target_pairs={{0,5},{1,4},{2,7},{3,6},{4,9},{5,8},{6,11},{7,10},{8,13},{9,12},{1... | collective-permute-start | bytes 983048 | tf_op jit(solution)/shard_map/ppermute | solution.py:274
  14.7 5.0 %collective-permute-start.6 = (bf16[136,1024]{1,0:T(8,128)(2,1)S(1)}, bf16[136,1024]{1,0:T(8,128)(2,1)S(1)}, u32[]{:S(2)}, u32[]{:S(2)}) collective-permute-start(bf16[136,1024]{1,0:T(8,128)(2,1)S(1)} %collective-permute-done.4.refs_3_), channel_id=1, source_target_pairs={{0,1},{1,0},{2,3},{3,2},{4,5},{5,4},{6,7},{7,6},{8,9},{9,8},{10,11... | collective-permute-start | bytes 835592 | tf_op jit(solution)/shard_map/ppermute | solution.py:270
  18.2 1.5 %collective-permute-start.5 = (bf16[128,1024]{1,0:T(8,128)(2,1)S(1)}, bf16[128,1024]{1,0:T(8,128)(2,1)S(1)}, u32[]{:S(2)}, u32[]{:S(2)}) collective-permute-start(bf16[128,1024]{1,0:T(8,128)(2,1)S(1)} %collective-permute-done.3.refs_2_), channel_id=1, source_target_pairs={{0,1},{1,0},{2,3},{3,2},{4,5},{5,4},{6,7},{7,6},{8,9},{9,8},{10,11... | collective-permute-start | bytes 786440 | tf_op jit(solution)/shard_map/ppermute | solution.py:270
  18.5 7.0 %collective-permute-start.8 = (bf16[104,1024]{1,0:T(8,128)(2,1)S(1)}, bf16[104,1024]{1,0:T(8,128)(2,1)S(1)}, u32[]{:S(2)}, u32[]{:S(2)}) collective-permute-start(bf16[104,1024]{1,0:T(8,128)(2,1)S(1)} %collective-permute-done.7.tail_ref), channel_id=1, source_target_pairs={{4,9},{5,8},{6,11},{7,10},{8,13},{9,12},{10,15},{11,14},{20,25},{2... | collective-permute-start | bytes 638984 | tf_op jit(solution)/shard_map/ppermute | solution.py:274
  21.7 5.3 %collective-permute-start.9 = (f32[1,256]{1,0:T(1,128)S(1)}, f32[1,256]{1,0:T(1,128)S(1)}, u32[]{:S(2)}, u32[]{:S(2)}) collective-permute-start(f32[1,256]{1,0:T(1,128)S(1)} %get-tuple-element.38), channel_id=1, source_target_pairs={{4,0},{5,1},{6,2},{7,3},{8,4},{9,5},{10,6},{11,7},{12,8},{13,9},{1... | collective-permute-start | bytes 3080 | tf_op jit(solution)/shard_map/ppermute | solution.py:274
  27.0 6.5 %collective-permute-start.10 = (f32[1,256]{1,0:T(1,128)S(1)}, f32[1,256]{1,0:T(1,128)S(1)}, u32[]{:S(2)}, u32[]{:S(2)}) collective-permute-start(f32[1,256]{1,0:T(1,128)S(1)} %get-tuple-element.41), channel_id=1, source_target_pairs={{8,1},{9,0},{10,3},{11,2},{12,5},{13,4},{14,7},{15,6},{24,17},{25,... | collective-permute-start | bytes 3080 | tf_op jit(solution)/shard_map/ppermute | solution.py:274
  28.5 5.0 %collective-permute-start.11 = (f32[1,256]{1,0:T(1,128)S(1)}, f32[1,256]{1,0:T(1,128)S(1)}, u32[]{:S(2)}, u32[]{:S(2)}) collective-permute-start(f32[1,256]{1,0:T(1,128)S(1)} %get-tuple-element.42), channel_id=1, source_target_pairs={{0,2},{1,3},{2,0},{3,1},{4,6},{5,7},{6,4},{7,5},{8,10},{9,11},{10,... | collective-permute-start | bytes 3080 | tf_op jit(solution)/shard_map/ppermute | solution.py:270
  30.1 3.5 %collective-permute-start.12 = (f32[1,256]{1,0:T(1,128)S(1)}, f32[1,256]{1,0:T(1,128)S(1)}, u32[]{:S(2)}, u32[]{:S(2)}) collective-permute-start(f32[1,256]{1,0:T(1,128)S(1)} %get-tuple-element.43), channel_id=1, source_target_pairs={{0,3},{1,2},{2,1},{3,0},{4,7},{5,6},{6,5},{7,4},{8,11},{9,10},{10,... | collective-permute-start | bytes 3080 | tf_op jit(solution)/shard_map/ppermute | solution.py:270
  30.1 3.5 %collective-permute-start.13 = (f32[1,256]{1,0:T(1,128)S(1)}, f32[1,256]{1,0:T(1,128)S(1)}, u32[]{:S(2)}, u32[]{:S(2)}) collective-permute-start(f32[1,256]{1,0:T(1,128)S(1)} %get-tuple-element.44), channel_id=1, source_target_pairs={{0,1},{1,0},{2,3},{3,2},{4,5},{5,4},{6,7},{7,6},{8,9},{9,8},{10,11... | collective-permute-start | bytes 3080 | tf_op jit(solution)/shard_map/ppermute | solution.py:270

commit v40 on v31

--- a/solution.py
+++ b/solution.py
@@ -329,7 +329,7 @@
         compiler_params=params,
     )(sums, mass)
     returned = [on_line(last_column, last_back, 1)]
-    returned += [in_plane(row_sums[step], step) for step in (3, 2, 1)]
+    returned += [in_plane(row_sums[step], step) for step in (1, 3, 2)]
     return jnp.log1p(sum(returned, row_sums[0] + returned_first)).reshape(row_count)
 
 

time: 34.4 us -> 34.7 us (level)
  transfers between devices with their start and end apart: 14 -> 14, of which waited for: 7 -> 8; matrix products, arithmetic and copies ran while one was open for 0% -> 0% of each run, Pallas kernels for 8% -> 8%
where the time goes in v40:
time: 34.7 us; the launch traced here: 34.3 us
  waiting for transfers between devices  15.7 us (45%)
  starting transfers between devices  14.1 us (41%)
  Pallas kernels  2.81 us (8%)
  local copies, waits for them, and re-layouts  1.08 us (3%)
  other arithmetic  0.58 us (2%)
    ppermute x6, waiting for transfers between devices, on_line(): return lax.ppermute(value, 'gx', pairs)  11.6 us
    ppermute x6, starting transfers between devices, on_line(): return lax.ppermute(value, 'gx', pairs)  9.63 us
    ppermute x8, starting transfers between devices, in_plane(): return lax.ppermute(value, 'gx', [(i, i ^ step) for i in range(peers)])  4.46 us
    ppermute x8, waiting for transfers between devices, in_plane(): return lax.ppermute(value, 'gx', [(i, i ^ step) for i in range(peers)])  4.09 us
    pallas_call x1, Pallas kernels, grid_plan(): pl.pallas_call(functools.partial(first_kernel, first_moves), out_shape=(l...  2.02 us
    slice x1, local copies, waits for them, and re-layouts, grid_plan(): first_head = on_line(embeddings[:part], first_moves, 0)  1.07 us
  transfers between devices with their start and end apart: 14, of which 8 were waited for; matrix products, arithmetic and copies ran while one was open for 0% of the time, Pallas kernels for 8%

profile of v40, /device:TPU:0, one launch (start us, length us, event | category | flops | bytes accessed | tf_op | source)
XLA Modules:
  0.0 34.3 jit_solution(3977743757459598319)
XLA Ops:
  0.0 0.0 copy-start
  0.0 1.1 %slice.3 = bf16[160,1024]{1,0:T(8,128)(2,1)S(1)} slice(bf16[256,1024]{1,0:T(8,128)(2,1)} %rows_ref.1), slice={[0:160], [0:1024]} | slice | bytes 655360 | tf_op jit(solution)/shard_map/slice | solution.py:285
  1.1 0.0 copy-start.1
  1.1 3.1 %collective-permute-start = (bf16[160,1024]{1,0:T(8,128)(2,1)S(1)}, bf16[160,1024]{1,0:T(8,128)(2,1)S(1)}, u32[]{:S(2)}, u32[]{:S(2)}) collective-permute-start(bf16[160,1024]{1,0:T(8,128)(2,1)S(1)} %slice.3), channel_id=1, source_target_pairs={{0,4},{1,5},{2,6},{3,7},{4,8},{5,9},{6,10},{7,11},{8,12},{9,13},{1... | collective-permute-start | bytes 983048 | tf_op jit(solution)/shard_map/ppermute | solution.py:274
  4.2 0.0 copy-done
  4.2 0.0 copy-done.1
  4.2 0.2 shard_map.28
  4.4 1.6 %collective-permute-start.4 = (bf16[136,1024]{1,0:T(8,128)(2,1)S(1)}, bf16[136,1024]{1,0:T(8,128)(2,1)S(1)}, u32[]{:S(2)}, u32[]{:S(2)}) collective-permute-start(bf16[136,1024]{1,0:T(8,128)(2,1)S(1)} %get-tuple-element.27), channel_id=1, source_target_pairs={{0,2},{1,3},{2,0},{3,1},{4,6},{5,7},{6,4},{7,5},{8,10},{9,11},{10,... | collective-permute-start | bytes 835592 | tf_op jit(solution)/shard_map/ppermute | solution.py:270
  5.9 0.0 collective-permute-start.2
  5.9 0.5 %collective-permute-start.3 = (bf16[128,1024]{1,0:T(8,128)(2,1)S(1)}, bf16[128,1024]{1,0:T(8,128)(2,1)S(1)}, u32[]{:S(2)}, u32[]{:S(2)}) collective-permute-start(bf16[128,1024]{1,0:T(8,128)(2,1)S(1)} %get-tuple-element.26), channel_id=1, source_target_pairs={{0,2},{1,3},{2,0},{3,1},{4,6},{5,7},{6,4},{7,5},{8,10},{9,11},{10,... | collective-permute-start | bytes 786440 | tf_op jit(solution)/shard_map/ppermute | solution.py:270
  6.5 0.3 %shard_map.30.own_mass_ref = f32[1,256]{1,0:T(1,128)S(1)} custom-call(bf16[264,1024]{1,0:T(8,128)(2,1)S(1)} %get-tuple-element.25.refs_0_.own_ref), custom_call_target="tpu_custom_call" | custom-call | flops 1 | bytes 1 | tf_op jit(solution)/shard_map/pallas_call | solution.py:292
  6.8 1.6 %collective-permute-start.7 = (bf16[104,1024]{1,0:T(8,128)(2,1)S(1)}, bf16[104,1024]{1,0:T(8,128)(2,1)S(1)}, u32[]{:S(2)}, u32[]{:S(2)}) collective-permute-start(bf16[104,1024]{1,0:T(8,128)(2,1)S(1)} %get-tuple-element.31), channel_id=1, source_target_pairs={{0,4},{1,5},{2,6},{3,7},{4,8},{5,9},{6,10},{7,11},{8,12},{9,13},{1... | collective-permute-start | bytes 638984 | tf_op jit(solution)/shard_map/ppermute | solution.py:274
  8.4 6.3 %collective-permute-done.head_ref = bf16[160,1024]{1,0:T(8,128)(2,1)S(1)} collective-permute-done((bf16[160,1024]{1,0:T(8,128)(2,1)S(1)}, bf16[160,1024]{1,0:T(8,128)(2,1)S(1)}, u32[]{:S(2)}, u32[]{:S(2)}) %collective-permute-start) | collective-permute-done | bytes 327712 | tf_op jit(solution)/shard_map/ppermute | solution.py:274
  14.7 0.0 collective-permute-start.1
  14.7 0.0 collective-permute-done.4.refs_3_
  14.7 0.1 collective-permute-start.6
  14.9 3.3 %collective-permute-done.3.refs_2_ = bf16[128,1024]{1,0:T(8,128)(2,1)S(1)} collective-permute-done((bf16[128,1024]{1,0:T(8,128)(2,1)S(1)}, bf16[128,1024]{1,0:T(8,128)(2,1)S(1)}, u32[]{:S(2)}, u32[]{:S(2)}) %collective-permute-start.3) | collective-permute-done | bytes 262176 | tf_op jit(solution)/shard_map/ppermute | solution.py:270
  18.2 0.0 collective-permute-start.5
  18.2 0.3 collective-permute-done.7.tail_ref
  18.5 0.7 %collective-permute-start.8 = (bf16[104,1024]{1,0:T(8,128)(2,1)S(1)}, bf16[104,1024]{1,0:T(8,128)(2,1)S(1)}, u32[]{:S(2)}, u32[]{:S(2)}) collective-permute-start(bf16[104,1024]{1,0:T(8,128)(2,1)S(1)} %collective-permute-done.7.tail_ref), channel_id=1, source_target_pairs={{4,9},{5,8},{6,11},{7,10},{8,13},{9,12},{10,15},{11,14},{20,25},{2... | collective-permute-start | bytes 638984 | tf_op jit(solution)/shard_map/ppermute | solution.py:274
  19.1 0.6 %collective-permute-done.5.refs_4_ = bf16[128,1024]{1,0:T(8,128)(2,1)S(1)} collective-permute-done((bf16[128,1024]{1,0:T(8,128)(2,1)S(1)}, bf16[128,1024]{1,0:T(8,128)(2,1)S(1)}, u32[]{:S(2)}, u32[]{:S(2)}) %collective-permute-start.5) | collective-permute-done | bytes 262176 | tf_op jit(solution)/shard_map/ppermute | solution.py:270
  19.7 0.0 collective-permute-done.2.refs_1_
  19.7 0.0 collective-permute-done.6.refs_5_
  19.7 2.0 %shard_map.31 = (f32[1024,128]{1,0:T(8,128)S(1)}, f32[1,256]{1,0:T(1,128)S(1)}, f32[1024,128]{1,0:T(8,128)S(1)}, f32[1,256]{1,0:T(1,128)S(1)}) custom-call(f32[1,256]{1,0:T(1,128)S(1)} %shard_map.30.own_mass_ref, bf16[160,1024]{1,0:T(8,128)(2,1)S(1)} %collective-permute-done.head_ref, bf16[104,1024]{1,0:T(8,128)(2,1)S(1)} %collective-permute-done.7.tail_ref, ...), custom_call_target="tpu_custom_call" | custom-call | flops 1 | bytes 1 | tf_op jit(solution)/shard_map/pallas_call | solution.py:303
  21.7 3.0 %collective-permute-start.9 = (f32[1,256]{1,0:T(1,128)S(1)}, f32[1,256]{1,0:T(1,128)S(1)}, u32[]{:S(2)}, u32[]{:S(2)}) collective-permute-start(f32[1,256]{1,0:T(1,128)S(1)} %get-tuple-element.38), channel_id=1, source_target_pairs={{4,0},{5,1},{6,2},{7,3},{8,4},{9,5},{10,6},{11,7},{12,8},{13,9},{1... | collective-permute-start | bytes 3080 | tf_op jit(solution)/shard_map/ppermute | solution.py:274
  24.7 0.8 %collective-permute-done.1.head_ref = bf16[160,1024]{1,0:T(8,128)(2,1)S(1)} collective-permute-done((bf16[160,1024]{1,0:T(8,128)(2,1)S(1)}, bf16[160,1024]{1,0:T(8,128)(2,1)S(1)}, u32[]{:S(2)}, u32[]{:S(2)}) %collective-permute-start.1) | collective-permute-done | bytes 327712 | tf_op jit(solution)/shard_map/ppermute | solution.py:274
  25.5 0.0 collective-permute-done.8.tail_ref
  25.5 1.5 %collective-permute-done.9 = f32[1,256]{1,0:T(1,128)S(1)} collective-permute-done((f32[1,256]{1,0:T(1,128)S(1)}, f32[1,256]{1,0:T(1,128)S(1)}, u32[]{:S(2)}, u32[]{:S(2)}) %collective-permute-start.9) | collective-permute-done | bytes 1056 | tf_op jit(solution)/shard_map/ppermute | solution.py:274
  27.0 1.3 %collective-permute-start.10 = (f32[1,256]{1,0:T(1,128)S(1)}, f32[1,256]{1,0:T(1,128)S(1)}, u32[]{:S(2)}, u32[]{:S(2)}) collective-permute-start(f32[1,256]{1,0:T(1,128)S(1)} %get-tuple-element.41), channel_id=1, source_target_pairs={{8,1},{9,0},{10,3},{11,2},{12,5},{13,4},{14,7},{15,6},{24,17},{25,... | collective-permute-start | bytes 3080 | tf_op jit(solution)/shard_map/ppermute | solution.py:274
  28.3 0.2 shard_map.33
  28.5 0.1 collective-permute-start.11
  28.6 1.6 %collective-permute-start.12 = (f32[1,256]{1,0:T(1,128)S(1)}, f32[1,256]{1,0:T(1,128)S(1)}, u32[]{:S(2)}, u32[]{:S(2)}) collective-permute-start(f32[1,256]{1,0:T(1,128)S(1)} %get-tuple-element.43), channel_id=1, source_target_pairs={{0,3},{1,2},{2,1},{3,0},{4,7},{5,6},{6,5},{7,4},{8,11},{9,10},{10,... | collective-permute-start | bytes 3080 | tf_op jit(solution)/shard_map/ppermute | solution.py:270
  30.2 0.5 %collective-permute-start.13 = (f32[1,256]{1,0:T(1,128)S(1)}, f32[1,256]{1,0:T(1,128)S(1)}, u32[]{:S(2)}, u32[]{:S(2)}) collective-permute-start(f32[1,256]{1,0:T(1,128)S(1)} %get-tuple-element.44), channel_id=1, source_target_pairs={{0,2},{1,3},{2,0},{3,1},{4,6},{5,7},{6,4},{7,5},{8,10},{9,11},{10,... | collective-permute-start | bytes 3080 | tf_op jit(solution)/shard_map/ppermute | solution.py:270
  30.7 2.8 %collective-permute-done.10 = f32[1,256]{1,0:T(1,128)S(1)} collective-permute-done((f32[1,256]{1,0:T(1,128)S(1)}, f32[1,256]{1,0:T(1,128)S(1)}, u32[]{:S(2)}, u32[]{:S(2)}) %collective-permute-start.10) | collective-permute-done | bytes 1056 | tf_op jit(solution)/shard_map/ppermute | solution.py:274
  33.5 0.0 collective-permute-done.11
  33.5 0.0 collective-permute-done.12
  33.5 0.2 collective-permute-done.13
  33.8 0.6 %add_log-plus-one_fusion = f32[1,256]{1,0:T(1,128)} fusion(f32[1,256]{1,0:T(1,128)S(1)} %collective-permute-done.13, f32[1,256]{1,0:T(1,128)S(1)} %collective-permute-done.12, f32[1,256]{1,0:T(1,128)S(1)} %collective-permute-done.11, f32[1,256]{1,0:T(1,128)S(1)} %collective-permute-done.10, f32[1,256]{1,0:T(1,128)S(1)} %get-tuple-element.37, ...), kind=kLoop, calls=%fused_computation | loop fusion | flops 1280 | bytes 7168 | tf_op jit(solution)/shard_map/log1p | solution.py:333
  (2 shorter events, 0.0 us)
Async XLA Ops:
  0.0 4.2 %copy-start = (bf16[256,1024]{1,0:T(8,128)(2,1)S(1)}, bf16[256,1024]{1,0:T(8,128)(2,1)}, u32[]{:S(2)}) copy-start(bf16[256,1024]{1,0:T(8,128)(2,1)} %rows_ref.1) | copy-start | bytes 1572868
  1.1 3.1 %copy-start.1 = (s32[256]{0:T(256)S(1)}, s32[256]{0:T(256)}, u32[]{:S(2)}) copy-start(s32[256]{0:T(256)} %param.3) | copy-start | bytes 3076
  1.1 13.6 %collective-permute-start = (bf16[160,1024]{1,0:T(8,128)(2,1)S(1)}, bf16[160,1024]{1,0:T(8,128)(2,1)S(1)}, u32[]{:S(2)}, u32[]{:S(2)}) collective-permute-start(bf16[160,1024]{1,0:T(8,128)(2,1)S(1)} %slice.3), channel_id=1, source_target_pairs={{0,4},{1,5},{2,6},{3,7},{4,8},{5,9},{6,10},{7,11},{8,12},{9,13},{1... | collective-permute-start | bytes 983048 | tf_op jit(solution)/shard_map/ppermute | solution.py:274
  4.4 10.4 %collective-permute-start.4 = (bf16[136,1024]{1,0:T(8,128)(2,1)S(1)}, bf16[136,1024]{1,0:T(8,128)(2,1)S(1)}, u32[]{:S(2)}, u32[]{:S(2)}) collective-permute-start(bf16[136,1024]{1,0:T(8,128)(2,1)S(1)} %get-tuple-element.27), channel_id=1, source_target_pairs={{0,2},{1,3},{2,0},{3,1},{4,6},{5,7},{6,4},{7,5},{8,10},{9,11},{10,... | collective-permute-start | bytes 835592 | tf_op jit(solution)/shard_map/ppermute | solution.py:270
  5.9 13.8 %collective-permute-start.2 = (bf16[264,1024]{1,0:T(8,128)(2,1)S(1)}, bf16[264,1024]{1,0:T(8,128)(2,1)S(1)}, u32[]{:S(2)}, u32[]{:S(2)}) collective-permute-start(bf16[264,1024]{1,0:T(8,128)(2,1)S(1)} %get-tuple-element.25.refs_0_.own_ref), channel_id=1, source_target_pairs={{0,1},{1,0},{2,3},{3,2},{4,5},{5,4},{6,7},{7,6},{8,9},{9,8},{10,11... | collective-permute-start | bytes 1622024 | tf_op jit(solution)/shard_map/ppermute | solution.py:270
  5.9 12.2 %collective-permute-start.3 = (bf16[128,1024]{1,0:T(8,128)(2,1)S(1)}, bf16[128,1024]{1,0:T(8,128)(2,1)S(1)}, u32[]{:S(2)}, u32[]{:S(2)}) collective-permute-start(bf16[128,1024]{1,0:T(8,128)(2,1)S(1)} %get-tuple-element.26), channel_id=1, source_target_pairs={{0,2},{1,3},{2,0},{3,1},{4,6},{5,7},{6,4},{7,5},{8,10},{9,11},{10,... | collective-permute-start | bytes 786440 | tf_op jit(solution)/shard_map/ppermute | solution.py:270
  6.8 11.6 %collective-permute-start.7 = (bf16[104,1024]{1,0:T(8,128)(2,1)S(1)}, bf16[104,1024]{1,0:T(8,128)(2,1)S(1)}, u32[]{:S(2)}, u32[]{:S(2)}) collective-permute-start(bf16[104,1024]{1,0:T(8,128)(2,1)S(1)} %get-tuple-element.31), channel_id=1, source_target_pairs={{0,4},{1,5},{2,6},{3,7},{4,8},{5,9},{6,10},{7,11},{8,12},{9,13},{1... | collective-permute-start | bytes 638984 | tf_op jit(solution)/shard_map/ppermute | solution.py:274
  14.7 10.8 %collective-permute-start.1 = (bf16[160,1024]{1,0:T(8,128)(2,1)S(1)}, bf16[160,1024]{1,0:T(8,128)(2,1)S(1)}, u32[]{:S(2)}, u32[]{:S(2)}) collective-permute-start(bf16[160,1024]{1,0:T(8,128)(2,1)S(1)} %collective-permute-done.head_ref), channel_id=1, source_target_pairs={{0,5},{1,4},{2,7},{3,6},{4,9},{5,8},{6,11},{7,10},{8,13},{9,12},{1... | collective-permute-start | bytes 983048 | tf_op jit(solution)/shard_map/ppermute | solution.py:274
  14.7 5.0 %collective-permute-start.6 = (bf16[136,1024]{1,0:T(8,128)(2,1)S(1)}, bf16[136,1024]{1,0:T(8,128)(2,1)S(1)}, u32[]{:S(2)}, u32[]{:S(2)}) collective-permute-start(bf16[136,1024]{1,0:T(8,128)(2,1)S(1)} %collective-permute-done.4.refs_3_), channel_id=1, source_target_pairs={{0,1},{1,0},{2,3},{3,2},{4,5},{5,4},{6,7},{7,6},{8,9},{9,8},{10,11... | collective-permute-start | bytes 835592 | tf_op jit(solution)/shard_map/ppermute | solution.py:270
  18.2 1.5 %collective-permute-start.5 = (bf16[128,1024]{1,0:T(8,128)(2,1)S(1)}, bf16[128,1024]{1,0:T(8,128)(2,1)S(1)}, u32[]{:S(2)}, u32[]{:S(2)}) collective-permute-start(bf16[128,1024]{1,0:T(8,128)(2,1)S(1)} %collective-permute-done.3.refs_2_), channel_id=1, source_target_pairs={{0,1},{1,0},{2,3},{3,2},{4,5},{5,4},{6,7},{7,6},{8,9},{9,8},{10,11... | collective-permute-start | bytes 786440 | tf_op jit(solution)/shard_map/ppermute | solution.py:270
  18.5 7.0 %collective-permute-start.8 = (bf16[104,1024]{1,0:T(8,128)(2,1)S(1)}, bf16[104,1024]{1,0:T(8,128)(2,1)S(1)}, u32[]{:S(2)}, u32[]{:S(2)}) collective-permute-start(bf16[104,1024]{1,0:T(8,128)(2,1)S(1)} %collective-permute-done.7.tail_ref), channel_id=1, source_target_pairs={{4,9},{5,8},{6,11},{7,10},{8,13},{9,12},{10,15},{11,14},{20,25},{2... | collective-permute-start | bytes 638984 | tf_op jit(solution)/shard_map/ppermute | solution.py:274
  21.7 5.3 %collective-permute-start.9 = (f32[1,256]{1,0:T(1,128)S(1)}, f32[1,256]{1,0:T(1,128)S(1)}, u32[]{:S(2)}, u32[]{:S(2)}) collective-permute-start(f32[1,256]{1,0:T(1,128)S(1)} %get-tuple-element.38), channel_id=1, source_target_pairs={{4,0},{5,1},{6,2},{7,3},{8,4},{9,5},{10,6},{11,7},{12,8},{13,9},{1... | collective-permute-start | bytes 3080 | tf_op jit(solution)/shard_map/ppermute | solution.py:274
  27.0 6.5 %collective-permute-start.10 = (f32[1,256]{1,0:T(1,128)S(1)}, f32[1,256]{1,0:T(1,128)S(1)}, u32[]{:S(2)}, u32[]{:S(2)}) collective-permute-start(f32[1,256]{1,0:T(1,128)S(1)} %get-tuple-element.41), channel_id=1, source_target_pairs={{8,1},{9,0},{10,3},{11,2},{12,5},{13,4},{14,7},{15,6},{24,17},{25,... | collective-permute-start | bytes 3080 | tf_op jit(solution)/shard_map/ppermute | solution.py:274
  28.5 5.0 %collective-permute-start.11 = (f32[1,256]{1,0:T(1,128)S(1)}, f32[1,256]{1,0:T(1,128)S(1)}, u32[]{:S(2)}, u32[]{:S(2)}) collective-permute-start(f32[1,256]{1,0:T(1,128)S(1)} %get-tuple-element.42), channel_id=1, source_target_pairs={{0,1},{1,0},{2,3},{3,2},{4,5},{5,4},{6,7},{7,6},{8,9},{9,8},{10,11... | collective-permute-start | bytes 3080 | tf_op jit(solution)/shard_map/ppermute | solution.py:270
  28.6 5.0 %collective-permute-start.12 = (f32[1,256]{1,0:T(1,128)S(1)}, f32[1,256]{1,0:T(1,128)S(1)}, u32[]{:S(2)}, u32[]{:S(2)}) collective-permute-start(f32[1,256]{1,0:T(1,128)S(1)} %get-tuple-element.43), channel_id=1, source_target_pairs={{0,3},{1,2},{2,1},{3,0},{4,7},{5,6},{6,5},{7,4},{8,11},{9,10},{10,... | collective-permute-start | bytes 3080 | tf_op jit(solution)/shard_map/ppermute | solution.py:270
  30.2 3.6 %collective-permute-start.13 = (f32[1,256]{1,0:T(1,128)S(1)}, f32[1,256]{1,0:T(1,128)S(1)}, u32[]{:S(2)}, u32[]{:S(2)}) collective-permute-start(f32[1,256]{1,0:T(1,128)S(1)} %get-tuple-element.44), channel_id=1, source_target_pairs={{0,2},{1,3},{2,0},{3,1},{4,6},{5,7},{6,4},{7,5},{8,10},{9,11},{10,... | collective-permute-start | bytes 3080 | tf_op jit(solution)/shard_map/ppermute | solution.py:270

commit v41 on v40

--- a/solution.py
+++ b/solution.py
@@ -328,8 +328,8 @@
         cost_estimate=small,
         compiler_params=params,
     )(sums, mass)
-    returned = [on_line(last_column, last_back, 1)]
-    returned += [in_plane(row_sums[step], step) for step in (1, 3, 2)]
+    returned = [in_plane(row_sums[step], step) for step in (2, 3, 1)]
+    returned += [on_line(last_column, last_back, 1)]
     return jnp.log1p(sum(returned, row_sums[0] + returned_first)).reshape(row_count)
 
 

time: 34.7 us -> 36.6 us (1.055)
  waiting for transfers between devices: 15.7 us -> 17.7 us
    ppermute x6, waiting for transfers between devices: 11.6 us -> 12.8 us  [on_line(): return lax.ppermute(value, 'gx', pairs)]
    ppermute x8, waiting for transfers between devices: 4.09 us -> 4.92 us  [in_plane(): return lax.ppermute(value, 'gx', [(i, i ^ step) for i in range(peers)])]
where the time goes in v41:
time: 36.6 us; the launch traced here: 36.3 us
  waiting for transfers between devices  17.7 us (48%)
  starting transfers between devices  14.1 us (39%)
  Pallas kernels  2.81 us (8%)
  local copies, waits for them, and re-layouts  1.08 us (3%)
  other arithmetic  0.58 us (2%)
    ppermute x6, waiting for transfers between devices, on_line(): return lax.ppermute(value, 'gx', pairs)  12.8 us
    ppermute x6, starting transfers between devices, on_line(): return lax.ppermute(value, 'gx', pairs)  9.64 us
    ppermute x8, waiting for transfers between devices, in_plane(): return lax.ppermute(value, 'gx', [(i, i ^ step) for i in range(peers)])  4.92 us
    ppermute x8, starting transfers between devices, in_plane(): return lax.ppermute(value, 'gx', [(i, i ^ step) for i in range(peers)])  4.45 us
    pallas_call x1, Pallas kernels, grid_plan(): pl.pallas_call(functools.partial(first_kernel, first_moves), out_shape=(l...  2.02 us
    slice x1, local copies, waits for them, and re-layouts, grid_plan(): first_head = on_line(embeddings[:part], first_moves, 0)  1.07 us
  transfers between devices with their start and end apart: 14, of which 8 were waited for; matrix products, arithmetic and copies ran while one was open for 0% of the time, Pallas kernels for 8%

profile of v41, /device:TPU:0, one launch (start us, length us, event | category | flops | bytes accessed | tf_op | source)
XLA Modules:
  0.0 36.3 jit_solution(15816603609211159401)
XLA Ops:
  0.0 0.0 copy-start
  0.0 1.1 %slice.3 = bf16[160,1024]{1,0:T(8,128)(2,1)S(1)} slice(bf16[256,1024]{1,0:T(8,128)(2,1)} %rows_ref.1), slice={[0:160], [0:1024]} | slice | bytes 655360 | tf_op jit(solution)/shard_map/slice | solution.py:285
  1.1 0.0 copy-start.1
  1.1 3.1 %collective-permute-start = (bf16[160,1024]{1,0:T(8,128)(2,1)S(1)}, bf16[160,1024]{1,0:T(8,128)(2,1)S(1)}, u32[]{:S(2)}, u32[]{:S(2)}) collective-permute-start(bf16[160,1024]{1,0:T(8,128)(2,1)S(1)} %slice.3), channel_id=1, source_target_pairs={{0,4},{1,5},{2,6},{3,7},{4,8},{5,9},{6,10},{7,11},{8,12},{9,13},{1... | collective-permute-start | bytes 983048 | tf_op jit(solution)/shard_map/ppermute | solution.py:274
  4.2 0.0 copy-done
  4.2 0.0 copy-done.1
  4.2 0.2 shard_map.28
  4.4 1.6 %collective-permute-start.4 = (bf16[136,1024]{1,0:T(8,128)(2,1)S(1)}, bf16[136,1024]{1,0:T(8,128)(2,1)S(1)}, u32[]{:S(2)}, u32[]{:S(2)}) collective-permute-start(bf16[136,1024]{1,0:T(8,128)(2,1)S(1)} %get-tuple-element.27), channel_id=1, source_target_pairs={{0,2},{1,3},{2,0},{3,1},{4,6},{5,7},{6,4},{7,5},{8,10},{9,11},{10,... | collective-permute-start | bytes 835592 | tf_op jit(solution)/shard_map/ppermute | solution.py:270
  5.9 0.0 collective-permute-start.2
  5.9 0.5 %collective-permute-start.3 = (bf16[128,1024]{1,0:T(8,128)(2,1)S(1)}, bf16[128,1024]{1,0:T(8,128)(2,1)S(1)}, u32[]{:S(2)}, u32[]{:S(2)}) collective-permute-start(bf16[128,1024]{1,0:T(8,128)(2,1)S(1)} %get-tuple-element.26), channel_id=1, source_target_pairs={{0,2},{1,3},{2,0},{3,1},{4,6},{5,7},{6,4},{7,5},{8,10},{9,11},{10,... | collective-permute-start | bytes 786440 | tf_op jit(solution)/shard_map/ppermute | solution.py:270
  6.5 0.3 shard_map.30.own_mass_ref
  6.8 1.6 %collective-permute-start.7 = (bf16[104,1024]{1,0:T(8,128)(2,1)S(1)}, bf16[104,1024]{1,0:T(8,128)(2,1)S(1)}, u32[]{:S(2)}, u32[]{:S(2)}) collective-permute-start(bf16[104,1024]{1,0:T(8,128)(2,1)S(1)} %get-tuple-element.31), channel_id=1, source_target_pairs={{0,4},{1,5},{2,6},{3,7},{4,8},{5,9},{6,10},{7,11},{8,12},{9,13},{1... | collective-permute-start | bytes 638984 | tf_op jit(solution)/shard_map/ppermute | solution.py:274
  8.4 6.3 %collective-permute-done.head_ref = bf16[160,1024]{1,0:T(8,128)(2,1)S(1)} collective-permute-done((bf16[160,1024]{1,0:T(8,128)(2,1)S(1)}, bf16[160,1024]{1,0:T(8,128)(2,1)S(1)}, u32[]{:S(2)}, u32[]{:S(2)}) %collective-permute-start) | collective-permute-done | bytes 327712 | tf_op jit(solution)/shard_map/ppermute | solution.py:274
  14.7 0.0 collective-permute-start.1
  14.7 0.0 collective-permute-done.4.refs_3_
  14.7 0.1 collective-permute-start.6
  14.9 3.3 %collective-permute-done.3.refs_2_ = bf16[128,1024]{1,0:T(8,128)(2,1)S(1)} collective-permute-done((bf16[128,1024]{1,0:T(8,128)(2,1)S(1)}, bf16[128,1024]{1,0:T(8,128)(2,1)S(1)}, u32[]{:S(2)}, u32[]{:S(2)}) %collective-permute-start.3) | collective-permute-done | bytes 262176 | tf_op jit(solution)/shard_map/ppermute | solution.py:270
  18.2 0.0 collective-permute-start.5
  18.2 0.3 collective-permute-done.7.tail_ref
  18.5 0.7 %collective-permute-start.8 = (bf16[104,1024]{1,0:T(8,128)(2,1)S(1)}, bf16[104,1024]{1,0:T(8,128)(2,1)S(1)}, u32[]{:S(2)}, u32[]{:S(2)}) collective-permute-start(bf16[104,1024]{1,0:T(8,128)(2,1)S(1)} %collective-permute-done.7.tail_ref), channel_id=1, source_target_pairs={{4,9},{5,8},{6,11},{7,10},{8,13},{9,12},{10,15},{11,14},{20,25},{2... | collective-permute-start | bytes 638984 | tf_op jit(solution)/shard_map/ppermute | solution.py:274
  19.1 0.6 %collective-permute-done.5.refs_4_ = bf16[128,1024]{1,0:T(8,128)(2,1)S(1)} collective-permute-done((bf16[128,1024]{1,0:T(8,128)(2,1)S(1)}, bf16[128,1024]{1,0:T(8,128)(2,1)S(1)}, u32[]{:S(2)}, u32[]{:S(2)}) %collective-permute-start.5) | collective-permute-done | bytes 262176 | tf_op jit(solution)/shard_map/ppermute | solution.py:270
  19.7 0.0 collective-permute-done.2.refs_1_
  19.7 0.0 collective-permute-done.6.refs_5_
  19.7 2.0 %shard_map.31 = (f32[1024,128]{1,0:T(8,128)S(1)}, f32[1,256]{1,0:T(1,128)S(1)}, f32[1024,128]{1,0:T(8,128)S(1)}, f32[1,256]{1,0:T(1,128)S(1)}) custom-call(f32[1,256]{1,0:T(1,128)S(1)} %shard_map.30.own_mass_ref, bf16[160,1024]{1,0:T(8,128)(2,1)S(1)} %collective-permute-done.head_ref, bf16[104,1024]{1,0:T(8,128)(2,1)S(1)} %collective-permute-done.7.tail_ref, ...), custom_call_target="tpu_custom_call" | custom-call | flops 1 | bytes 1 | tf_op jit(solution)/shard_map/pallas_call | solution.py:303
  21.7 3.0 %collective-permute-start.9 = (f32[1,256]{1,0:T(1,128)S(1)}, f32[1,256]{1,0:T(1,128)S(1)}, u32[]{:S(2)}, u32[]{:S(2)}) collective-permute-start(f32[1,256]{1,0:T(1,128)S(1)} %get-tuple-element.38), channel_id=1, source_target_pairs={{4,0},{5,1},{6,2},{7,3},{8,4},{9,5},{10,6},{11,7},{12,8},{13,9},{1... | collective-permute-start | bytes 3080 | tf_op jit(solution)/shard_map/ppermute | solution.py:274
  24.7 0.8 %collective-permute-done.1.head_ref = bf16[160,1024]{1,0:T(8,128)(2,1)S(1)} collective-permute-done((bf16[160,1024]{1,0:T(8,128)(2,1)S(1)}, bf16[160,1024]{1,0:T(8,128)(2,1)S(1)}, u32[]{:S(2)}, u32[]{:S(2)}) %collective-permute-start.1) | collective-permute-done | bytes 327712 | tf_op jit(solution)/shard_map/ppermute | solution.py:274
  25.5 0.0 collective-permute-done.8.tail_ref
  25.5 0.2 shard_map.33
  25.7 1.6 %collective-permute-start.10 = (f32[1,256]{1,0:T(1,128)S(1)}, f32[1,256]{1,0:T(1,128)S(1)}, u32[]{:S(2)}, u32[]{:S(2)}) collective-permute-start(f32[1,256]{1,0:T(1,128)S(1)} %get-tuple-element.41), channel_id=1, source_target_pairs={{0,2},{1,3},{2,0},{3,1},{4,6},{5,7},{6,4},{7,5},{8,10},{9,11},{10,... | collective-permute-start | bytes 3080 | tf_op jit(solution)/shard_map/ppermute | solution.py:270
  27.3 0.0 collective-permute-start.11
  27.3 0.6 %collective-permute-start.12 = (f32[1,256]{1,0:T(1,128)S(1)}, f32[1,256]{1,0:T(1,128)S(1)}, u32[]{:S(2)}, u32[]{:S(2)}) collective-permute-start(f32[1,256]{1,0:T(1,128)S(1)} %get-tuple-element.43), channel_id=1, source_target_pairs={{0,1},{1,0},{2,3},{3,2},{4,5},{5,4},{6,7},{7,6},{8,9},{9,8},{10,11... | collective-permute-start | bytes 3080 | tf_op jit(solution)/shard_map/ppermute | solution.py:270
  28.0 0.0 collective-permute-done.9
  28.0 1.3 %collective-permute-start.13 = (f32[1,256]{1,0:T(1,128)S(1)}, f32[1,256]{1,0:T(1,128)S(1)}, u32[]{:S(2)}, u32[]{:S(2)}) collective-permute-start(f32[1,256]{1,0:T(1,128)S(1)} %get-tuple-element.44), channel_id=1, source_target_pairs={{8,1},{9,0},{10,3},{11,2},{12,5},{13,4},{14,7},{15,6},{24,17},{25,... | collective-permute-start | bytes 3080 | tf_op jit(solution)/shard_map/ppermute | solution.py:274
  29.2 0.1 collective-permute-done.10
  29.4 0.9 %collective-permute-done.11 = f32[1,256]{1,0:T(1,128)S(1)} collective-permute-done((f32[1,256]{1,0:T(1,128)S(1)}, f32[1,256]{1,0:T(1,128)S(1)}, u32[]{:S(2)}, u32[]{:S(2)}) %collective-permute-start.11) | collective-permute-done | bytes 1056 | tf_op jit(solution)/shard_map/ppermute | solution.py:270
  30.3 0.0 collective-permute-done.12
  30.3 5.5 %collective-permute-done.13 = f32[1,256]{1,0:T(1,128)S(1)} collective-permute-done((f32[1,256]{1,0:T(1,128)S(1)}, f32[1,256]{1,0:T(1,128)S(1)}, u32[]{:S(2)}, u32[]{:S(2)}) %collective-permute-start.13) | collective-permute-done | bytes 1056 | tf_op jit(solution)/shard_map/ppermute | solution.py:274
  35.8 0.6 %add_log-plus-one_fusion = f32[1,256]{1,0:T(1,128)} fusion(f32[1,256]{1,0:T(1,128)S(1)} %collective-permute-done.13, f32[1,256]{1,0:T(1,128)S(1)} %collective-permute-done.12, f32[1,256]{1,0:T(1,128)S(1)} %collective-permute-done.11, f32[1,256]{1,0:T(1,128)S(1)} %collective-permute-done.10, f32[1,256]{1,0:T(1,128)S(1)} %get-tuple-element.37, ...), kind=kLoop, calls=%fused_computation | loop fusion | flops 1280 | bytes 7168 | tf_op jit(solution)/shard_map/log1p | solution.py:333
  (2 shorter events, 0.0 us)
Async XLA Ops:
  0.0 4.2 %copy-start = (bf16[256,1024]{1,0:T(8,128)(2,1)S(1)}, bf16[256,1024]{1,0:T(8,128)(2,1)}, u32[]{:S(2)}) copy-start(bf16[256,1024]{1,0:T(8,128)(2,1)} %rows_ref.1) | copy-start | bytes 1572868
  1.1 3.1 %copy-start.1 = (s32[256]{0:T(256)S(1)}, s32[256]{0:T(256)}, u32[]{:S(2)}) copy-start(s32[256]{0:T(256)} %param.3) | copy-start | bytes 3076
  1.1 13.6 %collective-permute-start = (bf16[160,1024]{1,0:T(8,128)(2,1)S(1)}, bf16[160,1024]{1,0:T(8,128)(2,1)S(1)}, u32[]{:S(2)}, u32[]{:S(2)}) collective-permute-start(bf16[160,1024]{1,0:T(8,128)(2,1)S(1)} %slice.3), channel_id=1, source_target_pairs={{0,4},{1,5},{2,6},{3,7},{4,8},{5,9},{6,10},{7,11},{8,12},{9,13},{1... | collective-permute-start | bytes 983048 | tf_op jit(solution)/shard_map/ppermute | solution.py:274
  4.4 10.4 %collective-permute-start.4 = (bf16[136,1024]{1,0:T(8,128)(2,1)S(1)}, bf16[136,1024]{1,0:T(8,128)(2,1)S(1)}, u32[]{:S(2)}, u32[]{:S(2)}) collective-permute-start(bf16[136,1024]{1,0:T(8,128)(2,1)S(1)} %get-tuple-element.27), channel_id=1, source_target_pairs={{0,2},{1,3},{2,0},{3,1},{4,6},{5,7},{6,4},{7,5},{8,10},{9,11},{10,... | collective-permute-start | bytes 835592 | tf_op jit(solution)/shard_map/ppermute | solution.py:270
  5.9 13.8 %collective-permute-start.2 = (bf16[264,1024]{1,0:T(8,128)(2,1)S(1)}, bf16[264,1024]{1,0:T(8,128)(2,1)S(1)}, u32[]{:S(2)}, u32[]{:S(2)}) collective-permute-start(bf16[264,1024]{1,0:T(8,128)(2,1)S(1)} %get-tuple-element.25.refs_0_.own_ref), channel_id=1, source_target_pairs={{0,1},{1,0},{2,3},{3,2},{4,5},{5,4},{6,7},{7,6},{8,9},{9,8},{10,11... | collective-permute-start | bytes 1622024 | tf_op jit(solution)/shard_map/ppermute | solution.py:270
  5.9 12.2 %collective-permute-start.3 = (bf16[128,1024]{1,0:T(8,128)(2,1)S(1)}, bf16[128,1024]{1,0:T(8,128)(2,1)S(1)}, u32[]{:S(2)}, u32[]{:S(2)}) collective-permute-start(bf16[128,1024]{1,0:T(8,128)(2,1)S(1)} %get-tuple-element.26), channel_id=1, source_target_pairs={{0,2},{1,3},{2,0},{3,1},{4,6},{5,7},{6,4},{7,5},{8,10},{9,11},{10,... | collective-permute-start | bytes 786440 | tf_op jit(solution)/shard_map/ppermute | solution.py:270
  6.8 11.6 %collective-permute-start.7 = (bf16[104,1024]{1,0:T(8,128)(2,1)S(1)}, bf16[104,1024]{1,0:T(8,128)(2,1)S(1)}, u32[]{:S(2)}, u32[]{:S(2)}) collective-permute-start(bf16[104,1024]{1,0:T(8,128)(2,1)S(1)} %get-tuple-element.31), channel_id=1, source_target_pairs={{0,4},{1,5},{2,6},{3,7},{4,8},{5,9},{6,10},{7,11},{8,12},{9,13},{1... | collective-permute-start | bytes 638984 | tf_op jit(solution)/shard_map/ppermute | solution.py:274
  14.7 10.8 %collective-permute-start.1 = (bf16[160,1024]{1,0:T(8,128)(2,1)S(1)}, bf16[160,1024]{1,0:T(8,128)(2,1)S(1)}, u32[]{:S(2)}, u32[]{:S(2)}) collective-permute-start(bf16[160,1024]{1,0:T(8,128)(2,1)S(1)} %collective-permute-done.head_ref), channel_id=1, source_target_pairs={{0,5},{1,4},{2,7},{3,6},{4,9},{5,8},{6,11},{7,10},{8,13},{9,12},{1... | collective-permute-start | bytes 983048 | tf_op jit(solution)/shard_map/ppermute | solution.py:274
  14.7 5.0 %collective-permute-start.6 = (bf16[136,1024]{1,0:T(8,128)(2,1)S(1)}, bf16[136,1024]{1,0:T(8,128)(2,1)S(1)}, u32[]{:S(2)}, u32[]{:S(2)}) collective-permute-start(bf16[136,1024]{1,0:T(8,128)(2,1)S(1)} %collective-permute-done.4.refs_3_), channel_id=1, source_target_pairs={{0,1},{1,0},{2,3},{3,2},{4,5},{5,4},{6,7},{7,6},{8,9},{9,8},{10,11... | collective-permute-start | bytes 835592 | tf_op jit(solution)/shard_map/ppermute | solution.py:270
  18.2 1.5 %collective-permute-start.5 = (bf16[128,1024]{1,0:T(8,128)(2,1)S(1)}, bf16[128,1024]{1,0:T(8,128)(2,1)S(1)}, u32[]{:S(2)}, u32[]{:S(2)}) collective-permute-start(bf16[128,1024]{1,0:T(8,128)(2,1)S(1)} %collective-permute-done.3.refs_2_), channel_id=1, source_target_pairs={{0,1},{1,0},{2,3},{3,2},{4,5},{5,4},{6,7},{7,6},{8,9},{9,8},{10,11... | collective-permute-start | bytes 786440 | tf_op jit(solution)/shard_map/ppermute | solution.py:270
  18.5 7.0 %collective-permute-start.8 = (bf16[104,1024]{1,0:T(8,128)(2,1)S(1)}, bf16[104,1024]{1,0:T(8,128)(2,1)S(1)}, u32[]{:S(2)}, u32[]{:S(2)}) collective-permute-start(bf16[104,1024]{1,0:T(8,128)(2,1)S(1)} %collective-permute-done.7.tail_ref), channel_id=1, source_target_pairs={{4,9},{5,8},{6,11},{7,10},{8,13},{9,12},{10,15},{11,14},{20,25},{2... | collective-permute-start | bytes 638984 | tf_op jit(solution)/shard_map/ppermute | solution.py:274
  21.7 6.2 %collective-permute-start.9 = (f32[1,256]{1,0:T(1,128)S(1)}, f32[1,256]{1,0:T(1,128)S(1)}, u32[]{:S(2)}, u32[]{:S(2)}) collective-permute-start(f32[1,256]{1,0:T(1,128)S(1)} %get-tuple-element.38), channel_id=1, source_target_pairs={{4,0},{5,1},{6,2},{7,3},{8,4},{9,5},{10,6},{11,7},{12,8},{13,9},{1... | collective-permute-start | bytes 3080 | tf_op jit(solution)/shard_map/ppermute | solution.py:274
  25.7 3.6 %collective-permute-start.10 = (f32[1,256]{1,0:T(1,128)S(1)}, f32[1,256]{1,0:T(1,128)S(1)}, u32[]{:S(2)}, u32[]{:S(2)}) collective-permute-start(f32[1,256]{1,0:T(1,128)S(1)} %get-tuple-element.41), channel_id=1, source_target_pairs={{0,2},{1,3},{2,0},{3,1},{4,6},{5,7},{6,4},{7,5},{8,10},{9,11},{10,... | collective-permute-start | bytes 3080 | tf_op jit(solution)/shard_map/ppermute | solution.py:270
  27.3 3.0 %collective-permute-start.11 = (f32[1,256]{1,0:T(1,128)S(1)}, f32[1,256]{1,0:T(1,128)S(1)}, u32[]{:S(2)}, u32[]{:S(2)}) collective-permute-start(f32[1,256]{1,0:T(1,128)S(1)} %get-tuple-element.42), channel_id=1, source_target_pairs={{0,3},{1,2},{2,1},{3,0},{4,7},{5,6},{6,5},{7,4},{8,11},{9,10},{10,... | collective-permute-start | bytes 3080 | tf_op jit(solution)/shard_map/ppermute | solution.py:270
  27.3 3.0 %collective-permute-start.12 = (f32[1,256]{1,0:T(1,128)S(1)}, f32[1,256]{1,0:T(1,128)S(1)}, u32[]{:S(2)}, u32[]{:S(2)}) collective-permute-start(f32[1,256]{1,0:T(1,128)S(1)} %get-tuple-element.43), channel_id=1, source_target_pairs={{0,1},{1,0},{2,3},{3,2},{4,5},{5,4},{6,7},{7,6},{8,9},{9,8},{10,11... | collective-permute-start | bytes 3080 | tf_op jit(solution)/shard_map/ppermute | solution.py:270
  28.0 7.8 %collective-permute-start.13 = (f32[1,256]{1,0:T(1,128)S(1)}, f32[1,256]{1,0:T(1,128)S(1)}, u32[]{:S(2)}, u32[]{:S(2)}) collective-permute-start(f32[1,256]{1,0:T(1,128)S(1)} %get-tuple-element.44), channel_id=1, source_target_pairs={{8,1},{9,0},{10,3},{11,2},{12,5},{13,4},{14,7},{15,6},{24,17},{25,... | collective-permute-start | bytes 3080 | tf_op jit(solution)/shard_map/ppermute | solution.py:274
